TPU v7x, 32 devices: a whole 2x2x4 slice. The times are simulated.
32 devices in a mesh: ex: 4 (over z), feat: 8 (over y, x, core).
Axes of the slice: x: 2, y: 2, z: 4, core: 2. Of those that a mesh axis runs over, the one named last changes fastest.
Arguments:
- dosages: bfloat16 [16384, 4096], P('ex', 'feat'), may hold values from -6 to 6
- coefficients: bfloat16 [4096], P('feat'), may hold values from -0.046875 to 0.046875
- directions: bfloat16 [4096, 128], P('feat'), may hold values from -6 to 6
- event_rank: int32 [16384], P('ex'), may hold values from 0 to 16383, as said below
- events: int32 [16384], P('ex'), may hold values from 0 to 1, as said below
Outputs:
- hessian_product: float32 [4096, 128], P('feat')
Inputs may be any that keep to these rules, and one draw needn't show every extreme that they name: `event_rank`: the 4096 persons of each aligned block b (one index of ex) hold the ranks b * 4096 to (b + 1) * 4096 - 1, each once, in any order. `events`: the first person of every aligned block of 4096 persons has an event.
All inputs are finite; a program needn't handle non-finite values.
Results may differ from a plain program's by a relative error of at most 0.00084.
Values may be sent and summed in bfloat16 or wider, within the bound.
No kernel may reach another device: no remote copies, remote signals or barrier semaphores. Data moves between devices by JAX's collectives and lax.ppermute only.
A program may use at most 64 MiB of HBM per device.

v0:
```python
import jax
import jax.numpy as jnp
from jax import lax
from jax.sharding import PartitionSpec as P


def carried_in(part, axis, combine, identity, reverse):
    count = lax.axis_size(axis)
    place = lax.axis_index(axis)
    ahead = count - 1 - place if reverse else place
    gathered = jax.tree.map(lambda a: lax.all_gather(a, axis), part)
    state = jax.tree.map(lambda a, e: jnp.zeros_like(a) + jnp.asarray(e, a.dtype), part, identity)

    def one(lap, state):
        source = count - 1 - lap if reverse else lap
        return combine(
            state, jax.tree.map(lambda a: lax.dynamic_index_in_dim(a, source, 0, False), gathered)
        )

    return lax.fori_loop(0, ahead, one, state)


def combine_sum(earlier, later):
    return jax.tree.map(lambda former, latter: former + latter, earlier, later)


def ordered_sums(values, local_rank, order, later):
    n_rows, length = values.shape
    tile_len = min(128, length)
    tile_count = length // tile_len
    placed = jnp.take(values, order, axis=1).reshape(n_rows, tile_count, tile_len)
    first_pos = lax.broadcasted_iota(jnp.int32, (tile_len, tile_len), 0)
    second_pos = lax.broadcasted_iota(jnp.int32, (tile_len, tile_len), 1)
    if later:
        member = (first_pos >= second_pos).astype(jnp.float32)
    else:
        member = (first_pos <= second_pos).astype(jnp.float32)
    inside = jnp.einsum("knt,ts->kns", placed, member, precision=lax.Precision.HIGHEST)
    totals = jnp.sum(placed, axis=2)
    running = lax.cumsum(totals, axis=1, reverse=later)
    nothing = jnp.zeros((n_rows, 1), jnp.float32)
    if later:
        carried = jnp.concatenate([running[:, 1:], nothing], axis=1)
    else:
        carried = jnp.concatenate([nothing, running[:, :-1]], axis=1)
    summed = (inside + carried[:, :, None]).reshape(n_rows, length)
    return jnp.take(summed, local_rank, axis=1)


def local(dosages, coefficients, directions, event_rank, events):
    persons = dosages.shape[0]
    event_flt = events.astype(jnp.float32)
    local_count = jnp.sum(event_flt)
    local_rank = event_rank - jnp.min(event_rank)
    order = jnp.zeros_like(local_rank).at[local_rank].set(lax.iota(jnp.int32, persons))
    event_count = lax.psum(local_count, "ex")
    linear_part = jnp.dot(dosages, coefficients, preferred_element_type=jnp.float32)
    tangent_part = lax.dot_general(
        directions, dosages, (((0,), (1,)), ((), ())), preferred_element_type=jnp.float32
    )
    tangent, linear = lax.psum((tangent_part, linear_part), "feat")
    risk = jnp.exp(linear)
    weighted_t = tangent * risk[None, :]
    zero_pair = (jnp.zeros((), jnp.float32), jnp.zeros((weighted_t.shape[0],), jnp.float32))
    risk_local = ordered_sums(risk[None, :], local_rank, order, True)[0]
    tangent_local = ordered_sums(weighted_t, local_rank, order, True)
    later_risk, later_tangent = carried_in(
        (jnp.sum(risk), jnp.sum(weighted_t, axis=1)), "ex", combine_sum, zero_pair, True
    )
    risk_sum = risk_local + later_risk
    tangent_sum = tangent_local + later_tangent[:, None]
    hazard = event_flt / risk_sum
    hazard_tangent = tangent_sum * (event_flt / (risk_sum * risk_sum))[None, :]
    hazard_prior = ordered_sums(hazard[None, :], local_rank, order, False)[0]
    tangent_prior = ordered_sums(hazard_tangent, local_rank, order, False)
    earlier_hazard, earlier_tangent = carried_in(
        (jnp.sum(hazard), jnp.sum(hazard_tangent, axis=1)), "ex", combine_sum, zero_pair, False
    )
    cumulative = hazard_prior + earlier_hazard
    cumulative_tangent = tangent_prior + earlier_tangent[:, None]
    weighted = (risk[None, :] * (tangent * cumulative[None, :] - cumulative_tangent)).astype(
        jnp.bfloat16
    )
    partial_sum = lax.dot_general(
        dosages, weighted, (((0,), (1,)), ((), ())), preferred_element_type=jnp.float32
    )
    total = lax.psum(partial_sum, "ex")
    return total / event_count


def solution(mesh):
    placed = (P("ex", "feat"), P("feat"), P("feat", None), P("ex"), P("ex"))
    return jax.shard_map(
        local, mesh=mesh, in_specs=placed, out_specs=P("feat", None), check_vma=False
    )
```

profile of v0, /device:TPU:0, one launch (start us, length us, event | category | flops | bytes accessed | tf_op | source)
XLA Modules:
  0.0 328.1 jit_solution(16383498592659852841)
XLA Ops:
  7.4 5.0 %fusion.33 = f32[128,4096]{1,0:T(8,128)} fusion(bf16[512,128]{1,0:T(8,128)(2,1)S(1)} %copy-done, bf16[4096,512]{1,0:T(8,128)(2,1)} %param.13), kind=kOutput, calls=%fused_computation.72 | convolution fusion | flops 536870912 | bytes 6422528 | tf_op jit(solution)/shard_map/dot_general | solution.py:58
  13.1 3.4 %fusion.32 = f32[1,4096]{1,0:T(1,128)S(1)} fusion(bf16[4096,512]{1,0:T(8,128)(2,1)} %param.13, bf16[512,1]{0,1:T(2,128)(2,1)S(1)} %reshape.208), kind=kOutput, calls=%fused_computation.71 | convolution fusion | flops 4194304 | bytes 4211712 | tf_op jit(solution)/shard_map/dot_general | solution.py:57
  16.5 26.0 %psum.28 = f32[4096]{0:T(1024)S(1)} all-reduce(f32[4096]{0:T(1024)S(1)} %bitcast.99), channel_id=1, replica_groups=mesh['ex'=4,'feat'=8] {'feat'}, use_global_device_ids=true, to_apply=%region_0.0 | all-reduce | flops 4096 | bytes 32768 | tf_op jit(solution)/shard_map/psum | solution.py:61
  45.1 11.8 %all-reduce.2 = f32[4]{0:T(128)S(1)} all-reduce(f32[4]{0:T(128)S(1)} %dynamic-update-slice), channel_id=1, replica_groups=mesh['ex'=4,'feat'=8] {'ex'}, use_global_device_ids=true, to_apply=%add.2 | all-reduce | flops 4 | bytes 32
  58.2 15.5 %scatter_custom_fusion = s32[4096]{0:T(1024)S(1)} fusion(s32[4096]{0:T(1024)S(1)} %get-tuple-element.165, s32[4096]{0:T(1024)S(1)} %iota.37, s32[]{:T(128)} %constant.81.clone.1), kind=kCustom, calls=%fused_computation.52 | custom fusion | bytes 16388 | tf_op jit(solution)/shard_map/scatter | solution.py:55
  73.7 23.0 %gather_fusion = f32[4096]{0:T(1024)S(1)} fusion(f32[4096]{0:T(1024)S(1)} %get-tuple-element.171, s32[4096]{0:T(1024)S(1)} %fusion.18), kind=kCustom, calls=%fused_computation.clone | custom fusion | bytes 49152 | tf_op jit(solution)/shard_map/jit(_take)/gather | solution.py:31
  97.4 23.1 %gather_fusion.1 = f32[4096]{0:T(1024)S(1)} fusion(f32[4096]{0:T(1024)S(1)} %fusion.5, s32[4096]{0:T(1024)S(1)} %get-tuple-element.164), kind=kCustom, calls=%fused_computation.2.clone | custom fusion | bytes 49152 | tf_op jit(solution)/shard_map/jit(_take)/gather | solution.py:47
  120.6 3.1 fusion.31
  125.6 14.1 %gather_fusion.4 = f32[4096,128]{1,0:T(8,128)} fusion(f32[128,4096]{0,1:T(8,128)S(1)} %copy.21, s32[4096]{0:T(1024)S(1)} %fusion.18), kind=kCustom, calls=%fused_computation.1.clone | custom fusion | bytes 4210688 | tf_op jit(solution)/shard_map/jit(_take)/gather | solution.py:31
  139.7 2.9 bitcast_reduce_fusion.3
  145.5 14.1 %gather_fusion.5 = f32[4096,128]{1,0:T(8,128)} fusion(f32[128,4096]{0,1:T(8,128)S(1)} %bitcast.96, s32[4096]{0:T(1024)S(1)} %get-tuple-element.164), kind=kCustom, calls=%fused_computation.5.clone | custom fusion | bytes 4210688 | tf_op jit(solution)/shard_map/jit(_take)/gather | solution.py:47
  159.6 7.5 %all-gather.2 = f32[4,1,128]{2,1,0:T(1,128)S(1)} all-gather(f32[1,1,128]{2,1,0:T(1,128)S(1)} %bitcast.107), channel_id=2, replica_groups=mesh['ex'=4,'feat'=8] {'ex'}, dimensions={0}, use_global_device_ids=true | all-gather | bytes 2560 | tf_op jit(solution)/shard_map/all_gather | solution.py:11
  167.1 4.1 %while.26 = (s32[]{:T(128)}, f32[]{:T(128)}, f32[128]{0:T(128)S(1)}, s32[]{:T(128)}, f32[4]{0:T(128)S(1)}, /*index=5*/f32[4,128]{1,0:T(4,128)S(1)}, s32[]{:T(128)}, s32[]{:T(128)}, s32[]{:T(128)}, s32[]{:T(128)}) while((s32[]{:T(128)}, f32[]{:T(128)}, f32[128]{0:T(128)S(1)}, s32[]{:T(128)}, f32[4]{0:T(128)S(1)}, ...), condition=%wide.region_9.11_spmd, body=%wide.region_8.10_spmd.sunk | while | flops 135 | bytes 1711 | solution.py:20
  172.0 3.2 fusion.28
  175.2 8.1 %all-gather.3 = f32[4,1,128]{2,1,0:T(1,128)S(1)} all-gather(f32[1,1,128]{2,1,0:T(1,128)S(1)} %bitcast.108), channel_id=3, replica_groups=mesh['ex'=4,'feat'=8] {'ex'}, dimensions={0}, use_global_device_ids=true | all-gather | bytes 2560 | tf_op jit(solution)/shard_map/all_gather | solution.py:11
  184.6 10.4 %all-reduce.4 = (f32[4]{0:T(128)S(1)}, f32[]{:T(128)}) all-reduce(f32[4]{0:T(128)S(1)} %dynamic-update-slice.1, f32[]{:T(128)} %get-tuple-element.169), channel_id=1, replica_groups=mesh['ex'=4,'feat'=8] {'ex'}, use_global_device_ids=true, to_apply=%add.3 | all-reduce | flops 5 | bytes 40
  195.0 23.0 %gather_fusion.2 = f32[4096]{0:T(1024)S(1)} fusion(f32[4096]{0:T(1024)S(1)} %get-tuple-element.155, s32[4096]{0:T(1024)S(1)} %fusion.18), kind=kCustom, calls=%fused_computation.3.clone | custom fusion | bytes 49152 | tf_op jit(solution)/shard_map/jit(_take)/gather | solution.py:31
  218.5 23.1 %gather_fusion.3 = f32[4096]{0:T(1024)S(1)} fusion(f32[4096]{0:T(1024)S(1)} %fusion.4, s32[4096]{0:T(1024)S(1)} %get-tuple-element.164), kind=kCustom, calls=%fused_computation.4.clone | custom fusion | bytes 49152 | tf_op jit(solution)/shard_map/jit(_take)/gather | solution.py:47
  241.6 14.1 %gather_fusion.6 = f32[4096,128]{1,0:T(8,128)} fusion(f32[128,4096]{0,1:T(8,128)S(1)} %get-tuple-element.153, s32[4096]{0:T(1024)S(1)} %fusion.18), kind=kCustom, calls=%fused_computation.6.clone | custom fusion | bytes 4210688 | tf_op jit(solution)/shard_map/jit(_take)/gather | solution.py:31
  255.7 2.9 bitcast_reduce_fusion.2
  261.5 14.1 %gather_fusion.7 = f32[4096,128]{1,0:T(8,128)} fusion(f32[128,4096]{0,1:T(8,128)S(1)} %bitcast.95, s32[4096]{0:T(1024)S(1)} %get-tuple-element.164), kind=kCustom, calls=%fused_computation.7.clone | custom fusion | bytes 4210688 | tf_op jit(solution)/shard_map/jit(_take)/gather | solution.py:47
  275.6 3.0 copy.24
  278.7 4.4 %convolution_bitcast_fusion = f32[512,128]{0,1:T(8,128)} fusion(bf16[4096,512]{1,0:T(8,128)(2,1)} %param.13, f32[4096,128]{0,1:T(8,128)} %copy.24, f32[128,4096]{1,0:T(8,128)S(1)} %copy-done.1, f32[128]{0:T(128)S(1)} %get-tuple-element.125, f32[4096]{0:T(1024)S(1)} %bitcast.100, f32[4096]{0:T(1024)S(1)} %get-tuple-element.171, ...), kind=kOutput, calls=%fused_computation.19 | convolution fusion | flops 540016640 | bytes 8688128 | tf_op jit(solution)/shard_map/dot_general | solution.py:84
  283.1 35.7 %all-reduce.10.cloned.1.call-done = f32[512,128]{0,1:T(8,128)} async-done(((f32[512,128]{0,1:T(8,128)}), f32[512,128]{0,1:T(8,128)}) %all-reduce.10.cloned.1.call-update) | async-done | bytes 262160 | tf_op jit(solution)/shard_map/psum | solution.py:87
  (61 shorter events, 20.9 us)
Async XLA Ops:
  6.5 0.9 copy-start
  6.5 114.0 %all-reduce.8.cloned.1.call-start = ((), (), s32[]{:S(2)}) async-start(), calls=%async_computation | async-start | bytes 4194304 | tf_op jit(solution)/shard_map/psum | solution.py:61
  12.4 0.7 copy-start.4
  12.4 306.3 %all-reduce.10.cloned.1.call-start = ((), (), s32[]{:S(2)}) async-start(), calls=%async_computation.1 | async-start | bytes 524288 | tf_op jit(solution)/shard_map/psum | solution.py:87
  13.1 30.0 %copy-start.5 = (u32[32]{0:T(128)S(1)}, u32[32]{0:T(128)}, u32[]{:S(2)}) copy-start(u32[32]{0:T(128)} %constant.94) | copy-start | bytes 388
  13.1 43.8 %copy-start.2 = (s32[4096]{0:T(1024)S(1)}, s32[4096]{0:T(1024)}, u32[]{:S(2)}) copy-start(s32[4096]{0:T(1024)} %param.16) | copy-start | bytes 49156
  145.5 25.8 %copy-start.3 = (s32[4096]{0:T(1024)S(1)}, s32[4096]{0:T(1024)}, u32[]{:S(2)}) copy-start(s32[4096]{0:T(1024)} %param.17) | copy-start | bytes 49156
  275.6 3.0 copy-start.1
Sparse Core Ops, SparseCore 0:
  12.6 64.2 all-reduce.7
  283.2 35.5 all-reduce.9
where the time goes:
time: 329 us; the launch traced here: 328 us
  local copies, waits for them, and re-layouts  177 us (54%)
  blocking collectives  63.8 us (19%)
  waiting for transfers between devices  35.8 us (11%)
  matrix products  18.6 us (6%)
  other arithmetic  17.4 us (5%)
  between operations  13.6 us (4%)
    gather x5, local copies, waits for them, and re-layouts, ordered_sums(): return jnp.take(summed, local_rank, axis=1)  77.4 us
    gather x4, local copies, waits for them, and re-layouts, ordered_sums(): jnp.take(values, order, axis=1).reshape(n_rows, tile_count, tile_len)  74.2 us
    psum x1, waiting for transfers between devices, local(): total = lax.psum(partial_sum, 'ex')  35.7 us
    psum x1, blocking collectives, local(): tangent, linear = lax.psum((tangent_part, linear_part), 'feat')  26 us
    unnamed x2, blocking collectives  22.2 us
    all_gather x2, blocking collectives, carried_in(): gathered = jax.tree.map(lambda a: lax.all_gather(a, axis), part)  15.6 us
    scatter x1, local copies, waits for them, and re-layouts, local(): jnp.zeros_like(local_rank).at[local_rank].set(lax.iota(jnp.int32, persons))  15.5 us
  transfers between devices with their start and end apart: 2, of which 1 were waited for; matrix products, arithmetic and copies ran while one was open for 21% of the time, Pallas kernels for 0%

commit v1 on v0

v1 whole, which is shorter than its diff:
```python
import functools

import jax
import jax.numpy as jnp
from jax import lax
from jax.experimental import pallas as pl
from jax.experimental.pallas import tpu as pltpu
from jax.sharding import PartitionSpec as P

F32 = jnp.float32
BF16 = jnp.bfloat16
LO = 256
NT = (((1,), (1,)), ((), ()))
VMEM = pl.BlockSpec(memory_space=pltpu.VMEM)
HIGHEST = lax.Precision.HIGHEST
PARAMS = dict(vmem_limit_bytes=48 * 1024 * 1024)


def swap(x, axis, i):
    count = lax.axis_size(axis)
    return lax.ppermute(x, axis, [(s, s ^ i) for s in range(count)])


def split_two(x):
    high = x.astype(BF16).astype(F32)
    return high, x - high


def split_three(x):
    first, rest = split_two(x)
    second, third = split_two(rest)
    return first, second, third


def one_hot(values, count, kind=BF16):
    shape = (count, values.shape[1])
    return jnp.where(lax.broadcasted_iota(jnp.int32, shape, 0) == values, 1.0, 0.0).astype(kind)


def triangle(n, keep):
    first = lax.broadcasted_iota(jnp.int32, (n, n), 0)
    second = lax.broadcasted_iota(jnp.int32, (n, n), 1)
    return jnp.where(keep(first, second), 1.0, 0.0)


def exact_dot(a, b):
    return jnp.dot(a, b, precision=HIGHEST, preferred_element_type=F32)


def product_kernel(feat, kf, directions, coefficients, dosages, *refs):
    linear, keep, send = refs[0], refs[1 : 1 + feat // 2], refs[1 + feat // 2 : 1 + feat]
    lhs, turned = refs[1 + feat :]
    me = lax.axis_index("feat")
    width = feat * kf

    @pl.when(pl.program_id(0) == 0)
    def _():
        turned[...] = directions[...].astype(F32).T.reshape(turned.shape)
        for i in range(feat):
            lhs[i * kf : (i + 1) * kf] = turned[me ^ i].astype(BF16)
        lhs[width:] = jnp.broadcast_to(coefficients[...].astype(F32), (16, lhs.shape[1])).astype(BF16)

    result = lax.dot_general(lhs[...], dosages[...], NT, preferred_element_type=F32)
    linear[...] = result[width : width + 1]
    for i in range(feat):
        (send if i % 2 else keep)[i // 2][...] = result[i * kf : (i + 1) * kf]


def products(dosages, coefficients, directions, feat):
    persons, variants = dosages.shape
    k = directions.shape[1]
    kf = k // feat
    chunk = min(512, persons)
    piece = jax.ShapeDtypeStruct((kf, persons), F32)
    out = pl.pallas_call(
        functools.partial(product_kernel, feat, kf),
        grid=(persons // chunk,),
        in_specs=[
            pl.BlockSpec((variants, k), lambda s: (0, 0)),
            pl.BlockSpec((1, variants), lambda s: (0, 0)),
            pl.BlockSpec((chunk, variants), lambda s: (s, 0)),
        ],
        out_shape=[jax.ShapeDtypeStruct((1, persons), F32)] + [piece] * feat,
        out_specs=[pl.BlockSpec((1, chunk), lambda s: (0, s))]
        + [pl.BlockSpec((kf, chunk), lambda s: (0, s))] * feat,
        scratch_shapes=[
            pltpu.VMEM((k + 16, variants), BF16),
            pltpu.VMEM((feat, kf, variants), F32),
        ],
        compiler_params=pltpu.CompilerParams(**PARAMS),
        cost_estimate=pl.CostEstimate(
            flops=2 * persons * variants * k, bytes_accessed=persons * (variants * 2 + k * 4), transcendentals=0
        ),
        name="products",
    )(directions, coefficients[None], dosages)
    return out[0], out[1 : 1 + feat // 2], out[1 + feat // 2 :]


def risk_kernel(rows, parts, *refs):
    linear, (rank, events) = refs[:parts], refs[parts : parts + 2]
    risk_out, sums_out, events_out, message = refs[parts + 2 :]
    groups = rows // LO
    total = linear[0][...]
    for part in linear[1:]:
        total = total + part[...]
    risk = jnp.exp(total)
    risk_out[...] = risk
    place = lax.rem(rank[...], rows)
    mask = one_hot(place // LO, groups, F32)
    pieces = [mask * part for part in split_three(risk)] + [mask * events[...].astype(F32)]
    lhs = jnp.concatenate(pieces, axis=0).astype(BF16)
    sorted_all = lax.dot_general(lhs, one_hot(lax.rem(place, LO), LO), NT, preferred_element_type=F32)
    ordered = sorted_all[:groups] + sorted_all[groups : 2 * groups] + sorted_all[2 * groups : 3 * groups]
    happened = sorted_all[3 * groups :]
    inside = exact_dot(ordered, triangle(LO, lambda a, b: a >= b))
    totals = exact_dot(ordered, jnp.ones((LO, LO), F32))
    carried = exact_dot(triangle(groups, lambda a, b: a < b), totals)
    sums_out[...] = inside + carried
    events_out[...] = happened
    everything = jnp.sum(totals, axis=0, keepdims=True)[:, :128]
    count = jnp.sum(exact_dot(happened, jnp.ones((LO, 128), F32)), axis=0, keepdims=True)
    message[...] = jnp.concatenate([everything, count, jnp.zeros((6, 128), F32)], axis=0)


def risks(linear, rank, events, rows):
    groups = rows // LO
    return pl.pallas_call(
        functools.partial(risk_kernel, rows, len(linear)),
        in_specs=[VMEM] * (len(linear) + 2),
        out_shape=[
            jax.ShapeDtypeStruct((1, rows), F32),
            jax.ShapeDtypeStruct((groups, LO), F32),
            jax.ShapeDtypeStruct((groups, LO), F32),
            jax.ShapeDtypeStruct((8, 128), F32),
        ],
        out_specs=[VMEM] * 4,
        compiler_params=pltpu.CompilerParams(**PARAMS),
        cost_estimate=pl.CostEstimate(flops=rows * LO * 128, bytes_accessed=rows * 64, transcendentals=rows),
        name="risks",
    )(*linear, rank, events)


def hazard_kernel(rows, ex, *refs):
    messages, (sums, events, rank) = refs[:ex], refs[ex : ex + 3]
    cumulative, squares, ordered_squares, message, count_out = refs[ex + 3 :]
    groups = rows // LO
    me = lax.axis_index("ex")
    later = jnp.zeros((1, 1), F32)
    count = messages[0][1:2, :]
    for i in range(1, ex):
        later = later + jnp.where((me ^ i) > me, messages[i][0:1, 0:1], 0.0)
        count = count + messages[i][1:2, :]
    count_out[...] = jnp.broadcast_to(count, count_out.shape)
    risk_sum = sums[...] + later
    hazard = events[...] / risk_sum
    square = events[...] / (risk_sum * risk_sum)
    ordered_squares[...] = square
    both = jnp.concatenate([hazard, square], axis=0)
    inside = exact_dot(both, triangle(LO, lambda a, b: a <= b))
    totals = exact_dot(both, jnp.ones((LO, LO), F32))
    before = triangle(groups, lambda a, b: a > b)
    carried = jnp.concatenate(
        [exact_dot(before, totals[:groups]), exact_dot(before, totals[groups:])], axis=0
    )
    message[...] = jnp.concatenate(
        [
            jnp.sum(totals[:groups], axis=0, keepdims=True)[:, :128],
            jnp.sum(totals[groups:], axis=0, keepdims=True)[:, :128],
            jnp.zeros((6, 128), F32),
        ],
        axis=0,
    )
    place = lax.rem(rank[...], rows)
    mask = one_hot(place // LO, groups, F32)
    spread = one_hot(lax.rem(place, LO), LO)
    placed = jnp.zeros((2 * groups, rows), F32)
    for part in split_three(inside + carried):
        placed = placed + jnp.dot(part.astype(BF16), spread, preferred_element_type=F32)
    cumulative[...] = jnp.sum(mask * placed[:groups], axis=0, keepdims=True)
    squares[...] = jnp.sum(mask * placed[groups:], axis=0, keepdims=True)


def hazards(messages, sums, events, rank, rows):
    groups = rows // LO
    row = jax.ShapeDtypeStruct((1, rows), F32)
    small = jax.ShapeDtypeStruct((8, 128), F32)
    return pl.pallas_call(
        functools.partial(hazard_kernel, rows, len(messages)),
        in_specs=[VMEM] * (len(messages) + 3),
        out_shape=[row, row, jax.ShapeDtypeStruct((groups, LO), F32), small, small],
        out_specs=[VMEM] * 5,
        compiler_params=pltpu.CompilerParams(**PARAMS),
        cost_estimate=pl.CostEstimate(flops=rows * LO * 200, bytes_accessed=rows * 64, transcendentals=0),
        name="hazards",
    )(*messages, sums, events, rank)


def scan_kernel(rows, kf, parts, *refs):
    tangents = refs[:parts]
    risk, rank, squares, hazard_message = refs[parts : parts + 4]
    tangent_out, cumulative_out, message = refs[parts + 4 : parts + 7]
    lhs, spread = refs[parts + 7 :]
    groups = rows // LO
    chunk = min(1024, rows)
    ordered = jnp.zeros((groups * 2 * kf, LO), F32)
    for start in range(0, rows, chunk):
        at = slice(start, start + chunk)
        tangent = tangents[0][:, at]
        for part in tangents[1:]:
            tangent = tangent + part[:, at]
        tangent_out[:, at] = tangent
        place = lax.rem(rank[:, at], rows)
        group = place // LO
        spread[:, at] = one_hot(lax.rem(place, LO), LO)
        both = jnp.concatenate(split_two(tangent * risk[:, at]), axis=0)
        for g in range(groups):
            lhs[g * 2 * kf : (g + 1) * 2 * kf, at] = jnp.where(group == g, both, 0.0).astype(BF16)
        ordered = ordered + lax.dot_general(lhs[:, at], spread[:, at], NT, preferred_element_type=F32)
    ordered = jnp.concatenate(
        [
            ordered[g * 2 * kf : g * 2 * kf + kf] + ordered[g * 2 * kf + kf : (g + 1) * 2 * kf]
            for g in range(groups)
        ],
        axis=0,
    )
    everything = jnp.ones((LO, LO), F32)
    inside = exact_dot(ordered, triangle(LO, lambda a, b: a >= b))
    totals = exact_dot(ordered, everything)
    carried = jnp.zeros((kf, LO), F32)
    hazard = [None] * groups
    for g in reversed(range(groups)):
        rows_of = slice(g * kf, (g + 1) * kf)
        hazard[g] = (inside[rows_of] + carried) * squares[g : g + 1, :]
        carried = carried + totals[rows_of]
    message[0] = carried[:, :128]
    hazard = jnp.concatenate(hazard, axis=0)
    inside = exact_dot(hazard, triangle(LO, lambda a, b: a <= b))
    totals = exact_dot(hazard, everything)
    carried = jnp.zeros((kf, LO), F32)
    summed = [None] * groups
    for g in range(groups):
        rows_of = slice(g * kf, (g + 1) * kf)
        summed[g] = inside[rows_of] + carried
        carried = carried + totals[rows_of]
    message[1] = carried[:, :128]
    message[2] = jnp.broadcast_to(hazard_message[0:1, :], (kf, 128))
    message[3] = jnp.broadcast_to(hazard_message[1:2, :], (kf, 128))
    high, low = split_two(jnp.concatenate(summed, axis=0))
    high, low = high.astype(BF16), low.astype(BF16)
    for start in range(0, rows, chunk):
        at = slice(start, start + chunk)
        group = lax.rem(rank[:, at], rows) // LO
        placed = jnp.dot(high, spread[:, at], preferred_element_type=F32) + jnp.dot(
            low, spread[:, at], preferred_element_type=F32
        )
        picked = jnp.zeros((kf, chunk), F32)
        for g in range(groups):
            picked = picked + jnp.where(group == g, placed[g * kf : (g + 1) * kf], 0.0)
        cumulative_out[:, at] = picked


def scans(tangents, risk, rank, squares, hazard_message, rows):
    kf = tangents[0].shape[0]
    groups = rows // LO
    block = jax.ShapeDtypeStruct((kf, rows), F32)
    return pl.pallas_call(
        functools.partial(scan_kernel, rows, kf, len(tangents)),
        in_specs=[VMEM] * (len(tangents) + 4),
        out_shape=[block, block, jax.ShapeDtypeStruct((4, kf, 128), F32)],
        out_specs=[VMEM] * 3,
        scratch_shapes=[pltpu.VMEM((groups * 2 * kf, rows), BF16), pltpu.VMEM((LO, rows), BF16)],
        compiler_params=pltpu.CompilerParams(**PARAMS),
        cost_estimate=pl.CostEstimate(
            flops=4 * rows * LO * groups * 2 * kf, bytes_accessed=rows * kf * 24, transcendentals=0
        ),
        name="scans",
    )(*tangents, risk, rank, squares, hazard_message)


def weight_kernel(ex, *refs):
    messages, (tangent, local, risk, cumulative, squares) = refs[:ex], refs[ex : ex + 5]
    weighted, placed = refs[ex + 5 :]
    me = lax.axis_index("ex")
    for i in range(ex):
        placed[me ^ i] = messages[i][...]
    later = jnp.zeros(placed.shape[2:], F32)
    own_later = later
    before = later
    hazard_before = later
    for b in reversed(range(ex)):
        own_later = own_later + jnp.where(b > me, placed[b, 0], 0.0)
        before = before + jnp.where(b < me, placed[b, 1] + placed[b, 3] * later, 0.0)
        hazard_before = hazard_before + jnp.where(b < me, placed[b, 2], 0.0)
        later = later + placed[b, 0]
    own_later, before = own_later[:, :1], before[:, :1]
    hazard_before = hazard_before[:1, :1]
    value = tangent[...] * (cumulative[...] + hazard_before) - (local[...] + squares[...] * own_later + before)
    weighted[...] = (risk[...] * value).astype(BF16)


def weights(messages, tangent, local, risk, cumulative, squares):
    ex = len(messages)
    return pl.pallas_call(
        functools.partial(weight_kernel, ex),
        in_specs=[VMEM] * (ex + 5),
        out_shape=jax.ShapeDtypeStruct(tangent.shape, BF16),
        out_specs=VMEM,
        scratch_shapes=[pltpu.VMEM((ex,) + messages[0].shape, F32)],
        compiler_params=pltpu.CompilerParams(**PARAMS),
        name="weights",
    )(*messages, tangent, local, risk, cumulative, squares)


def gradient_kernel(feat, ex, kf, *refs):
    parts, dosages, outs = refs[:feat], refs[feat], refs[feat + 1 : feat + 1 + ex]
    weighted, total, turned = refs[feat + 1 + ex :]
    step, steps = pl.program_id(0), pl.num_programs(0)
    me = lax.axis_index("feat")
    place = lax.axis_index("ex")
    chunk = dosages.shape[0]

    @pl.when(step == 0)
    def _():
        total[...] = jnp.zeros_like(total)
        for i in range(feat):
            weighted[pl.ds(pl.multiple_of((me ^ i) * kf, kf), kf), :] = parts[i][...]

    at = pl.ds(pl.multiple_of(step * chunk, chunk), chunk)
    total[...] += jnp.dot(weighted[:, at], dosages[...], preferred_element_type=F32)

    @pl.when(step == steps - 1)
    def _():
        turned[...] = total[...].T.reshape(turned.shape)
        for i in range(ex):
            outs[i][...] = turned[place ^ i]


def gradients(parts, dosages, ex):
    feat = len(parts)
    kf, persons = parts[0].shape
    k, variants = kf * feat, dosages.shape[1]
    chunk = min(512, persons)
    piece = (variants // ex, k)
    return pl.pallas_call(
        functools.partial(gradient_kernel, feat, ex, kf),
        grid=(persons // chunk,),
        in_specs=[pl.BlockSpec((kf, persons), lambda s: (0, 0))] * feat
        + [pl.BlockSpec((chunk, variants), lambda s: (s, 0))],
        out_shape=[jax.ShapeDtypeStruct(piece, F32)] * ex,
        out_specs=[pl.BlockSpec(piece, lambda s: (0, 0))] * ex,
        scratch_shapes=[
            pltpu.VMEM((k, persons), BF16),
            pltpu.VMEM((k, variants), F32),
            pltpu.VMEM((ex,) + piece, F32),
        ],
        compiler_params=pltpu.CompilerParams(**PARAMS),
        cost_estimate=pl.CostEstimate(
            flops=2 * persons * variants * k, bytes_accessed=persons * (variants * 2 + k * 2), transcendentals=0
        ),
        name="gradients",
    )(*parts, dosages)


def place_kernel(ex, *refs):
    parts, out = refs[:ex], refs[ex]
    me = lax.axis_index("ex")
    for i in range(ex):
        out[me ^ i] = parts[i][...]


def place_all(parts):
    ex = len(parts)
    out = pl.pallas_call(
        functools.partial(place_kernel, ex),
        in_specs=[VMEM] * ex,
        out_shape=jax.ShapeDtypeStruct((ex,) + parts[0].shape, F32),
        out_specs=VMEM,
        compiler_params=pltpu.CompilerParams(**PARAMS),
        name="place",
    )(*parts)
    return out.reshape(-1, parts[0].shape[1])


def local(dosages, coefficients, directions, event_rank, events):
    feat, ex = lax.axis_size("feat"), lax.axis_size("ex")
    rows = dosages.shape[0]
    variants, k = directions.shape
    each = k // feat
    padded = -(-each // 16) * 16
    if padded != each:
        directions = jnp.pad(directions.reshape(variants, feat, each), ((0, 0), (0, 0), (0, padded - each)))
        directions = directions.reshape(variants, feat * padded)
    rank, event_row = event_rank[None], events[None]

    linear, keep, send = products(dosages, coefficients, directions, feat)
    linear_parts = [linear] + [swap(linear, "feat", i) for i in range(1, feat)]
    order = list(range(1, feat // 2)) + [0]
    joined = {q: (keep[q], swap(send[q], "feat", 1)) for q in order}
    others = [swap(joined[q][0] + joined[q][1], "feat", 2 * q) for q in order[:-1]]

    risk, sums, ordered_events, message = risks(linear_parts, rank, event_row, rows)
    messages = [message] + [swap(message, "ex", i) for i in range(1, ex)]
    cumulative, squares, ordered_squares, hazard_message, count = hazards(
        messages, sums, ordered_events, rank, rows
    )

    tangent, summed, message = scans(
        list(joined[0]) + others, risk, rank, ordered_squares, hazard_message, rows
    )
    messages = [message] + [swap(message, "ex", i) for i in range(1, ex)]
    own = weights(messages, tangent, summed, risk, cumulative, squares)

    chips = {0: own}
    for q in order[:-1]:
        chips[q] = swap(own, "feat", 2 * q)
    parts = []
    for q in range(feat // 2):
        parts += [chips[q], swap(chips[q], "feat", 1)]

    pieces = gradients(parts, dosages, ex)
    total = pieces[0]
    for i in range(1, ex):
        total = total + swap(pieces[i], "ex", i)
    total = total / count[0, 0]
    result = place_all([total] + [swap(total, "ex", i) for i in range(1, ex)])
    if padded != each:
        result = result.reshape(variants, feat, padded)[:, :, :each].reshape(variants, k)
    return result


def solution(mesh):
    placed = (P("ex", "feat"), P("feat"), P("feat", None), P("ex"), P("ex"))
    return jax.shard_map(
        local, mesh=mesh, in_specs=placed, out_specs=P("feat", None), check_vma=False
    )
```

time: 329 us -> 108 us (0.33)
  local copies, waits for them, and re-layouts: 177 us -> 2.11 us
  blocking collectives: 63.8 us -> 0 us
  starting transfers between devices: 0.04 us -> 39.4 us
  Pallas kernels: 0 us -> 19.2 us
  matrix products: 18.6 us -> 0 us
  other arithmetic: 17.4 us -> 0.75 us
  between operations: 13.6 us -> 0.14 us
  waiting for transfers between devices: 35.8 us -> 46.3 us
    gather x9 -> x0, local copies, waits for them, and re-layouts: 152 us -> none  [the longest x5 77.4 us: ordered_sums(): return jnp.take(summed, local_rank, axis=1)]
    ppermute x0 -> x33, waiting for transfers between devices: none -> 46.3 us  [swap(): return lax.ppermute(x, axis, [(s, s ^ i) for s in range(count)])]
    ppermute x0 -> x33, starting transfers between devices: none -> 39.4 us  [swap(): return lax.ppermute(x, axis, [(s, s ^ i) for s in range(count)])]
    psum x2 -> x0, waiting for transfers between devices: 35.8 us -> none  [the longest x1 35.7 us: local(): total = lax.psum(partial_sum, 'ex')]
    psum x1 -> x0, blocking collectives: 26 us -> none  [local(): tangent, linear = lax.psum((tangent_part, linear_part), 'feat')]
    unnamed x2 -> x0, blocking collectives: 22.2 us -> none
    pallas_call x0 -> x7, Pallas kernels: none -> 19.2 us  [the longest x1 6.24 us: products(): pl.pallas_call(functools.partial(product_kernel, feat, kf), grid=(persons...]
    dot_general x7 -> x0, matrix products: 18.6 us -> none  [the longest x4 5.9 us: ordered_sums(): jnp.einsum('knt,ts->kns', placed, member, precision=lax.Precision.HIGHEST)]
  transfers between devices with their start and end apart: 2 -> 33, of which waited for: 1 -> 22; matrix products, arithmetic and copies ran while one was open for 21% -> 1% of each run, Pallas kernels for 0% -> 3%
where the time goes in v1:
time: 108 us
  waiting for transfers between devices  46.3 us (43%)
  starting transfers between devices  39.4 us (36%)
  Pallas kernels  19.2 us (18%)
  local copies, waits for them, and re-layouts  2.11 us (2%)
    ppermute x33, waiting for transfers between devices, swap(): return lax.ppermute(x, axis, [(s, s ^ i) for s in range(count)])  46.3 us
    ppermute x33, starting transfers between devices, swap(): return lax.ppermute(x, axis, [(s, s ^ i) for s in range(count)])  39.4 us
    pallas_call x1, Pallas kernels, products(): pl.pallas_call(functools.partial(product_kernel, feat, kf), grid=(persons...  6.24 us
    pallas_call x1, Pallas kernels, scans(): pl.pallas_call(functools.partial(scan_kernel, rows, kf, len(tangents)), i...  6.23 us
    pallas_call x1, Pallas kernels, gradients(): pl.pallas_call(functools.partial(gradient_kernel, feat, ex, kf), grid=(pe...  2.26 us
  transfers between devices with their start and end apart: 33, of which 22 were waited for; matrix products, arithmetic and copies ran while one was open for 1% of the time, Pallas kernels for 3%

profile of v1, /device:TPU:0, one launch (start us, length us, event | category | flops | bytes accessed | tf_op | source)
XLA Modules:
  0.0 108.0 jit_solution(6441811592937831580)
XLA Ops:
  1.6 6.2 %products.1 = (f32[1,4096]{1,0:T(1,128)S(1)}, f32[16,4096]{1,0:T(8,128)S(1)}, f32[16,4096]{1,0:T(8,128)S(1)}, f32[16,4096]{1,0:T(8,128)S(1)}, f32[16,4096]{1,0:T...) custom-call(bf16[512,128]{1,0:T(8,128)(2,1)S(1)} %copy-done.1, ...), custom_call_target="tpu_custom_call" | custom-call | flops 536870912 | bytes 6291456 | tf_op jit(solution)/shard_map/products/pallas_call | solution.py:75
  9.5 2.9 %collective-permute-start.2 = (f32[16,4096]{1,0:T(8,128)S(1)}, f32[16,4096]{1,0:T(8,128)S(1)}, u32[]{:S(2)}, u32[]{:S(2)}) collective-permute-start(f32[16,4096]{1,0:T(8,128)S(1)} %add.18), channel_id=1, source_target_pairs={{0,2},{1,3},{2,0},{3,1},{4,6},{5,7},{6,4},{7,5},{8,10},{9,11},{10,... | collective-permute-start | bytes 786440 | tf_op jit(solution)/shard_map/ppermute | solution.py:21
  17.3 7.7 %collective-permute-done.8.refs_2_ = f32[1,4096]{1,0:T(1,128)S(1)} collective-permute-done((f32[1,4096]{1,0:T(1,128)S(1)}, f32[1,4096]{1,0:T(1,128)S(1)}, u32[]{:S(2)}, u32[]{:S(2)}) %collective-permute-start.8) | collective-permute-done | bytes 16416 | tf_op jit(solution)/shard_map/ppermute | solution.py:21
  25.7 2.5 %collective-permute-done.9.refs_3_ = f32[1,4096]{1,0:T(1,128)S(1)} collective-permute-done((f32[1,4096]{1,0:T(1,128)S(1)}, f32[1,4096]{1,0:T(1,128)S(1)}, u32[]{:S(2)}, u32[]{:S(2)}) %collective-permute-start.9) | collective-permute-done | bytes 16416 | tf_op jit(solution)/shard_map/ppermute | solution.py:21
  28.2 1.9 %collective-permute-start.10 = (f32[1,4096]{1,0:T(1,128)S(1)}, f32[1,4096]{1,0:T(1,128)S(1)}, u32[]{:S(2)}, u32[]{:S(2)}) collective-permute-start(f32[1,4096]{1,0:T(1,128)S(1)} %get-tuple-element.38.refs_0_), channel_id=1, source_target_pairs={{0,4},{1,5},{2,6},{3,7},{4,0},{5,1},{6,2},{7,3},{8,12},{9,13},{10,... | collective-permute-start | bytes 49160 | tf_op jit(solution)/shard_map/ppermute | solution.py:21
  30.2 1.8 %collective-permute-done.10.refs_4_ = f32[1,4096]{1,0:T(1,128)S(1)} collective-permute-done((f32[1,4096]{1,0:T(1,128)S(1)}, f32[1,4096]{1,0:T(1,128)S(1)}, u32[]{:S(2)}, u32[]{:S(2)}) %collective-permute-start.10) | collective-permute-done | bytes 16416 | tf_op jit(solution)/shard_map/ppermute | solution.py:21
  32.5 2.7 %collective-permute-done.11.refs_5_ = f32[1,4096]{1,0:T(1,128)S(1)} collective-permute-done((f32[1,4096]{1,0:T(1,128)S(1)}, f32[1,4096]{1,0:T(1,128)S(1)}, u32[]{:S(2)}, u32[]{:S(2)}) %collective-permute-start.11) | collective-permute-done | bytes 16416 | tf_op jit(solution)/shard_map/ppermute | solution.py:21
  35.2 2.6 %collective-permute-start.12 = (f32[1,4096]{1,0:T(1,128)S(1)}, f32[1,4096]{1,0:T(1,128)S(1)}, u32[]{:S(2)}, u32[]{:S(2)}) collective-permute-start(f32[1,4096]{1,0:T(1,128)S(1)} %get-tuple-element.38.refs_0_), channel_id=1, source_target_pairs={{0,6},{1,7},{2,4},{3,5},{4,2},{5,3},{6,0},{7,1},{8,14},{9,15},{10,... | collective-permute-start | bytes 49160 | tf_op jit(solution)/shard_map/ppermute | solution.py:21
  37.8 2.0 %collective-permute-done.12.refs_6_ = f32[1,4096]{1,0:T(1,128)S(1)} collective-permute-done((f32[1,4096]{1,0:T(1,128)S(1)}, f32[1,4096]{1,0:T(1,128)S(1)}, u32[]{:S(2)}, u32[]{:S(2)}) %collective-permute-start.12) | collective-permute-done | bytes 16416 | tf_op jit(solution)/shard_map/ppermute | solution.py:21
  39.8 4.0 %collective-permute-done.13.refs_7_ = f32[1,4096]{1,0:T(1,128)S(1)} collective-permute-done((f32[1,4096]{1,0:T(1,128)S(1)}, f32[1,4096]{1,0:T(1,128)S(1)}, u32[]{:S(2)}, u32[]{:S(2)}) %collective-permute-start.13) | collective-permute-done | bytes 16416 | tf_op jit(solution)/shard_map/ppermute | solution.py:21
  45.4 2.1 %collective-permute-start.14 = (f32[8,128]{1,0:T(8,128)S(1)}, f32[8,128]{1,0:T(8,128)S(1)}, u32[]{:S(2)}, u32[]{:S(2)}) collective-permute-start(f32[8,128]{1,0:T(8,128)S(1)} %get-tuple-element.40.refs_0_), channel_id=1, source_target_pairs={{0,8},{8,0},{16,24},{24,16},{1,9},{9,1},{17,25},{25,17},{2,10},{10... | collective-permute-start | bytes 12296 | tf_op jit(solution)/shard_map/ppermute | solution.py:21
  49.1 3.0 %collective-permute-start.15 = (f32[8,128]{1,0:T(8,128)S(1)}, f32[8,128]{1,0:T(8,128)S(1)}, u32[]{:S(2)}, u32[]{:S(2)}) collective-permute-start(f32[8,128]{1,0:T(8,128)S(1)} %get-tuple-element.40.refs_0_), channel_id=1, source_target_pairs={{0,16},{8,24},{16,0},{24,8},{1,17},{9,25},{17,1},{25,9},{2,18},{10... | collective-permute-start | bytes 12296 | tf_op jit(solution)/shard_map/ppermute | solution.py:21
  53.7 3.9 %collective-permute-start.16 = (f32[8,128]{1,0:T(8,128)S(1)}, f32[8,128]{1,0:T(8,128)S(1)}, u32[]{:S(2)}, u32[]{:S(2)}) collective-permute-start(f32[8,128]{1,0:T(8,128)S(1)} %get-tuple-element.40.refs_0_), channel_id=1, source_target_pairs={{0,24},{8,16},{16,8},{24,0},{1,25},{9,17},{17,9},{25,1},{2,26},{10... | collective-permute-start | bytes 12296 | tf_op jit(solution)/shard_map/ppermute | solution.py:21
  59.2 2.1 %hazards.1 = (f32[1,4096]{1,0:T(1,128)S(1)}, f32[1,4096]{1,0:T(1,128)S(1)}, f32[16,256]{1,0:T(8,128)S(1)}, f32[8,128]{1,0:T(8,128)S(1)}, f32[8,128]{1,0:T(8,128)S(1)}) custom-call(f32[8,128]{1,0:T(8,128)S(1)} %get-tuple-element.40.refs_0_, f32[8,128]{1,0:T(8,128)S(1)} %collective-permute-done.14.refs_1_, f32[8,128]{1,0:T(8,128)S(1)} %collective-permute-done.15.refs_2_, ...), custom_call_target="tpu_custom_call" | custom-call | flops 209715200 | bytes 262144 | tf_op jit(solution)/shard_map/hazards/pallas_call | solution.py:187
  61.4 6.2 %scans.1 = (f32[16,4096]{1,0:T(8,128)S(1)}, f32[16,4096]{1,0:T(8,128)S(1)}, f32[4,16,128]{2,1,0:T(8,128)S(1)}) custom-call(f32[16,4096]{1,0:T(8,128)S(1)} %get-tuple-element.30.refs_0_, f32[16,4096]{1,0:T(8,128)S(1)} %collective-permute-done.refs_1_, f32[16,4096]{1,0:T(8,128)S(1)} %collective-permute-done.2.refs_2_, ...), custom_call_target="tpu_custom_call" | custom-call | flops 2147483648 | bytes 1572864 | tf_op jit(solution)/shard_map/scans/pallas_call | solution.py:266
  67.7 4.4 %collective-permute-start.18 = (f32[4,16,128]{2,1,0:T(8,128)S(1)}, f32[4,16,128]{2,1,0:T(8,128)S(1)}, u32[]{:S(2)}, u32[]{:S(2)}) collective-permute-start(f32[4,16,128]{2,1,0:T(8,128)S(1)} %get-tuple-element.45.refs_0_), channel_id=1, source_target_pairs={{0,16},{8,24},{16,0},{24,8},{1,17},{9,25},{17,1},{25,9},{2,18},{10... | collective-permute-start | bytes 98312 | tf_op jit(solution)/shard_map/ppermute | solution.py:21
  72.1 2.2 %collective-permute-done.18.refs_2_ = f32[4,16,128]{2,1,0:T(8,128)S(1)} collective-permute-done((f32[4,16,128]{2,1,0:T(8,128)S(1)}, f32[4,16,128]{2,1,0:T(8,128)S(1)}, u32[]{:S(2)}, u32[]{:S(2)}) %collective-permute-start.18) | collective-permute-done | bytes 32800 | tf_op jit(solution)/shard_map/ppermute | solution.py:21
  74.3 3.5 %collective-permute-done.19.refs_3_ = f32[4,16,128]{2,1,0:T(8,128)S(1)} collective-permute-done((f32[4,16,128]{2,1,0:T(8,128)S(1)}, f32[4,16,128]{2,1,0:T(8,128)S(1)}, u32[]{:S(2)}, u32[]{:S(2)}) %collective-permute-start.19) | collective-permute-done | bytes 32800 | tf_op jit(solution)/shard_map/ppermute | solution.py:21
  84.4 2.2 %collective-permute-done.25.refs_6_ = bf16[16,4096]{1,0:T(8,128)(2,1)S(1)} collective-permute-done((bf16[16,4096]{1,0:T(8,128)(2,1)S(1)}, bf16[16,4096]{1,0:T(8,128)(2,1)S(1)}, u32[]{:S(2)}, u32[]{:S(2)}) %collective-permute-start.25) | collective-permute-done | bytes 131104 | tf_op jit(solution)/shard_map/ppermute | solution.py:21
  88.0 2.3 %gradients.1 = (f32[128,128]{1,0:T(8,128)S(1)}, f32[128,128]{1,0:T(8,128)S(1)}, f32[128,128]{1,0:T(8,128)S(1)}, f32[128,128]{1,0:T(8,128)S(1)}) custom-call(bf16[16,4096]{1,0:T(8,128)(2,1)S(1)} %weights.1.refs_0_, bf16[16,4096]{1,0:T(8,128)(2,1)S(1)} %collective-permute-done.20.refs_1_, bf16[16,4096]{1,0:T(8,128)(2,1)S(1)} %collective-permute-done.21.refs_2_, ...), custom_call_target="tpu_custom_call" | custom-call | flops 536870912 | bytes 5242880 | tf_op jit(solution)/shard_map/gradients/pallas_call | solution.py:344
  90.7 4.0 %collective-permute-start.27 = (f32[128,128]{1,0:T(8,128)S(1)}, f32[128,128]{1,0:T(8,128)S(1)}, u32[]{:S(2)}, u32[]{:S(2)}) collective-permute-start(f32[128,128]{1,0:T(8,128)S(1)} %get-tuple-element.51), channel_id=1, source_target_pairs={{0,8},{8,0},{16,24},{24,16},{1,9},{9,1},{17,25},{25,17},{2,10},{10... | collective-permute-start | bytes 196616 | tf_op jit(solution)/shard_map/ppermute | solution.py:21
  95.2 1.9 %collective-permute-done.29 = f32[128,128]{1,0:T(8,128)S(1)} collective-permute-done((f32[128,128]{1,0:T(8,128)S(1)}, f32[128,128]{1,0:T(8,128)S(1)}, u32[]{:S(2)}, u32[]{:S(2)}) %collective-permute-start.29) | collective-permute-done | bytes 65568 | tf_op jit(solution)/shard_map/ppermute | solution.py:21
  101.1 2.4 %collective-permute-start.32 = (f32[128,128]{1,0:T(8,128)S(1)}, f32[128,128]{1,0:T(8,128)S(1)}, u32[]{:S(2)}, u32[]{:S(2)}) collective-permute-start(f32[128,128]{1,0:T(8,128)S(1)} %add_divide_fusion.refs_0_), channel_id=1, source_target_pairs={{0,24},{8,16},{16,8},{24,0},{1,25},{9,17},{17,9},{25,1},{2,26},{10... | collective-permute-start | bytes 196616 | tf_op jit(solution)/shard_map/ppermute | solution.py:21
  103.6 3.6 %collective-permute-done.31.refs_2_ = f32[128,128]{1,0:T(8,128)S(1)} collective-permute-done((f32[128,128]{1,0:T(8,128)S(1)}, f32[128,128]{1,0:T(8,128)S(1)}, u32[]{:S(2)}, u32[]{:S(2)}) %collective-permute-start.31) | collective-permute-done | bytes 65568 | tf_op jit(solution)/shard_map/ppermute | solution.py:21
  (63 shorter events, 29.5 us)
Async XLA Ops:
  8.3 4.1 %collective-permute-start.3 = (f32[16,4096]{1,0:T(8,128)S(1)}, f32[16,4096]{1,0:T(8,128)S(1)}, u32[]{:S(2)}, u32[]{:S(2)}) collective-permute-start(f32[16,4096]{1,0:T(8,128)S(1)} %get-tuple-element.35), channel_id=1, source_target_pairs={{0,1},{1,0},{2,3},{3,2},{4,5},{5,4},{6,7},{7,6},{8,9},{9,8},{10,11... | collective-permute-start | bytes 786440 | tf_op jit(solution)/shard_map/ppermute | solution.py:21
  8.4 5.7 %collective-permute-start.5 = (f32[16,4096]{1,0:T(8,128)S(1)}, f32[16,4096]{1,0:T(8,128)S(1)}, u32[]{:S(2)}, u32[]{:S(2)}) collective-permute-start(f32[16,4096]{1,0:T(8,128)S(1)} %get-tuple-element.37), channel_id=1, source_target_pairs={{0,1},{1,0},{2,3},{3,2},{4,5},{5,4},{6,7},{7,6},{8,9},{9,8},{10,11... | collective-permute-start | bytes 786440 | tf_op jit(solution)/shard_map/ppermute | solution.py:21
  8.9 52.5 %collective-permute-start = (f32[16,4096]{1,0:T(8,128)S(1)}, f32[16,4096]{1,0:T(8,128)S(1)}, u32[]{:S(2)}, u32[]{:S(2)}) collective-permute-start(f32[16,4096]{1,0:T(8,128)S(1)} %get-tuple-element.31), channel_id=1, source_target_pairs={{0,1},{1,0},{2,3},{3,2},{4,5},{5,4},{6,7},{7,6},{8,9},{9,8},{10,11... | collective-permute-start | bytes 786440 | tf_op jit(solution)/shard_map/ppermute | solution.py:21
  9.5 51.8 %collective-permute-start.2 = (f32[16,4096]{1,0:T(8,128)S(1)}, f32[16,4096]{1,0:T(8,128)S(1)}, u32[]{:S(2)}, u32[]{:S(2)}) collective-permute-start(f32[16,4096]{1,0:T(8,128)S(1)} %add.18), channel_id=1, source_target_pairs={{0,2},{1,3},{2,0},{3,1},{4,6},{5,7},{6,4},{7,5},{8,10},{9,11},{10,... | collective-permute-start | bytes 786440 | tf_op jit(solution)/shard_map/ppermute | solution.py:21
  12.5 48.8 %collective-permute-start.4 = (f32[16,4096]{1,0:T(8,128)S(1)}, f32[16,4096]{1,0:T(8,128)S(1)}, u32[]{:S(2)}, u32[]{:S(2)}) collective-permute-start(f32[16,4096]{1,0:T(8,128)S(1)} %add.19), channel_id=1, source_target_pairs={{0,4},{1,5},{2,6},{3,7},{4,0},{5,1},{6,2},{7,3},{8,12},{9,13},{10,... | collective-permute-start | bytes 786440 | tf_op jit(solution)/shard_map/ppermute | solution.py:21
  14.1 47.2 %collective-permute-start.6 = (f32[16,4096]{1,0:T(8,128)S(1)}, f32[16,4096]{1,0:T(8,128)S(1)}, u32[]{:S(2)}, u32[]{:S(2)}) collective-permute-start(f32[16,4096]{1,0:T(8,128)S(1)} %add.20), channel_id=1, source_target_pairs={{0,6},{1,7},{2,4},{3,5},{4,2},{5,3},{6,0},{7,1},{8,14},{9,15},{10,... | collective-permute-start | bytes 786440 | tf_op jit(solution)/shard_map/ppermute | solution.py:21
  15.6 9.5 %collective-permute-start.8 = (f32[1,4096]{1,0:T(1,128)S(1)}, f32[1,4096]{1,0:T(1,128)S(1)}, u32[]{:S(2)}, u32[]{:S(2)}) collective-permute-start(f32[1,4096]{1,0:T(1,128)S(1)} %get-tuple-element.38.refs_0_), channel_id=1, source_target_pairs={{0,2},{1,3},{2,0},{3,1},{4,6},{5,7},{6,4},{7,5},{8,10},{9,11},{10,... | collective-permute-start | bytes 49160 | tf_op jit(solution)/shard_map/ppermute | solution.py:21
  35.2 4.6 %collective-permute-start.12 = (f32[1,4096]{1,0:T(1,128)S(1)}, f32[1,4096]{1,0:T(1,128)S(1)}, u32[]{:S(2)}, u32[]{:S(2)}) collective-permute-start(f32[1,4096]{1,0:T(1,128)S(1)} %get-tuple-element.38.refs_0_), channel_id=1, source_target_pairs={{0,6},{1,7},{2,4},{3,5},{4,2},{5,3},{6,0},{7,1},{8,14},{9,15},{10,... | collective-permute-start | bytes 49160 | tf_op jit(solution)/shard_map/ppermute | solution.py:21
  39.8 4.1 %collective-permute-start.13 = (f32[1,4096]{1,0:T(1,128)S(1)}, f32[1,4096]{1,0:T(1,128)S(1)}, u32[]{:S(2)}, u32[]{:S(2)}) collective-permute-start(f32[1,4096]{1,0:T(1,128)S(1)} %get-tuple-element.38.refs_0_), channel_id=1, source_target_pairs={{0,7},{1,6},{2,5},{3,4},{4,3},{5,2},{6,1},{7,0},{8,15},{9,14},{10,... | collective-permute-start | bytes 49160 | tf_op jit(solution)/shard_map/ppermute | solution.py:21
  49.1 4.6 %collective-permute-start.15 = (f32[8,128]{1,0:T(8,128)S(1)}, f32[8,128]{1,0:T(8,128)S(1)}, u32[]{:S(2)}, u32[]{:S(2)}) collective-permute-start(f32[8,128]{1,0:T(8,128)S(1)} %get-tuple-element.40.refs_0_), channel_id=1, source_target_pairs={{0,16},{8,24},{16,0},{24,8},{1,17},{9,25},{17,1},{25,9},{2,18},{10... | collective-permute-start | bytes 12296 | tf_op jit(solution)/shard_map/ppermute | solution.py:21
  53.7 5.5 %collective-permute-start.16 = (f32[8,128]{1,0:T(8,128)S(1)}, f32[8,128]{1,0:T(8,128)S(1)}, u32[]{:S(2)}, u32[]{:S(2)}) collective-permute-start(f32[8,128]{1,0:T(8,128)S(1)} %get-tuple-element.40.refs_0_), channel_id=1, source_target_pairs={{0,24},{8,16},{16,8},{24,0},{1,25},{9,17},{17,9},{25,1},{2,26},{10... | collective-permute-start | bytes 12296 | tf_op jit(solution)/shard_map/ppermute | solution.py:21
  67.6 4.5 %collective-permute-start.17 = (f32[4,16,128]{2,1,0:T(8,128)S(1)}, f32[4,16,128]{2,1,0:T(8,128)S(1)}, u32[]{:S(2)}, u32[]{:S(2)}) collective-permute-start(f32[4,16,128]{2,1,0:T(8,128)S(1)} %get-tuple-element.45.refs_0_), channel_id=1, source_target_pairs={{0,8},{8,0},{16,24},{24,16},{1,9},{9,1},{17,25},{25,17},{2,10},{10... | collective-permute-start | bytes 98312 | tf_op jit(solution)/shard_map/ppermute | solution.py:21
  67.7 6.6 %collective-permute-start.18 = (f32[4,16,128]{2,1,0:T(8,128)S(1)}, f32[4,16,128]{2,1,0:T(8,128)S(1)}, u32[]{:S(2)}, u32[]{:S(2)}) collective-permute-start(f32[4,16,128]{2,1,0:T(8,128)S(1)} %get-tuple-element.45.refs_0_), channel_id=1, source_target_pairs={{0,16},{8,24},{16,0},{24,8},{1,17},{9,25},{17,1},{25,9},{2,18},{10... | collective-permute-start | bytes 98312 | tf_op jit(solution)/shard_map/ppermute | solution.py:21
  72.0 5.7 %collective-permute-start.19 = (f32[4,16,128]{2,1,0:T(8,128)S(1)}, f32[4,16,128]{2,1,0:T(8,128)S(1)}, u32[]{:S(2)}, u32[]{:S(2)}) collective-permute-start(f32[4,16,128]{2,1,0:T(8,128)S(1)} %get-tuple-element.45.refs_0_), channel_id=1, source_target_pairs={{0,24},{8,16},{16,8},{24,0},{1,25},{9,17},{17,9},{25,1},{2,26},{10... | collective-permute-start | bytes 98312 | tf_op jit(solution)/shard_map/ppermute | solution.py:21
  78.0 5.0 %collective-permute-start.21 = (bf16[16,4096]{1,0:T(8,128)(2,1)S(1)}, bf16[16,4096]{1,0:T(8,128)(2,1)S(1)}, u32[]{:S(2)}, u32[]{:S(2)}) collective-permute-start(bf16[16,4096]{1,0:T(8,128)(2,1)S(1)} %weights.1.refs_0_), channel_id=1, source_target_pairs={{0,2},{1,3},{2,0},{3,1},{4,6},{5,7},{6,4},{7,5},{8,10},{9,11},{10,... | collective-permute-start | bytes 393224 | tf_op jit(solution)/shard_map/ppermute | solution.py:21
  79.4 5.0 %collective-permute-start.23 = (bf16[16,4096]{1,0:T(8,128)(2,1)S(1)}, bf16[16,4096]{1,0:T(8,128)(2,1)S(1)}, u32[]{:S(2)}, u32[]{:S(2)}) collective-permute-start(bf16[16,4096]{1,0:T(8,128)(2,1)S(1)} %weights.1.refs_0_), channel_id=1, source_target_pairs={{0,4},{1,5},{2,6},{3,7},{4,0},{5,1},{6,2},{7,3},{8,12},{9,13},{10,... | collective-permute-start | bytes 393224 | tf_op jit(solution)/shard_map/ppermute | solution.py:21
  80.8 5.9 %collective-permute-start.25 = (bf16[16,4096]{1,0:T(8,128)(2,1)S(1)}, bf16[16,4096]{1,0:T(8,128)(2,1)S(1)}, u32[]{:S(2)}, u32[]{:S(2)}) collective-permute-start(bf16[16,4096]{1,0:T(8,128)(2,1)S(1)} %weights.1.refs_0_), channel_id=1, source_target_pairs={{0,6},{1,7},{2,4},{3,5},{4,2},{5,3},{6,0},{7,1},{8,14},{9,15},{10,... | collective-permute-start | bytes 393224 | tf_op jit(solution)/shard_map/ppermute | solution.py:21
  81.5 5.1 %collective-permute-start.20 = (bf16[16,4096]{1,0:T(8,128)(2,1)S(1)}, bf16[16,4096]{1,0:T(8,128)(2,1)S(1)}, u32[]{:S(2)}, u32[]{:S(2)}) collective-permute-start(bf16[16,4096]{1,0:T(8,128)(2,1)S(1)} %weights.1.refs_0_), channel_id=1, source_target_pairs={{0,1},{1,0},{2,3},{3,2},{4,5},{5,4},{6,7},{7,6},{8,9},{9,8},{10,11... | collective-permute-start | bytes 393224 | tf_op jit(solution)/shard_map/ppermute | solution.py:21
  90.2 6.8 %collective-permute-start.29 = (f32[128,128]{1,0:T(8,128)S(1)}, f32[128,128]{1,0:T(8,128)S(1)}, u32[]{:S(2)}, u32[]{:S(2)}) collective-permute-start(f32[128,128]{1,0:T(8,128)S(1)} %get-tuple-element.53), channel_id=1, source_target_pairs={{0,24},{8,16},{16,8},{24,0},{1,25},{9,17},{17,9},{25,1},{2,26},{10... | collective-permute-start | bytes 196616 | tf_op jit(solution)/shard_map/ppermute | solution.py:21
  90.7 7.6 %collective-permute-start.28 = (f32[128,128]{1,0:T(8,128)S(1)}, f32[128,128]{1,0:T(8,128)S(1)}, u32[]{:S(2)}, u32[]{:S(2)}) collective-permute-start(f32[128,128]{1,0:T(8,128)S(1)} %get-tuple-element.52), channel_id=1, source_target_pairs={{0,16},{8,24},{16,0},{24,8},{1,17},{9,25},{17,1},{25,9},{2,18},{10... | collective-permute-start | bytes 196616 | tf_op jit(solution)/shard_map/ppermute | solution.py:21
  90.7 7.7 %collective-permute-start.27 = (f32[128,128]{1,0:T(8,128)S(1)}, f32[128,128]{1,0:T(8,128)S(1)}, u32[]{:S(2)}, u32[]{:S(2)}) collective-permute-start(f32[128,128]{1,0:T(8,128)S(1)} %get-tuple-element.51), channel_id=1, source_target_pairs={{0,8},{8,0},{16,24},{24,16},{1,9},{9,1},{17,25},{25,17},{2,10},{10... | collective-permute-start | bytes 196616 | tf_op jit(solution)/shard_map/ppermute | solution.py:21
  99.0 4.6 %collective-permute-start.30 = (f32[128,128]{1,0:T(8,128)S(1)}, f32[128,128]{1,0:T(8,128)S(1)}, u32[]{:S(2)}, u32[]{:S(2)}) collective-permute-start(f32[128,128]{1,0:T(8,128)S(1)} %add_divide_fusion.refs_0_), channel_id=1, source_target_pairs={{0,8},{8,0},{16,24},{24,16},{1,9},{9,1},{17,25},{25,17},{2,10},{10... | collective-permute-start | bytes 196616 | tf_op jit(solution)/shard_map/ppermute | solution.py:21
  99.7 7.5 %collective-permute-start.31 = (f32[128,128]{1,0:T(8,128)S(1)}, f32[128,128]{1,0:T(8,128)S(1)}, u32[]{:S(2)}, u32[]{:S(2)}) collective-permute-start(f32[128,128]{1,0:T(8,128)S(1)} %add_divide_fusion.refs_0_), channel_id=1, source_target_pairs={{0,16},{8,24},{16,0},{24,8},{1,17},{9,25},{17,1},{25,9},{2,18},{10... | collective-permute-start | bytes 196616 | tf_op jit(solution)/shard_map/ppermute | solution.py:21
  101.1 6.1 %collective-permute-start.32 = (f32[128,128]{1,0:T(8,128)S(1)}, f32[128,128]{1,0:T(8,128)S(1)}, u32[]{:S(2)}, u32[]{:S(2)}) collective-permute-start(f32[128,128]{1,0:T(8,128)S(1)} %add_divide_fusion.refs_0_), channel_id=1, source_target_pairs={{0,24},{8,16},{16,8},{24,0},{1,25},{9,17},{17,9},{25,1},{2,26},{10... | collective-permute-start | bytes 196616 | tf_op jit(solution)/shard_map/ppermute | solution.py:21
  (13 other events, 136.0 us)

commit v2 on v1

v2 whole, which is shorter than its diff:
```python
import functools

import jax
import jax.numpy as jnp
from jax import lax
from jax.experimental import pallas as pl
from jax.experimental.pallas import tpu as pltpu
from jax.sharding import PartitionSpec as P

F32 = jnp.float32
BF16 = jnp.bfloat16
LO = 256
NT = (((1,), (1,)), ((), ()))
VMEM = pl.BlockSpec(memory_space=pltpu.VMEM)
HIGHEST = lax.Precision.HIGHEST
PARAMS = dict(vmem_limit_bytes=48 * 1024 * 1024)


def swap(x, axis, i):
    count = lax.axis_size(axis)
    return lax.ppermute(x, axis, [(s, s ^ i) for s in range(count)])


def exchange(x, axis):
    return lax.all_to_all(x, axis, 0, 0)


def split_two(x):
    high = x.astype(BF16).astype(F32)
    return high, x - high


def split_three(x):
    first, rest = split_two(x)
    second, third = split_two(rest)
    return first, second, third


def one_hot(values, count, kind=BF16):
    shape = (count, values.shape[1])
    return jnp.where(lax.broadcasted_iota(jnp.int32, shape, 0) == values, 1.0, 0.0).astype(kind)


def triangle(n, keep):
    first = lax.broadcasted_iota(jnp.int32, (n, n), 0)
    second = lax.broadcasted_iota(jnp.int32, (n, n), 1)
    return jnp.where(keep(first, second), 1.0, 0.0)


def exact_dot(a, b):
    return jnp.dot(a, b, precision=HIGHEST, preferred_element_type=F32)


def dot_binary(a, b):
    b = b.astype(BF16)
    total = None
    for part in split_three(a):
        term = jnp.dot(part.astype(BF16), b, preferred_element_type=F32)
        total = term if total is None else total + term
    return total


def product_kernel(feat, kf, directions, coefficients, dosages, *refs):
    linear, keep, send = refs[0], refs[1 : 1 + feat // 2], refs[1 + feat // 2 : 1 + feat]
    rhs, turned = refs[1 + feat :]
    me = lax.axis_index("feat")
    width = feat * kf
    variants = rhs.shape[0]

    @pl.when(pl.program_id(0) == 0)
    def _():
        rhs[:, :width] = directions[...]
        spread = jnp.broadcast_to(coefficients[...].astype(F32), (128, variants)).T
        rhs[:, width:] = spread.astype(BF16)

    result = jnp.dot(dosages[...], rhs[...], preferred_element_type=F32)
    turned[...] = result[:, :width].T.reshape(turned.shape)
    for i in range(feat):
        (send if i % 2 else keep)[i // 2][...] = turned[me ^ i]
    diagonal = triangle(128, lambda a, b: a == b)
    for start in range(0, dosages.shape[0], 128):
        block = result[start : start + 128, width:]
        row = jnp.sum(block * diagonal, axis=0, keepdims=True)
        linear[:, :, start : start + 128] = jnp.broadcast_to(row[None], (feat, 1, 128))


def products(dosages, coefficients, directions, feat):
    persons, variants = dosages.shape
    k = directions.shape[1]
    kf = k // feat
    chunk = min(512, persons)
    piece = jax.ShapeDtypeStruct((kf, persons), F32)
    out = pl.pallas_call(
        functools.partial(product_kernel, feat, kf),
        grid=(persons // chunk,),
        in_specs=[
            pl.BlockSpec((variants, k), lambda s: (0, 0)),
            pl.BlockSpec((1, variants), lambda s: (0, 0)),
            pl.BlockSpec((chunk, variants), lambda s: (s, 0)),
        ],
        out_shape=[jax.ShapeDtypeStruct((feat, 1, persons), F32)] + [piece] * feat,
        out_specs=[pl.BlockSpec((feat, 1, chunk), lambda s: (0, 0, s))]
        + [pl.BlockSpec((kf, chunk), lambda s: (0, s))] * feat,
        scratch_shapes=[
            pltpu.VMEM((variants, k + 128), BF16),
            pltpu.VMEM((feat, kf, chunk), F32),
        ],
        compiler_params=pltpu.CompilerParams(**PARAMS),
        cost_estimate=pl.CostEstimate(
            flops=2 * persons * variants * k, bytes_accessed=persons * (variants * 2 + k * 4), transcendentals=0
        ),
        name="products",
    )(directions, coefficients[None], dosages)
    return out[0], out[1 : 1 + feat // 2], out[1 + feat // 2 :]


def risk_kernel(rows, linear, rank, events, risk_out, sums_out, events_out, message):
    groups = rows // LO
    total = linear[0]
    for i in range(1, linear.shape[0]):
        total = total + linear[i]
    risk = jnp.exp(total)
    risk_out[...] = risk
    place = lax.rem(rank[...], rows)
    mask = one_hot(place // LO, groups, F32)
    pieces = [mask * part for part in split_three(risk)] + [mask * events[...].astype(F32)]
    lhs = jnp.concatenate(pieces, axis=0).astype(BF16)
    sorted_all = lax.dot_general(lhs, one_hot(lax.rem(place, LO), LO), NT, preferred_element_type=F32)
    ordered = sorted_all[:groups] + sorted_all[groups : 2 * groups] + sorted_all[2 * groups : 3 * groups]
    happened = sorted_all[3 * groups :]
    inside = dot_binary(ordered, triangle(LO, lambda a, b: a >= b))
    totals = jnp.broadcast_to(inside[:, :1], inside.shape)
    carried = exact_dot(triangle(groups, lambda a, b: a < b), totals)
    sums_out[...] = inside + carried
    events_out[...] = happened
    everything = jnp.sum(totals, axis=0, keepdims=True)[:, :128]
    count = jnp.sum(dot_binary(happened, jnp.ones((LO, 128), F32)), axis=0, keepdims=True)
    packed = jnp.concatenate([everything, count, jnp.zeros((6, 128), F32)], axis=0)
    message[...] = jnp.broadcast_to(packed[None], message.shape)


def risks(linear, rank, events, rows, ex):
    groups = rows // LO
    return pl.pallas_call(
        functools.partial(risk_kernel, rows),
        in_specs=[VMEM] * 3,
        out_shape=[
            jax.ShapeDtypeStruct((1, rows), F32),
            jax.ShapeDtypeStruct((groups, LO), F32),
            jax.ShapeDtypeStruct((groups, LO), F32),
            jax.ShapeDtypeStruct((ex, 8, 128), F32),
        ],
        out_specs=[VMEM] * 4,
        compiler_params=pltpu.CompilerParams(**PARAMS),
        cost_estimate=pl.CostEstimate(flops=rows * LO * 128, bytes_accessed=rows * 64, transcendentals=rows),
        name="risks",
    )(linear, rank, events)


def hazard_kernel(rows, messages, sums, events, rank, *outs):
    cumulative, squares, ordered_squares, message, count_out = outs
    groups = rows // LO
    me = lax.axis_index("ex")
    later = jnp.zeros((1, 1), F32)
    count = jnp.zeros((1, 128), F32)
    for b in range(messages.shape[0]):
        later = later + jnp.where(b > me, messages[b, 0:1, 0:1], 0.0)
        count = count + messages[b, 1:2, :]
    count_out[...] = jnp.broadcast_to(count, count_out.shape)
    risk_sum = sums[...] + later
    hazard = events[...] / risk_sum
    square = events[...] / (risk_sum * risk_sum)
    ordered_squares[...] = square
    both = jnp.concatenate([hazard, square], axis=0)
    inside = dot_binary(both, triangle(LO, lambda a, b: a <= b))
    totals = jnp.broadcast_to(inside[:, LO - 1 :], inside.shape)
    before = triangle(groups, lambda a, b: a > b)
    carried = jnp.concatenate(
        [exact_dot(before, totals[:groups]), exact_dot(before, totals[groups:])], axis=0
    )
    message[...] = jnp.concatenate(
        [
            jnp.sum(totals[:groups], axis=0, keepdims=True)[:, :128],
            jnp.sum(totals[groups:], axis=0, keepdims=True)[:, :128],
            jnp.zeros((6, 128), F32),
        ],
        axis=0,
    )
    place = lax.rem(rank[...], rows)
    mask = one_hot(place // LO, groups, F32)
    placed = dot_binary(inside + carried, one_hot(lax.rem(place, LO), LO))
    cumulative[...] = jnp.sum(mask * placed[:groups], axis=0, keepdims=True)
    squares[...] = jnp.sum(mask * placed[groups:], axis=0, keepdims=True)


def hazards(messages, sums, events, rank, rows):
    groups = rows // LO
    row = jax.ShapeDtypeStruct((1, rows), F32)
    small = jax.ShapeDtypeStruct((8, 128), F32)
    return pl.pallas_call(
        functools.partial(hazard_kernel, rows),
        in_specs=[VMEM] * 4,
        out_shape=[row, row, jax.ShapeDtypeStruct((groups, LO), F32), small, small],
        out_specs=[VMEM] * 5,
        compiler_params=pltpu.CompilerParams(**PARAMS),
        cost_estimate=pl.CostEstimate(flops=rows * LO * 200, bytes_accessed=rows * 64, transcendentals=0),
        name="hazards",
    )(messages, sums, events, rank)


def total_kernel(parts, *refs):
    tangents = refs[:parts]
    risk, squares, hazard_message, tangent_out, message = refs[parts:]
    kf, rows = tangent_out.shape
    plain = jnp.zeros((kf, 128), F32)
    scaled = jnp.zeros((kf, 128), F32)
    for start in range(0, rows, 128):
        at = slice(start, start + 128)
        tangent = tangents[0][:, at]
        for part in tangents[1:]:
            tangent = tangent + part[:, at]
        tangent_out[:, at] = tangent
        weighted = tangent * risk[:, at]
        plain = plain + weighted
        scaled = scaled + weighted * squares[:, at]
    packed = jnp.concatenate([plain, scaled, hazard_message[...]], axis=0)
    message[...] = jnp.broadcast_to(packed[None], message.shape)


def block_totals(tangents, risk, squares, hazard_message, ex):
    kf, rows = tangents[0].shape
    return pl.pallas_call(
        functools.partial(total_kernel, len(tangents)),
        in_specs=[VMEM] * (len(tangents) + 3),
        out_shape=[
            jax.ShapeDtypeStruct((kf, rows), F32),
            jax.ShapeDtypeStruct((ex, 2 * kf + 8, 128), F32),
        ],
        out_specs=[VMEM] * 2,
        compiler_params=pltpu.CompilerParams(**PARAMS),
        name="block_totals",
    )(*tangents, risk, squares, hazard_message)


def scan_kernel(rows, kf, tangent, risk, rank, squares, cumulative_out, lhs, spread):
    groups = rows // LO
    chunk = min(1024, rows)
    ordered = jnp.zeros((groups * 2 * kf, LO), F32)
    for start in range(0, rows, chunk):
        at = slice(start, start + chunk)
        place = lax.rem(rank[:, at], rows)
        group = place // LO
        spread[:, at] = one_hot(lax.rem(place, LO), LO)
        both = jnp.concatenate(split_two(tangent[:, at] * risk[:, at]), axis=0)
        for g in range(groups):
            lhs[g * 2 * kf : (g + 1) * 2 * kf, at] = jnp.where(group == g, both, 0.0).astype(BF16)
        ordered = ordered + lax.dot_general(lhs[:, at], spread[:, at], NT, preferred_element_type=F32)
    ordered = jnp.concatenate(
        [
            ordered[g * 2 * kf : g * 2 * kf + kf] + ordered[g * 2 * kf + kf : (g + 1) * 2 * kf]
            for g in range(groups)
        ],
        axis=0,
    )
    inside = dot_binary(ordered, triangle(LO, lambda a, b: a >= b))
    carried = jnp.zeros((kf, 1), F32)
    hazard = [None] * groups
    for g in reversed(range(groups)):
        rows_of = slice(g * kf, (g + 1) * kf)
        hazard[g] = (inside[rows_of] + carried) * squares[g : g + 1, :]
        carried = carried + inside[rows_of, :1]
    inside = dot_binary(jnp.concatenate(hazard, axis=0), triangle(LO, lambda a, b: a <= b))
    carried = jnp.zeros((kf, 1), F32)
    summed = [None] * groups
    for g in range(groups):
        rows_of = slice(g * kf, (g + 1) * kf)
        summed[g] = inside[rows_of] + carried
        carried = carried + inside[rows_of, LO - 1 :]
    high, low = split_two(jnp.concatenate(summed, axis=0))
    high, low = high.astype(BF16), low.astype(BF16)
    for start in range(0, rows, chunk):
        at = slice(start, start + chunk)
        group = lax.rem(rank[:, at], rows) // LO
        placed = jnp.dot(high, spread[:, at], preferred_element_type=F32) + jnp.dot(
            low, spread[:, at], preferred_element_type=F32
        )
        picked = jnp.zeros((kf, chunk), F32)
        for g in range(groups):
            picked = picked + jnp.where(group == g, placed[g * kf : (g + 1) * kf], 0.0)
        cumulative_out[:, at] = picked


def scans(tangent, risk, rank, squares):
    kf, rows = tangent.shape
    groups = rows // LO
    return pl.pallas_call(
        functools.partial(scan_kernel, rows, kf),
        in_specs=[VMEM] * 4,
        out_shape=jax.ShapeDtypeStruct((kf, rows), F32),
        out_specs=VMEM,
        scratch_shapes=[pltpu.VMEM((groups * 2 * kf, rows), BF16), pltpu.VMEM((LO, rows), BF16)],
        compiler_params=pltpu.CompilerParams(**PARAMS),
        cost_estimate=pl.CostEstimate(
            flops=4 * rows * LO * groups * 2 * kf, bytes_accessed=rows * kf * 24, transcendentals=0
        ),
        name="scans",
    )(tangent, risk, rank, squares)


def weight_kernel(kf, messages, tangent, local, risk, cumulative, squares, weighted):
    me = lax.axis_index("ex")
    ex = messages.shape[0]
    later = jnp.zeros((kf, 1), F32)
    own_later = later
    before = later
    hazard_before = jnp.zeros((1, 1), F32)
    for b in reversed(range(ex)):
        plain = jnp.sum(messages[b, :kf], axis=1, keepdims=True)
        scaled = jnp.sum(messages[b, kf : 2 * kf], axis=1, keepdims=True)
        hazard_total = messages[b, 2 * kf : 2 * kf + 1, :1]
        square_total = messages[b, 2 * kf + 1 : 2 * kf + 2, :1]
        own_later = own_later + jnp.where(b > me, plain, 0.0)
        before = before + jnp.where(b < me, scaled + square_total * later, 0.0)
        hazard_before = hazard_before + jnp.where(b < me, hazard_total, 0.0)
        later = later + plain
    value = tangent[...] * (cumulative[...] + hazard_before) - (local[...] + squares[...] * own_later + before)
    weighted[...] = (risk[...] * value).astype(BF16)


def weights(messages, tangent, local, risk, cumulative, squares):
    return pl.pallas_call(
        functools.partial(weight_kernel, tangent.shape[0]),
        in_specs=[VMEM] * 6,
        out_shape=jax.ShapeDtypeStruct(tangent.shape, BF16),
        out_specs=VMEM,
        compiler_params=pltpu.CompilerParams(**PARAMS),
        name="weights",
    )(messages, tangent, local, risk, cumulative, squares)


def gradient_kernel(feat, kf, *refs):
    parts, dosages, out, weighted = refs[:feat], refs[feat], refs[feat + 1], refs[feat + 2]
    me = lax.axis_index("feat")
    for i in range(feat):
        weighted[pl.ds(pl.multiple_of((me ^ i) * kf, kf), kf), :] = parts[i][...]
    total = jnp.dot(weighted[...], dosages[...], preferred_element_type=F32)
    out[...] = total.T.reshape(out.shape)


def gradients(parts, dosages, ex):
    feat = len(parts)
    kf, persons = parts[0].shape
    k, variants = kf * feat, dosages.shape[1]
    return pl.pallas_call(
        functools.partial(gradient_kernel, feat, kf),
        in_specs=[VMEM] * (feat + 1),
        out_shape=jax.ShapeDtypeStruct((ex, variants // ex, k), F32),
        out_specs=VMEM,
        scratch_shapes=[pltpu.VMEM((k, persons), BF16)],
        compiler_params=pltpu.CompilerParams(**PARAMS),
        cost_estimate=pl.CostEstimate(
            flops=2 * persons * variants * k, bytes_accessed=persons * (variants * 2 + k * 2), transcendentals=0
        ),
        name="gradients",
    )(*parts, dosages)


def finish_kernel(pieces, count, out):
    total = pieces[0]
    for b in range(1, pieces.shape[0]):
        total = total + pieces[b]
    total = total / count[0:1, 0:1]
    out[...] = jnp.broadcast_to(total[None], out.shape)


def finish(pieces, count):
    return pl.pallas_call(
        finish_kernel,
        in_specs=[VMEM] * 2,
        out_shape=jax.ShapeDtypeStruct(pieces.shape, F32),
        out_specs=VMEM,
        compiler_params=pltpu.CompilerParams(**PARAMS),
        name="finish",
    )(pieces, count)


def local(dosages, coefficients, directions, event_rank, events):
    feat, ex = lax.axis_size("feat"), lax.axis_size("ex")
    rows = dosages.shape[0]
    variants, k = directions.shape
    each = k // feat
    padded = -(-each // 16) * 16
    if padded != each:
        directions = jnp.pad(directions.reshape(variants, feat, each), ((0, 0), (0, 0), (0, padded - each)))
        directions = directions.reshape(variants, feat * padded)
    rank, event_row = event_rank[None], events[None]

    linear, keep, send = products(dosages, coefficients, directions, feat)
    order = list(range(1, feat // 2)) + [0]
    joined = {q: (keep[q], swap(send[q], "feat", 1)) for q in order}
    others = [swap(joined[q][0] + joined[q][1], "feat", 2 * q) for q in order[:-1]]

    risk, sums, ordered_events, message = risks(exchange(linear, "feat"), rank, event_row, rows, ex)
    cumulative, squares, ordered_squares, hazard_message, count = hazards(
        exchange(message, "ex"), sums, ordered_events, rank, rows
    )

    tangent, message = block_totals(list(joined[0]) + others, risk, squares, hazard_message, ex)
    messages = exchange(message, "ex")
    summed = scans(tangent, risk, rank, ordered_squares)
    own = weights(messages, tangent, summed, risk, cumulative, squares)

    chips = {0: own}
    for q in order[:-1]:
        chips[q] = swap(own, "feat", 2 * q)
    parts = []
    for q in range(feat // 2):
        parts += [chips[q], swap(chips[q], "feat", 1)]

    pieces = exchange(gradients(parts, dosages, ex), "ex")
    result = exchange(finish(pieces, count), "ex").reshape(variants, -1)
    if padded != each:
        result = result.reshape(variants, feat, padded)[:, :, :each].reshape(variants, k)
    return result


def solution(mesh):
    placed = (P("ex", "feat"), P("feat"), P("feat", None), P("ex"), P("ex"))
    return jax.shard_map(
        local, mesh=mesh, in_specs=placed, out_specs=P("feat", None), check_vma=False
    )
```

time: 108 us -> 90 us (0.83)
  blocking collectives: 0 us -> 48.5 us
  waiting for transfers between devices: 46.3 us -> 5.7 us
  starting transfers between devices: 39.4 us -> 13.3 us
  local copies, waits for them, and re-layouts: 2.11 us -> 4.48 us
  Pallas kernels: 19.2 us -> 17.3 us
    all_to_all x0 -> x4, blocking collectives: none -> 48.5 us  [exchange(): return lax.all_to_all(x, axis, 0, 0)]
    ppermute x33 -> x14, waiting for transfers between devices: 46.3 us -> 5.69 us  [swap(): return lax.ppermute(x, axis, [(s, s ^ i) for s in range(count)])]
    ppermute x33 -> x14, starting transfers between devices: 39.4 us -> 9.97 us  [swap(): return lax.ppermute(x, axis, [(s, s ^ i) for s in range(count)])]
    all_to_all x0 -> x1, starting transfers between devices: none -> 3.29 us  [exchange(): return lax.all_to_all(x, axis, 0, 0)]
    unnamed x8 -> x9, local copies, waits for them, and re-layouts: 0.92 us -> 3.8 us
    pallas_call x6 -> x7, Pallas kernels: 13 us -> 10.7 us  [the longest x1 5.74 us: scans(): pl.pallas_call(functools.partial(scan_kernel, rows, kf), in_specs=[VMEM]...]
  transfers between devices with their start and end apart: 33 -> 15, of which waited for: 22 -> 5; matrix products, arithmetic and copies ran while one was open for 1% -> 0% of each run, Pallas kernels for 3% -> 10%
where the time goes in v2:
time: 90 us; the launch traced here: 89.5 us
  blocking collectives  48.5 us (54%)
  Pallas kernels  17.3 us (19%)
  starting transfers between devices  13.3 us (15%)
  waiting for transfers between devices  5.7 us (6%)
  local copies, waits for them, and re-layouts  4.48 us (5%)
    all_to_all x4, blocking collectives, exchange(): return lax.all_to_all(x, axis, 0, 0)  48.5 us
    ppermute x14, starting transfers between devices, swap(): return lax.ppermute(x, axis, [(s, s ^ i) for s in range(count)])  9.97 us
    pallas_call x1, Pallas kernels, products(): pl.pallas_call(functools.partial(product_kernel, feat, kf), grid=(persons...  6.62 us
    pallas_call x1, Pallas kernels, scans(): pl.pallas_call(functools.partial(scan_kernel, rows, kf), in_specs=[VMEM]...  5.74 us
    ppermute x14, waiting for transfers between devices, swap(): return lax.ppermute(x, axis, [(s, s ^ i) for s in range(count)])  5.69 us
    unnamed x9, local copies, waits for them, and re-layouts  3.8 us
    all_to_all x1, starting transfers between devices, exchange(): return lax.all_to_all(x, axis, 0, 0)  3.29 us
  transfers between devices with their start and end apart: 15, of which 5 were waited for; matrix products, arithmetic and copies ran while one was open for 0% of the time, Pallas kernels for 10%

profile of v2, /device:TPU:0, one launch (start us, length us, event | category | flops | bytes accessed | tf_op | source)
XLA Modules:
  0.0 89.5 jit_solution(7918867397034541358)
XLA Ops:
  0.0 0.7 broadcast_in_dim.9.coefficients
  0.7 0.9 %copy-done.1 = bf16[512,128]{1,0:T(8,128)(2,1)S(1)} copy-done((bf16[512,128]{1,0:T(8,128)(2,1)S(1)}, bf16[512,128]{1,0:T(8,128)(2,1)}, u32[]{:S(2)}) %copy-start.1) | copy-done | bytes 131096
  1.6 6.6 %products.1 = (f32[8,1,4096]{2,1,0:T(1,128)S(1)}, f32[16,4096]{1,0:T(8,128)S(1)}, f32[16,4096]{1,0:T(8,128)S(1)}, f32[16,4096]{1,0:T(8,128)S(1)}, f32[16,4096]{1...) custom-call(bf16[512,128]{1,0:T(8,128)(2,1)S(1)} %copy-done.1, ...), custom_call_target="tpu_custom_call" | custom-call | flops 536870912 | bytes 6291456 | tf_op jit(solution)/shard_map/products/pallas_call | solution.py:93
  9.3 0.6 collective-permute-done.1
  9.9 2.9 %collective-permute-start.2 = (f32[16,4096]{1,0:T(8,128)S(1)}, f32[16,4096]{1,0:T(8,128)S(1)}, u32[]{:S(2)}, u32[]{:S(2)}) collective-permute-start(f32[16,4096]{1,0:T(8,128)S(1)} %add.9), channel_id=1, source_target_pairs={{0,2},{1,3},{2,0},{3,1},{4,6},{5,7},{6,4},{7,5},{8,10},{9,11},{10,... | collective-permute-start | bytes 786440 | tf_op jit(solution)/shard_map/ppermute | solution.py:21
  12.9 1.6 %collective-permute-start.4 = (f32[16,4096]{1,0:T(8,128)S(1)}, f32[16,4096]{1,0:T(8,128)S(1)}, u32[]{:S(2)}, u32[]{:S(2)}) collective-permute-start(f32[16,4096]{1,0:T(8,128)S(1)} %add.10), channel_id=1, source_target_pairs={{0,4},{1,5},{2,6},{3,7},{4,0},{5,1},{6,2},{7,3},{8,12},{9,13},{10,... | collective-permute-start | bytes 786440 | tf_op jit(solution)/shard_map/ppermute | solution.py:21
  14.8 13.3 %all_to_all.25.linear = f32[8,1,4096]{2,1,0:T(1,128)S(1)} all-to-all(f32[8,1,4096]{2,1,0:T(1,128)S(1)} %get-tuple-element.33), channel_id=1, replica_groups=mesh['ex'=4,'feat'=8] {'feat'}, dimensions={0} | all-to-all | bytes 262144 | tf_op jit(solution)/shard_map/all_to_all | solution.py:25
  28.1 1.3 %risks.1 = (f32[1,4096]{1,0:T(1,128)S(1)}, f32[16,256]{1,0:T(8,128)S(1)}, f32[16,256]{1,0:T(8,128)S(1)}, f32[4,8,128]{2,1,0:T(8,128)S(1)}) custom-call(f32[8,1,4096]{2,1,0:T(1,128)S(1)} %all_to_all.25.linear, s32[1,4096]{1,0:T(1,128)S(1)} %bitcast.4, s32[1,4096]{1,0:T(1,128)S(1)} %bitcast.3), custom_call_target="tpu_custom_call" | custom-call | flops 134217728 | bytes 262144 | tf_op jit(solution)/shard_map/risks/pallas_call | solution.py:144
  29.3 10.3 %all_to_all.26.messages = f32[4,8,128]{2,1,0:T(8,128)S(1)} all-to-all(f32[4,8,128]{2,1,0:T(8,128)S(1)} %get-tuple-element.35), channel_id=1, replica_groups=mesh['ex'=4,'feat'=8] {'ex'}, dimensions={0} | all-to-all | bytes 32768 | tf_op jit(solution)/shard_map/all_to_all | solution.py:25
  39.6 1.8 %hazards.1 = (f32[1,4096]{1,0:T(1,128)S(1)}, f32[1,4096]{1,0:T(1,128)S(1)}, f32[16,256]{1,0:T(8,128)S(1)}, f32[8,128]{1,0:T(8,128)S(1)}, f32[8,128]{1,0:T(8,128)S(1)}) custom-call(f32[4,8,128]{2,1,0:T(8,128)S(1)} %all_to_all.26.messages, f32[16,256]{1,0:T(8,128)S(1)} %get-tuple-element.36.sums, f32[16,256]{1,0:T(8,128)S(1)} %get-tuple-element.37.events, ...), custom_call_target="tpu_custom_call" | custom-call | flops 209715200 | bytes 262144 | tf_op jit(solution)/shard_map/hazards/pallas_call | solution.py:200
  41.4 0.8 block_totals.1
  42.2 3.3 %all-to-all-start.2 = ((f32[4,40,128]{2,1,0:T(8,128)}), f32[4,40,128]{2,1,0:T(8,128)S(1)}, u32[]{:S(2)}, u32[]{:S(2)}) async-start(f32[4,40,128]{2,1,0:T(8,128)} %get-tuple-element.40), calls=%async_computation.2 | async-start | bytes 163840 | tf_op jit(solution)/shard_map/all_to_all | solution.py:25
  45.5 5.7 %scans.1.local = f32[16,4096]{1,0:T(8,128)S(1)} custom-call(f32[16,4096]{1,0:T(8,128)S(1)} %get-tuple-element.41.tangent, f32[1,4096]{1,0:T(1,128)S(1)} %get-tuple-element.34.refs_5_.risk, s32[1,4096]{1,0:T(1,128)S(1)} %bitcast.6, f32[16,256]{1,0:T(8,128)S(1)} %get-tuple-element.42.squares), custom_call_target="tpu_custom_call" | custom-call | flops 2147483648 | bytes 1572864 | tf_op jit(solution)/shard_map/scans/pallas_call | solution.py:296
  51.5 1.6 %collective-permute-start.12 = (bf16[16,4096]{1,0:T(8,128)(2,1)S(1)}, bf16[16,4096]{1,0:T(8,128)(2,1)S(1)}, u32[]{:S(2)}, u32[]{:S(2)}) collective-permute-start(bf16[16,4096]{1,0:T(8,128)(2,1)S(1)} %weights.1.refs_0_), channel_id=1, source_target_pairs={{0,6},{1,7},{2,4},{3,5},{4,2},{5,3},{6,0},{7,1},{8,14},{9,15},{10,... | collective-permute-start | bytes 393224 | tf_op jit(solution)/shard_map/ppermute | solution.py:21
  53.1 1.1 %collective-permute-start.10 = (bf16[16,4096]{1,0:T(8,128)(2,1)S(1)}, bf16[16,4096]{1,0:T(8,128)(2,1)S(1)}, u32[]{:S(2)}, u32[]{:S(2)}) collective-permute-start(bf16[16,4096]{1,0:T(8,128)(2,1)S(1)} %weights.1.refs_0_), channel_id=1, source_target_pairs={{0,4},{1,5},{2,6},{3,7},{4,0},{5,1},{6,2},{7,3},{8,12},{9,13},{10,... | collective-permute-start | bytes 393224 | tf_op jit(solution)/shard_map/ppermute | solution.py:21
  54.2 0.9 collective-permute-start.8
  55.0 2.8 %collective-permute-done.12.refs_6_ = bf16[16,4096]{1,0:T(8,128)(2,1)S(1)} collective-permute-done((bf16[16,4096]{1,0:T(8,128)(2,1)S(1)}, bf16[16,4096]{1,0:T(8,128)(2,1)S(1)}, u32[]{:S(2)}, u32[]{:S(2)}) %collective-permute-start.12) | collective-permute-done | bytes 131104 | tf_op jit(solution)/shard_map/ppermute | solution.py:21
  57.8 1.3 %collective-permute-done.10.refs_4_ = bf16[16,4096]{1,0:T(8,128)(2,1)S(1)} collective-permute-done((bf16[16,4096]{1,0:T(8,128)(2,1)S(1)}, bf16[16,4096]{1,0:T(8,128)(2,1)S(1)}, u32[]{:S(2)}, u32[]{:S(2)}) %collective-permute-start.10) | collective-permute-done | bytes 131104 | tf_op jit(solution)/shard_map/ppermute | solution.py:21
  59.6 0.8 collective-permute-done.11.refs_5_
  60.7 2.2 %copy-done = bf16[4096,512]{1,0:T(8,128)(2,1)S(1)} copy-done((bf16[4096,512]{1,0:T(8,128)(2,1)S(1)}, bf16[4096,512]{1,0:T(8,128)(2,1)}, u32[]{:S(2)}) %copy-start) | copy-done | bytes 4194328
  62.9 0.9 gradients.1
  63.7 13.9 %all_to_all.27.pieces = f32[4,128,128]{2,1,0:T(8,128)S(1)} all-to-all(f32[4,128,128]{2,1,0:T(8,128)S(1)} %gradients.1), channel_id=1, replica_groups=mesh['ex'=4,'feat'=8] {'ex'}, dimensions={0} | all-to-all | bytes 524288 | tf_op jit(solution)/shard_map/all_to_all | solution.py:25
  77.7 11.0 %all_to_all.28 = f32[4,128,128]{2,1,0:T(8,128)S(1)} all-to-all(f32[4,128,128]{2,1,0:T(8,128)S(1)} %finish.1), channel_id=1, replica_groups=mesh['ex'=4,'feat'=8] {'ex'}, dimensions={0} | all-to-all | bytes 524288 | tf_op jit(solution)/shard_map/all_to_all | solution.py:25
  88.8 0.7 copy.7
  (31 shorter events, 2.5 us)
Async XLA Ops:
  0.7 0.9 %copy-start.1 = (bf16[512,128]{1,0:T(8,128)(2,1)S(1)}, bf16[512,128]{1,0:T(8,128)(2,1)}, u32[]{:S(2)}) copy-start(bf16[512,128]{1,0:T(8,128)(2,1)} %directions.1) | copy-start | bytes 393220
  1.6 26.5 %copy-start.2 = (s32[4096]{0:T(1024)S(1)}, s32[4096]{0:T(1024)}, u32[]{:S(2)}) copy-start(s32[4096]{0:T(1024)} %param.9) | copy-start | bytes 49156
  1.6 26.5 %copy-start.3 = (s32[4096]{0:T(1024)S(1)}, s32[4096]{0:T(1024)}, u32[]{:S(2)}) copy-start(s32[4096]{0:T(1024)} %param.8) | copy-start | bytes 49156
  8.2 1.7 %collective-permute-start.1 = (f32[16,4096]{1,0:T(8,128)S(1)}, f32[16,4096]{1,0:T(8,128)S(1)}, u32[]{:S(2)}, u32[]{:S(2)}) collective-permute-start(f32[16,4096]{1,0:T(8,128)S(1)} %get-tuple-element.28), channel_id=1, source_target_pairs={{0,1},{1,0},{2,3},{3,2},{4,5},{5,4},{6,7},{7,6},{8,9},{9,8},{10,11... | collective-permute-start | bytes 786440 | tf_op jit(solution)/shard_map/ppermute | solution.py:21
  8.7 4.1 %collective-permute-start.3 = (f32[16,4096]{1,0:T(8,128)S(1)}, f32[16,4096]{1,0:T(8,128)S(1)}, u32[]{:S(2)}, u32[]{:S(2)}) collective-permute-start(f32[16,4096]{1,0:T(8,128)S(1)} %get-tuple-element.30), channel_id=1, source_target_pairs={{0,1},{1,0},{2,3},{3,2},{4,5},{5,4},{6,7},{7,6},{8,9},{9,8},{10,11... | collective-permute-start | bytes 786440 | tf_op jit(solution)/shard_map/ppermute | solution.py:21
  8.8 5.7 %collective-permute-start.5 = (f32[16,4096]{1,0:T(8,128)S(1)}, f32[16,4096]{1,0:T(8,128)S(1)}, u32[]{:S(2)}, u32[]{:S(2)}) collective-permute-start(f32[16,4096]{1,0:T(8,128)S(1)} %get-tuple-element.32), channel_id=1, source_target_pairs={{0,1},{1,0},{2,3},{3,2},{4,5},{5,4},{6,7},{7,6},{8,9},{9,8},{10,11... | collective-permute-start | bytes 786440 | tf_op jit(solution)/shard_map/ppermute | solution.py:21
  9.3 32.1 %collective-permute-start = (f32[16,4096]{1,0:T(8,128)S(1)}, f32[16,4096]{1,0:T(8,128)S(1)}, u32[]{:S(2)}, u32[]{:S(2)}) collective-permute-start(f32[16,4096]{1,0:T(8,128)S(1)} %get-tuple-element.26), channel_id=1, source_target_pairs={{0,1},{1,0},{2,3},{3,2},{4,5},{5,4},{6,7},{7,6},{8,9},{9,8},{10,11... | collective-permute-start | bytes 786440 | tf_op jit(solution)/shard_map/ppermute | solution.py:21
  9.9 31.5 %collective-permute-start.2 = (f32[16,4096]{1,0:T(8,128)S(1)}, f32[16,4096]{1,0:T(8,128)S(1)}, u32[]{:S(2)}, u32[]{:S(2)}) collective-permute-start(f32[16,4096]{1,0:T(8,128)S(1)} %add.9), channel_id=1, source_target_pairs={{0,2},{1,3},{2,0},{3,1},{4,6},{5,7},{6,4},{7,5},{8,10},{9,11},{10,... | collective-permute-start | bytes 786440 | tf_op jit(solution)/shard_map/ppermute | solution.py:21
  12.9 28.5 %collective-permute-start.4 = (f32[16,4096]{1,0:T(8,128)S(1)}, f32[16,4096]{1,0:T(8,128)S(1)}, u32[]{:S(2)}, u32[]{:S(2)}) collective-permute-start(f32[16,4096]{1,0:T(8,128)S(1)} %add.10), channel_id=1, source_target_pairs={{0,4},{1,5},{2,6},{3,7},{4,0},{5,1},{6,2},{7,3},{8,12},{9,13},{10,... | collective-permute-start | bytes 786440 | tf_op jit(solution)/shard_map/ppermute | solution.py:21
  14.5 26.9 %collective-permute-start.6 = (f32[16,4096]{1,0:T(8,128)S(1)}, f32[16,4096]{1,0:T(8,128)S(1)}, u32[]{:S(2)}, u32[]{:S(2)}) collective-permute-start(f32[16,4096]{1,0:T(8,128)S(1)} %add.11), channel_id=1, source_target_pairs={{0,6},{1,7},{2,4},{3,5},{4,2},{5,3},{6,0},{7,1},{8,14},{9,15},{10,... | collective-permute-start | bytes 786440 | tf_op jit(solution)/shard_map/ppermute | solution.py:21
  42.2 9.1 %all-to-all-start.2 = ((f32[4,40,128]{2,1,0:T(8,128)}), f32[4,40,128]{2,1,0:T(8,128)S(1)}, u32[]{:S(2)}, u32[]{:S(2)}) async-start(f32[4,40,128]{2,1,0:T(8,128)} %get-tuple-element.40), calls=%async_computation.2 | async-start | bytes 163840 | tf_op jit(solution)/shard_map/all_to_all | solution.py:25
  51.5 6.3 %collective-permute-start.12 = (bf16[16,4096]{1,0:T(8,128)(2,1)S(1)}, bf16[16,4096]{1,0:T(8,128)(2,1)S(1)}, u32[]{:S(2)}, u32[]{:S(2)}) collective-permute-start(bf16[16,4096]{1,0:T(8,128)(2,1)S(1)} %weights.1.refs_0_), channel_id=1, source_target_pairs={{0,6},{1,7},{2,4},{3,5},{4,2},{5,3},{6,0},{7,1},{8,14},{9,15},{10,... | collective-permute-start | bytes 393224 | tf_op jit(solution)/shard_map/ppermute | solution.py:21
  53.1 6.1 %collective-permute-start.10 = (bf16[16,4096]{1,0:T(8,128)(2,1)S(1)}, bf16[16,4096]{1,0:T(8,128)(2,1)S(1)}, u32[]{:S(2)}, u32[]{:S(2)}) collective-permute-start(bf16[16,4096]{1,0:T(8,128)(2,1)S(1)} %weights.1.refs_0_), channel_id=1, source_target_pairs={{0,4},{1,5},{2,6},{3,7},{4,0},{5,1},{6,2},{7,3},{8,12},{9,13},{10,... | collective-permute-start | bytes 393224 | tf_op jit(solution)/shard_map/ppermute | solution.py:21
  54.2 5.0 %collective-permute-start.8 = (bf16[16,4096]{1,0:T(8,128)(2,1)S(1)}, bf16[16,4096]{1,0:T(8,128)(2,1)S(1)}, u32[]{:S(2)}, u32[]{:S(2)}) collective-permute-start(bf16[16,4096]{1,0:T(8,128)(2,1)S(1)} %weights.1.refs_0_), channel_id=1, source_target_pairs={{0,2},{1,3},{2,0},{3,1},{4,6},{5,7},{6,4},{7,5},{8,10},{9,11},{10,... | collective-permute-start | bytes 393224 | tf_op jit(solution)/shard_map/ppermute | solution.py:21
  55.0 4.6 %collective-permute-start.7 = (bf16[16,4096]{1,0:T(8,128)(2,1)S(1)}, bf16[16,4096]{1,0:T(8,128)(2,1)S(1)}, u32[]{:S(2)}, u32[]{:S(2)}) collective-permute-start(bf16[16,4096]{1,0:T(8,128)(2,1)S(1)} %weights.1.refs_0_), channel_id=1, source_target_pairs={{0,1},{1,0},{2,3},{3,2},{4,5},{5,4},{6,7},{7,6},{8,9},{9,8},{10,11... | collective-permute-start | bytes 393224 | tf_op jit(solution)/shard_map/ppermute | solution.py:21
  57.8 1.8 %collective-permute-start.13 = (bf16[16,4096]{1,0:T(8,128)(2,1)S(1)}, bf16[16,4096]{1,0:T(8,128)(2,1)S(1)}, u32[]{:S(2)}, u32[]{:S(2)}) collective-permute-start(bf16[16,4096]{1,0:T(8,128)(2,1)S(1)} %collective-permute-done.12.refs_6_), channel_id=1, source_target_pairs={{0,1},{1,0},{2,3},{3,2},{4,5},{5,4},{6,7},{7,6},{8,9},{9,8},{10,11... | collective-permute-start | bytes 393224 | tf_op jit(solution)/shard_map/ppermute | solution.py:21
  59.1 1.3 %collective-permute-start.11 = (bf16[16,4096]{1,0:T(8,128)(2,1)S(1)}, bf16[16,4096]{1,0:T(8,128)(2,1)S(1)}, u32[]{:S(2)}, u32[]{:S(2)}) collective-permute-start(bf16[16,4096]{1,0:T(8,128)(2,1)S(1)} %collective-permute-done.10.refs_4_), channel_id=1, source_target_pairs={{0,1},{1,0},{2,3},{3,2},{4,5},{5,4},{6,7},{7,6},{8,9},{9,8},{10,11... | collective-permute-start | bytes 393224 | tf_op jit(solution)/shard_map/ppermute | solution.py:21
  59.1 1.5 %collective-permute-start.9 = (bf16[16,4096]{1,0:T(8,128)(2,1)S(1)}, bf16[16,4096]{1,0:T(8,128)(2,1)S(1)}, u32[]{:S(2)}, u32[]{:S(2)}) collective-permute-start(bf16[16,4096]{1,0:T(8,128)(2,1)S(1)} %collective-permute-done.8.refs_2_), channel_id=1, source_target_pairs={{0,1},{1,0},{2,3},{3,2},{4,5},{5,4},{6,7},{7,6},{8,9},{9,8},{10,11... | collective-permute-start | bytes 393224 | tf_op jit(solution)/shard_map/ppermute | solution.py:21
  60.7 2.2 %copy-start = (bf16[4096,512]{1,0:T(8,128)(2,1)S(1)}, bf16[4096,512]{1,0:T(8,128)(2,1)}, u32[]{:S(2)}) copy-start(bf16[4096,512]{1,0:T(8,128)(2,1)} %refs_8_.1) | copy-start | bytes 12582916

commit v3 on v2

--- a/solution.py
+++ b/solution.py
@@ -13,16 +13,13 @@
 NT = (((1,), (1,)), ((), ()))
 VMEM = pl.BlockSpec(memory_space=pltpu.VMEM)
 HIGHEST = lax.Precision.HIGHEST
-PARAMS = dict(vmem_limit_bytes=48 * 1024 * 1024)
+HBM = pl.BlockSpec(memory_space=pltpu.HBM)
+PARAMS = dict(vmem_limit_bytes=24 * 1024 * 1024)
 
 
 def swap(x, axis, i):
     count = lax.axis_size(axis)
     return lax.ppermute(x, axis, [(s, s ^ i) for s in range(count)])
-
-
-def exchange(x, axis):
-    return lax.all_to_all(x, axis, 0, 0)
 
 
 def split_two(x):
@@ -60,28 +57,46 @@
     return total
 
 
-def product_kernel(feat, kf, directions, coefficients, dosages, *refs):
+def product_kernel(feat, kf, chunk, directions, coefficients, dosages, *refs):
     linear, keep, send = refs[0], refs[1 : 1 + feat // 2], refs[1 + feat // 2 : 1 + feat]
-    rhs, turned = refs[1 + feat :]
+    table, own_directions, own_coefficients, rhs, turned, sems = refs[1 + feat :]
     me = lax.axis_index("feat")
     width = feat * kf
-    variants = rhs.shape[0]
-
-    @pl.when(pl.program_id(0) == 0)
-    def _():
-        rhs[:, :width] = directions[...]
-        spread = jnp.broadcast_to(coefficients[...].astype(F32), (128, variants)).T
-        rhs[:, width:] = spread.astype(BF16)
-
-    result = jnp.dot(dosages[...], rhs[...], preferred_element_type=F32)
-    turned[...] = result[:, :width].T.reshape(turned.shape)
-    for i in range(feat):
-        (send if i % 2 else keep)[i // 2][...] = turned[me ^ i]
+    persons, variants = table.shape
+    steps = persons // chunk
+    small = [
+        pltpu.make_async_copy(directions, own_directions, sems.at[steps]),
+        pltpu.make_async_copy(coefficients, own_coefficients, sems.at[steps + 1]),
+    ]
+    large = [
+        pltpu.make_async_copy(
+            dosages.at[pl.ds(i * chunk, chunk)], table.at[pl.ds(i * chunk, chunk)], sems.at[i]
+        )
+        for i in range(steps)
+    ]
+    for copy in small + large:
+        copy.start()
+    for copy in small:
+        copy.wait()
+    turned[...] = own_directions[...].astype(F32).T.reshape(turned.shape)
+    placed = jnp.concatenate([turned[me ^ i] for i in range(feat)], axis=0)
+    rhs[:, :width] = placed.T.astype(BF16)
+    spread = jnp.broadcast_to(own_coefficients[...].astype(F32), (128, variants))
+    rhs[:, width:] = spread.T.astype(BF16)
     diagonal = triangle(128, lambda a, b: a == b)
-    for start in range(0, dosages.shape[0], 128):
-        block = result[start : start + 128, width:]
-        row = jnp.sum(block * diagonal, axis=0, keepdims=True)
-        linear[:, :, start : start + 128] = jnp.broadcast_to(row[None], (feat, 1, 128))
+    for i in range(steps):
+        large[i].wait()
+        at = slice(i * chunk, (i + 1) * chunk)
+        result = jnp.dot(table[at], rhs[...], preferred_element_type=F32)
+        tangent = result[:, :width].T
+        for j in range(feat):
+            (send if j % 2 else keep)[j // 2][:kf, at] = tangent[j * kf : (j + 1) * kf]
+        for start in range(0, chunk, 128):
+            block = result[start : start + 128, width:]
+            row = jnp.sum(block * diagonal, axis=0, keepdims=True)
+            here = slice(i * chunk + start, i * chunk + start + 128)
+            linear[:, here] = row
+            send[1][kf:, here] = jnp.broadcast_to(row, (8, 128))
 
 
 def products(dosages, coefficients, directions, feat):
@@ -90,20 +105,22 @@
     kf = k // feat
     chunk = min(512, persons)
     piece = jax.ShapeDtypeStruct((kf, persons), F32)
+    first = jax.ShapeDtypeStruct((kf + 8, persons), F32)
     out = pl.pallas_call(
-        functools.partial(product_kernel, feat, kf),
-        grid=(persons // chunk,),
-        in_specs=[
-            pl.BlockSpec((variants, k), lambda s: (0, 0)),
-            pl.BlockSpec((1, variants), lambda s: (0, 0)),
-            pl.BlockSpec((chunk, variants), lambda s: (s, 0)),
-        ],
-        out_shape=[jax.ShapeDtypeStruct((feat, 1, persons), F32)] + [piece] * feat,
-        out_specs=[pl.BlockSpec((feat, 1, chunk), lambda s: (0, 0, s))]
-        + [pl.BlockSpec((kf, chunk), lambda s: (0, s))] * feat,
+        functools.partial(product_kernel, feat, kf, chunk),
+        in_specs=[HBM, HBM, HBM],
+        out_shape=[jax.ShapeDtypeStruct((1, persons), F32)]
+        + [piece] * (feat // 2 + 1)
+        + [first]
+        + [piece] * (feat // 2 - 2),
+        out_specs=[VMEM] * (feat + 1),
         scratch_shapes=[
+            pltpu.VMEM((persons, variants), BF16),
+            pltpu.VMEM((variants, k), BF16),
+            pltpu.VMEM((1, variants), BF16),
             pltpu.VMEM((variants, k + 128), BF16),
-            pltpu.VMEM((feat, kf, chunk), F32),
+            pltpu.VMEM((feat, kf, variants), F32),
+            pltpu.SemaphoreType.DMA((persons // chunk + 2,)),
         ],
         compiler_params=pltpu.CompilerParams(**PARAMS),
         cost_estimate=pl.CostEstimate(
@@ -114,11 +131,48 @@
     return out[0], out[1 : 1 + feat // 2], out[1 + feat // 2 :]
 
 
-def risk_kernel(rows, linear, rank, events, risk_out, sums_out, events_out, message):
+def pair_kernel(linear, received, out):
+    kf = received.shape[0] - 8
+    out[...] = linear[...] + received[kf : kf + 1, :]
+
+
+def pair(linear, received):
+    return pl.pallas_call(
+        pair_kernel,
+        in_specs=[VMEM] * 2,
+        out_shape=jax.ShapeDtypeStruct(linear.shape, F32),
+        out_specs=VMEM,
+        compiler_params=pltpu.CompilerParams(**PARAMS),
+        name="pair",
+    )(linear, received)
+
+
+def join_kernel(count, *refs):
+    keep, received, outs = refs[:count], refs[count : 2 * count], refs[-count:]
+    for mine, other, out in zip(keep, received, outs):
+        kf = mine.shape[0]
+        out[...] = mine[...] + other[:kf, :]
+
+
+def join(keep, received, waited):
+    count = len(keep)
+    return pl.pallas_call(
+        functools.partial(join_kernel, count),
+        in_specs=[VMEM] * (2 * count) + [pl.BlockSpec(memory_space=pl.ANY)] * len(waited),
+        out_shape=[jax.ShapeDtypeStruct(k.shape, F32) for k in keep],
+        out_specs=[VMEM] * count,
+        compiler_params=pltpu.CompilerParams(**PARAMS),
+        name="join",
+    )(*keep, *received, *waited)
+
+
+def risk_kernel(rows, parts, *refs):
+    linear, (rank, events) = refs[:parts], refs[parts : parts + 2]
+    risk_out, sums_out, events_out, message = refs[parts + 2 :]
     groups = rows // LO
-    total = linear[0]
-    for i in range(1, linear.shape[0]):
-        total = total + linear[i]
+    total = linear[0][...]
+    for part in linear[1:]:
+        total = total + part[...]
     risk = jnp.exp(total)
     risk_out[...] = risk
     place = lax.rem(rank[...], rows)
@@ -135,39 +189,31 @@
     events_out[...] = happened
     everything = jnp.sum(totals, axis=0, keepdims=True)[:, :128]
     count = jnp.sum(dot_binary(happened, jnp.ones((LO, 128), F32)), axis=0, keepdims=True)
-    packed = jnp.concatenate([everything, count, jnp.zeros((6, 128), F32)], axis=0)
-    message[...] = jnp.broadcast_to(packed[None], message.shape)
-
-
-def risks(linear, rank, events, rows, ex):
+    message[...] = jnp.concatenate([everything, count, jnp.zeros((6, 128), F32)], axis=0)
+
+
+def risks(linear, rank, events, rows):
     groups = rows // LO
     return pl.pallas_call(
-        functools.partial(risk_kernel, rows),
-        in_specs=[VMEM] * 3,
+        functools.partial(risk_kernel, rows, len(linear)),
+        in_specs=[VMEM] * (len(linear) + 2),
         out_shape=[
             jax.ShapeDtypeStruct((1, rows), F32),
             jax.ShapeDtypeStruct((groups, LO), F32),
             jax.ShapeDtypeStruct((groups, LO), F32),
-            jax.ShapeDtypeStruct((ex, 8, 128), F32),
+            jax.ShapeDtypeStruct((8, 128), F32),
         ],
         out_specs=[VMEM] * 4,
         compiler_params=pltpu.CompilerParams(**PARAMS),
         cost_estimate=pl.CostEstimate(flops=rows * LO * 128, bytes_accessed=rows * 64, transcendentals=rows),
         name="risks",
-    )(linear, rank, events)
-
-
-def hazard_kernel(rows, messages, sums, events, rank, *outs):
-    cumulative, squares, ordered_squares, message, count_out = outs
+    )(*linear, rank, events)
+
+
+def hazard_kernel(rows, later, sums, events, rank, *outs):
+    cumulative, squares, ordered_squares, message = outs
     groups = rows // LO
-    me = lax.axis_index("ex")
-    later = jnp.zeros((1, 1), F32)
-    count = jnp.zeros((1, 128), F32)
-    for b in range(messages.shape[0]):
-        later = later + jnp.where(b > me, messages[b, 0:1, 0:1], 0.0)
-        count = count + messages[b, 1:2, :]
-    count_out[...] = jnp.broadcast_to(count, count_out.shape)
-    risk_sum = sums[...] + later
+    risk_sum = sums[...] + later[0:1, 0:1]
     hazard = events[...] / risk_sum
     square = events[...] / (risk_sum * risk_sum)
     ordered_squares[...] = square
@@ -193,19 +239,19 @@
     squares[...] = jnp.sum(mask * placed[groups:], axis=0, keepdims=True)
 
 
-def hazards(messages, sums, events, rank, rows):
+def hazards(later, sums, events, rank, rows):
     groups = rows // LO
     row = jax.ShapeDtypeStruct((1, rows), F32)
     small = jax.ShapeDtypeStruct((8, 128), F32)
     return pl.pallas_call(
         functools.partial(hazard_kernel, rows),
         in_specs=[VMEM] * 4,
-        out_shape=[row, row, jax.ShapeDtypeStruct((groups, LO), F32), small, small],
-        out_specs=[VMEM] * 5,
+        out_shape=[row, row, jax.ShapeDtypeStruct((groups, LO), F32), small],
+        out_specs=[VMEM] * 4,
         compiler_params=pltpu.CompilerParams(**PARAMS),
         cost_estimate=pl.CostEstimate(flops=rows * LO * 200, bytes_accessed=rows * 64, transcendentals=0),
         name="hazards",
-    )(messages, sums, events, rank)
+    )(later, sums, events, rank)
 
 
 def total_kernel(parts, *refs):
@@ -218,23 +264,22 @@
         at = slice(start, start + 128)
         tangent = tangents[0][:, at]
         for part in tangents[1:]:
-            tangent = tangent + part[:, at]
+            tangent = tangent + part[:kf, at]
         tangent_out[:, at] = tangent
         weighted = tangent * risk[:, at]
         plain = plain + weighted
         scaled = scaled + weighted * squares[:, at]
-    packed = jnp.concatenate([plain, scaled, hazard_message[...]], axis=0)
-    message[...] = jnp.broadcast_to(packed[None], message.shape)
-
-
-def block_totals(tangents, risk, squares, hazard_message, ex):
+    message[...] = jnp.concatenate([plain, scaled, hazard_message[...]], axis=0)
+
+
+def block_totals(tangents, risk, squares, hazard_message):
     kf, rows = tangents[0].shape
     return pl.pallas_call(
         functools.partial(total_kernel, len(tangents)),
         in_specs=[VMEM] * (len(tangents) + 3),
         out_shape=[
             jax.ShapeDtypeStruct((kf, rows), F32),
-            jax.ShapeDtypeStruct((ex, 2 * kf + 8, 128), F32),
+            jax.ShapeDtypeStruct((2 * kf + 8, 128), F32),
         ],
         out_specs=[VMEM] * 2,
         compiler_params=pltpu.CompilerParams(**PARAMS),
@@ -307,18 +352,21 @@
     )(tangent, risk, rank, squares)
 
 
-def weight_kernel(kf, messages, tangent, local, risk, cumulative, squares, weighted):
+def weight_kernel(kf, ex, *refs):
+    messages, (tangent, local, risk, cumulative, squares) = refs[:ex], refs[ex : ex + 5]
+    weighted, placed = refs[ex + 5 :]
     me = lax.axis_index("ex")
-    ex = messages.shape[0]
+    for i in range(ex):
+        placed[me ^ i] = messages[i][...]
     later = jnp.zeros((kf, 1), F32)
     own_later = later
     before = later
     hazard_before = jnp.zeros((1, 1), F32)
     for b in reversed(range(ex)):
-        plain = jnp.sum(messages[b, :kf], axis=1, keepdims=True)
-        scaled = jnp.sum(messages[b, kf : 2 * kf], axis=1, keepdims=True)
-        hazard_total = messages[b, 2 * kf : 2 * kf + 1, :1]
-        square_total = messages[b, 2 * kf + 1 : 2 * kf + 2, :1]
+        plain = jnp.sum(placed[b, :kf], axis=1, keepdims=True)
+        scaled = jnp.sum(placed[b, kf : 2 * kf], axis=1, keepdims=True)
+        hazard_total = placed[b, 2 * kf : 2 * kf + 1, :1]
+        square_total = placed[b, 2 * kf + 1 : 2 * kf + 2, :1]
         own_later = own_later + jnp.where(b > me, plain, 0.0)
         before = before + jnp.where(b < me, scaled + square_total * later, 0.0)
         hazard_before = hazard_before + jnp.where(b < me, hazard_total, 0.0)
@@ -329,34 +377,40 @@
 
 def weights(messages, tangent, local, risk, cumulative, squares):
     return pl.pallas_call(
-        functools.partial(weight_kernel, tangent.shape[0]),
-        in_specs=[VMEM] * 6,
+        functools.partial(weight_kernel, tangent.shape[0], len(messages)),
+        in_specs=[VMEM] * (len(messages) + 5),
         out_shape=jax.ShapeDtypeStruct(tangent.shape, BF16),
         out_specs=VMEM,
+        scratch_shapes=[pltpu.VMEM((len(messages),) + messages[0].shape, F32)],
         compiler_params=pltpu.CompilerParams(**PARAMS),
         name="weights",
-    )(messages, tangent, local, risk, cumulative, squares)
-
-
-def gradient_kernel(feat, kf, *refs):
-    parts, dosages, out, weighted = refs[:feat], refs[feat], refs[feat + 1], refs[feat + 2]
+    )(*messages, tangent, local, risk, cumulative, squares)
+
+
+def gradient_kernel(feat, ex, kf, *refs):
+    parts, dosages, outs = refs[:feat], refs[feat], refs[feat + 1 : feat + 1 + ex]
+    weighted, turned = refs[feat + 1 + ex :]
     me = lax.axis_index("feat")
+    place = lax.axis_index("ex")
     for i in range(feat):
         weighted[pl.ds(pl.multiple_of((me ^ i) * kf, kf), kf), :] = parts[i][...]
     total = jnp.dot(weighted[...], dosages[...], preferred_element_type=F32)
-    out[...] = total.T.reshape(out.shape)
+    turned[...] = total.T.reshape(turned.shape)
+    for i in range(ex):
+        outs[i][...] = turned[place ^ i]
 
 
 def gradients(parts, dosages, ex):
     feat = len(parts)
     kf, persons = parts[0].shape
     k, variants = kf * feat, dosages.shape[1]
-    return pl.pallas_call(
-        functools.partial(gradient_kernel, feat, kf),
+    piece = (variants // ex, k)
+    return pl.pallas_call(
+        functools.partial(gradient_kernel, feat, ex, kf),
         in_specs=[VMEM] * (feat + 1),
-        out_shape=jax.ShapeDtypeStruct((ex, variants // ex, k), F32),
-        out_specs=VMEM,
-        scratch_shapes=[pltpu.VMEM((k, persons), BF16)],
+        out_shape=[jax.ShapeDtypeStruct(piece, F32)] * ex,
+        out_specs=[VMEM] * ex,
+        scratch_shapes=[pltpu.VMEM((k, persons), BF16), pltpu.VMEM((ex,) + piece, F32)],
         compiler_params=pltpu.CompilerParams(**PARAMS),
         cost_estimate=pl.CostEstimate(
             flops=2 * persons * variants * k, bytes_accessed=persons * (variants * 2 + k * 2), transcendentals=0
@@ -365,23 +419,47 @@
     )(*parts, dosages)
 
 
-def finish_kernel(pieces, count, out):
-    total = pieces[0]
-    for b in range(1, pieces.shape[0]):
-        total = total + pieces[b]
-    total = total / count[0:1, 0:1]
-    out[...] = jnp.broadcast_to(total[None], out.shape)
+def finish_kernel(ex, *refs):
+    pieces, count, out = refs[:ex], refs[ex], refs[ex + 1]
+    total = pieces[0][...]
+    for piece in pieces[1:]:
+        total = total + piece[...]
+    out[...] = total / count[1:2, 0:1]
 
 
 def finish(pieces, count):
     return pl.pallas_call(
-        finish_kernel,
-        in_specs=[VMEM] * 2,
-        out_shape=jax.ShapeDtypeStruct(pieces.shape, F32),
+        functools.partial(finish_kernel, len(pieces)),
+        in_specs=[VMEM] * (len(pieces) + 1),
+        out_shape=jax.ShapeDtypeStruct(pieces[0].shape, F32),
         out_specs=VMEM,
         compiler_params=pltpu.CompilerParams(**PARAMS),
         name="finish",
-    )(pieces, count)
+    )(*pieces, count)
+
+
+def place_kernel(ex, *refs):
+    parts, out, sems = refs[:ex], refs[ex], refs[ex + 1]
+    me = lax.axis_index("ex")
+    copies = [pltpu.make_async_copy(parts[i], out.at[me ^ i], sems.at[i]) for i in range(ex)]
+    for copy in copies:
+        copy.start()
+    for copy in copies:
+        copy.wait()
+
+
+def place_all(parts):
+    ex = len(parts)
+    out = pl.pallas_call(
+        functools.partial(place_kernel, ex),
+        in_specs=[VMEM] * ex,
+        out_shape=jax.ShapeDtypeStruct((ex,) + parts[0].shape, F32),
+        out_specs=HBM,
+        scratch_shapes=[pltpu.SemaphoreType.DMA((ex,))],
+        compiler_params=pltpu.CompilerParams(**PARAMS),
+        name="place",
+    )(*parts)
+    return out.reshape(-1, parts[0].shape[1])
 
 
 def local(dosages, coefficients, directions, event_rank, events):
@@ -396,29 +474,39 @@
     rank, event_row = event_rank[None], events[None]
 
     linear, keep, send = products(dosages, coefficients, directions, feat)
-    order = list(range(1, feat // 2)) + [0]
-    joined = {q: (keep[q], swap(send[q], "feat", 1)) for q in order}
-    others = [swap(joined[q][0] + joined[q][1], "feat", 2 * q) for q in order[:-1]]
-
-    risk, sums, ordered_events, message = risks(exchange(linear, "feat"), rank, event_row, rows, ex)
-    cumulative, squares, ordered_squares, hazard_message, count = hazards(
-        exchange(message, "ex"), sums, ordered_events, rank, rows
+    received = [swap(piece, "feat", 1) for piece in send]
+    linear = pair(linear, received[1])
+    linears = [linear] + [swap(linear, "feat", 2 * q) for q in range(1, feat // 2)]
+    joined = join(keep[1:], received[1:], linears[1:])
+    others = [swap(joined[q - 1], "feat", 2 * q) for q in reversed(range(1, feat // 2))]
+
+    risk, sums, ordered_events, total = risks(linears, rank, event_row, rows)
+    later = jnp.zeros_like(total)
+    bit = 1
+    while bit < ex:
+        other = swap(total, "ex", bit)
+        later = later + jnp.where((lax.axis_index("ex") & bit) == 0, other, 0.0)
+        total = total + other
+        bit *= 2
+    cumulative, squares, ordered_squares, hazard_message = hazards(
+        later, sums, ordered_events, rank, rows
     )
 
-    tangent, message = block_totals(list(joined[0]) + others, risk, squares, hazard_message, ex)
-    messages = exchange(message, "ex")
+    tangent, message = block_totals([keep[0], received[0]] + others, risk, squares, hazard_message)
+    messages = [message] + [swap(message, "ex", i) for i in range(1, ex)]
     summed = scans(tangent, risk, rank, ordered_squares)
     own = weights(messages, tangent, summed, risk, cumulative, squares)
 
     chips = {0: own}
-    for q in order[:-1]:
+    for q in reversed(range(1, feat // 2)):
         chips[q] = swap(own, "feat", 2 * q)
     parts = []
     for q in range(feat // 2):
         parts += [chips[q], swap(chips[q], "feat", 1)]
 
-    pieces = exchange(gradients(parts, dosages, ex), "ex")
-    result = exchange(finish(pieces, count), "ex").reshape(variants, -1)
+    pieces = gradients(parts, dosages, ex)
+    mine = finish([pieces[0]] + [swap(pieces[i], "ex", i) for i in range(1, ex)], total)
+    result = place_all([mine] + [swap(mine, "ex", i) for i in range(1, ex)])
     if padded != each:
         result = result.reshape(variants, feat, padded)[:, :, :each].reshape(variants, k)
     return result

time: 90 us -> 74.1 us (0.82)
  blocking collectives: 48.5 us -> 0 us
  waiting for transfers between devices: 5.7 us -> 23.8 us
  starting transfers between devices: 13.3 us -> 30.7 us
  Pallas kernels: 17.3 us -> 15.5 us
    all_to_all x4 -> x0, blocking collectives: 48.5 us -> none  [exchange(): return lax.all_to_all(x, axis, 0, 0)]
    ppermute x14 -> x28, starting transfers between devices: 9.97 us -> 30.7 us  [swap(): return lax.ppermute(x, axis, [(s, s ^ i) for s in range(count)])]
    ppermute x14 -> x28, waiting for transfers between devices: 5.69 us -> 23.8 us  [swap(): return lax.ppermute(x, axis, [(s, s ^ i) for s in range(count)])]
    all_to_all x1 -> x0, starting transfers between devices: 3.29 us -> none  [exchange(): return lax.all_to_all(x, axis, 0, 0)]
    pallas_call x5 -> x8, Pallas kernels: 9.05 us -> 7.93 us  [the longest x1 4.68 us: products(): pl.pallas_call(functools.partial(product_kernel, feat, kf, chunk), in_spe...]
    unnamed x9 -> x10, local copies, waits for them, and re-layouts: 3.8 us -> 3.1 us
  transfers between devices with their start and end apart: 15 -> 28, of which waited for: 5 -> 14; matrix products, arithmetic and copies ran while one was open for 0% -> 0% of each run, Pallas kernels for 10% -> 12%
where the time goes in v3:
time: 74.1 us; the launch traced here: 74 us
  starting transfers between devices  30.7 us (41%)
  waiting for transfers between devices  23.8 us (32%)
  Pallas kernels  15.5 us (21%)
  local copies, waits for them, and re-layouts  3.78 us (5%)
    ppermute x28, starting transfers between devices, swap(): return lax.ppermute(x, axis, [(s, s ^ i) for s in range(count)])  30.7 us
    ppermute x28, waiting for transfers between devices, swap(): return lax.ppermute(x, axis, [(s, s ^ i) for s in range(count)])  23.8 us
    pallas_call x1, Pallas kernels, scans(): pl.pallas_call(functools.partial(scan_kernel, rows, kf), in_specs=[VMEM]...  5.74 us
    pallas_call x1, Pallas kernels, products(): pl.pallas_call(functools.partial(product_kernel, feat, kf, chunk), in_spe...  4.68 us
    unnamed x10, local copies, waits for them, and re-layouts  3.1 us
    pallas_call x1, Pallas kernels, hazards(): pl.pallas_call(functools.partial(hazard_kernel, rows), in_specs=[VMEM] *...  1.76 us
  transfers between devices with their start and end apart: 28, of which 14 were waited for; matrix products, arithmetic and copies ran while one was open for 0% of the time, Pallas kernels for 12%

profile of v3, /device:TPU:0, one launch (start us, length us, event | category | flops | bytes accessed | tf_op | source)
XLA Modules:
  0.0 74.0 jit_solution(18243646314871329041)
XLA Ops:
  0.7 2.2 %copy-done = bf16[4096,512]{1,0:T(8,128)(2,1)S(1)} copy-done((bf16[4096,512]{1,0:T(8,128)(2,1)S(1)}, bf16[4096,512]{1,0:T(8,128)(2,1)}, u32[]{:S(2)}) %copy-start) | copy-done | bytes 4194328
  3.8 4.7 %products.1 = (f32[1,4096]{1,0:T(1,128)S(1)}, f32[16,4096]{1,0:T(8,128)S(1)}, f32[16,4096]{1,0:T(8,128)S(1)}, f32[16,4096]{1,0:T(8,128)S(1)}, f32[16,4096]{1,0:T...) custom-call(bf16[512,128]{1,0:T(8,128)(2,1)S(1)} %copy-done.2, ...), custom_call_target="tpu_custom_call" | custom-call | flops 536870912 | bytes 6291456 | tf_op jit(solution)/shard_map/products/pallas_call | solution.py:109
  10.3 2.9 %collective-permute-start.4 = (f32[1,4096]{1,0:T(1,128)S(1)}, f32[1,4096]{1,0:T(1,128)S(1)}, u32[]{:S(2)}, u32[]{:S(2)}) collective-permute-start(f32[1,4096]{1,0:T(1,128)S(1)} %pair.1.refs_0_), channel_id=1, source_target_pairs={{0,2},{1,3},{2,0},{3,1},{4,6},{5,7},{6,4},{7,5},{8,10},{9,11},{10,... | collective-permute-start | bytes 49160 | tf_op jit(solution)/shard_map/ppermute | solution.py:22
  13.3 1.5 %collective-permute-start.5 = (f32[1,4096]{1,0:T(1,128)S(1)}, f32[1,4096]{1,0:T(1,128)S(1)}, u32[]{:S(2)}, u32[]{:S(2)}) collective-permute-start(f32[1,4096]{1,0:T(1,128)S(1)} %pair.1.refs_0_), channel_id=1, source_target_pairs={{0,4},{1,5},{2,6},{3,7},{4,0},{5,1},{6,2},{7,3},{8,12},{9,13},{10,... | collective-permute-start | bytes 49160 | tf_op jit(solution)/shard_map/ppermute | solution.py:22
  15.0 2.0 %collective-permute-done.5.refs_7_.refs_2_ = f32[1,4096]{1,0:T(1,128)S(1)} collective-permute-done((f32[1,4096]{1,0:T(1,128)S(1)}, f32[1,4096]{1,0:T(1,128)S(1)}, u32[]{:S(2)}, u32[]{:S(2)}) %collective-permute-start.5) | collective-permute-done | bytes 16416 | tf_op jit(solution)/shard_map/ppermute | solution.py:22
  17.0 2.4 %collective-permute-done.6.refs_8_.refs_3_ = f32[1,4096]{1,0:T(1,128)S(1)} collective-permute-done((f32[1,4096]{1,0:T(1,128)S(1)}, f32[1,4096]{1,0:T(1,128)S(1)}, u32[]{:S(2)}, u32[]{:S(2)}) %collective-permute-start.6) | collective-permute-done | bytes 16416 | tf_op jit(solution)/shard_map/ppermute | solution.py:22
  19.6 2.0 %collective-permute-start.8 = (f32[16,4096]{1,0:T(8,128)S(1)}, f32[16,4096]{1,0:T(8,128)S(1)}, u32[]{:S(2)}, u32[]{:S(2)}) collective-permute-start(f32[16,4096]{1,0:T(8,128)S(1)} %get-tuple-element.41), channel_id=1, source_target_pairs={{0,4},{1,5},{2,6},{3,7},{4,0},{5,1},{6,2},{7,3},{8,12},{9,13},{10,... | collective-permute-start | bytes 786440 | tf_op jit(solution)/shard_map/ppermute | solution.py:22
  21.6 1.5 %collective-permute-start.9 = (f32[16,4096]{1,0:T(8,128)S(1)}, f32[16,4096]{1,0:T(8,128)S(1)}, u32[]{:S(2)}, u32[]{:S(2)}) collective-permute-start(f32[16,4096]{1,0:T(8,128)S(1)} %get-tuple-element.42), channel_id=1, source_target_pairs={{0,2},{1,3},{2,0},{3,1},{4,6},{5,7},{6,4},{7,5},{8,10},{9,11},{10,... | collective-permute-start | bytes 786440 | tf_op jit(solution)/shard_map/ppermute | solution.py:22
  24.3 1.6 %collective-permute-start.10 = (f32[8,128]{1,0:T(8,128)S(1)}, f32[8,128]{1,0:T(8,128)S(1)}, u32[]{:S(2)}, u32[]{:S(2)}) collective-permute-start(f32[8,128]{1,0:T(8,128)S(1)} %get-tuple-element.44), channel_id=1, source_target_pairs={{0,8},{8,0},{16,24},{24,16},{1,9},{9,1},{17,25},{25,17},{2,10},{10... | collective-permute-start | bytes 12296 | tf_op jit(solution)/shard_map/ppermute | solution.py:22
  26.0 2.0 %collective-permute-done.10 = f32[8,128]{1,0:T(8,128)S(1)} collective-permute-done((f32[8,128]{1,0:T(8,128)S(1)}, f32[8,128]{1,0:T(8,128)S(1)}, u32[]{:S(2)}, u32[]{:S(2)}) %collective-permute-start.10) | collective-permute-done | bytes 4128 | tf_op jit(solution)/shard_map/ppermute | solution.py:22
  28.0 2.6 %collective-permute-start.11 = (f32[8,128]{1,0:T(8,128)S(1)}, f32[8,128]{1,0:T(8,128)S(1)}, u32[]{:S(2)}, u32[]{:S(2)}) collective-permute-start(f32[8,128]{1,0:T(8,128)S(1)} %add.9), channel_id=1, source_target_pairs={{0,16},{8,24},{16,0},{24,8},{1,17},{9,25},{17,1},{25,9},{2,18},{10... | collective-permute-start | bytes 12296 | tf_op jit(solution)/shard_map/ppermute | solution.py:22
  30.6 1.9 %collective-permute-done.11 = f32[8,128]{1,0:T(8,128)S(1)} collective-permute-done((f32[8,128]{1,0:T(8,128)S(1)}, f32[8,128]{1,0:T(8,128)S(1)}, u32[]{:S(2)}, u32[]{:S(2)}) %collective-permute-start.11) | collective-permute-done | bytes 4128 | tf_op jit(solution)/shard_map/ppermute | solution.py:22
  32.5 1.8 %hazards.1 = (f32[1,4096]{1,0:T(1,128)S(1)}, f32[1,4096]{1,0:T(1,128)S(1)}, f32[16,256]{1,0:T(8,128)S(1)}, f32[8,128]{1,0:T(8,128)S(1)}) custom-call(f32[8,128]{1,0:T(8,128)S(1)} %get-tuple-element.58.later, f32[16,256]{1,0:T(8,128)S(1)} %get-tuple-element.45.sums, f32[16,256]{1,0:T(8,128)S(1)} %get-tuple-element.46.events, s32[1,4096]{1,0:T(1,128)S(1)} %bitcast.5), custom_call_target="tpu_custom_call" | custom-call | flops 209715200 | bytes 262144 | tf_op jit(solution)/shard_map/hazards/pallas_call | solution.py:246
  34.4 1.6 %collective-permute-start.12 = (f32[40,128]{1,0:T(8,128)S(1)}, f32[40,128]{1,0:T(8,128)S(1)}, u32[]{:S(2)}, u32[]{:S(2)}) collective-permute-start(f32[40,128]{1,0:T(8,128)S(1)} %get-tuple-element.49.refs_0_), channel_id=1, source_target_pairs={{0,8},{8,0},{16,24},{24,16},{1,9},{9,1},{17,25},{25,17},{2,10},{10... | collective-permute-start | bytes 61448 | tf_op jit(solution)/shard_map/ppermute | solution.py:22
  36.1 2.6 %collective-permute-start.13 = (f32[40,128]{1,0:T(8,128)S(1)}, f32[40,128]{1,0:T(8,128)S(1)}, u32[]{:S(2)}, u32[]{:S(2)}) collective-permute-start(f32[40,128]{1,0:T(8,128)S(1)} %get-tuple-element.49.refs_0_), channel_id=1, source_target_pairs={{0,16},{8,24},{16,0},{24,8},{1,17},{9,25},{17,1},{25,9},{2,18},{10... | collective-permute-start | bytes 61448 | tf_op jit(solution)/shard_map/ppermute | solution.py:22
  38.9 5.7 %scans.1.refs_5_ = f32[16,4096]{1,0:T(8,128)S(1)} custom-call(f32[16,4096]{1,0:T(8,128)S(1)} %get-tuple-element.50.tangent.refs_4_, f32[1,4096]{1,0:T(1,128)S(1)} %get-tuple-element.43.refs_5_.risk.refs_6_, s32[1,4096]{1,0:T(1,128)S(1)} %bitcast.6, f32[16,256]{1,0:T(8,128)S(1)} %get-tuple-element.51.squares), custom_call_target="tpu_custom_call" | custom-call | flops 2147483648 | bytes 1572864 | tf_op jit(solution)/shard_map/scans/pallas_call | solution.py:341
  45.8 2.7 %collective-permute-start.20 = (bf16[16,4096]{1,0:T(8,128)(2,1)S(1)}, bf16[16,4096]{1,0:T(8,128)(2,1)S(1)}, u32[]{:S(2)}, u32[]{:S(2)}) collective-permute-start(bf16[16,4096]{1,0:T(8,128)(2,1)S(1)} %weights.1.refs_0_), channel_id=1, source_target_pairs={{0,6},{1,7},{2,4},{3,5},{4,2},{5,3},{6,0},{7,1},{8,14},{9,15},{10,... | collective-permute-start | bytes 393224 | tf_op jit(solution)/shard_map/ppermute | solution.py:22
  49.9 1.9 %collective-permute-done.18.refs_4_ = bf16[16,4096]{1,0:T(8,128)(2,1)S(1)} collective-permute-done((bf16[16,4096]{1,0:T(8,128)(2,1)S(1)}, bf16[16,4096]{1,0:T(8,128)(2,1)S(1)}, u32[]{:S(2)}, u32[]{:S(2)}) %collective-permute-start.18) | collective-permute-done | bytes 131104 | tf_op jit(solution)/shard_map/ppermute | solution.py:22
  54.9 3.5 %collective-permute-start.23 = (f32[128,128]{1,0:T(8,128)S(1)}, f32[128,128]{1,0:T(8,128)S(1)}, u32[]{:S(2)}, u32[]{:S(2)}) collective-permute-start(f32[128,128]{1,0:T(8,128)S(1)} %get-tuple-element.55), channel_id=1, source_target_pairs={{0,16},{8,24},{16,0},{24,8},{1,17},{9,25},{17,1},{25,9},{2,18},{10... | collective-permute-start | bytes 196616 | tf_op jit(solution)/shard_map/ppermute | solution.py:22
  58.8 3.7 %collective-permute-done.23.refs_2_ = f32[128,128]{1,0:T(8,128)S(1)} collective-permute-done((f32[128,128]{1,0:T(8,128)S(1)}, f32[128,128]{1,0:T(8,128)S(1)}, u32[]{:S(2)}, u32[]{:S(2)}) %collective-permute-start.23) | collective-permute-done | bytes 65568 | tf_op jit(solution)/shard_map/ppermute | solution.py:22
  62.4 2.1 %collective-permute-done.24.refs_3_ = f32[128,128]{1,0:T(8,128)S(1)} collective-permute-done((f32[128,128]{1,0:T(8,128)S(1)}, f32[128,128]{1,0:T(8,128)S(1)}, u32[]{:S(2)}, u32[]{:S(2)}) %collective-permute-start.24) | collective-permute-done | bytes 65568 | tf_op jit(solution)/shard_map/ppermute | solution.py:22
  65.4 1.7 %collective-permute-start.26 = (f32[128,128]{1,0:T(8,128)S(1)}, f32[128,128]{1,0:T(8,128)S(1)}, u32[]{:S(2)}, u32[]{:S(2)}) collective-permute-start(f32[128,128]{1,0:T(8,128)S(1)} %finish.1.refs_0_), channel_id=1, source_target_pairs={{0,16},{8,24},{16,0},{24,8},{1,17},{9,25},{17,1},{25,9},{2,18},{10... | collective-permute-start | bytes 196616 | tf_op jit(solution)/shard_map/ppermute | solution.py:22
  67.1 1.9 %collective-permute-start.27 = (f32[128,128]{1,0:T(8,128)S(1)}, f32[128,128]{1,0:T(8,128)S(1)}, u32[]{:S(2)}, u32[]{:S(2)}) collective-permute-start(f32[128,128]{1,0:T(8,128)S(1)} %finish.1.refs_0_), channel_id=1, source_target_pairs={{0,24},{8,16},{16,8},{24,0},{1,25},{9,17},{17,9},{25,1},{2,26},{10... | collective-permute-start | bytes 196616 | tf_op jit(solution)/shard_map/ppermute | solution.py:22
  69.1 2.8 %collective-permute-done.26.refs_2_ = f32[128,128]{1,0:T(8,128)S(1)} collective-permute-done((f32[128,128]{1,0:T(8,128)S(1)}, f32[128,128]{1,0:T(8,128)S(1)}, u32[]{:S(2)}, u32[]{:S(2)}) %collective-permute-start.26) | collective-permute-done | bytes 65568 | tf_op jit(solution)/shard_map/ppermute | solution.py:22
  (56 shorter events, 14.4 us)
Async XLA Ops:
  9.0 5.8 %collective-permute-start.2 = (f32[16,4096]{1,0:T(8,128)S(1)}, f32[16,4096]{1,0:T(8,128)S(1)}, u32[]{:S(2)}, u32[]{:S(2)}) collective-permute-start(f32[16,4096]{1,0:T(8,128)S(1)} %get-tuple-element.37), channel_id=1, source_target_pairs={{0,1},{1,0},{2,3},{3,2},{4,5},{5,4},{6,7},{7,6},{8,9},{9,8},{10,11... | collective-permute-start | bytes 786440 | tf_op jit(solution)/shard_map/ppermute | solution.py:22
  9.1 5.8 %collective-permute-start.3 = (f32[16,4096]{1,0:T(8,128)S(1)}, f32[16,4096]{1,0:T(8,128)S(1)}, u32[]{:S(2)}, u32[]{:S(2)}) collective-permute-start(f32[16,4096]{1,0:T(8,128)S(1)} %get-tuple-element.38), channel_id=1, source_target_pairs={{0,1},{1,0},{2,3},{3,2},{4,5},{5,4},{6,7},{7,6},{8,9},{9,8},{10,11... | collective-permute-start | bytes 786440 | tf_op jit(solution)/shard_map/ppermute | solution.py:22
  10.3 4.6 %collective-permute-start.4 = (f32[1,4096]{1,0:T(1,128)S(1)}, f32[1,4096]{1,0:T(1,128)S(1)}, u32[]{:S(2)}, u32[]{:S(2)}) collective-permute-start(f32[1,4096]{1,0:T(1,128)S(1)} %pair.1.refs_0_), channel_id=1, source_target_pairs={{0,2},{1,3},{2,0},{3,1},{4,6},{5,7},{6,4},{7,5},{8,10},{9,11},{10,... | collective-permute-start | bytes 49160 | tf_op jit(solution)/shard_map/ppermute | solution.py:22
  13.3 3.7 %collective-permute-start.5 = (f32[1,4096]{1,0:T(1,128)S(1)}, f32[1,4096]{1,0:T(1,128)S(1)}, u32[]{:S(2)}, u32[]{:S(2)}) collective-permute-start(f32[1,4096]{1,0:T(1,128)S(1)} %pair.1.refs_0_), channel_id=1, source_target_pairs={{0,4},{1,5},{2,6},{3,7},{4,0},{5,1},{6,2},{7,3},{8,12},{9,13},{10,... | collective-permute-start | bytes 49160 | tf_op jit(solution)/shard_map/ppermute | solution.py:22
  14.8 4.6 %collective-permute-start.6 = (f32[1,4096]{1,0:T(1,128)S(1)}, f32[1,4096]{1,0:T(1,128)S(1)}, u32[]{:S(2)}, u32[]{:S(2)}) collective-permute-start(f32[1,4096]{1,0:T(1,128)S(1)} %pair.1.refs_0_), channel_id=1, source_target_pairs={{0,6},{1,7},{2,4},{3,5},{4,2},{5,3},{6,0},{7,1},{8,14},{9,15},{10,... | collective-permute-start | bytes 49160 | tf_op jit(solution)/shard_map/ppermute | solution.py:22
  14.8 19.5 %collective-permute-start = (f32[16,4096]{1,0:T(8,128)S(1)}, f32[16,4096]{1,0:T(8,128)S(1)}, u32[]{:S(2)}, u32[]{:S(2)}) collective-permute-start(f32[16,4096]{1,0:T(8,128)S(1)} %get-tuple-element.32), channel_id=1, source_target_pairs={{0,1},{1,0},{2,3},{3,2},{4,5},{5,4},{6,7},{7,6},{8,9},{9,8},{10,11... | collective-permute-start | bytes 786440 | tf_op jit(solution)/shard_map/ppermute | solution.py:22
  19.5 14.8 %collective-permute-start.7 = (f32[16,4096]{1,0:T(8,128)S(1)}, f32[16,4096]{1,0:T(8,128)S(1)}, u32[]{:S(2)}, u32[]{:S(2)}) collective-permute-start(f32[16,4096]{1,0:T(8,128)S(1)} %get-tuple-element.40), channel_id=1, source_target_pairs={{0,6},{1,7},{2,4},{3,5},{4,2},{5,3},{6,0},{7,1},{8,14},{9,15},{10,... | collective-permute-start | bytes 786440 | tf_op jit(solution)/shard_map/ppermute | solution.py:22
  19.6 14.7 %collective-permute-start.8 = (f32[16,4096]{1,0:T(8,128)S(1)}, f32[16,4096]{1,0:T(8,128)S(1)}, u32[]{:S(2)}, u32[]{:S(2)}) collective-permute-start(f32[16,4096]{1,0:T(8,128)S(1)} %get-tuple-element.41), channel_id=1, source_target_pairs={{0,4},{1,5},{2,6},{3,7},{4,0},{5,1},{6,2},{7,3},{8,12},{9,13},{10,... | collective-permute-start | bytes 786440 | tf_op jit(solution)/shard_map/ppermute | solution.py:22
  21.6 12.7 %collective-permute-start.9 = (f32[16,4096]{1,0:T(8,128)S(1)}, f32[16,4096]{1,0:T(8,128)S(1)}, u32[]{:S(2)}, u32[]{:S(2)}) collective-permute-start(f32[16,4096]{1,0:T(8,128)S(1)} %get-tuple-element.42), channel_id=1, source_target_pairs={{0,2},{1,3},{2,0},{3,1},{4,6},{5,7},{6,4},{7,5},{8,10},{9,11},{10,... | collective-permute-start | bytes 786440 | tf_op jit(solution)/shard_map/ppermute | solution.py:22
  24.3 3.7 %collective-permute-start.10 = (f32[8,128]{1,0:T(8,128)S(1)}, f32[8,128]{1,0:T(8,128)S(1)}, u32[]{:S(2)}, u32[]{:S(2)}) collective-permute-start(f32[8,128]{1,0:T(8,128)S(1)} %get-tuple-element.44), channel_id=1, source_target_pairs={{0,8},{8,0},{16,24},{24,16},{1,9},{9,1},{17,25},{25,17},{2,10},{10... | collective-permute-start | bytes 12296 | tf_op jit(solution)/shard_map/ppermute | solution.py:22
  28.0 4.5 %collective-permute-start.11 = (f32[8,128]{1,0:T(8,128)S(1)}, f32[8,128]{1,0:T(8,128)S(1)}, u32[]{:S(2)}, u32[]{:S(2)}) collective-permute-start(f32[8,128]{1,0:T(8,128)S(1)} %add.9), channel_id=1, source_target_pairs={{0,16},{8,24},{16,0},{24,8},{1,17},{9,25},{17,1},{25,9},{2,18},{10... | collective-permute-start | bytes 12296 | tf_op jit(solution)/shard_map/ppermute | solution.py:22
  34.4 10.2 %collective-permute-start.12 = (f32[40,128]{1,0:T(8,128)S(1)}, f32[40,128]{1,0:T(8,128)S(1)}, u32[]{:S(2)}, u32[]{:S(2)}) collective-permute-start(f32[40,128]{1,0:T(8,128)S(1)} %get-tuple-element.49.refs_0_), channel_id=1, source_target_pairs={{0,8},{8,0},{16,24},{24,16},{1,9},{9,1},{17,25},{25,17},{2,10},{10... | collective-permute-start | bytes 61448 | tf_op jit(solution)/shard_map/ppermute | solution.py:22
  36.1 8.6 %collective-permute-start.13 = (f32[40,128]{1,0:T(8,128)S(1)}, f32[40,128]{1,0:T(8,128)S(1)}, u32[]{:S(2)}, u32[]{:S(2)}) collective-permute-start(f32[40,128]{1,0:T(8,128)S(1)} %get-tuple-element.49.refs_0_), channel_id=1, source_target_pairs={{0,16},{8,24},{16,0},{24,8},{1,17},{9,25},{17,1},{25,9},{2,18},{10... | collective-permute-start | bytes 61448 | tf_op jit(solution)/shard_map/ppermute | solution.py:22
  38.7 6.0 %collective-permute-start.14 = (f32[40,128]{1,0:T(8,128)S(1)}, f32[40,128]{1,0:T(8,128)S(1)}, u32[]{:S(2)}, u32[]{:S(2)}) collective-permute-start(f32[40,128]{1,0:T(8,128)S(1)} %get-tuple-element.49.refs_0_), channel_id=1, source_target_pairs={{0,24},{8,16},{16,8},{24,0},{1,25},{9,17},{17,9},{25,1},{2,26},{10... | collective-permute-start | bytes 61448 | tf_op jit(solution)/shard_map/ppermute | solution.py:22
  44.9 5.0 %collective-permute-start.16 = (bf16[16,4096]{1,0:T(8,128)(2,1)S(1)}, bf16[16,4096]{1,0:T(8,128)(2,1)S(1)}, u32[]{:S(2)}, u32[]{:S(2)}) collective-permute-start(bf16[16,4096]{1,0:T(8,128)(2,1)S(1)} %weights.1.refs_0_), channel_id=1, source_target_pairs={{0,2},{1,3},{2,0},{3,1},{4,6},{5,7},{6,4},{7,5},{8,10},{9,11},{10,... | collective-permute-start | bytes 393224 | tf_op jit(solution)/shard_map/ppermute | solution.py:22
  45.5 6.4 %collective-permute-start.18 = (bf16[16,4096]{1,0:T(8,128)(2,1)S(1)}, bf16[16,4096]{1,0:T(8,128)(2,1)S(1)}, u32[]{:S(2)}, u32[]{:S(2)}) collective-permute-start(bf16[16,4096]{1,0:T(8,128)(2,1)S(1)} %weights.1.refs_0_), channel_id=1, source_target_pairs={{0,4},{1,5},{2,6},{3,7},{4,0},{5,1},{6,2},{7,3},{8,12},{9,13},{10,... | collective-permute-start | bytes 393224 | tf_op jit(solution)/shard_map/ppermute | solution.py:22
  45.8 6.1 %collective-permute-start.20 = (bf16[16,4096]{1,0:T(8,128)(2,1)S(1)}, bf16[16,4096]{1,0:T(8,128)(2,1)S(1)}, u32[]{:S(2)}, u32[]{:S(2)}) collective-permute-start(bf16[16,4096]{1,0:T(8,128)(2,1)S(1)} %weights.1.refs_0_), channel_id=1, source_target_pairs={{0,6},{1,7},{2,4},{3,5},{4,2},{5,3},{6,0},{7,1},{8,14},{9,15},{10,... | collective-permute-start | bytes 393224 | tf_op jit(solution)/shard_map/ppermute | solution.py:22
  48.5 3.9 %collective-permute-start.15 = (bf16[16,4096]{1,0:T(8,128)(2,1)S(1)}, bf16[16,4096]{1,0:T(8,128)(2,1)S(1)}, u32[]{:S(2)}, u32[]{:S(2)}) collective-permute-start(bf16[16,4096]{1,0:T(8,128)(2,1)S(1)} %weights.1.refs_0_), channel_id=1, source_target_pairs={{0,1},{1,0},{2,3},{3,2},{4,5},{5,4},{6,7},{7,6},{8,9},{9,8},{10,11... | collective-permute-start | bytes 393224 | tf_op jit(solution)/shard_map/ppermute | solution.py:22
  54.3 4.5 %collective-permute-start.22 = (f32[128,128]{1,0:T(8,128)S(1)}, f32[128,128]{1,0:T(8,128)S(1)}, u32[]{:S(2)}, u32[]{:S(2)}) collective-permute-start(f32[128,128]{1,0:T(8,128)S(1)} %get-tuple-element.54), channel_id=1, source_target_pairs={{0,8},{8,0},{16,24},{24,16},{1,9},{9,1},{17,25},{25,17},{2,10},{10... | collective-permute-start | bytes 196616 | tf_op jit(solution)/shard_map/ppermute | solution.py:22
  54.9 7.6 %collective-permute-start.23 = (f32[128,128]{1,0:T(8,128)S(1)}, f32[128,128]{1,0:T(8,128)S(1)}, u32[]{:S(2)}, u32[]{:S(2)}) collective-permute-start(f32[128,128]{1,0:T(8,128)S(1)} %get-tuple-element.55), channel_id=1, source_target_pairs={{0,16},{8,24},{16,0},{24,8},{1,17},{9,25},{17,1},{25,9},{2,18},{10... | collective-permute-start | bytes 196616 | tf_op jit(solution)/shard_map/ppermute | solution.py:22
  58.4 6.2 %collective-permute-start.24 = (f32[128,128]{1,0:T(8,128)S(1)}, f32[128,128]{1,0:T(8,128)S(1)}, u32[]{:S(2)}, u32[]{:S(2)}) collective-permute-start(f32[128,128]{1,0:T(8,128)S(1)} %get-tuple-element.56), channel_id=1, source_target_pairs={{0,24},{8,16},{16,8},{24,0},{1,25},{9,17},{17,9},{25,1},{2,26},{10... | collective-permute-start | bytes 196616 | tf_op jit(solution)/shard_map/ppermute | solution.py:22
  64.6 4.5 %collective-permute-start.25 = (f32[128,128]{1,0:T(8,128)S(1)}, f32[128,128]{1,0:T(8,128)S(1)}, u32[]{:S(2)}, u32[]{:S(2)}) collective-permute-start(f32[128,128]{1,0:T(8,128)S(1)} %finish.1.refs_0_), channel_id=1, source_target_pairs={{0,8},{8,0},{16,24},{24,16},{1,9},{9,1},{17,25},{25,17},{2,10},{10... | collective-permute-start | bytes 196616 | tf_op jit(solution)/shard_map/ppermute | solution.py:22
  65.4 6.4 %collective-permute-start.26 = (f32[128,128]{1,0:T(8,128)S(1)}, f32[128,128]{1,0:T(8,128)S(1)}, u32[]{:S(2)}, u32[]{:S(2)}) collective-permute-start(f32[128,128]{1,0:T(8,128)S(1)} %finish.1.refs_0_), channel_id=1, source_target_pairs={{0,16},{8,24},{16,0},{24,8},{1,17},{9,25},{17,1},{25,9},{2,18},{10... | collective-permute-start | bytes 196616 | tf_op jit(solution)/shard_map/ppermute | solution.py:22
  67.1 6.1 %collective-permute-start.27 = (f32[128,128]{1,0:T(8,128)S(1)}, f32[128,128]{1,0:T(8,128)S(1)}, u32[]{:S(2)}, u32[]{:S(2)}) collective-permute-start(f32[128,128]{1,0:T(8,128)S(1)} %finish.1.refs_0_), channel_id=1, source_target_pairs={{0,24},{8,16},{16,8},{24,0},{1,25},{9,17},{17,9},{25,1},{2,26},{10... | collective-permute-start | bytes 196616 | tf_op jit(solution)/shard_map/ppermute | solution.py:22
  (9 other events, 63.4 us)

commit v4 on v3

--- a/solution.py
+++ b/solution.py
@@ -10,10 +10,12 @@
 F32 = jnp.float32
 BF16 = jnp.bfloat16
 LO = 256
+BLOCK = 64
 NT = (((1,), (1,)), ((), ()))
 VMEM = pl.BlockSpec(memory_space=pltpu.VMEM)
 HIGHEST = lax.Precision.HIGHEST
 HBM = pl.BlockSpec(memory_space=pltpu.HBM)
+PRODUCT_BYTES = 48 * 1024 * 1024
 PARAMS = dict(vmem_limit_bytes=24 * 1024 * 1024)
 
 
@@ -78,19 +80,17 @@
         copy.start()
     for copy in small:
         copy.wait()
-    turned[...] = own_directions[...].astype(F32).T.reshape(turned.shape)
-    placed = jnp.concatenate([turned[me ^ i] for i in range(feat)], axis=0)
-    rhs[:, :width] = placed.T.astype(BF16)
-    spread = jnp.broadcast_to(own_coefficients[...].astype(F32), (128, variants))
+    rhs[:, :width] = own_directions[...]
+    spread = jnp.broadcast_to(own_coefficients[...].astype(F32)[None, :], (128, variants))
     rhs[:, width:] = spread.T.astype(BF16)
     diagonal = triangle(128, lambda a, b: a == b)
     for i in range(steps):
         large[i].wait()
         at = slice(i * chunk, (i + 1) * chunk)
         result = jnp.dot(table[at], rhs[...], preferred_element_type=F32)
-        tangent = result[:, :width].T
+        turned[i] = result[:, :width].T.reshape(feat, kf, chunk)
         for j in range(feat):
-            (send if j % 2 else keep)[j // 2][:kf, at] = tangent[j * kf : (j + 1) * kf]
+            (send if j % 2 else keep)[j // 2][:kf, at] = turned[i, me ^ j]
         for start in range(0, chunk, 128):
             block = result[start : start + 128, width:]
             row = jnp.sum(block * diagonal, axis=0, keepdims=True)
@@ -117,17 +117,17 @@
         scratch_shapes=[
             pltpu.VMEM((persons, variants), BF16),
             pltpu.VMEM((variants, k), BF16),
-            pltpu.VMEM((1, variants), BF16),
+            pltpu.VMEM((variants,), BF16),
             pltpu.VMEM((variants, k + 128), BF16),
-            pltpu.VMEM((feat, kf, variants), F32),
+            pltpu.VMEM((persons // chunk, feat, kf, chunk), F32),
             pltpu.SemaphoreType.DMA((persons // chunk + 2,)),
         ],
-        compiler_params=pltpu.CompilerParams(**PARAMS),
+        compiler_params=pltpu.CompilerParams(vmem_limit_bytes=PRODUCT_BYTES),
         cost_estimate=pl.CostEstimate(
             flops=2 * persons * variants * k, bytes_accessed=persons * (variants * 2 + k * 4), transcendentals=0
         ),
         name="products",
-    )(directions, coefficients[None], dosages)
+    )(directions, coefficients, dosages)
     return out[0], out[1 : 1 + feat // 2], out[1 + feat // 2 :]
 
 
@@ -387,30 +387,49 @@
     )(*messages, tangent, local, risk, cumulative, squares)
 
 
-def gradient_kernel(feat, ex, kf, *refs):
-    parts, dosages, outs = refs[:feat], refs[feat], refs[feat + 1 : feat + 1 + ex]
-    weighted, turned = refs[feat + 1 + ex :]
+def encode(values, message):
+    height = values.shape[0]
+    block = min(BLOCK, height)
+    powers = []
+    for start in range(0, height, block):
+        part = values[start : start + block]
+        largest = jnp.max(jnp.abs(part), axis=0, keepdims=True)
+        power = jnp.ceil(jnp.log2(jnp.maximum(largest, 1e-30))) - 14.0
+        message[start : start + block] = jnp.round(part * jnp.exp2(-power)).astype(jnp.int32).astype(jnp.int16)
+        powers.append(power)
+    powers.append(jnp.zeros((message.shape[0] - height - len(powers), values.shape[1]), F32))
+    message[height:] = jnp.concatenate(powers, axis=0).astype(jnp.int32).astype(jnp.int16)
+
+
+def decode(message, height):
+    block = min(BLOCK, height)
+    powers = message[height:].astype(jnp.int32).astype(F32)
+    parts = []
+    for i in range(height // block):
+        part = message[i * block : (i + 1) * block].astype(jnp.int32).astype(F32)
+        parts.append(part * jnp.exp2(powers[i : i + 1]))
+    return jnp.concatenate(parts, axis=0)
+
+
+def gradient_kernel(feat, kf, *refs):
+    parts, dosages, out, weighted = refs[:feat], refs[feat], refs[feat + 1], refs[feat + 2]
     me = lax.axis_index("feat")
-    place = lax.axis_index("ex")
     for i in range(feat):
         weighted[pl.ds(pl.multiple_of((me ^ i) * kf, kf), kf), :] = parts[i][...]
     total = jnp.dot(weighted[...], dosages[...], preferred_element_type=F32)
-    turned[...] = total.T.reshape(turned.shape)
-    for i in range(ex):
-        outs[i][...] = turned[place ^ i]
-
-
-def gradients(parts, dosages, ex):
+    encode(total.T, out)
+
+
+def gradients(parts, dosages):
     feat = len(parts)
     kf, persons = parts[0].shape
     k, variants = kf * feat, dosages.shape[1]
-    piece = (variants // ex, k)
-    return pl.pallas_call(
-        functools.partial(gradient_kernel, feat, ex, kf),
+    return pl.pallas_call(
+        functools.partial(gradient_kernel, feat, kf),
         in_specs=[VMEM] * (feat + 1),
-        out_shape=[jax.ShapeDtypeStruct(piece, F32)] * ex,
-        out_specs=[VMEM] * ex,
-        scratch_shapes=[pltpu.VMEM((k, persons), BF16), pltpu.VMEM((ex,) + piece, F32)],
+        out_shape=jax.ShapeDtypeStruct((variants + 16, k), jnp.int16),
+        out_specs=VMEM,
+        scratch_shapes=[pltpu.VMEM((k, persons), BF16)],
         compiler_params=pltpu.CompilerParams(**PARAMS),
         cost_estimate=pl.CostEstimate(
             flops=2 * persons * variants * k, bytes_accessed=persons * (variants * 2 + k * 2), transcendentals=0
@@ -419,47 +438,36 @@
     )(*parts, dosages)
 
 
-def finish_kernel(ex, *refs):
-    pieces, count, out = refs[:ex], refs[ex], refs[ex + 1]
-    total = pieces[0][...]
-    for piece in pieces[1:]:
-        total = total + piece[...]
-    out[...] = total / count[1:2, 0:1]
-
-
-def finish(pieces, count):
-    return pl.pallas_call(
-        functools.partial(finish_kernel, len(pieces)),
-        in_specs=[VMEM] * (len(pieces) + 1),
-        out_shape=jax.ShapeDtypeStruct(pieces[0].shape, F32),
+def merge_kernel(mine, other, out):
+    height = mine.shape[0] - 16
+    encode(decode(mine, height) + decode(other, height), out)
+
+
+def merge(mine, other):
+    return pl.pallas_call(
+        merge_kernel,
+        in_specs=[VMEM] * 2,
+        out_shape=jax.ShapeDtypeStruct(mine.shape, jnp.int16),
         out_specs=VMEM,
         compiler_params=pltpu.CompilerParams(**PARAMS),
+        name="merge",
+    )(mine, other)
+
+
+def finish_kernel(mine, other, count, out):
+    height = mine.shape[0] - 16
+    out[...] = (decode(mine, height) + decode(other, height)) / count[1:2, 0:1]
+
+
+def finish(mine, other, count):
+    return pl.pallas_call(
+        finish_kernel,
+        in_specs=[VMEM] * 3,
+        out_shape=jax.ShapeDtypeStruct((mine.shape[0] - 16, mine.shape[1]), F32),
+        out_specs=VMEM,
+        compiler_params=pltpu.CompilerParams(**PARAMS),
         name="finish",
-    )(*pieces, count)
-
-
-def place_kernel(ex, *refs):
-    parts, out, sems = refs[:ex], refs[ex], refs[ex + 1]
-    me = lax.axis_index("ex")
-    copies = [pltpu.make_async_copy(parts[i], out.at[me ^ i], sems.at[i]) for i in range(ex)]
-    for copy in copies:
-        copy.start()
-    for copy in copies:
-        copy.wait()
-
-
-def place_all(parts):
-    ex = len(parts)
-    out = pl.pallas_call(
-        functools.partial(place_kernel, ex),
-        in_specs=[VMEM] * ex,
-        out_shape=jax.ShapeDtypeStruct((ex,) + parts[0].shape, F32),
-        out_specs=HBM,
-        scratch_shapes=[pltpu.SemaphoreType.DMA((ex,))],
-        compiler_params=pltpu.CompilerParams(**PARAMS),
-        name="place",
-    )(*parts)
-    return out.reshape(-1, parts[0].shape[1])
+    )(mine, other, count)
 
 
 def local(dosages, coefficients, directions, event_rank, events):
@@ -504,9 +512,12 @@
     for q in range(feat // 2):
         parts += [chips[q], swap(chips[q], "feat", 1)]
 
-    pieces = gradients(parts, dosages, ex)
-    mine = finish([pieces[0]] + [swap(pieces[i], "ex", i) for i in range(1, ex)], total)
-    result = place_all([mine] + [swap(mine, "ex", i) for i in range(1, ex)])
+    partial_sum = gradients(parts, dosages)
+    bit = 1
+    while 2 * bit < ex:
+        partial_sum = merge(partial_sum, swap(partial_sum, "ex", bit))
+        bit *= 2
+    result = finish(partial_sum, swap(partial_sum, "ex", bit), total)
     if padded != each:
         result = result.reshape(variants, feat, padded)[:, :, :each].reshape(variants, k)
     return result

time: 74.1 us -> 68.7 us (0.927)
  starting transfers between devices: 30.7 us -> 24.5 us
  local copies, waits for them, and re-layouts: 3.78 us -> 1.59 us
  waiting for transfers between devices: 23.8 us -> 25.9 us
  Pallas kernels: 15.5 us -> 16.4 us
    ppermute x28 -> x24, starting transfers between devices: 30.7 us -> 24.5 us  [swap(): return lax.ppermute(x, axis, [(s, s ^ i) for s in range(count)])]
    ppermute x28 -> x24, waiting for transfers between devices: 23.8 us -> 25.9 us  [swap(): return lax.ppermute(x, axis, [(s, s ^ i) for s in range(count)])]
    unnamed x10, local copies, waits for them, and re-layouts: 3.1 us -> 1.59 us
  transfers between devices with their start and end apart: 28 -> 24, of which waited for: 14 -> 12; matrix products, arithmetic and copies ran while one was open for 0% -> 0% of each run, Pallas kernels for 12% -> 13%
where the time goes in v4:
time: 68.7 us; the launch traced here: 68.5 us
  waiting for transfers between devices  25.9 us (38%)
  starting transfers between devices  24.5 us (36%)
  Pallas kernels  16.4 us (24%)
  local copies, waits for them, and re-layouts  1.59 us (2%)
    ppermute x24, waiting for transfers between devices, swap(): return lax.ppermute(x, axis, [(s, s ^ i) for s in range(count)])  25.9 us
    ppermute x24, starting transfers between devices, swap(): return lax.ppermute(x, axis, [(s, s ^ i) for s in range(count)])  24.5 us
    pallas_call x1, Pallas kernels, scans(): pl.pallas_call(functools.partial(scan_kernel, rows, kf), in_specs=[VMEM]...  5.75 us
    pallas_call x1, Pallas kernels, products(): pl.pallas_call(functools.partial(product_kernel, feat, kf, chunk), in_spe...  5.33 us
    pallas_call x1, Pallas kernels, hazards(): pl.pallas_call(functools.partial(hazard_kernel, rows), in_specs=[VMEM] *...  1.76 us
    unnamed x10, local copies, waits for them, and re-layouts  1.59 us
  transfers between devices with their start and end apart: 24, of which 12 were waited for; matrix products, arithmetic and copies ran while one was open for 0% of the time, Pallas kernels for 13%

profile of v4, /device:TPU:0, one launch (start us, length us, event | category | flops | bytes accessed | tf_op | source)
XLA Modules:
  0.0 68.5 jit_solution(16155387219478928499)
XLA Ops:
  0.0 0.9 %copy-done.1 = bf16[512,128]{1,0:T(8,128)(2,1)S(1)} copy-done((bf16[512,128]{1,0:T(8,128)(2,1)S(1)}, bf16[512,128]{1,0:T(8,128)(2,1)}, u32[]{:S(2)}) %copy-start.1) | copy-done | bytes 131096
  1.6 5.3 %products.1 = (f32[1,4096]{1,0:T(1,128)S(1)}, f32[16,4096]{1,0:T(8,128)S(1)}, f32[16,4096]{1,0:T(8,128)S(1)}, f32[16,4096]{1,0:T(8,128)S(1)}, f32[16,4096]{1,0:T...) custom-call(bf16[512,128]{1,0:T(8,128)(2,1)S(1)} %copy-done.1, ...), custom_call_target="tpu_custom_call" | custom-call | flops 536870912 | bytes 6291456 | tf_op jit(solution)/shard_map/products/pallas_call | solution.py:109
  8.8 2.9 %collective-permute-start.4 = (f32[1,4096]{1,0:T(1,128)S(1)}, f32[1,4096]{1,0:T(1,128)S(1)}, u32[]{:S(2)}, u32[]{:S(2)}) collective-permute-start(f32[1,4096]{1,0:T(1,128)S(1)} %pair.1.refs_0_), channel_id=1, source_target_pairs={{0,2},{1,3},{2,0},{3,1},{4,6},{5,7},{6,4},{7,5},{8,10},{9,11},{10,... | collective-permute-start | bytes 49160 | tf_op jit(solution)/shard_map/ppermute | solution.py:24
  11.7 1.5 %collective-permute-start.5 = (f32[1,4096]{1,0:T(1,128)S(1)}, f32[1,4096]{1,0:T(1,128)S(1)}, u32[]{:S(2)}, u32[]{:S(2)}) collective-permute-start(f32[1,4096]{1,0:T(1,128)S(1)} %pair.1.refs_0_), channel_id=1, source_target_pairs={{0,4},{1,5},{2,6},{3,7},{4,0},{5,1},{6,2},{7,3},{8,12},{9,13},{10,... | collective-permute-start | bytes 49160 | tf_op jit(solution)/shard_map/ppermute | solution.py:24
  13.5 2.0 %collective-permute-done.5.refs_7_.refs_2_ = f32[1,4096]{1,0:T(1,128)S(1)} collective-permute-done((f32[1,4096]{1,0:T(1,128)S(1)}, f32[1,4096]{1,0:T(1,128)S(1)}, u32[]{:S(2)}, u32[]{:S(2)}) %collective-permute-start.5) | collective-permute-done | bytes 16416 | tf_op jit(solution)/shard_map/ppermute | solution.py:24
  15.5 2.4 %collective-permute-done.6.refs_8_.refs_3_ = f32[1,4096]{1,0:T(1,128)S(1)} collective-permute-done((f32[1,4096]{1,0:T(1,128)S(1)}, f32[1,4096]{1,0:T(1,128)S(1)}, u32[]{:S(2)}, u32[]{:S(2)}) %collective-permute-start.6) | collective-permute-done | bytes 16416 | tf_op jit(solution)/shard_map/ppermute | solution.py:24
  18.1 2.0 %collective-permute-start.8 = (f32[16,4096]{1,0:T(8,128)S(1)}, f32[16,4096]{1,0:T(8,128)S(1)}, u32[]{:S(2)}, u32[]{:S(2)}) collective-permute-start(f32[16,4096]{1,0:T(8,128)S(1)} %get-tuple-element.37), channel_id=1, source_target_pairs={{0,4},{1,5},{2,6},{3,7},{4,0},{5,1},{6,2},{7,3},{8,12},{9,13},{10,... | collective-permute-start | bytes 786440 | tf_op jit(solution)/shard_map/ppermute | solution.py:24
  20.0 1.5 %collective-permute-start.9 = (f32[16,4096]{1,0:T(8,128)S(1)}, f32[16,4096]{1,0:T(8,128)S(1)}, u32[]{:S(2)}, u32[]{:S(2)}) collective-permute-start(f32[16,4096]{1,0:T(8,128)S(1)} %get-tuple-element.38), channel_id=1, source_target_pairs={{0,2},{1,3},{2,0},{3,1},{4,6},{5,7},{6,4},{7,5},{8,10},{9,11},{10,... | collective-permute-start | bytes 786440 | tf_op jit(solution)/shard_map/ppermute | solution.py:24
  21.5 1.3 %risks.1 = (f32[1,4096]{1,0:T(1,128)S(1)}, f32[16,256]{1,0:T(8,128)S(1)}, f32[16,256]{1,0:T(8,128)S(1)}, f32[8,128]{1,0:T(8,128)S(1)}) custom-call(f32[1,4096]{1,0:T(1,128)S(1)} %pair.1.refs_0_, f32[1,4096]{1,0:T(1,128)S(1)} %collective-permute-done.4.refs_6_.refs_1_, f32[1,4096]{1,0:T(1,128)S(1)} %collective-permute-done.5.refs_7_.refs_2_, ...), custom_call_target="tpu_custom_call" | custom-call | flops 134217728 | bytes 262144 | tf_op jit(solution)/shard_map/risks/pallas_call | solution.py:197
  22.8 1.6 %collective-permute-start.10 = (f32[8,128]{1,0:T(8,128)S(1)}, f32[8,128]{1,0:T(8,128)S(1)}, u32[]{:S(2)}, u32[]{:S(2)}) collective-permute-start(f32[8,128]{1,0:T(8,128)S(1)} %get-tuple-element.40), channel_id=1, source_target_pairs={{0,8},{8,0},{16,24},{24,16},{1,9},{9,1},{17,25},{25,17},{2,10},{10... | collective-permute-start | bytes 12296 | tf_op jit(solution)/shard_map/ppermute | solution.py:24
  24.5 2.0 %collective-permute-done.10 = f32[8,128]{1,0:T(8,128)S(1)} collective-permute-done((f32[8,128]{1,0:T(8,128)S(1)}, f32[8,128]{1,0:T(8,128)S(1)}, u32[]{:S(2)}, u32[]{:S(2)}) %collective-permute-start.10) | collective-permute-done | bytes 4128 | tf_op jit(solution)/shard_map/ppermute | solution.py:24
  26.5 2.6 %collective-permute-start.11 = (f32[8,128]{1,0:T(8,128)S(1)}, f32[8,128]{1,0:T(8,128)S(1)}, u32[]{:S(2)}, u32[]{:S(2)}) collective-permute-start(f32[8,128]{1,0:T(8,128)S(1)} %add.9), channel_id=1, source_target_pairs={{0,16},{8,24},{16,0},{24,8},{1,17},{9,25},{17,1},{25,9},{2,18},{10... | collective-permute-start | bytes 12296 | tf_op jit(solution)/shard_map/ppermute | solution.py:24
  29.1 1.9 %collective-permute-done.11 = f32[8,128]{1,0:T(8,128)S(1)} collective-permute-done((f32[8,128]{1,0:T(8,128)S(1)}, f32[8,128]{1,0:T(8,128)S(1)}, u32[]{:S(2)}, u32[]{:S(2)}) %collective-permute-start.11) | collective-permute-done | bytes 4128 | tf_op jit(solution)/shard_map/ppermute | solution.py:24
  31.0 1.8 %hazards.1 = (f32[1,4096]{1,0:T(1,128)S(1)}, f32[1,4096]{1,0:T(1,128)S(1)}, f32[16,256]{1,0:T(8,128)S(1)}, f32[8,128]{1,0:T(8,128)S(1)}) custom-call(f32[8,128]{1,0:T(8,128)S(1)} %get-tuple-element.50.later, f32[16,256]{1,0:T(8,128)S(1)} %get-tuple-element.41.sums, f32[16,256]{1,0:T(8,128)S(1)} %get-tuple-element.42.events, s32[1,4096]{1,0:T(1,128)S(1)} %bitcast.4), custom_call_target="tpu_custom_call" | custom-call | flops 209715200 | bytes 262144 | tf_op jit(solution)/shard_map/hazards/pallas_call | solution.py:246
  32.9 1.6 %collective-permute-start.12 = (f32[40,128]{1,0:T(8,128)S(1)}, f32[40,128]{1,0:T(8,128)S(1)}, u32[]{:S(2)}, u32[]{:S(2)}) collective-permute-start(f32[40,128]{1,0:T(8,128)S(1)} %get-tuple-element.45.refs_0_), channel_id=1, source_target_pairs={{0,8},{8,0},{16,24},{24,16},{1,9},{9,1},{17,25},{25,17},{2,10},{10... | collective-permute-start | bytes 61448 | tf_op jit(solution)/shard_map/ppermute | solution.py:24
  34.5 2.6 %collective-permute-start.13 = (f32[40,128]{1,0:T(8,128)S(1)}, f32[40,128]{1,0:T(8,128)S(1)}, u32[]{:S(2)}, u32[]{:S(2)}) collective-permute-start(f32[40,128]{1,0:T(8,128)S(1)} %get-tuple-element.45.refs_0_), channel_id=1, source_target_pairs={{0,16},{8,24},{16,0},{24,8},{1,17},{9,25},{17,1},{25,9},{2,18},{10... | collective-permute-start | bytes 61448 | tf_op jit(solution)/shard_map/ppermute | solution.py:24
  37.3 5.7 %scans.1.refs_5_ = f32[16,4096]{1,0:T(8,128)S(1)} custom-call(f32[16,4096]{1,0:T(8,128)S(1)} %get-tuple-element.46.tangent.refs_4_, f32[1,4096]{1,0:T(1,128)S(1)} %get-tuple-element.39.refs_5_.risk.refs_6_, s32[1,4096]{1,0:T(1,128)S(1)} %bitcast.5, f32[16,256]{1,0:T(8,128)S(1)} %get-tuple-element.47.squares), custom_call_target="tpu_custom_call" | custom-call | flops 2147483648 | bytes 1572864 | tf_op jit(solution)/shard_map/scans/pallas_call | solution.py:341
  44.3 2.7 %collective-permute-start.20 = (bf16[16,4096]{1,0:T(8,128)(2,1)S(1)}, bf16[16,4096]{1,0:T(8,128)(2,1)S(1)}, u32[]{:S(2)}, u32[]{:S(2)}) collective-permute-start(bf16[16,4096]{1,0:T(8,128)(2,1)S(1)} %weights.1.refs_0_), channel_id=1, source_target_pairs={{0,6},{1,7},{2,4},{3,5},{4,2},{5,3},{6,0},{7,1},{8,14},{9,15},{10,... | collective-permute-start | bytes 393224 | tf_op jit(solution)/shard_map/ppermute | solution.py:24
  46.9 1.5 %collective-permute-done.16.refs_2_ = bf16[16,4096]{1,0:T(8,128)(2,1)S(1)} collective-permute-done((bf16[16,4096]{1,0:T(8,128)(2,1)S(1)}, bf16[16,4096]{1,0:T(8,128)(2,1)S(1)}, u32[]{:S(2)}, u32[]{:S(2)}) %collective-permute-start.16) | collective-permute-done | bytes 131104 | tf_op jit(solution)/shard_map/ppermute | solution.py:24
  48.4 1.9 %collective-permute-done.18.refs_4_ = bf16[16,4096]{1,0:T(8,128)(2,1)S(1)} collective-permute-done((bf16[16,4096]{1,0:T(8,128)(2,1)S(1)}, bf16[16,4096]{1,0:T(8,128)(2,1)S(1)}, u32[]{:S(2)}, u32[]{:S(2)}) %collective-permute-start.18) | collective-permute-done | bytes 131104 | tf_op jit(solution)/shard_map/ppermute | solution.py:24
  51.9 1.0 %gradients.1.mine = s16[528,128]{1,0:T(8,128)(2,1)S(1)} custom-call(bf16[16,4096]{1,0:T(8,128)(2,1)S(1)} %weights.1.refs_0_, bf16[16,4096]{1,0:T(8,128)(2,1)S(1)} %collective-permute-done.15.refs_1_, bf16[16,4096]{1,0:T(8,128)(2,1)S(1)} %collective-permute-done.16.refs_2_, bf16[16,4096]{1,0:T(8,128)(2,1)S(1)} %collective-permute-done.17.refs_3_, ...), custom_call_target="tpu_custom_call" | custom-call | flops 536870912 | bytes 5242880 | tf_op jit(solution)/shard_map/gradients/pallas_call | solution.py:427
  53.4 5.3 %collective-permute-done.22.other = s16[528,128]{1,0:T(8,128)(2,1)S(1)} collective-permute-done((s16[528,128]{1,0:T(8,128)(2,1)S(1)}, s16[528,128]{1,0:T(8,128)(2,1)S(1)}, u32[]{:S(2)}, u32[]{:S(2)}) %collective-permute-start.22) | collective-permute-done | bytes 135200 | tf_op jit(solution)/shard_map/ppermute | solution.py:24
  58.9 2.1 %collective-permute-start.23 = (s16[528,128]{1,0:T(8,128)(2,1)S(1)}, s16[528,128]{1,0:T(8,128)(2,1)S(1)}, u32[]{:S(2)}, u32[]{:S(2)}) collective-permute-start(s16[528,128]{1,0:T(8,128)(2,1)S(1)} %merge.1.mine), channel_id=1, source_target_pairs={{0,16},{8,24},{16,0},{24,8},{1,17},{9,25},{17,1},{25,9},{2,18},{10... | collective-permute-start | bytes 405512 | tf_op jit(solution)/shard_map/ppermute | solution.py:24
  61.0 6.8 %collective-permute-done.23.other = s16[528,128]{1,0:T(8,128)(2,1)S(1)} collective-permute-done((s16[528,128]{1,0:T(8,128)(2,1)S(1)}, s16[528,128]{1,0:T(8,128)(2,1)S(1)}, u32[]{:S(2)}, u32[]{:S(2)}) %collective-permute-start.23) | collective-permute-done | bytes 135200 | tf_op jit(solution)/shard_map/ppermute | solution.py:24
  (47 shorter events, 7.3 us)
Async XLA Ops:
  6.9 1.9 %collective-permute-start.1 = (f32[24,4096]{1,0:T(8,128)S(1)}, f32[24,4096]{1,0:T(8,128)S(1)}, u32[]{:S(2)}, u32[]{:S(2)}) collective-permute-start(f32[24,4096]{1,0:T(8,128)S(1)} %get-tuple-element.32), channel_id=1, source_target_pairs={{0,1},{1,0},{2,3},{3,2},{4,5},{5,4},{6,7},{7,6},{8,9},{9,8},{10,11... | collective-permute-start | bytes 1179656 | tf_op jit(solution)/shard_map/ppermute | solution.py:24
  7.4 5.8 %collective-permute-start.2 = (f32[16,4096]{1,0:T(8,128)S(1)}, f32[16,4096]{1,0:T(8,128)S(1)}, u32[]{:S(2)}, u32[]{:S(2)}) collective-permute-start(f32[16,4096]{1,0:T(8,128)S(1)} %get-tuple-element.33), channel_id=1, source_target_pairs={{0,1},{1,0},{2,3},{3,2},{4,5},{5,4},{6,7},{7,6},{8,9},{9,8},{10,11... | collective-permute-start | bytes 786440 | tf_op jit(solution)/shard_map/ppermute | solution.py:24
  7.5 5.8 %collective-permute-start.3 = (f32[16,4096]{1,0:T(8,128)S(1)}, f32[16,4096]{1,0:T(8,128)S(1)}, u32[]{:S(2)}, u32[]{:S(2)}) collective-permute-start(f32[16,4096]{1,0:T(8,128)S(1)} %get-tuple-element.34), channel_id=1, source_target_pairs={{0,1},{1,0},{2,3},{3,2},{4,5},{5,4},{6,7},{7,6},{8,9},{9,8},{10,11... | collective-permute-start | bytes 786440 | tf_op jit(solution)/shard_map/ppermute | solution.py:24
  8.8 4.6 %collective-permute-start.4 = (f32[1,4096]{1,0:T(1,128)S(1)}, f32[1,4096]{1,0:T(1,128)S(1)}, u32[]{:S(2)}, u32[]{:S(2)}) collective-permute-start(f32[1,4096]{1,0:T(1,128)S(1)} %pair.1.refs_0_), channel_id=1, source_target_pairs={{0,2},{1,3},{2,0},{3,1},{4,6},{5,7},{6,4},{7,5},{8,10},{9,11},{10,... | collective-permute-start | bytes 49160 | tf_op jit(solution)/shard_map/ppermute | solution.py:24
  11.7 3.7 %collective-permute-start.5 = (f32[1,4096]{1,0:T(1,128)S(1)}, f32[1,4096]{1,0:T(1,128)S(1)}, u32[]{:S(2)}, u32[]{:S(2)}) collective-permute-start(f32[1,4096]{1,0:T(1,128)S(1)} %pair.1.refs_0_), channel_id=1, source_target_pairs={{0,4},{1,5},{2,6},{3,7},{4,0},{5,1},{6,2},{7,3},{8,12},{9,13},{10,... | collective-permute-start | bytes 49160 | tf_op jit(solution)/shard_map/ppermute | solution.py:24
  13.3 4.6 %collective-permute-start.6 = (f32[1,4096]{1,0:T(1,128)S(1)}, f32[1,4096]{1,0:T(1,128)S(1)}, u32[]{:S(2)}, u32[]{:S(2)}) collective-permute-start(f32[1,4096]{1,0:T(1,128)S(1)} %pair.1.refs_0_), channel_id=1, source_target_pairs={{0,6},{1,7},{2,4},{3,5},{4,2},{5,3},{6,0},{7,1},{8,14},{9,15},{10,... | collective-permute-start | bytes 49160 | tf_op jit(solution)/shard_map/ppermute | solution.py:24
  13.3 19.5 %collective-permute-start = (f32[16,4096]{1,0:T(8,128)S(1)}, f32[16,4096]{1,0:T(8,128)S(1)}, u32[]{:S(2)}, u32[]{:S(2)}) collective-permute-start(f32[16,4096]{1,0:T(8,128)S(1)} %get-tuple-element.28), channel_id=1, source_target_pairs={{0,1},{1,0},{2,3},{3,2},{4,5},{5,4},{6,7},{7,6},{8,9},{9,8},{10,11... | collective-permute-start | bytes 786440 | tf_op jit(solution)/shard_map/ppermute | solution.py:24
  18.0 14.8 %collective-permute-start.7 = (f32[16,4096]{1,0:T(8,128)S(1)}, f32[16,4096]{1,0:T(8,128)S(1)}, u32[]{:S(2)}, u32[]{:S(2)}) collective-permute-start(f32[16,4096]{1,0:T(8,128)S(1)} %get-tuple-element.36), channel_id=1, source_target_pairs={{0,6},{1,7},{2,4},{3,5},{4,2},{5,3},{6,0},{7,1},{8,14},{9,15},{10,... | collective-permute-start | bytes 786440 | tf_op jit(solution)/shard_map/ppermute | solution.py:24
  18.1 14.7 %collective-permute-start.8 = (f32[16,4096]{1,0:T(8,128)S(1)}, f32[16,4096]{1,0:T(8,128)S(1)}, u32[]{:S(2)}, u32[]{:S(2)}) collective-permute-start(f32[16,4096]{1,0:T(8,128)S(1)} %get-tuple-element.37), channel_id=1, source_target_pairs={{0,4},{1,5},{2,6},{3,7},{4,0},{5,1},{6,2},{7,3},{8,12},{9,13},{10,... | collective-permute-start | bytes 786440 | tf_op jit(solution)/shard_map/ppermute | solution.py:24
  20.0 12.8 %collective-permute-start.9 = (f32[16,4096]{1,0:T(8,128)S(1)}, f32[16,4096]{1,0:T(8,128)S(1)}, u32[]{:S(2)}, u32[]{:S(2)}) collective-permute-start(f32[16,4096]{1,0:T(8,128)S(1)} %get-tuple-element.38), channel_id=1, source_target_pairs={{0,2},{1,3},{2,0},{3,1},{4,6},{5,7},{6,4},{7,5},{8,10},{9,11},{10,... | collective-permute-start | bytes 786440 | tf_op jit(solution)/shard_map/ppermute | solution.py:24
  22.8 3.7 %collective-permute-start.10 = (f32[8,128]{1,0:T(8,128)S(1)}, f32[8,128]{1,0:T(8,128)S(1)}, u32[]{:S(2)}, u32[]{:S(2)}) collective-permute-start(f32[8,128]{1,0:T(8,128)S(1)} %get-tuple-element.40), channel_id=1, source_target_pairs={{0,8},{8,0},{16,24},{24,16},{1,9},{9,1},{17,25},{25,17},{2,10},{10... | collective-permute-start | bytes 12296 | tf_op jit(solution)/shard_map/ppermute | solution.py:24
  26.5 4.5 %collective-permute-start.11 = (f32[8,128]{1,0:T(8,128)S(1)}, f32[8,128]{1,0:T(8,128)S(1)}, u32[]{:S(2)}, u32[]{:S(2)}) collective-permute-start(f32[8,128]{1,0:T(8,128)S(1)} %add.9), channel_id=1, source_target_pairs={{0,16},{8,24},{16,0},{24,8},{1,17},{9,25},{17,1},{25,9},{2,18},{10... | collective-permute-start | bytes 12296 | tf_op jit(solution)/shard_map/ppermute | solution.py:24
  32.9 10.2 %collective-permute-start.12 = (f32[40,128]{1,0:T(8,128)S(1)}, f32[40,128]{1,0:T(8,128)S(1)}, u32[]{:S(2)}, u32[]{:S(2)}) collective-permute-start(f32[40,128]{1,0:T(8,128)S(1)} %get-tuple-element.45.refs_0_), channel_id=1, source_target_pairs={{0,8},{8,0},{16,24},{24,16},{1,9},{9,1},{17,25},{25,17},{2,10},{10... | collective-permute-start | bytes 61448 | tf_op jit(solution)/shard_map/ppermute | solution.py:24
  34.5 8.6 %collective-permute-start.13 = (f32[40,128]{1,0:T(8,128)S(1)}, f32[40,128]{1,0:T(8,128)S(1)}, u32[]{:S(2)}, u32[]{:S(2)}) collective-permute-start(f32[40,128]{1,0:T(8,128)S(1)} %get-tuple-element.45.refs_0_), channel_id=1, source_target_pairs={{0,16},{8,24},{16,0},{24,8},{1,17},{9,25},{17,1},{25,9},{2,18},{10... | collective-permute-start | bytes 61448 | tf_op jit(solution)/shard_map/ppermute | solution.py:24
  37.1 6.0 %collective-permute-start.14 = (f32[40,128]{1,0:T(8,128)S(1)}, f32[40,128]{1,0:T(8,128)S(1)}, u32[]{:S(2)}, u32[]{:S(2)}) collective-permute-start(f32[40,128]{1,0:T(8,128)S(1)} %get-tuple-element.45.refs_0_), channel_id=1, source_target_pairs={{0,24},{8,16},{16,8},{24,0},{1,25},{9,17},{17,9},{25,1},{2,26},{10... | collective-permute-start | bytes 61448 | tf_op jit(solution)/shard_map/ppermute | solution.py:24
  43.4 5.0 %collective-permute-start.16 = (bf16[16,4096]{1,0:T(8,128)(2,1)S(1)}, bf16[16,4096]{1,0:T(8,128)(2,1)S(1)}, u32[]{:S(2)}, u32[]{:S(2)}) collective-permute-start(bf16[16,4096]{1,0:T(8,128)(2,1)S(1)} %weights.1.refs_0_), channel_id=1, source_target_pairs={{0,2},{1,3},{2,0},{3,1},{4,6},{5,7},{6,4},{7,5},{8,10},{9,11},{10,... | collective-permute-start | bytes 393224 | tf_op jit(solution)/shard_map/ppermute | solution.py:24
  44.0 6.4 %collective-permute-start.18 = (bf16[16,4096]{1,0:T(8,128)(2,1)S(1)}, bf16[16,4096]{1,0:T(8,128)(2,1)S(1)}, u32[]{:S(2)}, u32[]{:S(2)}) collective-permute-start(bf16[16,4096]{1,0:T(8,128)(2,1)S(1)} %weights.1.refs_0_), channel_id=1, source_target_pairs={{0,4},{1,5},{2,6},{3,7},{4,0},{5,1},{6,2},{7,3},{8,12},{9,13},{10,... | collective-permute-start | bytes 393224 | tf_op jit(solution)/shard_map/ppermute | solution.py:24
  44.3 6.1 %collective-permute-start.20 = (bf16[16,4096]{1,0:T(8,128)(2,1)S(1)}, bf16[16,4096]{1,0:T(8,128)(2,1)S(1)}, u32[]{:S(2)}, u32[]{:S(2)}) collective-permute-start(bf16[16,4096]{1,0:T(8,128)(2,1)S(1)} %weights.1.refs_0_), channel_id=1, source_target_pairs={{0,6},{1,7},{2,4},{3,5},{4,2},{5,3},{6,0},{7,1},{8,14},{9,15},{10,... | collective-permute-start | bytes 393224 | tf_op jit(solution)/shard_map/ppermute | solution.py:24
  46.9 3.9 %collective-permute-start.15 = (bf16[16,4096]{1,0:T(8,128)(2,1)S(1)}, bf16[16,4096]{1,0:T(8,128)(2,1)S(1)}, u32[]{:S(2)}, u32[]{:S(2)}) collective-permute-start(bf16[16,4096]{1,0:T(8,128)(2,1)S(1)} %weights.1.refs_0_), channel_id=1, source_target_pairs={{0,1},{1,0},{2,3},{3,2},{4,5},{5,4},{6,7},{7,6},{8,9},{9,8},{10,11... | collective-permute-start | bytes 393224 | tf_op jit(solution)/shard_map/ppermute | solution.py:24
  48.4 2.4 %collective-permute-start.17 = (bf16[16,4096]{1,0:T(8,128)(2,1)S(1)}, bf16[16,4096]{1,0:T(8,128)(2,1)S(1)}, u32[]{:S(2)}, u32[]{:S(2)}) collective-permute-start(bf16[16,4096]{1,0:T(8,128)(2,1)S(1)} %collective-permute-done.16.refs_2_), channel_id=1, source_target_pairs={{0,1},{1,0},{2,3},{3,2},{4,5},{5,4},{6,7},{7,6},{8,9},{9,8},{10,11... | collective-permute-start | bytes 393224 | tf_op jit(solution)/shard_map/ppermute | solution.py:24
  50.3 1.3 %collective-permute-start.19 = (bf16[16,4096]{1,0:T(8,128)(2,1)S(1)}, bf16[16,4096]{1,0:T(8,128)(2,1)S(1)}, u32[]{:S(2)}, u32[]{:S(2)}) collective-permute-start(bf16[16,4096]{1,0:T(8,128)(2,1)S(1)} %collective-permute-done.18.refs_4_), channel_id=1, source_target_pairs={{0,1},{1,0},{2,3},{3,2},{4,5},{5,4},{6,7},{7,6},{8,9},{9,8},{10,11... | collective-permute-start | bytes 393224 | tf_op jit(solution)/shard_map/ppermute | solution.py:24
  50.3 1.5 %collective-permute-start.21 = (bf16[16,4096]{1,0:T(8,128)(2,1)S(1)}, bf16[16,4096]{1,0:T(8,128)(2,1)S(1)}, u32[]{:S(2)}, u32[]{:S(2)}) collective-permute-start(bf16[16,4096]{1,0:T(8,128)(2,1)S(1)} %collective-permute-done.20.refs_6_), channel_id=1, source_target_pairs={{0,1},{1,0},{2,3},{3,2},{4,5},{5,4},{6,7},{7,6},{8,9},{9,8},{10,11... | collective-permute-start | bytes 393224 | tf_op jit(solution)/shard_map/ppermute | solution.py:24
  52.9 5.9 %collective-permute-start.22 = (s16[528,128]{1,0:T(8,128)(2,1)S(1)}, s16[528,128]{1,0:T(8,128)(2,1)S(1)}, u32[]{:S(2)}, u32[]{:S(2)}) collective-permute-start(s16[528,128]{1,0:T(8,128)(2,1)S(1)} %gradients.1.mine), channel_id=1, source_target_pairs={{0,8},{8,0},{16,24},{24,16},{1,9},{9,1},{17,25},{25,17},{2,10},{10... | collective-permute-start | bytes 405512 | tf_op jit(solution)/shard_map/ppermute | solution.py:24
  58.9 8.9 %collective-permute-start.23 = (s16[528,128]{1,0:T(8,128)(2,1)S(1)}, s16[528,128]{1,0:T(8,128)(2,1)S(1)}, u32[]{:S(2)}, u32[]{:S(2)}) collective-permute-start(s16[528,128]{1,0:T(8,128)(2,1)S(1)} %merge.1.mine), channel_id=1, source_target_pairs={{0,16},{8,24},{16,0},{24,8},{1,17},{9,25},{17,1},{25,9},{2,18},{10... | collective-permute-start | bytes 405512 | tf_op jit(solution)/shard_map/ppermute | solution.py:24
  (5 other events, 56.0 us)

commit v5 on v4

--- a/solution.py
+++ b/solution.py
@@ -11,7 +11,7 @@
 BF16 = jnp.bfloat16
 LO = 256
 BLOCK = 64
-NT = (((1,), (1,)), ((), ()))
+SPAN = 512
 VMEM = pl.BlockSpec(memory_space=pltpu.VMEM)
 HIGHEST = lax.Precision.HIGHEST
 HBM = pl.BlockSpec(memory_space=pltpu.HBM)
@@ -61,7 +61,7 @@
 
 def product_kernel(feat, kf, chunk, directions, coefficients, dosages, *refs):
     linear, keep, send = refs[0], refs[1 : 1 + feat // 2], refs[1 + feat // 2 : 1 + feat]
-    table, own_directions, own_coefficients, rhs, turned, sems = refs[1 + feat :]
+    table, own_directions, own_coefficients, rhs, results, turned, sems = refs[1 + feat :]
     me = lax.axis_index("feat")
     width = feat * kf
     persons, variants = table.shape
@@ -84,19 +84,24 @@
     spread = jnp.broadcast_to(own_coefficients[...].astype(F32)[None, :], (128, variants))
     rhs[:, width:] = spread.T.astype(BF16)
     diagonal = triangle(128, lambda a, b: a == b)
-    for i in range(steps):
-        large[i].wait()
-        at = slice(i * chunk, (i + 1) * chunk)
-        result = jnp.dot(table[at], rhs[...], preferred_element_type=F32)
-        turned[i] = result[:, :width].T.reshape(feat, kf, chunk)
-        for j in range(feat):
-            (send if j % 2 else keep)[j // 2][:kf, at] = turned[i, me ^ j]
-        for start in range(0, chunk, 128):
-            block = result[start : start + 128, width:]
-            row = jnp.sum(block * diagonal, axis=0, keepdims=True)
-            here = slice(i * chunk + start, i * chunk + start + 128)
-            linear[:, here] = row
-            send[1][kf:, here] = jnp.broadcast_to(row, (8, 128))
+    for i in range(steps + 1):
+        if i < steps:
+            large[i].wait()
+            results[i % 2] = jnp.dot(
+                table[i * chunk : (i + 1) * chunk], rhs[...], preferred_element_type=F32
+            )
+        if i > 0:
+            result = results.at[(i - 1) % 2]
+            first = (i - 1) * chunk
+            turned[i % 2] = result[:, :width].T.reshape(feat, kf, chunk)
+            for j in range(feat):
+                (send if j % 2 else keep)[j // 2][:, first : first + chunk] = turned[i % 2, me ^ j]
+            for start in range(0, chunk, 128):
+                block = result[start : start + 128, width:]
+                row = jnp.sum(block * diagonal, axis=0, keepdims=True)
+                group, lane = divmod(first + start, LO)
+                linear[group : group + 1, lane : lane + 128] = row
+                send[1][group : group + 1, persons + lane : persons + lane + 128] = row
 
 
 def products(dosages, coefficients, directions, feat):
@@ -105,11 +110,11 @@
     kf = k // feat
     chunk = min(512, persons)
     piece = jax.ShapeDtypeStruct((kf, persons), F32)
-    first = jax.ShapeDtypeStruct((kf + 8, persons), F32)
+    first = jax.ShapeDtypeStruct((kf, persons + LO), F32)
     out = pl.pallas_call(
         functools.partial(product_kernel, feat, kf, chunk),
         in_specs=[HBM, HBM, HBM],
-        out_shape=[jax.ShapeDtypeStruct((1, persons), F32)]
+        out_shape=[jax.ShapeDtypeStruct((kf, LO), F32)]
         + [piece] * (feat // 2 + 1)
         + [first]
         + [piece] * (feat // 2 - 2),
@@ -119,7 +124,8 @@
             pltpu.VMEM((variants, k), BF16),
             pltpu.VMEM((variants,), BF16),
             pltpu.VMEM((variants, k + 128), BF16),
-            pltpu.VMEM((persons // chunk, feat, kf, chunk), F32),
+            pltpu.VMEM((2, chunk, k + 128), F32),
+            pltpu.VMEM((2, feat, kf, chunk), F32),
             pltpu.SemaphoreType.DMA((persons // chunk + 2,)),
         ],
         compiler_params=pltpu.CompilerParams(vmem_limit_bytes=PRODUCT_BYTES),
@@ -131,55 +137,108 @@
     return out[0], out[1 : 1 + feat // 2], out[1 + feat // 2 :]
 
 
-def pair_kernel(linear, received, out):
-    kf = received.shape[0] - 8
-    out[...] = linear[...] + received[kf : kf + 1, :]
-
-
-def pair(linear, received):
-    return pl.pallas_call(
-        pair_kernel,
-        in_specs=[VMEM] * 2,
-        out_shape=jax.ShapeDtypeStruct(linear.shape, F32),
-        out_specs=VMEM,
-        compiler_params=pltpu.CompilerParams(**PARAMS),
-        name="pair",
-    )(linear, received)
+def power_of(largest):
+    return jnp.ceil(jnp.log2(jnp.maximum(largest, 1e-30))) - 14.0
+
+
+def to_short(values):
+    return jnp.round(values).astype(jnp.int32).astype(jnp.int16)
+
+
+def from_short(values):
+    return values.astype(jnp.int32).astype(F32)
 
 
 def join_kernel(count, *refs):
-    keep, received, outs = refs[:count], refs[count : 2 * count], refs[-count:]
+    linear, keep, received = refs[0], refs[1 : 1 + count], refs[1 + count : 1 + 2 * count]
+    linear_out, outs = refs[1 + 2 * count], refs[2 + 2 * count :]
+    kf, rows = keep[0].shape
+    span = min(SPAN, rows)
+    lane = lax.broadcasted_iota(jnp.int32, (kf, 128), 1)
+    paired = linear[...] + received[0][:, rows:]
+    linear_out[...] = paired
+    linear_power = power_of(jnp.max(jnp.abs(paired), axis=1, keepdims=True))
+    scaled = paired * jnp.exp2(-linear_power)
+    whole = jnp.round(scaled)
+    high, low = to_short(whole), to_short((scaled - whole) * 32768.0)
     for mine, other, out in zip(keep, received, outs):
-        kf = mine.shape[0]
-        out[...] = mine[...] + other[:kf, :]
-
-
-def join(keep, received, waited):
+        powers = jnp.where(lane == rows // span, linear_power, 0.0)
+        for i in range(rows // span):
+            at = slice(i * span, (i + 1) * span)
+            total = mine[:, at] + other[:, at]
+            power = power_of(jnp.max(jnp.abs(total), axis=1, keepdims=True))
+            out[:, at] = to_short(total * jnp.exp2(-power))
+            powers = jnp.where(lane == i, power, powers)
+        out[:, rows : rows + LO] = high
+        out[:, rows + LO : rows + 2 * LO] = low
+        out[:, rows + 2 * LO :] = to_short(powers)
+
+
+def join(linear, keep, received):
     count = len(keep)
-    return pl.pallas_call(
+    kf, rows = keep[0].shape
+    message = jax.ShapeDtypeStruct((kf, rows + 2 * LO + 128), jnp.int16)
+    out = pl.pallas_call(
         functools.partial(join_kernel, count),
-        in_specs=[VMEM] * (2 * count) + [pl.BlockSpec(memory_space=pl.ANY)] * len(waited),
-        out_shape=[jax.ShapeDtypeStruct(k.shape, F32) for k in keep],
-        out_specs=[VMEM] * count,
+        in_specs=[VMEM] * (2 * count + 1),
+        out_shape=[jax.ShapeDtypeStruct(linear.shape, F32)] + [message] * count,
+        out_specs=[VMEM] * (count + 1),
         compiler_params=pltpu.CompilerParams(**PARAMS),
         name="join",
-    )(*keep, *received, *waited)
-
-
-def risk_kernel(rows, parts, *refs):
-    linear, (rank, events) = refs[:parts], refs[parts : parts + 2]
-    risk_out, sums_out, events_out, message = refs[parts + 2 :]
+    )(linear, *keep, *received)
+    return out[0], out[1:]
+
+
+def table_kernel(rows, rank, waited, spread, table, masks):
+    groups, height, _ = masks.shape
+    chunk = min(512, rows)
+    lane = lax.broadcasted_iota(jnp.int32, (chunk, 128), 1)
+    for start in range(0, rows, chunk):
+        at = slice(start, start + chunk)
+        place = lax.rem(rank[:, at], rows)
+        group, inner = place // LO, lax.rem(place, LO)
+        spread[:, at] = one_hot(inner, LO)
+        column = jnp.broadcast_to(inner.astype(F32), (128, chunk)).T.astype(jnp.int32)
+        for first in range(0, LO, 128):
+            table[at, first : first + 128] = jnp.where(column == lane + first, 1.0, 0.0).astype(BF16)
+        for g in range(groups):
+            mask = jnp.where(group == g, 1.0, 0.0)
+            masks[g, :, at] = jnp.broadcast_to(mask, (height, chunk)).astype(BF16)
+
+
+def tables(rank, waited, rows, height):
+    return pl.pallas_call(
+        functools.partial(table_kernel, rows),
+        in_specs=[VMEM, pl.BlockSpec(memory_space=pl.ANY)],
+        out_shape=[
+            jax.ShapeDtypeStruct((LO, rows), BF16),
+            jax.ShapeDtypeStruct((rows, LO), BF16),
+            jax.ShapeDtypeStruct((rows // LO, height, rows), BF16),
+        ],
+        out_specs=[VMEM] * 3,
+        compiler_params=pltpu.CompilerParams(**PARAMS),
+        cost_estimate=pl.CostEstimate(flops=rows * LO * 8, bytes_accessed=rows * LO * 6, transcendentals=0),
+        name="tables",
+    )(rank, waited)
+
+
+def risk_kernel(rows, parts, linear, *refs):
+    messages, (rank, events, table) = refs[:parts], refs[parts : parts + 3]
+    risk_out, sums_out, events_out, message = refs[parts + 3 :]
     groups = rows // LO
-    total = linear[0][...]
-    for part in linear[1:]:
-        total = total + part[...]
+    span = min(SPAN, rows)
+    total = linear[...]
+    for part in messages:
+        power = from_short(part[:, rows + 2 * LO :])[:, rows // span : rows // span + 1]
+        high, low = from_short(part[:, rows : rows + LO]), from_short(part[:, rows + LO : rows + 2 * LO])
+        total = total + (high + low * (1.0 / 32768.0)) * jnp.exp2(power)
     risk = jnp.exp(total)
-    risk_out[...] = risk
-    place = lax.rem(rank[...], rows)
-    mask = one_hot(place // LO, groups, F32)
-    pieces = [mask * part for part in split_three(risk)] + [mask * events[...].astype(F32)]
+    for g in range(groups):
+        risk_out[:, g * LO : (g + 1) * LO] = risk[g : g + 1]
+    mask = one_hot(lax.rem(rank[...], rows) // LO, groups, F32)
+    pieces = [mask * part for part in split_three(risk_out[...])] + [mask * events[...].astype(F32)]
     lhs = jnp.concatenate(pieces, axis=0).astype(BF16)
-    sorted_all = lax.dot_general(lhs, one_hot(lax.rem(place, LO), LO), NT, preferred_element_type=F32)
+    sorted_all = jnp.dot(lhs, table[...], preferred_element_type=F32)
     ordered = sorted_all[:groups] + sorted_all[groups : 2 * groups] + sorted_all[2 * groups : 3 * groups]
     happened = sorted_all[3 * groups :]
     inside = dot_binary(ordered, triangle(LO, lambda a, b: a >= b))
@@ -192,11 +251,11 @@
     message[...] = jnp.concatenate([everything, count, jnp.zeros((6, 128), F32)], axis=0)
 
 
-def risks(linear, rank, events, rows):
+def risks(linear, messages, rank, events, table, rows):
     groups = rows // LO
     return pl.pallas_call(
-        functools.partial(risk_kernel, rows, len(linear)),
-        in_specs=[VMEM] * (len(linear) + 2),
+        functools.partial(risk_kernel, rows, len(messages)),
+        in_specs=[VMEM] * (len(messages) + 4),
         out_shape=[
             jax.ShapeDtypeStruct((1, rows), F32),
             jax.ShapeDtypeStruct((groups, LO), F32),
@@ -207,10 +266,10 @@
         compiler_params=pltpu.CompilerParams(**PARAMS),
         cost_estimate=pl.CostEstimate(flops=rows * LO * 128, bytes_accessed=rows * 64, transcendentals=rows),
         name="risks",
-    )(*linear, rank, events)
-
-
-def hazard_kernel(rows, later, sums, events, rank, *outs):
+    )(linear, *messages, rank, events, table)
+
+
+def hazard_kernel(rows, later, sums, events, rank, spread, *outs):
     cumulative, squares, ordered_squares, message = outs
     groups = rows // LO
     risk_sum = sums[...] + later[0:1, 0:1]
@@ -232,88 +291,110 @@
         ],
         axis=0,
     )
-    place = lax.rem(rank[...], rows)
-    mask = one_hot(place // LO, groups, F32)
-    placed = dot_binary(inside + carried, one_hot(lax.rem(place, LO), LO))
+    mask = one_hot(lax.rem(rank[...], rows) // LO, groups, F32)
+    placed = dot_binary(inside + carried, spread[...])
     cumulative[...] = jnp.sum(mask * placed[:groups], axis=0, keepdims=True)
     squares[...] = jnp.sum(mask * placed[groups:], axis=0, keepdims=True)
 
 
-def hazards(later, sums, events, rank, rows):
+def hazards(later, sums, events, rank, spread, rows):
     groups = rows // LO
     row = jax.ShapeDtypeStruct((1, rows), F32)
     small = jax.ShapeDtypeStruct((8, 128), F32)
     return pl.pallas_call(
         functools.partial(hazard_kernel, rows),
-        in_specs=[VMEM] * 4,
+        in_specs=[VMEM] * 5,
         out_shape=[row, row, jax.ShapeDtypeStruct((groups, LO), F32), small],
         out_specs=[VMEM] * 4,
         compiler_params=pltpu.CompilerParams(**PARAMS),
         cost_estimate=pl.CostEstimate(flops=rows * LO * 200, bytes_accessed=rows * 64, transcendentals=0),
         name="hazards",
-    )(later, sums, events, rank)
-
-
-def total_kernel(parts, *refs):
-    tangents = refs[:parts]
-    risk, squares, hazard_message, tangent_out, message = refs[parts:]
-    kf, rows = tangent_out.shape
+    )(later, sums, events, rank, spread)
+
+
+def total_kernel(tangent, risk, squares, hazard_message, message):
+    kf, rows = tangent.shape
     plain = jnp.zeros((kf, 128), F32)
     scaled = jnp.zeros((kf, 128), F32)
     for start in range(0, rows, 128):
         at = slice(start, start + 128)
-        tangent = tangents[0][:, at]
-        for part in tangents[1:]:
-            tangent = tangent + part[:kf, at]
-        tangent_out[:, at] = tangent
-        weighted = tangent * risk[:, at]
+        weighted = tangent[:, at] * risk[:, at]
         plain = plain + weighted
         scaled = scaled + weighted * squares[:, at]
     message[...] = jnp.concatenate([plain, scaled, hazard_message[...]], axis=0)
 
 
-def block_totals(tangents, risk, squares, hazard_message):
-    kf, rows = tangents[0].shape
-    return pl.pallas_call(
-        functools.partial(total_kernel, len(tangents)),
-        in_specs=[VMEM] * (len(tangents) + 3),
-        out_shape=[
-            jax.ShapeDtypeStruct((kf, rows), F32),
-            jax.ShapeDtypeStruct((2 * kf + 8, 128), F32),
-        ],
-        out_specs=[VMEM] * 2,
+def block_totals(tangent, risk, squares, hazard_message):
+    kf, rows = tangent.shape
+    return pl.pallas_call(
+        total_kernel,
+        in_specs=[VMEM] * 4,
+        out_shape=jax.ShapeDtypeStruct((2 * kf + 8, 128), F32),
+        out_specs=VMEM,
         compiler_params=pltpu.CompilerParams(**PARAMS),
         name="block_totals",
-    )(*tangents, risk, squares, hazard_message)
-
-
-def scan_kernel(rows, kf, tangent, risk, rank, squares, cumulative_out, lhs, spread):
-    groups = rows // LO
-    chunk = min(1024, rows)
-    ordered = jnp.zeros((groups * 2 * kf, LO), F32)
-    for start in range(0, rows, chunk):
-        at = slice(start, start + chunk)
-        place = lax.rem(rank[:, at], rows)
-        group = place // LO
-        spread[:, at] = one_hot(lax.rem(place, LO), LO)
-        both = jnp.concatenate(split_two(tangent[:, at] * risk[:, at]), axis=0)
+    )(tangent, risk, squares, hazard_message)
+
+
+def suffix_kernel(parts, own, other, *refs):
+    messages, (risk, masks, table) = refs[:parts], refs[parts : parts + 3]
+    tangent_out, sums, lhs = refs[parts + 3 :]
+    kf, rows = own.shape
+    groups = masks.shape[0]
+    span = min(SPAN, rows)
+    powers = [jnp.exp2(from_short(part[:, rows + 2 * LO :])) for part in messages]
+    for i in range(rows // span):
+        at = slice(i * span, (i + 1) * span)
+        tangent = own[:, at] + other[:, at]
+        for part, power in zip(messages, powers):
+            tangent = tangent + from_short(part[:, at]) * power[:, i : i + 1]
+        tangent_out[:, at] = tangent
+        high, low = split_two(tangent * risk[:, at])
+        high, low = high.astype(BF16), low.astype(BF16)
         for g in range(groups):
-            lhs[g * 2 * kf : (g + 1) * 2 * kf, at] = jnp.where(group == g, both, 0.0).astype(BF16)
-        ordered = ordered + lax.dot_general(lhs[:, at], spread[:, at], NT, preferred_element_type=F32)
+            lhs[2 * g * kf : (2 * g + 1) * kf, at] = high * masks[g, :, at]
+            lhs[(2 * g + 1) * kf : (2 * g + 2) * kf, at] = low * masks[g, :, at]
+    ordered = jnp.dot(lhs[...], table[...], preferred_element_type=F32)
     ordered = jnp.concatenate(
         [
-            ordered[g * 2 * kf : g * 2 * kf + kf] + ordered[g * 2 * kf + kf : (g + 1) * 2 * kf]
+            ordered[2 * g * kf : (2 * g + 1) * kf] + ordered[(2 * g + 1) * kf : (2 * g + 2) * kf]
             for g in range(groups)
         ],
         axis=0,
     )
     inside = dot_binary(ordered, triangle(LO, lambda a, b: a >= b))
     carried = jnp.zeros((kf, 1), F32)
-    hazard = [None] * groups
     for g in reversed(range(groups)):
         rows_of = slice(g * kf, (g + 1) * kf)
-        hazard[g] = (inside[rows_of] + carried) * squares[g : g + 1, :]
+        sums[rows_of] = inside[rows_of] + carried
         carried = carried + inside[rows_of, :1]
+
+
+def suffix_sums(own, other, messages, risk, masks, table):
+    kf, rows = own.shape
+    groups = rows // LO
+    return pl.pallas_call(
+        functools.partial(suffix_kernel, len(messages)),
+        in_specs=[VMEM] * (len(messages) + 5),
+        out_shape=[
+            jax.ShapeDtypeStruct((kf, rows), F32),
+            jax.ShapeDtypeStruct((groups * kf, LO), F32),
+        ],
+        out_specs=[VMEM] * 2,
+        scratch_shapes=[pltpu.VMEM((groups * 2 * kf, rows), BF16)],
+        compiler_params=pltpu.CompilerParams(**PARAMS),
+        cost_estimate=pl.CostEstimate(
+            flops=2 * rows * LO * groups * 2 * kf, bytes_accessed=rows * kf * 24, transcendentals=0
+        ),
+        name="suffix_sums",
+    )(own, other, *messages, risk, masks, table)
+
+
+def prefix_kernel(sums, squares, rank, spread, out):
+    kf, rows = out.shape
+    groups = squares.shape[0]
+    chunk = min(512, rows)
+    hazard = [sums[g * kf : (g + 1) * kf] * squares[g : g + 1, :] for g in range(groups)]
     inside = dot_binary(jnp.concatenate(hazard, axis=0), triangle(LO, lambda a, b: a <= b))
     carried = jnp.zeros((kf, 1), F32)
     summed = [None] * groups
@@ -332,24 +413,22 @@
         picked = jnp.zeros((kf, chunk), F32)
         for g in range(groups):
             picked = picked + jnp.where(group == g, placed[g * kf : (g + 1) * kf], 0.0)
-        cumulative_out[:, at] = picked
-
-
-def scans(tangent, risk, rank, squares):
-    kf, rows = tangent.shape
-    groups = rows // LO
-    return pl.pallas_call(
-        functools.partial(scan_kernel, rows, kf),
+        out[:, at] = picked
+
+
+def prefix_sums(sums, squares, rank, spread, kf):
+    rows = rank.shape[1]
+    return pl.pallas_call(
+        prefix_kernel,
         in_specs=[VMEM] * 4,
         out_shape=jax.ShapeDtypeStruct((kf, rows), F32),
         out_specs=VMEM,
-        scratch_shapes=[pltpu.VMEM((groups * 2 * kf, rows), BF16), pltpu.VMEM((LO, rows), BF16)],
         compiler_params=pltpu.CompilerParams(**PARAMS),
         cost_estimate=pl.CostEstimate(
-            flops=4 * rows * LO * groups * 2 * kf, bytes_accessed=rows * kf * 24, transcendentals=0
+            flops=4 * rows * LO * (rows // LO) * kf, bytes_accessed=rows * kf * 24, transcendentals=0
         ),
-        name="scans",
-    )(tangent, risk, rank, squares)
+        name="prefix_sums",
+    )(sums, squares, rank, spread)
 
 
 def weight_kernel(kf, ex, *refs):
@@ -394,19 +473,19 @@
     for start in range(0, height, block):
         part = values[start : start + block]
         largest = jnp.max(jnp.abs(part), axis=0, keepdims=True)
-        power = jnp.ceil(jnp.log2(jnp.maximum(largest, 1e-30))) - 14.0
-        message[start : start + block] = jnp.round(part * jnp.exp2(-power)).astype(jnp.int32).astype(jnp.int16)
+        power = power_of(largest)
+        message[start : start + block] = to_short(part * jnp.exp2(-power))
         powers.append(power)
     powers.append(jnp.zeros((message.shape[0] - height - len(powers), values.shape[1]), F32))
-    message[height:] = jnp.concatenate(powers, axis=0).astype(jnp.int32).astype(jnp.int16)
+    message[height:] = to_short(jnp.concatenate(powers, axis=0))
 
 
 def decode(message, height):
     block = min(BLOCK, height)
-    powers = message[height:].astype(jnp.int32).astype(F32)
+    powers = from_short(message[height:])
     parts = []
     for i in range(height // block):
-        part = message[i * block : (i + 1) * block].astype(jnp.int32).astype(F32)
+        part = from_short(message[i * block : (i + 1) * block])
         parts.append(part * jnp.exp2(powers[i : i + 1]))
     return jnp.concatenate(parts, axis=0)
 
@@ -483,12 +562,11 @@
 
     linear, keep, send = products(dosages, coefficients, directions, feat)
     received = [swap(piece, "feat", 1) for piece in send]
-    linear = pair(linear, received[1])
-    linears = [linear] + [swap(linear, "feat", 2 * q) for q in range(1, feat // 2)]
-    joined = join(keep[1:], received[1:], linears[1:])
-    others = [swap(joined[q - 1], "feat", 2 * q) for q in reversed(range(1, feat // 2))]
-
-    risk, sums, ordered_events, total = risks(linears, rank, event_row, rows)
+    paired, joined = join(linear, keep[1:], received[1:])
+    others = [swap(joined[q - 1], "feat", 2 * q) for q in range(1, feat // 2)]
+    spread, table, masks = tables(rank, paired, rows, padded)
+
+    risk, sums, ordered_events, total = risks(paired, others, rank, event_row, table, rows)
     later = jnp.zeros_like(total)
     bit = 1
     while bit < ex:
@@ -496,13 +574,13 @@
         later = later + jnp.where((lax.axis_index("ex") & bit) == 0, other, 0.0)
         total = total + other
         bit *= 2
+    tangent, later_sums = suffix_sums(keep[0], received[0], others, risk, masks, table)
     cumulative, squares, ordered_squares, hazard_message = hazards(
-        later, sums, ordered_events, rank, rows
+        later, sums, ordered_events, rank, spread, rows
     )
-
-    tangent, message = block_totals([keep[0], received[0]] + others, risk, squares, hazard_message)
+    message = block_totals(tangent, risk, squares, hazard_message)
     messages = [message] + [swap(message, "ex", i) for i in range(1, ex)]
-    summed = scans(tangent, risk, rank, ordered_squares)
+    summed = prefix_sums(later_sums, ordered_squares, rank, spread, padded)
     own = weights(messages, tangent, summed, risk, cumulative, squares)
 
     chips = {0: own}

time: 68.7 us -> 67.7 us (0.985)
  starting transfers between devices: 24.5 us -> 18.9 us
  local copies, waits for them, and re-layouts: 1.59 us -> 5.86 us
  waiting for transfers between devices: 25.9 us -> 27.5 us
  Pallas kernels: 16.4 us -> 15.1 us
    ppermute x24 -> x21, starting transfers between devices: 24.5 us -> 18.9 us  [swap(): return lax.ppermute(x, axis, [(s, s ^ i) for s in range(count)])]
    unnamed x10 -> x18, local copies, waits for them, and re-layouts: 1.59 us -> 5.86 us
    ppermute x24 -> x21, waiting for transfers between devices: 25.9 us -> 27.5 us  [swap(): return lax.ppermute(x, axis, [(s, s ^ i) for s in range(count)])]
    pallas_call x4 -> x5, Pallas kernels: 7.1 us -> 6.4 us  [the longest x1 2.17 us: suffix_sums(): pl.pallas_call(functools.partial(suffix_kernel, len(messages)), in_specs=...]
  transfers between devices with their start and end apart: 24 -> 21, of which waited for: 12 -> 12; matrix products, arithmetic and copies ran while one was open for 0% -> 0% of each run, Pallas kernels for 13% -> 10%
where the time goes in v5:
time: 67.7 us; the launch traced here: 67.5 us
  waiting for transfers between devices  27.5 us (41%)
  starting transfers between devices  18.9 us (28%)
  Pallas kernels  15.1 us (22%)
  local copies, waits for them, and re-layouts  5.86 us (9%)
    ppermute x21, waiting for transfers between devices, swap(): return lax.ppermute(x, axis, [(s, s ^ i) for s in range(count)])  27.5 us
    ppermute x21, starting transfers between devices, swap(): return lax.ppermute(x, axis, [(s, s ^ i) for s in range(count)])  18.9 us
    unnamed x18, local copies, waits for them, and re-layouts  5.86 us
    pallas_call x1, Pallas kernels, products(): pl.pallas_call(functools.partial(product_kernel, feat, kf, chunk), in_spe...  4.73 us
    pallas_call x1, Pallas kernels, suffix_sums(): pl.pallas_call(functools.partial(suffix_kernel, len(messages)), in_specs=...  2.17 us
    pallas_call x1, Pallas kernels, hazards(): pl.pallas_call(functools.partial(hazard_kernel, rows), in_specs=[VMEM] *...  1.66 us
    pallas_call x1, Pallas kernels, tables(): pl.pallas_call(functools.partial(table_kernel, rows), in_specs=[VMEM, pl....  1.62 us
    pallas_call x1, Pallas kernels, prefix_sums(): pl.pallas_call(prefix_kernel, in_specs=[VMEM] * 4, out_shape=jax.ShapeDty...  1.52 us
  transfers between devices with their start and end apart: 21, of which 12 were waited for; matrix products, arithmetic and copies ran while one was open for 0% of the time, Pallas kernels for 10%

profile of v5, /device:TPU:0, one launch (start us, length us, event | category | flops | bytes accessed | tf_op | source)
XLA Modules:
  0.0 67.5 jit_solution(10222842586941674319)
XLA Ops:
  1.6 4.7 %products.1 = (f32[16,256]{1,0:T(8,128)S(1)}, f32[16,4096]{1,0:T(8,128)S(1)}, f32[16,4096]{1,0:T(8,128)S(1)}, f32[16,4096]{1,0:T(8,128)S(1)}, f32[16,4096]{1,0:T...) custom-call(bf16[512,128]{1,0:T(8,128)(2,1)S(1)} %copy-done.6, ...), custom_call_target="tpu_custom_call" | custom-call | flops 536870912 | bytes 6291456 | tf_op jit(solution)/shard_map/products/pallas_call | solution.py:114
  9.0 2.9 %collective-permute-start.4 = (s16[16,4736]{1,0:T(8,128)(2,1)S(1)}, s16[16,4736]{1,0:T(8,128)(2,1)S(1)}, u32[]{:S(2)}, u32[]{:S(2)}) collective-permute-start(s16[16,4736]{1,0:T(8,128)(2,1)S(1)} %get-tuple-element.40), channel_id=1, source_target_pairs={{0,2},{1,3},{2,0},{3,1},{4,6},{5,7},{6,4},{7,5},{8,10},{9,11},{10,... | collective-permute-start | bytes 454664 | tf_op jit(solution)/shard_map/ppermute | solution.py:24
  12.0 1.5 %collective-permute-start.5 = (s16[16,4736]{1,0:T(8,128)(2,1)S(1)}, s16[16,4736]{1,0:T(8,128)(2,1)S(1)}, u32[]{:S(2)}, u32[]{:S(2)}) collective-permute-start(s16[16,4736]{1,0:T(8,128)(2,1)S(1)} %get-tuple-element.41), channel_id=1, source_target_pairs={{0,4},{1,5},{2,6},{3,7},{4,0},{5,1},{6,2},{7,3},{8,12},{9,13},{10,... | collective-permute-start | bytes 454664 | tf_op jit(solution)/shard_map/ppermute | solution.py:24
  13.5 1.6 %tables.1 = (bf16[256,4096]{1,0:T(8,128)(2,1)S(1)}, bf16[4096,256]{1,0:T(8,128)(2,1)S(1)}, bf16[16,16,4096]{2,1,0:T(8,128)(2,1)S(1)}) custom-call(s32[1,4096]{1,0:T(1,128)S(1)} %bitcast.2, f32[16,256]{1,0:T(8,128)S(1)} %get-tuple-element.43.waited.linear), custom_call_target="tpu_custom_call" | custom-call | flops 8388608 | bytes 6291456 | tf_op jit(solution)/shard_map/tables/pallas_call | solution.py:210
  15.2 1.3 %copy-done.1 = bf16[256,4096]{1,0:T(8,128)(2,1)} copy-done((bf16[256,4096]{1,0:T(8,128)(2,1)}, bf16[256,4096]{1,0:T(8,128)(2,1)S(1)}, u32[]{:S(2)}) %copy-start.1) | copy-done | bytes 2097176
  16.5 1.3 %copy-done.3 = bf16[16,16,4096]{2,1,0:T(8,128)(2,1)} copy-done((bf16[16,16,4096]{2,1,0:T(8,128)(2,1)}, bf16[16,16,4096]{2,1,0:T(8,128)(2,1)S(1)}, u32[]{:S(2)}) %copy-start.3) | copy-done | bytes 2097176
  17.8 3.1 %collective-permute-done.5.refs_1_ = s16[16,4736]{1,0:T(8,128)(2,1)S(1)} collective-permute-done((s16[16,4736]{1,0:T(8,128)(2,1)S(1)}, s16[16,4736]{1,0:T(8,128)(2,1)S(1)}, u32[]{:S(2)}, u32[]{:S(2)}) %collective-permute-start.5) | collective-permute-done | bytes 151584 | tf_op jit(solution)/shard_map/ppermute | solution.py:24
  21.9 1.6 %collective-permute-start.7 = (f32[8,128]{1,0:T(8,128)S(1)}, f32[8,128]{1,0:T(8,128)S(1)}, u32[]{:S(2)}, u32[]{:S(2)}) collective-permute-start(f32[8,128]{1,0:T(8,128)S(1)} %get-tuple-element.48), channel_id=1, source_target_pairs={{0,8},{8,0},{16,24},{24,16},{1,9},{9,1},{17,25},{25,17},{2,10},{10... | collective-permute-start | bytes 12296 | tf_op jit(solution)/shard_map/ppermute | solution.py:24
  23.6 2.0 %collective-permute-done.7 = f32[8,128]{1,0:T(8,128)S(1)} collective-permute-done((f32[8,128]{1,0:T(8,128)S(1)}, f32[8,128]{1,0:T(8,128)S(1)}, u32[]{:S(2)}, u32[]{:S(2)}) %collective-permute-start.7) | collective-permute-done | bytes 4128 | tf_op jit(solution)/shard_map/ppermute | solution.py:24
  25.6 2.6 %collective-permute-start.8 = (f32[8,128]{1,0:T(8,128)S(1)}, f32[8,128]{1,0:T(8,128)S(1)}, u32[]{:S(2)}, u32[]{:S(2)}) collective-permute-start(f32[8,128]{1,0:T(8,128)S(1)} %add.9), channel_id=1, source_target_pairs={{0,16},{8,24},{16,0},{24,8},{1,17},{9,25},{17,1},{25,9},{2,18},{10... | collective-permute-start | bytes 12296 | tf_op jit(solution)/shard_map/ppermute | solution.py:24
  28.2 1.6 %copy-done.4 = bf16[16,16,4096]{2,1,0:T(8,128)(2,1)S(1)} copy-done((bf16[16,16,4096]{2,1,0:T(8,128)(2,1)S(1)}, bf16[16,16,4096]{2,1,0:T(8,128)(2,1)}, u32[]{:S(2)}) %copy-start.4) | copy-done | bytes 2097176
  29.8 2.2 %suffix_sums.1 = (f32[16,4096]{1,0:T(8,128)S(1)}, f32[256,256]{1,0:T(8,128)S(1)}) custom-call(f32[16,4096]{1,0:T(8,128)S(1)} %get-tuple-element.31.own, f32[16,4096]{1,0:T(8,128)S(1)} %collective-permute-done.other, s16[16,4736]{1,0:T(8,128)(2,1)S(1)} %collective-permute-done.4.refs_0_, s16[16,4736]{1,0:T(8,128)(2,1)S(1)} %collective-permute-done.5.refs_1_, ...), custom_call_target="tpu_custom_call" | custom-call | flops 1073741824 | bytes 1572864 | tf_op jit(solution)/shard_map/suffix_sums/pallas_call | solution.py:376
  32.0 1.7 %hazards.1 = (f32[1,4096]{1,0:T(1,128)S(1)}, f32[1,4096]{1,0:T(1,128)S(1)}, f32[16,256]{1,0:T(8,128)S(1)}, f32[8,128]{1,0:T(8,128)S(1)}) custom-call(f32[8,128]{1,0:T(8,128)S(1)} %get-tuple-element.58.later, f32[16,256]{1,0:T(8,128)S(1)} %get-tuple-element.49.sums, f32[16,256]{1,0:T(8,128)S(1)} %get-tuple-element.50.events, s32[1,4096]{1,0:T(1,128)S(1)} %bitcast.4, ...), custom_call_target="tpu_custom_call" | custom-call | flops 209715200 | bytes 262144 | tf_op jit(solution)/shard_map/hazards/pallas_call | solution.py:304
  33.8 1.6 %collective-permute-start.9 = (f32[40,128]{1,0:T(8,128)S(1)}, f32[40,128]{1,0:T(8,128)S(1)}, u32[]{:S(2)}, u32[]{:S(2)}) collective-permute-start(f32[40,128]{1,0:T(8,128)S(1)} %block_totals.1.refs_0_), channel_id=1, source_target_pairs={{0,8},{8,0},{16,24},{24,16},{1,9},{9,1},{17,25},{25,17},{2,10},{10... | collective-permute-start | bytes 61448 | tf_op jit(solution)/shard_map/ppermute | solution.py:24
  36.1 2.1 %collective-permute-start.11 = (f32[40,128]{1,0:T(8,128)S(1)}, f32[40,128]{1,0:T(8,128)S(1)}, u32[]{:S(2)}, u32[]{:S(2)}) collective-permute-start(f32[40,128]{1,0:T(8,128)S(1)} %block_totals.1.refs_0_), channel_id=1, source_target_pairs={{0,24},{8,16},{16,8},{24,0},{1,25},{9,17},{17,9},{25,1},{2,26},{10... | collective-permute-start | bytes 61448 | tf_op jit(solution)/shard_map/ppermute | solution.py:24
  38.2 1.5 %prefix_sums.1.refs_5_ = f32[16,4096]{1,0:T(8,128)S(1)} custom-call(f32[256,256]{1,0:T(8,128)S(1)} %get-tuple-element.54.sums, f32[16,256]{1,0:T(8,128)S(1)} %get-tuple-element.55.squares, s32[1,4096]{1,0:T(1,128)S(1)} %bitcast.5, bf16[256,4096]{1,0:T(8,128)(2,1)S(1)} %copy-done.2), custom_call_target="tpu_custom_call" | custom-call | flops 1073741824 | bytes 1572864 | tf_op jit(solution)/shard_map/prefix_sums/pallas_call | solution.py:421
  40.2 1.5 %collective-permute-done.11.refs_3_ = f32[40,128]{1,0:T(8,128)S(1)} collective-permute-done((f32[40,128]{1,0:T(8,128)S(1)}, f32[40,128]{1,0:T(8,128)S(1)}, u32[]{:S(2)}, u32[]{:S(2)}) %collective-permute-start.11) | collective-permute-done | bytes 20512 | tf_op jit(solution)/shard_map/ppermute | solution.py:24
  41.9 1.3 %collective-permute-start.13 = (bf16[16,4096]{1,0:T(8,128)(2,1)S(1)}, bf16[16,4096]{1,0:T(8,128)(2,1)S(1)}, u32[]{:S(2)}, u32[]{:S(2)}) collective-permute-start(bf16[16,4096]{1,0:T(8,128)(2,1)S(1)} %weights.1.refs_0_), channel_id=1, source_target_pairs={{0,2},{1,3},{2,0},{3,1},{4,6},{5,7},{6,4},{7,5},{8,10},{9,11},{10,... | collective-permute-start | bytes 393224 | tf_op jit(solution)/shard_map/ppermute | solution.py:24
  44.0 1.4 %collective-permute-start.17 = (bf16[16,4096]{1,0:T(8,128)(2,1)S(1)}, bf16[16,4096]{1,0:T(8,128)(2,1)S(1)}, u32[]{:S(2)}, u32[]{:S(2)}) collective-permute-start(bf16[16,4096]{1,0:T(8,128)(2,1)S(1)} %weights.1.refs_0_), channel_id=1, source_target_pairs={{0,6},{1,7},{2,4},{3,5},{4,2},{5,3},{6,0},{7,1},{8,14},{9,15},{10,... | collective-permute-start | bytes 393224 | tf_op jit(solution)/shard_map/ppermute | solution.py:24
  45.5 1.5 %collective-permute-done.13.refs_2_ = bf16[16,4096]{1,0:T(8,128)(2,1)S(1)} collective-permute-done((bf16[16,4096]{1,0:T(8,128)(2,1)S(1)}, bf16[16,4096]{1,0:T(8,128)(2,1)S(1)}, u32[]{:S(2)}, u32[]{:S(2)}) %collective-permute-start.13) | collective-permute-done | bytes 131104 | tf_op jit(solution)/shard_map/ppermute | solution.py:24
  48.2 1.7 %collective-permute-done.17.refs_6_ = bf16[16,4096]{1,0:T(8,128)(2,1)S(1)} collective-permute-done((bf16[16,4096]{1,0:T(8,128)(2,1)S(1)}, bf16[16,4096]{1,0:T(8,128)(2,1)S(1)}, u32[]{:S(2)}, u32[]{:S(2)}) %collective-permute-start.17) | collective-permute-done | bytes 131104 | tf_op jit(solution)/shard_map/ppermute | solution.py:24
  49.9 1.3 %collective-permute-done.18.refs_7_ = bf16[16,4096]{1,0:T(8,128)(2,1)S(1)} collective-permute-done((bf16[16,4096]{1,0:T(8,128)(2,1)S(1)}, bf16[16,4096]{1,0:T(8,128)(2,1)S(1)}, u32[]{:S(2)}, u32[]{:S(2)}) %collective-permute-start.18) | collective-permute-done | bytes 131104 | tf_op jit(solution)/shard_map/ppermute | solution.py:24
  52.3 5.6 %collective-permute-done.19.other = s16[528,128]{1,0:T(8,128)(2,1)S(1)} collective-permute-done((s16[528,128]{1,0:T(8,128)(2,1)S(1)}, s16[528,128]{1,0:T(8,128)(2,1)S(1)}, u32[]{:S(2)}, u32[]{:S(2)}) %collective-permute-start.19) | collective-permute-done | bytes 135200 | tf_op jit(solution)/shard_map/ppermute | solution.py:24
  59.1 7.7 %collective-permute-done.20.other = s16[528,128]{1,0:T(8,128)(2,1)S(1)} collective-permute-done((s16[528,128]{1,0:T(8,128)(2,1)S(1)}, s16[528,128]{1,0:T(8,128)(2,1)S(1)}, u32[]{:S(2)}, u32[]{:S(2)}) %collective-permute-start.20) | collective-permute-done | bytes 135200 | tf_op jit(solution)/shard_map/ppermute | solution.py:24
  (50 shorter events, 11.8 us)
Async XLA Ops:
  0.0 13.5 %copy-start.5 = (s32[4096]{0:T(1024)S(1)}, s32[4096]{0:T(1024)}, u32[]{:S(2)}) copy-start(s32[4096]{0:T(1024)} %param.8) | copy-start | bytes 49156
  1.6 19.3 %copy-start.7 = (s32[4096]{0:T(1024)S(1)}, s32[4096]{0:T(1024)}, u32[]{:S(2)}) copy-start(s32[4096]{0:T(1024)} %param.9) | copy-start | bytes 49156
  6.3 2.5 %collective-permute-start.1 = (f32[16,4352]{1,0:T(8,128)S(1)}, f32[16,4352]{1,0:T(8,128)S(1)}, u32[]{:S(2)}, u32[]{:S(2)}) collective-permute-start(f32[16,4352]{1,0:T(8,128)S(1)} %get-tuple-element.37), channel_id=1, source_target_pairs={{0,1},{1,0},{2,3},{3,2},{4,5},{5,4},{6,7},{7,6},{8,9},{9,8},{10,11... | collective-permute-start | bytes 835592 | tf_op jit(solution)/shard_map/ppermute | solution.py:24
  6.9 1.6 %collective-permute-start.2 = (f32[16,4096]{1,0:T(8,128)S(1)}, f32[16,4096]{1,0:T(8,128)S(1)}, u32[]{:S(2)}, u32[]{:S(2)}) collective-permute-start(f32[16,4096]{1,0:T(8,128)S(1)} %get-tuple-element.38), channel_id=1, source_target_pairs={{0,1},{1,0},{2,3},{3,2},{4,5},{5,4},{6,7},{7,6},{8,9},{9,8},{10,11... | collective-permute-start | bytes 786440 | tf_op jit(solution)/shard_map/ppermute | solution.py:24
  6.9 1.9 %collective-permute-start.3 = (f32[16,4096]{1,0:T(8,128)S(1)}, f32[16,4096]{1,0:T(8,128)S(1)}, u32[]{:S(2)}, u32[]{:S(2)}) collective-permute-start(f32[16,4096]{1,0:T(8,128)S(1)} %get-tuple-element.39), channel_id=1, source_target_pairs={{0,1},{1,0},{2,3},{3,2},{4,5},{5,4},{6,7},{7,6},{8,9},{9,8},{10,11... | collective-permute-start | bytes 786440 | tf_op jit(solution)/shard_map/ppermute | solution.py:24
  7.4 20.8 %collective-permute-start = (f32[16,4096]{1,0:T(8,128)S(1)}, f32[16,4096]{1,0:T(8,128)S(1)}, u32[]{:S(2)}, u32[]{:S(2)}) collective-permute-start(f32[16,4096]{1,0:T(8,128)S(1)} %get-tuple-element.32), channel_id=1, source_target_pairs={{0,1},{1,0},{2,3},{3,2},{4,5},{5,4},{6,7},{7,6},{8,9},{9,8},{10,11... | collective-permute-start | bytes 786440 | tf_op jit(solution)/shard_map/ppermute | solution.py:24
  9.0 8.8 %collective-permute-start.4 = (s16[16,4736]{1,0:T(8,128)(2,1)S(1)}, s16[16,4736]{1,0:T(8,128)(2,1)S(1)}, u32[]{:S(2)}, u32[]{:S(2)}) collective-permute-start(s16[16,4736]{1,0:T(8,128)(2,1)S(1)} %get-tuple-element.40), channel_id=1, source_target_pairs={{0,2},{1,3},{2,0},{3,1},{4,6},{5,7},{6,4},{7,5},{8,10},{9,11},{10,... | collective-permute-start | bytes 454664 | tf_op jit(solution)/shard_map/ppermute | solution.py:24
  12.0 8.9 %collective-permute-start.5 = (s16[16,4736]{1,0:T(8,128)(2,1)S(1)}, s16[16,4736]{1,0:T(8,128)(2,1)S(1)}, u32[]{:S(2)}, u32[]{:S(2)}) collective-permute-start(s16[16,4736]{1,0:T(8,128)(2,1)S(1)} %get-tuple-element.41), channel_id=1, source_target_pairs={{0,4},{1,5},{2,6},{3,7},{4,0},{5,1},{6,2},{7,3},{8,12},{9,13},{10,... | collective-permute-start | bytes 454664 | tf_op jit(solution)/shard_map/ppermute | solution.py:24
  13.5 7.4 %collective-permute-start.6 = (s16[16,4736]{1,0:T(8,128)(2,1)S(1)}, s16[16,4736]{1,0:T(8,128)(2,1)S(1)}, u32[]{:S(2)}, u32[]{:S(2)}) collective-permute-start(s16[16,4736]{1,0:T(8,128)(2,1)S(1)} %get-tuple-element.42), channel_id=1, source_target_pairs={{0,6},{1,7},{2,4},{3,5},{4,2},{5,3},{6,0},{7,1},{8,14},{9,15},{10,... | collective-permute-start | bytes 454664 | tf_op jit(solution)/shard_map/ppermute | solution.py:24
  21.9 3.7 %collective-permute-start.7 = (f32[8,128]{1,0:T(8,128)S(1)}, f32[8,128]{1,0:T(8,128)S(1)}, u32[]{:S(2)}, u32[]{:S(2)}) collective-permute-start(f32[8,128]{1,0:T(8,128)S(1)} %get-tuple-element.48), channel_id=1, source_target_pairs={{0,8},{8,0},{16,24},{24,16},{1,9},{9,1},{17,25},{25,17},{2,10},{10... | collective-permute-start | bytes 12296 | tf_op jit(solution)/shard_map/ppermute | solution.py:24
  25.6 6.4 %collective-permute-start.8 = (f32[8,128]{1,0:T(8,128)S(1)}, f32[8,128]{1,0:T(8,128)S(1)}, u32[]{:S(2)}, u32[]{:S(2)}) collective-permute-start(f32[8,128]{1,0:T(8,128)S(1)} %add.9), channel_id=1, source_target_pairs={{0,16},{8,24},{16,0},{24,8},{1,17},{9,25},{17,1},{25,9},{2,18},{10... | collective-permute-start | bytes 12296 | tf_op jit(solution)/shard_map/ppermute | solution.py:24
  33.8 6.0 %collective-permute-start.9 = (f32[40,128]{1,0:T(8,128)S(1)}, f32[40,128]{1,0:T(8,128)S(1)}, u32[]{:S(2)}, u32[]{:S(2)}) collective-permute-start(f32[40,128]{1,0:T(8,128)S(1)} %block_totals.1.refs_0_), channel_id=1, source_target_pairs={{0,8},{8,0},{16,24},{24,16},{1,9},{9,1},{17,25},{25,17},{2,10},{10... | collective-permute-start | bytes 61448 | tf_op jit(solution)/shard_map/ppermute | solution.py:24
  35.4 4.8 %collective-permute-start.10 = (f32[40,128]{1,0:T(8,128)S(1)}, f32[40,128]{1,0:T(8,128)S(1)}, u32[]{:S(2)}, u32[]{:S(2)}) collective-permute-start(f32[40,128]{1,0:T(8,128)S(1)} %block_totals.1.refs_0_), channel_id=1, source_target_pairs={{0,16},{8,24},{16,0},{24,8},{1,17},{9,25},{17,1},{25,9},{2,18},{10... | collective-permute-start | bytes 61448 | tf_op jit(solution)/shard_map/ppermute | solution.py:24
  36.1 5.6 %collective-permute-start.11 = (f32[40,128]{1,0:T(8,128)S(1)}, f32[40,128]{1,0:T(8,128)S(1)}, u32[]{:S(2)}, u32[]{:S(2)}) collective-permute-start(f32[40,128]{1,0:T(8,128)S(1)} %block_totals.1.refs_0_), channel_id=1, source_target_pairs={{0,24},{8,16},{16,8},{24,0},{1,25},{9,17},{17,9},{25,1},{2,26},{10... | collective-permute-start | bytes 61448 | tf_op jit(solution)/shard_map/ppermute | solution.py:24
  38.2 13.0 %copy-start = (bf16[4096,512]{1,0:T(8,128)(2,1)S(1)}, bf16[4096,512]{1,0:T(8,128)(2,1)}, u32[]{:S(2)}) copy-start(bf16[4096,512]{1,0:T(8,128)(2,1)} %refs_8_.1) | copy-start | bytes 12582916
  41.9 5.0 %collective-permute-start.13 = (bf16[16,4096]{1,0:T(8,128)(2,1)S(1)}, bf16[16,4096]{1,0:T(8,128)(2,1)S(1)}, u32[]{:S(2)}, u32[]{:S(2)}) collective-permute-start(bf16[16,4096]{1,0:T(8,128)(2,1)S(1)} %weights.1.refs_0_), channel_id=1, source_target_pairs={{0,2},{1,3},{2,0},{3,1},{4,6},{5,7},{6,4},{7,5},{8,10},{9,11},{10,... | collective-permute-start | bytes 393224 | tf_op jit(solution)/shard_map/ppermute | solution.py:24
  43.2 5.0 %collective-permute-start.15 = (bf16[16,4096]{1,0:T(8,128)(2,1)S(1)}, bf16[16,4096]{1,0:T(8,128)(2,1)S(1)}, u32[]{:S(2)}, u32[]{:S(2)}) collective-permute-start(bf16[16,4096]{1,0:T(8,128)(2,1)S(1)} %weights.1.refs_0_), channel_id=1, source_target_pairs={{0,4},{1,5},{2,6},{3,7},{4,0},{5,1},{6,2},{7,3},{8,12},{9,13},{10,... | collective-permute-start | bytes 393224 | tf_op jit(solution)/shard_map/ppermute | solution.py:24
  44.0 5.9 %collective-permute-start.17 = (bf16[16,4096]{1,0:T(8,128)(2,1)S(1)}, bf16[16,4096]{1,0:T(8,128)(2,1)S(1)}, u32[]{:S(2)}, u32[]{:S(2)}) collective-permute-start(bf16[16,4096]{1,0:T(8,128)(2,1)S(1)} %weights.1.refs_0_), channel_id=1, source_target_pairs={{0,6},{1,7},{2,4},{3,5},{4,2},{5,3},{6,0},{7,1},{8,14},{9,15},{10,... | collective-permute-start | bytes 393224 | tf_op jit(solution)/shard_map/ppermute | solution.py:24
  45.5 4.4 %collective-permute-start.12 = (bf16[16,4096]{1,0:T(8,128)(2,1)S(1)}, bf16[16,4096]{1,0:T(8,128)(2,1)S(1)}, u32[]{:S(2)}, u32[]{:S(2)}) collective-permute-start(bf16[16,4096]{1,0:T(8,128)(2,1)S(1)} %weights.1.refs_0_), channel_id=1, source_target_pairs={{0,1},{1,0},{2,3},{3,2},{4,5},{5,4},{6,7},{7,6},{8,9},{9,8},{10,11... | collective-permute-start | bytes 393224 | tf_op jit(solution)/shard_map/ppermute | solution.py:24
  47.0 3.0 %collective-permute-start.14 = (bf16[16,4096]{1,0:T(8,128)(2,1)S(1)}, bf16[16,4096]{1,0:T(8,128)(2,1)S(1)}, u32[]{:S(2)}, u32[]{:S(2)}) collective-permute-start(bf16[16,4096]{1,0:T(8,128)(2,1)S(1)} %collective-permute-done.13.refs_2_), channel_id=1, source_target_pairs={{0,1},{1,0},{2,3},{3,2},{4,5},{5,4},{6,7},{7,6},{8,9},{9,8},{10,11... | collective-permute-start | bytes 393224 | tf_op jit(solution)/shard_map/ppermute | solution.py:24
  48.2 1.7 %collective-permute-start.16 = (bf16[16,4096]{1,0:T(8,128)(2,1)S(1)}, bf16[16,4096]{1,0:T(8,128)(2,1)S(1)}, u32[]{:S(2)}, u32[]{:S(2)}) collective-permute-start(bf16[16,4096]{1,0:T(8,128)(2,1)S(1)} %collective-permute-done.15.refs_4_), channel_id=1, source_target_pairs={{0,1},{1,0},{2,3},{3,2},{4,5},{5,4},{6,7},{7,6},{8,9},{9,8},{10,11... | collective-permute-start | bytes 393224 | tf_op jit(solution)/shard_map/ppermute | solution.py:24
  49.9 1.3 %collective-permute-start.18 = (bf16[16,4096]{1,0:T(8,128)(2,1)S(1)}, bf16[16,4096]{1,0:T(8,128)(2,1)S(1)}, u32[]{:S(2)}, u32[]{:S(2)}) collective-permute-start(bf16[16,4096]{1,0:T(8,128)(2,1)S(1)} %collective-permute-done.17.refs_6_), channel_id=1, source_target_pairs={{0,1},{1,0},{2,3},{3,2},{4,5},{5,4},{6,7},{7,6},{8,9},{9,8},{10,11... | collective-permute-start | bytes 393224 | tf_op jit(solution)/shard_map/ppermute | solution.py:24
  52.2 5.7 %collective-permute-start.19 = (s16[528,128]{1,0:T(8,128)(2,1)S(1)}, s16[528,128]{1,0:T(8,128)(2,1)S(1)}, u32[]{:S(2)}, u32[]{:S(2)}) collective-permute-start(s16[528,128]{1,0:T(8,128)(2,1)S(1)} %gradients.1.mine), channel_id=1, source_target_pairs={{0,8},{8,0},{16,24},{24,16},{1,9},{9,1},{17,25},{25,17},{2,10},{10... | collective-permute-start | bytes 405512 | tf_op jit(solution)/shard_map/ppermute | solution.py:24
  58.1 8.7 %collective-permute-start.20 = (s16[528,128]{1,0:T(8,128)(2,1)S(1)}, s16[528,128]{1,0:T(8,128)(2,1)S(1)}, u32[]{:S(2)}, u32[]{:S(2)}) collective-permute-start(s16[528,128]{1,0:T(8,128)(2,1)S(1)} %merge.1.mine), channel_id=1, source_target_pairs={{0,16},{8,24},{16,0},{24,8},{1,17},{9,25},{17,1},{25,9},{2,18},{10... | collective-permute-start | bytes 405512 | tf_op jit(solution)/shard_map/ppermute | solution.py:24
  (6 other events, 8.1 us)

commit v6 on v5

--- a/solution.py
+++ b/solution.py
@@ -13,9 +13,8 @@
 BLOCK = 64
 SPAN = 512
 VMEM = pl.BlockSpec(memory_space=pltpu.VMEM)
-HIGHEST = lax.Precision.HIGHEST
 HBM = pl.BlockSpec(memory_space=pltpu.HBM)
-PRODUCT_BYTES = 48 * 1024 * 1024
+PRODUCT_BYTES = 24 * 1024 * 1024
 PARAMS = dict(vmem_limit_bytes=24 * 1024 * 1024)
 
 
@@ -44,10 +43,6 @@
     first = lax.broadcasted_iota(jnp.int32, (n, n), 0)
     second = lax.broadcasted_iota(jnp.int32, (n, n), 1)
     return jnp.where(keep(first, second), 1.0, 0.0)
-
-
-def exact_dot(a, b):
-    return jnp.dot(a, b, precision=HIGHEST, preferred_element_type=F32)
 
 
 def dot_binary(a, b):
@@ -55,6 +50,15 @@
     total = None
     for part in split_three(a):
         term = jnp.dot(part.astype(BF16), b, preferred_element_type=F32)
+        total = term if total is None else total + term
+    return total
+
+
+def binary_dot(a, b):
+    a = a.astype(BF16)
+    total = None
+    for part in split_three(b):
+        term = jnp.dot(a, part.astype(BF16), preferred_element_type=F32)
         total = term if total is None else total + term
     return total
 
@@ -133,7 +137,7 @@
             flops=2 * persons * variants * k, bytes_accessed=persons * (variants * 2 + k * 4), transcendentals=0
         ),
         name="products",
-    )(directions, coefficients, dosages)
+    )(*[pltpu.with_memory_space_constraint(x, pltpu.HBM) for x in (directions, coefficients, dosages)])
     return out[0], out[1 : 1 + feat // 2], out[1 + feat // 2 :]
 
 
@@ -189,35 +193,25 @@
     return out[0], out[1:]
 
 
-def table_kernel(rows, rank, waited, spread, table, masks):
-    groups, height, _ = masks.shape
+def table_kernel(rows, rank, waited, table):
     chunk = min(512, rows)
     lane = lax.broadcasted_iota(jnp.int32, (chunk, 128), 1)
     for start in range(0, rows, chunk):
         at = slice(start, start + chunk)
-        place = lax.rem(rank[:, at], rows)
-        group, inner = place // LO, lax.rem(place, LO)
-        spread[:, at] = one_hot(inner, LO)
+        inner = lax.rem(rank[:, at], LO)
         column = jnp.broadcast_to(inner.astype(F32), (128, chunk)).T.astype(jnp.int32)
         for first in range(0, LO, 128):
             table[at, first : first + 128] = jnp.where(column == lane + first, 1.0, 0.0).astype(BF16)
-        for g in range(groups):
-            mask = jnp.where(group == g, 1.0, 0.0)
-            masks[g, :, at] = jnp.broadcast_to(mask, (height, chunk)).astype(BF16)
-
-
-def tables(rank, waited, rows, height):
+
+
+def tables(rank, waited, rows):
     return pl.pallas_call(
         functools.partial(table_kernel, rows),
         in_specs=[VMEM, pl.BlockSpec(memory_space=pl.ANY)],
-        out_shape=[
-            jax.ShapeDtypeStruct((LO, rows), BF16),
-            jax.ShapeDtypeStruct((rows, LO), BF16),
-            jax.ShapeDtypeStruct((rows // LO, height, rows), BF16),
-        ],
-        out_specs=[VMEM] * 3,
-        compiler_params=pltpu.CompilerParams(**PARAMS),
-        cost_estimate=pl.CostEstimate(flops=rows * LO * 8, bytes_accessed=rows * LO * 6, transcendentals=0),
+        out_shape=jax.ShapeDtypeStruct((rows, LO), BF16),
+        out_specs=VMEM,
+        compiler_params=pltpu.CompilerParams(**PARAMS),
+        cost_estimate=pl.CostEstimate(flops=rows * LO * 8, bytes_accessed=rows * LO * 2, transcendentals=0),
         name="tables",
     )(rank, waited)
 
@@ -243,7 +237,7 @@
     happened = sorted_all[3 * groups :]
     inside = dot_binary(ordered, triangle(LO, lambda a, b: a >= b))
     totals = jnp.broadcast_to(inside[:, :1], inside.shape)
-    carried = exact_dot(triangle(groups, lambda a, b: a < b), totals)
+    carried = binary_dot(triangle(groups, lambda a, b: a < b), totals)
     sums_out[...] = inside + carried
     events_out[...] = happened
     everything = jnp.sum(totals, axis=0, keepdims=True)[:, :128]
@@ -269,47 +263,45 @@
     )(linear, *messages, rank, events, table)
 
 
-def hazard_kernel(rows, later, sums, events, rank, spread, *outs):
+def hazard_kernel(rows, later, sums, events, rank, *outs):
     cumulative, squares, ordered_squares, message = outs
     groups = rows // LO
     risk_sum = sums[...] + later[0:1, 0:1]
     hazard = events[...] / risk_sum
     square = events[...] / (risk_sum * risk_sum)
     ordered_squares[...] = square
-    both = jnp.concatenate([hazard, square], axis=0)
-    inside = dot_binary(both, triangle(LO, lambda a, b: a <= b))
-    totals = jnp.broadcast_to(inside[:, LO - 1 :], inside.shape)
+    inside = dot_binary(jnp.concatenate([hazard, square], axis=0), triangle(LO, lambda a, b: a <= b))
+    totals = jnp.broadcast_to(inside[:, LO - 1 :], (2 * groups, 128))
+    place = lax.rem(rank[...], rows)
+    mask = one_hot(place // LO, groups, F32)
+    placed = dot_binary(inside, one_hot(lax.rem(place, LO), LO))
     before = triangle(groups, lambda a, b: a > b)
-    carried = jnp.concatenate(
-        [exact_dot(before, totals[:groups]), exact_dot(before, totals[groups:])], axis=0
-    )
+    for first, out in ((0, cumulative), (groups, squares)):
+        carried = binary_dot(before, totals[first : first + groups])[:, :1]
+        out[...] = jnp.sum(mask * (placed[first : first + groups] + carried), axis=0, keepdims=True)
     message[...] = jnp.concatenate(
         [
-            jnp.sum(totals[:groups], axis=0, keepdims=True)[:, :128],
-            jnp.sum(totals[groups:], axis=0, keepdims=True)[:, :128],
+            jnp.sum(totals[:groups], axis=0, keepdims=True),
+            jnp.sum(totals[groups:], axis=0, keepdims=True),
             jnp.zeros((6, 128), F32),
         ],
         axis=0,
     )
-    mask = one_hot(lax.rem(rank[...], rows) // LO, groups, F32)
-    placed = dot_binary(inside + carried, spread[...])
-    cumulative[...] = jnp.sum(mask * placed[:groups], axis=0, keepdims=True)
-    squares[...] = jnp.sum(mask * placed[groups:], axis=0, keepdims=True)
-
-
-def hazards(later, sums, events, rank, spread, rows):
+
+
+def hazards(later, sums, events, rank, rows):
     groups = rows // LO
     row = jax.ShapeDtypeStruct((1, rows), F32)
     small = jax.ShapeDtypeStruct((8, 128), F32)
     return pl.pallas_call(
         functools.partial(hazard_kernel, rows),
-        in_specs=[VMEM] * 5,
+        in_specs=[VMEM] * 4,
         out_shape=[row, row, jax.ShapeDtypeStruct((groups, LO), F32), small],
         out_specs=[VMEM] * 4,
         compiler_params=pltpu.CompilerParams(**PARAMS),
         cost_estimate=pl.CostEstimate(flops=rows * LO * 200, bytes_accessed=rows * 64, transcendentals=0),
         name="hazards",
-    )(later, sums, events, rank, spread)
+    )(later, sums, events, rank)
 
 
 def total_kernel(tangent, risk, squares, hazard_message, message):
@@ -337,10 +329,10 @@
 
 
 def suffix_kernel(parts, own, other, *refs):
-    messages, (risk, masks, table) = refs[:parts], refs[parts : parts + 3]
+    messages, (risk, rank, table) = refs[:parts], refs[parts : parts + 3]
     tangent_out, sums, lhs = refs[parts + 3 :]
     kf, rows = own.shape
-    groups = masks.shape[0]
+    groups = rows // LO
     span = min(SPAN, rows)
     powers = [jnp.exp2(from_short(part[:, rows + 2 * LO :])) for part in messages]
     for i in range(rows // span):
@@ -351,9 +343,11 @@
         tangent_out[:, at] = tangent
         high, low = split_two(tangent * risk[:, at])
         high, low = high.astype(BF16), low.astype(BF16)
+        group = jnp.broadcast_to(lax.rem(rank[:, at], rows) // LO, (kf, span))
         for g in range(groups):
-            lhs[2 * g * kf : (2 * g + 1) * kf, at] = high * masks[g, :, at]
-            lhs[(2 * g + 1) * kf : (2 * g + 2) * kf, at] = low * masks[g, :, at]
+            mask = jnp.where(group == g, 1.0, 0.0).astype(BF16)
+            lhs[2 * g * kf : (2 * g + 1) * kf, at] = high * mask
+            lhs[(2 * g + 1) * kf : (2 * g + 2) * kf, at] = low * mask
     ordered = jnp.dot(lhs[...], table[...], preferred_element_type=F32)
     ordered = jnp.concatenate(
         [
@@ -370,7 +364,7 @@
         carried = carried + inside[rows_of, :1]
 
 
-def suffix_sums(own, other, messages, risk, masks, table):
+def suffix_sums(own, other, messages, risk, rank, table):
     kf, rows = own.shape
     groups = rows // LO
     return pl.pallas_call(
@@ -387,10 +381,10 @@
             flops=2 * rows * LO * groups * 2 * kf, bytes_accessed=rows * kf * 24, transcendentals=0
         ),
         name="suffix_sums",
-    )(own, other, *messages, risk, masks, table)
-
-
-def prefix_kernel(sums, squares, rank, spread, out):
+    )(own, other, *messages, risk, rank, table)
+
+
+def prefix_kernel(sums, squares, rank, out):
     kf, rows = out.shape
     groups = squares.shape[0]
     chunk = min(512, rows)
@@ -406,9 +400,11 @@
     high, low = high.astype(BF16), low.astype(BF16)
     for start in range(0, rows, chunk):
         at = slice(start, start + chunk)
-        group = lax.rem(rank[:, at], rows) // LO
-        placed = jnp.dot(high, spread[:, at], preferred_element_type=F32) + jnp.dot(
-            low, spread[:, at], preferred_element_type=F32
+        place = lax.rem(rank[:, at], rows)
+        group = place // LO
+        spread = one_hot(lax.rem(place, LO), LO)
+        placed = jnp.dot(high, spread, preferred_element_type=F32) + jnp.dot(
+            low, spread, preferred_element_type=F32
         )
         picked = jnp.zeros((kf, chunk), F32)
         for g in range(groups):
@@ -416,11 +412,11 @@
         out[:, at] = picked
 
 
-def prefix_sums(sums, squares, rank, spread, kf):
+def prefix_sums(sums, squares, rank, kf):
     rows = rank.shape[1]
     return pl.pallas_call(
         prefix_kernel,
-        in_specs=[VMEM] * 4,
+        in_specs=[VMEM] * 3,
         out_shape=jax.ShapeDtypeStruct((kf, rows), F32),
         out_specs=VMEM,
         compiler_params=pltpu.CompilerParams(**PARAMS),
@@ -428,42 +424,67 @@
             flops=4 * rows * LO * (rows // LO) * kf, bytes_accessed=rows * kf * 24, transcendentals=0
         ),
         name="prefix_sums",
-    )(sums, squares, rank, spread)
-
-
-def weight_kernel(kf, ex, *refs):
-    messages, (tangent, local, risk, cumulative, squares) = refs[:ex], refs[ex : ex + 5]
-    weighted, placed = refs[ex + 5 :]
-    me = lax.axis_index("ex")
-    for i in range(ex):
-        placed[me ^ i] = messages[i][...]
-    later = jnp.zeros((kf, 1), F32)
-    own_later = later
-    before = later
-    hazard_before = jnp.zeros((1, 1), F32)
-    for b in reversed(range(ex)):
-        plain = jnp.sum(placed[b, :kf], axis=1, keepdims=True)
-        scaled = jnp.sum(placed[b, kf : 2 * kf], axis=1, keepdims=True)
-        hazard_total = placed[b, 2 * kf : 2 * kf + 1, :1]
-        square_total = placed[b, 2 * kf + 1 : 2 * kf + 2, :1]
-        own_later = own_later + jnp.where(b > me, plain, 0.0)
-        before = before + jnp.where(b < me, scaled + square_total * later, 0.0)
-        hazard_before = hazard_before + jnp.where(b < me, hazard_total, 0.0)
-        later = later + plain
-    value = tangent[...] * (cumulative[...] + hazard_before) - (local[...] + squares[...] * own_later + before)
+    )(sums, squares, rank)
+
+
+def merged(kf, bit, mine, other, state):
+    later_other = (lax.axis_index("ex") & bit) == 0
+    plain, scaled, rest = mine[:kf], mine[kf : 2 * kf], mine[2 * kf :]
+    other_plain, other_scaled, other_rest = other[:kf], other[kf : 2 * kf], other[2 * kf :]
+    square, other_square = rest[1:2], other_rest[1:2]
+    crossed = jnp.where(later_other, square * other_plain, other_square * plain)
+    total = jnp.concatenate([plain + other_plain, scaled + other_scaled + crossed, rest + other_rest], axis=0)
+    if state is None:
+        state = jnp.zeros_like(mine)
+    later, before, before_rest = state[:kf], state[kf : 2 * kf], state[2 * kf :]
+    state = jnp.concatenate(
+        [
+            later + jnp.where(later_other, other_plain, 0.0),
+            before + jnp.where(later_other, before_rest[1:2] * other_plain, other_scaled + other_square * plain),
+            before_rest + jnp.where(later_other, 0.0, other_rest),
+        ],
+        axis=0,
+    )
+    return total, state
+
+
+def combine_kernel(kf, bit, count, *refs):
+    inputs, (total, state) = [ref[...] for ref in refs[:count]], refs[count:]
+    total[...], state[...] = merged(kf, bit, inputs[0], inputs[1], inputs[2] if count > 2 else None)
+
+
+def combine(kf, bit, inputs):
+    shape = jax.ShapeDtypeStruct(inputs[0].shape, F32)
+    return pl.pallas_call(
+        functools.partial(combine_kernel, kf, bit, len(inputs)),
+        in_specs=[VMEM] * len(inputs),
+        out_shape=[shape, shape],
+        out_specs=[VMEM] * 2,
+        compiler_params=pltpu.CompilerParams(**PARAMS),
+        name="combine",
+    )(*inputs)
+
+
+def weight_kernel(kf, bit, count, *refs):
+    inputs = [ref[...] for ref in refs[:count]]
+    tangent, local, risk, cumulative, squares, weighted = refs[count:]
+    _, state = merged(kf, bit, inputs[0], inputs[1], inputs[2] if count > 2 else None)
+    later = jnp.sum(state[:kf], axis=1, keepdims=True)
+    before = jnp.sum(state[kf : 2 * kf], axis=1, keepdims=True)
+    hazard_before = state[2 * kf : 2 * kf + 1, :1]
+    value = tangent[...] * (cumulative[...] + hazard_before) - (local[...] + squares[...] * later + before)
     weighted[...] = (risk[...] * value).astype(BF16)
 
 
-def weights(messages, tangent, local, risk, cumulative, squares):
-    return pl.pallas_call(
-        functools.partial(weight_kernel, tangent.shape[0], len(messages)),
-        in_specs=[VMEM] * (len(messages) + 5),
+def weights(bit, inputs, tangent, local, risk, cumulative, squares):
+    return pl.pallas_call(
+        functools.partial(weight_kernel, tangent.shape[0], bit, len(inputs)),
+        in_specs=[VMEM] * (len(inputs) + 5),
         out_shape=jax.ShapeDtypeStruct(tangent.shape, BF16),
         out_specs=VMEM,
-        scratch_shapes=[pltpu.VMEM((len(messages),) + messages[0].shape, F32)],
         compiler_params=pltpu.CompilerParams(**PARAMS),
         name="weights",
-    )(*messages, tangent, local, risk, cumulative, squares)
+    )(*inputs, tangent, local, risk, cumulative, squares)
 
 
 def encode(values, message):
@@ -533,17 +554,34 @@
     )(mine, other)
 
 
-def finish_kernel(mine, other, count, out):
+def finish_kernel(steps, mine, other, count, out, total, sems):
     height = mine.shape[0] - 16
-    out[...] = (decode(mine, height) + decode(other, height)) / count[1:2, 0:1]
+    step = height // steps
+    block = min(BLOCK, step)
+    scale = count[1:2, 0:1]
+    powers = [from_short(message[height:]) for message in (mine, other)]
+    copies = []
+    for i in range(steps):
+        for start in range(i * step, (i + 1) * step, block):
+            at, j = slice(start, start + block), start // block
+            terms = [from_short(m[at]) * jnp.exp2(p[j : j + 1]) for m, p in zip((mine, other), powers)]
+            total[at] = (terms[0] + terms[1]) / scale
+        at = pl.ds(i * step, step)
+        copies.append(pltpu.make_async_copy(total.at[at], out.at[at], sems.at[i]))
+        copies[i].start()
+    for copy in copies:
+        copy.wait()
 
 
 def finish(mine, other, count):
-    return pl.pallas_call(
-        finish_kernel,
+    height, k = mine.shape[0] - 16, mine.shape[1]
+    steps = max(1, min(4, height // BLOCK))
+    return pl.pallas_call(
+        functools.partial(finish_kernel, steps),
         in_specs=[VMEM] * 3,
-        out_shape=jax.ShapeDtypeStruct((mine.shape[0] - 16, mine.shape[1]), F32),
-        out_specs=VMEM,
+        out_shape=jax.ShapeDtypeStruct((height, k), F32),
+        out_specs=HBM,
+        scratch_shapes=[pltpu.VMEM((height, k), F32), pltpu.SemaphoreType.DMA((steps,))],
         compiler_params=pltpu.CompilerParams(**PARAMS),
         name="finish",
     )(mine, other, count)
@@ -564,7 +602,7 @@
     received = [swap(piece, "feat", 1) for piece in send]
     paired, joined = join(linear, keep[1:], received[1:])
     others = [swap(joined[q - 1], "feat", 2 * q) for q in range(1, feat // 2)]
-    spread, table, masks = tables(rank, paired, rows, padded)
+    table = tables(rank, paired, rows)
 
     risk, sums, ordered_events, total = risks(paired, others, rank, event_row, table, rows)
     later = jnp.zeros_like(total)
@@ -574,14 +612,18 @@
         later = later + jnp.where((lax.axis_index("ex") & bit) == 0, other, 0.0)
         total = total + other
         bit *= 2
-    tangent, later_sums = suffix_sums(keep[0], received[0], others, risk, masks, table)
+    tangent, later_sums = suffix_sums(keep[0], received[0], others, risk, rank, table)
     cumulative, squares, ordered_squares, hazard_message = hazards(
-        later, sums, ordered_events, rank, spread, rows
+        later, sums, ordered_events, rank, rows
     )
     message = block_totals(tangent, risk, squares, hazard_message)
-    messages = [message] + [swap(message, "ex", i) for i in range(1, ex)]
-    summed = prefix_sums(later_sums, ordered_squares, rank, spread, padded)
-    own = weights(messages, tangent, summed, risk, cumulative, squares)
+    state, bit = [], 1
+    while 2 * bit < ex:
+        message, *state = combine(padded, bit, [message, swap(message, "ex", bit)] + state)
+        bit *= 2
+    inputs = [message, swap(message, "ex", bit)] + state
+    summed = prefix_sums(later_sums, ordered_squares, rank, padded)
+    own = weights(bit, inputs, tangent, summed, risk, cumulative, squares)
 
     chips = {0: own}
     for q in reversed(range(1, feat // 2)):

time: 67.7 us -> 65 us (0.960)
  local copies, waits for them, and re-layouts: 5.86 us -> 0.01 us
  starting transfers between devices: 18.9 us -> 21.3 us
  waiting for transfers between devices: 27.5 us -> 29 us
    unnamed x18 -> x6, local copies, waits for them, and re-layouts: 5.86 us -> 0.01 us
    ppermute x21 -> x20, starting transfers between devices: 18.9 us -> 21.3 us  [swap(): return lax.ppermute(x, axis, [(s, s ^ i) for s in range(count)])]
    ppermute x21 -> x20, waiting for transfers between devices: 27.5 us -> 29 us  [swap(): return lax.ppermute(x, axis, [(s, s ^ i) for s in range(count)])]
    pallas_call x1, Pallas kernels: 1.62 us -> 0.64 us  [tables(): pl.pallas_call(functools.partial(table_kernel, rows), in_specs=[VMEM, pl....]
    pallas_call x3 -> x4, Pallas kernels: 2.53 us -> 2.91 us  [the longest x1 1.92 us: prefix_sums(): pl.pallas_call(prefix_kernel, in_specs=[VMEM] * 3, out_shape=jax.ShapeDty...]
  transfers between devices with their start and end apart: 21 -> 20, of which waited for: 12 -> 13; matrix products, arithmetic and copies ran while one was open for 0% -> 0% of each run, Pallas kernels for 10% -> 9%
where the time goes in v6:
time: 65 us; the launch traced here: 64.9 us
  waiting for transfers between devices  29 us (45%)
  starting transfers between devices  21.3 us (33%)
  Pallas kernels  14.5 us (22%)
    ppermute x20, waiting for transfers between devices, swap(): return lax.ppermute(x, axis, [(s, s ^ i) for s in range(count)])  29 us
    ppermute x20, starting transfers between devices, swap(): return lax.ppermute(x, axis, [(s, s ^ i) for s in range(count)])  21.3 us
    pallas_call x1, Pallas kernels, products(): pl.pallas_call(functools.partial(product_kernel, feat, kf, chunk), in_spe...  4.69 us
    pallas_call x1, Pallas kernels, suffix_sums(): pl.pallas_call(functools.partial(suffix_kernel, len(messages)), in_specs=...  2.21 us
    pallas_call x1, Pallas kernels, prefix_sums(): pl.pallas_call(prefix_kernel, in_specs=[VMEM] * 3, out_shape=jax.ShapeDty...  1.92 us
    pallas_call x1, Pallas kernels, hazards(): pl.pallas_call(functools.partial(hazard_kernel, rows), in_specs=[VMEM] *...  1.65 us
  transfers between devices with their start and end apart: 20, of which 13 were waited for; matrix products, arithmetic and copies ran while one was open for 0% of the time, Pallas kernels for 9%

profile of v6, /device:TPU:0, one launch (start us, length us, event | category | flops | bytes accessed | tf_op | source)
XLA Modules:
  0.0 64.9 jit_solution(4095929925934474286)
XLA Ops:
  0.0 4.7 %products.1 = (f32[16,256]{1,0:T(8,128)S(1)}, f32[16,4096]{1,0:T(8,128)S(1)}, f32[16,4096]{1,0:T(8,128)S(1)}, f32[16,4096]{1,0:T(8,128)S(1)}, f32[16,4096]{1,0:T...) custom-call(bf16[512,128]{1,0:T(8,128)(2,1)} %directions.1, ...), custom_call_target="tpu_custom_call" | custom-call | flops 536870912 | bytes 6291456 | tf_op jit(solution)/shard_map/products/pallas_call | solution.py:118
  7.4 2.9 %collective-permute-start.4 = (s16[16,4736]{1,0:T(8,128)(2,1)S(1)}, s16[16,4736]{1,0:T(8,128)(2,1)S(1)}, u32[]{:S(2)}, u32[]{:S(2)}) collective-permute-start(s16[16,4736]{1,0:T(8,128)(2,1)S(1)} %get-tuple-element.39), channel_id=1, source_target_pairs={{0,2},{1,3},{2,0},{3,1},{4,6},{5,7},{6,4},{7,5},{8,10},{9,11},{10,... | collective-permute-start | bytes 454664 | tf_op jit(solution)/shard_map/ppermute | solution.py:23
  10.3 1.5 %collective-permute-start.5 = (s16[16,4736]{1,0:T(8,128)(2,1)S(1)}, s16[16,4736]{1,0:T(8,128)(2,1)S(1)}, u32[]{:S(2)}, u32[]{:S(2)}) collective-permute-start(s16[16,4736]{1,0:T(8,128)(2,1)S(1)} %get-tuple-element.40), channel_id=1, source_target_pairs={{0,4},{1,5},{2,6},{3,7},{4,0},{5,1},{6,2},{7,3},{8,12},{9,13},{10,... | collective-permute-start | bytes 454664 | tf_op jit(solution)/shard_map/ppermute | solution.py:23
  12.5 2.5 %collective-permute-done.4.refs_0_ = s16[16,4736]{1,0:T(8,128)(2,1)S(1)} collective-permute-done((s16[16,4736]{1,0:T(8,128)(2,1)S(1)}, s16[16,4736]{1,0:T(8,128)(2,1)S(1)}, u32[]{:S(2)}, u32[]{:S(2)}) %collective-permute-start.4) | collective-permute-done | bytes 151584 | tf_op jit(solution)/shard_map/ppermute | solution.py:23
  15.0 4.2 %collective-permute-done.5.refs_1_ = s16[16,4736]{1,0:T(8,128)(2,1)S(1)} collective-permute-done((s16[16,4736]{1,0:T(8,128)(2,1)S(1)}, s16[16,4736]{1,0:T(8,128)(2,1)S(1)}, u32[]{:S(2)}, u32[]{:S(2)}) %collective-permute-start.5) | collective-permute-done | bytes 151584 | tf_op jit(solution)/shard_map/ppermute | solution.py:23
  20.3 1.6 %collective-permute-start.7 = (f32[8,128]{1,0:T(8,128)S(1)}, f32[8,128]{1,0:T(8,128)S(1)}, u32[]{:S(2)}, u32[]{:S(2)}) collective-permute-start(f32[8,128]{1,0:T(8,128)S(1)} %get-tuple-element.45), channel_id=1, source_target_pairs={{0,8},{8,0},{16,24},{24,16},{1,9},{9,1},{17,25},{25,17},{2,10},{10... | collective-permute-start | bytes 12296 | tf_op jit(solution)/shard_map/ppermute | solution.py:23
  21.9 2.0 %collective-permute-done.7 = f32[8,128]{1,0:T(8,128)S(1)} collective-permute-done((f32[8,128]{1,0:T(8,128)S(1)}, f32[8,128]{1,0:T(8,128)S(1)}, u32[]{:S(2)}, u32[]{:S(2)}) %collective-permute-start.7) | collective-permute-done | bytes 4128 | tf_op jit(solution)/shard_map/ppermute | solution.py:23
  23.9 2.6 %collective-permute-start.8 = (f32[8,128]{1,0:T(8,128)S(1)}, f32[8,128]{1,0:T(8,128)S(1)}, u32[]{:S(2)}, u32[]{:S(2)}) collective-permute-start(f32[8,128]{1,0:T(8,128)S(1)} %add.9), channel_id=1, source_target_pairs={{0,16},{8,24},{16,0},{24,8},{1,17},{9,25},{17,1},{25,9},{2,18},{10... | collective-permute-start | bytes 12296 | tf_op jit(solution)/shard_map/ppermute | solution.py:23
  26.5 2.2 %suffix_sums.1 = (f32[16,4096]{1,0:T(8,128)S(1)}, f32[256,256]{1,0:T(8,128)S(1)}) custom-call(f32[16,4096]{1,0:T(8,128)S(1)} %get-tuple-element.30.own, f32[16,4096]{1,0:T(8,128)S(1)} %collective-permute-done.other, s16[16,4736]{1,0:T(8,128)(2,1)S(1)} %collective-permute-done.4.refs_0_, s16[16,4736]{1,0:T(8,128)(2,1)S(1)} %collective-permute-done.5.refs_1_, ...), custom_call_target="tpu_custom_call" | custom-call | flops 1073741824 | bytes 1572864 | tf_op jit(solution)/shard_map/suffix_sums/pallas_call | solution.py:370
  28.8 1.6 %hazards.1 = (f32[1,4096]{1,0:T(1,128)S(1)}, f32[1,4096]{1,0:T(1,128)S(1)}, f32[16,256]{1,0:T(8,128)S(1)}, f32[8,128]{1,0:T(8,128)S(1)}) custom-call(f32[8,128]{1,0:T(8,128)S(1)} %get-tuple-element.56.later, f32[16,256]{1,0:T(8,128)S(1)} %get-tuple-element.46.sums, f32[16,256]{1,0:T(8,128)S(1)} %get-tuple-element.47.events, s32[1,4096]{1,0:T(1,128)S(1)} %bitcast.5), custom_call_target="tpu_custom_call" | custom-call | flops 209715200 | bytes 262144 | tf_op jit(solution)/shard_map/hazards/pallas_call | solution.py:296
  30.5 1.6 %collective-permute-start.9 = (f32[40,128]{1,0:T(8,128)S(1)}, f32[40,128]{1,0:T(8,128)S(1)}, u32[]{:S(2)}, u32[]{:S(2)}) collective-permute-start(f32[40,128]{1,0:T(8,128)S(1)} %block_totals.1.refs_0_), channel_id=1, source_target_pairs={{0,8},{8,0},{16,24},{24,16},{1,9},{9,1},{17,25},{25,17},{2,10},{10... | collective-permute-start | bytes 61448 | tf_op jit(solution)/shard_map/ppermute | solution.py:23
  32.1 2.2 %collective-permute-done.9.refs_1_ = f32[40,128]{1,0:T(8,128)S(1)} collective-permute-done((f32[40,128]{1,0:T(8,128)S(1)}, f32[40,128]{1,0:T(8,128)S(1)}, u32[]{:S(2)}, u32[]{:S(2)}) %collective-permute-start.9) | collective-permute-done | bytes 20512 | tf_op jit(solution)/shard_map/ppermute | solution.py:23
  34.3 2.3 %collective-permute-start.10 = (f32[40,128]{1,0:T(8,128)S(1)}, f32[40,128]{1,0:T(8,128)S(1)}, u32[]{:S(2)}, u32[]{:S(2)}) collective-permute-start(f32[40,128]{1,0:T(8,128)S(1)} %get-tuple-element.50.refs_0_), channel_id=1, source_target_pairs={{0,16},{8,24},{16,0},{24,8},{1,17},{9,25},{17,1},{25,9},{2,18},{10... | collective-permute-start | bytes 61448 | tf_op jit(solution)/shard_map/ppermute | solution.py:23
  36.7 1.9 %prefix_sums.1.refs_4_ = f32[16,4096]{1,0:T(8,128)S(1)} custom-call(f32[256,256]{1,0:T(8,128)S(1)} %get-tuple-element.52.sums, f32[16,256]{1,0:T(8,128)S(1)} %get-tuple-element.53.squares, s32[1,4096]{1,0:T(1,128)S(1)} %bitcast.6), custom_call_target="tpu_custom_call" | custom-call | flops 1073741824 | bytes 1572864 | tf_op jit(solution)/shard_map/prefix_sums/pallas_call | solution.py:417
  39.3 1.3 %collective-permute-start.12 = (bf16[16,4096]{1,0:T(8,128)(2,1)S(1)}, bf16[16,4096]{1,0:T(8,128)(2,1)S(1)}, u32[]{:S(2)}, u32[]{:S(2)}) collective-permute-start(bf16[16,4096]{1,0:T(8,128)(2,1)S(1)} %weights.1.refs_0_), channel_id=1, source_target_pairs={{0,2},{1,3},{2,0},{3,1},{4,6},{5,7},{6,4},{7,5},{8,10},{9,11},{10,... | collective-permute-start | bytes 393224 | tf_op jit(solution)/shard_map/ppermute | solution.py:23
  41.4 1.4 %collective-permute-start.16 = (bf16[16,4096]{1,0:T(8,128)(2,1)S(1)}, bf16[16,4096]{1,0:T(8,128)(2,1)S(1)}, u32[]{:S(2)}, u32[]{:S(2)}) collective-permute-start(bf16[16,4096]{1,0:T(8,128)(2,1)S(1)} %weights.1.refs_0_), channel_id=1, source_target_pairs={{0,6},{1,7},{2,4},{3,5},{4,2},{5,3},{6,0},{7,1},{8,14},{9,15},{10,... | collective-permute-start | bytes 393224 | tf_op jit(solution)/shard_map/ppermute | solution.py:23
  42.9 1.5 %collective-permute-done.12.refs_2_ = bf16[16,4096]{1,0:T(8,128)(2,1)S(1)} collective-permute-done((bf16[16,4096]{1,0:T(8,128)(2,1)S(1)}, bf16[16,4096]{1,0:T(8,128)(2,1)S(1)}, u32[]{:S(2)}, u32[]{:S(2)}) %collective-permute-start.12) | collective-permute-done | bytes 131104 | tf_op jit(solution)/shard_map/ppermute | solution.py:23
  44.3 1.2 %collective-permute-done.14.refs_4_ = bf16[16,4096]{1,0:T(8,128)(2,1)S(1)} collective-permute-done((bf16[16,4096]{1,0:T(8,128)(2,1)S(1)}, bf16[16,4096]{1,0:T(8,128)(2,1)S(1)}, u32[]{:S(2)}, u32[]{:S(2)}) %collective-permute-start.14) | collective-permute-done | bytes 131104 | tf_op jit(solution)/shard_map/ppermute | solution.py:23
  45.6 1.7 %collective-permute-done.16.refs_6_ = bf16[16,4096]{1,0:T(8,128)(2,1)S(1)} collective-permute-done((bf16[16,4096]{1,0:T(8,128)(2,1)S(1)}, bf16[16,4096]{1,0:T(8,128)(2,1)S(1)}, u32[]{:S(2)}, u32[]{:S(2)}) %collective-permute-start.16) | collective-permute-done | bytes 131104 | tf_op jit(solution)/shard_map/ppermute | solution.py:23
  47.3 1.3 %collective-permute-done.17.refs_7_ = bf16[16,4096]{1,0:T(8,128)(2,1)S(1)} collective-permute-done((bf16[16,4096]{1,0:T(8,128)(2,1)S(1)}, bf16[16,4096]{1,0:T(8,128)(2,1)S(1)}, u32[]{:S(2)}, u32[]{:S(2)}) %collective-permute-start.17) | collective-permute-done | bytes 131104 | tf_op jit(solution)/shard_map/ppermute | solution.py:23
  49.6 1.6 %collective-permute-start.18 = (s16[528,128]{1,0:T(8,128)(2,1)S(1)}, s16[528,128]{1,0:T(8,128)(2,1)S(1)}, u32[]{:S(2)}, u32[]{:S(2)}) collective-permute-start(s16[528,128]{1,0:T(8,128)(2,1)S(1)} %gradients.1.mine), channel_id=1, source_target_pairs={{0,8},{8,0},{16,24},{24,16},{1,9},{9,1},{17,25},{25,17},{2,10},{10... | collective-permute-start | bytes 405512 | tf_op jit(solution)/shard_map/ppermute | solution.py:23
  51.3 4.1 %collective-permute-done.18.other = s16[528,128]{1,0:T(8,128)(2,1)S(1)} collective-permute-done((s16[528,128]{1,0:T(8,128)(2,1)S(1)}, s16[528,128]{1,0:T(8,128)(2,1)S(1)}, u32[]{:S(2)}, u32[]{:S(2)}) %collective-permute-start.18) | collective-permute-done | bytes 135200 | tf_op jit(solution)/shard_map/ppermute | solution.py:23
  55.5 2.3 %collective-permute-start.19 = (s16[528,128]{1,0:T(8,128)(2,1)S(1)}, s16[528,128]{1,0:T(8,128)(2,1)S(1)}, u32[]{:S(2)}, u32[]{:S(2)}) collective-permute-start(s16[528,128]{1,0:T(8,128)(2,1)S(1)} %merge.1.mine), channel_id=1, source_target_pairs={{0,16},{8,24},{16,0},{24,8},{1,17},{9,25},{17,1},{25,9},{2,18},{10... | collective-permute-start | bytes 405512 | tf_op jit(solution)/shard_map/ppermute | solution.py:23
  57.8 6.3 %collective-permute-done.19.other = s16[528,128]{1,0:T(8,128)(2,1)S(1)} collective-permute-done((s16[528,128]{1,0:T(8,128)(2,1)S(1)}, s16[528,128]{1,0:T(8,128)(2,1)S(1)}, u32[]{:S(2)}, u32[]{:S(2)}) %collective-permute-start.19) | collective-permute-done | bytes 135200 | tf_op jit(solution)/shard_map/ppermute | solution.py:23
  (37 shorter events, 7.8 us)
Async XLA Ops:
  0.0 11.9 %copy-start.1 = (s32[4096]{0:T(1024)S(1)}, s32[4096]{0:T(1024)}, u32[]{:S(2)}) copy-start(s32[4096]{0:T(1024)} %param.8) | copy-start | bytes 49156
  0.0 19.3 %copy-start.2 = (s32[4096]{0:T(1024)S(1)}, s32[4096]{0:T(1024)}, u32[]{:S(2)}) copy-start(s32[4096]{0:T(1024)} %param.9) | copy-start | bytes 49156
  4.7 2.5 %collective-permute-start.1 = (f32[16,4352]{1,0:T(8,128)S(1)}, f32[16,4352]{1,0:T(8,128)S(1)}, u32[]{:S(2)}, u32[]{:S(2)}) collective-permute-start(f32[16,4352]{1,0:T(8,128)S(1)} %get-tuple-element.36), channel_id=1, source_target_pairs={{0,1},{1,0},{2,3},{3,2},{4,5},{5,4},{6,7},{7,6},{8,9},{9,8},{10,11... | collective-permute-start | bytes 835592 | tf_op jit(solution)/shard_map/ppermute | solution.py:23
  5.2 1.6 %collective-permute-start.2 = (f32[16,4096]{1,0:T(8,128)S(1)}, f32[16,4096]{1,0:T(8,128)S(1)}, u32[]{:S(2)}, u32[]{:S(2)}) collective-permute-start(f32[16,4096]{1,0:T(8,128)S(1)} %get-tuple-element.37), channel_id=1, source_target_pairs={{0,1},{1,0},{2,3},{3,2},{4,5},{5,4},{6,7},{7,6},{8,9},{9,8},{10,11... | collective-permute-start | bytes 786440 | tf_op jit(solution)/shard_map/ppermute | solution.py:23
  5.3 1.9 %collective-permute-start.3 = (f32[16,4096]{1,0:T(8,128)S(1)}, f32[16,4096]{1,0:T(8,128)S(1)}, u32[]{:S(2)}, u32[]{:S(2)}) collective-permute-start(f32[16,4096]{1,0:T(8,128)S(1)} %get-tuple-element.38), channel_id=1, source_target_pairs={{0,1},{1,0},{2,3},{3,2},{4,5},{5,4},{6,7},{7,6},{8,9},{9,8},{10,11... | collective-permute-start | bytes 786440 | tf_op jit(solution)/shard_map/ppermute | solution.py:23
  5.7 20.8 %collective-permute-start = (f32[16,4096]{1,0:T(8,128)S(1)}, f32[16,4096]{1,0:T(8,128)S(1)}, u32[]{:S(2)}, u32[]{:S(2)}) collective-permute-start(f32[16,4096]{1,0:T(8,128)S(1)} %get-tuple-element.31), channel_id=1, source_target_pairs={{0,1},{1,0},{2,3},{3,2},{4,5},{5,4},{6,7},{7,6},{8,9},{9,8},{10,11... | collective-permute-start | bytes 786440 | tf_op jit(solution)/shard_map/ppermute | solution.py:23
  7.4 7.6 %collective-permute-start.4 = (s16[16,4736]{1,0:T(8,128)(2,1)S(1)}, s16[16,4736]{1,0:T(8,128)(2,1)S(1)}, u32[]{:S(2)}, u32[]{:S(2)}) collective-permute-start(s16[16,4736]{1,0:T(8,128)(2,1)S(1)} %get-tuple-element.39), channel_id=1, source_target_pairs={{0,2},{1,3},{2,0},{3,1},{4,6},{5,7},{6,4},{7,5},{8,10},{9,11},{10,... | collective-permute-start | bytes 454664 | tf_op jit(solution)/shard_map/ppermute | solution.py:23
  10.3 8.9 %collective-permute-start.5 = (s16[16,4736]{1,0:T(8,128)(2,1)S(1)}, s16[16,4736]{1,0:T(8,128)(2,1)S(1)}, u32[]{:S(2)}, u32[]{:S(2)}) collective-permute-start(s16[16,4736]{1,0:T(8,128)(2,1)S(1)} %get-tuple-element.40), channel_id=1, source_target_pairs={{0,4},{1,5},{2,6},{3,7},{4,0},{5,1},{6,2},{7,3},{8,12},{9,13},{10,... | collective-permute-start | bytes 454664 | tf_op jit(solution)/shard_map/ppermute | solution.py:23
  11.8 7.4 %collective-permute-start.6 = (s16[16,4736]{1,0:T(8,128)(2,1)S(1)}, s16[16,4736]{1,0:T(8,128)(2,1)S(1)}, u32[]{:S(2)}, u32[]{:S(2)}) collective-permute-start(s16[16,4736]{1,0:T(8,128)(2,1)S(1)} %get-tuple-element.41), channel_id=1, source_target_pairs={{0,6},{1,7},{2,4},{3,5},{4,2},{5,3},{6,0},{7,1},{8,14},{9,15},{10,... | collective-permute-start | bytes 454664 | tf_op jit(solution)/shard_map/ppermute | solution.py:23
  20.3 3.7 %collective-permute-start.7 = (f32[8,128]{1,0:T(8,128)S(1)}, f32[8,128]{1,0:T(8,128)S(1)}, u32[]{:S(2)}, u32[]{:S(2)}) collective-permute-start(f32[8,128]{1,0:T(8,128)S(1)} %get-tuple-element.45), channel_id=1, source_target_pairs={{0,8},{8,0},{16,24},{24,16},{1,9},{9,1},{17,25},{25,17},{2,10},{10... | collective-permute-start | bytes 12296 | tf_op jit(solution)/shard_map/ppermute | solution.py:23
  23.9 4.8 %collective-permute-start.8 = (f32[8,128]{1,0:T(8,128)S(1)}, f32[8,128]{1,0:T(8,128)S(1)}, u32[]{:S(2)}, u32[]{:S(2)}) collective-permute-start(f32[8,128]{1,0:T(8,128)S(1)} %add.9), channel_id=1, source_target_pairs={{0,16},{8,24},{16,0},{24,8},{1,17},{9,25},{17,1},{25,9},{2,18},{10... | collective-permute-start | bytes 12296 | tf_op jit(solution)/shard_map/ppermute | solution.py:23
  26.5 22.1 %copy-start = (bf16[4096,512]{1,0:T(8,128)(2,1)S(1)}, bf16[4096,512]{1,0:T(8,128)(2,1)}, u32[]{:S(2)}) copy-start(bf16[4096,512]{1,0:T(8,128)(2,1)} %refs_8_.1) | copy-start | bytes 12582916
  30.5 3.8 %collective-permute-start.9 = (f32[40,128]{1,0:T(8,128)S(1)}, f32[40,128]{1,0:T(8,128)S(1)}, u32[]{:S(2)}, u32[]{:S(2)}) collective-permute-start(f32[40,128]{1,0:T(8,128)S(1)} %block_totals.1.refs_0_), channel_id=1, source_target_pairs={{0,8},{8,0},{16,24},{24,16},{1,9},{9,1},{17,25},{25,17},{2,10},{10... | collective-permute-start | bytes 61448 | tf_op jit(solution)/shard_map/ppermute | solution.py:23
  34.3 4.7 %collective-permute-start.10 = (f32[40,128]{1,0:T(8,128)S(1)}, f32[40,128]{1,0:T(8,128)S(1)}, u32[]{:S(2)}, u32[]{:S(2)}) collective-permute-start(f32[40,128]{1,0:T(8,128)S(1)} %get-tuple-element.50.refs_0_), channel_id=1, source_target_pairs={{0,16},{8,24},{16,0},{24,8},{1,17},{9,25},{17,1},{25,9},{2,18},{10... | collective-permute-start | bytes 61448 | tf_op jit(solution)/shard_map/ppermute | solution.py:23
  39.3 5.0 %collective-permute-start.12 = (bf16[16,4096]{1,0:T(8,128)(2,1)S(1)}, bf16[16,4096]{1,0:T(8,128)(2,1)S(1)}, u32[]{:S(2)}, u32[]{:S(2)}) collective-permute-start(bf16[16,4096]{1,0:T(8,128)(2,1)S(1)} %weights.1.refs_0_), channel_id=1, source_target_pairs={{0,2},{1,3},{2,0},{3,1},{4,6},{5,7},{6,4},{7,5},{8,10},{9,11},{10,... | collective-permute-start | bytes 393224 | tf_op jit(solution)/shard_map/ppermute | solution.py:23
  40.6 5.0 %collective-permute-start.14 = (bf16[16,4096]{1,0:T(8,128)(2,1)S(1)}, bf16[16,4096]{1,0:T(8,128)(2,1)S(1)}, u32[]{:S(2)}, u32[]{:S(2)}) collective-permute-start(bf16[16,4096]{1,0:T(8,128)(2,1)S(1)} %weights.1.refs_0_), channel_id=1, source_target_pairs={{0,4},{1,5},{2,6},{3,7},{4,0},{5,1},{6,2},{7,3},{8,12},{9,13},{10,... | collective-permute-start | bytes 393224 | tf_op jit(solution)/shard_map/ppermute | solution.py:23
  41.4 5.9 %collective-permute-start.16 = (bf16[16,4096]{1,0:T(8,128)(2,1)S(1)}, bf16[16,4096]{1,0:T(8,128)(2,1)S(1)}, u32[]{:S(2)}, u32[]{:S(2)}) collective-permute-start(bf16[16,4096]{1,0:T(8,128)(2,1)S(1)} %weights.1.refs_0_), channel_id=1, source_target_pairs={{0,6},{1,7},{2,4},{3,5},{4,2},{5,3},{6,0},{7,1},{8,14},{9,15},{10,... | collective-permute-start | bytes 393224 | tf_op jit(solution)/shard_map/ppermute | solution.py:23
  42.9 4.4 %collective-permute-start.11 = (bf16[16,4096]{1,0:T(8,128)(2,1)S(1)}, bf16[16,4096]{1,0:T(8,128)(2,1)S(1)}, u32[]{:S(2)}, u32[]{:S(2)}) collective-permute-start(bf16[16,4096]{1,0:T(8,128)(2,1)S(1)} %weights.1.refs_0_), channel_id=1, source_target_pairs={{0,1},{1,0},{2,3},{3,2},{4,5},{5,4},{6,7},{7,6},{8,9},{9,8},{10,11... | collective-permute-start | bytes 393224 | tf_op jit(solution)/shard_map/ppermute | solution.py:23
  44.3 3.0 %collective-permute-start.13 = (bf16[16,4096]{1,0:T(8,128)(2,1)S(1)}, bf16[16,4096]{1,0:T(8,128)(2,1)S(1)}, u32[]{:S(2)}, u32[]{:S(2)}) collective-permute-start(bf16[16,4096]{1,0:T(8,128)(2,1)S(1)} %collective-permute-done.12.refs_2_), channel_id=1, source_target_pairs={{0,1},{1,0},{2,3},{3,2},{4,5},{5,4},{6,7},{7,6},{8,9},{9,8},{10,11... | collective-permute-start | bytes 393224 | tf_op jit(solution)/shard_map/ppermute | solution.py:23
  45.6 1.7 %collective-permute-start.15 = (bf16[16,4096]{1,0:T(8,128)(2,1)S(1)}, bf16[16,4096]{1,0:T(8,128)(2,1)S(1)}, u32[]{:S(2)}, u32[]{:S(2)}) collective-permute-start(bf16[16,4096]{1,0:T(8,128)(2,1)S(1)} %collective-permute-done.14.refs_4_), channel_id=1, source_target_pairs={{0,1},{1,0},{2,3},{3,2},{4,5},{5,4},{6,7},{7,6},{8,9},{9,8},{10,11... | collective-permute-start | bytes 393224 | tf_op jit(solution)/shard_map/ppermute | solution.py:23
  47.3 1.3 %collective-permute-start.17 = (bf16[16,4096]{1,0:T(8,128)(2,1)S(1)}, bf16[16,4096]{1,0:T(8,128)(2,1)S(1)}, u32[]{:S(2)}, u32[]{:S(2)}) collective-permute-start(bf16[16,4096]{1,0:T(8,128)(2,1)S(1)} %collective-permute-done.16.refs_6_), channel_id=1, source_target_pairs={{0,1},{1,0},{2,3},{3,2},{4,5},{5,4},{6,7},{7,6},{8,9},{9,8},{10,11... | collective-permute-start | bytes 393224 | tf_op jit(solution)/shard_map/ppermute | solution.py:23
  49.6 5.7 %collective-permute-start.18 = (s16[528,128]{1,0:T(8,128)(2,1)S(1)}, s16[528,128]{1,0:T(8,128)(2,1)S(1)}, u32[]{:S(2)}, u32[]{:S(2)}) collective-permute-start(s16[528,128]{1,0:T(8,128)(2,1)S(1)} %gradients.1.mine), channel_id=1, source_target_pairs={{0,8},{8,0},{16,24},{24,16},{1,9},{9,1},{17,25},{25,17},{2,10},{10... | collective-permute-start | bytes 405512 | tf_op jit(solution)/shard_map/ppermute | solution.py:23
  55.5 8.7 %collective-permute-start.19 = (s16[528,128]{1,0:T(8,128)(2,1)S(1)}, s16[528,128]{1,0:T(8,128)(2,1)S(1)}, u32[]{:S(2)}, u32[]{:S(2)}) collective-permute-start(s16[528,128]{1,0:T(8,128)(2,1)S(1)} %merge.1.mine), channel_id=1, source_target_pairs={{0,16},{8,24},{16,0},{24,8},{1,17},{9,25},{17,1},{25,9},{2,18},{10... | collective-permute-start | bytes 405512 | tf_op jit(solution)/shard_map/ppermute | solution.py:23

commit v7 on v6

--- a/solution.py
+++ b/solution.py
@@ -10,11 +10,11 @@
 F32 = jnp.float32
 BF16 = jnp.bfloat16
 LO = 256
+NT = (((1,), (1,)), ((), ()))
 BLOCK = 64
 SPAN = 512
 VMEM = pl.BlockSpec(memory_space=pltpu.VMEM)
 HBM = pl.BlockSpec(memory_space=pltpu.HBM)
-PRODUCT_BYTES = 24 * 1024 * 1024
 PARAMS = dict(vmem_limit_bytes=24 * 1024 * 1024)
 
 
@@ -65,7 +65,7 @@
 
 def product_kernel(feat, kf, chunk, directions, coefficients, dosages, *refs):
     linear, keep, send = refs[0], refs[1 : 1 + feat // 2], refs[1 + feat // 2 : 1 + feat]
-    table, own_directions, own_coefficients, rhs, results, turned, sems = refs[1 + feat :]
+    table, own_directions, own_coefficients, lhs, turned, sems = refs[1 + feat :]
     me = lax.axis_index("feat")
     width = feat * kf
     persons, variants = table.shape
@@ -84,28 +84,23 @@
         copy.start()
     for copy in small:
         copy.wait()
-    rhs[:, :width] = own_directions[...]
-    spread = jnp.broadcast_to(own_coefficients[...].astype(F32)[None, :], (128, variants))
-    rhs[:, width:] = spread.T.astype(BF16)
-    diagonal = triangle(128, lambda a, b: a == b)
-    for i in range(steps + 1):
-        if i < steps:
-            large[i].wait()
-            results[i % 2] = jnp.dot(
-                table[i * chunk : (i + 1) * chunk], rhs[...], preferred_element_type=F32
-            )
-        if i > 0:
-            result = results.at[(i - 1) % 2]
-            first = (i - 1) * chunk
-            turned[i % 2] = result[:, :width].T.reshape(feat, kf, chunk)
-            for j in range(feat):
-                (send if j % 2 else keep)[j // 2][:, first : first + chunk] = turned[i % 2, me ^ j]
-            for start in range(0, chunk, 128):
-                block = result[start : start + 128, width:]
-                row = jnp.sum(block * diagonal, axis=0, keepdims=True)
-                group, lane = divmod(first + start, LO)
-                linear[group : group + 1, lane : lane + 128] = row
-                send[1][group : group + 1, persons + lane : persons + lane + 128] = row
+    turned[...] = own_directions[...].astype(F32).T.reshape(turned.shape)
+    for j in range(feat):
+        lhs[j * kf : (j + 1) * kf] = turned[me ^ j].astype(BF16)
+    lhs[width:] = jnp.broadcast_to(own_coefficients[...].astype(F32)[None, :], (16, variants)).astype(BF16)
+    for i in range(steps):
+        large[i].wait()
+        first = i * chunk
+        result = lax.dot_general(
+            lhs[...], table[first : first + chunk], NT, preferred_element_type=F32
+        )
+        for j in range(feat):
+            (send if j % 2 else keep)[j // 2][:, first : first + chunk] = result[j * kf : (j + 1) * kf]
+        for start in range(0, chunk, LO):
+            row = result[width : width + 1, start : start + LO]
+            group = (first + start) // LO
+            linear[group : group + 1, :] = row
+            send[1][group : group + 1, persons:] = row
 
 
 def products(dosages, coefficients, directions, feat):
@@ -127,12 +122,11 @@
             pltpu.VMEM((persons, variants), BF16),
             pltpu.VMEM((variants, k), BF16),
             pltpu.VMEM((variants,), BF16),
-            pltpu.VMEM((variants, k + 128), BF16),
-            pltpu.VMEM((2, chunk, k + 128), F32),
-            pltpu.VMEM((2, feat, kf, chunk), F32),
+            pltpu.VMEM((k + 16, variants), BF16),
+            pltpu.VMEM((feat, kf, variants), F32),
             pltpu.SemaphoreType.DMA((persons // chunk + 2,)),
         ],
-        compiler_params=pltpu.CompilerParams(vmem_limit_bytes=PRODUCT_BYTES),
+        compiler_params=pltpu.CompilerParams(**PARAMS),
         cost_estimate=pl.CostEstimate(
             flops=2 * persons * variants * k, bytes_accessed=persons * (variants * 2 + k * 4), transcendentals=0
         ),
@@ -263,14 +257,41 @@
     )(linear, *messages, rank, events, table)
 
 
-def hazard_kernel(rows, later, sums, events, rank, *outs):
-    cumulative, squares, ordered_squares, message = outs
-    groups = rows // LO
+def share_kernel(later, sums, events, plain, ordered, hazard_out, squares, message):
+    kf = plain.shape[0]
+    groups = sums.shape[0]
     risk_sum = sums[...] + later[0:1, 0:1]
     hazard = events[...] / risk_sum
     square = events[...] / (risk_sum * risk_sum)
-    ordered_squares[...] = square
-    inside = dot_binary(jnp.concatenate([hazard, square], axis=0), triangle(LO, lambda a, b: a <= b))
+    hazard_out[...] = hazard
+    squares[...] = square
+    scaled = jnp.zeros((kf, LO), F32)
+    for g in range(groups):
+        scaled = scaled + ordered[g * kf : (g + 1) * kf] * square[g : g + 1]
+    message[:kf] = plain[...]
+    message[kf : 2 * kf] = sum(scaled[:, start : start + 128] for start in range(0, LO, 128))
+    totals = [jnp.sum(jnp.sum(v, axis=0, keepdims=True), axis=1, keepdims=True) for v in (hazard, square)]
+    rows = [jnp.broadcast_to(v, (1, 128)) for v in totals]
+    message[2 * kf :] = jnp.concatenate(rows + [jnp.zeros((6, 128), F32)], axis=0)
+
+
+def shares(later, sums, events, plain, ordered):
+    flat = jax.ShapeDtypeStruct(sums.shape, F32)
+    return pl.pallas_call(
+        share_kernel,
+        in_specs=[VMEM] * 5,
+        out_shape=[flat, flat, jax.ShapeDtypeStruct((2 * plain.shape[0] + 8, 128), F32)],
+        out_specs=[VMEM] * 3,
+        compiler_params=pltpu.CompilerParams(**PARAMS),
+        name="shares",
+    )(later, sums, events, plain, ordered)
+
+
+def hazard_kernel(rows, hazard, square, rank, cumulative, squares):
+    groups = rows // LO
+    inside = dot_binary(
+        jnp.concatenate([hazard[...], square[...]], axis=0), triangle(LO, lambda a, b: a <= b)
+    )
     totals = jnp.broadcast_to(inside[:, LO - 1 :], (2 * groups, 128))
     place = lax.rem(rank[...], rows)
     mask = one_hot(place // LO, groups, F32)
@@ -279,59 +300,26 @@
     for first, out in ((0, cumulative), (groups, squares)):
         carried = binary_dot(before, totals[first : first + groups])[:, :1]
         out[...] = jnp.sum(mask * (placed[first : first + groups] + carried), axis=0, keepdims=True)
-    message[...] = jnp.concatenate(
-        [
-            jnp.sum(totals[:groups], axis=0, keepdims=True),
-            jnp.sum(totals[groups:], axis=0, keepdims=True),
-            jnp.zeros((6, 128), F32),
-        ],
-        axis=0,
-    )
-
-
-def hazards(later, sums, events, rank, rows):
-    groups = rows // LO
+
+
+def hazards(hazard, square, rank, rows):
     row = jax.ShapeDtypeStruct((1, rows), F32)
-    small = jax.ShapeDtypeStruct((8, 128), F32)
     return pl.pallas_call(
         functools.partial(hazard_kernel, rows),
-        in_specs=[VMEM] * 4,
-        out_shape=[row, row, jax.ShapeDtypeStruct((groups, LO), F32), small],
-        out_specs=[VMEM] * 4,
+        in_specs=[VMEM] * 3,
+        out_shape=[row, row],
+        out_specs=[VMEM] * 2,
         compiler_params=pltpu.CompilerParams(**PARAMS),
         cost_estimate=pl.CostEstimate(flops=rows * LO * 200, bytes_accessed=rows * 64, transcendentals=0),
         name="hazards",
-    )(later, sums, events, rank)
-
-
-def total_kernel(tangent, risk, squares, hazard_message, message):
-    kf, rows = tangent.shape
-    plain = jnp.zeros((kf, 128), F32)
-    scaled = jnp.zeros((kf, 128), F32)
-    for start in range(0, rows, 128):
-        at = slice(start, start + 128)
-        weighted = tangent[:, at] * risk[:, at]
-        plain = plain + weighted
-        scaled = scaled + weighted * squares[:, at]
-    message[...] = jnp.concatenate([plain, scaled, hazard_message[...]], axis=0)
-
-
-def block_totals(tangent, risk, squares, hazard_message):
-    kf, rows = tangent.shape
-    return pl.pallas_call(
-        total_kernel,
-        in_specs=[VMEM] * 4,
-        out_shape=jax.ShapeDtypeStruct((2 * kf + 8, 128), F32),
-        out_specs=VMEM,
-        compiler_params=pltpu.CompilerParams(**PARAMS),
-        name="block_totals",
-    )(tangent, risk, squares, hazard_message)
+    )(hazard, square, rank)
 
 
 def suffix_kernel(parts, own, other, *refs):
     messages, (risk, rank, table) = refs[:parts], refs[parts : parts + 3]
-    tangent_out, sums, lhs = refs[parts + 3 :]
+    tangent_out, sums, plain, lhs = refs[parts + 3 :]
     kf, rows = own.shape
+    folded = jnp.zeros((kf, 128), F32)
     groups = rows // LO
     span = min(SPAN, rows)
     powers = [jnp.exp2(from_short(part[:, rows + 2 * LO :])) for part in messages]
@@ -341,13 +329,16 @@
         for part, power in zip(messages, powers):
             tangent = tangent + from_short(part[:, at]) * power[:, i : i + 1]
         tangent_out[:, at] = tangent
-        high, low = split_two(tangent * risk[:, at])
+        weighted = tangent * risk[:, at]
+        folded = folded + sum(weighted[:, j : j + 128] for j in range(0, span, 128))
+        high, low = split_two(weighted)
         high, low = high.astype(BF16), low.astype(BF16)
         group = jnp.broadcast_to(lax.rem(rank[:, at], rows) // LO, (kf, span))
         for g in range(groups):
             mask = jnp.where(group == g, 1.0, 0.0).astype(BF16)
             lhs[2 * g * kf : (2 * g + 1) * kf, at] = high * mask
             lhs[(2 * g + 1) * kf : (2 * g + 2) * kf, at] = low * mask
+    plain[...] = folded
     ordered = jnp.dot(lhs[...], table[...], preferred_element_type=F32)
     ordered = jnp.concatenate(
         [
@@ -373,8 +364,9 @@
         out_shape=[
             jax.ShapeDtypeStruct((kf, rows), F32),
             jax.ShapeDtypeStruct((groups * kf, LO), F32),
+            jax.ShapeDtypeStruct((kf, 128), F32),
         ],
-        out_specs=[VMEM] * 2,
+        out_specs=[VMEM] * 3,
         scratch_shapes=[pltpu.VMEM((groups * 2 * kf, rows), BF16)],
         compiler_params=pltpu.CompilerParams(**PARAMS),
         cost_estimate=pl.CostEstimate(
@@ -449,20 +441,20 @@
 
 
 def combine_kernel(kf, bit, count, *refs):
-    inputs, (total, state) = [ref[...] for ref in refs[:count]], refs[count:]
+    inputs, (total, state) = [ref[...] for ref in refs[:count]], refs[count + 1 :]
     total[...], state[...] = merged(kf, bit, inputs[0], inputs[1], inputs[2] if count > 2 else None)
 
 
-def combine(kf, bit, inputs):
+def combine(kf, bit, inputs, waited):
     shape = jax.ShapeDtypeStruct(inputs[0].shape, F32)
     return pl.pallas_call(
         functools.partial(combine_kernel, kf, bit, len(inputs)),
-        in_specs=[VMEM] * len(inputs),
+        in_specs=[VMEM] * len(inputs) + [pl.BlockSpec(memory_space=pl.ANY)],
         out_shape=[shape, shape],
         out_specs=[VMEM] * 2,
         compiler_params=pltpu.CompilerParams(**PARAMS),
         name="combine",
-    )(*inputs)
+    )(*inputs, waited)
 
 
 def weight_kernel(kf, bit, count, *refs):
@@ -601,7 +593,7 @@
     linear, keep, send = products(dosages, coefficients, directions, feat)
     received = [swap(piece, "feat", 1) for piece in send]
     paired, joined = join(linear, keep[1:], received[1:])
-    others = [swap(joined[q - 1], "feat", 2 * q) for q in range(1, feat // 2)]
+    others = [swap(joined[q - 1], "feat", 2 * q) for q in reversed(range(1, feat // 2))]
     table = tables(rank, paired, rows)
 
     risk, sums, ordered_events, total = risks(paired, others, rank, event_row, table, rows)
@@ -612,14 +604,12 @@
         later = later + jnp.where((lax.axis_index("ex") & bit) == 0, other, 0.0)
         total = total + other
         bit *= 2
-    tangent, later_sums = suffix_sums(keep[0], received[0], others, risk, rank, table)
-    cumulative, squares, ordered_squares, hazard_message = hazards(
-        later, sums, ordered_events, rank, rows
-    )
-    message = block_totals(tangent, risk, squares, hazard_message)
+    tangent, later_sums, plain = suffix_sums(keep[0], received[0], others, risk, rank, table)
+    hazard, ordered_squares, message = shares(later, sums, ordered_events, plain, later_sums)
+    cumulative, squares = hazards(hazard, ordered_squares, rank, rows)
     state, bit = [], 1
     while 2 * bit < ex:
-        message, *state = combine(padded, bit, [message, swap(message, "ex", bit)] + state)
+        message, *state = combine(padded, bit, [message, swap(message, "ex", bit)] + state, cumulative)
         bit *= 2
     inputs = [message, swap(message, "ex", bit)] + state
     summed = prefix_sums(later_sums, ordered_squares, rank, padded)

time: 65 us -> 62.4 us (0.960)
  waiting for transfers between devices: 29 us -> 27.2 us
  Pallas kernels: 14.5 us -> 13.6 us
    ppermute x20, waiting for transfers between devices: 29 us -> 27.2 us  [swap(): return lax.ppermute(x, axis, [(s, s ^ i) for s in range(count)])]
    pallas_call x1, Pallas kernels: 4.69 us -> 3.76 us  [products(): pl.pallas_call(functools.partial(product_kernel, feat, kf, chunk), in_spe...]
  transfers between devices with their start and end apart: 20 -> 20, of which waited for: 13 -> 14; matrix products, arithmetic and copies ran while one was open for 0% -> 0% of each run, Pallas kernels for 9% -> 12%
where the time goes in v7:
time: 62.4 us; the launch traced here: 62.3 us
  waiting for transfers between devices  27.2 us (44%)
  starting transfers between devices  21.3 us (34%)
  Pallas kernels  13.6 us (22%)
    ppermute x20, waiting for transfers between devices, swap(): return lax.ppermute(x, axis, [(s, s ^ i) for s in range(count)])  27.2 us
    ppermute x20, starting transfers between devices, swap(): return lax.ppermute(x, axis, [(s, s ^ i) for s in range(count)])  21.3 us
    pallas_call x1, Pallas kernels, products(): pl.pallas_call(functools.partial(product_kernel, feat, kf, chunk), in_spe...  3.76 us
    pallas_call x1, Pallas kernels, suffix_sums(): pl.pallas_call(functools.partial(suffix_kernel, len(messages)), in_specs=...  2.23 us
    pallas_call x1, Pallas kernels, prefix_sums(): pl.pallas_call(prefix_kernel, in_specs=[VMEM] * 3, out_shape=jax.ShapeDty...  1.92 us
    pallas_call x1, Pallas kernels, hazards(): pl.pallas_call(functools.partial(hazard_kernel, rows), in_specs=[VMEM] *...  1.63 us
  transfers between devices with their start and end apart: 20, of which 14 were waited for; matrix products, arithmetic and copies ran while one was open for 0% of the time, Pallas kernels for 12%

profile of v7, /device:TPU:0, one launch (start us, length us, event | category | flops | bytes accessed | tf_op | source)
XLA Modules:
  0.0 62.3 jit_solution(6899408057682062500)
XLA Ops:
  0.0 3.8 %products.1 = (f32[16,256]{1,0:T(8,128)S(1)}, f32[16,4096]{1,0:T(8,128)S(1)}, f32[16,4096]{1,0:T(8,128)S(1)}, f32[16,4096]{1,0:T(8,128)S(1)}, f32[16,4096]{1,0:T...) custom-call(bf16[512,128]{1,0:T(8,128)(2,1)} %directions.1, ...), custom_call_target="tpu_custom_call" | custom-call | flops 536870912 | bytes 6291456 | tf_op jit(solution)/shard_map/products/pallas_call | solution.py:113
  4.9 1.0 %collective-permute-done.1.refs_5_ = f32[16,4096]{1,0:T(8,128)S(1)} collective-permute-done((f32[16,4096]{1,0:T(8,128)S(1)}, f32[16,4096]{1,0:T(8,128)S(1)}, u32[]{:S(2)}, u32[]{:S(2)}) %collective-permute-start.1) | collective-permute-done | bytes 262176 | tf_op jit(solution)/shard_map/ppermute | solution.py:23
  6.5 3.9 %collective-permute-start.3 = (s16[16,4736]{1,0:T(8,128)(2,1)S(1)}, s16[16,4736]{1,0:T(8,128)(2,1)S(1)}, u32[]{:S(2)}, u32[]{:S(2)}) collective-permute-start(s16[16,4736]{1,0:T(8,128)(2,1)S(1)} %get-tuple-element.40), channel_id=1, source_target_pairs={{0,6},{1,7},{2,4},{3,5},{4,2},{5,3},{6,0},{7,1},{8,14},{9,15},{10,... | collective-permute-start | bytes 454664 | tf_op jit(solution)/shard_map/ppermute | solution.py:23
  11.6 3.4 %collective-permute-done.3.refs_0_ = s16[16,4736]{1,0:T(8,128)(2,1)S(1)} collective-permute-done((s16[16,4736]{1,0:T(8,128)(2,1)S(1)}, s16[16,4736]{1,0:T(8,128)(2,1)S(1)}, u32[]{:S(2)}, u32[]{:S(2)}) %collective-permute-start.3) | collective-permute-done | bytes 151584 | tf_op jit(solution)/shard_map/ppermute | solution.py:23
  15.1 2.8 %collective-permute-done.4.refs_1_ = s16[16,4736]{1,0:T(8,128)(2,1)S(1)} collective-permute-done((s16[16,4736]{1,0:T(8,128)(2,1)S(1)}, s16[16,4736]{1,0:T(8,128)(2,1)S(1)}, u32[]{:S(2)}, u32[]{:S(2)}) %collective-permute-start.4) | collective-permute-done | bytes 151584 | tf_op jit(solution)/shard_map/ppermute | solution.py:23
  18.1 1.0 %risks.1 = (f32[1,4096]{1,0:T(1,128)S(1)}, f32[16,256]{1,0:T(8,128)S(1)}, f32[16,256]{1,0:T(8,128)S(1)}, f32[8,128]{1,0:T(8,128)S(1)}) custom-call(f32[16,256]{1,0:T(8,128)S(1)} %get-tuple-element.39.waited.linear, s16[16,4736]{1,0:T(8,128)(2,1)S(1)} %collective-permute-done.3.refs_0_, s16[16,4736]{1,0:T(8,128)(2,1)S(1)} %collective-permute-done.4.refs_1_, ...), custom_call_target="tpu_custom_call" | custom-call | flops 134217728 | bytes 262144 | tf_op jit(solution)/shard_map/risks/pallas_call | solution.py:244
  19.1 1.6 %collective-permute-start.6 = (f32[8,128]{1,0:T(8,128)S(1)}, f32[8,128]{1,0:T(8,128)S(1)}, u32[]{:S(2)}, u32[]{:S(2)}) collective-permute-start(f32[8,128]{1,0:T(8,128)S(1)} %get-tuple-element.43), channel_id=1, source_target_pairs={{0,8},{8,0},{16,24},{24,16},{1,9},{9,1},{17,25},{25,17},{2,10},{10... | collective-permute-start | bytes 12296 | tf_op jit(solution)/shard_map/ppermute | solution.py:23
  20.7 2.0 %collective-permute-done.6 = f32[8,128]{1,0:T(8,128)S(1)} collective-permute-done((f32[8,128]{1,0:T(8,128)S(1)}, f32[8,128]{1,0:T(8,128)S(1)}, u32[]{:S(2)}, u32[]{:S(2)}) %collective-permute-start.6) | collective-permute-done | bytes 4128 | tf_op jit(solution)/shard_map/ppermute | solution.py:23
  22.8 2.6 %collective-permute-start.7 = (f32[8,128]{1,0:T(8,128)S(1)}, f32[8,128]{1,0:T(8,128)S(1)}, u32[]{:S(2)}, u32[]{:S(2)}) collective-permute-start(f32[8,128]{1,0:T(8,128)S(1)} %add.9), channel_id=1, source_target_pairs={{0,16},{8,24},{16,0},{24,8},{1,17},{9,25},{17,1},{25,9},{2,18},{10... | collective-permute-start | bytes 12296 | tf_op jit(solution)/shard_map/ppermute | solution.py:23
  25.4 2.2 %suffix_sums.1 = (f32[16,4096]{1,0:T(8,128)S(1)}, f32[256,256]{1,0:T(8,128)S(1)}, f32[16,128]{1,0:T(8,128)S(1)}) custom-call(f32[16,4096]{1,0:T(8,128)S(1)} %get-tuple-element.46.own, f32[16,4096]{1,0:T(8,128)S(1)} %collective-permute-done.8.other, s16[16,4736]{1,0:T(8,128)(2,1)S(1)} %collective-permute-done.3.refs_0_, ...), custom_call_target="tpu_custom_call" | custom-call | flops 1073741824 | bytes 1572864 | tf_op jit(solution)/shard_map/suffix_sums/pallas_call | solution.py:361
  27.8 1.6 %collective-permute-start.9 = (f32[40,128]{1,0:T(8,128)S(1)}, f32[40,128]{1,0:T(8,128)S(1)}, u32[]{:S(2)}, u32[]{:S(2)}) collective-permute-start(f32[40,128]{1,0:T(8,128)S(1)} %get-tuple-element.51.refs_0_), channel_id=1, source_target_pairs={{0,8},{8,0},{16,24},{24,16},{1,9},{9,1},{17,25},{25,17},{2,10},{10... | collective-permute-start | bytes 61448 | tf_op jit(solution)/shard_map/ppermute | solution.py:23
  29.4 1.6 %hazards.1 = (f32[1,4096]{1,0:T(1,128)S(1)}, f32[1,4096]{1,0:T(1,128)S(1)}) custom-call(f32[16,256]{1,0:T(8,128)S(1)} %get-tuple-element.52.hazard, f32[16,256]{1,0:T(8,128)S(1)} %get-tuple-element.53.square.squares, s32[1,4096]{1,0:T(1,128)S(1)} %bitcast.5), custom_call_target="tpu_custom_call" | custom-call | flops 209715200 | bytes 262144 | tf_op jit(solution)/shard_map/hazards/pallas_call | solution.py:307
  31.6 2.3 %collective-permute-start.10 = (f32[40,128]{1,0:T(8,128)S(1)}, f32[40,128]{1,0:T(8,128)S(1)}, u32[]{:S(2)}, u32[]{:S(2)}) collective-permute-start(f32[40,128]{1,0:T(8,128)S(1)} %get-tuple-element.55.refs_0_), channel_id=1, source_target_pairs={{0,16},{8,24},{16,0},{24,8},{1,17},{9,25},{17,1},{25,9},{2,18},{10... | collective-permute-start | bytes 61448 | tf_op jit(solution)/shard_map/ppermute | solution.py:23
  33.9 1.9 %prefix_sums.1.refs_4_ = f32[16,4096]{1,0:T(8,128)S(1)} custom-call(f32[256,256]{1,0:T(8,128)S(1)} %get-tuple-element.50.ordered.sums, f32[16,256]{1,0:T(8,128)S(1)} %get-tuple-element.53.square.squares, s32[1,4096]{1,0:T(1,128)S(1)} %bitcast.6), custom_call_target="tpu_custom_call" | custom-call | flops 1073741824 | bytes 1572864 | tf_op jit(solution)/shard_map/prefix_sums/pallas_call | solution.py:409
  36.5 1.6 %collective-permute-start.12 = (bf16[16,4096]{1,0:T(8,128)(2,1)S(1)}, bf16[16,4096]{1,0:T(8,128)(2,1)S(1)}, u32[]{:S(2)}, u32[]{:S(2)}) collective-permute-start(bf16[16,4096]{1,0:T(8,128)(2,1)S(1)} %weights.1.refs_0_), channel_id=1, source_target_pairs={{0,2},{1,3},{2,0},{3,1},{4,6},{5,7},{6,4},{7,5},{8,10},{9,11},{10,... | collective-permute-start | bytes 393224 | tf_op jit(solution)/shard_map/ppermute | solution.py:23
  38.8 1.3 %collective-permute-start.16 = (bf16[16,4096]{1,0:T(8,128)(2,1)S(1)}, bf16[16,4096]{1,0:T(8,128)(2,1)S(1)}, u32[]{:S(2)}, u32[]{:S(2)}) collective-permute-start(bf16[16,4096]{1,0:T(8,128)(2,1)S(1)} %weights.1.refs_0_), channel_id=1, source_target_pairs={{0,6},{1,7},{2,4},{3,5},{4,2},{5,3},{6,0},{7,1},{8,14},{9,15},{10,... | collective-permute-start | bytes 393224 | tf_op jit(solution)/shard_map/ppermute | solution.py:23
  40.1 1.5 %collective-permute-done.12.refs_2_ = bf16[16,4096]{1,0:T(8,128)(2,1)S(1)} collective-permute-done((bf16[16,4096]{1,0:T(8,128)(2,1)S(1)}, bf16[16,4096]{1,0:T(8,128)(2,1)S(1)}, u32[]{:S(2)}, u32[]{:S(2)}) %collective-permute-start.12) | collective-permute-done | bytes 131104 | tf_op jit(solution)/shard_map/ppermute | solution.py:23
  41.6 1.5 %collective-permute-done.14.refs_4_ = bf16[16,4096]{1,0:T(8,128)(2,1)S(1)} collective-permute-done((bf16[16,4096]{1,0:T(8,128)(2,1)S(1)}, bf16[16,4096]{1,0:T(8,128)(2,1)S(1)}, u32[]{:S(2)}, u32[]{:S(2)}) %collective-permute-start.14) | collective-permute-done | bytes 131104 | tf_op jit(solution)/shard_map/ppermute | solution.py:23
  43.1 1.6 %collective-permute-done.16.refs_6_ = bf16[16,4096]{1,0:T(8,128)(2,1)S(1)} collective-permute-done((bf16[16,4096]{1,0:T(8,128)(2,1)S(1)}, bf16[16,4096]{1,0:T(8,128)(2,1)S(1)}, u32[]{:S(2)}, u32[]{:S(2)}) %collective-permute-start.16) | collective-permute-done | bytes 131104 | tf_op jit(solution)/shard_map/ppermute | solution.py:23
  44.7 1.3 %collective-permute-done.17.refs_7_ = bf16[16,4096]{1,0:T(8,128)(2,1)S(1)} collective-permute-done((bf16[16,4096]{1,0:T(8,128)(2,1)S(1)}, bf16[16,4096]{1,0:T(8,128)(2,1)S(1)}, u32[]{:S(2)}, u32[]{:S(2)}) %collective-permute-start.17) | collective-permute-done | bytes 131104 | tf_op jit(solution)/shard_map/ppermute | solution.py:23
  47.0 1.6 %collective-permute-start.18 = (s16[528,128]{1,0:T(8,128)(2,1)S(1)}, s16[528,128]{1,0:T(8,128)(2,1)S(1)}, u32[]{:S(2)}, u32[]{:S(2)}) collective-permute-start(s16[528,128]{1,0:T(8,128)(2,1)S(1)} %gradients.1.mine), channel_id=1, source_target_pairs={{0,8},{8,0},{16,24},{24,16},{1,9},{9,1},{17,25},{25,17},{2,10},{10... | collective-permute-start | bytes 405512 | tf_op jit(solution)/shard_map/ppermute | solution.py:23
  48.7 4.1 %collective-permute-done.18.other = s16[528,128]{1,0:T(8,128)(2,1)S(1)} collective-permute-done((s16[528,128]{1,0:T(8,128)(2,1)S(1)}, s16[528,128]{1,0:T(8,128)(2,1)S(1)}, u32[]{:S(2)}, u32[]{:S(2)}) %collective-permute-start.18) | collective-permute-done | bytes 135200 | tf_op jit(solution)/shard_map/ppermute | solution.py:23
  52.9 2.4 %collective-permute-start.19 = (s16[528,128]{1,0:T(8,128)(2,1)S(1)}, s16[528,128]{1,0:T(8,128)(2,1)S(1)}, u32[]{:S(2)}, u32[]{:S(2)}) collective-permute-start(s16[528,128]{1,0:T(8,128)(2,1)S(1)} %merge.1.mine), channel_id=1, source_target_pairs={{0,16},{8,24},{16,0},{24,8},{1,17},{9,25},{17,1},{25,9},{2,18},{10... | collective-permute-start | bytes 405512 | tf_op jit(solution)/shard_map/ppermute | solution.py:23
  55.2 6.3 %collective-permute-done.19.other = s16[528,128]{1,0:T(8,128)(2,1)S(1)} collective-permute-done((s16[528,128]{1,0:T(8,128)(2,1)S(1)}, s16[528,128]{1,0:T(8,128)(2,1)S(1)}, u32[]{:S(2)}, u32[]{:S(2)}) %collective-permute-start.19) | collective-permute-done | bytes 135200 | tf_op jit(solution)/shard_map/ppermute | solution.py:23
  (37 shorter events, 7.3 us)
Async XLA Ops:
  0.0 11.0 %copy-start.1 = (s32[4096]{0:T(1024)S(1)}, s32[4096]{0:T(1024)}, u32[]{:S(2)}) copy-start(s32[4096]{0:T(1024)} %param.8) | copy-start | bytes 49156
  0.0 18.1 %copy-start.2 = (s32[4096]{0:T(1024)S(1)}, s32[4096]{0:T(1024)}, u32[]{:S(2)}) copy-start(s32[4096]{0:T(1024)} %param.9) | copy-start | bytes 49156
  3.8 2.5 %collective-permute-start = (f32[16,4352]{1,0:T(8,128)S(1)}, f32[16,4352]{1,0:T(8,128)S(1)}, u32[]{:S(2)}, u32[]{:S(2)}) collective-permute-start(f32[16,4352]{1,0:T(8,128)S(1)} %get-tuple-element.36), channel_id=1, source_target_pairs={{0,1},{1,0},{2,3},{3,2},{4,5},{5,4},{6,7},{7,6},{8,9},{9,8},{10,11... | collective-permute-start | bytes 835592 | tf_op jit(solution)/shard_map/ppermute | solution.py:23
  4.3 1.6 %collective-permute-start.1 = (f32[16,4096]{1,0:T(8,128)S(1)}, f32[16,4096]{1,0:T(8,128)S(1)}, u32[]{:S(2)}, u32[]{:S(2)}) collective-permute-start(f32[16,4096]{1,0:T(8,128)S(1)} %get-tuple-element.37), channel_id=1, source_target_pairs={{0,1},{1,0},{2,3},{3,2},{4,5},{5,4},{6,7},{7,6},{8,9},{9,8},{10,11... | collective-permute-start | bytes 786440 | tf_op jit(solution)/shard_map/ppermute | solution.py:23
  4.4 1.9 %collective-permute-start.2 = (f32[16,4096]{1,0:T(8,128)S(1)}, f32[16,4096]{1,0:T(8,128)S(1)}, u32[]{:S(2)}, u32[]{:S(2)}) collective-permute-start(f32[16,4096]{1,0:T(8,128)S(1)} %get-tuple-element.38), channel_id=1, source_target_pairs={{0,1},{1,0},{2,3},{3,2},{4,5},{5,4},{6,7},{7,6},{8,9},{9,8},{10,11... | collective-permute-start | bytes 786440 | tf_op jit(solution)/shard_map/ppermute | solution.py:23
  4.8 20.6 %collective-permute-start.8 = (f32[16,4096]{1,0:T(8,128)S(1)}, f32[16,4096]{1,0:T(8,128)S(1)}, u32[]{:S(2)}, u32[]{:S(2)}) collective-permute-start(f32[16,4096]{1,0:T(8,128)S(1)} %get-tuple-element.47), channel_id=1, source_target_pairs={{0,1},{1,0},{2,3},{3,2},{4,5},{5,4},{6,7},{7,6},{8,9},{9,8},{10,11... | collective-permute-start | bytes 786440 | tf_op jit(solution)/shard_map/ppermute | solution.py:23
  6.5 8.6 %collective-permute-start.3 = (s16[16,4736]{1,0:T(8,128)(2,1)S(1)}, s16[16,4736]{1,0:T(8,128)(2,1)S(1)}, u32[]{:S(2)}, u32[]{:S(2)}) collective-permute-start(s16[16,4736]{1,0:T(8,128)(2,1)S(1)} %get-tuple-element.40), channel_id=1, source_target_pairs={{0,6},{1,7},{2,4},{3,5},{4,2},{5,3},{6,0},{7,1},{8,14},{9,15},{10,... | collective-permute-start | bytes 454664 | tf_op jit(solution)/shard_map/ppermute | solution.py:23
  10.3 7.5 %collective-permute-start.4 = (s16[16,4736]{1,0:T(8,128)(2,1)S(1)}, s16[16,4736]{1,0:T(8,128)(2,1)S(1)}, u32[]{:S(2)}, u32[]{:S(2)}) collective-permute-start(s16[16,4736]{1,0:T(8,128)(2,1)S(1)} %get-tuple-element.41), channel_id=1, source_target_pairs={{0,4},{1,5},{2,6},{3,7},{4,0},{5,1},{6,2},{7,3},{8,12},{9,13},{10,... | collective-permute-start | bytes 454664 | tf_op jit(solution)/shard_map/ppermute | solution.py:23
  10.8 7.3 %collective-permute-start.5 = (s16[16,4736]{1,0:T(8,128)(2,1)S(1)}, s16[16,4736]{1,0:T(8,128)(2,1)S(1)}, u32[]{:S(2)}, u32[]{:S(2)}) collective-permute-start(s16[16,4736]{1,0:T(8,128)(2,1)S(1)} %get-tuple-element.42), channel_id=1, source_target_pairs={{0,2},{1,3},{2,0},{3,1},{4,6},{5,7},{6,4},{7,5},{8,10},{9,11},{10,... | collective-permute-start | bytes 454664 | tf_op jit(solution)/shard_map/ppermute | solution.py:23
  19.1 3.7 %collective-permute-start.6 = (f32[8,128]{1,0:T(8,128)S(1)}, f32[8,128]{1,0:T(8,128)S(1)}, u32[]{:S(2)}, u32[]{:S(2)}) collective-permute-start(f32[8,128]{1,0:T(8,128)S(1)} %get-tuple-element.43), channel_id=1, source_target_pairs={{0,8},{8,0},{16,24},{24,16},{1,9},{9,1},{17,25},{25,17},{2,10},{10... | collective-permute-start | bytes 12296 | tf_op jit(solution)/shard_map/ppermute | solution.py:23
  22.8 4.8 %collective-permute-start.7 = (f32[8,128]{1,0:T(8,128)S(1)}, f32[8,128]{1,0:T(8,128)S(1)}, u32[]{:S(2)}, u32[]{:S(2)}) collective-permute-start(f32[8,128]{1,0:T(8,128)S(1)} %add.9), channel_id=1, source_target_pairs={{0,16},{8,24},{16,0},{24,8},{1,17},{9,25},{17,1},{25,9},{2,18},{10... | collective-permute-start | bytes 12296 | tf_op jit(solution)/shard_map/ppermute | solution.py:23
  25.4 20.7 %copy-start = (bf16[4096,512]{1,0:T(8,128)(2,1)S(1)}, bf16[4096,512]{1,0:T(8,128)(2,1)}, u32[]{:S(2)}) copy-start(bf16[4096,512]{1,0:T(8,128)(2,1)} %refs_8_.1) | copy-start | bytes 12582916
  27.8 3.8 %collective-permute-start.9 = (f32[40,128]{1,0:T(8,128)S(1)}, f32[40,128]{1,0:T(8,128)S(1)}, u32[]{:S(2)}, u32[]{:S(2)}) collective-permute-start(f32[40,128]{1,0:T(8,128)S(1)} %get-tuple-element.51.refs_0_), channel_id=1, source_target_pairs={{0,8},{8,0},{16,24},{24,16},{1,9},{9,1},{17,25},{25,17},{2,10},{10... | collective-permute-start | bytes 61448 | tf_op jit(solution)/shard_map/ppermute | solution.py:23
  31.6 4.7 %collective-permute-start.10 = (f32[40,128]{1,0:T(8,128)S(1)}, f32[40,128]{1,0:T(8,128)S(1)}, u32[]{:S(2)}, u32[]{:S(2)}) collective-permute-start(f32[40,128]{1,0:T(8,128)S(1)} %get-tuple-element.55.refs_0_), channel_id=1, source_target_pairs={{0,16},{8,24},{16,0},{24,8},{1,17},{9,25},{17,1},{25,9},{2,18},{10... | collective-permute-start | bytes 61448 | tf_op jit(solution)/shard_map/ppermute | solution.py:23
  36.5 5.0 %collective-permute-start.12 = (bf16[16,4096]{1,0:T(8,128)(2,1)S(1)}, bf16[16,4096]{1,0:T(8,128)(2,1)S(1)}, u32[]{:S(2)}, u32[]{:S(2)}) collective-permute-start(bf16[16,4096]{1,0:T(8,128)(2,1)S(1)} %weights.1.refs_0_), channel_id=1, source_target_pairs={{0,2},{1,3},{2,0},{3,1},{4,6},{5,7},{6,4},{7,5},{8,10},{9,11},{10,... | collective-permute-start | bytes 393224 | tf_op jit(solution)/shard_map/ppermute | solution.py:23
  38.1 5.0 %collective-permute-start.14 = (bf16[16,4096]{1,0:T(8,128)(2,1)S(1)}, bf16[16,4096]{1,0:T(8,128)(2,1)S(1)}, u32[]{:S(2)}, u32[]{:S(2)}) collective-permute-start(bf16[16,4096]{1,0:T(8,128)(2,1)S(1)} %weights.1.refs_0_), channel_id=1, source_target_pairs={{0,4},{1,5},{2,6},{3,7},{4,0},{5,1},{6,2},{7,3},{8,12},{9,13},{10,... | collective-permute-start | bytes 393224 | tf_op jit(solution)/shard_map/ppermute | solution.py:23
  38.8 5.9 %collective-permute-start.16 = (bf16[16,4096]{1,0:T(8,128)(2,1)S(1)}, bf16[16,4096]{1,0:T(8,128)(2,1)S(1)}, u32[]{:S(2)}, u32[]{:S(2)}) collective-permute-start(bf16[16,4096]{1,0:T(8,128)(2,1)S(1)} %weights.1.refs_0_), channel_id=1, source_target_pairs={{0,6},{1,7},{2,4},{3,5},{4,2},{5,3},{6,0},{7,1},{8,14},{9,15},{10,... | collective-permute-start | bytes 393224 | tf_op jit(solution)/shard_map/ppermute | solution.py:23
  40.1 4.6 %collective-permute-start.11 = (bf16[16,4096]{1,0:T(8,128)(2,1)S(1)}, bf16[16,4096]{1,0:T(8,128)(2,1)S(1)}, u32[]{:S(2)}, u32[]{:S(2)}) collective-permute-start(bf16[16,4096]{1,0:T(8,128)(2,1)S(1)} %weights.1.refs_0_), channel_id=1, source_target_pairs={{0,1},{1,0},{2,3},{3,2},{4,5},{5,4},{6,7},{7,6},{8,9},{9,8},{10,11... | collective-permute-start | bytes 393224 | tf_op jit(solution)/shard_map/ppermute | solution.py:23
  41.6 3.1 %collective-permute-start.13 = (bf16[16,4096]{1,0:T(8,128)(2,1)S(1)}, bf16[16,4096]{1,0:T(8,128)(2,1)S(1)}, u32[]{:S(2)}, u32[]{:S(2)}) collective-permute-start(bf16[16,4096]{1,0:T(8,128)(2,1)S(1)} %collective-permute-done.12.refs_2_), channel_id=1, source_target_pairs={{0,1},{1,0},{2,3},{3,2},{4,5},{5,4},{6,7},{7,6},{8,9},{9,8},{10,11... | collective-permute-start | bytes 393224 | tf_op jit(solution)/shard_map/ppermute | solution.py:23
  43.1 1.6 %collective-permute-start.15 = (bf16[16,4096]{1,0:T(8,128)(2,1)S(1)}, bf16[16,4096]{1,0:T(8,128)(2,1)S(1)}, u32[]{:S(2)}, u32[]{:S(2)}) collective-permute-start(bf16[16,4096]{1,0:T(8,128)(2,1)S(1)} %collective-permute-done.14.refs_4_), channel_id=1, source_target_pairs={{0,1},{1,0},{2,3},{3,2},{4,5},{5,4},{6,7},{7,6},{8,9},{9,8},{10,11... | collective-permute-start | bytes 393224 | tf_op jit(solution)/shard_map/ppermute | solution.py:23
  44.7 1.3 %collective-permute-start.17 = (bf16[16,4096]{1,0:T(8,128)(2,1)S(1)}, bf16[16,4096]{1,0:T(8,128)(2,1)S(1)}, u32[]{:S(2)}, u32[]{:S(2)}) collective-permute-start(bf16[16,4096]{1,0:T(8,128)(2,1)S(1)} %collective-permute-done.16.refs_6_), channel_id=1, source_target_pairs={{0,1},{1,0},{2,3},{3,2},{4,5},{5,4},{6,7},{7,6},{8,9},{9,8},{10,11... | collective-permute-start | bytes 393224 | tf_op jit(solution)/shard_map/ppermute | solution.py:23
  47.0 5.7 %collective-permute-start.18 = (s16[528,128]{1,0:T(8,128)(2,1)S(1)}, s16[528,128]{1,0:T(8,128)(2,1)S(1)}, u32[]{:S(2)}, u32[]{:S(2)}) collective-permute-start(s16[528,128]{1,0:T(8,128)(2,1)S(1)} %gradients.1.mine), channel_id=1, source_target_pairs={{0,8},{8,0},{16,24},{24,16},{1,9},{9,1},{17,25},{25,17},{2,10},{10... | collective-permute-start | bytes 405512 | tf_op jit(solution)/shard_map/ppermute | solution.py:23
  52.9 8.7 %collective-permute-start.19 = (s16[528,128]{1,0:T(8,128)(2,1)S(1)}, s16[528,128]{1,0:T(8,128)(2,1)S(1)}, u32[]{:S(2)}, u32[]{:S(2)}) collective-permute-start(s16[528,128]{1,0:T(8,128)(2,1)S(1)} %merge.1.mine), channel_id=1, source_target_pairs={{0,16},{8,24},{16,0},{24,8},{1,17},{9,25},{17,1},{25,9},{2,18},{10... | collective-permute-start | bytes 405512 | tf_op jit(solution)/shard_map/ppermute | solution.py:23

commit v8 on v7

--- a/solution.py
+++ b/solution.py
@@ -45,13 +45,18 @@
     return jnp.where(keep(first, second), 1.0, 0.0)
 
 
+def stacked(parts):
+    return jnp.concatenate(parts, axis=0).astype(BF16)
+
+
+def unstacked(values, count):
+    height = values.shape[0] // count
+    return sum(values[i * height : (i + 1) * height] for i in range(count))
+
+
 def dot_binary(a, b):
-    b = b.astype(BF16)
-    total = None
-    for part in split_three(a):
-        term = jnp.dot(part.astype(BF16), b, preferred_element_type=F32)
-        total = term if total is None else total + term
-    return total
+    parts = jnp.dot(stacked(split_three(a)), b.astype(BF16), preferred_element_type=F32)
+    return unstacked(parts, 3)
 
 
 def binary_dot(a, b):
@@ -100,7 +105,7 @@
             row = result[width : width + 1, start : start + LO]
             group = (first + start) // LO
             linear[group : group + 1, :] = row
-            send[1][group : group + 1, persons:] = row
+            send[-1][group : group + 1, persons:] = row
 
 
 def products(dosages, coefficients, directions, feat):
@@ -114,9 +119,8 @@
         functools.partial(product_kernel, feat, kf, chunk),
         in_specs=[HBM, HBM, HBM],
         out_shape=[jax.ShapeDtypeStruct((kf, LO), F32)]
-        + [piece] * (feat // 2 + 1)
-        + [first]
-        + [piece] * (feat // 2 - 2),
+        + [piece] * (feat - 1)
+        + [first],
         out_specs=[VMEM] * (feat + 1),
         scratch_shapes=[
             pltpu.VMEM((persons, variants), BF16),
@@ -147,44 +151,45 @@
     return values.astype(jnp.int32).astype(F32)
 
 
-def join_kernel(count, *refs):
-    linear, keep, received = refs[0], refs[1 : 1 + count], refs[1 + count : 1 + 2 * count]
-    linear_out, outs = refs[1 + 2 * count], refs[2 + 2 * count :]
-    kf, rows = keep[0].shape
+def join_kernel(linear, *refs):
+    mine, other = refs[:2]
+    out = refs[-1]
+    kf, rows = mine.shape
     span = min(SPAN, rows)
     lane = lax.broadcasted_iota(jnp.int32, (kf, 128), 1)
-    paired = linear[...] + received[0][:, rows:]
-    linear_out[...] = paired
+    paired = linear[...]
+    if len(refs) > 3:
+        paired = paired + other[:, rows:]
+        refs[2][...] = paired
     linear_power = power_of(jnp.max(jnp.abs(paired), axis=1, keepdims=True))
     scaled = paired * jnp.exp2(-linear_power)
     whole = jnp.round(scaled)
-    high, low = to_short(whole), to_short((scaled - whole) * 32768.0)
-    for mine, other, out in zip(keep, received, outs):
-        powers = jnp.where(lane == rows // span, linear_power, 0.0)
-        for i in range(rows // span):
-            at = slice(i * span, (i + 1) * span)
-            total = mine[:, at] + other[:, at]
-            power = power_of(jnp.max(jnp.abs(total), axis=1, keepdims=True))
-            out[:, at] = to_short(total * jnp.exp2(-power))
-            powers = jnp.where(lane == i, power, powers)
-        out[:, rows : rows + LO] = high
-        out[:, rows + LO : rows + 2 * LO] = low
-        out[:, rows + 2 * LO :] = to_short(powers)
+    powers = jnp.where(lane == rows // span, linear_power, 0.0)
+    for i in range(rows // span):
+        at = slice(i * span, (i + 1) * span)
+        total = mine[:, at] + other[:, at]
+        power = power_of(jnp.max(jnp.abs(total), axis=1, keepdims=True))
+        out[:, at] = to_short(total * jnp.exp2(-power))
+        powers = jnp.where(lane == i, power, powers)
+    out[:, rows : rows + LO] = to_short(whole)
+    out[:, rows + LO : rows + 2 * LO] = to_short((scaled - whole) * 32768.0)
+    out[:, rows + 2 * LO :] = to_short(powers)
 
 
 def join(linear, keep, received):
-    count = len(keep)
-    kf, rows = keep[0].shape
+    kf, rows = keep.shape
     message = jax.ShapeDtypeStruct((kf, rows + 2 * LO + 128), jnp.int16)
-    out = pl.pallas_call(
-        functools.partial(join_kernel, count),
-        in_specs=[VMEM] * (2 * count + 1),
-        out_shape=[jax.ShapeDtypeStruct(linear.shape, F32)] + [message] * count,
-        out_specs=[VMEM] * (count + 1),
+    shapes = [message]
+    if received.shape[1] > rows:
+        shapes = [jax.ShapeDtypeStruct(linear.shape, F32), message]
+    return pl.pallas_call(
+        join_kernel,
+        in_specs=[VMEM] * 3,
+        out_shape=shapes,
+        out_specs=[VMEM] * len(shapes),
         compiler_params=pltpu.CompilerParams(**PARAMS),
         name="join",
-    )(linear, *keep, *received)
-    return out[0], out[1:]
+    )(linear, keep, received)
 
 
 def table_kernel(rows, rank, waited, table):
@@ -257,10 +262,19 @@
     )(linear, *messages, rank, events, table)
 
 
-def share_kernel(later, sums, events, plain, ordered, hazard_out, squares, message):
+def share_kernel(ex, *refs):
+    messages, (sums, events, plain, ordered) = refs[:ex], refs[ex : ex + 4]
+    hazard_out, squares, message, count_out = refs[ex + 4 :]
     kf = plain.shape[0]
     groups = sums.shape[0]
-    risk_sum = sums[...] + later[0:1, 0:1]
+    me = lax.axis_index("ex")
+    later = jnp.zeros((1, 1), F32)
+    count = messages[0][1:2]
+    for i in range(1, ex):
+        later = later + jnp.where((me ^ i) > me, messages[i][0:1, 0:1], 0.0)
+        count = count + messages[i][1:2]
+    count_out[...] = jnp.broadcast_to(count, count_out.shape)
+    risk_sum = sums[...] + later
     hazard = events[...] / risk_sum
     square = events[...] / (risk_sum * risk_sum)
     hazard_out[...] = hazard
@@ -275,16 +289,21 @@
     message[2 * kf :] = jnp.concatenate(rows + [jnp.zeros((6, 128), F32)], axis=0)
 
 
-def shares(later, sums, events, plain, ordered):
+def shares(messages, sums, events, plain, ordered):
     flat = jax.ShapeDtypeStruct(sums.shape, F32)
     return pl.pallas_call(
-        share_kernel,
-        in_specs=[VMEM] * 5,
-        out_shape=[flat, flat, jax.ShapeDtypeStruct((2 * plain.shape[0] + 8, 128), F32)],
-        out_specs=[VMEM] * 3,
+        functools.partial(share_kernel, len(messages)),
+        in_specs=[VMEM] * (len(messages) + 4),
+        out_shape=[
+            flat,
+            flat,
+            jax.ShapeDtypeStruct((2 * plain.shape[0] + 8, 128), F32),
+            jax.ShapeDtypeStruct((8, 128), F32),
+        ],
+        out_specs=[VMEM] * 4,
         compiler_params=pltpu.CompilerParams(**PARAMS),
         name="shares",
-    )(later, sums, events, plain, ordered)
+    )(*messages, sums, events, plain, ordered)
 
 
 def hazard_kernel(rows, hazard, square, rank, cumulative, squares):
@@ -388,16 +407,13 @@
         rows_of = slice(g * kf, (g + 1) * kf)
         summed[g] = inside[rows_of] + carried
         carried = carried + inside[rows_of, LO - 1 :]
-    high, low = split_two(jnp.concatenate(summed, axis=0))
-    high, low = high.astype(BF16), low.astype(BF16)
+    both = stacked(split_two(jnp.concatenate(summed, axis=0)))
     for start in range(0, rows, chunk):
         at = slice(start, start + chunk)
         place = lax.rem(rank[:, at], rows)
         group = place // LO
         spread = one_hot(lax.rem(place, LO), LO)
-        placed = jnp.dot(high, spread, preferred_element_type=F32) + jnp.dot(
-            low, spread, preferred_element_type=F32
-        )
+        placed = unstacked(jnp.dot(both, spread, preferred_element_type=F32), 2)
         picked = jnp.zeros((kf, chunk), F32)
         for g in range(groups):
             picked = picked + jnp.where(group == g, placed[g * kf : (g + 1) * kf], 0.0)
@@ -419,64 +435,40 @@
     )(sums, squares, rank)
 
 
-def merged(kf, bit, mine, other, state):
-    later_other = (lax.axis_index("ex") & bit) == 0
-    plain, scaled, rest = mine[:kf], mine[kf : 2 * kf], mine[2 * kf :]
-    other_plain, other_scaled, other_rest = other[:kf], other[kf : 2 * kf], other[2 * kf :]
-    square, other_square = rest[1:2], other_rest[1:2]
-    crossed = jnp.where(later_other, square * other_plain, other_square * plain)
-    total = jnp.concatenate([plain + other_plain, scaled + other_scaled + crossed, rest + other_rest], axis=0)
-    if state is None:
-        state = jnp.zeros_like(mine)
-    later, before, before_rest = state[:kf], state[kf : 2 * kf], state[2 * kf :]
-    state = jnp.concatenate(
-        [
-            later + jnp.where(later_other, other_plain, 0.0),
-            before + jnp.where(later_other, before_rest[1:2] * other_plain, other_scaled + other_square * plain),
-            before_rest + jnp.where(later_other, 0.0, other_rest),
-        ],
-        axis=0,
-    )
-    return total, state
-
-
-def combine_kernel(kf, bit, count, *refs):
-    inputs, (total, state) = [ref[...] for ref in refs[:count]], refs[count + 1 :]
-    total[...], state[...] = merged(kf, bit, inputs[0], inputs[1], inputs[2] if count > 2 else None)
-
-
-def combine(kf, bit, inputs, waited):
-    shape = jax.ShapeDtypeStruct(inputs[0].shape, F32)
-    return pl.pallas_call(
-        functools.partial(combine_kernel, kf, bit, len(inputs)),
-        in_specs=[VMEM] * len(inputs) + [pl.BlockSpec(memory_space=pl.ANY)],
-        out_shape=[shape, shape],
-        out_specs=[VMEM] * 2,
-        compiler_params=pltpu.CompilerParams(**PARAMS),
-        name="combine",
-    )(*inputs, waited)
-
-
-def weight_kernel(kf, bit, count, *refs):
-    inputs = [ref[...] for ref in refs[:count]]
-    tangent, local, risk, cumulative, squares, weighted = refs[count:]
-    _, state = merged(kf, bit, inputs[0], inputs[1], inputs[2] if count > 2 else None)
-    later = jnp.sum(state[:kf], axis=1, keepdims=True)
-    before = jnp.sum(state[kf : 2 * kf], axis=1, keepdims=True)
-    hazard_before = state[2 * kf : 2 * kf + 1, :1]
-    value = tangent[...] * (cumulative[...] + hazard_before) - (local[...] + squares[...] * later + before)
+def weight_kernel(ex, *refs):
+    messages, (tangent, local, risk, cumulative, squares) = refs[:ex], refs[ex : ex + 5]
+    weighted, placed = refs[ex + 5 :]
+    kf = tangent.shape[0]
+    me = lax.axis_index("ex")
+    for i in range(ex):
+        placed[me ^ i] = messages[i][...]
+    later = jnp.zeros((kf, 128), F32)
+    own_later, before = later, later
+    hazard_before = jnp.zeros((1, 128), F32)
+    for b in reversed(range(ex)):
+        plain, scaled, square = placed[b, :kf], placed[b, kf : 2 * kf], placed[b, 2 * kf + 1 : 2 * kf + 2]
+        own_later = own_later + jnp.where(b > me, plain, 0.0)
+        before = before + jnp.where(b < me, scaled + square * later, 0.0)
+        hazard_before = hazard_before + jnp.where(b < me, placed[b, 2 * kf : 2 * kf + 1], 0.0)
+        later = later + plain
+    own_later = jnp.sum(own_later, axis=1, keepdims=True)
+    before = jnp.sum(before, axis=1, keepdims=True)
+    hazard_before = hazard_before[:, :1]
+    value = tangent[...] * (cumulative[...] + hazard_before) - (local[...] + squares[...] * own_later + before)
     weighted[...] = (risk[...] * value).astype(BF16)
 
 
-def weights(bit, inputs, tangent, local, risk, cumulative, squares):
-    return pl.pallas_call(
-        functools.partial(weight_kernel, tangent.shape[0], bit, len(inputs)),
-        in_specs=[VMEM] * (len(inputs) + 5),
+def weights(messages, tangent, local, risk, cumulative, squares):
+    ex = len(messages)
+    return pl.pallas_call(
+        functools.partial(weight_kernel, ex),
+        in_specs=[VMEM] * (ex + 5),
         out_shape=jax.ShapeDtypeStruct(tangent.shape, BF16),
         out_specs=VMEM,
+        scratch_shapes=[pltpu.VMEM((ex,) + messages[0].shape, F32)],
         compiler_params=pltpu.CompilerParams(**PARAMS),
         name="weights",
-    )(*inputs, tangent, local, risk, cumulative, squares)
+    )(*messages, tangent, local, risk, cumulative, squares)
 
 
 def encode(values, message):
@@ -503,21 +495,22 @@
     return jnp.concatenate(parts, axis=0)
 
 
-def gradient_kernel(feat, kf, *refs):
+def gradient_kernel(feat, kf, start, *refs):
     parts, dosages, out, weighted = refs[:feat], refs[feat], refs[feat + 1], refs[feat + 2]
+    width = out.shape[0] - 16
     me = lax.axis_index("feat")
     for i in range(feat):
         weighted[pl.ds(pl.multiple_of((me ^ i) * kf, kf), kf), :] = parts[i][...]
-    total = jnp.dot(weighted[...], dosages[...], preferred_element_type=F32)
+    total = jnp.dot(weighted[...], dosages[:, start : start + width], preferred_element_type=F32)
     encode(total.T, out)
 
 
-def gradients(parts, dosages):
+def gradients(parts, dosages, start, variants):
     feat = len(parts)
     kf, persons = parts[0].shape
-    k, variants = kf * feat, dosages.shape[1]
-    return pl.pallas_call(
-        functools.partial(gradient_kernel, feat, kf),
+    k = kf * feat
+    return pl.pallas_call(
+        functools.partial(gradient_kernel, feat, kf, start),
         in_specs=[VMEM] * (feat + 1),
         out_shape=jax.ShapeDtypeStruct((variants + 16, k), jnp.int16),
         out_specs=VMEM,
@@ -546,11 +539,12 @@
     )(mine, other)
 
 
-def finish_kernel(steps, mine, other, count, out, total, sems):
+def finish_kernel(first, steps, mine, other, count, *refs):
+    out, total, sems = refs[-3:]
     height = mine.shape[0] - 16
     step = height // steps
     block = min(BLOCK, step)
-    scale = count[1:2, 0:1]
+    scale = count[0:1, 0:1]
     powers = [from_short(message[height:]) for message in (mine, other)]
     copies = []
     for i in range(steps):
@@ -558,25 +552,29 @@
             at, j = slice(start, start + block), start // block
             terms = [from_short(m[at]) * jnp.exp2(p[j : j + 1]) for m, p in zip((mine, other), powers)]
             total[at] = (terms[0] + terms[1]) / scale
-        at = pl.ds(i * step, step)
-        copies.append(pltpu.make_async_copy(total.at[at], out.at[at], sems.at[i]))
+        copies.append(
+            pltpu.make_async_copy(
+                total.at[pl.ds(i * step, step)], out.at[pl.ds(first + i * step, step)], sems.at[i]
+            )
+        )
         copies[i].start()
     for copy in copies:
         copy.wait()
 
 
-def finish(mine, other, count):
+def finish(mine, other, count, first, variants, done):
     height, k = mine.shape[0] - 16, mine.shape[1]
-    steps = max(1, min(4, height // BLOCK))
-    return pl.pallas_call(
-        functools.partial(finish_kernel, steps),
-        in_specs=[VMEM] * 3,
-        out_shape=jax.ShapeDtypeStruct((height, k), F32),
+    steps = max(1, min(2, height // BLOCK))
+    return pl.pallas_call(
+        functools.partial(finish_kernel, first, steps),
+        in_specs=[VMEM] * 3 + [HBM] * len(done),
+        out_shape=jax.ShapeDtypeStruct((variants, k), F32),
         out_specs=HBM,
         scratch_shapes=[pltpu.VMEM((height, k), F32), pltpu.SemaphoreType.DMA((steps,))],
+        input_output_aliases={3: 0} if done else {},
         compiler_params=pltpu.CompilerParams(**PARAMS),
         name="finish",
-    )(mine, other, count)
+    )(mine, other, count, *done)
 
 
 def local(dosages, coefficients, directions, event_rank, events):
@@ -591,29 +589,23 @@
     rank, event_row = event_rank[None], events[None]
 
     linear, keep, send = products(dosages, coefficients, directions, feat)
-    received = [swap(piece, "feat", 1) for piece in send]
-    paired, joined = join(linear, keep[1:], received[1:])
-    others = [swap(joined[q - 1], "feat", 2 * q) for q in reversed(range(1, feat // 2))]
+    order = list(reversed(range(1, feat // 2)))
+    received = {q: swap(send[q], "feat", 1) for q in order + [0]}
+    others, paired = [], linear
+    for q in order:
+        *first, message = join(paired, keep[q], received[q])
+        paired = first[0] if first else paired
+        others.append(swap(message, "feat", 2 * q))
     table = tables(rank, paired, rows)
 
-    risk, sums, ordered_events, total = risks(paired, others, rank, event_row, table, rows)
-    later = jnp.zeros_like(total)
-    bit = 1
-    while bit < ex:
-        other = swap(total, "ex", bit)
-        later = later + jnp.where((lax.axis_index("ex") & bit) == 0, other, 0.0)
-        total = total + other
-        bit *= 2
+    risk, sums, ordered_events, message = risks(paired, others, rank, event_row, table, rows)
+    messages = [message] + [swap(message, "ex", i) for i in range(1, ex)]
     tangent, later_sums, plain = suffix_sums(keep[0], received[0], others, risk, rank, table)
-    hazard, ordered_squares, message = shares(later, sums, ordered_events, plain, later_sums)
+    hazard, ordered_squares, message, count = shares(messages, sums, ordered_events, plain, later_sums)
+    messages = [message] + [swap(message, "ex", i) for i in range(1, ex)]
     cumulative, squares = hazards(hazard, ordered_squares, rank, rows)
-    state, bit = [], 1
-    while 2 * bit < ex:
-        message, *state = combine(padded, bit, [message, swap(message, "ex", bit)] + state, cumulative)
-        bit *= 2
-    inputs = [message, swap(message, "ex", bit)] + state
     summed = prefix_sums(later_sums, ordered_squares, rank, padded)
-    own = weights(bit, inputs, tangent, summed, risk, cumulative, squares)
+    own = weights(messages, tangent, summed, risk, cumulative, squares)
 
     chips = {0: own}
     for q in reversed(range(1, feat // 2)):
@@ -622,12 +614,18 @@
     for q in range(feat // 2):
         parts += [chips[q], swap(chips[q], "feat", 1)]
 
-    partial_sum = gradients(parts, dosages)
+    half = variants // 2
+    partial_sums = [gradients(parts, dosages, start, half) for start in (0, half)]
     bit = 1
     while 2 * bit < ex:
-        partial_sum = merge(partial_sum, swap(partial_sum, "ex", bit))
+        received = [swap(message, "ex", bit) for message in partial_sums]
+        partial_sums = [merge(mine, other) for mine, other in zip(partial_sums, received)]
         bit *= 2
-    result = finish(partial_sum, swap(partial_sum, "ex", bit), total)
+    received = [swap(message, "ex", bit) for message in partial_sums]
+    done = []
+    for i in range(2):
+        done = [finish(partial_sums[i], received[i], count, i * half, variants, done)]
+    result = done[0]
     if padded != each:
         result = result.reshape(variants, feat, padded)[:, :, :each].reshape(variants, k)
     return result

time: 62.4 us -> 57.8 us (0.926)
  waiting for transfers between devices: 27.2 us -> 19.9 us
  starting transfers between devices: 21.3 us -> 23.8 us
    ppermute x20 -> x24, waiting for transfers between devices: 27.2 us -> 19.9 us  [swap(): return lax.ppermute(x, axis, [(s, s ^ i) for s in range(count)])]
    ppermute x20 -> x24, starting transfers between devices: 21.3 us -> 23.8 us  [swap(): return lax.ppermute(x, axis, [(s, s ^ i) for s in range(count)])]
    pallas_call x6 -> x9, Pallas kernels: 2.31 us -> 3.52 us  [the longest x2 1.43 us: finish(): pl.pallas_call(functools.partial(finish_kernel, first, steps), in_specs=[...]
    pallas_call x1, Pallas kernels: 1.63 us -> 0.89 us  [hazards(): pl.pallas_call(functools.partial(hazard_kernel, rows), in_specs=[VMEM] *...]
  transfers between devices with their start and end apart: 20 -> 24, of which waited for: 14 -> 12; matrix products, arithmetic and copies ran while one was open for 0% -> 0% of each run, Pallas kernels for 12% -> 15%
where the time goes in v8:
time: 57.8 us; the launch traced here: 57.7 us
  starting transfers between devices  23.8 us (41%)
  waiting for transfers between devices  19.9 us (34%)
  Pallas kernels  13.9 us (24%)
    ppermute x24, starting transfers between devices, swap(): return lax.ppermute(x, axis, [(s, s ^ i) for s in range(count)])  23.8 us
    ppermute x24, waiting for transfers between devices, swap(): return lax.ppermute(x, axis, [(s, s ^ i) for s in range(count)])  19.9 us
    pallas_call x1, Pallas kernels, products(): pl.pallas_call(functools.partial(product_kernel, feat, kf, chunk), in_spe...  3.76 us
    pallas_call x1, Pallas kernels, suffix_sums(): pl.pallas_call(functools.partial(suffix_kernel, len(messages)), in_specs=...  2.24 us
    pallas_call x1, Pallas kernels, prefix_sums(): pl.pallas_call(prefix_kernel, in_specs=[VMEM] * 3, out_shape=jax.ShapeDty...  1.75 us
    pallas_call x2, Pallas kernels, finish(): pl.pallas_call(functools.partial(finish_kernel, first, steps), in_specs=[...  1.43 us
    pallas_call x2, Pallas kernels, gradients(): pl.pallas_call(functools.partial(gradient_kernel, feat, kf, start), in_sp...  1.29 us
  transfers between devices with their start and end apart: 24, of which 12 were waited for; matrix products, arithmetic and copies ran while one was open for 0% of the time, Pallas kernels for 15%

profile of v8, /device:TPU:0, one launch (start us, length us, event | category | flops | bytes accessed | tf_op | source)
XLA Modules:
  0.0 57.7 jit_solution(3273291705619478838)
XLA Ops:
  0.0 3.8 %products.1 = (f32[16,256]{1,0:T(8,128)S(1)}, f32[16,4096]{1,0:T(8,128)S(1)}, f32[16,4096]{1,0:T(8,128)S(1)}, f32[16,4096]{1,0:T(8,128)S(1)}, f32[16,4096]{1,0:T...) custom-call(bf16[512,128]{1,0:T(8,128)(2,1)} %directions.1, ...), custom_call_target="tpu_custom_call" | custom-call | flops 536870912 | bytes 6291456 | tf_op jit(solution)/shard_map/products/pallas_call | solution.py:118
  5.6 3.9 %collective-permute-start.1 = (s16[16,4736]{1,0:T(8,128)(2,1)S(1)}, s16[16,4736]{1,0:T(8,128)(2,1)S(1)}, u32[]{:S(2)}, u32[]{:S(2)}) collective-permute-start(s16[16,4736]{1,0:T(8,128)(2,1)S(1)} %get-tuple-element.33), channel_id=1, source_target_pairs={{0,6},{1,7},{2,4},{3,5},{4,2},{5,3},{6,0},{7,1},{8,14},{9,15},{10,... | collective-permute-start | bytes 454664 | tf_op jit(solution)/shard_map/ppermute | solution.py:23
  11.3 2.5 %collective-permute-done.1.refs_0_ = s16[16,4736]{1,0:T(8,128)(2,1)S(1)} collective-permute-done((s16[16,4736]{1,0:T(8,128)(2,1)S(1)}, s16[16,4736]{1,0:T(8,128)(2,1)S(1)}, u32[]{:S(2)}, u32[]{:S(2)}) %collective-permute-start.1) | collective-permute-done | bytes 151584 | tf_op jit(solution)/shard_map/ppermute | solution.py:23
  13.9 3.1 %collective-permute-done.3.refs_1_ = s16[16,4736]{1,0:T(8,128)(2,1)S(1)} collective-permute-done((s16[16,4736]{1,0:T(8,128)(2,1)S(1)}, s16[16,4736]{1,0:T(8,128)(2,1)S(1)}, u32[]{:S(2)}, u32[]{:S(2)}) %collective-permute-start.3) | collective-permute-done | bytes 151584 | tf_op jit(solution)/shard_map/ppermute | solution.py:23
  17.3 0.9 %risks.1 = (f32[1,4096]{1,0:T(1,128)S(1)}, f32[16,256]{1,0:T(8,128)S(1)}, f32[16,256]{1,0:T(8,128)S(1)}, f32[8,128]{1,0:T(8,128)S(1)}) custom-call(f32[16,256]{1,0:T(8,128)S(1)} %get-tuple-element.32.linear.waited, s16[16,4736]{1,0:T(8,128)(2,1)S(1)} %collective-permute-done.1.refs_0_, s16[16,4736]{1,0:T(8,128)(2,1)S(1)} %collective-permute-done.3.refs_1_, ...), custom_call_target="tpu_custom_call" | custom-call | flops 134217728 | bytes 262144 | tf_op jit(solution)/shard_map/risks/pallas_call | solution.py:249
  18.2 3.7 %collective-permute-start.8 = (f32[8,128]{1,0:T(8,128)S(1)}, f32[8,128]{1,0:T(8,128)S(1)}, u32[]{:S(2)}, u32[]{:S(2)}) collective-permute-start(f32[8,128]{1,0:T(8,128)S(1)} %get-tuple-element.38.refs_0_), channel_id=1, source_target_pairs={{0,24},{8,16},{16,8},{24,0},{1,25},{9,17},{17,9},{25,1},{2,26},{10... | collective-permute-start | bytes 12296 | tf_op jit(solution)/shard_map/ppermute | solution.py:23
  21.9 0.8 %collective-permute-start.6 = (f32[8,128]{1,0:T(8,128)S(1)}, f32[8,128]{1,0:T(8,128)S(1)}, u32[]{:S(2)}, u32[]{:S(2)}) collective-permute-start(f32[8,128]{1,0:T(8,128)S(1)} %get-tuple-element.38.refs_0_), channel_id=1, source_target_pairs={{0,8},{8,0},{16,24},{24,16},{1,9},{9,1},{17,25},{25,17},{2,10},{10... | collective-permute-start | bytes 12296 | tf_op jit(solution)/shard_map/ppermute | solution.py:23
  22.7 2.2 %suffix_sums.1 = (f32[16,4096]{1,0:T(8,128)S(1)}, f32[256,256]{1,0:T(8,128)S(1)}, f32[16,128]{1,0:T(8,128)S(1)}) custom-call(f32[16,4096]{1,0:T(8,128)S(1)} %get-tuple-element.41.own, f32[16,4096]{1,0:T(8,128)S(1)} %collective-permute-done.9.other, s16[16,4736]{1,0:T(8,128)(2,1)S(1)} %collective-permute-done.1.refs_0_, ...), custom_call_target="tpu_custom_call" | custom-call | flops 1073741824 | bytes 1572864 | tf_op jit(solution)/shard_map/suffix_sums/pallas_call | solution.py:380
  24.9 1.5 %collective-permute-done.7.refs_2_ = f32[8,128]{1,0:T(8,128)S(1)} collective-permute-done((f32[8,128]{1,0:T(8,128)S(1)}, f32[8,128]{1,0:T(8,128)S(1)}, u32[]{:S(2)}, u32[]{:S(2)}) %collective-permute-start.7) | collective-permute-done | bytes 4128 | tf_op jit(solution)/shard_map/ppermute | solution.py:23
  26.5 2.2 %collective-permute-start.12 = (f32[40,128]{1,0:T(8,128)S(1)}, f32[40,128]{1,0:T(8,128)S(1)}, u32[]{:S(2)}, u32[]{:S(2)}) collective-permute-start(f32[40,128]{1,0:T(8,128)S(1)} %get-tuple-element.46.refs_0_), channel_id=1, source_target_pairs={{0,24},{8,16},{16,8},{24,0},{1,25},{9,17},{17,9},{25,1},{2,26},{10... | collective-permute-start | bytes 61448 | tf_op jit(solution)/shard_map/ppermute | solution.py:23
  28.7 2.2 %collective-permute-start.10 = (f32[40,128]{1,0:T(8,128)S(1)}, f32[40,128]{1,0:T(8,128)S(1)}, u32[]{:S(2)}, u32[]{:S(2)}) collective-permute-start(f32[40,128]{1,0:T(8,128)S(1)} %get-tuple-element.46.refs_0_), channel_id=1, source_target_pairs={{0,8},{8,0},{16,24},{24,16},{1,9},{9,1},{17,25},{25,17},{2,10},{10... | collective-permute-start | bytes 61448 | tf_op jit(solution)/shard_map/ppermute | solution.py:23
  30.9 1.8 %prefix_sums.1.refs_5_ = f32[16,4096]{1,0:T(8,128)S(1)} custom-call(f32[256,256]{1,0:T(8,128)S(1)} %get-tuple-element.45.refs_7_.sums, f32[16,256]{1,0:T(8,128)S(1)} %get-tuple-element.48.squares.square, s32[1,4096]{1,0:T(1,128)S(1)} %bitcast.5), custom_call_target="tpu_custom_call" | custom-call | flops 1073741824 | bytes 1572864 | tf_op jit(solution)/shard_map/prefix_sums/pallas_call | solution.py:425
  32.7 0.9 %hazards.1 = (f32[1,4096]{1,0:T(1,128)S(1)}, f32[1,4096]{1,0:T(1,128)S(1)}) custom-call(f32[16,256]{1,0:T(8,128)S(1)} %get-tuple-element.49.hazard, f32[16,256]{1,0:T(8,128)S(1)} %get-tuple-element.48.squares.square, s32[1,4096]{1,0:T(1,128)S(1)} %bitcast.6), custom_call_target="tpu_custom_call" | custom-call | flops 209715200 | bytes 262144 | tf_op jit(solution)/shard_map/hazards/pallas_call | solution.py:326
  33.8 1.9 %collective-permute-start.18 = (bf16[16,4096]{1,0:T(8,128)(2,1)S(1)}, bf16[16,4096]{1,0:T(8,128)(2,1)S(1)}, u32[]{:S(2)}, u32[]{:S(2)}) collective-permute-start(bf16[16,4096]{1,0:T(8,128)(2,1)S(1)} %weights.1.refs_0_), channel_id=1, source_target_pairs={{0,6},{1,7},{2,4},{3,5},{4,2},{5,3},{6,0},{7,1},{8,14},{9,15},{10,... | collective-permute-start | bytes 393224 | tf_op jit(solution)/shard_map/ppermute | solution.py:23
  35.8 1.1 %collective-permute-start.16 = (bf16[16,4096]{1,0:T(8,128)(2,1)S(1)}, bf16[16,4096]{1,0:T(8,128)(2,1)S(1)}, u32[]{:S(2)}, u32[]{:S(2)}) collective-permute-start(bf16[16,4096]{1,0:T(8,128)(2,1)S(1)} %weights.1.refs_0_), channel_id=1, source_target_pairs={{0,4},{1,5},{2,6},{3,7},{4,0},{5,1},{6,2},{7,3},{8,12},{9,13},{10,... | collective-permute-start | bytes 393224 | tf_op jit(solution)/shard_map/ppermute | solution.py:23
  37.4 2.4 %collective-permute-done.18.refs_6_ = bf16[16,4096]{1,0:T(8,128)(2,1)S(1)} collective-permute-done((bf16[16,4096]{1,0:T(8,128)(2,1)S(1)}, bf16[16,4096]{1,0:T(8,128)(2,1)S(1)}, u32[]{:S(2)}, u32[]{:S(2)}) %collective-permute-start.18) | collective-permute-done | bytes 131104 | tf_op jit(solution)/shard_map/ppermute | solution.py:23
  39.8 1.4 %collective-permute-done.16.refs_4_ = bf16[16,4096]{1,0:T(8,128)(2,1)S(1)} collective-permute-done((bf16[16,4096]{1,0:T(8,128)(2,1)S(1)}, bf16[16,4096]{1,0:T(8,128)(2,1)S(1)}, u32[]{:S(2)}, u32[]{:S(2)}) %collective-permute-start.16) | collective-permute-done | bytes 131104 | tf_op jit(solution)/shard_map/ppermute | solution.py:23
  43.8 1.1 %collective-permute-start.22 = (s16[272,128]{1,0:T(8,128)(2,1)S(1)}, s16[272,128]{1,0:T(8,128)(2,1)S(1)}, u32[]{:S(2)}, u32[]{:S(2)}) collective-permute-start(s16[272,128]{1,0:T(8,128)(2,1)S(1)} %gradients.3.mine), channel_id=1, source_target_pairs={{0,8},{8,0},{16,24},{24,16},{1,9},{9,1},{17,25},{25,17},{2,10},{10... | collective-permute-start | bytes 208904 | tf_op jit(solution)/shard_map/ppermute | solution.py:23
  45.6 1.0 %collective-permute-start.20 = (s16[272,128]{1,0:T(8,128)(2,1)S(1)}, s16[272,128]{1,0:T(8,128)(2,1)S(1)}, u32[]{:S(2)}, u32[]{:S(2)}) collective-permute-start(s16[272,128]{1,0:T(8,128)(2,1)S(1)} %gradients.2.mine), channel_id=1, source_target_pairs={{0,8},{8,0},{16,24},{24,16},{1,9},{9,1},{17,25},{25,17},{2,10},{10... | collective-permute-start | bytes 208904 | tf_op jit(solution)/shard_map/ppermute | solution.py:23
  46.6 1.6 %collective-permute-done.22.other = s16[272,128]{1,0:T(8,128)(2,1)S(1)} collective-permute-done((s16[272,128]{1,0:T(8,128)(2,1)S(1)}, s16[272,128]{1,0:T(8,128)(2,1)S(1)}, u32[]{:S(2)}, u32[]{:S(2)}) %collective-permute-start.22) | collective-permute-done | bytes 69664 | tf_op jit(solution)/shard_map/ppermute | solution.py:23
  48.3 2.0 %collective-permute-start.23 = (s16[272,128]{1,0:T(8,128)(2,1)S(1)}, s16[272,128]{1,0:T(8,128)(2,1)S(1)}, u32[]{:S(2)}, u32[]{:S(2)}) collective-permute-start(s16[272,128]{1,0:T(8,128)(2,1)S(1)} %merge.3.mine), channel_id=1, source_target_pairs={{0,16},{8,24},{16,0},{24,8},{1,17},{9,25},{17,1},{25,9},{2,18},{10... | collective-permute-start | bytes 208904 | tf_op jit(solution)/shard_map/ppermute | solution.py:23
  50.4 1.3 %collective-permute-start.21 = (s16[272,128]{1,0:T(8,128)(2,1)S(1)}, s16[272,128]{1,0:T(8,128)(2,1)S(1)}, u32[]{:S(2)}, u32[]{:S(2)}) collective-permute-start(s16[272,128]{1,0:T(8,128)(2,1)S(1)} %merge.2.mine), channel_id=1, source_target_pairs={{0,16},{8,24},{16,0},{24,8},{1,17},{9,25},{17,1},{25,9},{2,18},{10... | collective-permute-start | bytes 208904 | tf_op jit(solution)/shard_map/ppermute | solution.py:23
  51.8 4.4 %collective-permute-done.23.other = s16[272,128]{1,0:T(8,128)(2,1)S(1)} collective-permute-done((s16[272,128]{1,0:T(8,128)(2,1)S(1)}, s16[272,128]{1,0:T(8,128)(2,1)S(1)}, u32[]{:S(2)}, u32[]{:S(2)}) %collective-permute-start.23) | collective-permute-done | bytes 69664 | tf_op jit(solution)/shard_map/ppermute | solution.py:23
  56.2 0.7 %finish.2.refs_0_ = f32[512,128]{1,0:T(8,128)} custom-call(s16[272,128]{1,0:T(8,128)(2,1)S(1)} %merge.3.mine, s16[272,128]{1,0:T(8,128)(2,1)S(1)} %collective-permute-done.23.other, f32[8,128]{1,0:T(8,128)S(1)} %get-tuple-element.52.count), custom_call_target="tpu_custom_call" | custom-call | tf_op jit(solution)/shard_map/finish/pallas_call | solution.py:568
  (47 shorter events, 9.0 us)
Async XLA Ops:
  3.8 1.7 %collective-permute-start = (f32[16,4352]{1,0:T(8,128)S(1)}, f32[16,4352]{1,0:T(8,128)S(1)}, u32[]{:S(2)}, u32[]{:S(2)}) collective-permute-start(f32[16,4352]{1,0:T(8,128)S(1)} %get-tuple-element.31), channel_id=1, source_target_pairs={{0,1},{1,0},{2,3},{3,2},{4,5},{5,4},{6,7},{7,6},{8,9},{9,8},{10,11... | collective-permute-start | bytes 835592 | tf_op jit(solution)/shard_map/ppermute | solution.py:23
  4.3 5.2 %collective-permute-start.2 = (f32[16,4096]{1,0:T(8,128)S(1)}, f32[16,4096]{1,0:T(8,128)S(1)}, u32[]{:S(2)}, u32[]{:S(2)}) collective-permute-start(f32[16,4096]{1,0:T(8,128)S(1)} %get-tuple-element.35), channel_id=1, source_target_pairs={{0,1},{1,0},{2,3},{3,2},{4,5},{5,4},{6,7},{7,6},{8,9},{9,8},{10,11... | collective-permute-start | bytes 786440 | tf_op jit(solution)/shard_map/ppermute | solution.py:23
  4.4 5.9 %collective-permute-start.4 = (f32[16,4096]{1,0:T(8,128)S(1)}, f32[16,4096]{1,0:T(8,128)S(1)}, u32[]{:S(2)}, u32[]{:S(2)}) collective-permute-start(f32[16,4096]{1,0:T(8,128)S(1)} %get-tuple-element.37), channel_id=1, source_target_pairs={{0,1},{1,0},{2,3},{3,2},{4,5},{5,4},{6,7},{7,6},{8,9},{9,8},{10,11... | collective-permute-start | bytes 786440 | tf_op jit(solution)/shard_map/ppermute | solution.py:23
  4.8 17.9 %collective-permute-start.9 = (f32[16,4096]{1,0:T(8,128)S(1)}, f32[16,4096]{1,0:T(8,128)S(1)}, u32[]{:S(2)}, u32[]{:S(2)}) collective-permute-start(f32[16,4096]{1,0:T(8,128)S(1)} %get-tuple-element.42), channel_id=1, source_target_pairs={{0,1},{1,0},{2,3},{3,2},{4,5},{5,4},{6,7},{7,6},{8,9},{9,8},{10,11... | collective-permute-start | bytes 786440 | tf_op jit(solution)/shard_map/ppermute | solution.py:23
  5.6 8.2 %collective-permute-start.1 = (s16[16,4736]{1,0:T(8,128)(2,1)S(1)}, s16[16,4736]{1,0:T(8,128)(2,1)S(1)}, u32[]{:S(2)}, u32[]{:S(2)}) collective-permute-start(s16[16,4736]{1,0:T(8,128)(2,1)S(1)} %get-tuple-element.33), channel_id=1, source_target_pairs={{0,6},{1,7},{2,4},{3,5},{4,2},{5,3},{6,0},{7,1},{8,14},{9,15},{10,... | collective-permute-start | bytes 454664 | tf_op jit(solution)/shard_map/ppermute | solution.py:23
  9.7 7.3 %collective-permute-start.3 = (s16[16,4736]{1,0:T(8,128)(2,1)S(1)}, s16[16,4736]{1,0:T(8,128)(2,1)S(1)}, u32[]{:S(2)}, u32[]{:S(2)}) collective-permute-start(s16[16,4736]{1,0:T(8,128)(2,1)S(1)} %join.4), channel_id=1, source_target_pairs={{0,4},{1,5},{2,6},{3,7},{4,0},{5,1},{6,2},{7,3},{8,12},{9,13},{10,... | collective-permute-start | bytes 454664 | tf_op jit(solution)/shard_map/ppermute | solution.py:23
  10.4 6.9 %collective-permute-start.5 = (s16[16,4736]{1,0:T(8,128)(2,1)S(1)}, s16[16,4736]{1,0:T(8,128)(2,1)S(1)}, u32[]{:S(2)}, u32[]{:S(2)}) collective-permute-start(s16[16,4736]{1,0:T(8,128)(2,1)S(1)} %join.5), channel_id=1, source_target_pairs={{0,2},{1,3},{2,0},{3,1},{4,6},{5,7},{6,4},{7,5},{8,10},{9,11},{10,... | collective-permute-start | bytes 454664 | tf_op jit(solution)/shard_map/ppermute | solution.py:23
  18.2 6.7 %collective-permute-start.8 = (f32[8,128]{1,0:T(8,128)S(1)}, f32[8,128]{1,0:T(8,128)S(1)}, u32[]{:S(2)}, u32[]{:S(2)}) collective-permute-start(f32[8,128]{1,0:T(8,128)S(1)} %get-tuple-element.38.refs_0_), channel_id=1, source_target_pairs={{0,24},{8,16},{16,8},{24,0},{1,25},{9,17},{17,9},{25,1},{2,26},{10... | collective-permute-start | bytes 12296 | tf_op jit(solution)/shard_map/ppermute | solution.py:23
  21.9 4.5 %collective-permute-start.7 = (f32[8,128]{1,0:T(8,128)S(1)}, f32[8,128]{1,0:T(8,128)S(1)}, u32[]{:S(2)}, u32[]{:S(2)}) collective-permute-start(f32[8,128]{1,0:T(8,128)S(1)} %get-tuple-element.38.refs_0_), channel_id=1, source_target_pairs={{0,16},{8,24},{16,0},{24,8},{1,17},{9,25},{17,1},{25,9},{2,18},{10... | collective-permute-start | bytes 12296 | tf_op jit(solution)/shard_map/ppermute | solution.py:23
  21.9 4.5 %collective-permute-start.6 = (f32[8,128]{1,0:T(8,128)S(1)}, f32[8,128]{1,0:T(8,128)S(1)}, u32[]{:S(2)}, u32[]{:S(2)}) collective-permute-start(f32[8,128]{1,0:T(8,128)S(1)} %get-tuple-element.38.refs_0_), channel_id=1, source_target_pairs={{0,8},{8,0},{16,24},{24,16},{1,9},{9,1},{17,25},{25,17},{2,10},{10... | collective-permute-start | bytes 12296 | tf_op jit(solution)/shard_map/ppermute | solution.py:23
  26.5 7.1 %collective-permute-start.12 = (f32[40,128]{1,0:T(8,128)S(1)}, f32[40,128]{1,0:T(8,128)S(1)}, u32[]{:S(2)}, u32[]{:S(2)}) collective-permute-start(f32[40,128]{1,0:T(8,128)S(1)} %get-tuple-element.46.refs_0_), channel_id=1, source_target_pairs={{0,24},{8,16},{16,8},{24,0},{1,25},{9,17},{17,9},{25,1},{2,26},{10... | collective-permute-start | bytes 61448 | tf_op jit(solution)/shard_map/ppermute | solution.py:23
  28.7 4.9 %collective-permute-start.11 = (f32[40,128]{1,0:T(8,128)S(1)}, f32[40,128]{1,0:T(8,128)S(1)}, u32[]{:S(2)}, u32[]{:S(2)}) collective-permute-start(f32[40,128]{1,0:T(8,128)S(1)} %get-tuple-element.46.refs_0_), channel_id=1, source_target_pairs={{0,16},{8,24},{16,0},{24,8},{1,17},{9,25},{17,1},{25,9},{2,18},{10... | collective-permute-start | bytes 61448 | tf_op jit(solution)/shard_map/ppermute | solution.py:23
  28.7 4.9 %collective-permute-start.10 = (f32[40,128]{1,0:T(8,128)S(1)}, f32[40,128]{1,0:T(8,128)S(1)}, u32[]{:S(2)}, u32[]{:S(2)}) collective-permute-start(f32[40,128]{1,0:T(8,128)S(1)} %get-tuple-element.46.refs_0_), channel_id=1, source_target_pairs={{0,8},{8,0},{16,24},{24,16},{1,9},{9,1},{17,25},{25,17},{2,10},{10... | collective-permute-start | bytes 61448 | tf_op jit(solution)/shard_map/ppermute | solution.py:23
  33.8 6.0 %collective-permute-start.18 = (bf16[16,4096]{1,0:T(8,128)(2,1)S(1)}, bf16[16,4096]{1,0:T(8,128)(2,1)S(1)}, u32[]{:S(2)}, u32[]{:S(2)}) collective-permute-start(bf16[16,4096]{1,0:T(8,128)(2,1)S(1)} %weights.1.refs_0_), channel_id=1, source_target_pairs={{0,6},{1,7},{2,4},{3,5},{4,2},{5,3},{6,0},{7,1},{8,14},{9,15},{10,... | collective-permute-start | bytes 393224 | tf_op jit(solution)/shard_map/ppermute | solution.py:23
  35.8 5.4 %collective-permute-start.16 = (bf16[16,4096]{1,0:T(8,128)(2,1)S(1)}, bf16[16,4096]{1,0:T(8,128)(2,1)S(1)}, u32[]{:S(2)}, u32[]{:S(2)}) collective-permute-start(bf16[16,4096]{1,0:T(8,128)(2,1)S(1)} %weights.1.refs_0_), channel_id=1, source_target_pairs={{0,4},{1,5},{2,6},{3,7},{4,0},{5,1},{6,2},{7,3},{8,12},{9,13},{10,... | collective-permute-start | bytes 393224 | tf_op jit(solution)/shard_map/ppermute | solution.py:23
  36.9 5.0 %collective-permute-start.14 = (bf16[16,4096]{1,0:T(8,128)(2,1)S(1)}, bf16[16,4096]{1,0:T(8,128)(2,1)S(1)}, u32[]{:S(2)}, u32[]{:S(2)}) collective-permute-start(bf16[16,4096]{1,0:T(8,128)(2,1)S(1)} %weights.1.refs_0_), channel_id=1, source_target_pairs={{0,2},{1,3},{2,0},{3,1},{4,6},{5,7},{6,4},{7,5},{8,10},{9,11},{10,... | collective-permute-start | bytes 393224 | tf_op jit(solution)/shard_map/ppermute | solution.py:23
  37.4 4.4 %collective-permute-start.13 = (bf16[16,4096]{1,0:T(8,128)(2,1)S(1)}, bf16[16,4096]{1,0:T(8,128)(2,1)S(1)}, u32[]{:S(2)}, u32[]{:S(2)}) collective-permute-start(bf16[16,4096]{1,0:T(8,128)(2,1)S(1)} %weights.1.refs_0_), channel_id=1, source_target_pairs={{0,1},{1,0},{2,3},{3,2},{4,5},{5,4},{6,7},{7,6},{8,9},{9,8},{10,11... | collective-permute-start | bytes 393224 | tf_op jit(solution)/shard_map/ppermute | solution.py:23
  39.8 2.0 %collective-permute-start.19 = (bf16[16,4096]{1,0:T(8,128)(2,1)S(1)}, bf16[16,4096]{1,0:T(8,128)(2,1)S(1)}, u32[]{:S(2)}, u32[]{:S(2)}) collective-permute-start(bf16[16,4096]{1,0:T(8,128)(2,1)S(1)} %collective-permute-done.18.refs_6_), channel_id=1, source_target_pairs={{0,1},{1,0},{2,3},{3,2},{4,5},{5,4},{6,7},{7,6},{8,9},{9,8},{10,11... | collective-permute-start | bytes 393224 | tf_op jit(solution)/shard_map/ppermute | solution.py:23
  41.2 1.3 %collective-permute-start.17 = (bf16[16,4096]{1,0:T(8,128)(2,1)S(1)}, bf16[16,4096]{1,0:T(8,128)(2,1)S(1)}, u32[]{:S(2)}, u32[]{:S(2)}) collective-permute-start(bf16[16,4096]{1,0:T(8,128)(2,1)S(1)} %collective-permute-done.16.refs_4_), channel_id=1, source_target_pairs={{0,1},{1,0},{2,3},{3,2},{4,5},{5,4},{6,7},{7,6},{8,9},{9,8},{10,11... | collective-permute-start | bytes 393224 | tf_op jit(solution)/shard_map/ppermute | solution.py:23
  41.8 1.3 %collective-permute-start.15 = (bf16[16,4096]{1,0:T(8,128)(2,1)S(1)}, bf16[16,4096]{1,0:T(8,128)(2,1)S(1)}, u32[]{:S(2)}, u32[]{:S(2)}) collective-permute-start(bf16[16,4096]{1,0:T(8,128)(2,1)S(1)} %collective-permute-done.14.refs_2_), channel_id=1, source_target_pairs={{0,1},{1,0},{2,3},{3,2},{4,5},{5,4},{6,7},{7,6},{8,9},{9,8},{10,11... | collective-permute-start | bytes 393224 | tf_op jit(solution)/shard_map/ppermute | solution.py:23
  43.8 4.5 %collective-permute-start.22 = (s16[272,128]{1,0:T(8,128)(2,1)S(1)}, s16[272,128]{1,0:T(8,128)(2,1)S(1)}, u32[]{:S(2)}, u32[]{:S(2)}) collective-permute-start(s16[272,128]{1,0:T(8,128)(2,1)S(1)} %gradients.3.mine), channel_id=1, source_target_pairs={{0,8},{8,0},{16,24},{24,16},{1,9},{9,1},{17,25},{25,17},{2,10},{10... | collective-permute-start | bytes 208904 | tf_op jit(solution)/shard_map/ppermute | solution.py:23
  45.6 4.7 %collective-permute-start.20 = (s16[272,128]{1,0:T(8,128)(2,1)S(1)}, s16[272,128]{1,0:T(8,128)(2,1)S(1)}, u32[]{:S(2)}, u32[]{:S(2)}) collective-permute-start(s16[272,128]{1,0:T(8,128)(2,1)S(1)} %gradients.2.mine), channel_id=1, source_target_pairs={{0,8},{8,0},{16,24},{24,16},{1,9},{9,1},{17,25},{25,17},{2,10},{10... | collective-permute-start | bytes 208904 | tf_op jit(solution)/shard_map/ppermute | solution.py:23
  48.3 7.9 %collective-permute-start.23 = (s16[272,128]{1,0:T(8,128)(2,1)S(1)}, s16[272,128]{1,0:T(8,128)(2,1)S(1)}, u32[]{:S(2)}, u32[]{:S(2)}) collective-permute-start(s16[272,128]{1,0:T(8,128)(2,1)S(1)} %merge.3.mine), channel_id=1, source_target_pairs={{0,16},{8,24},{16,0},{24,8},{1,17},{9,25},{17,1},{25,9},{2,18},{10... | collective-permute-start | bytes 208904 | tf_op jit(solution)/shard_map/ppermute | solution.py:23
  50.4 6.5 %collective-permute-start.21 = (s16[272,128]{1,0:T(8,128)(2,1)S(1)}, s16[272,128]{1,0:T(8,128)(2,1)S(1)}, u32[]{:S(2)}, u32[]{:S(2)}) collective-permute-start(s16[272,128]{1,0:T(8,128)(2,1)S(1)} %merge.2.mine), channel_id=1, source_target_pairs={{0,16},{8,24},{16,0},{24,8},{1,17},{9,25},{17,1},{25,9},{2,18},{10... | collective-permute-start | bytes 208904 | tf_op jit(solution)/shard_map/ppermute | solution.py:23
  (3 other events, 48.5 us)

commit v9 on v8

--- a/solution.py
+++ b/solution.py
@@ -11,7 +11,6 @@
 BF16 = jnp.bfloat16
 LO = 256
 NT = (((1,), (1,)), ((), ()))
-BLOCK = 64
 SPAN = 512
 VMEM = pl.BlockSpec(memory_space=pltpu.VMEM)
 HBM = pl.BlockSpec(memory_space=pltpu.HBM)
@@ -151,45 +150,46 @@
     return values.astype(jnp.int32).astype(F32)
 
 
-def join_kernel(linear, *refs):
-    mine, other = refs[:2]
+def pair_kernel(linear, received, out):
+    out[...] = linear[...] + received[:, received.shape[1] - LO :]
+
+
+def pair(linear, received):
+    return pl.pallas_call(
+        pair_kernel,
+        in_specs=[VMEM] * 2,
+        out_shape=jax.ShapeDtypeStruct(linear.shape, F32),
+        out_specs=VMEM,
+        compiler_params=pltpu.CompilerParams(**PARAMS),
+        name="pair",
+    )(linear, received)
+
+
+def join_kernel(mine, other, *refs):
     out = refs[-1]
     kf, rows = mine.shape
     span = min(SPAN, rows)
     lane = lax.broadcasted_iota(jnp.int32, (kf, 128), 1)
-    paired = linear[...]
-    if len(refs) > 3:
-        paired = paired + other[:, rows:]
-        refs[2][...] = paired
-    linear_power = power_of(jnp.max(jnp.abs(paired), axis=1, keepdims=True))
-    scaled = paired * jnp.exp2(-linear_power)
-    whole = jnp.round(scaled)
-    powers = jnp.where(lane == rows // span, linear_power, 0.0)
+    powers = jnp.zeros((kf, 128), F32)
     for i in range(rows // span):
         at = slice(i * span, (i + 1) * span)
         total = mine[:, at] + other[:, at]
         power = power_of(jnp.max(jnp.abs(total), axis=1, keepdims=True))
         out[:, at] = to_short(total * jnp.exp2(-power))
         powers = jnp.where(lane == i, power, powers)
-    out[:, rows : rows + LO] = to_short(whole)
-    out[:, rows + LO : rows + 2 * LO] = to_short((scaled - whole) * 32768.0)
-    out[:, rows + 2 * LO :] = to_short(powers)
-
-
-def join(linear, keep, received):
+    out[:, rows:] = to_short(powers)
+
+
+def join(keep, received, waited):
     kf, rows = keep.shape
-    message = jax.ShapeDtypeStruct((kf, rows + 2 * LO + 128), jnp.int16)
-    shapes = [message]
-    if received.shape[1] > rows:
-        shapes = [jax.ShapeDtypeStruct(linear.shape, F32), message]
     return pl.pallas_call(
         join_kernel,
-        in_specs=[VMEM] * 3,
-        out_shape=shapes,
-        out_specs=[VMEM] * len(shapes),
+        in_specs=[VMEM] * 2 + [pl.BlockSpec(memory_space=pl.ANY)] * len(waited),
+        out_shape=jax.ShapeDtypeStruct((kf, rows + 128), jnp.int16),
+        out_specs=VMEM,
         compiler_params=pltpu.CompilerParams(**PARAMS),
         name="join",
-    )(linear, keep, received)
+    )(keep, received, *waited)
 
 
 def table_kernel(rows, rank, waited, table):
@@ -215,16 +215,13 @@
     )(rank, waited)
 
 
-def risk_kernel(rows, parts, linear, *refs):
-    messages, (rank, events, table) = refs[:parts], refs[parts : parts + 3]
-    risk_out, sums_out, events_out, message = refs[parts + 3 :]
+def risk_kernel(rows, parts, *refs):
+    linear, (rank, events, table) = refs[:parts], refs[parts : parts + 3]
+    risk_out, sums_out, events_out, message = refs[-4:]
     groups = rows // LO
-    span = min(SPAN, rows)
-    total = linear[...]
-    for part in messages:
-        power = from_short(part[:, rows + 2 * LO :])[:, rows // span : rows // span + 1]
-        high, low = from_short(part[:, rows : rows + LO]), from_short(part[:, rows + LO : rows + 2 * LO])
-        total = total + (high + low * (1.0 / 32768.0)) * jnp.exp2(power)
+    total = linear[0][...]
+    for part in linear[1:]:
+        total = total + part[...]
     risk = jnp.exp(total)
     for g in range(groups):
         risk_out[:, g * LO : (g + 1) * LO] = risk[g : g + 1]
@@ -244,11 +241,11 @@
     message[...] = jnp.concatenate([everything, count, jnp.zeros((6, 128), F32)], axis=0)
 
 
-def risks(linear, messages, rank, events, table, rows):
+def risks(linear, rank, events, table, rows, waited):
     groups = rows // LO
     return pl.pallas_call(
-        functools.partial(risk_kernel, rows, len(messages)),
-        in_specs=[VMEM] * (len(messages) + 4),
+        functools.partial(risk_kernel, rows, len(linear)),
+        in_specs=[VMEM] * (len(linear) + 3) + [pl.BlockSpec(memory_space=pl.ANY)] * len(waited),
         out_shape=[
             jax.ShapeDtypeStruct((1, rows), F32),
             jax.ShapeDtypeStruct((groups, LO), F32),
@@ -259,22 +256,13 @@
         compiler_params=pltpu.CompilerParams(**PARAMS),
         cost_estimate=pl.CostEstimate(flops=rows * LO * 128, bytes_accessed=rows * 64, transcendentals=rows),
         name="risks",
-    )(linear, *messages, rank, events, table)
-
-
-def share_kernel(ex, *refs):
-    messages, (sums, events, plain, ordered) = refs[:ex], refs[ex : ex + 4]
-    hazard_out, squares, message, count_out = refs[ex + 4 :]
+    )(*linear, rank, events, table, *waited)
+
+
+def share_kernel(later, sums, events, plain, ordered, hazard_out, squares, message):
     kf = plain.shape[0]
     groups = sums.shape[0]
-    me = lax.axis_index("ex")
-    later = jnp.zeros((1, 1), F32)
-    count = messages[0][1:2]
-    for i in range(1, ex):
-        later = later + jnp.where((me ^ i) > me, messages[i][0:1, 0:1], 0.0)
-        count = count + messages[i][1:2]
-    count_out[...] = jnp.broadcast_to(count, count_out.shape)
-    risk_sum = sums[...] + later
+    risk_sum = sums[...] + later[0:1, 0:1]
     hazard = events[...] / risk_sum
     square = events[...] / (risk_sum * risk_sum)
     hazard_out[...] = hazard
@@ -289,21 +277,16 @@
     message[2 * kf :] = jnp.concatenate(rows + [jnp.zeros((6, 128), F32)], axis=0)
 
 
-def shares(messages, sums, events, plain, ordered):
+def shares(later, sums, events, plain, ordered):
     flat = jax.ShapeDtypeStruct(sums.shape, F32)
     return pl.pallas_call(
-        functools.partial(share_kernel, len(messages)),
-        in_specs=[VMEM] * (len(messages) + 4),
-        out_shape=[
-            flat,
-            flat,
-            jax.ShapeDtypeStruct((2 * plain.shape[0] + 8, 128), F32),
-            jax.ShapeDtypeStruct((8, 128), F32),
-        ],
-        out_specs=[VMEM] * 4,
+        share_kernel,
+        in_specs=[VMEM] * 5,
+        out_shape=[flat, flat, jax.ShapeDtypeStruct((2 * plain.shape[0] + 8, 128), F32)],
+        out_specs=[VMEM] * 3,
         compiler_params=pltpu.CompilerParams(**PARAMS),
         name="shares",
-    )(*messages, sums, events, plain, ordered)
+    )(later, sums, events, plain, ordered)
 
 
 def hazard_kernel(rows, hazard, square, rank, cumulative, squares):
@@ -334,6 +317,25 @@
     )(hazard, square, rank)
 
 
+def range_kernel(bit, count, *refs):
+    total, other, later = refs[:3]
+    total_out, later_out = refs[3 + count :]
+    is_later = (lax.axis_index("ex") & bit) == 0
+    later_out[...] = later[...] + jnp.where(is_later, other[...], 0.0)
+    total_out[...] = total[...] + other[...]
+
+
+def ranges(bit, total, other, later, waited):
+    return pl.pallas_call(
+        functools.partial(range_kernel, bit, len(waited)),
+        in_specs=[VMEM] * 3 + [pl.BlockSpec(memory_space=pl.ANY)] * len(waited),
+        out_shape=[jax.ShapeDtypeStruct(total.shape, F32)] * 2,
+        out_specs=[VMEM] * 2,
+        compiler_params=pltpu.CompilerParams(**PARAMS),
+        name="ranges",
+    )(total, other, later, *waited)
+
+
 def suffix_kernel(parts, own, other, *refs):
     messages, (risk, rank, table) = refs[:parts], refs[parts : parts + 3]
     tangent_out, sums, plain, lhs = refs[parts + 3 :]
@@ -341,7 +343,7 @@
     folded = jnp.zeros((kf, 128), F32)
     groups = rows // LO
     span = min(SPAN, rows)
-    powers = [jnp.exp2(from_short(part[:, rows + 2 * LO :])) for part in messages]
+    powers = [jnp.exp2(from_short(part[:, rows:])) for part in messages]
     for i in range(rows // span):
         at = slice(i * span, (i + 1) * span)
         tangent = own[:, at] + other[:, at]
@@ -471,48 +473,50 @@
     )(*messages, tangent, local, risk, cumulative, squares)
 
 
+def tiles_of(height, width):
+    return [
+        (slice(row, row + 16), slice(column, column + 128))
+        for row in range(0, height, 16)
+        for column in range(0, width, 128)
+    ]
+
+
 def encode(values, message):
-    height = values.shape[0]
-    block = min(BLOCK, height)
-    powers = []
-    for start in range(0, height, block):
-        part = values[start : start + block]
-        largest = jnp.max(jnp.abs(part), axis=0, keepdims=True)
-        power = power_of(largest)
-        message[start : start + block] = to_short(part * jnp.exp2(-power))
-        powers.append(power)
-    powers.append(jnp.zeros((message.shape[0] - height - len(powers), values.shape[1]), F32))
-    message[height:] = to_short(jnp.concatenate(powers, axis=0))
-
-
-def decode(message, height):
-    block = min(BLOCK, height)
-    powers = from_short(message[height:])
-    parts = []
-    for i in range(height // block):
-        part = from_short(message[i * block : (i + 1) * block])
-        parts.append(part * jnp.exp2(powers[i : i + 1]))
-    return jnp.concatenate(parts, axis=0)
-
-
-def gradient_kernel(feat, kf, start, *refs):
-    parts, dosages, out, weighted = refs[:feat], refs[feat], refs[feat + 1], refs[feat + 2]
-    width = out.shape[0] - 16
-    me = lax.axis_index("feat")
-    for i in range(feat):
-        weighted[pl.ds(pl.multiple_of((me ^ i) * kf, kf), kf), :] = parts[i][...]
-    total = jnp.dot(weighted[...], dosages[:, start : start + width], preferred_element_type=F32)
-    encode(total.T, out)
-
-
-def gradients(parts, dosages, start, variants):
-    feat = len(parts)
-    kf, persons = parts[0].shape
-    k = kf * feat
-    return pl.pallas_call(
-        functools.partial(gradient_kernel, feat, kf, start),
-        in_specs=[VMEM] * (feat + 1),
-        out_shape=jax.ShapeDtypeStruct((variants + 16, k), jnp.int16),
+    lane = lax.broadcasted_iota(jnp.int32, (16, 128), 1)
+    powers = jnp.zeros((16, 128), F32)
+    for i, value in enumerate(values):
+        power = power_of(jnp.max(jnp.abs(value), axis=1, keepdims=True))
+        message[i] = to_short(value * jnp.exp2(-power))
+        powers = jnp.where(lane == i, power, powers)
+    message[message.shape[0] - 1] = to_short(powers)
+
+
+def decode(message):
+    last = message.shape[0] - 1
+    scales = jnp.exp2(from_short(message[last]))
+    return [from_short(message[i]) * scales[:, i : i + 1] for i in range(last)]
+
+
+def decode_sum(mine, other):
+    return [one + two for one, two in zip(decode(mine), decode(other))]
+
+
+def gradient_kernel(parts, kf, *refs):
+    pieces, dosages, out, weighted = refs[:parts], refs[parts], refs[parts + 1], refs[parts + 2]
+    for i in range(parts):
+        weighted[i * kf : (i + 1) * kf, :] = pieces[i][...]
+    total = jnp.dot(weighted[...], dosages[...], preferred_element_type=F32)
+    encode([total[at] for at in tiles_of(*total.shape)], out)
+
+
+def gradients(pieces, dosages):
+    parts = len(pieces)
+    kf, persons = pieces[0].shape
+    k, variants = kf * parts, dosages.shape[1]
+    return pl.pallas_call(
+        functools.partial(gradient_kernel, parts, kf),
+        in_specs=[VMEM] * (parts + 1),
+        out_shape=jax.ShapeDtypeStruct((k * variants // 2048 + 1, 16, 128), jnp.int16),
         out_specs=VMEM,
         scratch_shapes=[pltpu.VMEM((k, persons), BF16)],
         compiler_params=pltpu.CompilerParams(**PARAMS),
@@ -520,12 +524,11 @@
             flops=2 * persons * variants * k, bytes_accessed=persons * (variants * 2 + k * 2), transcendentals=0
         ),
         name="gradients",
-    )(*parts, dosages)
+    )(*pieces, dosages)
 
 
 def merge_kernel(mine, other, out):
-    height = mine.shape[0] - 16
-    encode(decode(mine, height) + decode(other, height), out)
+    encode(decode_sum(mine, other), out)
 
 
 def merge(mine, other):
@@ -539,22 +542,38 @@
     )(mine, other)
 
 
-def finish_kernel(first, steps, mine, other, count, *refs):
-    out, total, sems = refs[-3:]
-    height = mine.shape[0] - 16
-    step = height // steps
-    block = min(BLOCK, step)
-    scale = count[0:1, 0:1]
-    powers = [from_short(message[height:]) for message in (mine, other)]
+def add_kernel(mine, other, out):
+    for at, value in zip(tiles_of(*out.shape), decode_sum(mine, other)):
+        out[at] = value
+
+
+def add(mine, other, variants):
+    return pl.pallas_call(
+        add_kernel,
+        in_specs=[VMEM] * 2,
+        out_shape=jax.ShapeDtypeStruct(((mine.shape[0] - 1) * 2048 // variants, variants), F32),
+        out_specs=VMEM,
+        compiler_params=pltpu.CompilerParams(**PARAMS),
+        name="add",
+    )(mine, other)
+
+
+def finish_kernel(feat, kf, first, mine, other, count, out, placed, total, sems):
+    me = lax.axis_index("feat")
+    variants = out.shape[0]
+    scale = count[1:2, 0:1]
+    for q in range(feat // 2):
+        placed[me ^ (2 * q)] = first[q * kf : (q + 1) * kf]
+    for (rows, columns), value in zip(tiles_of(feat // 2 * kf, variants), decode_sum(mine, other)):
+        q, row = divmod(rows.start, kf)
+        placed[me ^ (2 * q + 1), row : row + 16, columns] = value
     copies = []
-    for i in range(steps):
-        for start in range(i * step, (i + 1) * step, block):
-            at, j = slice(start, start + block), start // block
-            terms = [from_short(m[at]) * jnp.exp2(p[j : j + 1]) for m, p in zip((mine, other), powers)]
-            total[at] = (terms[0] + terms[1]) / scale
+    for i in range(variants // 128):
+        at = slice(i * 128, (i + 1) * 128)
+        total[at] = placed[:, :, at].reshape(feat * kf, 128).T / scale
         copies.append(
             pltpu.make_async_copy(
-                total.at[pl.ds(i * step, step)], out.at[pl.ds(first + i * step, step)], sems.at[i]
+                total.at[pl.ds(i * 128, 128)], out.at[pl.ds(i * 128, 128)], sems.at[i]
             )
         )
         copies[i].start()
@@ -562,19 +581,22 @@
         copy.wait()
 
 
-def finish(mine, other, count, first, variants, done):
-    height, k = mine.shape[0] - 16, mine.shape[1]
-    steps = max(1, min(2, height // BLOCK))
-    return pl.pallas_call(
-        functools.partial(finish_kernel, first, steps),
-        in_specs=[VMEM] * 3 + [HBM] * len(done),
+def finish(first, mine, other, count, feat):
+    k, variants = 2 * first.shape[0], first.shape[1]
+    kf = k // feat
+    return pl.pallas_call(
+        functools.partial(finish_kernel, feat, kf),
+        in_specs=[VMEM] * 4,
         out_shape=jax.ShapeDtypeStruct((variants, k), F32),
         out_specs=HBM,
-        scratch_shapes=[pltpu.VMEM((height, k), F32), pltpu.SemaphoreType.DMA((steps,))],
-        input_output_aliases={3: 0} if done else {},
+        scratch_shapes=[
+            pltpu.VMEM((feat, kf, variants), F32),
+            pltpu.VMEM((variants, k), F32),
+            pltpu.SemaphoreType.DMA((variants // 128,)),
+        ],
         compiler_params=pltpu.CompilerParams(**PARAMS),
         name="finish",
-    )(mine, other, count, *done)
+    )(first, mine, other, count)
 
 
 def local(dosages, coefficients, directions, event_rank, events):
@@ -591,17 +613,20 @@
     linear, keep, send = products(dosages, coefficients, directions, feat)
     order = list(reversed(range(1, feat // 2)))
     received = {q: swap(send[q], "feat", 1) for q in order + [0]}
-    others, paired = [], linear
-    for q in order:
-        *first, message = join(paired, keep[q], received[q])
-        paired = first[0] if first else paired
-        others.append(swap(message, "feat", 2 * q))
+    paired = pair(linear, received[order[0]])
+    linears = [swap(paired, "feat", 2 * q) for q in order]
     table = tables(rank, paired, rows)
-
-    risk, sums, ordered_events, message = risks(paired, others, rank, event_row, table, rows)
-    messages = [message] + [swap(message, "ex", i) for i in range(1, ex)]
+    joined = [join(keep[q], received[q], linears + [table]) for q in order]
+    others = [swap(message, "feat", 2 * q) for message, q in zip(joined, order)]
+
+    risk, sums, ordered_events, total = risks([paired] + linears, rank, event_row, table, rows, joined)
+    later = jnp.zeros_like(total)
+    bit = 1
+    while bit < ex:
+        total, later = ranges(bit, total, swap(total, "ex", bit), later, others if bit == 1 else [])
+        bit *= 2
     tangent, later_sums, plain = suffix_sums(keep[0], received[0], others, risk, rank, table)
-    hazard, ordered_squares, message, count = shares(messages, sums, ordered_events, plain, later_sums)
+    hazard, ordered_squares, message = shares(later, sums, ordered_events, plain, later_sums)
     messages = [message] + [swap(message, "ex", i) for i in range(1, ex)]
     cumulative, squares = hazards(hazard, ordered_squares, rank, rows)
     summed = prefix_sums(later_sums, ordered_squares, rank, padded)
@@ -610,22 +635,17 @@
     chips = {0: own}
     for q in reversed(range(1, feat // 2)):
         chips[q] = swap(own, "feat", 2 * q)
-    parts = []
-    for q in range(feat // 2):
-        parts += [chips[q], swap(chips[q], "feat", 1)]
-
-    half = variants // 2
-    partial_sums = [gradients(parts, dosages, start, half) for start in (0, half)]
+    near = [chips[q] for q in range(feat // 2)]
+    far = [swap(chips[q], "feat", 1) for q in range(feat // 2)]
+    partial_sums = [gradients(pieces, dosages) for pieces in (near, far)]
     bit = 1
     while 2 * bit < ex:
         received = [swap(message, "ex", bit) for message in partial_sums]
         partial_sums = [merge(mine, other) for mine, other in zip(partial_sums, received)]
         bit *= 2
     received = [swap(message, "ex", bit) for message in partial_sums]
-    done = []
-    for i in range(2):
-        done = [finish(partial_sums[i], received[i], count, i * half, variants, done)]
-    result = done[0]
+    first = add(partial_sums[0], received[0], variants)
+    result = finish(first, partial_sums[1], received[1], total, feat)
     if padded != each:
         result = result.reshape(variants, feat, padded)[:, :, :each].reshape(variants, k)
     return result

time: 57.8 us -> 63.9 us (1.11)
  starting transfers between devices: 23.8 us -> 28.1 us
  waiting for transfers between devices: 19.9 us -> 21 us
    ppermute x24 -> x26, starting transfers between devices: 23.8 us -> 28.1 us  [swap(): return lax.ppermute(x, axis, [(s, s ^ i) for s in range(count)])]
    ppermute x24 -> x26, waiting for transfers between devices: 19.9 us -> 21 us  [swap(): return lax.ppermute(x, axis, [(s, s ^ i) for s in range(count)])]
    pallas_call x9 -> x12, Pallas kernels: 4.2 us -> 4.5 us  [the longest x2 1.91 us: gradients(): pl.pallas_call(functools.partial(gradient_kernel, parts, kf), in_specs=[V...]
  transfers between devices with their start and end apart: 24 -> 26, of which waited for: 12 -> 14; matrix products, arithmetic and copies ran while one was open for 0% -> 0% of each run, Pallas kernels for 15% -> 15%
where the time goes in v9:
time: 63.9 us; the launch traced here: 63.8 us
  starting transfers between devices  28.1 us (44%)
  waiting for transfers between devices  21 us (33%)
  Pallas kernels  14.5 us (23%)
    ppermute x26, starting transfers between devices, swap(): return lax.ppermute(x, axis, [(s, s ^ i) for s in range(count)])  28.1 us
    ppermute x26, waiting for transfers between devices, swap(): return lax.ppermute(x, axis, [(s, s ^ i) for s in range(count)])  21 us
    pallas_call x1, Pallas kernels, products(): pl.pallas_call(functools.partial(product_kernel, feat, kf, chunk), in_spe...  3.75 us
    pallas_call x1, Pallas kernels, suffix_sums(): pl.pallas_call(functools.partial(suffix_kernel, len(messages)), in_specs=...  2.23 us
    pallas_call x2, Pallas kernels, gradients(): pl.pallas_call(functools.partial(gradient_kernel, parts, kf), in_specs=[V...  1.91 us
    pallas_call x1, Pallas kernels, prefix_sums(): pl.pallas_call(prefix_kernel, in_specs=[VMEM] * 3, out_shape=jax.ShapeDty...  1.75 us
  transfers between devices with their start and end apart: 26, of which 14 were waited for; matrix products, arithmetic and copies ran while one was open for 0% of the time, Pallas kernels for 15%

profile of v9, /device:TPU:0, one launch (start us, length us, event | category | flops | bytes accessed | tf_op | source)
XLA Modules:
  0.0 63.8 jit_solution(16128149234726085643)
XLA Ops:
  0.0 3.8 %products.1 = (f32[16,256]{1,0:T(8,128)S(1)}, f32[16,4096]{1,0:T(8,128)S(1)}, f32[16,4096]{1,0:T(8,128)S(1)}, f32[16,4096]{1,0:T(8,128)S(1)}, f32[16,4096]{1,0:T...) custom-call(bf16[512,128]{1,0:T(8,128)(2,1)} %directions.1, ...), custom_call_target="tpu_custom_call" | custom-call | flops 536870912 | bytes 6291456 | tf_op jit(solution)/shard_map/products/pallas_call | solution.py:117
  5.5 3.8 %collective-permute-start.1 = (f32[16,256]{1,0:T(8,128)S(1)}, f32[16,256]{1,0:T(8,128)S(1)}, u32[]{:S(2)}, u32[]{:S(2)}) collective-permute-start(f32[16,256]{1,0:T(8,128)S(1)} %pair.1.waited.refs_0_), channel_id=1, source_target_pairs={{0,6},{1,7},{2,4},{3,5},{4,2},{5,3},{6,0},{7,1},{8,14},{9,15},{10,... | collective-permute-start | bytes 49160 | tf_op jit(solution)/shard_map/ppermute | solution.py:22
  9.8 1.2 %collective-permute-done.1.refs_0_.refs_1_ = f32[16,256]{1,0:T(8,128)S(1)} collective-permute-done((f32[16,256]{1,0:T(8,128)S(1)}, f32[16,256]{1,0:T(8,128)S(1)}, u32[]{:S(2)}, u32[]{:S(2)}) %collective-permute-start.1) | collective-permute-done | bytes 16416 | tf_op jit(solution)/shard_map/ppermute | solution.py:22
  11.0 2.0 %collective-permute-start.3 = (f32[16,256]{1,0:T(8,128)S(1)}, f32[16,256]{1,0:T(8,128)S(1)}, u32[]{:S(2)}, u32[]{:S(2)}) collective-permute-start(f32[16,256]{1,0:T(8,128)S(1)} %pair.1.waited.refs_0_), channel_id=1, source_target_pairs={{0,2},{1,3},{2,0},{3,1},{4,6},{5,7},{6,4},{7,5},{8,10},{9,11},{10,... | collective-permute-start | bytes 49160 | tf_op jit(solution)/shard_map/ppermute | solution.py:22
  13.6 1.1 %collective-permute-done.3.refs_2_.refs_3_ = f32[16,256]{1,0:T(8,128)S(1)} collective-permute-done((f32[16,256]{1,0:T(8,128)S(1)}, f32[16,256]{1,0:T(8,128)S(1)}, u32[]{:S(2)}, u32[]{:S(2)}) %collective-permute-start.3) | collective-permute-done | bytes 16416 | tf_op jit(solution)/shard_map/ppermute | solution.py:22
  14.9 3.0 %collective-permute-start.7 = (s16[16,4224]{1,0:T(8,128)(2,1)S(1)}, s16[16,4224]{1,0:T(8,128)(2,1)S(1)}, u32[]{:S(2)}, u32[]{:S(2)}) collective-permute-start(s16[16,4224]{1,0:T(8,128)(2,1)S(1)} %join.3.refs_7_), channel_id=1, source_target_pairs={{0,6},{1,7},{2,4},{3,5},{4,2},{5,3},{6,0},{7,1},{8,14},{9,15},{10,... | collective-permute-start | bytes 405512 | tf_op jit(solution)/shard_map/ppermute | solution.py:22
  19.7 2.1 %collective-permute-start.6 = (f32[8,128]{1,0:T(8,128)S(1)}, f32[8,128]{1,0:T(8,128)S(1)}, u32[]{:S(2)}, u32[]{:S(2)}) collective-permute-start(f32[8,128]{1,0:T(8,128)S(1)} %get-tuple-element.37.refs_0_), channel_id=1, source_target_pairs={{0,8},{8,0},{16,24},{24,16},{1,9},{9,1},{17,25},{25,17},{2,10},{10... | collective-permute-start | bytes 12296 | tf_op jit(solution)/shard_map/ppermute | solution.py:22
  21.8 1.6 %collective-permute-done.6.refs_1_ = f32[8,128]{1,0:T(8,128)S(1)} collective-permute-done((f32[8,128]{1,0:T(8,128)S(1)}, f32[8,128]{1,0:T(8,128)S(1)}, u32[]{:S(2)}, u32[]{:S(2)}) %collective-permute-start.6) | collective-permute-done | bytes 4128 | tf_op jit(solution)/shard_map/ppermute | solution.py:22
  23.8 2.7 %collective-permute-start.10 = (f32[8,128]{1,0:T(8,128)S(1)}, f32[8,128]{1,0:T(8,128)S(1)}, u32[]{:S(2)}, u32[]{:S(2)}) collective-permute-start(f32[8,128]{1,0:T(8,128)S(1)} %get-tuple-element.38.refs_0_), channel_id=1, source_target_pairs={{0,16},{8,24},{16,0},{24,8},{1,17},{9,25},{17,1},{25,9},{2,18},{10... | collective-permute-start | bytes 12296 | tf_op jit(solution)/shard_map/ppermute | solution.py:22
  26.5 2.2 %suffix_sums.1 = (f32[16,4096]{1,0:T(8,128)S(1)}, f32[256,256]{1,0:T(8,128)S(1)}, f32[16,128]{1,0:T(8,128)S(1)}) custom-call(f32[16,4096]{1,0:T(8,128)S(1)} %get-tuple-element.43.own, f32[16,4096]{1,0:T(8,128)S(1)} %collective-permute-done.11.other, s16[16,4224]{1,0:T(8,128)(2,1)S(1)} %collective-permute-done.7.refs_3_.refs_0_, ...), custom_call_target="tpu_custom_call" | custom-call | flops 1073741824 | bytes 1572864 | tf_op jit(solution)/shard_map/suffix_sums/pallas_call | solution.py:382
  28.9 1.6 %collective-permute-start.12 = (f32[40,128]{1,0:T(8,128)S(1)}, f32[40,128]{1,0:T(8,128)S(1)}, u32[]{:S(2)}, u32[]{:S(2)}) collective-permute-start(f32[40,128]{1,0:T(8,128)S(1)} %get-tuple-element.48.refs_0_), channel_id=1, source_target_pairs={{0,8},{8,0},{16,24},{24,16},{1,9},{9,1},{17,25},{25,17},{2,10},{10... | collective-permute-start | bytes 61448 | tf_op jit(solution)/shard_map/ppermute | solution.py:22
  30.5 2.2 %collective-permute-start.13 = (f32[40,128]{1,0:T(8,128)S(1)}, f32[40,128]{1,0:T(8,128)S(1)}, u32[]{:S(2)}, u32[]{:S(2)}) collective-permute-start(f32[40,128]{1,0:T(8,128)S(1)} %get-tuple-element.48.refs_0_), channel_id=1, source_target_pairs={{0,16},{8,24},{16,0},{24,8},{1,17},{9,25},{17,1},{25,9},{2,18},{10... | collective-permute-start | bytes 61448 | tf_op jit(solution)/shard_map/ppermute | solution.py:22
  33.4 1.8 %prefix_sums.1.refs_5_ = f32[16,4096]{1,0:T(8,128)S(1)} custom-call(f32[256,256]{1,0:T(8,128)S(1)} %get-tuple-element.47.ordered.sums, f32[16,256]{1,0:T(8,128)S(1)} %get-tuple-element.50.squares.square, s32[1,4096]{1,0:T(1,128)S(1)} %bitcast.5), custom_call_target="tpu_custom_call" | custom-call | flops 1073741824 | bytes 1572864 | tf_op jit(solution)/shard_map/prefix_sums/pallas_call | solution.py:427
  36.0 2.3 %collective-permute-done.14.refs_3_ = f32[40,128]{1,0:T(8,128)S(1)} collective-permute-done((f32[40,128]{1,0:T(8,128)S(1)}, f32[40,128]{1,0:T(8,128)S(1)}, u32[]{:S(2)}, u32[]{:S(2)}) %collective-permute-start.14) | collective-permute-done | bytes 20512 | tf_op jit(solution)/shard_map/ppermute | solution.py:22
  38.6 1.6 %collective-permute-start.15 = (bf16[16,4096]{1,0:T(8,128)(2,1)S(1)}, bf16[16,4096]{1,0:T(8,128)(2,1)S(1)}, u32[]{:S(2)}, u32[]{:S(2)}) collective-permute-start(bf16[16,4096]{1,0:T(8,128)(2,1)S(1)} %weights.1.refs_0_), channel_id=1, source_target_pairs={{0,2},{1,3},{2,0},{3,1},{4,6},{5,7},{6,4},{7,5},{8,10},{9,11},{10,... | collective-permute-start | bytes 393224 | tf_op jit(solution)/shard_map/ppermute | solution.py:22
  40.2 1.6 %collective-permute-start.16 = (bf16[16,4096]{1,0:T(8,128)(2,1)S(1)}, bf16[16,4096]{1,0:T(8,128)(2,1)S(1)}, u32[]{:S(2)}, u32[]{:S(2)}) collective-permute-start(bf16[16,4096]{1,0:T(8,128)(2,1)S(1)} %weights.1.refs_0_), channel_id=1, source_target_pairs={{0,4},{1,5},{2,6},{3,7},{4,0},{5,1},{6,2},{7,3},{8,12},{9,13},{10,... | collective-permute-start | bytes 393224 | tf_op jit(solution)/shard_map/ppermute | solution.py:22
  42.1 1.5 %collective-permute-done.15.refs_1_ = bf16[16,4096]{1,0:T(8,128)(2,1)S(1)} collective-permute-done((bf16[16,4096]{1,0:T(8,128)(2,1)S(1)}, bf16[16,4096]{1,0:T(8,128)(2,1)S(1)}, u32[]{:S(2)}, u32[]{:S(2)}) %collective-permute-start.15) | collective-permute-done | bytes 131104 | tf_op jit(solution)/shard_map/ppermute | solution.py:22
  43.6 1.5 %collective-permute-done.16.refs_2_ = bf16[16,4096]{1,0:T(8,128)(2,1)S(1)} collective-permute-done((bf16[16,4096]{1,0:T(8,128)(2,1)S(1)}, bf16[16,4096]{1,0:T(8,128)(2,1)S(1)}, u32[]{:S(2)}, u32[]{:S(2)}) %collective-permute-start.16) | collective-permute-done | bytes 131104 | tf_op jit(solution)/shard_map/ppermute | solution.py:22
  45.1 2.5 %collective-permute-done.17.refs_3_ = bf16[16,4096]{1,0:T(8,128)(2,1)S(1)} collective-permute-done((bf16[16,4096]{1,0:T(8,128)(2,1)S(1)}, bf16[16,4096]{1,0:T(8,128)(2,1)S(1)}, u32[]{:S(2)}, u32[]{:S(2)}) %collective-permute-start.17) | collective-permute-done | bytes 131104 | tf_op jit(solution)/shard_map/ppermute | solution.py:22
  50.0 1.8 %collective-permute-start.24 = (s16[17,16,128]{2,1,0:T(8,128)(2,1)S(1)}, s16[17,16,128]{2,1,0:T(8,128)(2,1)S(1)}, u32[]{:S(2)}, u32[]{:S(2)}) collective-permute-start(s16[17,16,128]{2,1,0:T(8,128)(2,1)S(1)} %gradients.3.mine), channel_id=1, source_target_pairs={{0,8},{8,0},{16,24},{24,16},{1,9},{9,1},{17,25},{25,17},{2,10},{10... | collective-permute-start | bytes 208904 | tf_op jit(solution)/shard_map/ppermute | solution.py:22
  51.8 1.9 %collective-permute-done.18.other = s16[17,16,128]{2,1,0:T(8,128)(2,1)S(1)} collective-permute-done((s16[17,16,128]{2,1,0:T(8,128)(2,1)S(1)}, s16[17,16,128]{2,1,0:T(8,128)(2,1)S(1)}, u32[]{:S(2)}, u32[]{:S(2)}) %collective-permute-start.18) | collective-permute-done | bytes 69664 | tf_op jit(solution)/shard_map/ppermute | solution.py:22
  55.0 2.2 %collective-permute-start.25 = (s16[17,16,128]{2,1,0:T(8,128)(2,1)S(1)}, s16[17,16,128]{2,1,0:T(8,128)(2,1)S(1)}, u32[]{:S(2)}, u32[]{:S(2)}) collective-permute-start(s16[17,16,128]{2,1,0:T(8,128)(2,1)S(1)} %merge.3.mine), channel_id=1, source_target_pairs={{0,16},{8,24},{16,0},{24,8},{1,17},{9,25},{17,1},{25,9},{2,18},{10... | collective-permute-start | bytes 208904 | tf_op jit(solution)/shard_map/ppermute | solution.py:22
  57.3 4.3 %collective-permute-done.19.other = s16[17,16,128]{2,1,0:T(8,128)(2,1)S(1)} collective-permute-done((s16[17,16,128]{2,1,0:T(8,128)(2,1)S(1)}, s16[17,16,128]{2,1,0:T(8,128)(2,1)S(1)}, u32[]{:S(2)}, u32[]{:S(2)}) %collective-permute-start.19) | collective-permute-done | bytes 69664 | tf_op jit(solution)/shard_map/ppermute | solution.py:22
  61.7 1.0 %collective-permute-done.25.other = s16[17,16,128]{2,1,0:T(8,128)(2,1)S(1)} collective-permute-done((s16[17,16,128]{2,1,0:T(8,128)(2,1)S(1)}, s16[17,16,128]{2,1,0:T(8,128)(2,1)S(1)}, u32[]{:S(2)}, u32[]{:S(2)}) %collective-permute-start.25) | collective-permute-done | bytes 69664 | tf_op jit(solution)/shard_map/ppermute | solution.py:22
  (55 shorter events, 12.2 us)
Async XLA Ops:
  4.3 13.6 %collective-permute-start.4 = (f32[16,4096]{1,0:T(8,128)S(1)}, f32[16,4096]{1,0:T(8,128)S(1)}, u32[]{:S(2)}, u32[]{:S(2)}) collective-permute-start(f32[16,4096]{1,0:T(8,128)S(1)} %get-tuple-element.34), channel_id=1, source_target_pairs={{0,1},{1,0},{2,3},{3,2},{4,5},{5,4},{6,7},{7,6},{8,9},{9,8},{10,11... | collective-permute-start | bytes 786440 | tf_op jit(solution)/shard_map/ppermute | solution.py:22
  4.3 14.2 %collective-permute-start.5 = (f32[16,4096]{1,0:T(8,128)S(1)}, f32[16,4096]{1,0:T(8,128)S(1)}, u32[]{:S(2)}, u32[]{:S(2)}) collective-permute-start(f32[16,4096]{1,0:T(8,128)S(1)} %get-tuple-element.36), channel_id=1, source_target_pairs={{0,1},{1,0},{2,3},{3,2},{4,5},{5,4},{6,7},{7,6},{8,9},{9,8},{10,11... | collective-permute-start | bytes 786440 | tf_op jit(solution)/shard_map/ppermute | solution.py:22
  4.8 21.8 %collective-permute-start.11 = (f32[16,4096]{1,0:T(8,128)S(1)}, f32[16,4096]{1,0:T(8,128)S(1)}, u32[]{:S(2)}, u32[]{:S(2)}) collective-permute-start(f32[16,4096]{1,0:T(8,128)S(1)} %get-tuple-element.44), channel_id=1, source_target_pairs={{0,1},{1,0},{2,3},{3,2},{4,5},{5,4},{6,7},{7,6},{8,9},{9,8},{10,11... | collective-permute-start | bytes 786440 | tf_op jit(solution)/shard_map/ppermute | solution.py:22
  5.5 5.5 %collective-permute-start.1 = (f32[16,256]{1,0:T(8,128)S(1)}, f32[16,256]{1,0:T(8,128)S(1)}, u32[]{:S(2)}, u32[]{:S(2)}) collective-permute-start(f32[16,256]{1,0:T(8,128)S(1)} %pair.1.waited.refs_0_), channel_id=1, source_target_pairs={{0,6},{1,7},{2,4},{3,5},{4,2},{5,3},{6,0},{7,1},{8,14},{9,15},{10,... | collective-permute-start | bytes 49160 | tf_op jit(solution)/shard_map/ppermute | solution.py:22
  9.3 4.3 %collective-permute-start.2 = (f32[16,256]{1,0:T(8,128)S(1)}, f32[16,256]{1,0:T(8,128)S(1)}, u32[]{:S(2)}, u32[]{:S(2)}) collective-permute-start(f32[16,256]{1,0:T(8,128)S(1)} %pair.1.waited.refs_0_), channel_id=1, source_target_pairs={{0,4},{1,5},{2,6},{3,7},{4,0},{5,1},{6,2},{7,3},{8,12},{9,13},{10,... | collective-permute-start | bytes 49160 | tf_op jit(solution)/shard_map/ppermute | solution.py:22
  11.0 3.7 %collective-permute-start.3 = (f32[16,256]{1,0:T(8,128)S(1)}, f32[16,256]{1,0:T(8,128)S(1)}, u32[]{:S(2)}, u32[]{:S(2)}) collective-permute-start(f32[16,256]{1,0:T(8,128)S(1)} %pair.1.waited.refs_0_), channel_id=1, source_target_pairs={{0,2},{1,3},{2,0},{3,1},{4,6},{5,7},{6,4},{7,5},{8,10},{9,11},{10,... | collective-permute-start | bytes 49160 | tf_op jit(solution)/shard_map/ppermute | solution.py:22
  14.9 8.5 %collective-permute-start.7 = (s16[16,4224]{1,0:T(8,128)(2,1)S(1)}, s16[16,4224]{1,0:T(8,128)(2,1)S(1)}, u32[]{:S(2)}, u32[]{:S(2)}) collective-permute-start(s16[16,4224]{1,0:T(8,128)(2,1)S(1)} %join.3.refs_7_), channel_id=1, source_target_pairs={{0,6},{1,7},{2,4},{3,5},{4,2},{5,3},{6,0},{7,1},{8,14},{9,15},{10,... | collective-permute-start | bytes 405512 | tf_op jit(solution)/shard_map/ppermute | solution.py:22
  18.0 5.4 %collective-permute-start.8 = (s16[16,4224]{1,0:T(8,128)(2,1)S(1)}, s16[16,4224]{1,0:T(8,128)(2,1)S(1)}, u32[]{:S(2)}, u32[]{:S(2)}) collective-permute-start(s16[16,4224]{1,0:T(8,128)(2,1)S(1)} %join.4.refs_8_), channel_id=1, source_target_pairs={{0,4},{1,5},{2,6},{3,7},{4,0},{5,1},{6,2},{7,3},{8,12},{9,13},{10,... | collective-permute-start | bytes 405512 | tf_op jit(solution)/shard_map/ppermute | solution.py:22
  18.7 5.1 %collective-permute-start.9 = (s16[16,4224]{1,0:T(8,128)(2,1)S(1)}, s16[16,4224]{1,0:T(8,128)(2,1)S(1)}, u32[]{:S(2)}, u32[]{:S(2)}) collective-permute-start(s16[16,4224]{1,0:T(8,128)(2,1)S(1)} %join.5.refs_9_), channel_id=1, source_target_pairs={{0,2},{1,3},{2,0},{3,1},{4,6},{5,7},{6,4},{7,5},{8,10},{9,11},{10,... | collective-permute-start | bytes 405512 | tf_op jit(solution)/shard_map/ppermute | solution.py:22
  19.7 3.7 %collective-permute-start.6 = (f32[8,128]{1,0:T(8,128)S(1)}, f32[8,128]{1,0:T(8,128)S(1)}, u32[]{:S(2)}, u32[]{:S(2)}) collective-permute-start(f32[8,128]{1,0:T(8,128)S(1)} %get-tuple-element.37.refs_0_), channel_id=1, source_target_pairs={{0,8},{8,0},{16,24},{24,16},{1,9},{9,1},{17,25},{25,17},{2,10},{10... | collective-permute-start | bytes 12296 | tf_op jit(solution)/shard_map/ppermute | solution.py:22
  23.8 5.0 %collective-permute-start.10 = (f32[8,128]{1,0:T(8,128)S(1)}, f32[8,128]{1,0:T(8,128)S(1)}, u32[]{:S(2)}, u32[]{:S(2)}) collective-permute-start(f32[8,128]{1,0:T(8,128)S(1)} %get-tuple-element.38.refs_0_), channel_id=1, source_target_pairs={{0,16},{8,24},{16,0},{24,8},{1,17},{9,25},{17,1},{25,9},{2,18},{10... | collective-permute-start | bytes 12296 | tf_op jit(solution)/shard_map/ppermute | solution.py:22
  28.9 7.1 %collective-permute-start.12 = (f32[40,128]{1,0:T(8,128)S(1)}, f32[40,128]{1,0:T(8,128)S(1)}, u32[]{:S(2)}, u32[]{:S(2)}) collective-permute-start(f32[40,128]{1,0:T(8,128)S(1)} %get-tuple-element.48.refs_0_), channel_id=1, source_target_pairs={{0,8},{8,0},{16,24},{24,16},{1,9},{9,1},{17,25},{25,17},{2,10},{10... | collective-permute-start | bytes 61448 | tf_op jit(solution)/shard_map/ppermute | solution.py:22
  30.5 5.5 %collective-permute-start.13 = (f32[40,128]{1,0:T(8,128)S(1)}, f32[40,128]{1,0:T(8,128)S(1)}, u32[]{:S(2)}, u32[]{:S(2)}) collective-permute-start(f32[40,128]{1,0:T(8,128)S(1)} %get-tuple-element.48.refs_0_), channel_id=1, source_target_pairs={{0,16},{8,24},{16,0},{24,8},{1,17},{9,25},{17,1},{25,9},{2,18},{10... | collective-permute-start | bytes 61448 | tf_op jit(solution)/shard_map/ppermute | solution.py:22
  32.8 5.6 %collective-permute-start.14 = (f32[40,128]{1,0:T(8,128)S(1)}, f32[40,128]{1,0:T(8,128)S(1)}, u32[]{:S(2)}, u32[]{:S(2)}) collective-permute-start(f32[40,128]{1,0:T(8,128)S(1)} %get-tuple-element.48.refs_0_), channel_id=1, source_target_pairs={{0,24},{8,16},{16,8},{24,0},{1,25},{9,17},{17,9},{25,1},{2,26},{10... | collective-permute-start | bytes 61448 | tf_op jit(solution)/shard_map/ppermute | solution.py:22
  38.6 5.0 %collective-permute-start.15 = (bf16[16,4096]{1,0:T(8,128)(2,1)S(1)}, bf16[16,4096]{1,0:T(8,128)(2,1)S(1)}, u32[]{:S(2)}, u32[]{:S(2)}) collective-permute-start(bf16[16,4096]{1,0:T(8,128)(2,1)S(1)} %weights.1.refs_0_), channel_id=1, source_target_pairs={{0,2},{1,3},{2,0},{3,1},{4,6},{5,7},{6,4},{7,5},{8,10},{9,11},{10,... | collective-permute-start | bytes 393224 | tf_op jit(solution)/shard_map/ppermute | solution.py:22
  40.2 5.0 %collective-permute-start.16 = (bf16[16,4096]{1,0:T(8,128)(2,1)S(1)}, bf16[16,4096]{1,0:T(8,128)(2,1)S(1)}, u32[]{:S(2)}, u32[]{:S(2)}) collective-permute-start(bf16[16,4096]{1,0:T(8,128)(2,1)S(1)} %weights.1.refs_0_), channel_id=1, source_target_pairs={{0,4},{1,5},{2,6},{3,7},{4,0},{5,1},{6,2},{7,3},{8,12},{9,13},{10,... | collective-permute-start | bytes 393224 | tf_op jit(solution)/shard_map/ppermute | solution.py:22
  41.8 5.9 %collective-permute-start.17 = (bf16[16,4096]{1,0:T(8,128)(2,1)S(1)}, bf16[16,4096]{1,0:T(8,128)(2,1)S(1)}, u32[]{:S(2)}, u32[]{:S(2)}) collective-permute-start(bf16[16,4096]{1,0:T(8,128)(2,1)S(1)} %weights.1.refs_0_), channel_id=1, source_target_pairs={{0,6},{1,7},{2,4},{3,5},{4,2},{5,3},{6,0},{7,1},{8,14},{9,15},{10,... | collective-permute-start | bytes 393224 | tf_op jit(solution)/shard_map/ppermute | solution.py:22
  42.1 6.6 %collective-permute-start.20 = (bf16[16,4096]{1,0:T(8,128)(2,1)S(1)}, bf16[16,4096]{1,0:T(8,128)(2,1)S(1)}, u32[]{:S(2)}, u32[]{:S(2)}) collective-permute-start(bf16[16,4096]{1,0:T(8,128)(2,1)S(1)} %weights.1.refs_0_), channel_id=1, source_target_pairs={{0,1},{1,0},{2,3},{3,2},{4,5},{5,4},{6,7},{7,6},{8,9},{9,8},{10,11... | collective-permute-start | bytes 393224 | tf_op jit(solution)/shard_map/ppermute | solution.py:22
  43.6 5.1 %collective-permute-start.21 = (bf16[16,4096]{1,0:T(8,128)(2,1)S(1)}, bf16[16,4096]{1,0:T(8,128)(2,1)S(1)}, u32[]{:S(2)}, u32[]{:S(2)}) collective-permute-start(bf16[16,4096]{1,0:T(8,128)(2,1)S(1)} %collective-permute-done.15.refs_1_), channel_id=1, source_target_pairs={{0,1},{1,0},{2,3},{3,2},{4,5},{5,4},{6,7},{7,6},{8,9},{9,8},{10,11... | collective-permute-start | bytes 393224 | tf_op jit(solution)/shard_map/ppermute | solution.py:22
  45.1 3.6 %collective-permute-start.22 = (bf16[16,4096]{1,0:T(8,128)(2,1)S(1)}, bf16[16,4096]{1,0:T(8,128)(2,1)S(1)}, u32[]{:S(2)}, u32[]{:S(2)}) collective-permute-start(bf16[16,4096]{1,0:T(8,128)(2,1)S(1)} %collective-permute-done.16.refs_2_), channel_id=1, source_target_pairs={{0,1},{1,0},{2,3},{3,2},{4,5},{5,4},{6,7},{7,6},{8,9},{9,8},{10,11... | collective-permute-start | bytes 393224 | tf_op jit(solution)/shard_map/ppermute | solution.py:22
  48.6 5.0 %collective-permute-start.18 = (s16[17,16,128]{2,1,0:T(8,128)(2,1)S(1)}, s16[17,16,128]{2,1,0:T(8,128)(2,1)S(1)}, u32[]{:S(2)}, u32[]{:S(2)}) collective-permute-start(s16[17,16,128]{2,1,0:T(8,128)(2,1)S(1)} %gradients.2.mine), channel_id=1, source_target_pairs={{0,8},{8,0},{16,24},{24,16},{1,9},{9,1},{17,25},{25,17},{2,10},{10... | collective-permute-start | bytes 208904 | tf_op jit(solution)/shard_map/ppermute | solution.py:22
  50.0 4.8 %collective-permute-start.24 = (s16[17,16,128]{2,1,0:T(8,128)(2,1)S(1)}, s16[17,16,128]{2,1,0:T(8,128)(2,1)S(1)}, u32[]{:S(2)}, u32[]{:S(2)}) collective-permute-start(s16[17,16,128]{2,1,0:T(8,128)(2,1)S(1)} %gradients.3.mine), channel_id=1, source_target_pairs={{0,8},{8,0},{16,24},{24,16},{1,9},{9,1},{17,25},{25,17},{2,10},{10... | collective-permute-start | bytes 208904 | tf_op jit(solution)/shard_map/ppermute | solution.py:22
  53.9 7.6 %collective-permute-start.19 = (s16[17,16,128]{2,1,0:T(8,128)(2,1)S(1)}, s16[17,16,128]{2,1,0:T(8,128)(2,1)S(1)}, u32[]{:S(2)}, u32[]{:S(2)}) collective-permute-start(s16[17,16,128]{2,1,0:T(8,128)(2,1)S(1)} %merge.2.mine), channel_id=1, source_target_pairs={{0,16},{8,24},{16,0},{24,8},{1,17},{9,25},{17,1},{25,9},{2,18},{10... | collective-permute-start | bytes 208904 | tf_op jit(solution)/shard_map/ppermute | solution.py:22
  55.0 7.7 %collective-permute-start.25 = (s16[17,16,128]{2,1,0:T(8,128)(2,1)S(1)}, s16[17,16,128]{2,1,0:T(8,128)(2,1)S(1)}, u32[]{:S(2)}, u32[]{:S(2)}) collective-permute-start(s16[17,16,128]{2,1,0:T(8,128)(2,1)S(1)} %merge.3.mine), channel_id=1, source_target_pairs={{0,16},{8,24},{16,0},{24,8},{1,17},{9,25},{17,1},{25,9},{2,18},{10... | collective-permute-start | bytes 208904 | tf_op jit(solution)/shard_map/ppermute | solution.py:22
  (5 other events, 41.3 us)

commit v10 on v8

--- a/solution.py
+++ b/solution.py
@@ -151,45 +151,54 @@
     return values.astype(jnp.int32).astype(F32)
 
 
-def join_kernel(linear, *refs):
-    mine, other = refs[:2]
-    out = refs[-1]
-    kf, rows = mine.shape
-    span = min(SPAN, rows)
+def pair_kernel(linear, received, out):
+    out[...] = linear[...] + received[:, received.shape[1] - LO :]
+
+
+def pair(linear, received):
+    return pl.pallas_call(
+        pair_kernel,
+        in_specs=[VMEM] * 2,
+        out_shape=jax.ShapeDtypeStruct(linear.shape, F32),
+        out_specs=VMEM,
+        compiler_params=pltpu.CompilerParams(**PARAMS),
+        name="pair",
+    )(linear, received)
+
+
+def join_kernel(start, width, mine, other, *refs):
+    linear, out = refs[0], refs[-1]
+    kf = mine.shape[0]
+    span = min(SPAN, width)
     lane = lax.broadcasted_iota(jnp.int32, (kf, 128), 1)
-    paired = linear[...]
-    if len(refs) > 3:
-        paired = paired + other[:, rows:]
-        refs[2][...] = paired
-    linear_power = power_of(jnp.max(jnp.abs(paired), axis=1, keepdims=True))
-    scaled = paired * jnp.exp2(-linear_power)
-    whole = jnp.round(scaled)
-    powers = jnp.where(lane == rows // span, linear_power, 0.0)
-    for i in range(rows // span):
-        at = slice(i * span, (i + 1) * span)
+    powers = jnp.zeros((kf, 128), F32)
+    for i in range(width // span):
+        at = slice(start + i * span, start + (i + 1) * span)
         total = mine[:, at] + other[:, at]
         power = power_of(jnp.max(jnp.abs(total), axis=1, keepdims=True))
-        out[:, at] = to_short(total * jnp.exp2(-power))
+        out[:, i * span : (i + 1) * span] = to_short(total * jnp.exp2(-power))
         powers = jnp.where(lane == i, power, powers)
-    out[:, rows : rows + LO] = to_short(whole)
-    out[:, rows + LO : rows + 2 * LO] = to_short((scaled - whole) * 32768.0)
-    out[:, rows + 2 * LO :] = to_short(powers)
-
-
-def join(linear, keep, received):
+    if start == 0:
+        power = power_of(jnp.max(jnp.abs(linear[...]), axis=1, keepdims=True))
+        scaled = linear[...] * jnp.exp2(-power)
+        whole = jnp.round(scaled)
+        out[:, width : width + LO] = to_short(whole)
+        out[:, width + LO : width + 2 * LO] = to_short((scaled - whole) * 32768.0)
+        powers = jnp.where(lane == 127, power, powers)
+    out[:, out.shape[1] - 128 :] = to_short(powers)
+
+
+def join(keep, received, start, width, linear, waited):
     kf, rows = keep.shape
-    message = jax.ShapeDtypeStruct((kf, rows + 2 * LO + 128), jnp.int16)
-    shapes = [message]
-    if received.shape[1] > rows:
-        shapes = [jax.ShapeDtypeStruct(linear.shape, F32), message]
-    return pl.pallas_call(
-        join_kernel,
-        in_specs=[VMEM] * 3,
-        out_shape=shapes,
-        out_specs=[VMEM] * len(shapes),
+    extra = 2 * LO if start == 0 else 0
+    return pl.pallas_call(
+        functools.partial(join_kernel, start, width),
+        in_specs=[VMEM] * 3 + [pl.BlockSpec(memory_space=pl.ANY)] * len(waited),
+        out_shape=jax.ShapeDtypeStruct((kf, width + extra + 128), jnp.int16),
+        out_specs=VMEM,
         compiler_params=pltpu.CompilerParams(**PARAMS),
         name="join",
-    )(linear, keep, received)
+    )(keep, received, linear, *waited)
 
 
 def table_kernel(rows, rank, waited, table):
@@ -217,13 +226,13 @@
 
 def risk_kernel(rows, parts, linear, *refs):
     messages, (rank, events, table) = refs[:parts], refs[parts : parts + 3]
-    risk_out, sums_out, events_out, message = refs[parts + 3 :]
+    risk_out, sums_out, events_out, message = refs[-4:]
     groups = rows // LO
-    span = min(SPAN, rows)
     total = linear[...]
     for part in messages:
-        power = from_short(part[:, rows + 2 * LO :])[:, rows // span : rows // span + 1]
-        high, low = from_short(part[:, rows : rows + LO]), from_short(part[:, rows + LO : rows + 2 * LO])
+        end = part.shape[1] - 128
+        power = from_short(part[:, end:])[:, 127:]
+        high, low = from_short(part[:, end - 2 * LO : end - LO]), from_short(part[:, end - LO : end])
         total = total + (high + low * (1.0 / 32768.0)) * jnp.exp2(power)
     risk = jnp.exp(total)
     for g in range(groups):
@@ -262,19 +271,10 @@
     )(linear, *messages, rank, events, table)
 
 
-def share_kernel(ex, *refs):
-    messages, (sums, events, plain, ordered) = refs[:ex], refs[ex : ex + 4]
-    hazard_out, squares, message, count_out = refs[ex + 4 :]
+def share_kernel(later, sums, events, plain, ordered, hazard_out, squares, message):
     kf = plain.shape[0]
     groups = sums.shape[0]
-    me = lax.axis_index("ex")
-    later = jnp.zeros((1, 1), F32)
-    count = messages[0][1:2]
-    for i in range(1, ex):
-        later = later + jnp.where((me ^ i) > me, messages[i][0:1, 0:1], 0.0)
-        count = count + messages[i][1:2]
-    count_out[...] = jnp.broadcast_to(count, count_out.shape)
-    risk_sum = sums[...] + later
+    risk_sum = sums[...] + later[0:1, 0:1]
     hazard = events[...] / risk_sum
     square = events[...] / (risk_sum * risk_sum)
     hazard_out[...] = hazard
@@ -289,21 +289,16 @@
     message[2 * kf :] = jnp.concatenate(rows + [jnp.zeros((6, 128), F32)], axis=0)
 
 
-def shares(messages, sums, events, plain, ordered):
+def shares(later, sums, events, plain, ordered):
     flat = jax.ShapeDtypeStruct(sums.shape, F32)
     return pl.pallas_call(
-        functools.partial(share_kernel, len(messages)),
-        in_specs=[VMEM] * (len(messages) + 4),
-        out_shape=[
-            flat,
-            flat,
-            jax.ShapeDtypeStruct((2 * plain.shape[0] + 8, 128), F32),
-            jax.ShapeDtypeStruct((8, 128), F32),
-        ],
-        out_specs=[VMEM] * 4,
+        share_kernel,
+        in_specs=[VMEM] * 5,
+        out_shape=[flat, flat, jax.ShapeDtypeStruct((2 * plain.shape[0] + 8, 128), F32)],
+        out_specs=[VMEM] * 3,
         compiler_params=pltpu.CompilerParams(**PARAMS),
         name="shares",
-    )(*messages, sums, events, plain, ordered)
+    )(later, sums, events, plain, ordered)
 
 
 def hazard_kernel(rows, hazard, square, rank, cumulative, squares):
@@ -334,6 +329,25 @@
     )(hazard, square, rank)
 
 
+def range_kernel(bit, count, *refs):
+    total, other, later = refs[:3]
+    total_out, later_out = refs[3 + count :]
+    is_later = (lax.axis_index("ex") & bit) == 0
+    later_out[...] = later[...] + jnp.where(is_later, other[...], 0.0)
+    total_out[...] = total[...] + other[...]
+
+
+def ranges(bit, total, other, later, waited):
+    return pl.pallas_call(
+        functools.partial(range_kernel, bit, len(waited)),
+        in_specs=[VMEM] * 3 + [pl.BlockSpec(memory_space=pl.ANY)] * len(waited),
+        out_shape=[jax.ShapeDtypeStruct(total.shape, F32)] * 2,
+        out_specs=[VMEM] * 2,
+        compiler_params=pltpu.CompilerParams(**PARAMS),
+        name="ranges",
+    )(total, other, later, *waited)
+
+
 def suffix_kernel(parts, own, other, *refs):
     messages, (risk, rank, table) = refs[:parts], refs[parts : parts + 3]
     tangent_out, sums, plain, lhs = refs[parts + 3 :]
@@ -341,12 +355,16 @@
     folded = jnp.zeros((kf, 128), F32)
     groups = rows // LO
     span = min(SPAN, rows)
-    powers = [jnp.exp2(from_short(part[:, rows + 2 * LO :])) for part in messages]
+    powers = [jnp.exp2(from_short(part[:, part.shape[1] - 128 :])) for part in messages]
+    half = rows // 2
+    later = len(messages) // 2
     for i in range(rows // span):
         at = slice(i * span, (i + 1) * span)
         tangent = own[:, at] + other[:, at]
-        for part, power in zip(messages, powers):
-            tangent = tangent + from_short(part[:, at]) * power[:, i : i + 1]
+        first = 0 if i * span < half else later
+        here = i - (first and half // span)
+        for part, power in zip(messages[first : first + later], powers[first : first + later]):
+            tangent = tangent + from_short(part[:, here * span : (here + 1) * span]) * power[:, here : here + 1]
         tangent_out[:, at] = tangent
         weighted = tangent * risk[:, at]
         folded = folded + sum(weighted[:, j : j + 128] for j in range(0, span, 128))
@@ -539,22 +557,23 @@
     )(mine, other)
 
 
-def finish_kernel(first, steps, mine, other, count, *refs):
-    out, total, sems = refs[-3:]
-    height = mine.shape[0] - 16
-    step = height // steps
+def finish_kernel(parts, *refs):
+    mine, other, count = refs[:parts], refs[parts : 2 * parts], refs[2 * parts]
+    out, total, sems = refs[2 * parts + 1 :]
+    step = mine[0].shape[0] - 16
     block = min(BLOCK, step)
-    scale = count[0:1, 0:1]
-    powers = [from_short(message[height:]) for message in (mine, other)]
+    scale = count[1:2, 0:1]
     copies = []
-    for i in range(steps):
-        for start in range(i * step, (i + 1) * step, block):
-            at, j = slice(start, start + block), start // block
-            terms = [from_short(m[at]) * jnp.exp2(p[j : j + 1]) for m, p in zip((mine, other), powers)]
-            total[at] = (terms[0] + terms[1]) / scale
+    for i in range(parts):
+        messages = (mine[i], other[i])
+        powers = [jnp.exp2(from_short(message[step:])) for message in messages]
+        for j in range(step // block):
+            at = slice(j * block, (j + 1) * block)
+            terms = [from_short(m[at]) * p[j : j + 1] for m, p in zip(messages, powers)]
+            total[i * step + j * block : i * step + (j + 1) * block] = (terms[0] + terms[1]) / scale
         copies.append(
             pltpu.make_async_copy(
-                total.at[pl.ds(i * step, step)], out.at[pl.ds(first + i * step, step)], sems.at[i]
+                total.at[pl.ds(i * step, step)], out.at[pl.ds(i * step, step)], sems.at[i]
             )
         )
         copies[i].start()
@@ -562,19 +581,18 @@
         copy.wait()
 
 
-def finish(mine, other, count, first, variants, done):
-    height, k = mine.shape[0] - 16, mine.shape[1]
-    steps = max(1, min(2, height // BLOCK))
-    return pl.pallas_call(
-        functools.partial(finish_kernel, first, steps),
-        in_specs=[VMEM] * 3 + [HBM] * len(done),
-        out_shape=jax.ShapeDtypeStruct((variants, k), F32),
+def finish(mine, other, count):
+    parts = len(mine)
+    height, k = parts * (mine[0].shape[0] - 16), mine[0].shape[1]
+    return pl.pallas_call(
+        functools.partial(finish_kernel, parts),
+        in_specs=[VMEM] * (2 * parts + 1),
+        out_shape=jax.ShapeDtypeStruct((height, k), F32),
         out_specs=HBM,
-        scratch_shapes=[pltpu.VMEM((height, k), F32), pltpu.SemaphoreType.DMA((steps,))],
-        input_output_aliases={3: 0} if done else {},
+        scratch_shapes=[pltpu.VMEM((height, k), F32), pltpu.SemaphoreType.DMA((parts,))],
         compiler_params=pltpu.CompilerParams(**PARAMS),
         name="finish",
-    )(mine, other, count, *done)
+    )(*mine, *other, count)
 
 
 def local(dosages, coefficients, directions, event_rank, events):
@@ -591,17 +609,25 @@
     linear, keep, send = products(dosages, coefficients, directions, feat)
     order = list(reversed(range(1, feat // 2)))
     received = {q: swap(send[q], "feat", 1) for q in order + [0]}
-    others, paired = [], linear
-    for q in order:
-        *first, message = join(paired, keep[q], received[q])
-        paired = first[0] if first else paired
-        others.append(swap(message, "feat", 2 * q))
+    paired = pair(linear, received[order[0]])
+    middle = rows // 2
+    firsts = [
+        swap(join(keep[q], received[q], 0, middle, paired, []), "feat", 2 * q) for q in order
+    ]
+    rests = [
+        swap(join(keep[q], received[q], middle, middle, paired, [received[0]]), "feat", 2 * q)
+        for q in order
+    ]
     table = tables(rank, paired, rows)
 
-    risk, sums, ordered_events, message = risks(paired, others, rank, event_row, table, rows)
-    messages = [message] + [swap(message, "ex", i) for i in range(1, ex)]
-    tangent, later_sums, plain = suffix_sums(keep[0], received[0], others, risk, rank, table)
-    hazard, ordered_squares, message, count = shares(messages, sums, ordered_events, plain, later_sums)
+    risk, sums, ordered_events, total = risks(paired, firsts, rank, event_row, table, rows)
+    later = jnp.zeros_like(total)
+    bit = 1
+    while bit < ex:
+        total, later = ranges(bit, total, swap(total, "ex", bit), later, rests if bit == 1 else [])
+        bit *= 2
+    tangent, later_sums, plain = suffix_sums(keep[0], received[0], firsts + rests, risk, rank, table)
+    hazard, ordered_squares, message = shares(later, sums, ordered_events, plain, later_sums)
     messages = [message] + [swap(message, "ex", i) for i in range(1, ex)]
     cumulative, squares = hazards(hazard, ordered_squares, rank, rows)
     summed = prefix_sums(later_sums, ordered_squares, rank, padded)
@@ -622,10 +648,7 @@
         partial_sums = [merge(mine, other) for mine, other in zip(partial_sums, received)]
         bit *= 2
     received = [swap(message, "ex", bit) for message in partial_sums]
-    done = []
-    for i in range(2):
-        done = [finish(partial_sums[i], received[i], count, i * half, variants, done)]
-    result = done[0]
+    result = finish(partial_sums, received, total)
     if padded != each:
         result = result.reshape(variants, feat, padded)[:, :, :each].reshape(variants, k)
     return result

time: 57.8 us -> 57.5 us (level)
  starting transfers between devices: 23.8 us -> 27.8 us
  waiting for transfers between devices: 19.9 us -> 15.9 us
    ppermute x24 -> x26, starting transfers between devices: 23.8 us -> 27.8 us  [swap(): return lax.ppermute(x, axis, [(s, s ^ i) for s in range(count)])]
    ppermute x24 -> x26, waiting for transfers between devices: 19.9 us -> 15.9 us  [swap(): return lax.ppermute(x, axis, [(s, s ^ i) for s in range(count)])]
    pallas_call x6 -> x11, Pallas kernels: 2.01 us -> 1.64 us  [the longest x1 0.76 us: finish(): pl.pallas_call(functools.partial(finish_kernel, parts), in_specs=[VMEM] *...]
  transfers between devices with their start and end apart: 24 -> 26, of which waited for: 12 -> 13; matrix products, arithmetic and copies ran while one was open for 0% -> 0% of each run, Pallas kernels for 15% -> 14%
where the time goes in v10:
time: 57.5 us; the launch traced here: 57.4 us
  starting transfers between devices  27.8 us (48%)
  waiting for transfers between devices  15.9 us (28%)
  Pallas kernels  13.5 us (23%)
    ppermute x26, starting transfers between devices, swap(): return lax.ppermute(x, axis, [(s, s ^ i) for s in range(count)])  27.8 us
    ppermute x26, waiting for transfers between devices, swap(): return lax.ppermute(x, axis, [(s, s ^ i) for s in range(count)])  15.9 us
    pallas_call x1, Pallas kernels, products(): pl.pallas_call(functools.partial(product_kernel, feat, kf, chunk), in_spe...  3.75 us
    pallas_call x1, Pallas kernels, suffix_sums(): pl.pallas_call(functools.partial(suffix_kernel, len(messages)), in_specs=...  2.25 us
    pallas_call x1, Pallas kernels, prefix_sums(): pl.pallas_call(prefix_kernel, in_specs=[VMEM] * 3, out_shape=jax.ShapeDty...  1.75 us
    pallas_call x2, Pallas kernels, gradients(): pl.pallas_call(functools.partial(gradient_kernel, feat, kf, start), in_sp...  1.29 us
  transfers between devices with their start and end apart: 26, of which 13 were waited for; matrix products, arithmetic and copies ran while one was open for 0% of the time, Pallas kernels for 14%

profile of v10, /device:TPU:0, one launch (start us, length us, event | category | flops | bytes accessed | tf_op | source)
XLA Modules:
  0.0 57.4 jit_solution(11451304271997048602)
XLA Ops:
  0.0 3.8 %products.1 = (f32[16,256]{1,0:T(8,128)S(1)}, f32[16,4096]{1,0:T(8,128)S(1)}, f32[16,4096]{1,0:T(8,128)S(1)}, f32[16,4096]{1,0:T(8,128)S(1)}, f32[16,4096]{1,0:T...) custom-call(bf16[512,128]{1,0:T(8,128)(2,1)} %directions.1, ...), custom_call_target="tpu_custom_call" | custom-call | flops 536870912 | bytes 6291456 | tf_op jit(solution)/shard_map/products/pallas_call | solution.py:118
  5.6 3.9 %collective-permute-start.1 = (s16[16,2688]{1,0:T(8,128)(2,1)S(1)}, s16[16,2688]{1,0:T(8,128)(2,1)S(1)}, u32[]{:S(2)}, u32[]{:S(2)}) collective-permute-start(s16[16,2688]{1,0:T(8,128)(2,1)S(1)} %join.6), channel_id=1, source_target_pairs={{0,6},{1,7},{2,4},{3,5},{4,2},{5,3},{6,0},{7,1},{8,14},{9,15},{10,... | collective-permute-start | bytes 258056 | tf_op jit(solution)/shard_map/ppermute | solution.py:23
  10.7 2.8 %collective-permute-start.8 = (s16[16,2176]{1,0:T(8,128)(2,1)S(1)}, s16[16,2176]{1,0:T(8,128)(2,1)S(1)}, u32[]{:S(2)}, u32[]{:S(2)}) collective-permute-start(s16[16,2176]{1,0:T(8,128)(2,1)S(1)} %join.9), channel_id=1, source_target_pairs={{0,6},{1,7},{2,4},{3,5},{4,2},{5,3},{6,0},{7,1},{8,14},{9,15},{10,... | collective-permute-start | bytes 208904 | tf_op jit(solution)/shard_map/ppermute | solution.py:23
  15.6 0.9 %risks.1 = (f32[1,4096]{1,0:T(1,128)S(1)}, f32[16,256]{1,0:T(8,128)S(1)}, f32[16,256]{1,0:T(8,128)S(1)}, f32[8,128]{1,0:T(8,128)S(1)}) custom-call(f32[16,256]{1,0:T(8,128)S(1)} %pair.1.refs_0_.waited.linear, s16[16,2688]{1,0:T(8,128)(2,1)S(1)} %collective-permute-done.1.refs_0_, s16[16,2688]{1,0:T(8,128)(2,1)S(1)} %collective-permute-done.3.refs_1_, ...), custom_call_target="tpu_custom_call" | custom-call | flops 134217728 | bytes 262144 | tf_op jit(solution)/shard_map/risks/pallas_call | solution.py:258
  16.5 1.7 %collective-permute-start.6 = (f32[8,128]{1,0:T(8,128)S(1)}, f32[8,128]{1,0:T(8,128)S(1)}, u32[]{:S(2)}, u32[]{:S(2)}) collective-permute-start(f32[8,128]{1,0:T(8,128)S(1)} %get-tuple-element.37.refs_0_), channel_id=1, source_target_pairs={{0,8},{8,0},{16,24},{24,16},{1,9},{9,1},{17,25},{25,17},{2,10},{10... | collective-permute-start | bytes 12296 | tf_op jit(solution)/shard_map/ppermute | solution.py:23
  18.7 1.4 %collective-permute-done.6.refs_1_ = f32[8,128]{1,0:T(8,128)S(1)} collective-permute-done((f32[8,128]{1,0:T(8,128)S(1)}, f32[8,128]{1,0:T(8,128)S(1)}, u32[]{:S(2)}, u32[]{:S(2)}) %collective-permute-start.6) | collective-permute-done | bytes 4128 | tf_op jit(solution)/shard_map/ppermute | solution.py:23
  20.2 2.7 %collective-permute-start.11 = (f32[8,128]{1,0:T(8,128)S(1)}, f32[8,128]{1,0:T(8,128)S(1)}, u32[]{:S(2)}, u32[]{:S(2)}) collective-permute-start(f32[8,128]{1,0:T(8,128)S(1)} %get-tuple-element.39.refs_0_), channel_id=1, source_target_pairs={{0,16},{8,24},{16,0},{24,8},{1,17},{9,25},{17,1},{25,9},{2,18},{10... | collective-permute-start | bytes 12296 | tf_op jit(solution)/shard_map/ppermute | solution.py:23
  22.9 2.3 %suffix_sums.1 = (f32[16,4096]{1,0:T(8,128)S(1)}, f32[256,256]{1,0:T(8,128)S(1)}, f32[16,128]{1,0:T(8,128)S(1)}) custom-call(f32[16,4096]{1,0:T(8,128)S(1)} %get-tuple-element.44.own, f32[16,4096]{1,0:T(8,128)S(1)} %collective-permute-done.7.refs_1_.other, s16[16,2688]{1,0:T(8,128)(2,1)S(1)} %collective-permute-done.1.refs_0_, ...), custom_call_target="tpu_custom_call" | custom-call | flops 1073741824 | bytes 1572864 | tf_op jit(solution)/shard_map/suffix_sums/pallas_call | solution.py:398
  25.3 3.2 %collective-permute-start.14 = (f32[40,128]{1,0:T(8,128)S(1)}, f32[40,128]{1,0:T(8,128)S(1)}, u32[]{:S(2)}, u32[]{:S(2)}) collective-permute-start(f32[40,128]{1,0:T(8,128)S(1)} %get-tuple-element.48.refs_0_), channel_id=1, source_target_pairs={{0,24},{8,16},{16,8},{24,0},{1,25},{9,17},{17,9},{25,1},{2,26},{10... | collective-permute-start | bytes 61448 | tf_op jit(solution)/shard_map/ppermute | solution.py:23
  28.6 1.2 %collective-permute-start.12 = (f32[40,128]{1,0:T(8,128)S(1)}, f32[40,128]{1,0:T(8,128)S(1)}, u32[]{:S(2)}, u32[]{:S(2)}) collective-permute-start(f32[40,128]{1,0:T(8,128)S(1)} %get-tuple-element.48.refs_0_), channel_id=1, source_target_pairs={{0,8},{8,0},{16,24},{24,16},{1,9},{9,1},{17,25},{25,17},{2,10},{10... | collective-permute-start | bytes 61448 | tf_op jit(solution)/shard_map/ppermute | solution.py:23
  29.7 1.8 %prefix_sums.1.refs_5_ = f32[16,4096]{1,0:T(8,128)S(1)} custom-call(f32[256,256]{1,0:T(8,128)S(1)} %get-tuple-element.47.ordered.sums, f32[16,256]{1,0:T(8,128)S(1)} %get-tuple-element.50.squares.square, s32[1,4096]{1,0:T(1,128)S(1)} %bitcast.5), custom_call_target="tpu_custom_call" | custom-call | flops 1073741824 | bytes 1572864 | tf_op jit(solution)/shard_map/prefix_sums/pallas_call | solution.py:443
  31.5 0.9 %hazards.1 = (f32[1,4096]{1,0:T(1,128)S(1)}, f32[1,4096]{1,0:T(1,128)S(1)}) custom-call(f32[16,256]{1,0:T(8,128)S(1)} %get-tuple-element.51.hazard, f32[16,256]{1,0:T(8,128)S(1)} %get-tuple-element.50.squares.square, s32[1,4096]{1,0:T(1,128)S(1)} %bitcast.6), custom_call_target="tpu_custom_call" | custom-call | flops 209715200 | bytes 262144 | tf_op jit(solution)/shard_map/hazards/pallas_call | solution.py:321
  32.4 0.9 %collective-permute-done.13.refs_2_ = f32[40,128]{1,0:T(8,128)S(1)} collective-permute-done((f32[40,128]{1,0:T(8,128)S(1)}, f32[40,128]{1,0:T(8,128)S(1)}, u32[]{:S(2)}, u32[]{:S(2)}) %collective-permute-start.13) | collective-permute-done | bytes 20512 | tf_op jit(solution)/shard_map/ppermute | solution.py:23
  33.5 2.5 %collective-permute-start.20 = (bf16[16,4096]{1,0:T(8,128)(2,1)S(1)}, bf16[16,4096]{1,0:T(8,128)(2,1)S(1)}, u32[]{:S(2)}, u32[]{:S(2)}) collective-permute-start(bf16[16,4096]{1,0:T(8,128)(2,1)S(1)} %weights.1.refs_0_), channel_id=1, source_target_pairs={{0,6},{1,7},{2,4},{3,5},{4,2},{5,3},{6,0},{7,1},{8,14},{9,15},{10,... | collective-permute-start | bytes 393224 | tf_op jit(solution)/shard_map/ppermute | solution.py:23
  37.0 2.4 %collective-permute-done.20.refs_6_ = bf16[16,4096]{1,0:T(8,128)(2,1)S(1)} collective-permute-done((bf16[16,4096]{1,0:T(8,128)(2,1)S(1)}, bf16[16,4096]{1,0:T(8,128)(2,1)S(1)}, u32[]{:S(2)}, u32[]{:S(2)}) %collective-permute-start.20) | collective-permute-done | bytes 131104 | tf_op jit(solution)/shard_map/ppermute | solution.py:23
  39.4 1.5 %collective-permute-done.18.refs_4_ = bf16[16,4096]{1,0:T(8,128)(2,1)S(1)} collective-permute-done((bf16[16,4096]{1,0:T(8,128)(2,1)S(1)}, bf16[16,4096]{1,0:T(8,128)(2,1)S(1)}, u32[]{:S(2)}, u32[]{:S(2)}) %collective-permute-start.18) | collective-permute-done | bytes 131104 | tf_op jit(solution)/shard_map/ppermute | solution.py:23
  41.5 0.8 %collective-permute-done.19.refs_5_ = bf16[16,4096]{1,0:T(8,128)(2,1)S(1)} collective-permute-done((bf16[16,4096]{1,0:T(8,128)(2,1)S(1)}, bf16[16,4096]{1,0:T(8,128)(2,1)S(1)}, u32[]{:S(2)}, u32[]{:S(2)}) %collective-permute-start.19) | collective-permute-done | bytes 131104 | tf_op jit(solution)/shard_map/ppermute | solution.py:23
  44.4 1.8 %collective-permute-start.23 = (s16[272,128]{1,0:T(8,128)(2,1)S(1)}, s16[272,128]{1,0:T(8,128)(2,1)S(1)}, u32[]{:S(2)}, u32[]{:S(2)}) collective-permute-start(s16[272,128]{1,0:T(8,128)(2,1)S(1)} %gradients.3.mine), channel_id=1, source_target_pairs={{0,8},{8,0},{16,24},{24,16},{1,9},{9,1},{17,25},{25,17},{2,10},{10... | collective-permute-start | bytes 208904 | tf_op jit(solution)/shard_map/ppermute | solution.py:23
  46.3 2.2 %collective-permute-done.22.other = s16[272,128]{1,0:T(8,128)(2,1)S(1)} collective-permute-done((s16[272,128]{1,0:T(8,128)(2,1)S(1)}, s16[272,128]{1,0:T(8,128)(2,1)S(1)}, u32[]{:S(2)}, u32[]{:S(2)}) %collective-permute-start.22) | collective-permute-done | bytes 69664 | tf_op jit(solution)/shard_map/ppermute | solution.py:23
  48.6 1.7 %collective-permute-start.24 = (s16[272,128]{1,0:T(8,128)(2,1)S(1)}, s16[272,128]{1,0:T(8,128)(2,1)S(1)}, u32[]{:S(2)}, u32[]{:S(2)}) collective-permute-start(s16[272,128]{1,0:T(8,128)(2,1)S(1)} %merge.2.refs_0_), channel_id=1, source_target_pairs={{0,16},{8,24},{16,0},{24,8},{1,17},{9,25},{17,1},{25,9},{2,18},{10... | collective-permute-start | bytes 208904 | tf_op jit(solution)/shard_map/ppermute | solution.py:23
  50.3 2.1 %collective-permute-start.25 = (s16[272,128]{1,0:T(8,128)(2,1)S(1)}, s16[272,128]{1,0:T(8,128)(2,1)S(1)}, u32[]{:S(2)}, u32[]{:S(2)}) collective-permute-start(s16[272,128]{1,0:T(8,128)(2,1)S(1)} %merge.3.refs_1_), channel_id=1, source_target_pairs={{0,16},{8,24},{16,0},{24,8},{1,17},{9,25},{17,1},{25,9},{2,18},{10... | collective-permute-start | bytes 208904 | tf_op jit(solution)/shard_map/ppermute | solution.py:23
  52.4 2.7 %collective-permute-done.24.refs_2_ = s16[272,128]{1,0:T(8,128)(2,1)S(1)} collective-permute-done((s16[272,128]{1,0:T(8,128)(2,1)S(1)}, s16[272,128]{1,0:T(8,128)(2,1)S(1)}, u32[]{:S(2)}, u32[]{:S(2)}) %collective-permute-start.24) | collective-permute-done | bytes 69664 | tf_op jit(solution)/shard_map/ppermute | solution.py:23
  55.1 1.5 %collective-permute-done.25.refs_3_ = s16[272,128]{1,0:T(8,128)(2,1)S(1)} collective-permute-done((s16[272,128]{1,0:T(8,128)(2,1)S(1)}, s16[272,128]{1,0:T(8,128)(2,1)S(1)}, u32[]{:S(2)}, u32[]{:S(2)}) %collective-permute-start.25) | collective-permute-done | bytes 69664 | tf_op jit(solution)/shard_map/ppermute | solution.py:23
  56.6 0.8 %finish.1 = f32[512,128]{1,0:T(8,128)} custom-call(s16[272,128]{1,0:T(8,128)(2,1)S(1)} %merge.2.refs_0_, s16[272,128]{1,0:T(8,128)(2,1)S(1)} %merge.3.refs_1_, s16[272,128]{1,0:T(8,128)(2,1)S(1)} %collective-permute-done.24.refs_2_, s16[272,128]{1,0:T(8,128)(2,1)S(1)} %collective-permute-done.25.refs_3_, f32[8,128]{1,0:T(8,128)S(1)} %get-tuple-element.54.refs_4_), custom_call_target="tpu_custom_call" | custom-call | tf_op jit(solution)/shard_map/finish/pallas_call | solution.py:587
  (57 shorter events, 9.8 us)
Async XLA Ops:
  3.8 1.7 %collective-permute-start = (f32[16,4352]{1,0:T(8,128)S(1)}, f32[16,4352]{1,0:T(8,128)S(1)}, u32[]{:S(2)}, u32[]{:S(2)}) collective-permute-start(f32[16,4352]{1,0:T(8,128)S(1)} %get-tuple-element.31), channel_id=1, source_target_pairs={{0,1},{1,0},{2,3},{3,2},{4,5},{5,4},{6,7},{7,6},{8,9},{9,8},{10,11... | collective-permute-start | bytes 835592 | tf_op jit(solution)/shard_map/ppermute | solution.py:23
  4.3 5.2 %collective-permute-start.2 = (f32[16,4096]{1,0:T(8,128)S(1)}, f32[16,4096]{1,0:T(8,128)S(1)}, u32[]{:S(2)}, u32[]{:S(2)}) collective-permute-start(f32[16,4096]{1,0:T(8,128)S(1)} %get-tuple-element.34), channel_id=1, source_target_pairs={{0,1},{1,0},{2,3},{3,2},{4,5},{5,4},{6,7},{7,6},{8,9},{9,8},{10,11... | collective-permute-start | bytes 786440 | tf_op jit(solution)/shard_map/ppermute | solution.py:23
  4.4 5.8 %collective-permute-start.4 = (f32[16,4096]{1,0:T(8,128)S(1)}, f32[16,4096]{1,0:T(8,128)S(1)}, u32[]{:S(2)}, u32[]{:S(2)}) collective-permute-start(f32[16,4096]{1,0:T(8,128)S(1)} %get-tuple-element.36), channel_id=1, source_target_pairs={{0,1},{1,0},{2,3},{3,2},{4,5},{5,4},{6,7},{7,6},{8,9},{9,8},{10,11... | collective-permute-start | bytes 786440 | tf_op jit(solution)/shard_map/ppermute | solution.py:23
  4.8 5.8 %collective-permute-start.7 = (f32[16,4096]{1,0:T(8,128)S(1)}, f32[16,4096]{1,0:T(8,128)S(1)}, u32[]{:S(2)}, u32[]{:S(2)}) collective-permute-start(f32[16,4096]{1,0:T(8,128)S(1)} %get-tuple-element.38), channel_id=1, source_target_pairs={{0,1},{1,0},{2,3},{3,2},{4,5},{5,4},{6,7},{7,6},{8,9},{9,8},{10,11... | collective-permute-start | bytes 786440 | tf_op jit(solution)/shard_map/ppermute | solution.py:23
  5.6 8.8 %collective-permute-start.1 = (s16[16,2688]{1,0:T(8,128)(2,1)S(1)}, s16[16,2688]{1,0:T(8,128)(2,1)S(1)}, u32[]{:S(2)}, u32[]{:S(2)}) collective-permute-start(s16[16,2688]{1,0:T(8,128)(2,1)S(1)} %join.6), channel_id=1, source_target_pairs={{0,6},{1,7},{2,4},{3,5},{4,2},{5,3},{6,0},{7,1},{8,14},{9,15},{10,... | collective-permute-start | bytes 258056 | tf_op jit(solution)/shard_map/ppermute | solution.py:23
  9.6 5.7 %collective-permute-start.3 = (s16[16,2688]{1,0:T(8,128)(2,1)S(1)}, s16[16,2688]{1,0:T(8,128)(2,1)S(1)}, u32[]{:S(2)}, u32[]{:S(2)}) collective-permute-start(s16[16,2688]{1,0:T(8,128)(2,1)S(1)} %join.7), channel_id=1, source_target_pairs={{0,4},{1,5},{2,6},{3,7},{4,0},{5,1},{6,2},{7,3},{8,12},{9,13},{10,... | collective-permute-start | bytes 258056 | tf_op jit(solution)/shard_map/ppermute | solution.py:23
  10.3 5.3 %collective-permute-start.5 = (s16[16,2688]{1,0:T(8,128)(2,1)S(1)}, s16[16,2688]{1,0:T(8,128)(2,1)S(1)}, u32[]{:S(2)}, u32[]{:S(2)}) collective-permute-start(s16[16,2688]{1,0:T(8,128)(2,1)S(1)} %join.8), channel_id=1, source_target_pairs={{0,2},{1,3},{2,0},{3,1},{4,6},{5,7},{6,4},{7,5},{8,10},{9,11},{10,... | collective-permute-start | bytes 258056 | tf_op jit(solution)/shard_map/ppermute | solution.py:23
  10.7 7.5 %collective-permute-start.8 = (s16[16,2176]{1,0:T(8,128)(2,1)S(1)}, s16[16,2176]{1,0:T(8,128)(2,1)S(1)}, u32[]{:S(2)}, u32[]{:S(2)}) collective-permute-start(s16[16,2176]{1,0:T(8,128)(2,1)S(1)} %join.9), channel_id=1, source_target_pairs={{0,6},{1,7},{2,4},{3,5},{4,2},{5,3},{6,0},{7,1},{8,14},{9,15},{10,... | collective-permute-start | bytes 208904 | tf_op jit(solution)/shard_map/ppermute | solution.py:23
  13.7 4.5 %collective-permute-start.9 = (s16[16,2176]{1,0:T(8,128)(2,1)S(1)}, s16[16,2176]{1,0:T(8,128)(2,1)S(1)}, u32[]{:S(2)}, u32[]{:S(2)}) collective-permute-start(s16[16,2176]{1,0:T(8,128)(2,1)S(1)} %join.10), channel_id=1, source_target_pairs={{0,4},{1,5},{2,6},{3,7},{4,0},{5,1},{6,2},{7,3},{8,12},{9,13},{10,... | collective-permute-start | bytes 208904 | tf_op jit(solution)/shard_map/ppermute | solution.py:23
  14.4 4.4 %collective-permute-start.10 = (s16[16,2176]{1,0:T(8,128)(2,1)S(1)}, s16[16,2176]{1,0:T(8,128)(2,1)S(1)}, u32[]{:S(2)}, u32[]{:S(2)}) collective-permute-start(s16[16,2176]{1,0:T(8,128)(2,1)S(1)} %join.11), channel_id=1, source_target_pairs={{0,2},{1,3},{2,0},{3,1},{4,6},{5,7},{6,4},{7,5},{8,10},{9,11},{10,... | collective-permute-start | bytes 208904 | tf_op jit(solution)/shard_map/ppermute | solution.py:23
  16.5 3.7 %collective-permute-start.6 = (f32[8,128]{1,0:T(8,128)S(1)}, f32[8,128]{1,0:T(8,128)S(1)}, u32[]{:S(2)}, u32[]{:S(2)}) collective-permute-start(f32[8,128]{1,0:T(8,128)S(1)} %get-tuple-element.37.refs_0_), channel_id=1, source_target_pairs={{0,8},{8,0},{16,24},{24,16},{1,9},{9,1},{17,25},{25,17},{2,10},{10... | collective-permute-start | bytes 12296 | tf_op jit(solution)/shard_map/ppermute | solution.py:23
  20.2 5.0 %collective-permute-start.11 = (f32[8,128]{1,0:T(8,128)S(1)}, f32[8,128]{1,0:T(8,128)S(1)}, u32[]{:S(2)}, u32[]{:S(2)}) collective-permute-start(f32[8,128]{1,0:T(8,128)S(1)} %get-tuple-element.39.refs_0_), channel_id=1, source_target_pairs={{0,16},{8,24},{16,0},{24,8},{1,17},{9,25},{17,1},{25,9},{2,18},{10... | collective-permute-start | bytes 12296 | tf_op jit(solution)/shard_map/ppermute | solution.py:23
  25.3 7.1 %collective-permute-start.14 = (f32[40,128]{1,0:T(8,128)S(1)}, f32[40,128]{1,0:T(8,128)S(1)}, u32[]{:S(2)}, u32[]{:S(2)}) collective-permute-start(f32[40,128]{1,0:T(8,128)S(1)} %get-tuple-element.48.refs_0_), channel_id=1, source_target_pairs={{0,24},{8,16},{16,8},{24,0},{1,25},{9,17},{17,9},{25,1},{2,26},{10... | collective-permute-start | bytes 61448 | tf_op jit(solution)/shard_map/ppermute | solution.py:23
  28.6 4.7 %collective-permute-start.13 = (f32[40,128]{1,0:T(8,128)S(1)}, f32[40,128]{1,0:T(8,128)S(1)}, u32[]{:S(2)}, u32[]{:S(2)}) collective-permute-start(f32[40,128]{1,0:T(8,128)S(1)} %get-tuple-element.48.refs_0_), channel_id=1, source_target_pairs={{0,16},{8,24},{16,0},{24,8},{1,17},{9,25},{17,1},{25,9},{2,18},{10... | collective-permute-start | bytes 61448 | tf_op jit(solution)/shard_map/ppermute | solution.py:23
  28.6 4.7 %collective-permute-start.12 = (f32[40,128]{1,0:T(8,128)S(1)}, f32[40,128]{1,0:T(8,128)S(1)}, u32[]{:S(2)}, u32[]{:S(2)}) collective-permute-start(f32[40,128]{1,0:T(8,128)S(1)} %get-tuple-element.48.refs_0_), channel_id=1, source_target_pairs={{0,8},{8,0},{16,24},{24,16},{1,9},{9,1},{17,25},{25,17},{2,10},{10... | collective-permute-start | bytes 61448 | tf_op jit(solution)/shard_map/ppermute | solution.py:23
  33.5 5.9 %collective-permute-start.20 = (bf16[16,4096]{1,0:T(8,128)(2,1)S(1)}, bf16[16,4096]{1,0:T(8,128)(2,1)S(1)}, u32[]{:S(2)}, u32[]{:S(2)}) collective-permute-start(bf16[16,4096]{1,0:T(8,128)(2,1)S(1)} %weights.1.refs_0_), channel_id=1, source_target_pairs={{0,6},{1,7},{2,4},{3,5},{4,2},{5,3},{6,0},{7,1},{8,14},{9,15},{10,... | collective-permute-start | bytes 393224 | tf_op jit(solution)/shard_map/ppermute | solution.py:23
  36.0 5.0 %collective-permute-start.18 = (bf16[16,4096]{1,0:T(8,128)(2,1)S(1)}, bf16[16,4096]{1,0:T(8,128)(2,1)S(1)}, u32[]{:S(2)}, u32[]{:S(2)}) collective-permute-start(bf16[16,4096]{1,0:T(8,128)(2,1)S(1)} %weights.1.refs_0_), channel_id=1, source_target_pairs={{0,4},{1,5},{2,6},{3,7},{4,0},{5,1},{6,2},{7,3},{8,12},{9,13},{10,... | collective-permute-start | bytes 393224 | tf_op jit(solution)/shard_map/ppermute | solution.py:23
  36.5 5.0 %collective-permute-start.16 = (bf16[16,4096]{1,0:T(8,128)(2,1)S(1)}, bf16[16,4096]{1,0:T(8,128)(2,1)S(1)}, u32[]{:S(2)}, u32[]{:S(2)}) collective-permute-start(bf16[16,4096]{1,0:T(8,128)(2,1)S(1)} %weights.1.refs_0_), channel_id=1, source_target_pairs={{0,2},{1,3},{2,0},{3,1},{4,6},{5,7},{6,4},{7,5},{8,10},{9,11},{10,... | collective-permute-start | bytes 393224 | tf_op jit(solution)/shard_map/ppermute | solution.py:23
  37.0 4.4 %collective-permute-start.15 = (bf16[16,4096]{1,0:T(8,128)(2,1)S(1)}, bf16[16,4096]{1,0:T(8,128)(2,1)S(1)}, u32[]{:S(2)}, u32[]{:S(2)}) collective-permute-start(bf16[16,4096]{1,0:T(8,128)(2,1)S(1)} %weights.1.refs_0_), channel_id=1, source_target_pairs={{0,1},{1,0},{2,3},{3,2},{4,5},{5,4},{6,7},{7,6},{8,9},{9,8},{10,11... | collective-permute-start | bytes 393224 | tf_op jit(solution)/shard_map/ppermute | solution.py:23
  39.4 2.1 %collective-permute-start.21 = (bf16[16,4096]{1,0:T(8,128)(2,1)S(1)}, bf16[16,4096]{1,0:T(8,128)(2,1)S(1)}, u32[]{:S(2)}, u32[]{:S(2)}) collective-permute-start(bf16[16,4096]{1,0:T(8,128)(2,1)S(1)} %collective-permute-done.20.refs_6_), channel_id=1, source_target_pairs={{0,1},{1,0},{2,3},{3,2},{4,5},{5,4},{6,7},{7,6},{8,9},{9,8},{10,11... | collective-permute-start | bytes 393224 | tf_op jit(solution)/shard_map/ppermute | solution.py:23
  43.5 5.0 %collective-permute-start.22 = (s16[272,128]{1,0:T(8,128)(2,1)S(1)}, s16[272,128]{1,0:T(8,128)(2,1)S(1)}, u32[]{:S(2)}, u32[]{:S(2)}) collective-permute-start(s16[272,128]{1,0:T(8,128)(2,1)S(1)} %gradients.2.mine), channel_id=1, source_target_pairs={{0,8},{8,0},{16,24},{24,16},{1,9},{9,1},{17,25},{25,17},{2,10},{10... | collective-permute-start | bytes 208904 | tf_op jit(solution)/shard_map/ppermute | solution.py:23
  44.4 5.8 %collective-permute-start.23 = (s16[272,128]{1,0:T(8,128)(2,1)S(1)}, s16[272,128]{1,0:T(8,128)(2,1)S(1)}, u32[]{:S(2)}, u32[]{:S(2)}) collective-permute-start(s16[272,128]{1,0:T(8,128)(2,1)S(1)} %gradients.3.mine), channel_id=1, source_target_pairs={{0,8},{8,0},{16,24},{24,16},{1,9},{9,1},{17,25},{25,17},{2,10},{10... | collective-permute-start | bytes 208904 | tf_op jit(solution)/shard_map/ppermute | solution.py:23
  48.6 6.5 %collective-permute-start.24 = (s16[272,128]{1,0:T(8,128)(2,1)S(1)}, s16[272,128]{1,0:T(8,128)(2,1)S(1)}, u32[]{:S(2)}, u32[]{:S(2)}) collective-permute-start(s16[272,128]{1,0:T(8,128)(2,1)S(1)} %merge.2.refs_0_), channel_id=1, source_target_pairs={{0,16},{8,24},{16,0},{24,8},{1,17},{9,25},{17,1},{25,9},{2,18},{10... | collective-permute-start | bytes 208904 | tf_op jit(solution)/shard_map/ppermute | solution.py:23
  50.3 6.3 %collective-permute-start.25 = (s16[272,128]{1,0:T(8,128)(2,1)S(1)}, s16[272,128]{1,0:T(8,128)(2,1)S(1)}, u32[]{:S(2)}, u32[]{:S(2)}) collective-permute-start(s16[272,128]{1,0:T(8,128)(2,1)S(1)} %merge.3.refs_1_), channel_id=1, source_target_pairs={{0,16},{8,24},{16,0},{24,8},{1,17},{9,25},{17,1},{25,9},{2,18},{10... | collective-permute-start | bytes 208904 | tf_op jit(solution)/shard_map/ppermute | solution.py:23
  (5 other events, 49.1 us)

commit v11 on v10

--- a/solution.py
+++ b/solution.py
@@ -356,8 +356,8 @@
     groups = rows // LO
     span = min(SPAN, rows)
     powers = [jnp.exp2(from_short(part[:, part.shape[1] - 128 :])) for part in messages]
-    half = rows // 2
     later = len(messages) // 2
+    half = messages[0].shape[1] - 2 * LO - 128
     for i in range(rows // span):
         at = slice(i * span, (i + 1) * span)
         tangent = own[:, at] + other[:, at]
@@ -610,21 +610,21 @@
     order = list(reversed(range(1, feat // 2)))
     received = {q: swap(send[q], "feat", 1) for q in order + [0]}
     paired = pair(linear, received[order[0]])
-    middle = rows // 2
+    middle = min(SPAN, rows // 2)
     firsts = [
         swap(join(keep[q], received[q], 0, middle, paired, []), "feat", 2 * q) for q in order
     ]
+    table = tables(rank, paired, rows)
+
+    risk, sums, ordered_events, total = risks(paired, firsts, rank, event_row, table, rows)
     rests = [
-        swap(join(keep[q], received[q], middle, middle, paired, [received[0]]), "feat", 2 * q)
+        swap(join(keep[q], received[q], middle, rows - middle, paired, [received[0], total]), "feat", 2 * q)
         for q in order
     ]
-    table = tables(rank, paired, rows)
-
-    risk, sums, ordered_events, total = risks(paired, firsts, rank, event_row, table, rows)
     later = jnp.zeros_like(total)
     bit = 1
     while bit < ex:
-        total, later = ranges(bit, total, swap(total, "ex", bit), later, rests if bit == 1 else [])
+        total, later = ranges(bit, total, swap(total, "ex", bit), later, rests if 2 * bit == ex else [])
         bit *= 2
     tangent, later_sums, plain = suffix_sums(keep[0], received[0], firsts + rests, risk, rank, table)
     hazard, ordered_squares, message = shares(later, sums, ordered_events, plain, later_sums)

time: 57.5 us -> 60.1 us (1.045)
  waiting for transfers between devices: 15.9 us -> 18.8 us
    ppermute x26, waiting for transfers between devices: 15.9 us -> 18.8 us  [swap(): return lax.ppermute(x, axis, [(s, s ^ i) for s in range(count)])]
  transfers between devices with their start and end apart: 26 -> 26, of which waited for: 13 -> 14; matrix products, arithmetic and copies ran while one was open for 0% -> 0% of each run, Pallas kernels for 14% -> 13%
where the time goes in v11:
time: 60.1 us; the launch traced here: 59.9 us
  starting transfers between devices  27.4 us (46%)
  waiting for transfers between devices  18.8 us (31%)
  Pallas kernels  13.5 us (22%)
    ppermute x26, starting transfers between devices, swap(): return lax.ppermute(x, axis, [(s, s ^ i) for s in range(count)])  27.4 us
    ppermute x26, waiting for transfers between devices, swap(): return lax.ppermute(x, axis, [(s, s ^ i) for s in range(count)])  18.8 us
    pallas_call x1, Pallas kernels, products(): pl.pallas_call(functools.partial(product_kernel, feat, kf, chunk), in_spe...  3.76 us
    pallas_call x1, Pallas kernels, suffix_sums(): pl.pallas_call(functools.partial(suffix_kernel, len(messages)), in_specs=...  2.27 us
    pallas_call x1, Pallas kernels, prefix_sums(): pl.pallas_call(prefix_kernel, in_specs=[VMEM] * 3, out_shape=jax.ShapeDty...  1.75 us
    pallas_call x2, Pallas kernels, gradients(): pl.pallas_call(functools.partial(gradient_kernel, feat, kf, start), in_sp...  1.29 us
  transfers between devices with their start and end apart: 26, of which 14 were waited for; matrix products, arithmetic and copies ran while one was open for 0% of the time, Pallas kernels for 13%

profile of v11, /device:TPU:0, one launch (start us, length us, event | category | flops | bytes accessed | tf_op | source)
XLA Modules:
  0.0 59.9 jit_solution(15767369663626259541)
XLA Ops:
  0.0 3.8 %products.1 = (f32[16,256]{1,0:T(8,128)S(1)}, f32[16,4096]{1,0:T(8,128)S(1)}, f32[16,4096]{1,0:T(8,128)S(1)}, f32[16,4096]{1,0:T(8,128)S(1)}, f32[16,4096]{1,0:T...) custom-call(bf16[512,128]{1,0:T(8,128)(2,1)} %directions.1, ...), custom_call_target="tpu_custom_call" | custom-call | flops 536870912 | bytes 6291456 | tf_op jit(solution)/shard_map/products/pallas_call | solution.py:118
  5.6 3.9 %collective-permute-start.1 = (s16[16,1152]{1,0:T(8,128)(2,1)S(1)}, s16[16,1152]{1,0:T(8,128)(2,1)S(1)}, u32[]{:S(2)}, u32[]{:S(2)}) collective-permute-start(s16[16,1152]{1,0:T(8,128)(2,1)S(1)} %join.6), channel_id=1, source_target_pairs={{0,6},{1,7},{2,4},{3,5},{4,2},{5,3},{6,0},{7,1},{8,14},{9,15},{10,... | collective-permute-start | bytes 110600 | tf_op jit(solution)/shard_map/ppermute | solution.py:23
  11.4 2.2 %collective-permute-done.3.refs_1_ = s16[16,1152]{1,0:T(8,128)(2,1)S(1)} collective-permute-done((s16[16,1152]{1,0:T(8,128)(2,1)S(1)}, s16[16,1152]{1,0:T(8,128)(2,1)S(1)}, u32[]{:S(2)}, u32[]{:S(2)}) %collective-permute-start.3) | collective-permute-done | bytes 36896 | tf_op jit(solution)/shard_map/ppermute | solution.py:23
  14.3 0.9 %risks.1 = (f32[1,4096]{1,0:T(1,128)S(1)}, f32[16,256]{1,0:T(8,128)S(1)}, f32[16,256]{1,0:T(8,128)S(1)}, f32[8,128]{1,0:T(8,128)S(1)}) custom-call(f32[16,256]{1,0:T(8,128)S(1)} %pair.1.refs_0_.waited.linear, s16[16,1152]{1,0:T(8,128)(2,1)S(1)} %collective-permute-done.1.refs_0_, s16[16,1152]{1,0:T(8,128)(2,1)S(1)} %collective-permute-done.3.refs_1_, ...), custom_call_target="tpu_custom_call" | custom-call | flops 134217728 | bytes 262144 | tf_op jit(solution)/shard_map/risks/pallas_call | solution.py:258
  15.4 1.6 %collective-permute-start.10 = (s16[16,3712]{1,0:T(8,128)(2,1)S(1)}, s16[16,3712]{1,0:T(8,128)(2,1)S(1)}, u32[]{:S(2)}, u32[]{:S(2)}) collective-permute-start(s16[16,3712]{1,0:T(8,128)(2,1)S(1)} %join.10), channel_id=1, source_target_pairs={{0,4},{1,5},{2,6},{3,7},{4,0},{5,1},{6,2},{7,3},{8,12},{9,13},{10,... | collective-permute-start | bytes 356360 | tf_op jit(solution)/shard_map/ppermute | solution.py:23
  17.8 1.5 %collective-permute-start.9 = (s16[16,3712]{1,0:T(8,128)(2,1)S(1)}, s16[16,3712]{1,0:T(8,128)(2,1)S(1)}, u32[]{:S(2)}, u32[]{:S(2)}) collective-permute-start(s16[16,3712]{1,0:T(8,128)(2,1)S(1)} %join.9), channel_id=1, source_target_pairs={{0,6},{1,7},{2,4},{3,5},{4,2},{5,3},{6,0},{7,1},{8,14},{9,15},{10,... | collective-permute-start | bytes 356360 | tf_op jit(solution)/shard_map/ppermute | solution.py:23
  19.3 1.6 %collective-permute-start.6 = (f32[8,128]{1,0:T(8,128)S(1)}, f32[8,128]{1,0:T(8,128)S(1)}, u32[]{:S(2)}, u32[]{:S(2)}) collective-permute-start(f32[8,128]{1,0:T(8,128)S(1)} %get-tuple-element.37.refs_0_.refs_2_), channel_id=1, source_target_pairs={{0,8},{8,0},{16,24},{24,16},{1,9},{9,1},{17,25},{25,17},{2,10},{10... | collective-permute-start | bytes 12296 | tf_op jit(solution)/shard_map/ppermute | solution.py:23
  20.9 2.0 %collective-permute-done.6.refs_1_ = f32[8,128]{1,0:T(8,128)S(1)} collective-permute-done((f32[8,128]{1,0:T(8,128)S(1)}, f32[8,128]{1,0:T(8,128)S(1)}, u32[]{:S(2)}, u32[]{:S(2)}) %collective-permute-start.6) | collective-permute-done | bytes 4128 | tf_op jit(solution)/shard_map/ppermute | solution.py:23
  22.9 2.6 %collective-permute-start.7 = (f32[8,128]{1,0:T(8,128)S(1)}, f32[8,128]{1,0:T(8,128)S(1)}, u32[]{:S(2)}, u32[]{:S(2)}) collective-permute-start(f32[8,128]{1,0:T(8,128)S(1)} %get-tuple-element.38.refs_0_), channel_id=1, source_target_pairs={{0,16},{8,24},{16,0},{24,8},{1,17},{9,25},{17,1},{25,9},{2,18},{10... | collective-permute-start | bytes 12296 | tf_op jit(solution)/shard_map/ppermute | solution.py:23
  25.6 2.3 %suffix_sums.1 = (f32[16,4096]{1,0:T(8,128)S(1)}, f32[256,256]{1,0:T(8,128)S(1)}, f32[16,128]{1,0:T(8,128)S(1)}) custom-call(f32[16,4096]{1,0:T(8,128)S(1)} %get-tuple-element.44.own, f32[16,4096]{1,0:T(8,128)S(1)} %collective-permute-done.8.refs_1_.other, s16[16,1152]{1,0:T(8,128)(2,1)S(1)} %collective-permute-done.1.refs_0_, ...), custom_call_target="tpu_custom_call" | custom-call | flops 1073741824 | bytes 1572864 | tf_op jit(solution)/shard_map/suffix_sums/pallas_call | solution.py:398
  28.0 3.2 %collective-permute-start.14 = (f32[40,128]{1,0:T(8,128)S(1)}, f32[40,128]{1,0:T(8,128)S(1)}, u32[]{:S(2)}, u32[]{:S(2)}) collective-permute-start(f32[40,128]{1,0:T(8,128)S(1)} %get-tuple-element.48.refs_0_), channel_id=1, source_target_pairs={{0,24},{8,16},{16,8},{24,0},{1,25},{9,17},{17,9},{25,1},{2,26},{10... | collective-permute-start | bytes 61448 | tf_op jit(solution)/shard_map/ppermute | solution.py:23
  31.3 1.2 %collective-permute-start.12 = (f32[40,128]{1,0:T(8,128)S(1)}, f32[40,128]{1,0:T(8,128)S(1)}, u32[]{:S(2)}, u32[]{:S(2)}) collective-permute-start(f32[40,128]{1,0:T(8,128)S(1)} %get-tuple-element.48.refs_0_), channel_id=1, source_target_pairs={{0,8},{8,0},{16,24},{24,16},{1,9},{9,1},{17,25},{25,17},{2,10},{10... | collective-permute-start | bytes 61448 | tf_op jit(solution)/shard_map/ppermute | solution.py:23
  32.5 1.7 %prefix_sums.1.refs_5_ = f32[16,4096]{1,0:T(8,128)S(1)} custom-call(f32[256,256]{1,0:T(8,128)S(1)} %get-tuple-element.47.ordered.sums, f32[16,256]{1,0:T(8,128)S(1)} %get-tuple-element.50.squares.square, s32[1,4096]{1,0:T(1,128)S(1)} %bitcast.5), custom_call_target="tpu_custom_call" | custom-call | flops 1073741824 | bytes 1572864 | tf_op jit(solution)/shard_map/prefix_sums/pallas_call | solution.py:443
  34.2 0.9 %hazards.1 = (f32[1,4096]{1,0:T(1,128)S(1)}, f32[1,4096]{1,0:T(1,128)S(1)}) custom-call(f32[16,256]{1,0:T(8,128)S(1)} %get-tuple-element.51.hazard, f32[16,256]{1,0:T(8,128)S(1)} %get-tuple-element.50.squares.square, s32[1,4096]{1,0:T(1,128)S(1)} %bitcast.6), custom_call_target="tpu_custom_call" | custom-call | flops 209715200 | bytes 262144 | tf_op jit(solution)/shard_map/hazards/pallas_call | solution.py:321
  36.2 1.6 %collective-permute-start.20 = (bf16[16,4096]{1,0:T(8,128)(2,1)S(1)}, bf16[16,4096]{1,0:T(8,128)(2,1)S(1)}, u32[]{:S(2)}, u32[]{:S(2)}) collective-permute-start(bf16[16,4096]{1,0:T(8,128)(2,1)S(1)} %weights.1.refs_0_), channel_id=1, source_target_pairs={{0,6},{1,7},{2,4},{3,5},{4,2},{5,3},{6,0},{7,1},{8,14},{9,15},{10,... | collective-permute-start | bytes 393224 | tf_op jit(solution)/shard_map/ppermute | solution.py:23
  38.2 1.5 %collective-permute-start.16 = (bf16[16,4096]{1,0:T(8,128)(2,1)S(1)}, bf16[16,4096]{1,0:T(8,128)(2,1)S(1)}, u32[]{:S(2)}, u32[]{:S(2)}) collective-permute-start(bf16[16,4096]{1,0:T(8,128)(2,1)S(1)} %weights.1.refs_0_), channel_id=1, source_target_pairs={{0,2},{1,3},{2,0},{3,1},{4,6},{5,7},{6,4},{7,5},{8,10},{9,11},{10,... | collective-permute-start | bytes 393224 | tf_op jit(solution)/shard_map/ppermute | solution.py:23
  39.7 2.5 %collective-permute-done.20.refs_6_ = bf16[16,4096]{1,0:T(8,128)(2,1)S(1)} collective-permute-done((bf16[16,4096]{1,0:T(8,128)(2,1)S(1)}, bf16[16,4096]{1,0:T(8,128)(2,1)S(1)}, u32[]{:S(2)}, u32[]{:S(2)}) %collective-permute-start.20) | collective-permute-done | bytes 131104 | tf_op jit(solution)/shard_map/ppermute | solution.py:23
  42.2 1.3 %collective-permute-done.18.refs_4_ = bf16[16,4096]{1,0:T(8,128)(2,1)S(1)} collective-permute-done((bf16[16,4096]{1,0:T(8,128)(2,1)S(1)}, bf16[16,4096]{1,0:T(8,128)(2,1)S(1)}, u32[]{:S(2)}, u32[]{:S(2)}) %collective-permute-start.18) | collective-permute-done | bytes 131104 | tf_op jit(solution)/shard_map/ppermute | solution.py:23
  44.0 0.8 %collective-permute-done.19.refs_5_ = bf16[16,4096]{1,0:T(8,128)(2,1)S(1)} collective-permute-done((bf16[16,4096]{1,0:T(8,128)(2,1)S(1)}, bf16[16,4096]{1,0:T(8,128)(2,1)S(1)}, u32[]{:S(2)}, u32[]{:S(2)}) %collective-permute-start.19) | collective-permute-done | bytes 131104 | tf_op jit(solution)/shard_map/ppermute | solution.py:23
  46.7 1.8 %collective-permute-start.23 = (s16[272,128]{1,0:T(8,128)(2,1)S(1)}, s16[272,128]{1,0:T(8,128)(2,1)S(1)}, u32[]{:S(2)}, u32[]{:S(2)}) collective-permute-start(s16[272,128]{1,0:T(8,128)(2,1)S(1)} %gradients.3.mine), channel_id=1, source_target_pairs={{0,8},{8,0},{16,24},{24,16},{1,9},{9,1},{17,25},{25,17},{2,10},{10... | collective-permute-start | bytes 208904 | tf_op jit(solution)/shard_map/ppermute | solution.py:23
  48.5 2.2 %collective-permute-done.22.other = s16[272,128]{1,0:T(8,128)(2,1)S(1)} collective-permute-done((s16[272,128]{1,0:T(8,128)(2,1)S(1)}, s16[272,128]{1,0:T(8,128)(2,1)S(1)}, u32[]{:S(2)}, u32[]{:S(2)}) %collective-permute-start.22) | collective-permute-done | bytes 69664 | tf_op jit(solution)/shard_map/ppermute | solution.py:23
  50.8 1.6 %collective-permute-start.24 = (s16[272,128]{1,0:T(8,128)(2,1)S(1)}, s16[272,128]{1,0:T(8,128)(2,1)S(1)}, u32[]{:S(2)}, u32[]{:S(2)}) collective-permute-start(s16[272,128]{1,0:T(8,128)(2,1)S(1)} %merge.2.refs_0_), channel_id=1, source_target_pairs={{0,16},{8,24},{16,0},{24,8},{1,17},{9,25},{17,1},{25,9},{2,18},{10... | collective-permute-start | bytes 208904 | tf_op jit(solution)/shard_map/ppermute | solution.py:23
  52.6 1.5 %collective-permute-start.25 = (s16[272,128]{1,0:T(8,128)(2,1)S(1)}, s16[272,128]{1,0:T(8,128)(2,1)S(1)}, u32[]{:S(2)}, u32[]{:S(2)}) collective-permute-start(s16[272,128]{1,0:T(8,128)(2,1)S(1)} %merge.3.refs_1_), channel_id=1, source_target_pairs={{0,16},{8,24},{16,0},{24,8},{1,17},{9,25},{17,1},{25,9},{2,18},{10... | collective-permute-start | bytes 208904 | tf_op jit(solution)/shard_map/ppermute | solution.py:23
  54.0 4.4 %collective-permute-done.24.refs_2_ = s16[272,128]{1,0:T(8,128)(2,1)S(1)} collective-permute-done((s16[272,128]{1,0:T(8,128)(2,1)S(1)}, s16[272,128]{1,0:T(8,128)(2,1)S(1)}, u32[]{:S(2)}, u32[]{:S(2)}) %collective-permute-start.24) | collective-permute-done | bytes 69664 | tf_op jit(solution)/shard_map/ppermute | solution.py:23
  (57 shorter events, 11.2 us)
Async XLA Ops:
  3.8 1.7 %collective-permute-start = (f32[16,4352]{1,0:T(8,128)S(1)}, f32[16,4352]{1,0:T(8,128)S(1)}, u32[]{:S(2)}, u32[]{:S(2)}) collective-permute-start(f32[16,4352]{1,0:T(8,128)S(1)} %get-tuple-element.31), channel_id=1, source_target_pairs={{0,1},{1,0},{2,3},{3,2},{4,5},{5,4},{6,7},{7,6},{8,9},{9,8},{10,11... | collective-permute-start | bytes 835592 | tf_op jit(solution)/shard_map/ppermute | solution.py:23
  4.3 5.2 %collective-permute-start.2 = (f32[16,4096]{1,0:T(8,128)S(1)}, f32[16,4096]{1,0:T(8,128)S(1)}, u32[]{:S(2)}, u32[]{:S(2)}) collective-permute-start(f32[16,4096]{1,0:T(8,128)S(1)} %get-tuple-element.34), channel_id=1, source_target_pairs={{0,1},{1,0},{2,3},{3,2},{4,5},{5,4},{6,7},{7,6},{8,9},{9,8},{10,11... | collective-permute-start | bytes 786440 | tf_op jit(solution)/shard_map/ppermute | solution.py:23
  4.4 5.8 %collective-permute-start.4 = (f32[16,4096]{1,0:T(8,128)S(1)}, f32[16,4096]{1,0:T(8,128)S(1)}, u32[]{:S(2)}, u32[]{:S(2)}) collective-permute-start(f32[16,4096]{1,0:T(8,128)S(1)} %get-tuple-element.36), channel_id=1, source_target_pairs={{0,1},{1,0},{2,3},{3,2},{4,5},{5,4},{6,7},{7,6},{8,9},{9,8},{10,11... | collective-permute-start | bytes 786440 | tf_op jit(solution)/shard_map/ppermute | solution.py:23
  4.8 10.4 %collective-permute-start.8 = (f32[16,4096]{1,0:T(8,128)S(1)}, f32[16,4096]{1,0:T(8,128)S(1)}, u32[]{:S(2)}, u32[]{:S(2)}) collective-permute-start(f32[16,4096]{1,0:T(8,128)S(1)} %get-tuple-element.40), channel_id=1, source_target_pairs={{0,1},{1,0},{2,3},{3,2},{4,5},{5,4},{6,7},{7,6},{8,9},{9,8},{10,11... | collective-permute-start | bytes 786440 | tf_op jit(solution)/shard_map/ppermute | solution.py:23
  5.6 5.8 %collective-permute-start.1 = (s16[16,1152]{1,0:T(8,128)(2,1)S(1)}, s16[16,1152]{1,0:T(8,128)(2,1)S(1)}, u32[]{:S(2)}, u32[]{:S(2)}) collective-permute-start(s16[16,1152]{1,0:T(8,128)(2,1)S(1)} %join.6), channel_id=1, source_target_pairs={{0,6},{1,7},{2,4},{3,5},{4,2},{5,3},{6,0},{7,1},{8,14},{9,15},{10,... | collective-permute-start | bytes 110600 | tf_op jit(solution)/shard_map/ppermute | solution.py:23
  9.6 4.0 %collective-permute-start.3 = (s16[16,1152]{1,0:T(8,128)(2,1)S(1)}, s16[16,1152]{1,0:T(8,128)(2,1)S(1)}, u32[]{:S(2)}, u32[]{:S(2)}) collective-permute-start(s16[16,1152]{1,0:T(8,128)(2,1)S(1)} %join.7), channel_id=1, source_target_pairs={{0,4},{1,5},{2,6},{3,7},{4,0},{5,1},{6,2},{7,3},{8,12},{9,13},{10,... | collective-permute-start | bytes 110600 | tf_op jit(solution)/shard_map/ppermute | solution.py:23
  10.3 4.0 %collective-permute-start.5 = (s16[16,1152]{1,0:T(8,128)(2,1)S(1)}, s16[16,1152]{1,0:T(8,128)(2,1)S(1)}, u32[]{:S(2)}, u32[]{:S(2)}) collective-permute-start(s16[16,1152]{1,0:T(8,128)(2,1)S(1)} %join.8), channel_id=1, source_target_pairs={{0,2},{1,3},{2,0},{3,1},{4,6},{5,7},{6,4},{7,5},{8,10},{9,11},{10,... | collective-permute-start | bytes 110600 | tf_op jit(solution)/shard_map/ppermute | solution.py:23
  15.4 10.2 %collective-permute-start.10 = (s16[16,3712]{1,0:T(8,128)(2,1)S(1)}, s16[16,3712]{1,0:T(8,128)(2,1)S(1)}, u32[]{:S(2)}, u32[]{:S(2)}) collective-permute-start(s16[16,3712]{1,0:T(8,128)(2,1)S(1)} %join.10), channel_id=1, source_target_pairs={{0,4},{1,5},{2,6},{3,7},{4,0},{5,1},{6,2},{7,3},{8,12},{9,13},{10,... | collective-permute-start | bytes 356360 | tf_op jit(solution)/shard_map/ppermute | solution.py:23
  17.1 8.5 %collective-permute-start.11 = (s16[16,3712]{1,0:T(8,128)(2,1)S(1)}, s16[16,3712]{1,0:T(8,128)(2,1)S(1)}, u32[]{:S(2)}, u32[]{:S(2)}) collective-permute-start(s16[16,3712]{1,0:T(8,128)(2,1)S(1)} %join.11), channel_id=1, source_target_pairs={{0,2},{1,3},{2,0},{3,1},{4,6},{5,7},{6,4},{7,5},{8,10},{9,11},{10,... | collective-permute-start | bytes 356360 | tf_op jit(solution)/shard_map/ppermute | solution.py:23
  17.8 7.8 %collective-permute-start.9 = (s16[16,3712]{1,0:T(8,128)(2,1)S(1)}, s16[16,3712]{1,0:T(8,128)(2,1)S(1)}, u32[]{:S(2)}, u32[]{:S(2)}) collective-permute-start(s16[16,3712]{1,0:T(8,128)(2,1)S(1)} %join.9), channel_id=1, source_target_pairs={{0,6},{1,7},{2,4},{3,5},{4,2},{5,3},{6,0},{7,1},{8,14},{9,15},{10,... | collective-permute-start | bytes 356360 | tf_op jit(solution)/shard_map/ppermute | solution.py:23
  19.3 3.6 %collective-permute-start.6 = (f32[8,128]{1,0:T(8,128)S(1)}, f32[8,128]{1,0:T(8,128)S(1)}, u32[]{:S(2)}, u32[]{:S(2)}) collective-permute-start(f32[8,128]{1,0:T(8,128)S(1)} %get-tuple-element.37.refs_0_.refs_2_), channel_id=1, source_target_pairs={{0,8},{8,0},{16,24},{24,16},{1,9},{9,1},{17,25},{25,17},{2,10},{10... | collective-permute-start | bytes 12296 | tf_op jit(solution)/shard_map/ppermute | solution.py:23
  22.9 5.0 %collective-permute-start.7 = (f32[8,128]{1,0:T(8,128)S(1)}, f32[8,128]{1,0:T(8,128)S(1)}, u32[]{:S(2)}, u32[]{:S(2)}) collective-permute-start(f32[8,128]{1,0:T(8,128)S(1)} %get-tuple-element.38.refs_0_), channel_id=1, source_target_pairs={{0,16},{8,24},{16,0},{24,8},{1,17},{9,25},{17,1},{25,9},{2,18},{10... | collective-permute-start | bytes 12296 | tf_op jit(solution)/shard_map/ppermute | solution.py:23
  28.0 7.1 %collective-permute-start.14 = (f32[40,128]{1,0:T(8,128)S(1)}, f32[40,128]{1,0:T(8,128)S(1)}, u32[]{:S(2)}, u32[]{:S(2)}) collective-permute-start(f32[40,128]{1,0:T(8,128)S(1)} %get-tuple-element.48.refs_0_), channel_id=1, source_target_pairs={{0,24},{8,16},{16,8},{24,0},{1,25},{9,17},{17,9},{25,1},{2,26},{10... | collective-permute-start | bytes 61448 | tf_op jit(solution)/shard_map/ppermute | solution.py:23
  31.3 4.7 %collective-permute-start.13 = (f32[40,128]{1,0:T(8,128)S(1)}, f32[40,128]{1,0:T(8,128)S(1)}, u32[]{:S(2)}, u32[]{:S(2)}) collective-permute-start(f32[40,128]{1,0:T(8,128)S(1)} %get-tuple-element.48.refs_0_), channel_id=1, source_target_pairs={{0,16},{8,24},{16,0},{24,8},{1,17},{9,25},{17,1},{25,9},{2,18},{10... | collective-permute-start | bytes 61448 | tf_op jit(solution)/shard_map/ppermute | solution.py:23
  31.3 4.7 %collective-permute-start.12 = (f32[40,128]{1,0:T(8,128)S(1)}, f32[40,128]{1,0:T(8,128)S(1)}, u32[]{:S(2)}, u32[]{:S(2)}) collective-permute-start(f32[40,128]{1,0:T(8,128)S(1)} %get-tuple-element.48.refs_0_), channel_id=1, source_target_pairs={{0,8},{8,0},{16,24},{24,16},{1,9},{9,1},{17,25},{25,17},{2,10},{10... | collective-permute-start | bytes 61448 | tf_op jit(solution)/shard_map/ppermute | solution.py:23
  36.2 6.0 %collective-permute-start.20 = (bf16[16,4096]{1,0:T(8,128)(2,1)S(1)}, bf16[16,4096]{1,0:T(8,128)(2,1)S(1)}, u32[]{:S(2)}, u32[]{:S(2)}) collective-permute-start(bf16[16,4096]{1,0:T(8,128)(2,1)S(1)} %weights.1.refs_0_), channel_id=1, source_target_pairs={{0,6},{1,7},{2,4},{3,5},{4,2},{5,3},{6,0},{7,1},{8,14},{9,15},{10,... | collective-permute-start | bytes 393224 | tf_op jit(solution)/shard_map/ppermute | solution.py:23
  37.7 5.8 %collective-permute-start.18 = (bf16[16,4096]{1,0:T(8,128)(2,1)S(1)}, bf16[16,4096]{1,0:T(8,128)(2,1)S(1)}, u32[]{:S(2)}, u32[]{:S(2)}) collective-permute-start(bf16[16,4096]{1,0:T(8,128)(2,1)S(1)} %weights.1.refs_0_), channel_id=1, source_target_pairs={{0,4},{1,5},{2,6},{3,7},{4,0},{5,1},{6,2},{7,3},{8,12},{9,13},{10,... | collective-permute-start | bytes 393224 | tf_op jit(solution)/shard_map/ppermute | solution.py:23
  38.2 5.4 %collective-permute-start.16 = (bf16[16,4096]{1,0:T(8,128)(2,1)S(1)}, bf16[16,4096]{1,0:T(8,128)(2,1)S(1)}, u32[]{:S(2)}, u32[]{:S(2)}) collective-permute-start(bf16[16,4096]{1,0:T(8,128)(2,1)S(1)} %weights.1.refs_0_), channel_id=1, source_target_pairs={{0,2},{1,3},{2,0},{3,1},{4,6},{5,7},{6,4},{7,5},{8,10},{9,11},{10,... | collective-permute-start | bytes 393224 | tf_op jit(solution)/shard_map/ppermute | solution.py:23
  39.7 4.3 %collective-permute-start.15 = (bf16[16,4096]{1,0:T(8,128)(2,1)S(1)}, bf16[16,4096]{1,0:T(8,128)(2,1)S(1)}, u32[]{:S(2)}, u32[]{:S(2)}) collective-permute-start(bf16[16,4096]{1,0:T(8,128)(2,1)S(1)} %weights.1.refs_0_), channel_id=1, source_target_pairs={{0,1},{1,0},{2,3},{3,2},{4,5},{5,4},{6,7},{7,6},{8,9},{9,8},{10,11... | collective-permute-start | bytes 393224 | tf_op jit(solution)/shard_map/ppermute | solution.py:23
  42.2 1.8 %collective-permute-start.21 = (bf16[16,4096]{1,0:T(8,128)(2,1)S(1)}, bf16[16,4096]{1,0:T(8,128)(2,1)S(1)}, u32[]{:S(2)}, u32[]{:S(2)}) collective-permute-start(bf16[16,4096]{1,0:T(8,128)(2,1)S(1)} %collective-permute-done.20.refs_6_), channel_id=1, source_target_pairs={{0,1},{1,0},{2,3},{3,2},{4,5},{5,4},{6,7},{7,6},{8,9},{9,8},{10,11... | collective-permute-start | bytes 393224 | tf_op jit(solution)/shard_map/ppermute | solution.py:23
  45.7 5.1 %collective-permute-start.22 = (s16[272,128]{1,0:T(8,128)(2,1)S(1)}, s16[272,128]{1,0:T(8,128)(2,1)S(1)}, u32[]{:S(2)}, u32[]{:S(2)}) collective-permute-start(s16[272,128]{1,0:T(8,128)(2,1)S(1)} %gradients.2.mine), channel_id=1, source_target_pairs={{0,8},{8,0},{16,24},{24,16},{1,9},{9,1},{17,25},{25,17},{2,10},{10... | collective-permute-start | bytes 208904 | tf_op jit(solution)/shard_map/ppermute | solution.py:23
  46.7 5.8 %collective-permute-start.23 = (s16[272,128]{1,0:T(8,128)(2,1)S(1)}, s16[272,128]{1,0:T(8,128)(2,1)S(1)}, u32[]{:S(2)}, u32[]{:S(2)}) collective-permute-start(s16[272,128]{1,0:T(8,128)(2,1)S(1)} %gradients.3.mine), channel_id=1, source_target_pairs={{0,8},{8,0},{16,24},{24,16},{1,9},{9,1},{17,25},{25,17},{2,10},{10... | collective-permute-start | bytes 208904 | tf_op jit(solution)/shard_map/ppermute | solution.py:23
  50.8 7.6 %collective-permute-start.24 = (s16[272,128]{1,0:T(8,128)(2,1)S(1)}, s16[272,128]{1,0:T(8,128)(2,1)S(1)}, u32[]{:S(2)}, u32[]{:S(2)}) collective-permute-start(s16[272,128]{1,0:T(8,128)(2,1)S(1)} %merge.2.refs_0_), channel_id=1, source_target_pairs={{0,16},{8,24},{16,0},{24,8},{1,17},{9,25},{17,1},{25,9},{2,18},{10... | collective-permute-start | bytes 208904 | tf_op jit(solution)/shard_map/ppermute | solution.py:23
  52.6 6.6 %collective-permute-start.25 = (s16[272,128]{1,0:T(8,128)(2,1)S(1)}, s16[272,128]{1,0:T(8,128)(2,1)S(1)}, u32[]{:S(2)}, u32[]{:S(2)}) collective-permute-start(s16[272,128]{1,0:T(8,128)(2,1)S(1)} %merge.3.refs_1_), channel_id=1, source_target_pairs={{0,16},{8,24},{16,0},{24,8},{1,17},{9,25},{17,1},{25,9},{2,18},{10... | collective-permute-start | bytes 208904 | tf_op jit(solution)/shard_map/ppermute | solution.py:23
  (5 other events, 47.1 us)

commit v12 on v10

--- a/solution.py
+++ b/solution.py
@@ -13,6 +13,7 @@
 NT = (((1,), (1,)), ((), ()))
 BLOCK = 64
 SPAN = 512
+AHEAD = 3
 VMEM = pl.BlockSpec(memory_space=pltpu.VMEM)
 HBM = pl.BlockSpec(memory_space=pltpu.HBM)
 PARAMS = dict(vmem_limit_bytes=24 * 1024 * 1024)
@@ -85,7 +86,7 @@
         )
         for i in range(steps)
     ]
-    for copy in small + large:
+    for copy in small + large[:AHEAD]:
         copy.start()
     for copy in small:
         copy.wait()
@@ -95,6 +96,8 @@
     lhs[width:] = jnp.broadcast_to(own_coefficients[...].astype(F32)[None, :], (16, variants)).astype(BF16)
     for i in range(steps):
         large[i].wait()
+        if i + AHEAD < steps:
+            large[i + AHEAD].start()
         first = i * chunk
         result = lax.dot_general(
             lhs[...], table[first : first + chunk], NT, preferred_element_type=F32
@@ -271,7 +274,7 @@
     )(linear, *messages, rank, events, table)
 
 
-def share_kernel(later, sums, events, plain, ordered, hazard_out, squares, message):
+def share_kernel(later, sums, events, plain, more, ordered, hazard_out, squares, message):
     kf = plain.shape[0]
     groups = sums.shape[0]
     risk_sum = sums[...] + later[0:1, 0:1]
@@ -282,23 +285,23 @@
     scaled = jnp.zeros((kf, LO), F32)
     for g in range(groups):
         scaled = scaled + ordered[g * kf : (g + 1) * kf] * square[g : g + 1]
-    message[:kf] = plain[...]
+    message[:kf] = plain[...] + more[...]
     message[kf : 2 * kf] = sum(scaled[:, start : start + 128] for start in range(0, LO, 128))
     totals = [jnp.sum(jnp.sum(v, axis=0, keepdims=True), axis=1, keepdims=True) for v in (hazard, square)]
     rows = [jnp.broadcast_to(v, (1, 128)) for v in totals]
     message[2 * kf :] = jnp.concatenate(rows + [jnp.zeros((6, 128), F32)], axis=0)
 
 
-def shares(later, sums, events, plain, ordered):
+def shares(later, sums, events, plain, more, ordered):
     flat = jax.ShapeDtypeStruct(sums.shape, F32)
     return pl.pallas_call(
         share_kernel,
-        in_specs=[VMEM] * 5,
+        in_specs=[VMEM] * 6,
         out_shape=[flat, flat, jax.ShapeDtypeStruct((2 * plain.shape[0] + 8, 128), F32)],
         out_specs=[VMEM] * 3,
         compiler_params=pltpu.CompilerParams(**PARAMS),
         name="shares",
-    )(later, sums, events, plain, ordered)
+    )(later, sums, events, plain, more, ordered)
 
 
 def hazard_kernel(rows, hazard, square, rank, cumulative, squares):
@@ -348,24 +351,22 @@
     )(total, other, later, *waited)
 
 
-def suffix_kernel(parts, own, other, *refs):
+def order_kernel(start, parts, own, other, *refs):
     messages, (risk, rank, table) = refs[:parts], refs[parts : parts + 3]
-    tangent_out, sums, plain, lhs = refs[parts + 3 :]
-    kf, rows = own.shape
+    tangent_out, ordered_out, plain, lhs = refs[-4:]
+    kf, width = tangent_out.shape
+    rows = own.shape[1]
+    groups = rows // LO
+    span = min(SPAN, width)
     folded = jnp.zeros((kf, 128), F32)
-    groups = rows // LO
-    span = min(SPAN, rows)
     powers = [jnp.exp2(from_short(part[:, part.shape[1] - 128 :])) for part in messages]
-    half = rows // 2
-    later = len(messages) // 2
-    for i in range(rows // span):
-        at = slice(i * span, (i + 1) * span)
+    for i in range(width // span):
+        at = slice(start + i * span, start + (i + 1) * span)
+        here = slice(i * span, (i + 1) * span)
         tangent = own[:, at] + other[:, at]
-        first = 0 if i * span < half else later
-        here = i - (first and half // span)
-        for part, power in zip(messages[first : first + later], powers[first : first + later]):
-            tangent = tangent + from_short(part[:, here * span : (here + 1) * span]) * power[:, here : here + 1]
-        tangent_out[:, at] = tangent
+        for part, power in zip(messages, powers):
+            tangent = tangent + from_short(part[:, here]) * power[:, i : i + 1]
+        tangent_out[:, here] = tangent
         weighted = tangent * risk[:, at]
         folded = folded + sum(weighted[:, j : j + 128] for j in range(0, span, 128))
         high, low = split_two(weighted)
@@ -373,18 +374,40 @@
         group = jnp.broadcast_to(lax.rem(rank[:, at], rows) // LO, (kf, span))
         for g in range(groups):
             mask = jnp.where(group == g, 1.0, 0.0).astype(BF16)
-            lhs[2 * g * kf : (2 * g + 1) * kf, at] = high * mask
-            lhs[(2 * g + 1) * kf : (2 * g + 2) * kf, at] = low * mask
+            lhs[2 * g * kf : (2 * g + 1) * kf, here] = high * mask
+            lhs[(2 * g + 1) * kf : (2 * g + 2) * kf, here] = low * mask
     plain[...] = folded
-    ordered = jnp.dot(lhs[...], table[...], preferred_element_type=F32)
-    ordered = jnp.concatenate(
-        [
+    ordered = jnp.dot(lhs[...], table[start : start + width], preferred_element_type=F32)
+    for g in range(groups):
+        ordered_out[g * kf : (g + 1) * kf] = (
             ordered[2 * g * kf : (2 * g + 1) * kf] + ordered[(2 * g + 1) * kf : (2 * g + 2) * kf]
-            for g in range(groups)
+        )
+
+
+def ordered_values(own, other, messages, risk, rank, table, start, width):
+    kf, rows = own.shape
+    groups = rows // LO
+    return pl.pallas_call(
+        functools.partial(order_kernel, start, len(messages)),
+        in_specs=[VMEM] * (len(messages) + 5),
+        out_shape=[
+            jax.ShapeDtypeStruct((kf, width), F32),
+            jax.ShapeDtypeStruct((groups * kf, LO), F32),
+            jax.ShapeDtypeStruct((kf, 128), F32),
         ],
-        axis=0,
-    )
-    inside = dot_binary(ordered, triangle(LO, lambda a, b: a >= b))
+        out_specs=[VMEM] * 3,
+        scratch_shapes=[pltpu.VMEM((groups * 2 * kf, width), BF16)],
+        compiler_params=pltpu.CompilerParams(**PARAMS),
+        cost_estimate=pl.CostEstimate(
+            flops=2 * width * LO * groups * 2 * kf, bytes_accessed=width * kf * 24, transcendentals=0
+        ),
+        name="ordered_values",
+    )(own, other, *messages, risk, rank, table)
+
+
+def suffix_kernel(kf, one, two, sums):
+    groups = sums.shape[0] // kf
+    inside = dot_binary(one[...] + two[...], triangle(LO, lambda a, b: a >= b))
     carried = jnp.zeros((kf, 1), F32)
     for g in reversed(range(groups)):
         rows_of = slice(g * kf, (g + 1) * kf)
@@ -392,25 +415,15 @@
         carried = carried + inside[rows_of, :1]
 
 
-def suffix_sums(own, other, messages, risk, rank, table):
-    kf, rows = own.shape
-    groups = rows // LO
-    return pl.pallas_call(
-        functools.partial(suffix_kernel, len(messages)),
-        in_specs=[VMEM] * (len(messages) + 5),
-        out_shape=[
-            jax.ShapeDtypeStruct((kf, rows), F32),
-            jax.ShapeDtypeStruct((groups * kf, LO), F32),
-            jax.ShapeDtypeStruct((kf, 128), F32),
-        ],
-        out_specs=[VMEM] * 3,
-        scratch_shapes=[pltpu.VMEM((groups * 2 * kf, rows), BF16)],
-        compiler_params=pltpu.CompilerParams(**PARAMS),
-        cost_estimate=pl.CostEstimate(
-            flops=2 * rows * LO * groups * 2 * kf, bytes_accessed=rows * kf * 24, transcendentals=0
-        ),
+def suffix_sums(one, two, kf):
+    return pl.pallas_call(
+        functools.partial(suffix_kernel, kf),
+        in_specs=[VMEM] * 2,
+        out_shape=jax.ShapeDtypeStruct(one.shape, F32),
+        out_specs=VMEM,
+        compiler_params=pltpu.CompilerParams(**PARAMS),
         name="suffix_sums",
-    )(own, other, *messages, risk, rank, table)
+    )(one, two)
 
 
 def prefix_kernel(sums, squares, rank, out):
@@ -454,9 +467,9 @@
 
 
 def weight_kernel(ex, *refs):
-    messages, (tangent, local, risk, cumulative, squares) = refs[:ex], refs[ex : ex + 5]
-    weighted, placed = refs[ex + 5 :]
-    kf = tangent.shape[0]
+    messages, (first, rest, local, risk, cumulative, squares) = refs[:ex], refs[ex : ex + 6]
+    weighted, placed = refs[ex + 6 :]
+    kf = first.shape[0]
     me = lax.axis_index("ex")
     for i in range(ex):
         placed[me ^ i] = messages[i][...]
@@ -472,21 +485,25 @@
     own_later = jnp.sum(own_later, axis=1, keepdims=True)
     before = jnp.sum(before, axis=1, keepdims=True)
     hazard_before = hazard_before[:, :1]
-    value = tangent[...] * (cumulative[...] + hazard_before) - (local[...] + squares[...] * own_later + before)
-    weighted[...] = (risk[...] * value).astype(BF16)
-
-
-def weights(messages, tangent, local, risk, cumulative, squares):
+    for start, part in ((0, first), (first.shape[1], rest)):
+        at = slice(start, start + part.shape[1])
+        value = part[...] * (cumulative[:, at] + hazard_before) - (
+            local[:, at] + squares[:, at] * own_later + before
+        )
+        weighted[:, at] = (risk[:, at] * value).astype(BF16)
+
+
+def weights(messages, first, rest, local, risk, cumulative, squares):
     ex = len(messages)
     return pl.pallas_call(
         functools.partial(weight_kernel, ex),
-        in_specs=[VMEM] * (ex + 5),
-        out_shape=jax.ShapeDtypeStruct(tangent.shape, BF16),
+        in_specs=[VMEM] * (ex + 6),
+        out_shape=jax.ShapeDtypeStruct(local.shape, BF16),
         out_specs=VMEM,
         scratch_shapes=[pltpu.VMEM((ex,) + messages[0].shape, F32)],
         compiler_params=pltpu.CompilerParams(**PARAMS),
         name="weights",
-    )(*messages, tangent, local, risk, cumulative, squares)
+    )(*messages, first, rest, local, risk, cumulative, squares)
 
 
 def encode(values, message):
@@ -610,12 +627,12 @@
     order = list(reversed(range(1, feat // 2)))
     received = {q: swap(send[q], "feat", 1) for q in order + [0]}
     paired = pair(linear, received[order[0]])
-    middle = rows // 2
+    middle = min(3 * SPAN, rows // 2)
     firsts = [
         swap(join(keep[q], received[q], 0, middle, paired, []), "feat", 2 * q) for q in order
     ]
     rests = [
-        swap(join(keep[q], received[q], middle, middle, paired, [received[0]]), "feat", 2 * q)
+        swap(join(keep[q], received[q], middle, rows - middle, paired, [received[0]]), "feat", 2 * q)
         for q in order
     ]
     table = tables(rank, paired, rows)
@@ -626,12 +643,16 @@
     while bit < ex:
         total, later = ranges(bit, total, swap(total, "ex", bit), later, rests if bit == 1 else [])
         bit *= 2
-    tangent, later_sums, plain = suffix_sums(keep[0], received[0], firsts + rests, risk, rank, table)
-    hazard, ordered_squares, message = shares(later, sums, ordered_events, plain, later_sums)
+    tangent, one, plain = ordered_values(keep[0], received[0], firsts, risk, rank, table, 0, middle)
+    more_tangent, two, more = ordered_values(
+        keep[0], received[0], rests, risk, rank, table, middle, rows - middle
+    )
+    later_sums = suffix_sums(one, two, padded)
+    hazard, ordered_squares, message = shares(later, sums, ordered_events, plain, more, later_sums)
     messages = [message] + [swap(message, "ex", i) for i in range(1, ex)]
     cumulative, squares = hazards(hazard, ordered_squares, rank, rows)
     summed = prefix_sums(later_sums, ordered_squares, rank, padded)
-    own = weights(messages, tangent, summed, risk, cumulative, squares)
+    own = weights(messages, tangent, more_tangent, summed, risk, cumulative, squares)
 
     chips = {0: own}
     for q in reversed(range(1, feat // 2)):

time: 57.5 us -> 57.9 us (level)
    pallas_call x2 -> x4, Pallas kernels: 2.38 us -> 2.48 us  [the longest x2 1.97 us: ordered_values(): pl.pallas_call(functools.partial(order_kernel, start, len(messages)), in_...]
where the time goes in v12:
time: 57.9 us; the launch traced here: 57.7 us
  starting transfers between devices  27.9 us (48%)
  waiting for transfers between devices  15.8 us (27%)
  Pallas kernels  13.9 us (24%)
    ppermute x26, starting transfers between devices, swap(): return lax.ppermute(x, axis, [(s, s ^ i) for s in range(count)])  27.9 us
    ppermute x26, waiting for transfers between devices, swap(): return lax.ppermute(x, axis, [(s, s ^ i) for s in range(count)])  15.8 us
    pallas_call x1, Pallas kernels, products(): pl.pallas_call(functools.partial(product_kernel, feat, kf, chunk), in_spe...  4.11 us
    pallas_call x2, Pallas kernels, ordered_values(): pl.pallas_call(functools.partial(order_kernel, start, len(messages)), in_...  1.97 us
    pallas_call x1, Pallas kernels, prefix_sums(): pl.pallas_call(prefix_kernel, in_specs=[VMEM] * 3, out_shape=jax.ShapeDty...  1.75 us
    pallas_call x2, Pallas kernels, gradients(): pl.pallas_call(functools.partial(gradient_kernel, feat, kf, start), in_sp...  1.29 us
  transfers between devices with their start and end apart: 26, of which 13 were waited for; matrix products, arithmetic and copies ran while one was open for 0% of the time, Pallas kernels for 14%

profile of v12, /device:TPU:0, one launch (start us, length us, event | category | flops | bytes accessed | tf_op | source)
XLA Modules:
  0.0 57.7 jit_solution(7420927542333778415)
XLA Ops:
  0.0 4.1 %products.1 = (f32[16,256]{1,0:T(8,128)S(1)}, f32[16,4096]{1,0:T(8,128)S(1)}, f32[16,4096]{1,0:T(8,128)S(1)}, f32[16,4096]{1,0:T(8,128)S(1)}, f32[16,4096]{1,0:T...) custom-call(bf16[512,128]{1,0:T(8,128)(2,1)} %directions.1, ...), custom_call_target="tpu_custom_call" | custom-call | flops 536870912 | bytes 6291456 | tf_op jit(solution)/shard_map/products/pallas_call | solution.py:121
  6.0 3.9 %collective-permute-start.1 = (s16[16,2176]{1,0:T(8,128)(2,1)S(1)}, s16[16,2176]{1,0:T(8,128)(2,1)S(1)}, u32[]{:S(2)}, u32[]{:S(2)}) collective-permute-start(s16[16,2176]{1,0:T(8,128)(2,1)S(1)} %join.6), channel_id=1, source_target_pairs={{0,6},{1,7},{2,4},{3,5},{4,2},{5,3},{6,0},{7,1},{8,14},{9,15},{10,... | collective-permute-start | bytes 208904 | tf_op jit(solution)/shard_map/ppermute | solution.py:24
  11.1 2.8 %collective-permute-start.8 = (s16[16,2688]{1,0:T(8,128)(2,1)S(1)}, s16[16,2688]{1,0:T(8,128)(2,1)S(1)}, u32[]{:S(2)}, u32[]{:S(2)}) collective-permute-start(s16[16,2688]{1,0:T(8,128)(2,1)S(1)} %join.9), channel_id=1, source_target_pairs={{0,6},{1,7},{2,4},{3,5},{4,2},{5,3},{6,0},{7,1},{8,14},{9,15},{10,... | collective-permute-start | bytes 258056 | tf_op jit(solution)/shard_map/ppermute | solution.py:24
  15.8 0.9 %risks.1 = (f32[1,4096]{1,0:T(1,128)S(1)}, f32[16,256]{1,0:T(8,128)S(1)}, f32[16,256]{1,0:T(8,128)S(1)}, f32[8,128]{1,0:T(8,128)S(1)}) custom-call(f32[16,256]{1,0:T(8,128)S(1)} %pair.1.refs_0_.waited.linear, s16[16,2176]{1,0:T(8,128)(2,1)S(1)} %collective-permute-done.1.refs_0_, s16[16,2176]{1,0:T(8,128)(2,1)S(1)} %collective-permute-done.3.refs_1_, ...), custom_call_target="tpu_custom_call" | custom-call | flops 134217728 | bytes 262144 | tf_op jit(solution)/shard_map/risks/pallas_call | solution.py:261
  16.7 1.9 %collective-permute-start.6 = (f32[8,128]{1,0:T(8,128)S(1)}, f32[8,128]{1,0:T(8,128)S(1)}, u32[]{:S(2)}, u32[]{:S(2)}) collective-permute-start(f32[8,128]{1,0:T(8,128)S(1)} %get-tuple-element.40.refs_0_), channel_id=1, source_target_pairs={{0,8},{8,0},{16,24},{24,16},{1,9},{9,1},{17,25},{25,17},{2,10},{10... | collective-permute-start | bytes 12296 | tf_op jit(solution)/shard_map/ppermute | solution.py:24
  18.6 0.8 %ordered_values.2 = (f32[16,1536]{1,0:T(8,128)S(1)}, f32[256,256]{1,0:T(8,128)S(1)}, f32[16,128]{1,0:T(8,128)S(1)}) custom-call(f32[16,4096]{1,0:T(8,128)S(1)} %get-tuple-element.47.own, f32[16,4096]{1,0:T(8,128)S(1)} %collective-permute-done.7.refs_1_.other, s16[16,2176]{1,0:T(8,128)(2,1)S(1)} %collective-permute-done.1.refs_0_, ...), custom_call_target="tpu_custom_call" | custom-call | flops 402653184 | bytes 589824 | tf_op jit(solution)/shard_map/ordered_values/pallas_call | solution.py:390
  19.4 1.0 %collective-permute-done.6.refs_1_ = f32[8,128]{1,0:T(8,128)S(1)} collective-permute-done((f32[8,128]{1,0:T(8,128)S(1)}, f32[8,128]{1,0:T(8,128)S(1)}, u32[]{:S(2)}, u32[]{:S(2)}) %collective-permute-start.6) | collective-permute-done | bytes 4128 | tf_op jit(solution)/shard_map/ppermute | solution.py:24
  20.4 2.9 %collective-permute-start.11 = (f32[8,128]{1,0:T(8,128)S(1)}, f32[8,128]{1,0:T(8,128)S(1)}, u32[]{:S(2)}, u32[]{:S(2)}) collective-permute-start(f32[8,128]{1,0:T(8,128)S(1)} %get-tuple-element.42.refs_0_), channel_id=1, source_target_pairs={{0,16},{8,24},{16,0},{24,8},{1,17},{9,25},{17,1},{25,9},{2,18},{10... | collective-permute-start | bytes 12296 | tf_op jit(solution)/shard_map/ppermute | solution.py:24
  23.3 1.2 %ordered_values.3 = (f32[16,2560]{1,0:T(8,128)S(1)}, f32[256,256]{1,0:T(8,128)S(1)}, f32[16,128]{1,0:T(8,128)S(1)}) custom-call(f32[16,4096]{1,0:T(8,128)S(1)} %get-tuple-element.47.own, f32[16,4096]{1,0:T(8,128)S(1)} %collective-permute-done.7.refs_1_.other, s16[16,2688]{1,0:T(8,128)(2,1)S(1)} %collective-permute-done.8.refs_3_.refs_0_, ...), custom_call_target="tpu_custom_call" | custom-call | flops 671088640 | bytes 983040 | tf_op jit(solution)/shard_map/ordered_values/pallas_call | solution.py:390
  25.1 3.9 %collective-permute-start.14 = (f32[40,128]{1,0:T(8,128)S(1)}, f32[40,128]{1,0:T(8,128)S(1)}, u32[]{:S(2)}, u32[]{:S(2)}) collective-permute-start(f32[40,128]{1,0:T(8,128)S(1)} %get-tuple-element.53.refs_0_), channel_id=1, source_target_pairs={{0,24},{8,16},{16,8},{24,0},{1,25},{9,17},{17,9},{25,1},{2,26},{10... | collective-permute-start | bytes 61448 | tf_op jit(solution)/shard_map/ppermute | solution.py:24
  29.6 1.7 %prefix_sums.1.refs_6_ = f32[16,4096]{1,0:T(8,128)S(1)} custom-call(f32[256,256]{1,0:T(8,128)S(1)} %suffix_sums.1.ordered.sums, f32[16,256]{1,0:T(8,128)S(1)} %get-tuple-element.56.squares.square, s32[1,4096]{1,0:T(1,128)S(1)} %bitcast.6), custom_call_target="tpu_custom_call" | custom-call | flops 1073741824 | bytes 1572864 | tf_op jit(solution)/shard_map/prefix_sums/pallas_call | solution.py:456
  31.4 0.9 %hazards.1 = (f32[1,4096]{1,0:T(1,128)S(1)}, f32[1,4096]{1,0:T(1,128)S(1)}) custom-call(f32[16,256]{1,0:T(8,128)S(1)} %get-tuple-element.57.hazard, f32[16,256]{1,0:T(8,128)S(1)} %get-tuple-element.56.squares.square, s32[1,4096]{1,0:T(1,128)S(1)} %bitcast.7), custom_call_target="tpu_custom_call" | custom-call | flops 209715200 | bytes 262144 | tf_op jit(solution)/shard_map/hazards/pallas_call | solution.py:324
  32.3 1.4 %collective-permute-done.13.refs_2_ = f32[40,128]{1,0:T(8,128)S(1)} collective-permute-done((f32[40,128]{1,0:T(8,128)S(1)}, f32[40,128]{1,0:T(8,128)S(1)}, u32[]{:S(2)}, u32[]{:S(2)}) %collective-permute-start.13) | collective-permute-done | bytes 20512 | tf_op jit(solution)/shard_map/ppermute | solution.py:24
  33.8 2.5 %collective-permute-start.20 = (bf16[16,4096]{1,0:T(8,128)(2,1)S(1)}, bf16[16,4096]{1,0:T(8,128)(2,1)S(1)}, u32[]{:S(2)}, u32[]{:S(2)}) collective-permute-start(bf16[16,4096]{1,0:T(8,128)(2,1)S(1)} %weights.1.refs_0_), channel_id=1, source_target_pairs={{0,6},{1,7},{2,4},{3,5},{4,2},{5,3},{6,0},{7,1},{8,14},{9,15},{10,... | collective-permute-start | bytes 393224 | tf_op jit(solution)/shard_map/ppermute | solution.py:24
  37.4 2.4 %collective-permute-done.20.refs_6_ = bf16[16,4096]{1,0:T(8,128)(2,1)S(1)} collective-permute-done((bf16[16,4096]{1,0:T(8,128)(2,1)S(1)}, bf16[16,4096]{1,0:T(8,128)(2,1)S(1)}, u32[]{:S(2)}, u32[]{:S(2)}) %collective-permute-start.20) | collective-permute-done | bytes 131104 | tf_op jit(solution)/shard_map/ppermute | solution.py:24
  39.8 1.6 %collective-permute-done.18.refs_4_ = bf16[16,4096]{1,0:T(8,128)(2,1)S(1)} collective-permute-done((bf16[16,4096]{1,0:T(8,128)(2,1)S(1)}, bf16[16,4096]{1,0:T(8,128)(2,1)S(1)}, u32[]{:S(2)}, u32[]{:S(2)}) %collective-permute-start.18) | collective-permute-done | bytes 131104 | tf_op jit(solution)/shard_map/ppermute | solution.py:24
  41.9 0.8 %collective-permute-done.19.refs_5_ = bf16[16,4096]{1,0:T(8,128)(2,1)S(1)} collective-permute-done((bf16[16,4096]{1,0:T(8,128)(2,1)S(1)}, bf16[16,4096]{1,0:T(8,128)(2,1)S(1)}, u32[]{:S(2)}, u32[]{:S(2)}) %collective-permute-start.19) | collective-permute-done | bytes 131104 | tf_op jit(solution)/shard_map/ppermute | solution.py:24
  44.6 2.1 %collective-permute-start.23 = (s16[272,128]{1,0:T(8,128)(2,1)S(1)}, s16[272,128]{1,0:T(8,128)(2,1)S(1)}, u32[]{:S(2)}, u32[]{:S(2)}) collective-permute-start(s16[272,128]{1,0:T(8,128)(2,1)S(1)} %gradients.3.mine), channel_id=1, source_target_pairs={{0,8},{8,0},{16,24},{24,16},{1,9},{9,1},{17,25},{25,17},{2,10},{10... | collective-permute-start | bytes 208904 | tf_op jit(solution)/shard_map/ppermute | solution.py:24
  46.6 2.2 %collective-permute-done.22.other = s16[272,128]{1,0:T(8,128)(2,1)S(1)} collective-permute-done((s16[272,128]{1,0:T(8,128)(2,1)S(1)}, s16[272,128]{1,0:T(8,128)(2,1)S(1)}, u32[]{:S(2)}, u32[]{:S(2)}) %collective-permute-start.22) | collective-permute-done | bytes 69664 | tf_op jit(solution)/shard_map/ppermute | solution.py:24
  49.0 1.7 %collective-permute-start.24 = (s16[272,128]{1,0:T(8,128)(2,1)S(1)}, s16[272,128]{1,0:T(8,128)(2,1)S(1)}, u32[]{:S(2)}, u32[]{:S(2)}) collective-permute-start(s16[272,128]{1,0:T(8,128)(2,1)S(1)} %merge.2.refs_0_), channel_id=1, source_target_pairs={{0,16},{8,24},{16,0},{24,8},{1,17},{9,25},{17,1},{25,9},{2,18},{10... | collective-permute-start | bytes 208904 | tf_op jit(solution)/shard_map/ppermute | solution.py:24
  50.7 1.6 %collective-permute-start.25 = (s16[272,128]{1,0:T(8,128)(2,1)S(1)}, s16[272,128]{1,0:T(8,128)(2,1)S(1)}, u32[]{:S(2)}, u32[]{:S(2)}) collective-permute-start(s16[272,128]{1,0:T(8,128)(2,1)S(1)} %merge.3.refs_1_), channel_id=1, source_target_pairs={{0,16},{8,24},{16,0},{24,8},{1,17},{9,25},{17,1},{25,9},{2,18},{10... | collective-permute-start | bytes 208904 | tf_op jit(solution)/shard_map/ppermute | solution.py:24
  52.3 3.1 %collective-permute-done.24.refs_2_ = s16[272,128]{1,0:T(8,128)(2,1)S(1)} collective-permute-done((s16[272,128]{1,0:T(8,128)(2,1)S(1)}, s16[272,128]{1,0:T(8,128)(2,1)S(1)}, u32[]{:S(2)}, u32[]{:S(2)}) %collective-permute-start.24) | collective-permute-done | bytes 69664 | tf_op jit(solution)/shard_map/ppermute | solution.py:24
  55.5 1.5 %collective-permute-done.25.refs_3_ = s16[272,128]{1,0:T(8,128)(2,1)S(1)} collective-permute-done((s16[272,128]{1,0:T(8,128)(2,1)S(1)}, s16[272,128]{1,0:T(8,128)(2,1)S(1)}, u32[]{:S(2)}, u32[]{:S(2)}) %collective-permute-start.25) | collective-permute-done | bytes 69664 | tf_op jit(solution)/shard_map/ppermute | solution.py:24
  57.0 0.8 %finish.1 = f32[512,128]{1,0:T(8,128)} custom-call(s16[272,128]{1,0:T(8,128)(2,1)S(1)} %merge.2.refs_0_, s16[272,128]{1,0:T(8,128)(2,1)S(1)} %merge.3.refs_1_, s16[272,128]{1,0:T(8,128)(2,1)S(1)} %collective-permute-done.24.refs_2_, s16[272,128]{1,0:T(8,128)(2,1)S(1)} %collective-permute-done.25.refs_3_, f32[8,128]{1,0:T(8,128)S(1)} %get-tuple-element.60.refs_4_), custom_call_target="tpu_custom_call" | custom-call | tf_op jit(solution)/shard_map/finish/pallas_call | solution.py:604
  (59 shorter events, 10.0 us)
Async XLA Ops:
  4.1 1.7 %collective-permute-start = (f32[16,4352]{1,0:T(8,128)S(1)}, f32[16,4352]{1,0:T(8,128)S(1)}, u32[]{:S(2)}, u32[]{:S(2)}) collective-permute-start(f32[16,4352]{1,0:T(8,128)S(1)} %get-tuple-element.34), channel_id=1, source_target_pairs={{0,1},{1,0},{2,3},{3,2},{4,5},{5,4},{6,7},{7,6},{8,9},{9,8},{10,11... | collective-permute-start | bytes 835592 | tf_op jit(solution)/shard_map/ppermute | solution.py:24
  4.6 5.2 %collective-permute-start.2 = (f32[16,4096]{1,0:T(8,128)S(1)}, f32[16,4096]{1,0:T(8,128)S(1)}, u32[]{:S(2)}, u32[]{:S(2)}) collective-permute-start(f32[16,4096]{1,0:T(8,128)S(1)} %get-tuple-element.37), channel_id=1, source_target_pairs={{0,1},{1,0},{2,3},{3,2},{4,5},{5,4},{6,7},{7,6},{8,9},{9,8},{10,11... | collective-permute-start | bytes 786440 | tf_op jit(solution)/shard_map/ppermute | solution.py:24
  4.7 5.8 %collective-permute-start.4 = (f32[16,4096]{1,0:T(8,128)S(1)}, f32[16,4096]{1,0:T(8,128)S(1)}, u32[]{:S(2)}, u32[]{:S(2)}) collective-permute-start(f32[16,4096]{1,0:T(8,128)S(1)} %get-tuple-element.39), channel_id=1, source_target_pairs={{0,1},{1,0},{2,3},{3,2},{4,5},{5,4},{6,7},{7,6},{8,9},{9,8},{10,11... | collective-permute-start | bytes 786440 | tf_op jit(solution)/shard_map/ppermute | solution.py:24
  5.2 5.8 %collective-permute-start.7 = (f32[16,4096]{1,0:T(8,128)S(1)}, f32[16,4096]{1,0:T(8,128)S(1)}, u32[]{:S(2)}, u32[]{:S(2)}) collective-permute-start(f32[16,4096]{1,0:T(8,128)S(1)} %get-tuple-element.41), channel_id=1, source_target_pairs={{0,1},{1,0},{2,3},{3,2},{4,5},{5,4},{6,7},{7,6},{8,9},{9,8},{10,11... | collective-permute-start | bytes 786440 | tf_op jit(solution)/shard_map/ppermute | solution.py:24
  6.0 8.8 %collective-permute-start.1 = (s16[16,2176]{1,0:T(8,128)(2,1)S(1)}, s16[16,2176]{1,0:T(8,128)(2,1)S(1)}, u32[]{:S(2)}, u32[]{:S(2)}) collective-permute-start(s16[16,2176]{1,0:T(8,128)(2,1)S(1)} %join.6), channel_id=1, source_target_pairs={{0,6},{1,7},{2,4},{3,5},{4,2},{5,3},{6,0},{7,1},{8,14},{9,15},{10,... | collective-permute-start | bytes 208904 | tf_op jit(solution)/shard_map/ppermute | solution.py:24
  10.0 5.7 %collective-permute-start.3 = (s16[16,2176]{1,0:T(8,128)(2,1)S(1)}, s16[16,2176]{1,0:T(8,128)(2,1)S(1)}, u32[]{:S(2)}, u32[]{:S(2)}) collective-permute-start(s16[16,2176]{1,0:T(8,128)(2,1)S(1)} %join.7), channel_id=1, source_target_pairs={{0,4},{1,5},{2,6},{3,7},{4,0},{5,1},{6,2},{7,3},{8,12},{9,13},{10,... | collective-permute-start | bytes 208904 | tf_op jit(solution)/shard_map/ppermute | solution.py:24
  10.7 5.1 %collective-permute-start.5 = (s16[16,2176]{1,0:T(8,128)(2,1)S(1)}, s16[16,2176]{1,0:T(8,128)(2,1)S(1)}, u32[]{:S(2)}, u32[]{:S(2)}) collective-permute-start(s16[16,2176]{1,0:T(8,128)(2,1)S(1)} %join.8), channel_id=1, source_target_pairs={{0,2},{1,3},{2,0},{3,1},{4,6},{5,7},{6,4},{7,5},{8,10},{9,11},{10,... | collective-permute-start | bytes 208904 | tf_op jit(solution)/shard_map/ppermute | solution.py:24
  11.1 9.3 %collective-permute-start.8 = (s16[16,2688]{1,0:T(8,128)(2,1)S(1)}, s16[16,2688]{1,0:T(8,128)(2,1)S(1)}, u32[]{:S(2)}, u32[]{:S(2)}) collective-permute-start(s16[16,2688]{1,0:T(8,128)(2,1)S(1)} %join.9), channel_id=1, source_target_pairs={{0,6},{1,7},{2,4},{3,5},{4,2},{5,3},{6,0},{7,1},{8,14},{9,15},{10,... | collective-permute-start | bytes 258056 | tf_op jit(solution)/shard_map/ppermute | solution.py:24
  14.0 6.3 %collective-permute-start.9 = (s16[16,2688]{1,0:T(8,128)(2,1)S(1)}, s16[16,2688]{1,0:T(8,128)(2,1)S(1)}, u32[]{:S(2)}, u32[]{:S(2)}) collective-permute-start(s16[16,2688]{1,0:T(8,128)(2,1)S(1)} %join.10), channel_id=1, source_target_pairs={{0,4},{1,5},{2,6},{3,7},{4,0},{5,1},{6,2},{7,3},{8,12},{9,13},{10,... | collective-permute-start | bytes 258056 | tf_op jit(solution)/shard_map/ppermute | solution.py:24
  14.7 5.6 %collective-permute-start.10 = (s16[16,2688]{1,0:T(8,128)(2,1)S(1)}, s16[16,2688]{1,0:T(8,128)(2,1)S(1)}, u32[]{:S(2)}, u32[]{:S(2)}) collective-permute-start(s16[16,2688]{1,0:T(8,128)(2,1)S(1)} %join.11), channel_id=1, source_target_pairs={{0,2},{1,3},{2,0},{3,1},{4,6},{5,7},{6,4},{7,5},{8,10},{9,11},{10,... | collective-permute-start | bytes 258056 | tf_op jit(solution)/shard_map/ppermute | solution.py:24
  16.7 3.7 %collective-permute-start.6 = (f32[8,128]{1,0:T(8,128)S(1)}, f32[8,128]{1,0:T(8,128)S(1)}, u32[]{:S(2)}, u32[]{:S(2)}) collective-permute-start(f32[8,128]{1,0:T(8,128)S(1)} %get-tuple-element.40.refs_0_), channel_id=1, source_target_pairs={{0,8},{8,0},{16,24},{24,16},{1,9},{9,1},{17,25},{25,17},{2,10},{10... | collective-permute-start | bytes 12296 | tf_op jit(solution)/shard_map/ppermute | solution.py:24
  20.4 4.6 %collective-permute-start.11 = (f32[8,128]{1,0:T(8,128)S(1)}, f32[8,128]{1,0:T(8,128)S(1)}, u32[]{:S(2)}, u32[]{:S(2)}) collective-permute-start(f32[8,128]{1,0:T(8,128)S(1)} %get-tuple-element.42.refs_0_), channel_id=1, source_target_pairs={{0,16},{8,24},{16,0},{24,8},{1,17},{9,25},{17,1},{25,9},{2,18},{10... | collective-permute-start | bytes 12296 | tf_op jit(solution)/shard_map/ppermute | solution.py:24
  25.1 7.2 %collective-permute-start.14 = (f32[40,128]{1,0:T(8,128)S(1)}, f32[40,128]{1,0:T(8,128)S(1)}, u32[]{:S(2)}, u32[]{:S(2)}) collective-permute-start(f32[40,128]{1,0:T(8,128)S(1)} %get-tuple-element.53.refs_0_), channel_id=1, source_target_pairs={{0,24},{8,16},{16,8},{24,0},{1,25},{9,17},{17,9},{25,1},{2,26},{10... | collective-permute-start | bytes 61448 | tf_op jit(solution)/shard_map/ppermute | solution.py:24
  29.0 4.7 %collective-permute-start.13 = (f32[40,128]{1,0:T(8,128)S(1)}, f32[40,128]{1,0:T(8,128)S(1)}, u32[]{:S(2)}, u32[]{:S(2)}) collective-permute-start(f32[40,128]{1,0:T(8,128)S(1)} %get-tuple-element.53.refs_0_), channel_id=1, source_target_pairs={{0,16},{8,24},{16,0},{24,8},{1,17},{9,25},{17,1},{25,9},{2,18},{10... | collective-permute-start | bytes 61448 | tf_op jit(solution)/shard_map/ppermute | solution.py:24
  29.0 4.7 %collective-permute-start.12 = (f32[40,128]{1,0:T(8,128)S(1)}, f32[40,128]{1,0:T(8,128)S(1)}, u32[]{:S(2)}, u32[]{:S(2)}) collective-permute-start(f32[40,128]{1,0:T(8,128)S(1)} %get-tuple-element.53.refs_0_), channel_id=1, source_target_pairs={{0,8},{8,0},{16,24},{24,16},{1,9},{9,1},{17,25},{25,17},{2,10},{10... | collective-permute-start | bytes 61448 | tf_op jit(solution)/shard_map/ppermute | solution.py:24
  33.8 5.9 %collective-permute-start.20 = (bf16[16,4096]{1,0:T(8,128)(2,1)S(1)}, bf16[16,4096]{1,0:T(8,128)(2,1)S(1)}, u32[]{:S(2)}, u32[]{:S(2)}) collective-permute-start(bf16[16,4096]{1,0:T(8,128)(2,1)S(1)} %weights.1.refs_0_), channel_id=1, source_target_pairs={{0,6},{1,7},{2,4},{3,5},{4,2},{5,3},{6,0},{7,1},{8,14},{9,15},{10,... | collective-permute-start | bytes 393224 | tf_op jit(solution)/shard_map/ppermute | solution.py:24
  36.4 5.0 %collective-permute-start.18 = (bf16[16,4096]{1,0:T(8,128)(2,1)S(1)}, bf16[16,4096]{1,0:T(8,128)(2,1)S(1)}, u32[]{:S(2)}, u32[]{:S(2)}) collective-permute-start(bf16[16,4096]{1,0:T(8,128)(2,1)S(1)} %weights.1.refs_0_), channel_id=1, source_target_pairs={{0,4},{1,5},{2,6},{3,7},{4,0},{5,1},{6,2},{7,3},{8,12},{9,13},{10,... | collective-permute-start | bytes 393224 | tf_op jit(solution)/shard_map/ppermute | solution.py:24
  36.9 5.0 %collective-permute-start.16 = (bf16[16,4096]{1,0:T(8,128)(2,1)S(1)}, bf16[16,4096]{1,0:T(8,128)(2,1)S(1)}, u32[]{:S(2)}, u32[]{:S(2)}) collective-permute-start(bf16[16,4096]{1,0:T(8,128)(2,1)S(1)} %weights.1.refs_0_), channel_id=1, source_target_pairs={{0,2},{1,3},{2,0},{3,1},{4,6},{5,7},{6,4},{7,5},{8,10},{9,11},{10,... | collective-permute-start | bytes 393224 | tf_op jit(solution)/shard_map/ppermute | solution.py:24
  37.4 4.5 %collective-permute-start.15 = (bf16[16,4096]{1,0:T(8,128)(2,1)S(1)}, bf16[16,4096]{1,0:T(8,128)(2,1)S(1)}, u32[]{:S(2)}, u32[]{:S(2)}) collective-permute-start(bf16[16,4096]{1,0:T(8,128)(2,1)S(1)} %weights.1.refs_0_), channel_id=1, source_target_pairs={{0,1},{1,0},{2,3},{3,2},{4,5},{5,4},{6,7},{7,6},{8,9},{9,8},{10,11... | collective-permute-start | bytes 393224 | tf_op jit(solution)/shard_map/ppermute | solution.py:24
  39.8 2.1 %collective-permute-start.21 = (bf16[16,4096]{1,0:T(8,128)(2,1)S(1)}, bf16[16,4096]{1,0:T(8,128)(2,1)S(1)}, u32[]{:S(2)}, u32[]{:S(2)}) collective-permute-start(bf16[16,4096]{1,0:T(8,128)(2,1)S(1)} %collective-permute-done.20.refs_6_), channel_id=1, source_target_pairs={{0,1},{1,0},{2,3},{3,2},{4,5},{5,4},{6,7},{7,6},{8,9},{9,8},{10,11... | collective-permute-start | bytes 393224 | tf_op jit(solution)/shard_map/ppermute | solution.py:24
  43.8 5.0 %collective-permute-start.22 = (s16[272,128]{1,0:T(8,128)(2,1)S(1)}, s16[272,128]{1,0:T(8,128)(2,1)S(1)}, u32[]{:S(2)}, u32[]{:S(2)}) collective-permute-start(s16[272,128]{1,0:T(8,128)(2,1)S(1)} %gradients.2.mine), channel_id=1, source_target_pairs={{0,8},{8,0},{16,24},{24,16},{1,9},{9,1},{17,25},{25,17},{2,10},{10... | collective-permute-start | bytes 208904 | tf_op jit(solution)/shard_map/ppermute | solution.py:24
  44.6 6.0 %collective-permute-start.23 = (s16[272,128]{1,0:T(8,128)(2,1)S(1)}, s16[272,128]{1,0:T(8,128)(2,1)S(1)}, u32[]{:S(2)}, u32[]{:S(2)}) collective-permute-start(s16[272,128]{1,0:T(8,128)(2,1)S(1)} %gradients.3.mine), channel_id=1, source_target_pairs={{0,8},{8,0},{16,24},{24,16},{1,9},{9,1},{17,25},{25,17},{2,10},{10... | collective-permute-start | bytes 208904 | tf_op jit(solution)/shard_map/ppermute | solution.py:24
  49.0 6.5 %collective-permute-start.24 = (s16[272,128]{1,0:T(8,128)(2,1)S(1)}, s16[272,128]{1,0:T(8,128)(2,1)S(1)}, u32[]{:S(2)}, u32[]{:S(2)}) collective-permute-start(s16[272,128]{1,0:T(8,128)(2,1)S(1)} %merge.2.refs_0_), channel_id=1, source_target_pairs={{0,16},{8,24},{16,0},{24,8},{1,17},{9,25},{17,1},{25,9},{2,18},{10... | collective-permute-start | bytes 208904 | tf_op jit(solution)/shard_map/ppermute | solution.py:24
  50.7 6.3 %collective-permute-start.25 = (s16[272,128]{1,0:T(8,128)(2,1)S(1)}, s16[272,128]{1,0:T(8,128)(2,1)S(1)}, u32[]{:S(2)}, u32[]{:S(2)}) collective-permute-start(s16[272,128]{1,0:T(8,128)(2,1)S(1)} %merge.3.refs_1_), channel_id=1, source_target_pairs={{0,16},{8,24},{16,0},{24,8},{1,17},{9,25},{17,1},{25,9},{2,18},{10... | collective-permute-start | bytes 208904 | tf_op jit(solution)/shard_map/ppermute | solution.py:24
  (5 other events, 52.2 us)

commit v13 on v12

--- a/solution.py
+++ b/solution.py
@@ -13,7 +13,7 @@
 NT = (((1,), (1,)), ((), ()))
 BLOCK = 64
 SPAN = 512
-AHEAD = 3
+SPLIT = 2
 VMEM = pl.BlockSpec(memory_space=pltpu.VMEM)
 HBM = pl.BlockSpec(memory_space=pltpu.HBM)
 PARAMS = dict(vmem_limit_bytes=24 * 1024 * 1024)
@@ -77,16 +77,17 @@
     persons, variants = table.shape
     steps = persons // chunk
     small = [
-        pltpu.make_async_copy(directions, own_directions, sems.at[steps]),
-        pltpu.make_async_copy(coefficients, own_coefficients, sems.at[steps + 1]),
+        pltpu.make_async_copy(directions, own_directions, sems.at[SPLIT * steps]),
+        pltpu.make_async_copy(coefficients, own_coefficients, sems.at[SPLIT * steps + 1]),
     ]
+    piece = chunk // SPLIT
     large = [
         pltpu.make_async_copy(
-            dosages.at[pl.ds(i * chunk, chunk)], table.at[pl.ds(i * chunk, chunk)], sems.at[i]
+            dosages.at[pl.ds(i * piece, piece)], table.at[pl.ds(i * piece, piece)], sems.at[i]
         )
-        for i in range(steps)
+        for i in range(SPLIT * steps)
     ]
-    for copy in small + large[:AHEAD]:
+    for copy in small + large:
         copy.start()
     for copy in small:
         copy.wait()
@@ -95,9 +96,8 @@
         lhs[j * kf : (j + 1) * kf] = turned[me ^ j].astype(BF16)
     lhs[width:] = jnp.broadcast_to(own_coefficients[...].astype(F32)[None, :], (16, variants)).astype(BF16)
     for i in range(steps):
-        large[i].wait()
-        if i + AHEAD < steps:
-            large[i + AHEAD].start()
+        for copy in large[i * SPLIT : (i + 1) * SPLIT]:
+            copy.wait()
         first = i * chunk
         result = lax.dot_general(
             lhs[...], table[first : first + chunk], NT, preferred_element_type=F32
@@ -131,7 +131,7 @@
             pltpu.VMEM((variants,), BF16),
             pltpu.VMEM((k + 16, variants), BF16),
             pltpu.VMEM((feat, kf, variants), F32),
-            pltpu.SemaphoreType.DMA((persons // chunk + 2,)),
+            pltpu.SemaphoreType.DMA((SPLIT * (persons // chunk) + 2,)),
         ],
         compiler_params=pltpu.CompilerParams(**PARAMS),
         cost_estimate=pl.CostEstimate(
@@ -466,44 +466,68 @@
     )(sums, squares, rank)
 
 
-def weight_kernel(ex, *refs):
-    messages, (first, rest, local, risk, cumulative, squares) = refs[:ex], refs[ex : ex + 6]
-    weighted, placed = refs[ex + 6 :]
-    kf = first.shape[0]
-    me = lax.axis_index("ex")
-    for i in range(ex):
-        placed[me ^ i] = messages[i][...]
-    later = jnp.zeros((kf, 128), F32)
-    own_later, before = later, later
-    hazard_before = jnp.zeros((1, 128), F32)
-    for b in reversed(range(ex)):
-        plain, scaled, square = placed[b, :kf], placed[b, kf : 2 * kf], placed[b, 2 * kf + 1 : 2 * kf + 2]
-        own_later = own_later + jnp.where(b > me, plain, 0.0)
-        before = before + jnp.where(b < me, scaled + square * later, 0.0)
-        hazard_before = hazard_before + jnp.where(b < me, placed[b, 2 * kf : 2 * kf + 1], 0.0)
-        later = later + plain
-    own_later = jnp.sum(own_later, axis=1, keepdims=True)
-    before = jnp.sum(before, axis=1, keepdims=True)
-    hazard_before = hazard_before[:, :1]
+def merged(kf, bit, mine, other, state):
+    later_other = (lax.axis_index("ex") & bit) == 0
+    plain, scaled, rest = mine[:kf], mine[kf : 2 * kf], mine[2 * kf :]
+    other_plain, other_scaled, other_rest = other[:kf], other[kf : 2 * kf], other[2 * kf :]
+    square, other_square = rest[1:2], other_rest[1:2]
+    crossed = jnp.where(later_other, square * other_plain, other_square * plain)
+    total = jnp.concatenate([plain + other_plain, scaled + other_scaled + crossed, rest + other_rest], axis=0)
+    if state is None:
+        state = jnp.zeros_like(mine)
+    later, before, before_rest = state[:kf], state[kf : 2 * kf], state[2 * kf :]
+    state = jnp.concatenate(
+        [
+            later + jnp.where(later_other, other_plain, 0.0),
+            before + jnp.where(later_other, before_rest[1:2] * other_plain, other_scaled + other_square * plain),
+            before_rest + jnp.where(later_other, 0.0, other_rest),
+        ],
+        axis=0,
+    )
+    return total, state
+
+
+def combine_kernel(kf, bit, count, *refs):
+    inputs, (total, state) = [ref[...] for ref in refs[:count]], refs[count + 1 :]
+    total[...], state[...] = merged(kf, bit, inputs[0], inputs[1], inputs[2] if count > 2 else None)
+
+
+def combine(kf, bit, inputs, waited):
+    shape = jax.ShapeDtypeStruct(inputs[0].shape, F32)
+    return pl.pallas_call(
+        functools.partial(combine_kernel, kf, bit, len(inputs)),
+        in_specs=[VMEM] * len(inputs) + [pl.BlockSpec(memory_space=pl.ANY)],
+        out_shape=[shape, shape],
+        out_specs=[VMEM] * 2,
+        compiler_params=pltpu.CompilerParams(**PARAMS),
+        name="combine",
+    )(*inputs, waited)
+
+
+def weight_kernel(kf, bit, count, *refs):
+    inputs = [ref[...] for ref in refs[:count]]
+    first, rest, local, risk, cumulative, squares, weighted = refs[count:]
+    _, state = merged(kf, bit, inputs[0], inputs[1], inputs[2] if count > 2 else None)
+    later = jnp.sum(state[:kf], axis=1, keepdims=True)
+    before = jnp.sum(state[kf : 2 * kf], axis=1, keepdims=True)
+    hazard_before = state[2 * kf : 2 * kf + 1, :1]
     for start, part in ((0, first), (first.shape[1], rest)):
         at = slice(start, start + part.shape[1])
         value = part[...] * (cumulative[:, at] + hazard_before) - (
-            local[:, at] + squares[:, at] * own_later + before
+            local[:, at] + squares[:, at] * later + before
         )
         weighted[:, at] = (risk[:, at] * value).astype(BF16)
 
 
-def weights(messages, first, rest, local, risk, cumulative, squares):
-    ex = len(messages)
-    return pl.pallas_call(
-        functools.partial(weight_kernel, ex),
-        in_specs=[VMEM] * (ex + 6),
+def weights(bit, inputs, first, rest, local, risk, cumulative, squares):
+    return pl.pallas_call(
+        functools.partial(weight_kernel, first.shape[0], bit, len(inputs)),
+        in_specs=[VMEM] * (len(inputs) + 6),
         out_shape=jax.ShapeDtypeStruct(local.shape, BF16),
         out_specs=VMEM,
-        scratch_shapes=[pltpu.VMEM((ex,) + messages[0].shape, F32)],
         compiler_params=pltpu.CompilerParams(**PARAMS),
         name="weights",
-    )(*messages, first, rest, local, risk, cumulative, squares)
+    )(*inputs, first, rest, local, risk, cumulative, squares)
 
 
 def encode(values, message):
@@ -649,10 +673,14 @@
     )
     later_sums = suffix_sums(one, two, padded)
     hazard, ordered_squares, message = shares(later, sums, ordered_events, plain, more, later_sums)
-    messages = [message] + [swap(message, "ex", i) for i in range(1, ex)]
     cumulative, squares = hazards(hazard, ordered_squares, rank, rows)
+    state, bit = [], 1
+    while 2 * bit < ex:
+        message, *state = combine(padded, bit, [message, swap(message, "ex", bit)] + state, cumulative)
+        bit *= 2
+    inputs = [message, swap(message, "ex", bit)] + state
     summed = prefix_sums(later_sums, ordered_squares, rank, padded)
-    own = weights(messages, tangent, more_tangent, summed, risk, cumulative, squares)
+    own = weights(bit, inputs, tangent, more_tangent, summed, risk, cumulative, squares)
 
     chips = {0: own}
     for q in reversed(range(1, feat // 2)):

time: 57.9 us -> 57.8 us (level)
  starting transfers between devices: 27.9 us -> 30.2 us
  waiting for transfers between devices: 15.8 us -> 13.7 us
    ppermute x26 -> x25, starting transfers between devices: 27.9 us -> 30.2 us  [swap(): return lax.ppermute(x, axis, [(s, s ^ i) for s in range(count)])]
    ppermute x26 -> x25, waiting for transfers between devices: 15.8 us -> 13.7 us  [swap(): return lax.ppermute(x, axis, [(s, s ^ i) for s in range(count)])]
  transfers between devices with their start and end apart: 26 -> 25, of which waited for: 13 -> 14; matrix products, arithmetic and copies ran while one was open for 0% -> 0% of each run, Pallas kernels for 14% -> 14%
where the time goes in v13:
time: 57.8 us; the launch traced here: 57.7 us
  starting transfers between devices  30.2 us (52%)
  waiting for transfers between devices  13.7 us (24%)
  Pallas kernels  13.6 us (24%)
    ppermute x25, starting transfers between devices, swap(): return lax.ppermute(x, axis, [(s, s ^ i) for s in range(count)])  30.2 us
    ppermute x25, waiting for transfers between devices, swap(): return lax.ppermute(x, axis, [(s, s ^ i) for s in range(count)])  13.7 us
    pallas_call x1, Pallas kernels, products(): pl.pallas_call(functools.partial(product_kernel, feat, kf, chunk), in_spe...  3.84 us
    pallas_call x2, Pallas kernels, ordered_values(): pl.pallas_call(functools.partial(order_kernel, start, len(messages)), in_...  1.97 us
    pallas_call x1, Pallas kernels, prefix_sums(): pl.pallas_call(prefix_kernel, in_specs=[VMEM] * 3, out_shape=jax.ShapeDty...  1.75 us
    pallas_call x2, Pallas kernels, gradients(): pl.pallas_call(functools.partial(gradient_kernel, feat, kf, start), in_sp...  1.28 us
  transfers between devices with their start and end apart: 25, of which 14 were waited for; matrix products, arithmetic and copies ran while one was open for 0% of the time, Pallas kernels for 14%

profile of v13, /device:TPU:0, one launch (start us, length us, event | category | flops | bytes accessed | tf_op | source)
XLA Modules:
  0.0 57.7 jit_solution(17172104865708655100)
XLA Ops:
  0.0 3.8 %products.1 = (f32[16,256]{1,0:T(8,128)S(1)}, f32[16,4096]{1,0:T(8,128)S(1)}, f32[16,4096]{1,0:T(8,128)S(1)}, f32[16,4096]{1,0:T(8,128)S(1)}, f32[16,4096]{1,0:T...) custom-call(bf16[512,128]{1,0:T(8,128)(2,1)} %directions.1, ...), custom_call_target="tpu_custom_call" | custom-call | flops 536870912 | bytes 6291456 | tf_op jit(solution)/shard_map/products/pallas_call | solution.py:121
  5.7 3.9 %collective-permute-start.1 = (s16[16,2176]{1,0:T(8,128)(2,1)S(1)}, s16[16,2176]{1,0:T(8,128)(2,1)S(1)}, u32[]{:S(2)}, u32[]{:S(2)}) collective-permute-start(s16[16,2176]{1,0:T(8,128)(2,1)S(1)} %join.6), channel_id=1, source_target_pairs={{0,6},{1,7},{2,4},{3,5},{4,2},{5,3},{6,0},{7,1},{8,14},{9,15},{10,... | collective-permute-start | bytes 208904 | tf_op jit(solution)/shard_map/ppermute | solution.py:24
  10.8 2.8 %collective-permute-start.8 = (s16[16,2688]{1,0:T(8,128)(2,1)S(1)}, s16[16,2688]{1,0:T(8,128)(2,1)S(1)}, u32[]{:S(2)}, u32[]{:S(2)}) collective-permute-start(s16[16,2688]{1,0:T(8,128)(2,1)S(1)} %join.9), channel_id=1, source_target_pairs={{0,6},{1,7},{2,4},{3,5},{4,2},{5,3},{6,0},{7,1},{8,14},{9,15},{10,... | collective-permute-start | bytes 258056 | tf_op jit(solution)/shard_map/ppermute | solution.py:24
  15.5 0.9 %risks.1 = (f32[1,4096]{1,0:T(1,128)S(1)}, f32[16,256]{1,0:T(8,128)S(1)}, f32[16,256]{1,0:T(8,128)S(1)}, f32[8,128]{1,0:T(8,128)S(1)}) custom-call(f32[16,256]{1,0:T(8,128)S(1)} %pair.1.refs_0_.waited.linear, s16[16,2176]{1,0:T(8,128)(2,1)S(1)} %collective-permute-done.1.refs_0_, s16[16,2176]{1,0:T(8,128)(2,1)S(1)} %collective-permute-done.3.refs_1_, ...), custom_call_target="tpu_custom_call" | custom-call | flops 134217728 | bytes 262144 | tf_op jit(solution)/shard_map/risks/pallas_call | solution.py:261
  16.4 1.9 %collective-permute-start.6 = (f32[8,128]{1,0:T(8,128)S(1)}, f32[8,128]{1,0:T(8,128)S(1)}, u32[]{:S(2)}, u32[]{:S(2)}) collective-permute-start(f32[8,128]{1,0:T(8,128)S(1)} %get-tuple-element.42.refs_0_), channel_id=1, source_target_pairs={{0,8},{8,0},{16,24},{24,16},{1,9},{9,1},{17,25},{25,17},{2,10},{10... | collective-permute-start | bytes 12296 | tf_op jit(solution)/shard_map/ppermute | solution.py:24
  18.3 0.8 %ordered_values.2 = (f32[16,1536]{1,0:T(8,128)S(1)}, f32[256,256]{1,0:T(8,128)S(1)}, f32[16,128]{1,0:T(8,128)S(1)}) custom-call(f32[16,4096]{1,0:T(8,128)S(1)} %get-tuple-element.49.own, f32[16,4096]{1,0:T(8,128)S(1)} %collective-permute-done.7.refs_1_.other, s16[16,2176]{1,0:T(8,128)(2,1)S(1)} %collective-permute-done.1.refs_0_, ...), custom_call_target="tpu_custom_call" | custom-call | flops 402653184 | bytes 589824 | tf_op jit(solution)/shard_map/ordered_values/pallas_call | solution.py:390
  19.1 1.0 %collective-permute-done.6.refs_1_ = f32[8,128]{1,0:T(8,128)S(1)} collective-permute-done((f32[8,128]{1,0:T(8,128)S(1)}, f32[8,128]{1,0:T(8,128)S(1)}, u32[]{:S(2)}, u32[]{:S(2)}) %collective-permute-start.6) | collective-permute-done | bytes 4128 | tf_op jit(solution)/shard_map/ppermute | solution.py:24
  20.1 2.9 %collective-permute-start.11 = (f32[8,128]{1,0:T(8,128)S(1)}, f32[8,128]{1,0:T(8,128)S(1)}, u32[]{:S(2)}, u32[]{:S(2)}) collective-permute-start(f32[8,128]{1,0:T(8,128)S(1)} %get-tuple-element.44.refs_0_), channel_id=1, source_target_pairs={{0,16},{8,24},{16,0},{24,8},{1,17},{9,25},{17,1},{25,9},{2,18},{10... | collective-permute-start | bytes 12296 | tf_op jit(solution)/shard_map/ppermute | solution.py:24
  23.0 1.2 %ordered_values.3 = (f32[16,2560]{1,0:T(8,128)S(1)}, f32[256,256]{1,0:T(8,128)S(1)}, f32[16,128]{1,0:T(8,128)S(1)}) custom-call(f32[16,4096]{1,0:T(8,128)S(1)} %get-tuple-element.49.own, f32[16,4096]{1,0:T(8,128)S(1)} %collective-permute-done.7.refs_1_.other, s16[16,2688]{1,0:T(8,128)(2,1)S(1)} %collective-permute-done.8.refs_3_.refs_0_, ...), custom_call_target="tpu_custom_call" | custom-call | flops 671088640 | bytes 983040 | tf_op jit(solution)/shard_map/ordered_values/pallas_call | solution.py:390
  24.8 1.8 %collective-permute-start.12 = (f32[40,128]{1,0:T(8,128)S(1)}, f32[40,128]{1,0:T(8,128)S(1)}, u32[]{:S(2)}, u32[]{:S(2)}) collective-permute-start(f32[40,128]{1,0:T(8,128)S(1)} %get-tuple-element.55.refs_0_), channel_id=1, source_target_pairs={{0,8},{8,0},{16,24},{24,16},{1,9},{9,1},{17,25},{25,17},{2,10},{10... | collective-permute-start | bytes 61448 | tf_op jit(solution)/shard_map/ppermute | solution.py:24
  26.7 0.9 %hazards.1 = (f32[1,4096]{1,0:T(1,128)S(1)}, f32[1,4096]{1,0:T(1,128)S(1)}) custom-call(f32[16,256]{1,0:T(8,128)S(1)} %get-tuple-element.56.hazard, f32[16,256]{1,0:T(8,128)S(1)} %get-tuple-element.57.square.squares, s32[1,4096]{1,0:T(1,128)S(1)} %bitcast.6), custom_call_target="tpu_custom_call" | custom-call | flops 209715200 | bytes 262144 | tf_op jit(solution)/shard_map/hazards/pallas_call | solution.py:324
  27.6 1.2 %collective-permute-done.12.refs_1_ = f32[40,128]{1,0:T(8,128)S(1)} collective-permute-done((f32[40,128]{1,0:T(8,128)S(1)}, f32[40,128]{1,0:T(8,128)S(1)}, u32[]{:S(2)}, u32[]{:S(2)}) %collective-permute-start.12) | collective-permute-done | bytes 20512 | tf_op jit(solution)/shard_map/ppermute | solution.py:24
  28.8 2.7 %collective-permute-start.13 = (f32[40,128]{1,0:T(8,128)S(1)}, f32[40,128]{1,0:T(8,128)S(1)}, u32[]{:S(2)}, u32[]{:S(2)}) collective-permute-start(f32[40,128]{1,0:T(8,128)S(1)} %get-tuple-element.59.refs_0_), channel_id=1, source_target_pairs={{0,16},{8,24},{16,0},{24,8},{1,17},{9,25},{17,1},{25,9},{2,18},{10... | collective-permute-start | bytes 61448 | tf_op jit(solution)/shard_map/ppermute | solution.py:24
  31.6 1.8 %prefix_sums.1.refs_5_ = f32[16,4096]{1,0:T(8,128)S(1)} custom-call(f32[256,256]{1,0:T(8,128)S(1)} %suffix_sums.1.ordered.sums, f32[16,256]{1,0:T(8,128)S(1)} %get-tuple-element.57.square.squares, s32[1,4096]{1,0:T(1,128)S(1)} %bitcast.7), custom_call_target="tpu_custom_call" | custom-call | flops 1073741824 | bytes 1572864 | tf_op jit(solution)/shard_map/prefix_sums/pallas_call | solution.py:456
  33.8 2.7 %collective-permute-start.19 = (bf16[16,4096]{1,0:T(8,128)(2,1)S(1)}, bf16[16,4096]{1,0:T(8,128)(2,1)S(1)}, u32[]{:S(2)}, u32[]{:S(2)}) collective-permute-start(bf16[16,4096]{1,0:T(8,128)(2,1)S(1)} %weights.1.refs_0_), channel_id=1, source_target_pairs={{0,6},{1,7},{2,4},{3,5},{4,2},{5,3},{6,0},{7,1},{8,14},{9,15},{10,... | collective-permute-start | bytes 393224 | tf_op jit(solution)/shard_map/ppermute | solution.py:24
  37.3 2.4 %collective-permute-done.19.refs_6_ = bf16[16,4096]{1,0:T(8,128)(2,1)S(1)} collective-permute-done((bf16[16,4096]{1,0:T(8,128)(2,1)S(1)}, bf16[16,4096]{1,0:T(8,128)(2,1)S(1)}, u32[]{:S(2)}, u32[]{:S(2)}) %collective-permute-start.19) | collective-permute-done | bytes 131104 | tf_op jit(solution)/shard_map/ppermute | solution.py:24
  39.7 1.8 %collective-permute-done.17.refs_4_ = bf16[16,4096]{1,0:T(8,128)(2,1)S(1)} collective-permute-done((bf16[16,4096]{1,0:T(8,128)(2,1)S(1)}, bf16[16,4096]{1,0:T(8,128)(2,1)S(1)}, u32[]{:S(2)}, u32[]{:S(2)}) %collective-permute-start.17) | collective-permute-done | bytes 131104 | tf_op jit(solution)/shard_map/ppermute | solution.py:24
  42.0 0.8 %collective-permute-done.18.refs_5_ = bf16[16,4096]{1,0:T(8,128)(2,1)S(1)} collective-permute-done((bf16[16,4096]{1,0:T(8,128)(2,1)S(1)}, bf16[16,4096]{1,0:T(8,128)(2,1)S(1)}, u32[]{:S(2)}, u32[]{:S(2)}) %collective-permute-start.18) | collective-permute-done | bytes 131104 | tf_op jit(solution)/shard_map/ppermute | solution.py:24
  44.0 1.5 %collective-permute-start.21 = (s16[272,128]{1,0:T(8,128)(2,1)S(1)}, s16[272,128]{1,0:T(8,128)(2,1)S(1)}, u32[]{:S(2)}, u32[]{:S(2)}) collective-permute-start(s16[272,128]{1,0:T(8,128)(2,1)S(1)} %gradients.2.mine), channel_id=1, source_target_pairs={{0,8},{8,0},{16,24},{24,16},{1,9},{9,1},{17,25},{25,17},{2,10},{10... | collective-permute-start | bytes 208904 | tf_op jit(solution)/shard_map/ppermute | solution.py:24
  46.8 1.6 %collective-permute-done.21.other = s16[272,128]{1,0:T(8,128)(2,1)S(1)} collective-permute-done((s16[272,128]{1,0:T(8,128)(2,1)S(1)}, s16[272,128]{1,0:T(8,128)(2,1)S(1)}, u32[]{:S(2)}, u32[]{:S(2)}) %collective-permute-start.21) | collective-permute-done | bytes 69664 | tf_op jit(solution)/shard_map/ppermute | solution.py:24
  48.4 2.5 %collective-permute-start.23 = (s16[272,128]{1,0:T(8,128)(2,1)S(1)}, s16[272,128]{1,0:T(8,128)(2,1)S(1)}, u32[]{:S(2)}, u32[]{:S(2)}) collective-permute-start(s16[272,128]{1,0:T(8,128)(2,1)S(1)} %merge.2.refs_0_), channel_id=1, source_target_pairs={{0,16},{8,24},{16,0},{24,8},{1,17},{9,25},{17,1},{25,9},{2,18},{10... | collective-permute-start | bytes 208904 | tf_op jit(solution)/shard_map/ppermute | solution.py:24
  51.0 3.0 %collective-permute-start.24 = (s16[272,128]{1,0:T(8,128)(2,1)S(1)}, s16[272,128]{1,0:T(8,128)(2,1)S(1)}, u32[]{:S(2)}, u32[]{:S(2)}) collective-permute-start(s16[272,128]{1,0:T(8,128)(2,1)S(1)} %merge.3.refs_1_), channel_id=1, source_target_pairs={{0,16},{8,24},{16,0},{24,8},{1,17},{9,25},{17,1},{25,9},{2,18},{10... | collective-permute-start | bytes 208904 | tf_op jit(solution)/shard_map/ppermute | solution.py:24
  54.0 2.0 %collective-permute-done.23.refs_2_ = s16[272,128]{1,0:T(8,128)(2,1)S(1)} collective-permute-done((s16[272,128]{1,0:T(8,128)(2,1)S(1)}, s16[272,128]{1,0:T(8,128)(2,1)S(1)}, u32[]{:S(2)}, u32[]{:S(2)}) %collective-permute-start.23) | collective-permute-done | bytes 69664 | tf_op jit(solution)/shard_map/ppermute | solution.py:24
  56.0 0.9 %collective-permute-done.24.refs_3_ = s16[272,128]{1,0:T(8,128)(2,1)S(1)} collective-permute-done((s16[272,128]{1,0:T(8,128)(2,1)S(1)}, s16[272,128]{1,0:T(8,128)(2,1)S(1)}, u32[]{:S(2)}, u32[]{:S(2)}) %collective-permute-start.24) | collective-permute-done | bytes 69664 | tf_op jit(solution)/shard_map/ppermute | solution.py:24
  (58 shorter events, 10.7 us)
Async XLA Ops:
  3.9 1.7 %collective-permute-start = (f32[16,4352]{1,0:T(8,128)S(1)}, f32[16,4352]{1,0:T(8,128)S(1)}, u32[]{:S(2)}, u32[]{:S(2)}) collective-permute-start(f32[16,4352]{1,0:T(8,128)S(1)} %get-tuple-element.36), channel_id=1, source_target_pairs={{0,1},{1,0},{2,3},{3,2},{4,5},{5,4},{6,7},{7,6},{8,9},{9,8},{10,11... | collective-permute-start | bytes 835592 | tf_op jit(solution)/shard_map/ppermute | solution.py:24
  4.4 5.2 %collective-permute-start.2 = (f32[16,4096]{1,0:T(8,128)S(1)}, f32[16,4096]{1,0:T(8,128)S(1)}, u32[]{:S(2)}, u32[]{:S(2)}) collective-permute-start(f32[16,4096]{1,0:T(8,128)S(1)} %get-tuple-element.39), channel_id=1, source_target_pairs={{0,1},{1,0},{2,3},{3,2},{4,5},{5,4},{6,7},{7,6},{8,9},{9,8},{10,11... | collective-permute-start | bytes 786440 | tf_op jit(solution)/shard_map/ppermute | solution.py:24
  4.5 5.8 %collective-permute-start.4 = (f32[16,4096]{1,0:T(8,128)S(1)}, f32[16,4096]{1,0:T(8,128)S(1)}, u32[]{:S(2)}, u32[]{:S(2)}) collective-permute-start(f32[16,4096]{1,0:T(8,128)S(1)} %get-tuple-element.41), channel_id=1, source_target_pairs={{0,1},{1,0},{2,3},{3,2},{4,5},{5,4},{6,7},{7,6},{8,9},{9,8},{10,11... | collective-permute-start | bytes 786440 | tf_op jit(solution)/shard_map/ppermute | solution.py:24
  4.9 5.8 %collective-permute-start.7 = (f32[16,4096]{1,0:T(8,128)S(1)}, f32[16,4096]{1,0:T(8,128)S(1)}, u32[]{:S(2)}, u32[]{:S(2)}) collective-permute-start(f32[16,4096]{1,0:T(8,128)S(1)} %get-tuple-element.43), channel_id=1, source_target_pairs={{0,1},{1,0},{2,3},{3,2},{4,5},{5,4},{6,7},{7,6},{8,9},{9,8},{10,11... | collective-permute-start | bytes 786440 | tf_op jit(solution)/shard_map/ppermute | solution.py:24
  5.7 8.8 %collective-permute-start.1 = (s16[16,2176]{1,0:T(8,128)(2,1)S(1)}, s16[16,2176]{1,0:T(8,128)(2,1)S(1)}, u32[]{:S(2)}, u32[]{:S(2)}) collective-permute-start(s16[16,2176]{1,0:T(8,128)(2,1)S(1)} %join.6), channel_id=1, source_target_pairs={{0,6},{1,7},{2,4},{3,5},{4,2},{5,3},{6,0},{7,1},{8,14},{9,15},{10,... | collective-permute-start | bytes 208904 | tf_op jit(solution)/shard_map/ppermute | solution.py:24
  9.7 5.7 %collective-permute-start.3 = (s16[16,2176]{1,0:T(8,128)(2,1)S(1)}, s16[16,2176]{1,0:T(8,128)(2,1)S(1)}, u32[]{:S(2)}, u32[]{:S(2)}) collective-permute-start(s16[16,2176]{1,0:T(8,128)(2,1)S(1)} %join.7), channel_id=1, source_target_pairs={{0,4},{1,5},{2,6},{3,7},{4,0},{5,1},{6,2},{7,3},{8,12},{9,13},{10,... | collective-permute-start | bytes 208904 | tf_op jit(solution)/shard_map/ppermute | solution.py:24
  10.4 5.1 %collective-permute-start.5 = (s16[16,2176]{1,0:T(8,128)(2,1)S(1)}, s16[16,2176]{1,0:T(8,128)(2,1)S(1)}, u32[]{:S(2)}, u32[]{:S(2)}) collective-permute-start(s16[16,2176]{1,0:T(8,128)(2,1)S(1)} %join.8), channel_id=1, source_target_pairs={{0,2},{1,3},{2,0},{3,1},{4,6},{5,7},{6,4},{7,5},{8,10},{9,11},{10,... | collective-permute-start | bytes 208904 | tf_op jit(solution)/shard_map/ppermute | solution.py:24
  10.8 9.3 %collective-permute-start.8 = (s16[16,2688]{1,0:T(8,128)(2,1)S(1)}, s16[16,2688]{1,0:T(8,128)(2,1)S(1)}, u32[]{:S(2)}, u32[]{:S(2)}) collective-permute-start(s16[16,2688]{1,0:T(8,128)(2,1)S(1)} %join.9), channel_id=1, source_target_pairs={{0,6},{1,7},{2,4},{3,5},{4,2},{5,3},{6,0},{7,1},{8,14},{9,15},{10,... | collective-permute-start | bytes 258056 | tf_op jit(solution)/shard_map/ppermute | solution.py:24
  13.8 6.3 %collective-permute-start.9 = (s16[16,2688]{1,0:T(8,128)(2,1)S(1)}, s16[16,2688]{1,0:T(8,128)(2,1)S(1)}, u32[]{:S(2)}, u32[]{:S(2)}) collective-permute-start(s16[16,2688]{1,0:T(8,128)(2,1)S(1)} %join.10), channel_id=1, source_target_pairs={{0,4},{1,5},{2,6},{3,7},{4,0},{5,1},{6,2},{7,3},{8,12},{9,13},{10,... | collective-permute-start | bytes 258056 | tf_op jit(solution)/shard_map/ppermute | solution.py:24
  14.5 5.6 %collective-permute-start.10 = (s16[16,2688]{1,0:T(8,128)(2,1)S(1)}, s16[16,2688]{1,0:T(8,128)(2,1)S(1)}, u32[]{:S(2)}, u32[]{:S(2)}) collective-permute-start(s16[16,2688]{1,0:T(8,128)(2,1)S(1)} %join.11), channel_id=1, source_target_pairs={{0,2},{1,3},{2,0},{3,1},{4,6},{5,7},{6,4},{7,5},{8,10},{9,11},{10,... | collective-permute-start | bytes 258056 | tf_op jit(solution)/shard_map/ppermute | solution.py:24
  16.4 3.7 %collective-permute-start.6 = (f32[8,128]{1,0:T(8,128)S(1)}, f32[8,128]{1,0:T(8,128)S(1)}, u32[]{:S(2)}, u32[]{:S(2)}) collective-permute-start(f32[8,128]{1,0:T(8,128)S(1)} %get-tuple-element.42.refs_0_), channel_id=1, source_target_pairs={{0,8},{8,0},{16,24},{24,16},{1,9},{9,1},{17,25},{25,17},{2,10},{10... | collective-permute-start | bytes 12296 | tf_op jit(solution)/shard_map/ppermute | solution.py:24
  20.1 4.6 %collective-permute-start.11 = (f32[8,128]{1,0:T(8,128)S(1)}, f32[8,128]{1,0:T(8,128)S(1)}, u32[]{:S(2)}, u32[]{:S(2)}) collective-permute-start(f32[8,128]{1,0:T(8,128)S(1)} %get-tuple-element.44.refs_0_), channel_id=1, source_target_pairs={{0,16},{8,24},{16,0},{24,8},{1,17},{9,25},{17,1},{25,9},{2,18},{10... | collective-permute-start | bytes 12296 | tf_op jit(solution)/shard_map/ppermute | solution.py:24
  24.8 4.0 %collective-permute-start.12 = (f32[40,128]{1,0:T(8,128)S(1)}, f32[40,128]{1,0:T(8,128)S(1)}, u32[]{:S(2)}, u32[]{:S(2)}) collective-permute-start(f32[40,128]{1,0:T(8,128)S(1)} %get-tuple-element.55.refs_0_), channel_id=1, source_target_pairs={{0,8},{8,0},{16,24},{24,16},{1,9},{9,1},{17,25},{25,17},{2,10},{10... | collective-permute-start | bytes 61448 | tf_op jit(solution)/shard_map/ppermute | solution.py:24
  28.8 4.7 %collective-permute-start.13 = (f32[40,128]{1,0:T(8,128)S(1)}, f32[40,128]{1,0:T(8,128)S(1)}, u32[]{:S(2)}, u32[]{:S(2)}) collective-permute-start(f32[40,128]{1,0:T(8,128)S(1)} %get-tuple-element.59.refs_0_), channel_id=1, source_target_pairs={{0,16},{8,24},{16,0},{24,8},{1,17},{9,25},{17,1},{25,9},{2,18},{10... | collective-permute-start | bytes 61448 | tf_op jit(solution)/shard_map/ppermute | solution.py:24
  33.8 5.9 %collective-permute-start.19 = (bf16[16,4096]{1,0:T(8,128)(2,1)S(1)}, bf16[16,4096]{1,0:T(8,128)(2,1)S(1)}, u32[]{:S(2)}, u32[]{:S(2)}) collective-permute-start(bf16[16,4096]{1,0:T(8,128)(2,1)S(1)} %weights.1.refs_0_), channel_id=1, source_target_pairs={{0,6},{1,7},{2,4},{3,5},{4,2},{5,3},{6,0},{7,1},{8,14},{9,15},{10,... | collective-permute-start | bytes 393224 | tf_op jit(solution)/shard_map/ppermute | solution.py:24
  36.5 5.0 %collective-permute-start.17 = (bf16[16,4096]{1,0:T(8,128)(2,1)S(1)}, bf16[16,4096]{1,0:T(8,128)(2,1)S(1)}, u32[]{:S(2)}, u32[]{:S(2)}) collective-permute-start(bf16[16,4096]{1,0:T(8,128)(2,1)S(1)} %weights.1.refs_0_), channel_id=1, source_target_pairs={{0,4},{1,5},{2,6},{3,7},{4,0},{5,1},{6,2},{7,3},{8,12},{9,13},{10,... | collective-permute-start | bytes 393224 | tf_op jit(solution)/shard_map/ppermute | solution.py:24
  37.0 5.0 %collective-permute-start.15 = (bf16[16,4096]{1,0:T(8,128)(2,1)S(1)}, bf16[16,4096]{1,0:T(8,128)(2,1)S(1)}, u32[]{:S(2)}, u32[]{:S(2)}) collective-permute-start(bf16[16,4096]{1,0:T(8,128)(2,1)S(1)} %weights.1.refs_0_), channel_id=1, source_target_pairs={{0,2},{1,3},{2,0},{3,1},{4,6},{5,7},{6,4},{7,5},{8,10},{9,11},{10,... | collective-permute-start | bytes 393224 | tf_op jit(solution)/shard_map/ppermute | solution.py:24
  37.3 4.7 %collective-permute-start.14 = (bf16[16,4096]{1,0:T(8,128)(2,1)S(1)}, bf16[16,4096]{1,0:T(8,128)(2,1)S(1)}, u32[]{:S(2)}, u32[]{:S(2)}) collective-permute-start(bf16[16,4096]{1,0:T(8,128)(2,1)S(1)} %weights.1.refs_0_), channel_id=1, source_target_pairs={{0,1},{1,0},{2,3},{3,2},{4,5},{5,4},{6,7},{7,6},{8,9},{9,8},{10,11... | collective-permute-start | bytes 393224 | tf_op jit(solution)/shard_map/ppermute | solution.py:24
  39.7 2.3 %collective-permute-start.20 = (bf16[16,4096]{1,0:T(8,128)(2,1)S(1)}, bf16[16,4096]{1,0:T(8,128)(2,1)S(1)}, u32[]{:S(2)}, u32[]{:S(2)}) collective-permute-start(bf16[16,4096]{1,0:T(8,128)(2,1)S(1)} %collective-permute-done.19.refs_6_), channel_id=1, source_target_pairs={{0,1},{1,0},{2,3},{3,2},{4,5},{5,4},{6,7},{7,6},{8,9},{9,8},{10,11... | collective-permute-start | bytes 393224 | tf_op jit(solution)/shard_map/ppermute | solution.py:24
  41.5 1.3 %collective-permute-start.18 = (bf16[16,4096]{1,0:T(8,128)(2,1)S(1)}, bf16[16,4096]{1,0:T(8,128)(2,1)S(1)}, u32[]{:S(2)}, u32[]{:S(2)}) collective-permute-start(bf16[16,4096]{1,0:T(8,128)(2,1)S(1)} %collective-permute-done.17.refs_4_), channel_id=1, source_target_pairs={{0,1},{1,0},{2,3},{3,2},{4,5},{5,4},{6,7},{7,6},{8,9},{9,8},{10,11... | collective-permute-start | bytes 393224 | tf_op jit(solution)/shard_map/ppermute | solution.py:24
  44.0 4.4 %collective-permute-start.21 = (s16[272,128]{1,0:T(8,128)(2,1)S(1)}, s16[272,128]{1,0:T(8,128)(2,1)S(1)}, u32[]{:S(2)}, u32[]{:S(2)}) collective-permute-start(s16[272,128]{1,0:T(8,128)(2,1)S(1)} %gradients.2.mine), channel_id=1, source_target_pairs={{0,8},{8,0},{16,24},{24,16},{1,9},{9,1},{17,25},{25,17},{2,10},{10... | collective-permute-start | bytes 208904 | tf_op jit(solution)/shard_map/ppermute | solution.py:24
  46.1 4.8 %collective-permute-start.22 = (s16[272,128]{1,0:T(8,128)(2,1)S(1)}, s16[272,128]{1,0:T(8,128)(2,1)S(1)}, u32[]{:S(2)}, u32[]{:S(2)}) collective-permute-start(s16[272,128]{1,0:T(8,128)(2,1)S(1)} %gradients.3.mine), channel_id=1, source_target_pairs={{0,8},{8,0},{16,24},{24,16},{1,9},{9,1},{17,25},{25,17},{2,10},{10... | collective-permute-start | bytes 208904 | tf_op jit(solution)/shard_map/ppermute | solution.py:24
  48.4 7.6 %collective-permute-start.23 = (s16[272,128]{1,0:T(8,128)(2,1)S(1)}, s16[272,128]{1,0:T(8,128)(2,1)S(1)}, u32[]{:S(2)}, u32[]{:S(2)}) collective-permute-start(s16[272,128]{1,0:T(8,128)(2,1)S(1)} %merge.2.refs_0_), channel_id=1, source_target_pairs={{0,16},{8,24},{16,0},{24,8},{1,17},{9,25},{17,1},{25,9},{2,18},{10... | collective-permute-start | bytes 208904 | tf_op jit(solution)/shard_map/ppermute | solution.py:24
  51.0 5.9 %collective-permute-start.24 = (s16[272,128]{1,0:T(8,128)(2,1)S(1)}, s16[272,128]{1,0:T(8,128)(2,1)S(1)}, u32[]{:S(2)}, u32[]{:S(2)}) collective-permute-start(s16[272,128]{1,0:T(8,128)(2,1)S(1)} %merge.3.refs_1_), channel_id=1, source_target_pairs={{0,16},{8,24},{16,0},{24,8},{1,17},{9,25},{17,1},{25,9},{2,18},{10... | collective-permute-start | bytes 208904 | tf_op jit(solution)/shard_map/ppermute | solution.py:24
  (4 other events, 51.0 us)

commit v14 on v12

--- a/solution.py
+++ b/solution.py
@@ -11,9 +11,7 @@
 BF16 = jnp.bfloat16
 LO = 256
 NT = (((1,), (1,)), ((), ()))
-BLOCK = 64
 SPAN = 512
-AHEAD = 3
 VMEM = pl.BlockSpec(memory_space=pltpu.VMEM)
 HBM = pl.BlockSpec(memory_space=pltpu.HBM)
 PARAMS = dict(vmem_limit_bytes=24 * 1024 * 1024)
@@ -86,7 +84,7 @@
         )
         for i in range(steps)
     ]
-    for copy in small + large[:AHEAD]:
+    for copy in small + large:
         copy.start()
     for copy in small:
         copy.wait()
@@ -96,8 +94,6 @@
     lhs[width:] = jnp.broadcast_to(own_coefficients[...].astype(F32)[None, :], (16, variants)).astype(BF16)
     for i in range(steps):
         large[i].wait()
-        if i + AHEAD < steps:
-            large[i + AHEAD].start()
         first = i * chunk
         result = lax.dot_general(
             lhs[...], table[first : first + chunk], NT, preferred_element_type=F32
@@ -154,19 +150,19 @@
     return values.astype(jnp.int32).astype(F32)
 
 
-def pair_kernel(linear, received, out):
+def pair_kernel(linear, received, waited, out):
     out[...] = linear[...] + received[:, received.shape[1] - LO :]
 
 
-def pair(linear, received):
+def pair(linear, received, waited):
     return pl.pallas_call(
         pair_kernel,
-        in_specs=[VMEM] * 2,
+        in_specs=[VMEM] * 2 + [pl.BlockSpec(memory_space=pl.ANY)],
         out_shape=jax.ShapeDtypeStruct(linear.shape, F32),
         out_specs=VMEM,
         compiler_params=pltpu.CompilerParams(**PARAMS),
         name="pair",
-    )(linear, received)
+    )(linear, received, waited)
 
 
 def join_kernel(start, width, mine, other, *refs):
@@ -507,47 +503,48 @@
 
 
 def encode(values, message):
-    height = values.shape[0]
-    block = min(BLOCK, height)
+    columns = len(values)
     powers = []
-    for start in range(0, height, block):
-        part = values[start : start + block]
-        largest = jnp.max(jnp.abs(part), axis=0, keepdims=True)
-        power = power_of(largest)
-        message[start : start + block] = to_short(part * jnp.exp2(-power))
+    for i, value in enumerate(values):
+        power = power_of(jnp.max(jnp.abs(value), axis=0, keepdims=True))
+        scaled = to_short(value * jnp.exp2(-power))
+        for j in range(value.shape[0] // 16):
+            message[j * columns + i] = scaled[j * 16 : (j + 1) * 16]
         powers.append(power)
-    powers.append(jnp.zeros((message.shape[0] - height - len(powers), values.shape[1]), F32))
-    message[height:] = to_short(jnp.concatenate(powers, axis=0))
-
-
-def decode(message, height):
-    block = min(BLOCK, height)
-    powers = from_short(message[height:])
-    parts = []
-    for i in range(height // block):
-        part = from_short(message[i * block : (i + 1) * block])
-        parts.append(part * jnp.exp2(powers[i : i + 1]))
-    return jnp.concatenate(parts, axis=0)
-
-
-def gradient_kernel(feat, kf, start, *refs):
-    parts, dosages, out, weighted = refs[:feat], refs[feat], refs[feat + 1], refs[feat + 2]
-    width = out.shape[0] - 16
-    me = lax.axis_index("feat")
-    for i in range(feat):
-        weighted[pl.ds(pl.multiple_of((me ^ i) * kf, kf), kf), :] = parts[i][...]
-    total = jnp.dot(weighted[...], dosages[:, start : start + width], preferred_element_type=F32)
-    encode(total.T, out)
-
-
-def gradients(parts, dosages, start, variants):
-    feat = len(parts)
-    kf, persons = parts[0].shape
-    k = kf * feat
-    return pl.pallas_call(
-        functools.partial(gradient_kernel, feat, kf, start),
-        in_specs=[VMEM] * (feat + 1),
-        out_shape=jax.ShapeDtypeStruct((variants + 16, k), jnp.int16),
+    powers.append(jnp.zeros((16 - columns, 128), F32))
+    message[message.shape[0] - 1] = to_short(jnp.concatenate(powers, axis=0))
+
+
+def decode(message, columns):
+    last = message.shape[0] - 1
+    scales = jnp.exp2(from_short(message[last]))
+    values = []
+    for i in range(columns):
+        value = jnp.concatenate([from_short(message[j]) for j in range(i, last, columns)], axis=0)
+        values.append(value * scales[i : i + 1])
+    return values
+
+
+def decode_sum(mine, other, columns):
+    return [one + two for one, two in zip(decode(mine, columns), decode(other, columns))]
+
+
+def gradient_kernel(parts, kf, *refs):
+    pieces, dosages, out, weighted = refs[:parts], refs[parts], refs[parts + 1], refs[parts + 2]
+    for i in range(parts):
+        weighted[i * kf : (i + 1) * kf, :] = pieces[i][...]
+    total = jnp.dot(weighted[...], dosages[...], preferred_element_type=F32)
+    encode([total[:, at : at + 128] for at in range(0, total.shape[1], 128)], out)
+
+
+def gradients(pieces, dosages):
+    parts = len(pieces)
+    kf, persons = pieces[0].shape
+    k, variants = kf * parts, dosages.shape[1]
+    return pl.pallas_call(
+        functools.partial(gradient_kernel, parts, kf),
+        in_specs=[VMEM] * (parts + 1),
+        out_shape=jax.ShapeDtypeStruct((k * variants // 2048 + 1, 16, 128), jnp.int16),
         out_specs=VMEM,
         scratch_shapes=[pltpu.VMEM((k, persons), BF16)],
         compiler_params=pltpu.CompilerParams(**PARAMS),
@@ -555,17 +552,16 @@
             flops=2 * persons * variants * k, bytes_accessed=persons * (variants * 2 + k * 2), transcendentals=0
         ),
         name="gradients",
-    )(*parts, dosages)
-
-
-def merge_kernel(mine, other, out):
-    height = mine.shape[0] - 16
-    encode(decode(mine, height) + decode(other, height), out)
-
-
-def merge(mine, other):
-    return pl.pallas_call(
-        merge_kernel,
+    )(*pieces, dosages)
+
+
+def merge_kernel(columns, mine, other, out):
+    encode(decode_sum(mine, other, columns), out)
+
+
+def merge(mine, other, variants):
+    return pl.pallas_call(
+        functools.partial(merge_kernel, variants // 128),
         in_specs=[VMEM] * 2,
         out_shape=jax.ShapeDtypeStruct(mine.shape, jnp.int16),
         out_specs=VMEM,
@@ -574,23 +570,38 @@
     )(mine, other)
 
 
-def finish_kernel(parts, *refs):
-    mine, other, count = refs[:parts], refs[parts : 2 * parts], refs[2 * parts]
-    out, total, sems = refs[2 * parts + 1 :]
-    step = mine[0].shape[0] - 16
-    block = min(BLOCK, step)
+def add_kernel(mine, other, out):
+    for i, value in enumerate(decode_sum(mine, other, out.shape[1] // 128)):
+        out[:, i * 128 : (i + 1) * 128] = value
+
+
+def add(mine, other, variants):
+    return pl.pallas_call(
+        add_kernel,
+        in_specs=[VMEM] * 2,
+        out_shape=jax.ShapeDtypeStruct(((mine.shape[0] - 1) * 2048 // variants, variants), F32),
+        out_specs=VMEM,
+        compiler_params=pltpu.CompilerParams(**PARAMS),
+        name="add",
+    )(mine, other)
+
+
+def finish_kernel(feat, kf, first, mine, other, count, out, placed, total, sems):
+    me = lax.axis_index("feat")
+    variants = out.shape[0]
     scale = count[1:2, 0:1]
+    for q in range(feat // 2):
+        placed[me ^ (2 * q)] = first[q * kf : (q + 1) * kf]
+    for i, value in enumerate(decode_sum(mine, other, variants // 128)):
+        for q in range(feat // 2):
+            placed[me ^ (2 * q + 1), :, i * 128 : (i + 1) * 128] = value[q * kf : (q + 1) * kf]
     copies = []
-    for i in range(parts):
-        messages = (mine[i], other[i])
-        powers = [jnp.exp2(from_short(message[step:])) for message in messages]
-        for j in range(step // block):
-            at = slice(j * block, (j + 1) * block)
-            terms = [from_short(m[at]) * p[j : j + 1] for m, p in zip(messages, powers)]
-            total[i * step + j * block : i * step + (j + 1) * block] = (terms[0] + terms[1]) / scale
+    for i in range(variants // 128):
+        at = slice(i * 128, (i + 1) * 128)
+        total[at] = placed[:, :, at].reshape(feat * kf, 128).T / scale
         copies.append(
             pltpu.make_async_copy(
-                total.at[pl.ds(i * step, step)], out.at[pl.ds(i * step, step)], sems.at[i]
+                total.at[pl.ds(i * 128, 128)], out.at[pl.ds(i * 128, 128)], sems.at[i]
             )
         )
         copies[i].start()
@@ -598,18 +609,22 @@
         copy.wait()
 
 
-def finish(mine, other, count):
-    parts = len(mine)
-    height, k = parts * (mine[0].shape[0] - 16), mine[0].shape[1]
-    return pl.pallas_call(
-        functools.partial(finish_kernel, parts),
-        in_specs=[VMEM] * (2 * parts + 1),
-        out_shape=jax.ShapeDtypeStruct((height, k), F32),
+def finish(first, mine, other, count, feat):
+    k, variants = 2 * first.shape[0], first.shape[1]
+    kf = k // feat
+    return pl.pallas_call(
+        functools.partial(finish_kernel, feat, kf),
+        in_specs=[VMEM] * 4,
+        out_shape=jax.ShapeDtypeStruct((variants, k), F32),
         out_specs=HBM,
-        scratch_shapes=[pltpu.VMEM((height, k), F32), pltpu.SemaphoreType.DMA((parts,))],
+        scratch_shapes=[
+            pltpu.VMEM((feat, kf, variants), F32),
+            pltpu.VMEM((variants, k), F32),
+            pltpu.SemaphoreType.DMA((variants // 128,)),
+        ],
         compiler_params=pltpu.CompilerParams(**PARAMS),
         name="finish",
-    )(*mine, *other, count)
+    )(first, mine, other, count)
 
 
 def local(dosages, coefficients, directions, event_rank, events):
@@ -626,7 +641,8 @@
     linear, keep, send = products(dosages, coefficients, directions, feat)
     order = list(reversed(range(1, feat // 2)))
     received = {q: swap(send[q], "feat", 1) for q in order + [0]}
-    paired = pair(linear, received[order[0]])
+    table = tables(rank, linear, rows)
+    paired = pair(linear, received[order[0]], table)
     middle = min(3 * SPAN, rows // 2)
     firsts = [
         swap(join(keep[q], received[q], 0, middle, paired, []), "feat", 2 * q) for q in order
@@ -635,7 +651,6 @@
         swap(join(keep[q], received[q], middle, rows - middle, paired, [received[0]]), "feat", 2 * q)
         for q in order
     ]
-    table = tables(rank, paired, rows)
 
     risk, sums, ordered_events, total = risks(paired, firsts, rank, event_row, table, rows)
     later = jnp.zeros_like(total)
@@ -657,19 +672,17 @@
     chips = {0: own}
     for q in reversed(range(1, feat // 2)):
         chips[q] = swap(own, "feat", 2 * q)
-    parts = []
-    for q in range(feat // 2):
-        parts += [chips[q], swap(chips[q], "feat", 1)]
-
-    half = variants // 2
-    partial_sums = [gradients(parts, dosages, start, half) for start in (0, half)]
+    near = [chips[q] for q in range(feat // 2)]
+    far = [swap(chips[q], "feat", 1) for q in range(feat // 2)]
+    partial_sums = [gradients(pieces, dosages) for pieces in (near, far)]
     bit = 1
     while 2 * bit < ex:
         received = [swap(message, "ex", bit) for message in partial_sums]
-        partial_sums = [merge(mine, other) for mine, other in zip(partial_sums, received)]
+        partial_sums = [merge(mine, other, variants) for mine, other in zip(partial_sums, received)]
         bit *= 2
     received = [swap(message, "ex", bit) for message in partial_sums]
-    result = finish(partial_sums, received, total)
+    first = add(partial_sums[0], received[0], variants)
+    result = finish(first, partial_sums[1], received[1], total, feat)
     if padded != each:
         result = result.reshape(variants, feat, padded)[:, :, :each].reshape(variants, k)
     return result

time: 57.9 us -> 56.3 us (0.972)
  waiting for transfers between devices: 15.8 us -> 13.7 us
    ppermute x26, waiting for transfers between devices: 15.8 us -> 13.7 us  [swap(): return lax.ppermute(x, axis, [(s, s ^ i) for s in range(count)])]
    pallas_call x6 -> x7, Pallas kernels: 2.21 us -> 2.83 us  [the longest x2 1.76 us: gradients(): pl.pallas_call(functools.partial(gradient_kernel, parts, kf), in_specs=[V...]
  transfers between devices with their start and end apart: 26 -> 26, of which waited for: 13 -> 10; matrix products, arithmetic and copies ran while one was open for 0% -> 0% of each run, Pallas kernels for 14% -> 16%
where the time goes in v14:
time: 56.3 us; the launch traced here: 56.2 us
  starting transfers between devices  28.1 us (50%)
  Pallas kernels  14.1 us (25%)
  waiting for transfers between devices  13.7 us (24%)
    ppermute x26, starting transfers between devices, swap(): return lax.ppermute(x, axis, [(s, s ^ i) for s in range(count)])  28.1 us
    ppermute x26, waiting for transfers between devices, swap(): return lax.ppermute(x, axis, [(s, s ^ i) for s in range(count)])  13.7 us
    pallas_call x1, Pallas kernels, products(): pl.pallas_call(functools.partial(product_kernel, feat, kf, chunk), in_spe...  3.75 us
    pallas_call x2, Pallas kernels, ordered_values(): pl.pallas_call(functools.partial(order_kernel, start, len(messages)), in_...  1.97 us
    pallas_call x2, Pallas kernels, gradients(): pl.pallas_call(functools.partial(gradient_kernel, parts, kf), in_specs=[V...  1.76 us
    pallas_call x1, Pallas kernels, prefix_sums(): pl.pallas_call(prefix_kernel, in_specs=[VMEM] * 3, out_shape=jax.ShapeDty...  1.75 us
  transfers between devices with their start and end apart: 26, of which 10 were waited for; matrix products, arithmetic and copies ran while one was open for 0% of the time, Pallas kernels for 16%

profile of v14, /device:TPU:0, one launch (start us, length us, event | category | flops | bytes accessed | tf_op | source)
XLA Modules:
  0.0 56.2 jit_solution(3779682270564838141)
XLA Ops:
  0.0 3.8 %products.1 = (f32[16,256]{1,0:T(8,128)S(1)}, f32[16,4096]{1,0:T(8,128)S(1)}, f32[16,4096]{1,0:T(8,128)S(1)}, f32[16,4096]{1,0:T(8,128)S(1)}, f32[16,4096]{1,0:T...) custom-call(bf16[512,128]{1,0:T(8,128)(2,1)} %directions.1, ...), custom_call_target="tpu_custom_call" | custom-call | flops 536870912 | bytes 6291456 | tf_op jit(solution)/shard_map/products/pallas_call | solution.py:117
  5.7 3.9 %collective-permute-start.1 = (s16[16,2176]{1,0:T(8,128)(2,1)S(1)}, s16[16,2176]{1,0:T(8,128)(2,1)S(1)}, u32[]{:S(2)}, u32[]{:S(2)}) collective-permute-start(s16[16,2176]{1,0:T(8,128)(2,1)S(1)} %join.6), channel_id=1, source_target_pairs={{0,6},{1,7},{2,4},{3,5},{4,2},{5,3},{6,0},{7,1},{8,14},{9,15},{10,... | collective-permute-start | bytes 208904 | tf_op jit(solution)/shard_map/ppermute | solution.py:22
  10.7 2.9 %collective-permute-start.8 = (s16[16,2688]{1,0:T(8,128)(2,1)S(1)}, s16[16,2688]{1,0:T(8,128)(2,1)S(1)}, u32[]{:S(2)}, u32[]{:S(2)}) collective-permute-start(s16[16,2688]{1,0:T(8,128)(2,1)S(1)} %join.9), channel_id=1, source_target_pairs={{0,6},{1,7},{2,4},{3,5},{4,2},{5,3},{6,0},{7,1},{8,14},{9,15},{10,... | collective-permute-start | bytes 258056 | tf_op jit(solution)/shard_map/ppermute | solution.py:22
  15.5 0.9 %risks.1 = (f32[1,4096]{1,0:T(1,128)S(1)}, f32[16,256]{1,0:T(8,128)S(1)}, f32[16,256]{1,0:T(8,128)S(1)}, f32[8,128]{1,0:T(8,128)S(1)}) custom-call(f32[16,256]{1,0:T(8,128)S(1)} %pair.1.refs_0_.linear, s16[16,2176]{1,0:T(8,128)(2,1)S(1)} %collective-permute-done.1.refs_0_, s16[16,2176]{1,0:T(8,128)(2,1)S(1)} %collective-permute-done.3.refs_1_, ...), custom_call_target="tpu_custom_call" | custom-call | flops 134217728 | bytes 262144 | tf_op jit(solution)/shard_map/risks/pallas_call | solution.py:257
  16.4 1.7 %collective-permute-start.6 = (f32[8,128]{1,0:T(8,128)S(1)}, f32[8,128]{1,0:T(8,128)S(1)}, u32[]{:S(2)}, u32[]{:S(2)}) collective-permute-start(f32[8,128]{1,0:T(8,128)S(1)} %get-tuple-element.40.refs_0_), channel_id=1, source_target_pairs={{0,8},{8,0},{16,24},{24,16},{1,9},{9,1},{17,25},{25,17},{2,10},{10... | collective-permute-start | bytes 12296 | tf_op jit(solution)/shard_map/ppermute | solution.py:22
  18.9 1.2 %collective-permute-done.6.refs_1_ = f32[8,128]{1,0:T(8,128)S(1)} collective-permute-done((f32[8,128]{1,0:T(8,128)S(1)}, f32[8,128]{1,0:T(8,128)S(1)}, u32[]{:S(2)}, u32[]{:S(2)}) %collective-permute-start.6) | collective-permute-done | bytes 4128 | tf_op jit(solution)/shard_map/ppermute | solution.py:22
  20.2 2.7 %collective-permute-start.11 = (f32[8,128]{1,0:T(8,128)S(1)}, f32[8,128]{1,0:T(8,128)S(1)}, u32[]{:S(2)}, u32[]{:S(2)}) collective-permute-start(f32[8,128]{1,0:T(8,128)S(1)} %get-tuple-element.42.refs_0_), channel_id=1, source_target_pairs={{0,16},{8,24},{16,0},{24,8},{1,17},{9,25},{17,1},{25,9},{2,18},{10... | collective-permute-start | bytes 12296 | tf_op jit(solution)/shard_map/ppermute | solution.py:22
  22.8 1.2 %ordered_values.3 = (f32[16,2560]{1,0:T(8,128)S(1)}, f32[256,256]{1,0:T(8,128)S(1)}, f32[16,128]{1,0:T(8,128)S(1)}) custom-call(f32[16,4096]{1,0:T(8,128)S(1)} %get-tuple-element.47.own, f32[16,4096]{1,0:T(8,128)S(1)} %collective-permute-done.7.refs_1_.other, s16[16,2688]{1,0:T(8,128)(2,1)S(1)} %collective-permute-done.8.refs_3_.refs_0_, ...), custom_call_target="tpu_custom_call" | custom-call | flops 671088640 | bytes 983040 | tf_op jit(solution)/shard_map/ordered_values/pallas_call | solution.py:386
  24.9 3.6 %collective-permute-start.14 = (f32[40,128]{1,0:T(8,128)S(1)}, f32[40,128]{1,0:T(8,128)S(1)}, u32[]{:S(2)}, u32[]{:S(2)}) collective-permute-start(f32[40,128]{1,0:T(8,128)S(1)} %get-tuple-element.53.refs_0_), channel_id=1, source_target_pairs={{0,24},{8,16},{16,8},{24,0},{1,25},{9,17},{17,9},{25,1},{2,26},{10... | collective-permute-start | bytes 61448 | tf_op jit(solution)/shard_map/ppermute | solution.py:22
  29.3 1.7 %prefix_sums.1.refs_6_ = f32[16,4096]{1,0:T(8,128)S(1)} custom-call(f32[256,256]{1,0:T(8,128)S(1)} %suffix_sums.1.ordered.sums, f32[16,256]{1,0:T(8,128)S(1)} %get-tuple-element.56.squares.square, s32[1,4096]{1,0:T(1,128)S(1)} %bitcast.6), custom_call_target="tpu_custom_call" | custom-call | flops 1073741824 | bytes 1572864 | tf_op jit(solution)/shard_map/prefix_sums/pallas_call | solution.py:452
  31.0 0.9 %hazards.1 = (f32[1,4096]{1,0:T(1,128)S(1)}, f32[1,4096]{1,0:T(1,128)S(1)}) custom-call(f32[16,256]{1,0:T(8,128)S(1)} %get-tuple-element.57.hazard, f32[16,256]{1,0:T(8,128)S(1)} %get-tuple-element.56.squares.square, s32[1,4096]{1,0:T(1,128)S(1)} %bitcast.7), custom_call_target="tpu_custom_call" | custom-call | flops 209715200 | bytes 262144 | tf_op jit(solution)/shard_map/hazards/pallas_call | solution.py:320
  31.9 1.2 %collective-permute-done.13.refs_2_ = f32[40,128]{1,0:T(8,128)S(1)} collective-permute-done((f32[40,128]{1,0:T(8,128)S(1)}, f32[40,128]{1,0:T(8,128)S(1)}, u32[]{:S(2)}, u32[]{:S(2)}) %collective-permute-start.13) | collective-permute-done | bytes 20512 | tf_op jit(solution)/shard_map/ppermute | solution.py:22
  33.4 2.1 %collective-permute-start.17 = (bf16[16,4096]{1,0:T(8,128)(2,1)S(1)}, bf16[16,4096]{1,0:T(8,128)(2,1)S(1)}, u32[]{:S(2)}, u32[]{:S(2)}) collective-permute-start(bf16[16,4096]{1,0:T(8,128)(2,1)S(1)} %weights.1.refs_0_), channel_id=1, source_target_pairs={{0,6},{1,7},{2,4},{3,5},{4,2},{5,3},{6,0},{7,1},{8,14},{9,15},{10,... | collective-permute-start | bytes 393224 | tf_op jit(solution)/shard_map/ppermute | solution.py:22
  36.0 1.0 %collective-permute-start.15 = (bf16[16,4096]{1,0:T(8,128)(2,1)S(1)}, bf16[16,4096]{1,0:T(8,128)(2,1)S(1)}, u32[]{:S(2)}, u32[]{:S(2)}) collective-permute-start(bf16[16,4096]{1,0:T(8,128)(2,1)S(1)} %weights.1.refs_0_), channel_id=1, source_target_pairs={{0,2},{1,3},{2,0},{3,1},{4,6},{5,7},{6,4},{7,5},{8,10},{9,11},{10,... | collective-permute-start | bytes 393224 | tf_op jit(solution)/shard_map/ppermute | solution.py:22
  36.9 2.4 %collective-permute-done.17.refs_3_ = bf16[16,4096]{1,0:T(8,128)(2,1)S(1)} collective-permute-done((bf16[16,4096]{1,0:T(8,128)(2,1)S(1)}, bf16[16,4096]{1,0:T(8,128)(2,1)S(1)}, u32[]{:S(2)}, u32[]{:S(2)}) %collective-permute-start.17) | collective-permute-done | bytes 131104 | tf_op jit(solution)/shard_map/ppermute | solution.py:22
  39.3 1.4 %collective-permute-done.16.refs_2_ = bf16[16,4096]{1,0:T(8,128)(2,1)S(1)} collective-permute-done((bf16[16,4096]{1,0:T(8,128)(2,1)S(1)}, bf16[16,4096]{1,0:T(8,128)(2,1)S(1)}, u32[]{:S(2)}, u32[]{:S(2)}) %collective-permute-start.16) | collective-permute-done | bytes 131104 | tf_op jit(solution)/shard_map/ppermute | solution.py:22
  41.2 0.9 %gradients.2.mine = s16[17,16,128]{2,1,0:T(8,128)(2,1)S(1)} custom-call(bf16[16,4096]{1,0:T(8,128)(2,1)S(1)} %weights.1.refs_0_, bf16[16,4096]{1,0:T(8,128)(2,1)S(1)} %collective-permute-done.15.refs_1_, bf16[16,4096]{1,0:T(8,128)(2,1)S(1)} %collective-permute-done.16.refs_2_, bf16[16,4096]{1,0:T(8,128)(2,1)S(1)} %collective-permute-done.17.refs_3_, ...), custom_call_target="tpu_custom_call" | custom-call | flops 268435456 | bytes 4718592 | tf_op jit(solution)/shard_map/gradients/pallas_call | solution.py:544
  42.3 0.9 %gradients.3.mine = s16[17,16,128]{2,1,0:T(8,128)(2,1)S(1)} custom-call(bf16[16,4096]{1,0:T(8,128)(2,1)S(1)} %collective-permute-done.20.refs_0_, bf16[16,4096]{1,0:T(8,128)(2,1)S(1)} %collective-permute-done.21.refs_1_, bf16[16,4096]{1,0:T(8,128)(2,1)S(1)} %collective-permute-done.22.refs_2_, bf16[16,4096]{1,0:T(8,128)(2,1)S(1)} %collective-permute-done.23.refs_3_, ...), custom_call_target="tpu_custom_call" | custom-call | flops 268435456 | bytes 4718592 | tf_op jit(solution)/shard_map/gradients/pallas_call | solution.py:544
  43.2 2.0 %collective-permute-start.24 = (s16[17,16,128]{2,1,0:T(8,128)(2,1)S(1)}, s16[17,16,128]{2,1,0:T(8,128)(2,1)S(1)}, u32[]{:S(2)}, u32[]{:S(2)}) collective-permute-start(s16[17,16,128]{2,1,0:T(8,128)(2,1)S(1)} %gradients.3.mine), channel_id=1, source_target_pairs={{0,8},{8,0},{16,24},{24,16},{1,9},{9,1},{17,25},{25,17},{2,10},{10... | collective-permute-start | bytes 208904 | tf_op jit(solution)/shard_map/ppermute | solution.py:22
  45.2 1.8 %collective-permute-done.18.other = s16[17,16,128]{2,1,0:T(8,128)(2,1)S(1)} collective-permute-done((s16[17,16,128]{2,1,0:T(8,128)(2,1)S(1)}, s16[17,16,128]{2,1,0:T(8,128)(2,1)S(1)}, u32[]{:S(2)}, u32[]{:S(2)}) %collective-permute-start.18) | collective-permute-done | bytes 69664 | tf_op jit(solution)/shard_map/ppermute | solution.py:22
  47.1 1.6 %collective-permute-start.19 = (s16[17,16,128]{2,1,0:T(8,128)(2,1)S(1)}, s16[17,16,128]{2,1,0:T(8,128)(2,1)S(1)}, u32[]{:S(2)}, u32[]{:S(2)}) collective-permute-start(s16[17,16,128]{2,1,0:T(8,128)(2,1)S(1)} %merge.2.mine), channel_id=1, source_target_pairs={{0,16},{8,24},{16,0},{24,8},{1,17},{9,25},{17,1},{25,9},{2,18},{10... | collective-permute-start | bytes 208904 | tf_op jit(solution)/shard_map/ppermute | solution.py:22
  48.7 2.3 %collective-permute-start.25 = (s16[17,16,128]{2,1,0:T(8,128)(2,1)S(1)}, s16[17,16,128]{2,1,0:T(8,128)(2,1)S(1)}, u32[]{:S(2)}, u32[]{:S(2)}) collective-permute-start(s16[17,16,128]{2,1,0:T(8,128)(2,1)S(1)} %merge.3.mine), channel_id=1, source_target_pairs={{0,16},{8,24},{16,0},{24,8},{1,17},{9,25},{17,1},{25,9},{2,18},{10... | collective-permute-start | bytes 208904 | tf_op jit(solution)/shard_map/ppermute | solution.py:22
  51.0 3.5 %collective-permute-done.19.other = s16[17,16,128]{2,1,0:T(8,128)(2,1)S(1)} collective-permute-done((s16[17,16,128]{2,1,0:T(8,128)(2,1)S(1)}, s16[17,16,128]{2,1,0:T(8,128)(2,1)S(1)}, u32[]{:S(2)}, u32[]{:S(2)}) %collective-permute-start.19) | collective-permute-done | bytes 69664 | tf_op jit(solution)/shard_map/ppermute | solution.py:22
  55.3 0.9 %finish.1 = f32[512,128]{1,0:T(8,128)} custom-call(f32[64,512]{1,0:T(8,128)S(1)} %add.1.first, s16[17,16,128]{2,1,0:T(8,128)(2,1)S(1)} %merge.3.mine, s16[17,16,128]{2,1,0:T(8,128)(2,1)S(1)} %collective-permute-done.25.other, f32[8,128]{1,0:T(8,128)S(1)} %get-tuple-element.60.count), custom_call_target="tpu_custom_call" | custom-call | tf_op jit(solution)/shard_map/finish/pallas_call | solution.py:615
  (60 shorter events, 9.5 us)
Async XLA Ops:
  3.8 1.8 %collective-permute-start = (f32[16,4352]{1,0:T(8,128)S(1)}, f32[16,4352]{1,0:T(8,128)S(1)}, u32[]{:S(2)}, u32[]{:S(2)}) collective-permute-start(f32[16,4352]{1,0:T(8,128)S(1)} %get-tuple-element.34), channel_id=1, source_target_pairs={{0,1},{1,0},{2,3},{3,2},{4,5},{5,4},{6,7},{7,6},{8,9},{9,8},{10,11... | collective-permute-start | bytes 835592 | tf_op jit(solution)/shard_map/ppermute | solution.py:22
  4.3 5.3 %collective-permute-start.2 = (f32[16,4096]{1,0:T(8,128)S(1)}, f32[16,4096]{1,0:T(8,128)S(1)}, u32[]{:S(2)}, u32[]{:S(2)}) collective-permute-start(f32[16,4096]{1,0:T(8,128)S(1)} %get-tuple-element.37), channel_id=1, source_target_pairs={{0,1},{1,0},{2,3},{3,2},{4,5},{5,4},{6,7},{7,6},{8,9},{9,8},{10,11... | collective-permute-start | bytes 786440 | tf_op jit(solution)/shard_map/ppermute | solution.py:22
  4.3 5.9 %collective-permute-start.4 = (f32[16,4096]{1,0:T(8,128)S(1)}, f32[16,4096]{1,0:T(8,128)S(1)}, u32[]{:S(2)}, u32[]{:S(2)}) collective-permute-start(f32[16,4096]{1,0:T(8,128)S(1)} %get-tuple-element.39), channel_id=1, source_target_pairs={{0,1},{1,0},{2,3},{3,2},{4,5},{5,4},{6,7},{7,6},{8,9},{9,8},{10,11... | collective-permute-start | bytes 786440 | tf_op jit(solution)/shard_map/ppermute | solution.py:22
  4.8 5.8 %collective-permute-start.7 = (f32[16,4096]{1,0:T(8,128)S(1)}, f32[16,4096]{1,0:T(8,128)S(1)}, u32[]{:S(2)}, u32[]{:S(2)}) collective-permute-start(f32[16,4096]{1,0:T(8,128)S(1)} %get-tuple-element.41), channel_id=1, source_target_pairs={{0,1},{1,0},{2,3},{3,2},{4,5},{5,4},{6,7},{7,6},{8,9},{9,8},{10,11... | collective-permute-start | bytes 786440 | tf_op jit(solution)/shard_map/ppermute | solution.py:22
  5.7 8.8 %collective-permute-start.1 = (s16[16,2176]{1,0:T(8,128)(2,1)S(1)}, s16[16,2176]{1,0:T(8,128)(2,1)S(1)}, u32[]{:S(2)}, u32[]{:S(2)}) collective-permute-start(s16[16,2176]{1,0:T(8,128)(2,1)S(1)} %join.6), channel_id=1, source_target_pairs={{0,6},{1,7},{2,4},{3,5},{4,2},{5,3},{6,0},{7,1},{8,14},{9,15},{10,... | collective-permute-start | bytes 208904 | tf_op jit(solution)/shard_map/ppermute | solution.py:22
  9.7 4.9 %collective-permute-start.3 = (s16[16,2176]{1,0:T(8,128)(2,1)S(1)}, s16[16,2176]{1,0:T(8,128)(2,1)S(1)}, u32[]{:S(2)}, u32[]{:S(2)}) collective-permute-start(s16[16,2176]{1,0:T(8,128)(2,1)S(1)} %join.7), channel_id=1, source_target_pairs={{0,4},{1,5},{2,6},{3,7},{4,0},{5,1},{6,2},{7,3},{8,12},{9,13},{10,... | collective-permute-start | bytes 208904 | tf_op jit(solution)/shard_map/ppermute | solution.py:22
  10.4 5.1 %collective-permute-start.5 = (s16[16,2176]{1,0:T(8,128)(2,1)S(1)}, s16[16,2176]{1,0:T(8,128)(2,1)S(1)}, u32[]{:S(2)}, u32[]{:S(2)}) collective-permute-start(s16[16,2176]{1,0:T(8,128)(2,1)S(1)} %join.8), channel_id=1, source_target_pairs={{0,2},{1,3},{2,0},{3,1},{4,6},{5,7},{6,4},{7,5},{8,10},{9,11},{10,... | collective-permute-start | bytes 208904 | tf_op jit(solution)/shard_map/ppermute | solution.py:22
  10.7 9.4 %collective-permute-start.8 = (s16[16,2688]{1,0:T(8,128)(2,1)S(1)}, s16[16,2688]{1,0:T(8,128)(2,1)S(1)}, u32[]{:S(2)}, u32[]{:S(2)}) collective-permute-start(s16[16,2688]{1,0:T(8,128)(2,1)S(1)} %join.9), channel_id=1, source_target_pairs={{0,6},{1,7},{2,4},{3,5},{4,2},{5,3},{6,0},{7,1},{8,14},{9,15},{10,... | collective-permute-start | bytes 258056 | tf_op jit(solution)/shard_map/ppermute | solution.py:22
  13.8 6.3 %collective-permute-start.9 = (s16[16,2688]{1,0:T(8,128)(2,1)S(1)}, s16[16,2688]{1,0:T(8,128)(2,1)S(1)}, u32[]{:S(2)}, u32[]{:S(2)}) collective-permute-start(s16[16,2688]{1,0:T(8,128)(2,1)S(1)} %join.10), channel_id=1, source_target_pairs={{0,4},{1,5},{2,6},{3,7},{4,0},{5,1},{6,2},{7,3},{8,12},{9,13},{10,... | collective-permute-start | bytes 258056 | tf_op jit(solution)/shard_map/ppermute | solution.py:22
  14.5 5.6 %collective-permute-start.10 = (s16[16,2688]{1,0:T(8,128)(2,1)S(1)}, s16[16,2688]{1,0:T(8,128)(2,1)S(1)}, u32[]{:S(2)}, u32[]{:S(2)}) collective-permute-start(s16[16,2688]{1,0:T(8,128)(2,1)S(1)} %join.11), channel_id=1, source_target_pairs={{0,2},{1,3},{2,0},{3,1},{4,6},{5,7},{6,4},{7,5},{8,10},{9,11},{10,... | collective-permute-start | bytes 258056 | tf_op jit(solution)/shard_map/ppermute | solution.py:22
  16.4 3.7 %collective-permute-start.6 = (f32[8,128]{1,0:T(8,128)S(1)}, f32[8,128]{1,0:T(8,128)S(1)}, u32[]{:S(2)}, u32[]{:S(2)}) collective-permute-start(f32[8,128]{1,0:T(8,128)S(1)} %get-tuple-element.40.refs_0_), channel_id=1, source_target_pairs={{0,8},{8,0},{16,24},{24,16},{1,9},{9,1},{17,25},{25,17},{2,10},{10... | collective-permute-start | bytes 12296 | tf_op jit(solution)/shard_map/ppermute | solution.py:22
  20.2 4.6 %collective-permute-start.11 = (f32[8,128]{1,0:T(8,128)S(1)}, f32[8,128]{1,0:T(8,128)S(1)}, u32[]{:S(2)}, u32[]{:S(2)}) collective-permute-start(f32[8,128]{1,0:T(8,128)S(1)} %get-tuple-element.42.refs_0_), channel_id=1, source_target_pairs={{0,16},{8,24},{16,0},{24,8},{1,17},{9,25},{17,1},{25,9},{2,18},{10... | collective-permute-start | bytes 12296 | tf_op jit(solution)/shard_map/ppermute | solution.py:22
  24.9 7.1 %collective-permute-start.14 = (f32[40,128]{1,0:T(8,128)S(1)}, f32[40,128]{1,0:T(8,128)S(1)}, u32[]{:S(2)}, u32[]{:S(2)}) collective-permute-start(f32[40,128]{1,0:T(8,128)S(1)} %get-tuple-element.53.refs_0_), channel_id=1, source_target_pairs={{0,24},{8,16},{16,8},{24,0},{1,25},{9,17},{17,9},{25,1},{2,26},{10... | collective-permute-start | bytes 61448 | tf_op jit(solution)/shard_map/ppermute | solution.py:22
  28.5 4.7 %collective-permute-start.13 = (f32[40,128]{1,0:T(8,128)S(1)}, f32[40,128]{1,0:T(8,128)S(1)}, u32[]{:S(2)}, u32[]{:S(2)}) collective-permute-start(f32[40,128]{1,0:T(8,128)S(1)} %get-tuple-element.53.refs_0_), channel_id=1, source_target_pairs={{0,16},{8,24},{16,0},{24,8},{1,17},{9,25},{17,1},{25,9},{2,18},{10... | collective-permute-start | bytes 61448 | tf_op jit(solution)/shard_map/ppermute | solution.py:22
  28.5 4.7 %collective-permute-start.12 = (f32[40,128]{1,0:T(8,128)S(1)}, f32[40,128]{1,0:T(8,128)S(1)}, u32[]{:S(2)}, u32[]{:S(2)}) collective-permute-start(f32[40,128]{1,0:T(8,128)S(1)} %get-tuple-element.53.refs_0_), channel_id=1, source_target_pairs={{0,8},{8,0},{16,24},{24,16},{1,9},{9,1},{17,25},{25,17},{2,10},{10... | collective-permute-start | bytes 61448 | tf_op jit(solution)/shard_map/ppermute | solution.py:22
  33.4 6.0 %collective-permute-start.17 = (bf16[16,4096]{1,0:T(8,128)(2,1)S(1)}, bf16[16,4096]{1,0:T(8,128)(2,1)S(1)}, u32[]{:S(2)}, u32[]{:S(2)}) collective-permute-start(bf16[16,4096]{1,0:T(8,128)(2,1)S(1)} %weights.1.refs_0_), channel_id=1, source_target_pairs={{0,6},{1,7},{2,4},{3,5},{4,2},{5,3},{6,0},{7,1},{8,14},{9,15},{10,... | collective-permute-start | bytes 393224 | tf_op jit(solution)/shard_map/ppermute | solution.py:22
  35.5 5.3 %collective-permute-start.16 = (bf16[16,4096]{1,0:T(8,128)(2,1)S(1)}, bf16[16,4096]{1,0:T(8,128)(2,1)S(1)}, u32[]{:S(2)}, u32[]{:S(2)}) collective-permute-start(bf16[16,4096]{1,0:T(8,128)(2,1)S(1)} %weights.1.refs_0_), channel_id=1, source_target_pairs={{0,4},{1,5},{2,6},{3,7},{4,0},{5,1},{6,2},{7,3},{8,12},{9,13},{10,... | collective-permute-start | bytes 393224 | tf_op jit(solution)/shard_map/ppermute | solution.py:22
  36.0 5.0 %collective-permute-start.15 = (bf16[16,4096]{1,0:T(8,128)(2,1)S(1)}, bf16[16,4096]{1,0:T(8,128)(2,1)S(1)}, u32[]{:S(2)}, u32[]{:S(2)}) collective-permute-start(bf16[16,4096]{1,0:T(8,128)(2,1)S(1)} %weights.1.refs_0_), channel_id=1, source_target_pairs={{0,2},{1,3},{2,0},{3,1},{4,6},{5,7},{6,4},{7,5},{8,10},{9,11},{10,... | collective-permute-start | bytes 393224 | tf_op jit(solution)/shard_map/ppermute | solution.py:22
  36.9 5.3 %collective-permute-start.20 = (bf16[16,4096]{1,0:T(8,128)(2,1)S(1)}, bf16[16,4096]{1,0:T(8,128)(2,1)S(1)}, u32[]{:S(2)}, u32[]{:S(2)}) collective-permute-start(bf16[16,4096]{1,0:T(8,128)(2,1)S(1)} %weights.1.refs_0_), channel_id=1, source_target_pairs={{0,1},{1,0},{2,3},{3,2},{4,5},{5,4},{6,7},{7,6},{8,9},{9,8},{10,11... | collective-permute-start | bytes 393224 | tf_op jit(solution)/shard_map/ppermute | solution.py:22
  39.3 2.9 %collective-permute-start.23 = (bf16[16,4096]{1,0:T(8,128)(2,1)S(1)}, bf16[16,4096]{1,0:T(8,128)(2,1)S(1)}, u32[]{:S(2)}, u32[]{:S(2)}) collective-permute-start(bf16[16,4096]{1,0:T(8,128)(2,1)S(1)} %collective-permute-done.17.refs_3_), channel_id=1, source_target_pairs={{0,1},{1,0},{2,3},{3,2},{4,5},{5,4},{6,7},{7,6},{8,9},{9,8},{10,11... | collective-permute-start | bytes 393224 | tf_op jit(solution)/shard_map/ppermute | solution.py:22
  42.1 4.8 %collective-permute-start.18 = (s16[17,16,128]{2,1,0:T(8,128)(2,1)S(1)}, s16[17,16,128]{2,1,0:T(8,128)(2,1)S(1)}, u32[]{:S(2)}, u32[]{:S(2)}) collective-permute-start(s16[17,16,128]{2,1,0:T(8,128)(2,1)S(1)} %gradients.2.mine), channel_id=1, source_target_pairs={{0,8},{8,0},{16,24},{24,16},{1,9},{9,1},{17,25},{25,17},{2,10},{10... | collective-permute-start | bytes 208904 | tf_op jit(solution)/shard_map/ppermute | solution.py:22
  43.2 5.5 %collective-permute-start.24 = (s16[17,16,128]{2,1,0:T(8,128)(2,1)S(1)}, s16[17,16,128]{2,1,0:T(8,128)(2,1)S(1)}, u32[]{:S(2)}, u32[]{:S(2)}) collective-permute-start(s16[17,16,128]{2,1,0:T(8,128)(2,1)S(1)} %gradients.3.mine), channel_id=1, source_target_pairs={{0,8},{8,0},{16,24},{24,16},{1,9},{9,1},{17,25},{25,17},{2,10},{10... | collective-permute-start | bytes 208904 | tf_op jit(solution)/shard_map/ppermute | solution.py:22
  47.1 7.5 %collective-permute-start.19 = (s16[17,16,128]{2,1,0:T(8,128)(2,1)S(1)}, s16[17,16,128]{2,1,0:T(8,128)(2,1)S(1)}, u32[]{:S(2)}, u32[]{:S(2)}) collective-permute-start(s16[17,16,128]{2,1,0:T(8,128)(2,1)S(1)} %merge.2.mine), channel_id=1, source_target_pairs={{0,16},{8,24},{16,0},{24,8},{1,17},{9,25},{17,1},{25,9},{2,18},{10... | collective-permute-start | bytes 208904 | tf_op jit(solution)/shard_map/ppermute | solution.py:22
  48.7 6.5 %collective-permute-start.25 = (s16[17,16,128]{2,1,0:T(8,128)(2,1)S(1)}, s16[17,16,128]{2,1,0:T(8,128)(2,1)S(1)}, u32[]{:S(2)}, u32[]{:S(2)}) collective-permute-start(s16[17,16,128]{2,1,0:T(8,128)(2,1)S(1)} %merge.3.mine), channel_id=1, source_target_pairs={{0,16},{8,24},{16,0},{24,8},{1,17},{9,25},{17,1},{25,9},{2,18},{10... | collective-permute-start | bytes 208904 | tf_op jit(solution)/shard_map/ppermute | solution.py:22
  (5 other events, 39.5 us)

commit v15 on v14

--- a/solution.py
+++ b/solution.py
@@ -84,8 +84,8 @@
         )
         for i in range(steps)
     ]
-    for copy in small + large:
-        copy.start()
+    for i, copy in enumerate(small + large):
+        copy.start(priority=i % 2)
     for copy in small:
         copy.wait()
     turned[...] = own_directions[...].astype(F32).T.reshape(turned.shape)
@@ -281,11 +281,13 @@
     scaled = jnp.zeros((kf, LO), F32)
     for g in range(groups):
         scaled = scaled + ordered[g * kf : (g + 1) * kf] * square[g : g + 1]
-    message[:kf] = plain[...] + more[...]
-    message[kf : 2 * kf] = sum(scaled[:, start : start + 128] for start in range(0, LO, 128))
-    totals = [jnp.sum(jnp.sum(v, axis=0, keepdims=True), axis=1, keepdims=True) for v in (hazard, square)]
-    rows = [jnp.broadcast_to(v, (1, 128)) for v in totals]
-    message[2 * kf :] = jnp.concatenate(rows + [jnp.zeros((6, 128), F32)], axis=0)
+    columns = [plain[...] + more[...], sum(scaled[:, start : start + 128] for start in range(0, LO, 128))]
+    columns += [jnp.sum(v, axis=0, keepdims=True) for v in (hazard, square)]
+    lane = lax.broadcasted_iota(jnp.int32, (kf, 128), 1)
+    packed = jnp.zeros((kf, 128), F32)
+    for i, column in enumerate(columns):
+        packed = jnp.where(lane == i, jnp.sum(column, axis=1, keepdims=True), packed)
+    message[...] = packed
 
 
 def shares(later, sums, events, plain, more, ordered):
@@ -293,7 +295,7 @@
     return pl.pallas_call(
         share_kernel,
         in_specs=[VMEM] * 6,
-        out_shape=[flat, flat, jax.ShapeDtypeStruct((2 * plain.shape[0] + 8, 128), F32)],
+        out_shape=[flat, flat, jax.ShapeDtypeStruct(plain.shape, F32)],
         out_specs=[VMEM] * 3,
         compiler_params=pltpu.CompilerParams(**PARAMS),
         name="shares",
@@ -469,18 +471,14 @@
     me = lax.axis_index("ex")
     for i in range(ex):
         placed[me ^ i] = messages[i][...]
-    later = jnp.zeros((kf, 128), F32)
-    own_later, before = later, later
-    hazard_before = jnp.zeros((1, 128), F32)
+    later = jnp.zeros((kf, 1), F32)
+    own_later, before, hazard_before = later, later, later
     for b in reversed(range(ex)):
-        plain, scaled, square = placed[b, :kf], placed[b, kf : 2 * kf], placed[b, 2 * kf + 1 : 2 * kf + 2]
+        plain, scaled, hazard, square = [placed[b, :, i : i + 1] for i in range(4)]
         own_later = own_later + jnp.where(b > me, plain, 0.0)
         before = before + jnp.where(b < me, scaled + square * later, 0.0)
-        hazard_before = hazard_before + jnp.where(b < me, placed[b, 2 * kf : 2 * kf + 1], 0.0)
+        hazard_before = hazard_before + jnp.where(b < me, hazard, 0.0)
         later = later + plain
-    own_later = jnp.sum(own_later, axis=1, keepdims=True)
-    before = jnp.sum(before, axis=1, keepdims=True)
-    hazard_before = hazard_before[:, :1]
     for start, part in ((0, first), (first.shape[1], rest)):
         at = slice(start, start + part.shape[1])
         value = part[...] * (cumulative[:, at] + hazard_before) - (

time: 56.3 us -> 56.6 us (level)
  no operation moved by 1% of the time
where the time goes in v15:
time: 56.6 us; the launch traced here: 56.5 us
  starting transfers between devices  28.4 us (50%)
  Pallas kernels  14.6 us (26%)
  waiting for transfers between devices  13.2 us (23%)
    ppermute x26, starting transfers between devices, swap(): return lax.ppermute(x, axis, [(s, s ^ i) for s in range(count)])  28.4 us
    ppermute x26, waiting for transfers between devices, swap(): return lax.ppermute(x, axis, [(s, s ^ i) for s in range(count)])  13.2 us
    pallas_call x1, Pallas kernels, products(): pl.pallas_call(functools.partial(product_kernel, feat, kf, chunk), in_spe...  4.11 us
    pallas_call x2, Pallas kernels, ordered_values(): pl.pallas_call(functools.partial(order_kernel, start, len(messages)), in_...  1.97 us
    pallas_call x2, Pallas kernels, gradients(): pl.pallas_call(functools.partial(gradient_kernel, parts, kf), in_specs=[V...  1.76 us
    pallas_call x1, Pallas kernels, prefix_sums(): pl.pallas_call(prefix_kernel, in_specs=[VMEM] * 3, out_shape=jax.ShapeDty...  1.75 us
  transfers between devices with their start and end apart: 26, of which 10 were waited for; matrix products, arithmetic and copies ran while one was open for 0% of the time, Pallas kernels for 16%

profile of v15, /device:TPU:0, one launch (start us, length us, event | category | flops | bytes accessed | tf_op | source)
XLA Modules:
  0.0 56.5 jit_solution(497272190185745560)
XLA Ops:
  0.0 4.1 %products.1 = (f32[16,256]{1,0:T(8,128)S(1)}, f32[16,4096]{1,0:T(8,128)S(1)}, f32[16,4096]{1,0:T(8,128)S(1)}, f32[16,4096]{1,0:T(8,128)S(1)}, f32[16,4096]{1,0:T...) custom-call(bf16[512,128]{1,0:T(8,128)(2,1)} %directions.1, ...), custom_call_target="tpu_custom_call" | custom-call | flops 536870912 | bytes 6291456 | tf_op jit(solution)/shard_map/products/pallas_call | solution.py:117
  6.0 3.9 %collective-permute-start.1 = (s16[16,2176]{1,0:T(8,128)(2,1)S(1)}, s16[16,2176]{1,0:T(8,128)(2,1)S(1)}, u32[]{:S(2)}, u32[]{:S(2)}) collective-permute-start(s16[16,2176]{1,0:T(8,128)(2,1)S(1)} %join.6), channel_id=1, source_target_pairs={{0,6},{1,7},{2,4},{3,5},{4,2},{5,3},{6,0},{7,1},{8,14},{9,15},{10,... | collective-permute-start | bytes 208904 | tf_op jit(solution)/shard_map/ppermute | solution.py:22
  11.1 2.9 %collective-permute-start.8 = (s16[16,2688]{1,0:T(8,128)(2,1)S(1)}, s16[16,2688]{1,0:T(8,128)(2,1)S(1)}, u32[]{:S(2)}, u32[]{:S(2)}) collective-permute-start(s16[16,2688]{1,0:T(8,128)(2,1)S(1)} %join.9), channel_id=1, source_target_pairs={{0,6},{1,7},{2,4},{3,5},{4,2},{5,3},{6,0},{7,1},{8,14},{9,15},{10,... | collective-permute-start | bytes 258056 | tf_op jit(solution)/shard_map/ppermute | solution.py:22
  15.9 0.9 %risks.1 = (f32[1,4096]{1,0:T(1,128)S(1)}, f32[16,256]{1,0:T(8,128)S(1)}, f32[16,256]{1,0:T(8,128)S(1)}, f32[8,128]{1,0:T(8,128)S(1)}) custom-call(f32[16,256]{1,0:T(8,128)S(1)} %pair.1.refs_0_.linear, s16[16,2176]{1,0:T(8,128)(2,1)S(1)} %collective-permute-done.1.refs_0_, s16[16,2176]{1,0:T(8,128)(2,1)S(1)} %collective-permute-done.3.refs_1_, ...), custom_call_target="tpu_custom_call" | custom-call | flops 134217728 | bytes 262144 | tf_op jit(solution)/shard_map/risks/pallas_call | solution.py:257
  16.8 1.6 %collective-permute-start.6 = (f32[8,128]{1,0:T(8,128)S(1)}, f32[8,128]{1,0:T(8,128)S(1)}, u32[]{:S(2)}, u32[]{:S(2)}) collective-permute-start(f32[8,128]{1,0:T(8,128)S(1)} %get-tuple-element.40.refs_0_), channel_id=1, source_target_pairs={{0,8},{8,0},{16,24},{24,16},{1,9},{9,1},{17,25},{25,17},{2,10},{10... | collective-permute-start | bytes 12296 | tf_op jit(solution)/shard_map/ppermute | solution.py:22
  19.3 1.2 %collective-permute-done.6.refs_1_ = f32[8,128]{1,0:T(8,128)S(1)} collective-permute-done((f32[8,128]{1,0:T(8,128)S(1)}, f32[8,128]{1,0:T(8,128)S(1)}, u32[]{:S(2)}, u32[]{:S(2)}) %collective-permute-start.6) | collective-permute-done | bytes 4128 | tf_op jit(solution)/shard_map/ppermute | solution.py:22
  20.5 2.7 %collective-permute-start.11 = (f32[8,128]{1,0:T(8,128)S(1)}, f32[8,128]{1,0:T(8,128)S(1)}, u32[]{:S(2)}, u32[]{:S(2)}) collective-permute-start(f32[8,128]{1,0:T(8,128)S(1)} %get-tuple-element.42.refs_0_), channel_id=1, source_target_pairs={{0,16},{8,24},{16,0},{24,8},{1,17},{9,25},{17,1},{25,9},{2,18},{10... | collective-permute-start | bytes 12296 | tf_op jit(solution)/shard_map/ppermute | solution.py:22
  23.2 1.2 %ordered_values.3 = (f32[16,2560]{1,0:T(8,128)S(1)}, f32[256,256]{1,0:T(8,128)S(1)}, f32[16,128]{1,0:T(8,128)S(1)}) custom-call(f32[16,4096]{1,0:T(8,128)S(1)} %get-tuple-element.47.own, f32[16,4096]{1,0:T(8,128)S(1)} %collective-permute-done.7.refs_1_.other, s16[16,2688]{1,0:T(8,128)(2,1)S(1)} %collective-permute-done.8.refs_3_.refs_0_, ...), custom_call_target="tpu_custom_call" | custom-call | flops 671088640 | bytes 983040 | tf_op jit(solution)/shard_map/ordered_values/pallas_call | solution.py:388
  25.3 3.6 %collective-permute-start.14 = (f32[16,128]{1,0:T(8,128)S(1)}, f32[16,128]{1,0:T(8,128)S(1)}, u32[]{:S(2)}, u32[]{:S(2)}) collective-permute-start(f32[16,128]{1,0:T(8,128)S(1)} %get-tuple-element.53.refs_0_), channel_id=1, source_target_pairs={{0,24},{8,16},{16,8},{24,0},{1,25},{9,17},{17,9},{25,1},{2,26},{10... | collective-permute-start | bytes 24584 | tf_op jit(solution)/shard_map/ppermute | solution.py:22
  29.7 1.8 %prefix_sums.1.refs_6_ = f32[16,4096]{1,0:T(8,128)S(1)} custom-call(f32[256,256]{1,0:T(8,128)S(1)} %suffix_sums.1.ordered.sums, f32[16,256]{1,0:T(8,128)S(1)} %get-tuple-element.56.squares.square, s32[1,4096]{1,0:T(1,128)S(1)} %bitcast.6), custom_call_target="tpu_custom_call" | custom-call | flops 1073741824 | bytes 1572864 | tf_op jit(solution)/shard_map/prefix_sums/pallas_call | solution.py:454
  31.4 0.9 %hazards.1 = (f32[1,4096]{1,0:T(1,128)S(1)}, f32[1,4096]{1,0:T(1,128)S(1)}) custom-call(f32[16,256]{1,0:T(8,128)S(1)} %get-tuple-element.57.hazard, f32[16,256]{1,0:T(8,128)S(1)} %get-tuple-element.56.squares.square, s32[1,4096]{1,0:T(1,128)S(1)} %bitcast.7), custom_call_target="tpu_custom_call" | custom-call | flops 209715200 | bytes 262144 | tf_op jit(solution)/shard_map/hazards/pallas_call | solution.py:322
  32.3 1.1 %collective-permute-done.13.refs_2_ = f32[16,128]{1,0:T(8,128)S(1)} collective-permute-done((f32[16,128]{1,0:T(8,128)S(1)}, f32[16,128]{1,0:T(8,128)S(1)}, u32[]{:S(2)}, u32[]{:S(2)}) %collective-permute-start.13) | collective-permute-done | bytes 8224 | tf_op jit(solution)/shard_map/ppermute | solution.py:22
  33.7 2.1 %collective-permute-start.17 = (bf16[16,4096]{1,0:T(8,128)(2,1)S(1)}, bf16[16,4096]{1,0:T(8,128)(2,1)S(1)}, u32[]{:S(2)}, u32[]{:S(2)}) collective-permute-start(bf16[16,4096]{1,0:T(8,128)(2,1)S(1)} %weights.1.refs_0_), channel_id=1, source_target_pairs={{0,6},{1,7},{2,4},{3,5},{4,2},{5,3},{6,0},{7,1},{8,14},{9,15},{10,... | collective-permute-start | bytes 393224 | tf_op jit(solution)/shard_map/ppermute | solution.py:22
  36.3 1.0 %collective-permute-start.15 = (bf16[16,4096]{1,0:T(8,128)(2,1)S(1)}, bf16[16,4096]{1,0:T(8,128)(2,1)S(1)}, u32[]{:S(2)}, u32[]{:S(2)}) collective-permute-start(bf16[16,4096]{1,0:T(8,128)(2,1)S(1)} %weights.1.refs_0_), channel_id=1, source_target_pairs={{0,2},{1,3},{2,0},{3,1},{4,6},{5,7},{6,4},{7,5},{8,10},{9,11},{10,... | collective-permute-start | bytes 393224 | tf_op jit(solution)/shard_map/ppermute | solution.py:22
  37.3 2.4 %collective-permute-done.17.refs_3_ = bf16[16,4096]{1,0:T(8,128)(2,1)S(1)} collective-permute-done((bf16[16,4096]{1,0:T(8,128)(2,1)S(1)}, bf16[16,4096]{1,0:T(8,128)(2,1)S(1)}, u32[]{:S(2)}, u32[]{:S(2)}) %collective-permute-start.17) | collective-permute-done | bytes 131104 | tf_op jit(solution)/shard_map/ppermute | solution.py:22
  39.7 1.4 %collective-permute-done.16.refs_2_ = bf16[16,4096]{1,0:T(8,128)(2,1)S(1)} collective-permute-done((bf16[16,4096]{1,0:T(8,128)(2,1)S(1)}, bf16[16,4096]{1,0:T(8,128)(2,1)S(1)}, u32[]{:S(2)}, u32[]{:S(2)}) %collective-permute-start.16) | collective-permute-done | bytes 131104 | tf_op jit(solution)/shard_map/ppermute | solution.py:22
  41.6 0.9 %gradients.2.mine = s16[17,16,128]{2,1,0:T(8,128)(2,1)S(1)} custom-call(bf16[16,4096]{1,0:T(8,128)(2,1)S(1)} %weights.1.refs_0_, bf16[16,4096]{1,0:T(8,128)(2,1)S(1)} %collective-permute-done.15.refs_1_, bf16[16,4096]{1,0:T(8,128)(2,1)S(1)} %collective-permute-done.16.refs_2_, bf16[16,4096]{1,0:T(8,128)(2,1)S(1)} %collective-permute-done.17.refs_3_, ...), custom_call_target="tpu_custom_call" | custom-call | flops 268435456 | bytes 4718592 | tf_op jit(solution)/shard_map/gradients/pallas_call | solution.py:542
  43.6 1.9 %collective-permute-start.24 = (s16[17,16,128]{2,1,0:T(8,128)(2,1)S(1)}, s16[17,16,128]{2,1,0:T(8,128)(2,1)S(1)}, u32[]{:S(2)}, u32[]{:S(2)}) collective-permute-start(s16[17,16,128]{2,1,0:T(8,128)(2,1)S(1)} %gradients.3.mine), channel_id=1, source_target_pairs={{0,8},{8,0},{16,24},{24,16},{1,9},{9,1},{17,25},{25,17},{2,10},{10... | collective-permute-start | bytes 208904 | tf_op jit(solution)/shard_map/ppermute | solution.py:22
  45.5 1.8 %collective-permute-done.18.other = s16[17,16,128]{2,1,0:T(8,128)(2,1)S(1)} collective-permute-done((s16[17,16,128]{2,1,0:T(8,128)(2,1)S(1)}, s16[17,16,128]{2,1,0:T(8,128)(2,1)S(1)}, u32[]{:S(2)}, u32[]{:S(2)}) %collective-permute-start.18) | collective-permute-done | bytes 69664 | tf_op jit(solution)/shard_map/ppermute | solution.py:22
  47.4 1.6 %collective-permute-start.19 = (s16[17,16,128]{2,1,0:T(8,128)(2,1)S(1)}, s16[17,16,128]{2,1,0:T(8,128)(2,1)S(1)}, u32[]{:S(2)}, u32[]{:S(2)}) collective-permute-start(s16[17,16,128]{2,1,0:T(8,128)(2,1)S(1)} %merge.2.mine), channel_id=1, source_target_pairs={{0,16},{8,24},{16,0},{24,8},{1,17},{9,25},{17,1},{25,9},{2,18},{10... | collective-permute-start | bytes 208904 | tf_op jit(solution)/shard_map/ppermute | solution.py:22
  49.1 2.6 %collective-permute-start.25 = (s16[17,16,128]{2,1,0:T(8,128)(2,1)S(1)}, s16[17,16,128]{2,1,0:T(8,128)(2,1)S(1)}, u32[]{:S(2)}, u32[]{:S(2)}) collective-permute-start(s16[17,16,128]{2,1,0:T(8,128)(2,1)S(1)} %merge.3.mine), channel_id=1, source_target_pairs={{0,16},{8,24},{16,0},{24,8},{1,17},{9,25},{17,1},{25,9},{2,18},{10... | collective-permute-start | bytes 208904 | tf_op jit(solution)/shard_map/ppermute | solution.py:22
  51.7 2.5 %collective-permute-done.19.other = s16[17,16,128]{2,1,0:T(8,128)(2,1)S(1)} collective-permute-done((s16[17,16,128]{2,1,0:T(8,128)(2,1)S(1)}, s16[17,16,128]{2,1,0:T(8,128)(2,1)S(1)}, u32[]{:S(2)}, u32[]{:S(2)}) %collective-permute-start.19) | collective-permute-done | bytes 69664 | tf_op jit(solution)/shard_map/ppermute | solution.py:22
  54.2 1.4 %collective-permute-done.25.other = s16[17,16,128]{2,1,0:T(8,128)(2,1)S(1)} collective-permute-done((s16[17,16,128]{2,1,0:T(8,128)(2,1)S(1)}, s16[17,16,128]{2,1,0:T(8,128)(2,1)S(1)}, u32[]{:S(2)}, u32[]{:S(2)}) %collective-permute-start.25) | collective-permute-done | bytes 69664 | tf_op jit(solution)/shard_map/ppermute | solution.py:22
  55.6 0.9 %finish.1 = f32[512,128]{1,0:T(8,128)} custom-call(f32[64,512]{1,0:T(8,128)S(1)} %add.1.first, s16[17,16,128]{2,1,0:T(8,128)(2,1)S(1)} %merge.3.mine, s16[17,16,128]{2,1,0:T(8,128)(2,1)S(1)} %collective-permute-done.25.other, f32[8,128]{1,0:T(8,128)S(1)} %get-tuple-element.60.count), custom_call_target="tpu_custom_call" | custom-call | tf_op jit(solution)/shard_map/finish/pallas_call | solution.py:613
  (60 shorter events, 9.9 us)
Async XLA Ops:
  4.1 1.8 %collective-permute-start = (f32[16,4352]{1,0:T(8,128)S(1)}, f32[16,4352]{1,0:T(8,128)S(1)}, u32[]{:S(2)}, u32[]{:S(2)}) collective-permute-start(f32[16,4352]{1,0:T(8,128)S(1)} %get-tuple-element.34), channel_id=1, source_target_pairs={{0,1},{1,0},{2,3},{3,2},{4,5},{5,4},{6,7},{7,6},{8,9},{9,8},{10,11... | collective-permute-start | bytes 835592 | tf_op jit(solution)/shard_map/ppermute | solution.py:22
  4.6 5.3 %collective-permute-start.2 = (f32[16,4096]{1,0:T(8,128)S(1)}, f32[16,4096]{1,0:T(8,128)S(1)}, u32[]{:S(2)}, u32[]{:S(2)}) collective-permute-start(f32[16,4096]{1,0:T(8,128)S(1)} %get-tuple-element.37), channel_id=1, source_target_pairs={{0,1},{1,0},{2,3},{3,2},{4,5},{5,4},{6,7},{7,6},{8,9},{9,8},{10,11... | collective-permute-start | bytes 786440 | tf_op jit(solution)/shard_map/ppermute | solution.py:22
  4.7 5.9 %collective-permute-start.4 = (f32[16,4096]{1,0:T(8,128)S(1)}, f32[16,4096]{1,0:T(8,128)S(1)}, u32[]{:S(2)}, u32[]{:S(2)}) collective-permute-start(f32[16,4096]{1,0:T(8,128)S(1)} %get-tuple-element.39), channel_id=1, source_target_pairs={{0,1},{1,0},{2,3},{3,2},{4,5},{5,4},{6,7},{7,6},{8,9},{9,8},{10,11... | collective-permute-start | bytes 786440 | tf_op jit(solution)/shard_map/ppermute | solution.py:22
  5.2 5.8 %collective-permute-start.7 = (f32[16,4096]{1,0:T(8,128)S(1)}, f32[16,4096]{1,0:T(8,128)S(1)}, u32[]{:S(2)}, u32[]{:S(2)}) collective-permute-start(f32[16,4096]{1,0:T(8,128)S(1)} %get-tuple-element.41), channel_id=1, source_target_pairs={{0,1},{1,0},{2,3},{3,2},{4,5},{5,4},{6,7},{7,6},{8,9},{9,8},{10,11... | collective-permute-start | bytes 786440 | tf_op jit(solution)/shard_map/ppermute | solution.py:22
  6.0 8.8 %collective-permute-start.1 = (s16[16,2176]{1,0:T(8,128)(2,1)S(1)}, s16[16,2176]{1,0:T(8,128)(2,1)S(1)}, u32[]{:S(2)}, u32[]{:S(2)}) collective-permute-start(s16[16,2176]{1,0:T(8,128)(2,1)S(1)} %join.6), channel_id=1, source_target_pairs={{0,6},{1,7},{2,4},{3,5},{4,2},{5,3},{6,0},{7,1},{8,14},{9,15},{10,... | collective-permute-start | bytes 208904 | tf_op jit(solution)/shard_map/ppermute | solution.py:22
  10.1 4.9 %collective-permute-start.3 = (s16[16,2176]{1,0:T(8,128)(2,1)S(1)}, s16[16,2176]{1,0:T(8,128)(2,1)S(1)}, u32[]{:S(2)}, u32[]{:S(2)}) collective-permute-start(s16[16,2176]{1,0:T(8,128)(2,1)S(1)} %join.7), channel_id=1, source_target_pairs={{0,4},{1,5},{2,6},{3,7},{4,0},{5,1},{6,2},{7,3},{8,12},{9,13},{10,... | collective-permute-start | bytes 208904 | tf_op jit(solution)/shard_map/ppermute | solution.py:22
  10.8 5.1 %collective-permute-start.5 = (s16[16,2176]{1,0:T(8,128)(2,1)S(1)}, s16[16,2176]{1,0:T(8,128)(2,1)S(1)}, u32[]{:S(2)}, u32[]{:S(2)}) collective-permute-start(s16[16,2176]{1,0:T(8,128)(2,1)S(1)} %join.8), channel_id=1, source_target_pairs={{0,2},{1,3},{2,0},{3,1},{4,6},{5,7},{6,4},{7,5},{8,10},{9,11},{10,... | collective-permute-start | bytes 208904 | tf_op jit(solution)/shard_map/ppermute | solution.py:22
  11.1 9.4 %collective-permute-start.8 = (s16[16,2688]{1,0:T(8,128)(2,1)S(1)}, s16[16,2688]{1,0:T(8,128)(2,1)S(1)}, u32[]{:S(2)}, u32[]{:S(2)}) collective-permute-start(s16[16,2688]{1,0:T(8,128)(2,1)S(1)} %join.9), channel_id=1, source_target_pairs={{0,6},{1,7},{2,4},{3,5},{4,2},{5,3},{6,0},{7,1},{8,14},{9,15},{10,... | collective-permute-start | bytes 258056 | tf_op jit(solution)/shard_map/ppermute | solution.py:22
  14.1 6.3 %collective-permute-start.9 = (s16[16,2688]{1,0:T(8,128)(2,1)S(1)}, s16[16,2688]{1,0:T(8,128)(2,1)S(1)}, u32[]{:S(2)}, u32[]{:S(2)}) collective-permute-start(s16[16,2688]{1,0:T(8,128)(2,1)S(1)} %join.10), channel_id=1, source_target_pairs={{0,4},{1,5},{2,6},{3,7},{4,0},{5,1},{6,2},{7,3},{8,12},{9,13},{10,... | collective-permute-start | bytes 258056 | tf_op jit(solution)/shard_map/ppermute | solution.py:22
  14.9 5.6 %collective-permute-start.10 = (s16[16,2688]{1,0:T(8,128)(2,1)S(1)}, s16[16,2688]{1,0:T(8,128)(2,1)S(1)}, u32[]{:S(2)}, u32[]{:S(2)}) collective-permute-start(s16[16,2688]{1,0:T(8,128)(2,1)S(1)} %join.11), channel_id=1, source_target_pairs={{0,2},{1,3},{2,0},{3,1},{4,6},{5,7},{6,4},{7,5},{8,10},{9,11},{10,... | collective-permute-start | bytes 258056 | tf_op jit(solution)/shard_map/ppermute | solution.py:22
  16.8 3.7 %collective-permute-start.6 = (f32[8,128]{1,0:T(8,128)S(1)}, f32[8,128]{1,0:T(8,128)S(1)}, u32[]{:S(2)}, u32[]{:S(2)}) collective-permute-start(f32[8,128]{1,0:T(8,128)S(1)} %get-tuple-element.40.refs_0_), channel_id=1, source_target_pairs={{0,8},{8,0},{16,24},{24,16},{1,9},{9,1},{17,25},{25,17},{2,10},{10... | collective-permute-start | bytes 12296 | tf_op jit(solution)/shard_map/ppermute | solution.py:22
  20.5 4.6 %collective-permute-start.11 = (f32[8,128]{1,0:T(8,128)S(1)}, f32[8,128]{1,0:T(8,128)S(1)}, u32[]{:S(2)}, u32[]{:S(2)}) collective-permute-start(f32[8,128]{1,0:T(8,128)S(1)} %get-tuple-element.42.refs_0_), channel_id=1, source_target_pairs={{0,16},{8,24},{16,0},{24,8},{1,17},{9,25},{17,1},{25,9},{2,18},{10... | collective-permute-start | bytes 12296 | tf_op jit(solution)/shard_map/ppermute | solution.py:22
  25.3 7.1 %collective-permute-start.14 = (f32[16,128]{1,0:T(8,128)S(1)}, f32[16,128]{1,0:T(8,128)S(1)}, u32[]{:S(2)}, u32[]{:S(2)}) collective-permute-start(f32[16,128]{1,0:T(8,128)S(1)} %get-tuple-element.53.refs_0_), channel_id=1, source_target_pairs={{0,24},{8,16},{16,8},{24,0},{1,25},{9,17},{17,9},{25,1},{2,26},{10... | collective-permute-start | bytes 24584 | tf_op jit(solution)/shard_map/ppermute | solution.py:22
  28.9 4.5 %collective-permute-start.13 = (f32[16,128]{1,0:T(8,128)S(1)}, f32[16,128]{1,0:T(8,128)S(1)}, u32[]{:S(2)}, u32[]{:S(2)}) collective-permute-start(f32[16,128]{1,0:T(8,128)S(1)} %get-tuple-element.53.refs_0_), channel_id=1, source_target_pairs={{0,16},{8,24},{16,0},{24,8},{1,17},{9,25},{17,1},{25,9},{2,18},{10... | collective-permute-start | bytes 24584 | tf_op jit(solution)/shard_map/ppermute | solution.py:22
  28.9 4.5 %collective-permute-start.12 = (f32[16,128]{1,0:T(8,128)S(1)}, f32[16,128]{1,0:T(8,128)S(1)}, u32[]{:S(2)}, u32[]{:S(2)}) collective-permute-start(f32[16,128]{1,0:T(8,128)S(1)} %get-tuple-element.53.refs_0_), channel_id=1, source_target_pairs={{0,8},{8,0},{16,24},{24,16},{1,9},{9,1},{17,25},{25,17},{2,10},{10... | collective-permute-start | bytes 24584 | tf_op jit(solution)/shard_map/ppermute | solution.py:22
  33.7 6.0 %collective-permute-start.17 = (bf16[16,4096]{1,0:T(8,128)(2,1)S(1)}, bf16[16,4096]{1,0:T(8,128)(2,1)S(1)}, u32[]{:S(2)}, u32[]{:S(2)}) collective-permute-start(bf16[16,4096]{1,0:T(8,128)(2,1)S(1)} %weights.1.refs_0_), channel_id=1, source_target_pairs={{0,6},{1,7},{2,4},{3,5},{4,2},{5,3},{6,0},{7,1},{8,14},{9,15},{10,... | collective-permute-start | bytes 393224 | tf_op jit(solution)/shard_map/ppermute | solution.py:22
  35.8 5.3 %collective-permute-start.16 = (bf16[16,4096]{1,0:T(8,128)(2,1)S(1)}, bf16[16,4096]{1,0:T(8,128)(2,1)S(1)}, u32[]{:S(2)}, u32[]{:S(2)}) collective-permute-start(bf16[16,4096]{1,0:T(8,128)(2,1)S(1)} %weights.1.refs_0_), channel_id=1, source_target_pairs={{0,4},{1,5},{2,6},{3,7},{4,0},{5,1},{6,2},{7,3},{8,12},{9,13},{10,... | collective-permute-start | bytes 393224 | tf_op jit(solution)/shard_map/ppermute | solution.py:22
  36.3 5.0 %collective-permute-start.15 = (bf16[16,4096]{1,0:T(8,128)(2,1)S(1)}, bf16[16,4096]{1,0:T(8,128)(2,1)S(1)}, u32[]{:S(2)}, u32[]{:S(2)}) collective-permute-start(bf16[16,4096]{1,0:T(8,128)(2,1)S(1)} %weights.1.refs_0_), channel_id=1, source_target_pairs={{0,2},{1,3},{2,0},{3,1},{4,6},{5,7},{6,4},{7,5},{8,10},{9,11},{10,... | collective-permute-start | bytes 393224 | tf_op jit(solution)/shard_map/ppermute | solution.py:22
  37.3 5.4 %collective-permute-start.20 = (bf16[16,4096]{1,0:T(8,128)(2,1)S(1)}, bf16[16,4096]{1,0:T(8,128)(2,1)S(1)}, u32[]{:S(2)}, u32[]{:S(2)}) collective-permute-start(bf16[16,4096]{1,0:T(8,128)(2,1)S(1)} %weights.1.refs_0_), channel_id=1, source_target_pairs={{0,1},{1,0},{2,3},{3,2},{4,5},{5,4},{6,7},{7,6},{8,9},{9,8},{10,11... | collective-permute-start | bytes 393224 | tf_op jit(solution)/shard_map/ppermute | solution.py:22
  39.7 3.0 %collective-permute-start.23 = (bf16[16,4096]{1,0:T(8,128)(2,1)S(1)}, bf16[16,4096]{1,0:T(8,128)(2,1)S(1)}, u32[]{:S(2)}, u32[]{:S(2)}) collective-permute-start(bf16[16,4096]{1,0:T(8,128)(2,1)S(1)} %collective-permute-done.17.refs_3_), channel_id=1, source_target_pairs={{0,1},{1,0},{2,3},{3,2},{4,5},{5,4},{6,7},{7,6},{8,9},{9,8},{10,11... | collective-permute-start | bytes 393224 | tf_op jit(solution)/shard_map/ppermute | solution.py:22
  42.4 4.8 %collective-permute-start.18 = (s16[17,16,128]{2,1,0:T(8,128)(2,1)S(1)}, s16[17,16,128]{2,1,0:T(8,128)(2,1)S(1)}, u32[]{:S(2)}, u32[]{:S(2)}) collective-permute-start(s16[17,16,128]{2,1,0:T(8,128)(2,1)S(1)} %gradients.2.mine), channel_id=1, source_target_pairs={{0,8},{8,0},{16,24},{24,16},{1,9},{9,1},{17,25},{25,17},{2,10},{10... | collective-permute-start | bytes 208904 | tf_op jit(solution)/shard_map/ppermute | solution.py:22
  43.6 5.4 %collective-permute-start.24 = (s16[17,16,128]{2,1,0:T(8,128)(2,1)S(1)}, s16[17,16,128]{2,1,0:T(8,128)(2,1)S(1)}, u32[]{:S(2)}, u32[]{:S(2)}) collective-permute-start(s16[17,16,128]{2,1,0:T(8,128)(2,1)S(1)} %gradients.3.mine), channel_id=1, source_target_pairs={{0,8},{8,0},{16,24},{24,16},{1,9},{9,1},{17,25},{25,17},{2,10},{10... | collective-permute-start | bytes 208904 | tf_op jit(solution)/shard_map/ppermute | solution.py:22
  47.4 6.8 %collective-permute-start.19 = (s16[17,16,128]{2,1,0:T(8,128)(2,1)S(1)}, s16[17,16,128]{2,1,0:T(8,128)(2,1)S(1)}, u32[]{:S(2)}, u32[]{:S(2)}) collective-permute-start(s16[17,16,128]{2,1,0:T(8,128)(2,1)S(1)} %merge.2.mine), channel_id=1, source_target_pairs={{0,16},{8,24},{16,0},{24,8},{1,17},{9,25},{17,1},{25,9},{2,18},{10... | collective-permute-start | bytes 208904 | tf_op jit(solution)/shard_map/ppermute | solution.py:22
  49.1 6.5 %collective-permute-start.25 = (s16[17,16,128]{2,1,0:T(8,128)(2,1)S(1)}, s16[17,16,128]{2,1,0:T(8,128)(2,1)S(1)}, u32[]{:S(2)}, u32[]{:S(2)}) collective-permute-start(s16[17,16,128]{2,1,0:T(8,128)(2,1)S(1)} %merge.3.mine), channel_id=1, source_target_pairs={{0,16},{8,24},{16,0},{24,8},{1,17},{9,25},{17,1},{25,9},{2,18},{10... | collective-permute-start | bytes 208904 | tf_op jit(solution)/shard_map/ppermute | solution.py:22
  (5 other events, 40.0 us)

commit v16 on v14

--- a/solution.py
+++ b/solution.py
@@ -111,7 +111,7 @@
     persons, variants = dosages.shape
     k = directions.shape[1]
     kf = k // feat
-    chunk = min(512, persons)
+    chunk = min(1024, persons)
     piece = jax.ShapeDtypeStruct((kf, persons), F32)
     first = jax.ShapeDtypeStruct((kf, persons + LO), F32)
     out = pl.pallas_call(
@@ -670,7 +670,7 @@
     own = weights(messages, tangent, more_tangent, summed, risk, cumulative, squares)
 
     chips = {0: own}
-    for q in reversed(range(1, feat // 2)):
+    for q in range(1, feat // 2):
         chips[q] = swap(own, "feat", 2 * q)
     near = [chips[q] for q in range(feat // 2)]
     far = [swap(chips[q], "feat", 1) for q in range(feat // 2)]

time: 56.3 us -> 55.9 us (level)
  no operation moved by 1% of the time
where the time goes in v16:
time: 55.9 us; the launch traced here: 55.8 us
  starting transfers between devices  28 us (50%)
  waiting for transfers between devices  13.8 us (25%)
  Pallas kernels  13.7 us (25%)
    ppermute x26, starting transfers between devices, swap(): return lax.ppermute(x, axis, [(s, s ^ i) for s in range(count)])  28 us
    ppermute x26, waiting for transfers between devices, swap(): return lax.ppermute(x, axis, [(s, s ^ i) for s in range(count)])  13.8 us
    pallas_call x1, Pallas kernels, products(): pl.pallas_call(functools.partial(product_kernel, feat, kf, chunk), in_spe...  3.35 us
    pallas_call x2, Pallas kernels, ordered_values(): pl.pallas_call(functools.partial(order_kernel, start, len(messages)), in_...  1.97 us
    pallas_call x2, Pallas kernels, gradients(): pl.pallas_call(functools.partial(gradient_kernel, parts, kf), in_specs=[V...  1.75 us
    pallas_call x1, Pallas kernels, prefix_sums(): pl.pallas_call(prefix_kernel, in_specs=[VMEM] * 3, out_shape=jax.ShapeDty...  1.75 us
  transfers between devices with their start and end apart: 26, of which 10 were waited for; matrix products, arithmetic and copies ran while one was open for 0% of the time, Pallas kernels for 16%

profile of v16, /device:TPU:0, one launch (start us, length us, event | category | flops | bytes accessed | tf_op | source)
XLA Modules:
  0.0 55.8 jit_solution(14275768320531185475)
XLA Ops:
  0.0 3.3 %products.1 = (f32[16,256]{1,0:T(8,128)S(1)}, f32[16,4096]{1,0:T(8,128)S(1)}, f32[16,4096]{1,0:T(8,128)S(1)}, f32[16,4096]{1,0:T(8,128)S(1)}, f32[16,4096]{1,0:T...) custom-call(bf16[512,128]{1,0:T(8,128)(2,1)} %directions.1, ...), custom_call_target="tpu_custom_call" | custom-call | flops 536870912 | bytes 6291456 | tf_op jit(solution)/shard_map/products/pallas_call | solution.py:117
  5.3 3.9 %collective-permute-start.1 = (s16[16,2176]{1,0:T(8,128)(2,1)S(1)}, s16[16,2176]{1,0:T(8,128)(2,1)S(1)}, u32[]{:S(2)}, u32[]{:S(2)}) collective-permute-start(s16[16,2176]{1,0:T(8,128)(2,1)S(1)} %join.6), channel_id=1, source_target_pairs={{0,6},{1,7},{2,4},{3,5},{4,2},{5,3},{6,0},{7,1},{8,14},{9,15},{10,... | collective-permute-start | bytes 208904 | tf_op jit(solution)/shard_map/ppermute | solution.py:22
  10.3 2.9 %collective-permute-start.8 = (s16[16,2688]{1,0:T(8,128)(2,1)S(1)}, s16[16,2688]{1,0:T(8,128)(2,1)S(1)}, u32[]{:S(2)}, u32[]{:S(2)}) collective-permute-start(s16[16,2688]{1,0:T(8,128)(2,1)S(1)} %join.9), channel_id=1, source_target_pairs={{0,6},{1,7},{2,4},{3,5},{4,2},{5,3},{6,0},{7,1},{8,14},{9,15},{10,... | collective-permute-start | bytes 258056 | tf_op jit(solution)/shard_map/ppermute | solution.py:22
  14.3 0.9 %collective-permute-done.5.refs_2_ = s16[16,2176]{1,0:T(8,128)(2,1)S(1)} collective-permute-done((s16[16,2176]{1,0:T(8,128)(2,1)S(1)}, s16[16,2176]{1,0:T(8,128)(2,1)S(1)}, u32[]{:S(2)}, u32[]{:S(2)}) %collective-permute-start.5) | collective-permute-done | bytes 69664 | tf_op jit(solution)/shard_map/ppermute | solution.py:22
  15.1 0.9 %risks.1 = (f32[1,4096]{1,0:T(1,128)S(1)}, f32[16,256]{1,0:T(8,128)S(1)}, f32[16,256]{1,0:T(8,128)S(1)}, f32[8,128]{1,0:T(8,128)S(1)}) custom-call(f32[16,256]{1,0:T(8,128)S(1)} %pair.1.refs_0_.linear, s16[16,2176]{1,0:T(8,128)(2,1)S(1)} %collective-permute-done.1.refs_0_, s16[16,2176]{1,0:T(8,128)(2,1)S(1)} %collective-permute-done.3.refs_1_, ...), custom_call_target="tpu_custom_call" | custom-call | flops 134217728 | bytes 262144 | tf_op jit(solution)/shard_map/risks/pallas_call | solution.py:257
  16.0 1.6 %collective-permute-start.6 = (f32[8,128]{1,0:T(8,128)S(1)}, f32[8,128]{1,0:T(8,128)S(1)}, u32[]{:S(2)}, u32[]{:S(2)}) collective-permute-start(f32[8,128]{1,0:T(8,128)S(1)} %get-tuple-element.40.refs_0_), channel_id=1, source_target_pairs={{0,8},{8,0},{16,24},{24,16},{1,9},{9,1},{17,25},{25,17},{2,10},{10... | collective-permute-start | bytes 12296 | tf_op jit(solution)/shard_map/ppermute | solution.py:22
  18.5 1.2 %collective-permute-done.6.refs_1_ = f32[8,128]{1,0:T(8,128)S(1)} collective-permute-done((f32[8,128]{1,0:T(8,128)S(1)}, f32[8,128]{1,0:T(8,128)S(1)}, u32[]{:S(2)}, u32[]{:S(2)}) %collective-permute-start.6) | collective-permute-done | bytes 4128 | tf_op jit(solution)/shard_map/ppermute | solution.py:22
  19.8 2.6 %collective-permute-start.11 = (f32[8,128]{1,0:T(8,128)S(1)}, f32[8,128]{1,0:T(8,128)S(1)}, u32[]{:S(2)}, u32[]{:S(2)}) collective-permute-start(f32[8,128]{1,0:T(8,128)S(1)} %get-tuple-element.42.refs_0_), channel_id=1, source_target_pairs={{0,16},{8,24},{16,0},{24,8},{1,17},{9,25},{17,1},{25,9},{2,18},{10... | collective-permute-start | bytes 12296 | tf_op jit(solution)/shard_map/ppermute | solution.py:22
  22.4 1.2 %ordered_values.3 = (f32[16,2560]{1,0:T(8,128)S(1)}, f32[256,256]{1,0:T(8,128)S(1)}, f32[16,128]{1,0:T(8,128)S(1)}) custom-call(f32[16,4096]{1,0:T(8,128)S(1)} %get-tuple-element.47.own, f32[16,4096]{1,0:T(8,128)S(1)} %collective-permute-done.7.refs_1_.other, s16[16,2688]{1,0:T(8,128)(2,1)S(1)} %collective-permute-done.8.refs_3_.refs_0_, ...), custom_call_target="tpu_custom_call" | custom-call | flops 671088640 | bytes 983040 | tf_op jit(solution)/shard_map/ordered_values/pallas_call | solution.py:386
  24.5 3.6 %collective-permute-start.14 = (f32[40,128]{1,0:T(8,128)S(1)}, f32[40,128]{1,0:T(8,128)S(1)}, u32[]{:S(2)}, u32[]{:S(2)}) collective-permute-start(f32[40,128]{1,0:T(8,128)S(1)} %get-tuple-element.53.refs_0_), channel_id=1, source_target_pairs={{0,24},{8,16},{16,8},{24,0},{1,25},{9,17},{17,9},{25,1},{2,26},{10... | collective-permute-start | bytes 61448 | tf_op jit(solution)/shard_map/ppermute | solution.py:22
  28.9 1.7 %prefix_sums.1.refs_6_ = f32[16,4096]{1,0:T(8,128)S(1)} custom-call(f32[256,256]{1,0:T(8,128)S(1)} %suffix_sums.1.ordered.sums, f32[16,256]{1,0:T(8,128)S(1)} %get-tuple-element.56.squares.square, s32[1,4096]{1,0:T(1,128)S(1)} %bitcast.6), custom_call_target="tpu_custom_call" | custom-call | flops 1073741824 | bytes 1572864 | tf_op jit(solution)/shard_map/prefix_sums/pallas_call | solution.py:452
  30.7 0.9 %hazards.1 = (f32[1,4096]{1,0:T(1,128)S(1)}, f32[1,4096]{1,0:T(1,128)S(1)}) custom-call(f32[16,256]{1,0:T(8,128)S(1)} %get-tuple-element.57.hazard, f32[16,256]{1,0:T(8,128)S(1)} %get-tuple-element.56.squares.square, s32[1,4096]{1,0:T(1,128)S(1)} %bitcast.7), custom_call_target="tpu_custom_call" | custom-call | flops 209715200 | bytes 262144 | tf_op jit(solution)/shard_map/hazards/pallas_call | solution.py:320
  31.6 1.2 %collective-permute-done.13.refs_2_ = f32[40,128]{1,0:T(8,128)S(1)} collective-permute-done((f32[40,128]{1,0:T(8,128)S(1)}, f32[40,128]{1,0:T(8,128)S(1)}, u32[]{:S(2)}, u32[]{:S(2)}) %collective-permute-start.13) | collective-permute-done | bytes 20512 | tf_op jit(solution)/shard_map/ppermute | solution.py:22
  33.0 2.1 %collective-permute-start.17 = (bf16[16,4096]{1,0:T(8,128)(2,1)S(1)}, bf16[16,4096]{1,0:T(8,128)(2,1)S(1)}, u32[]{:S(2)}, u32[]{:S(2)}) collective-permute-start(bf16[16,4096]{1,0:T(8,128)(2,1)S(1)} %weights.1.refs_0_), channel_id=1, source_target_pairs={{0,6},{1,7},{2,4},{3,5},{4,2},{5,3},{6,0},{7,1},{8,14},{9,15},{10,... | collective-permute-start | bytes 393224 | tf_op jit(solution)/shard_map/ppermute | solution.py:22
  35.6 1.0 %collective-permute-start.15 = (bf16[16,4096]{1,0:T(8,128)(2,1)S(1)}, bf16[16,4096]{1,0:T(8,128)(2,1)S(1)}, u32[]{:S(2)}, u32[]{:S(2)}) collective-permute-start(bf16[16,4096]{1,0:T(8,128)(2,1)S(1)} %weights.1.refs_0_), channel_id=1, source_target_pairs={{0,2},{1,3},{2,0},{3,1},{4,6},{5,7},{6,4},{7,5},{8,10},{9,11},{10,... | collective-permute-start | bytes 393224 | tf_op jit(solution)/shard_map/ppermute | solution.py:22
  36.5 2.4 %collective-permute-done.17.refs_3_ = bf16[16,4096]{1,0:T(8,128)(2,1)S(1)} collective-permute-done((bf16[16,4096]{1,0:T(8,128)(2,1)S(1)}, bf16[16,4096]{1,0:T(8,128)(2,1)S(1)}, u32[]{:S(2)}, u32[]{:S(2)}) %collective-permute-start.17) | collective-permute-done | bytes 131104 | tf_op jit(solution)/shard_map/ppermute | solution.py:22
  38.9 1.4 %collective-permute-done.16.refs_2_ = bf16[16,4096]{1,0:T(8,128)(2,1)S(1)} collective-permute-done((bf16[16,4096]{1,0:T(8,128)(2,1)S(1)}, bf16[16,4096]{1,0:T(8,128)(2,1)S(1)}, u32[]{:S(2)}, u32[]{:S(2)}) %collective-permute-start.16) | collective-permute-done | bytes 131104 | tf_op jit(solution)/shard_map/ppermute | solution.py:22
  40.8 0.9 %gradients.2.mine = s16[17,16,128]{2,1,0:T(8,128)(2,1)S(1)} custom-call(bf16[16,4096]{1,0:T(8,128)(2,1)S(1)} %weights.1.refs_0_, bf16[16,4096]{1,0:T(8,128)(2,1)S(1)} %collective-permute-done.15.refs_1_, bf16[16,4096]{1,0:T(8,128)(2,1)S(1)} %collective-permute-done.16.refs_2_, bf16[16,4096]{1,0:T(8,128)(2,1)S(1)} %collective-permute-done.17.refs_3_, ...), custom_call_target="tpu_custom_call" | custom-call | flops 268435456 | bytes 4718592 | tf_op jit(solution)/shard_map/gradients/pallas_call | solution.py:544
  42.8 2.0 %collective-permute-start.24 = (s16[17,16,128]{2,1,0:T(8,128)(2,1)S(1)}, s16[17,16,128]{2,1,0:T(8,128)(2,1)S(1)}, u32[]{:S(2)}, u32[]{:S(2)}) collective-permute-start(s16[17,16,128]{2,1,0:T(8,128)(2,1)S(1)} %gradients.3.mine), channel_id=1, source_target_pairs={{0,8},{8,0},{16,24},{24,16},{1,9},{9,1},{17,25},{25,17},{2,10},{10... | collective-permute-start | bytes 208904 | tf_op jit(solution)/shard_map/ppermute | solution.py:22
  44.8 1.8 %collective-permute-done.18.other = s16[17,16,128]{2,1,0:T(8,128)(2,1)S(1)} collective-permute-done((s16[17,16,128]{2,1,0:T(8,128)(2,1)S(1)}, s16[17,16,128]{2,1,0:T(8,128)(2,1)S(1)}, u32[]{:S(2)}, u32[]{:S(2)}) %collective-permute-start.18) | collective-permute-done | bytes 69664 | tf_op jit(solution)/shard_map/ppermute | solution.py:22
  46.6 1.6 %collective-permute-start.19 = (s16[17,16,128]{2,1,0:T(8,128)(2,1)S(1)}, s16[17,16,128]{2,1,0:T(8,128)(2,1)S(1)}, u32[]{:S(2)}, u32[]{:S(2)}) collective-permute-start(s16[17,16,128]{2,1,0:T(8,128)(2,1)S(1)} %merge.2.mine), channel_id=1, source_target_pairs={{0,16},{8,24},{16,0},{24,8},{1,17},{9,25},{17,1},{25,9},{2,18},{10... | collective-permute-start | bytes 208904 | tf_op jit(solution)/shard_map/ppermute | solution.py:22
  48.3 2.2 %collective-permute-start.25 = (s16[17,16,128]{2,1,0:T(8,128)(2,1)S(1)}, s16[17,16,128]{2,1,0:T(8,128)(2,1)S(1)}, u32[]{:S(2)}, u32[]{:S(2)}) collective-permute-start(s16[17,16,128]{2,1,0:T(8,128)(2,1)S(1)} %merge.3.mine), channel_id=1, source_target_pairs={{0,16},{8,24},{16,0},{24,8},{1,17},{9,25},{17,1},{25,9},{2,18},{10... | collective-permute-start | bytes 208904 | tf_op jit(solution)/shard_map/ppermute | solution.py:22
  50.6 3.5 %collective-permute-done.19.other = s16[17,16,128]{2,1,0:T(8,128)(2,1)S(1)} collective-permute-done((s16[17,16,128]{2,1,0:T(8,128)(2,1)S(1)}, s16[17,16,128]{2,1,0:T(8,128)(2,1)S(1)}, u32[]{:S(2)}, u32[]{:S(2)}) %collective-permute-start.19) | collective-permute-done | bytes 69664 | tf_op jit(solution)/shard_map/ppermute | solution.py:22
  54.9 0.9 %finish.1 = f32[512,128]{1,0:T(8,128)} custom-call(f32[64,512]{1,0:T(8,128)S(1)} %add.1.first, s16[17,16,128]{2,1,0:T(8,128)(2,1)S(1)} %merge.3.mine, s16[17,16,128]{2,1,0:T(8,128)(2,1)S(1)} %collective-permute-done.25.other, f32[8,128]{1,0:T(8,128)S(1)} %get-tuple-element.60.count), custom_call_target="tpu_custom_call" | custom-call | tf_op jit(solution)/shard_map/finish/pallas_call | solution.py:615
  (60 shorter events, 9.6 us)
Async XLA Ops:
  3.4 1.8 %collective-permute-start = (f32[16,4352]{1,0:T(8,128)S(1)}, f32[16,4352]{1,0:T(8,128)S(1)}, u32[]{:S(2)}, u32[]{:S(2)}) collective-permute-start(f32[16,4352]{1,0:T(8,128)S(1)} %get-tuple-element.34), channel_id=1, source_target_pairs={{0,1},{1,0},{2,3},{3,2},{4,5},{5,4},{6,7},{7,6},{8,9},{9,8},{10,11... | collective-permute-start | bytes 835592 | tf_op jit(solution)/shard_map/ppermute | solution.py:22
  3.9 5.3 %collective-permute-start.2 = (f32[16,4096]{1,0:T(8,128)S(1)}, f32[16,4096]{1,0:T(8,128)S(1)}, u32[]{:S(2)}, u32[]{:S(2)}) collective-permute-start(f32[16,4096]{1,0:T(8,128)S(1)} %get-tuple-element.37), channel_id=1, source_target_pairs={{0,1},{1,0},{2,3},{3,2},{4,5},{5,4},{6,7},{7,6},{8,9},{9,8},{10,11... | collective-permute-start | bytes 786440 | tf_op jit(solution)/shard_map/ppermute | solution.py:22
  4.0 5.9 %collective-permute-start.4 = (f32[16,4096]{1,0:T(8,128)S(1)}, f32[16,4096]{1,0:T(8,128)S(1)}, u32[]{:S(2)}, u32[]{:S(2)}) collective-permute-start(f32[16,4096]{1,0:T(8,128)S(1)} %get-tuple-element.39), channel_id=1, source_target_pairs={{0,1},{1,0},{2,3},{3,2},{4,5},{5,4},{6,7},{7,6},{8,9},{9,8},{10,11... | collective-permute-start | bytes 786440 | tf_op jit(solution)/shard_map/ppermute | solution.py:22
  4.4 5.8 %collective-permute-start.7 = (f32[16,4096]{1,0:T(8,128)S(1)}, f32[16,4096]{1,0:T(8,128)S(1)}, u32[]{:S(2)}, u32[]{:S(2)}) collective-permute-start(f32[16,4096]{1,0:T(8,128)S(1)} %get-tuple-element.41), channel_id=1, source_target_pairs={{0,1},{1,0},{2,3},{3,2},{4,5},{5,4},{6,7},{7,6},{8,9},{9,8},{10,11... | collective-permute-start | bytes 786440 | tf_op jit(solution)/shard_map/ppermute | solution.py:22
  5.3 8.8 %collective-permute-start.1 = (s16[16,2176]{1,0:T(8,128)(2,1)S(1)}, s16[16,2176]{1,0:T(8,128)(2,1)S(1)}, u32[]{:S(2)}, u32[]{:S(2)}) collective-permute-start(s16[16,2176]{1,0:T(8,128)(2,1)S(1)} %join.6), channel_id=1, source_target_pairs={{0,6},{1,7},{2,4},{3,5},{4,2},{5,3},{6,0},{7,1},{8,14},{9,15},{10,... | collective-permute-start | bytes 208904 | tf_op jit(solution)/shard_map/ppermute | solution.py:22
  9.3 4.9 %collective-permute-start.3 = (s16[16,2176]{1,0:T(8,128)(2,1)S(1)}, s16[16,2176]{1,0:T(8,128)(2,1)S(1)}, u32[]{:S(2)}, u32[]{:S(2)}) collective-permute-start(s16[16,2176]{1,0:T(8,128)(2,1)S(1)} %join.7), channel_id=1, source_target_pairs={{0,4},{1,5},{2,6},{3,7},{4,0},{5,1},{6,2},{7,3},{8,12},{9,13},{10,... | collective-permute-start | bytes 208904 | tf_op jit(solution)/shard_map/ppermute | solution.py:22
  10.0 5.1 %collective-permute-start.5 = (s16[16,2176]{1,0:T(8,128)(2,1)S(1)}, s16[16,2176]{1,0:T(8,128)(2,1)S(1)}, u32[]{:S(2)}, u32[]{:S(2)}) collective-permute-start(s16[16,2176]{1,0:T(8,128)(2,1)S(1)} %join.8), channel_id=1, source_target_pairs={{0,2},{1,3},{2,0},{3,1},{4,6},{5,7},{6,4},{7,5},{8,10},{9,11},{10,... | collective-permute-start | bytes 208904 | tf_op jit(solution)/shard_map/ppermute | solution.py:22
  10.3 9.4 %collective-permute-start.8 = (s16[16,2688]{1,0:T(8,128)(2,1)S(1)}, s16[16,2688]{1,0:T(8,128)(2,1)S(1)}, u32[]{:S(2)}, u32[]{:S(2)}) collective-permute-start(s16[16,2688]{1,0:T(8,128)(2,1)S(1)} %join.9), channel_id=1, source_target_pairs={{0,6},{1,7},{2,4},{3,5},{4,2},{5,3},{6,0},{7,1},{8,14},{9,15},{10,... | collective-permute-start | bytes 258056 | tf_op jit(solution)/shard_map/ppermute | solution.py:22
  13.4 6.3 %collective-permute-start.9 = (s16[16,2688]{1,0:T(8,128)(2,1)S(1)}, s16[16,2688]{1,0:T(8,128)(2,1)S(1)}, u32[]{:S(2)}, u32[]{:S(2)}) collective-permute-start(s16[16,2688]{1,0:T(8,128)(2,1)S(1)} %join.10), channel_id=1, source_target_pairs={{0,4},{1,5},{2,6},{3,7},{4,0},{5,1},{6,2},{7,3},{8,12},{9,13},{10,... | collective-permute-start | bytes 258056 | tf_op jit(solution)/shard_map/ppermute | solution.py:22
  14.1 5.6 %collective-permute-start.10 = (s16[16,2688]{1,0:T(8,128)(2,1)S(1)}, s16[16,2688]{1,0:T(8,128)(2,1)S(1)}, u32[]{:S(2)}, u32[]{:S(2)}) collective-permute-start(s16[16,2688]{1,0:T(8,128)(2,1)S(1)} %join.11), channel_id=1, source_target_pairs={{0,2},{1,3},{2,0},{3,1},{4,6},{5,7},{6,4},{7,5},{8,10},{9,11},{10,... | collective-permute-start | bytes 258056 | tf_op jit(solution)/shard_map/ppermute | solution.py:22
  16.0 3.7 %collective-permute-start.6 = (f32[8,128]{1,0:T(8,128)S(1)}, f32[8,128]{1,0:T(8,128)S(1)}, u32[]{:S(2)}, u32[]{:S(2)}) collective-permute-start(f32[8,128]{1,0:T(8,128)S(1)} %get-tuple-element.40.refs_0_), channel_id=1, source_target_pairs={{0,8},{8,0},{16,24},{24,16},{1,9},{9,1},{17,25},{25,17},{2,10},{10... | collective-permute-start | bytes 12296 | tf_op jit(solution)/shard_map/ppermute | solution.py:22
  19.8 4.6 %collective-permute-start.11 = (f32[8,128]{1,0:T(8,128)S(1)}, f32[8,128]{1,0:T(8,128)S(1)}, u32[]{:S(2)}, u32[]{:S(2)}) collective-permute-start(f32[8,128]{1,0:T(8,128)S(1)} %get-tuple-element.42.refs_0_), channel_id=1, source_target_pairs={{0,16},{8,24},{16,0},{24,8},{1,17},{9,25},{17,1},{25,9},{2,18},{10... | collective-permute-start | bytes 12296 | tf_op jit(solution)/shard_map/ppermute | solution.py:22
  24.5 7.1 %collective-permute-start.14 = (f32[40,128]{1,0:T(8,128)S(1)}, f32[40,128]{1,0:T(8,128)S(1)}, u32[]{:S(2)}, u32[]{:S(2)}) collective-permute-start(f32[40,128]{1,0:T(8,128)S(1)} %get-tuple-element.53.refs_0_), channel_id=1, source_target_pairs={{0,24},{8,16},{16,8},{24,0},{1,25},{9,17},{17,9},{25,1},{2,26},{10... | collective-permute-start | bytes 61448 | tf_op jit(solution)/shard_map/ppermute | solution.py:22
  28.1 4.7 %collective-permute-start.13 = (f32[40,128]{1,0:T(8,128)S(1)}, f32[40,128]{1,0:T(8,128)S(1)}, u32[]{:S(2)}, u32[]{:S(2)}) collective-permute-start(f32[40,128]{1,0:T(8,128)S(1)} %get-tuple-element.53.refs_0_), channel_id=1, source_target_pairs={{0,16},{8,24},{16,0},{24,8},{1,17},{9,25},{17,1},{25,9},{2,18},{10... | collective-permute-start | bytes 61448 | tf_op jit(solution)/shard_map/ppermute | solution.py:22
  28.1 4.7 %collective-permute-start.12 = (f32[40,128]{1,0:T(8,128)S(1)}, f32[40,128]{1,0:T(8,128)S(1)}, u32[]{:S(2)}, u32[]{:S(2)}) collective-permute-start(f32[40,128]{1,0:T(8,128)S(1)} %get-tuple-element.53.refs_0_), channel_id=1, source_target_pairs={{0,8},{8,0},{16,24},{24,16},{1,9},{9,1},{17,25},{25,17},{2,10},{10... | collective-permute-start | bytes 61448 | tf_op jit(solution)/shard_map/ppermute | solution.py:22
  33.0 6.0 %collective-permute-start.17 = (bf16[16,4096]{1,0:T(8,128)(2,1)S(1)}, bf16[16,4096]{1,0:T(8,128)(2,1)S(1)}, u32[]{:S(2)}, u32[]{:S(2)}) collective-permute-start(bf16[16,4096]{1,0:T(8,128)(2,1)S(1)} %weights.1.refs_0_), channel_id=1, source_target_pairs={{0,6},{1,7},{2,4},{3,5},{4,2},{5,3},{6,0},{7,1},{8,14},{9,15},{10,... | collective-permute-start | bytes 393224 | tf_op jit(solution)/shard_map/ppermute | solution.py:22
  35.0 5.3 %collective-permute-start.16 = (bf16[16,4096]{1,0:T(8,128)(2,1)S(1)}, bf16[16,4096]{1,0:T(8,128)(2,1)S(1)}, u32[]{:S(2)}, u32[]{:S(2)}) collective-permute-start(bf16[16,4096]{1,0:T(8,128)(2,1)S(1)} %weights.1.refs_0_), channel_id=1, source_target_pairs={{0,4},{1,5},{2,6},{3,7},{4,0},{5,1},{6,2},{7,3},{8,12},{9,13},{10,... | collective-permute-start | bytes 393224 | tf_op jit(solution)/shard_map/ppermute | solution.py:22
  35.6 5.0 %collective-permute-start.15 = (bf16[16,4096]{1,0:T(8,128)(2,1)S(1)}, bf16[16,4096]{1,0:T(8,128)(2,1)S(1)}, u32[]{:S(2)}, u32[]{:S(2)}) collective-permute-start(bf16[16,4096]{1,0:T(8,128)(2,1)S(1)} %weights.1.refs_0_), channel_id=1, source_target_pairs={{0,2},{1,3},{2,0},{3,1},{4,6},{5,7},{6,4},{7,5},{8,10},{9,11},{10,... | collective-permute-start | bytes 393224 | tf_op jit(solution)/shard_map/ppermute | solution.py:22
  36.5 5.3 %collective-permute-start.20 = (bf16[16,4096]{1,0:T(8,128)(2,1)S(1)}, bf16[16,4096]{1,0:T(8,128)(2,1)S(1)}, u32[]{:S(2)}, u32[]{:S(2)}) collective-permute-start(bf16[16,4096]{1,0:T(8,128)(2,1)S(1)} %weights.1.refs_0_), channel_id=1, source_target_pairs={{0,1},{1,0},{2,3},{3,2},{4,5},{5,4},{6,7},{7,6},{8,9},{9,8},{10,11... | collective-permute-start | bytes 393224 | tf_op jit(solution)/shard_map/ppermute | solution.py:22
  38.9 2.9 %collective-permute-start.23 = (bf16[16,4096]{1,0:T(8,128)(2,1)S(1)}, bf16[16,4096]{1,0:T(8,128)(2,1)S(1)}, u32[]{:S(2)}, u32[]{:S(2)}) collective-permute-start(bf16[16,4096]{1,0:T(8,128)(2,1)S(1)} %collective-permute-done.17.refs_3_), channel_id=1, source_target_pairs={{0,1},{1,0},{2,3},{3,2},{4,5},{5,4},{6,7},{7,6},{8,9},{9,8},{10,11... | collective-permute-start | bytes 393224 | tf_op jit(solution)/shard_map/ppermute | solution.py:22
  41.7 4.8 %collective-permute-start.18 = (s16[17,16,128]{2,1,0:T(8,128)(2,1)S(1)}, s16[17,16,128]{2,1,0:T(8,128)(2,1)S(1)}, u32[]{:S(2)}, u32[]{:S(2)}) collective-permute-start(s16[17,16,128]{2,1,0:T(8,128)(2,1)S(1)} %gradients.2.mine), channel_id=1, source_target_pairs={{0,8},{8,0},{16,24},{24,16},{1,9},{9,1},{17,25},{25,17},{2,10},{10... | collective-permute-start | bytes 208904 | tf_op jit(solution)/shard_map/ppermute | solution.py:22
  42.8 5.5 %collective-permute-start.24 = (s16[17,16,128]{2,1,0:T(8,128)(2,1)S(1)}, s16[17,16,128]{2,1,0:T(8,128)(2,1)S(1)}, u32[]{:S(2)}, u32[]{:S(2)}) collective-permute-start(s16[17,16,128]{2,1,0:T(8,128)(2,1)S(1)} %gradients.3.mine), channel_id=1, source_target_pairs={{0,8},{8,0},{16,24},{24,16},{1,9},{9,1},{17,25},{25,17},{2,10},{10... | collective-permute-start | bytes 208904 | tf_op jit(solution)/shard_map/ppermute | solution.py:22
  46.6 7.5 %collective-permute-start.19 = (s16[17,16,128]{2,1,0:T(8,128)(2,1)S(1)}, s16[17,16,128]{2,1,0:T(8,128)(2,1)S(1)}, u32[]{:S(2)}, u32[]{:S(2)}) collective-permute-start(s16[17,16,128]{2,1,0:T(8,128)(2,1)S(1)} %merge.2.mine), channel_id=1, source_target_pairs={{0,16},{8,24},{16,0},{24,8},{1,17},{9,25},{17,1},{25,9},{2,18},{10... | collective-permute-start | bytes 208904 | tf_op jit(solution)/shard_map/ppermute | solution.py:22
  48.3 6.5 %collective-permute-start.25 = (s16[17,16,128]{2,1,0:T(8,128)(2,1)S(1)}, s16[17,16,128]{2,1,0:T(8,128)(2,1)S(1)}, u32[]{:S(2)}, u32[]{:S(2)}) collective-permute-start(s16[17,16,128]{2,1,0:T(8,128)(2,1)S(1)} %merge.3.mine), channel_id=1, source_target_pairs={{0,16},{8,24},{16,0},{24,8},{1,17},{9,25},{17,1},{25,9},{2,18},{10... | collective-permute-start | bytes 208904 | tf_op jit(solution)/shard_map/ppermute | solution.py:22
  (5 other events, 39.1 us)

commit v17 on v16

--- a/solution.py
+++ b/solution.py
@@ -20,6 +20,16 @@
 def swap(x, axis, i):
     count = lax.axis_size(axis)
     return lax.ppermute(x, axis, [(s, s ^ i) for s in range(count)])
+
+
+def swap_odd(x, i):
+    ex, feat = lax.axis_size("ex"), lax.axis_size("feat")
+    pairs = [(e * feat + f, (e ^ i) * feat + f) for e in range(ex) for f in range(1, feat, 2)]
+    return lax.ppermute(x, ("ex", "feat"), pairs)
+
+
+def hand_over(x):
+    return lax.ppermute(x, "feat", [(f, f - 1) for f in range(1, lax.axis_size("feat"), 2)])
 
 
 def split_two(x):
@@ -249,7 +259,8 @@
     events_out[...] = happened
     everything = jnp.sum(totals, axis=0, keepdims=True)[:, :128]
     count = jnp.sum(dot_binary(happened, jnp.ones((LO, 128), F32)), axis=0, keepdims=True)
-    message[...] = jnp.concatenate([everything, count, jnp.zeros((6, 128), F32)], axis=0)
+    message[0] = jnp.concatenate([everything, count, jnp.zeros((6, 128), F32)], axis=0)
+    message[1] = jnp.zeros((8, 128), F32)
 
 
 def risks(linear, messages, rank, events, table, rows):
@@ -261,7 +272,7 @@
             jax.ShapeDtypeStruct((1, rows), F32),
             jax.ShapeDtypeStruct((groups, LO), F32),
             jax.ShapeDtypeStruct((groups, LO), F32),
-            jax.ShapeDtypeStruct((8, 128), F32),
+            jax.ShapeDtypeStruct((2, 8, 128), F32),
         ],
         out_specs=[VMEM] * 4,
         compiler_params=pltpu.CompilerParams(**PARAMS),
@@ -270,9 +281,13 @@
     )(linear, *messages, rank, events, table)
 
 
-def share_kernel(later, sums, events, plain, more, ordered, hazard_out, squares, message):
+def share_kernel(state, handed, sums, events, plain, more, ordered, *outs):
+    hazard_out, squares, message, total = outs
     kf = plain.shape[0]
     groups = sums.shape[0]
+    odd = (lax.axis_index("feat") & 1) == 1
+    total[...] = jnp.where(odd, state[0], handed[0])
+    later = jnp.where(odd, state[1], handed[1])
     risk_sum = sums[...] + later[0:1, 0:1]
     hazard = events[...] / risk_sum
     square = events[...] / (risk_sum * risk_sum)
@@ -288,16 +303,21 @@
     message[2 * kf :] = jnp.concatenate(rows + [jnp.zeros((6, 128), F32)], axis=0)
 
 
-def shares(later, sums, events, plain, more, ordered):
+def shares(state, handed, sums, events, plain, more, ordered):
     flat = jax.ShapeDtypeStruct(sums.shape, F32)
     return pl.pallas_call(
         share_kernel,
-        in_specs=[VMEM] * 6,
-        out_shape=[flat, flat, jax.ShapeDtypeStruct((2 * plain.shape[0] + 8, 128), F32)],
-        out_specs=[VMEM] * 3,
+        in_specs=[VMEM] * 7,
+        out_shape=[
+            flat,
+            flat,
+            jax.ShapeDtypeStruct((2 * plain.shape[0] + 8, 128), F32),
+            jax.ShapeDtypeStruct((8, 128), F32),
+        ],
+        out_specs=[VMEM] * 4,
         compiler_params=pltpu.CompilerParams(**PARAMS),
         name="shares",
-    )(later, sums, events, plain, more, ordered)
+    )(state, handed, sums, events, plain, more, ordered)
 
 
 def hazard_kernel(rows, hazard, square, rank, cumulative, squares):
@@ -329,22 +349,21 @@
 
 
 def range_kernel(bit, count, *refs):
-    total, other, later = refs[:3]
-    total_out, later_out = refs[3 + count :]
+    state, other, out = refs[0], refs[1], refs[2 + count]
     is_later = (lax.axis_index("ex") & bit) == 0
-    later_out[...] = later[...] + jnp.where(is_later, other[...], 0.0)
-    total_out[...] = total[...] + other[...]
-
-
-def ranges(bit, total, other, later, waited):
+    out[0] = state[0] + other[0]
+    out[1] = state[1] + jnp.where(is_later, other[0], 0.0)
+
+
+def ranges(bit, state, other, waited):
     return pl.pallas_call(
         functools.partial(range_kernel, bit, len(waited)),
-        in_specs=[VMEM] * 3 + [pl.BlockSpec(memory_space=pl.ANY)] * len(waited),
-        out_shape=[jax.ShapeDtypeStruct(total.shape, F32)] * 2,
-        out_specs=[VMEM] * 2,
+        in_specs=[VMEM] * 2 + [pl.BlockSpec(memory_space=pl.ANY)] * len(waited),
+        out_shape=jax.ShapeDtypeStruct(state.shape, F32),
+        out_specs=VMEM,
         compiler_params=pltpu.CompilerParams(**PARAMS),
         name="ranges",
-    )(total, other, later, *waited)
+    )(state, other, *waited)
 
 
 def order_kernel(start, parts, own, other, *refs):
@@ -652,18 +671,19 @@
         for q in order
     ]
 
-    risk, sums, ordered_events, total = risks(paired, firsts, rank, event_row, table, rows)
-    later = jnp.zeros_like(total)
+    risk, sums, ordered_events, state = risks(paired, firsts, rank, event_row, table, rows)
     bit = 1
     while bit < ex:
-        total, later = ranges(bit, total, swap(total, "ex", bit), later, rests if bit == 1 else [])
+        state = ranges(bit, state, swap_odd(state, bit), rests if bit == 1 else [])
         bit *= 2
     tangent, one, plain = ordered_values(keep[0], received[0], firsts, risk, rank, table, 0, middle)
     more_tangent, two, more = ordered_values(
         keep[0], received[0], rests, risk, rank, table, middle, rows - middle
     )
     later_sums = suffix_sums(one, two, padded)
-    hazard, ordered_squares, message = shares(later, sums, ordered_events, plain, more, later_sums)
+    hazard, ordered_squares, message, total = shares(
+        state, hand_over(state), sums, ordered_events, plain, more, later_sums
+    )
     messages = [message] + [swap(message, "ex", i) for i in range(1, ex)]
     cumulative, squares = hazards(hazard, ordered_squares, rank, rows)
     summed = prefix_sums(later_sums, ordered_squares, rank, padded)

time: 55.9 us -> 58.4 us (1.045)
  waiting for transfers between devices: 13.8 us -> 16.4 us
    ppermute x26 -> x24, starting transfers between devices: 28 us -> 25 us  [swap(): return lax.ppermute(x, axis, [(s, s ^ i) for s in range(count)])]
    ppermute x0 -> x3, waiting for transfers between devices: none -> 2.92 us  [the longest x1 2.91 us: hand_over(): lax.ppermute(x, 'feat', [(f, f - 1) for f in range(1, lax.axis_size('feat...]
    ppermute x0 -> x3, starting transfers between devices: none -> 2.87 us  [the longest x1 1.56 us: hand_over(): lax.ppermute(x, 'feat', [(f, f - 1) for f in range(1, lax.axis_size('feat...]
    ppermute x26 -> x24, waiting for transfers between devices: 13.8 us -> 13.5 us  [swap(): return lax.ppermute(x, axis, [(s, s ^ i) for s in range(count)])]
  transfers between devices with their start and end apart: 26 -> 27, of which waited for: 10 -> 11; matrix products, arithmetic and copies ran while one was open for 0% -> 0% of each run, Pallas kernels for 16% -> 16%
where the time goes in v17:
time: 58.4 us; the launch traced here: 58.3 us
  starting transfers between devices  27.9 us (48%)
  waiting for transfers between devices  16.4 us (28%)
  Pallas kernels  13.8 us (24%)
    ppermute x24, starting transfers between devices, swap(): return lax.ppermute(x, axis, [(s, s ^ i) for s in range(count)])  25 us
    ppermute x24, waiting for transfers between devices, swap(): return lax.ppermute(x, axis, [(s, s ^ i) for s in range(count)])  13.5 us
    pallas_call x1, Pallas kernels, products(): pl.pallas_call(functools.partial(product_kernel, feat, kf, chunk), in_spe...  3.35 us
    ppermute x1, waiting for transfers between devices, hand_over(): lax.ppermute(x, 'feat', [(f, f - 1) for f in range(1, lax.axis_size('feat...  2.91 us
    pallas_call x2, Pallas kernels, ordered_values(): pl.pallas_call(functools.partial(order_kernel, start, len(messages)), in_...  1.98 us
    pallas_call x2, Pallas kernels, gradients(): pl.pallas_call(functools.partial(gradient_kernel, parts, kf), in_specs=[V...  1.76 us
    pallas_call x1, Pallas kernels, prefix_sums(): pl.pallas_call(prefix_kernel, in_specs=[VMEM] * 3, out_shape=jax.ShapeDty...  1.75 us
    ppermute x1, starting transfers between devices, hand_over(): lax.ppermute(x, 'feat', [(f, f - 1) for f in range(1, lax.axis_size('feat...  1.56 us
  transfers between devices with their start and end apart: 27, of which 11 were waited for; matrix products, arithmetic and copies ran while one was open for 0% of the time, Pallas kernels for 16%

profile of v17, /device:TPU:0, one launch (start us, length us, event | category | flops | bytes accessed | tf_op | source)
XLA Modules:
  0.0 58.3 jit_solution(1029209031596016283)
XLA Ops:
  0.0 3.3 %products.1 = (f32[16,256]{1,0:T(8,128)S(1)}, f32[16,4096]{1,0:T(8,128)S(1)}, f32[16,4096]{1,0:T(8,128)S(1)}, f32[16,4096]{1,0:T(8,128)S(1)}, f32[16,4096]{1,0:T...) custom-call(bf16[512,128]{1,0:T(8,128)(2,1)} %directions.1, ...), custom_call_target="tpu_custom_call" | custom-call | flops 536870912 | bytes 6291456 | tf_op jit(solution)/shard_map/products/pallas_call | solution.py:127
  5.3 3.9 %collective-permute-start.1 = (s16[16,2176]{1,0:T(8,128)(2,1)S(1)}, s16[16,2176]{1,0:T(8,128)(2,1)S(1)}, u32[]{:S(2)}, u32[]{:S(2)}) collective-permute-start(s16[16,2176]{1,0:T(8,128)(2,1)S(1)} %join.6), channel_id=1, source_target_pairs={{0,6},{1,7},{2,4},{3,5},{4,2},{5,3},{6,0},{7,1},{8,14},{9,15},{10,... | collective-permute-start | bytes 208904 | tf_op jit(solution)/shard_map/ppermute | solution.py:22
  10.3 2.9 %collective-permute-start.8 = (s16[16,2688]{1,0:T(8,128)(2,1)S(1)}, s16[16,2688]{1,0:T(8,128)(2,1)S(1)}, u32[]{:S(2)}, u32[]{:S(2)}) collective-permute-start(s16[16,2688]{1,0:T(8,128)(2,1)S(1)} %join.9), channel_id=1, source_target_pairs={{0,6},{1,7},{2,4},{3,5},{4,2},{5,3},{6,0},{7,1},{8,14},{9,15},{10,... | collective-permute-start | bytes 258056 | tf_op jit(solution)/shard_map/ppermute | solution.py:22
  14.3 0.9 %collective-permute-done.5.refs_2_ = s16[16,2176]{1,0:T(8,128)(2,1)S(1)} collective-permute-done((s16[16,2176]{1,0:T(8,128)(2,1)S(1)}, s16[16,2176]{1,0:T(8,128)(2,1)S(1)}, u32[]{:S(2)}, u32[]{:S(2)}) %collective-permute-start.5) | collective-permute-done | bytes 69664 | tf_op jit(solution)/shard_map/ppermute | solution.py:22
  15.1 0.9 %risks.1 = (f32[1,4096]{1,0:T(1,128)S(1)}, f32[16,256]{1,0:T(8,128)S(1)}, f32[16,256]{1,0:T(8,128)S(1)}, f32[2,8,128]{2,1,0:T(8,128)S(1)}) custom-call(f32[16,256]{1,0:T(8,128)S(1)} %pair.1.refs_0_.linear, s16[16,2176]{1,0:T(8,128)(2,1)S(1)} %collective-permute-done.1.refs_0_, s16[16,2176]{1,0:T(8,128)(2,1)S(1)} %collective-permute-done.3.refs_1_, ...), custom_call_target="tpu_custom_call" | custom-call | flops 134217728 | bytes 262144 | tf_op jit(solution)/shard_map/risks/pallas_call | solution.py:268
  16.7 1.2 %collective-permute-done.9.refs_3_.refs_1_ = s16[16,2688]{1,0:T(8,128)(2,1)S(1)} collective-permute-done((s16[16,2688]{1,0:T(8,128)(2,1)S(1)}, s16[16,2688]{1,0:T(8,128)(2,1)S(1)}, u32[]{:S(2)}, u32[]{:S(2)}) %collective-permute-start.9) | collective-permute-done | bytes 86048 | tf_op jit(solution)/shard_map/ppermute | solution.py:22
  20.2 1.6 %collective-permute-start.12 = (f32[2,8,128]{2,1,0:T(8,128)S(1)}, f32[2,8,128]{2,1,0:T(8,128)S(1)}, u32[]{:S(2)}, u32[]{:S(2)}) collective-permute-start(f32[2,8,128]{2,1,0:T(8,128)S(1)} %ranges.3.state), channel_id=1, source_target_pairs={{1,0},{3,2},{5,4},{7,6},{9,8},{11,10},{13,12},{15,14},{17,16},{19,... | collective-permute-start | bytes 24584 | tf_op jit(solution)/shard_map/ppermute | solution.py:32
  21.7 1.2 %ordered_values.3 = (f32[16,2560]{1,0:T(8,128)S(1)}, f32[256,256]{1,0:T(8,128)S(1)}, f32[16,128]{1,0:T(8,128)S(1)}) custom-call(f32[16,4096]{1,0:T(8,128)S(1)} %get-tuple-element.41.own, f32[16,4096]{1,0:T(8,128)S(1)} %collective-permute-done.7.refs_1_.other, s16[16,2688]{1,0:T(8,128)(2,1)S(1)} %collective-permute-done.8.refs_2_.refs_0_, ...), custom_call_target="tpu_custom_call" | custom-call | flops 671088640 | bytes 983040 | tf_op jit(solution)/shard_map/ordered_values/pallas_call | solution.py:405
  23.3 2.9 %collective-permute-done.12.handed = f32[2,8,128]{2,1,0:T(8,128)S(1)} collective-permute-done((f32[2,8,128]{2,1,0:T(8,128)S(1)}, f32[2,8,128]{2,1,0:T(8,128)S(1)}, u32[]{:S(2)}, u32[]{:S(2)}) %collective-permute-start.12) | collective-permute-done | bytes 8224 | tf_op jit(solution)/shard_map/ppermute | solution.py:32
  26.3 3.7 %collective-permute-start.15 = (f32[40,128]{1,0:T(8,128)S(1)}, f32[40,128]{1,0:T(8,128)S(1)}, u32[]{:S(2)}, u32[]{:S(2)}) collective-permute-start(f32[40,128]{1,0:T(8,128)S(1)} %get-tuple-element.47.refs_0_), channel_id=1, source_target_pairs={{0,24},{8,16},{16,8},{24,0},{1,25},{9,17},{17,9},{25,1},{2,26},{10... | collective-permute-start | bytes 61448 | tf_op jit(solution)/shard_map/ppermute | solution.py:22
  30.7 1.7 %prefix_sums.1.refs_6_ = f32[16,4096]{1,0:T(8,128)S(1)} custom-call(f32[256,256]{1,0:T(8,128)S(1)} %suffix_sums.1.ordered.sums, f32[16,256]{1,0:T(8,128)S(1)} %get-tuple-element.50.squares.square, s32[1,4096]{1,0:T(1,128)S(1)} %bitcast.6), custom_call_target="tpu_custom_call" | custom-call | flops 1073741824 | bytes 1572864 | tf_op jit(solution)/shard_map/prefix_sums/pallas_call | solution.py:471
  32.5 0.9 %hazards.1 = (f32[1,4096]{1,0:T(1,128)S(1)}, f32[1,4096]{1,0:T(1,128)S(1)}) custom-call(f32[16,256]{1,0:T(8,128)S(1)} %get-tuple-element.51.hazard, f32[16,256]{1,0:T(8,128)S(1)} %get-tuple-element.50.squares.square, s32[1,4096]{1,0:T(1,128)S(1)} %bitcast.7), custom_call_target="tpu_custom_call" | custom-call | flops 209715200 | bytes 262144 | tf_op jit(solution)/shard_map/hazards/pallas_call | solution.py:340
  33.4 1.3 %collective-permute-done.14.refs_2_ = f32[40,128]{1,0:T(8,128)S(1)} collective-permute-done((f32[40,128]{1,0:T(8,128)S(1)}, f32[40,128]{1,0:T(8,128)S(1)}, u32[]{:S(2)}, u32[]{:S(2)}) %collective-permute-start.14) | collective-permute-done | bytes 20512 | tf_op jit(solution)/shard_map/ppermute | solution.py:22
  34.9 2.2 %collective-permute-start.18 = (bf16[16,4096]{1,0:T(8,128)(2,1)S(1)}, bf16[16,4096]{1,0:T(8,128)(2,1)S(1)}, u32[]{:S(2)}, u32[]{:S(2)}) collective-permute-start(bf16[16,4096]{1,0:T(8,128)(2,1)S(1)} %weights.1.refs_0_), channel_id=1, source_target_pairs={{0,6},{1,7},{2,4},{3,5},{4,2},{5,3},{6,0},{7,1},{8,14},{9,15},{10,... | collective-permute-start | bytes 393224 | tf_op jit(solution)/shard_map/ppermute | solution.py:22
  38.4 3.1 %collective-permute-done.18.refs_3_ = bf16[16,4096]{1,0:T(8,128)(2,1)S(1)} collective-permute-done((bf16[16,4096]{1,0:T(8,128)(2,1)S(1)}, bf16[16,4096]{1,0:T(8,128)(2,1)S(1)}, u32[]{:S(2)}, u32[]{:S(2)}) %collective-permute-start.18) | collective-permute-done | bytes 131104 | tf_op jit(solution)/shard_map/ppermute | solution.py:22
  41.6 2.0 %collective-permute-done.17.refs_2_ = bf16[16,4096]{1,0:T(8,128)(2,1)S(1)} collective-permute-done((bf16[16,4096]{1,0:T(8,128)(2,1)S(1)}, bf16[16,4096]{1,0:T(8,128)(2,1)S(1)}, u32[]{:S(2)}, u32[]{:S(2)}) %collective-permute-start.17) | collective-permute-done | bytes 131104 | tf_op jit(solution)/shard_map/ppermute | solution.py:22
  44.1 0.9 %gradients.2.mine = s16[17,16,128]{2,1,0:T(8,128)(2,1)S(1)} custom-call(bf16[16,4096]{1,0:T(8,128)(2,1)S(1)} %weights.1.refs_0_, bf16[16,4096]{1,0:T(8,128)(2,1)S(1)} %collective-permute-done.16.refs_1_, bf16[16,4096]{1,0:T(8,128)(2,1)S(1)} %collective-permute-done.17.refs_2_, bf16[16,4096]{1,0:T(8,128)(2,1)S(1)} %collective-permute-done.18.refs_3_, ...), custom_call_target="tpu_custom_call" | custom-call | flops 268435456 | bytes 4718592 | tf_op jit(solution)/shard_map/gradients/pallas_call | solution.py:563
  45.0 1.0 %collective-permute-start.19 = (s16[17,16,128]{2,1,0:T(8,128)(2,1)S(1)}, s16[17,16,128]{2,1,0:T(8,128)(2,1)S(1)}, u32[]{:S(2)}, u32[]{:S(2)}) collective-permute-start(s16[17,16,128]{2,1,0:T(8,128)(2,1)S(1)} %gradients.2.mine), channel_id=1, source_target_pairs={{0,8},{8,0},{16,24},{24,16},{1,9},{9,1},{17,25},{25,17},{2,10},{10... | collective-permute-start | bytes 208904 | tf_op jit(solution)/shard_map/ppermute | solution.py:22
  46.9 1.2 %collective-permute-start.25 = (s16[17,16,128]{2,1,0:T(8,128)(2,1)S(1)}, s16[17,16,128]{2,1,0:T(8,128)(2,1)S(1)}, u32[]{:S(2)}, u32[]{:S(2)}) collective-permute-start(s16[17,16,128]{2,1,0:T(8,128)(2,1)S(1)} %gradients.3.mine), channel_id=1, source_target_pairs={{0,8},{8,0},{16,24},{24,16},{1,9},{9,1},{17,25},{25,17},{2,10},{10... | collective-permute-start | bytes 208904 | tf_op jit(solution)/shard_map/ppermute | solution.py:22
  48.0 1.3 %collective-permute-done.19.other = s16[17,16,128]{2,1,0:T(8,128)(2,1)S(1)} collective-permute-done((s16[17,16,128]{2,1,0:T(8,128)(2,1)S(1)}, s16[17,16,128]{2,1,0:T(8,128)(2,1)S(1)}, u32[]{:S(2)}, u32[]{:S(2)}) %collective-permute-start.19) | collective-permute-done | bytes 69664 | tf_op jit(solution)/shard_map/ppermute | solution.py:22
  49.4 1.9 %collective-permute-start.20 = (s16[17,16,128]{2,1,0:T(8,128)(2,1)S(1)}, s16[17,16,128]{2,1,0:T(8,128)(2,1)S(1)}, u32[]{:S(2)}, u32[]{:S(2)}) collective-permute-start(s16[17,16,128]{2,1,0:T(8,128)(2,1)S(1)} %merge.2.mine), channel_id=1, source_target_pairs={{0,16},{8,24},{16,0},{24,8},{1,17},{9,25},{17,1},{25,9},{2,18},{10... | collective-permute-start | bytes 208904 | tf_op jit(solution)/shard_map/ppermute | solution.py:22
  51.4 3.2 %collective-permute-start.26 = (s16[17,16,128]{2,1,0:T(8,128)(2,1)S(1)}, s16[17,16,128]{2,1,0:T(8,128)(2,1)S(1)}, u32[]{:S(2)}, u32[]{:S(2)}) collective-permute-start(s16[17,16,128]{2,1,0:T(8,128)(2,1)S(1)} %merge.3.mine), channel_id=1, source_target_pairs={{0,16},{8,24},{16,0},{24,8},{1,17},{9,25},{17,1},{25,9},{2,18},{10... | collective-permute-start | bytes 208904 | tf_op jit(solution)/shard_map/ppermute | solution.py:22
  54.5 2.1 %collective-permute-done.20.other = s16[17,16,128]{2,1,0:T(8,128)(2,1)S(1)} collective-permute-done((s16[17,16,128]{2,1,0:T(8,128)(2,1)S(1)}, s16[17,16,128]{2,1,0:T(8,128)(2,1)S(1)}, u32[]{:S(2)}, u32[]{:S(2)}) %collective-permute-start.20) | collective-permute-done | bytes 69664 | tf_op jit(solution)/shard_map/ppermute | solution.py:22
  57.4 0.9 %finish.1 = f32[512,128]{1,0:T(8,128)} custom-call(f32[64,512]{1,0:T(8,128)S(1)} %add.1.first, s16[17,16,128]{2,1,0:T(8,128)(2,1)S(1)} %merge.3.mine, s16[17,16,128]{2,1,0:T(8,128)(2,1)S(1)} %collective-permute-done.26.other, f32[8,128]{1,0:T(8,128)S(1)} %get-tuple-element.54.count), custom_call_target="tpu_custom_call" | custom-call | tf_op jit(solution)/shard_map/finish/pallas_call | solution.py:634
  (61 shorter events, 11.9 us)
Async XLA Ops:
  3.9 5.3 %collective-permute-start.2 = (f32[16,4096]{1,0:T(8,128)S(1)}, f32[16,4096]{1,0:T(8,128)S(1)}, u32[]{:S(2)}, u32[]{:S(2)}) collective-permute-start(f32[16,4096]{1,0:T(8,128)S(1)} %get-tuple-element.34), channel_id=1, source_target_pairs={{0,1},{1,0},{2,3},{3,2},{4,5},{5,4},{6,7},{7,6},{8,9},{9,8},{10,11... | collective-permute-start | bytes 786440 | tf_op jit(solution)/shard_map/ppermute | solution.py:22
  4.0 5.9 %collective-permute-start.4 = (f32[16,4096]{1,0:T(8,128)S(1)}, f32[16,4096]{1,0:T(8,128)S(1)}, u32[]{:S(2)}, u32[]{:S(2)}) collective-permute-start(f32[16,4096]{1,0:T(8,128)S(1)} %get-tuple-element.36), channel_id=1, source_target_pairs={{0,1},{1,0},{2,3},{3,2},{4,5},{5,4},{6,7},{7,6},{8,9},{9,8},{10,11... | collective-permute-start | bytes 786440 | tf_op jit(solution)/shard_map/ppermute | solution.py:22
  4.4 5.8 %collective-permute-start.7 = (f32[16,4096]{1,0:T(8,128)S(1)}, f32[16,4096]{1,0:T(8,128)S(1)}, u32[]{:S(2)}, u32[]{:S(2)}) collective-permute-start(f32[16,4096]{1,0:T(8,128)S(1)} %get-tuple-element.38), channel_id=1, source_target_pairs={{0,1},{1,0},{2,3},{3,2},{4,5},{5,4},{6,7},{7,6},{8,9},{9,8},{10,11... | collective-permute-start | bytes 786440 | tf_op jit(solution)/shard_map/ppermute | solution.py:22
  5.3 8.8 %collective-permute-start.1 = (s16[16,2176]{1,0:T(8,128)(2,1)S(1)}, s16[16,2176]{1,0:T(8,128)(2,1)S(1)}, u32[]{:S(2)}, u32[]{:S(2)}) collective-permute-start(s16[16,2176]{1,0:T(8,128)(2,1)S(1)} %join.6), channel_id=1, source_target_pairs={{0,6},{1,7},{2,4},{3,5},{4,2},{5,3},{6,0},{7,1},{8,14},{9,15},{10,... | collective-permute-start | bytes 208904 | tf_op jit(solution)/shard_map/ppermute | solution.py:22
  9.3 4.9 %collective-permute-start.3 = (s16[16,2176]{1,0:T(8,128)(2,1)S(1)}, s16[16,2176]{1,0:T(8,128)(2,1)S(1)}, u32[]{:S(2)}, u32[]{:S(2)}) collective-permute-start(s16[16,2176]{1,0:T(8,128)(2,1)S(1)} %join.7), channel_id=1, source_target_pairs={{0,4},{1,5},{2,6},{3,7},{4,0},{5,1},{6,2},{7,3},{8,12},{9,13},{10,... | collective-permute-start | bytes 208904 | tf_op jit(solution)/shard_map/ppermute | solution.py:22
  10.0 5.1 %collective-permute-start.5 = (s16[16,2176]{1,0:T(8,128)(2,1)S(1)}, s16[16,2176]{1,0:T(8,128)(2,1)S(1)}, u32[]{:S(2)}, u32[]{:S(2)}) collective-permute-start(s16[16,2176]{1,0:T(8,128)(2,1)S(1)} %join.8), channel_id=1, source_target_pairs={{0,2},{1,3},{2,0},{3,1},{4,6},{5,7},{6,4},{7,5},{8,10},{9,11},{10,... | collective-permute-start | bytes 208904 | tf_op jit(solution)/shard_map/ppermute | solution.py:22
  10.3 6.4 %collective-permute-start.8 = (s16[16,2688]{1,0:T(8,128)(2,1)S(1)}, s16[16,2688]{1,0:T(8,128)(2,1)S(1)}, u32[]{:S(2)}, u32[]{:S(2)}) collective-permute-start(s16[16,2688]{1,0:T(8,128)(2,1)S(1)} %join.9), channel_id=1, source_target_pairs={{0,6},{1,7},{2,4},{3,5},{4,2},{5,3},{6,0},{7,1},{8,14},{9,15},{10,... | collective-permute-start | bytes 258056 | tf_op jit(solution)/shard_map/ppermute | solution.py:22
  13.4 4.6 %collective-permute-start.9 = (s16[16,2688]{1,0:T(8,128)(2,1)S(1)}, s16[16,2688]{1,0:T(8,128)(2,1)S(1)}, u32[]{:S(2)}, u32[]{:S(2)}) collective-permute-start(s16[16,2688]{1,0:T(8,128)(2,1)S(1)} %join.10), channel_id=1, source_target_pairs={{0,4},{1,5},{2,6},{3,7},{4,0},{5,1},{6,2},{7,3},{8,12},{9,13},{10,... | collective-permute-start | bytes 258056 | tf_op jit(solution)/shard_map/ppermute | solution.py:22
  14.1 4.6 %collective-permute-start.10 = (s16[16,2688]{1,0:T(8,128)(2,1)S(1)}, s16[16,2688]{1,0:T(8,128)(2,1)S(1)}, u32[]{:S(2)}, u32[]{:S(2)}) collective-permute-start(s16[16,2688]{1,0:T(8,128)(2,1)S(1)} %join.11), channel_id=1, source_target_pairs={{0,2},{1,3},{2,0},{3,1},{4,6},{5,7},{6,4},{7,5},{8,10},{9,11},{10,... | collective-permute-start | bytes 258056 | tf_op jit(solution)/shard_map/ppermute | solution.py:22
  20.2 6.0 %collective-permute-start.12 = (f32[2,8,128]{2,1,0:T(8,128)S(1)}, f32[2,8,128]{2,1,0:T(8,128)S(1)}, u32[]{:S(2)}, u32[]{:S(2)}) collective-permute-start(f32[2,8,128]{2,1,0:T(8,128)S(1)} %ranges.3.state), channel_id=1, source_target_pairs={{1,0},{3,2},{5,4},{7,6},{9,8},{11,10},{13,12},{15,14},{17,16},{19,... | collective-permute-start | bytes 24584 | tf_op jit(solution)/shard_map/ppermute | solution.py:32
  26.3 7.1 %collective-permute-start.15 = (f32[40,128]{1,0:T(8,128)S(1)}, f32[40,128]{1,0:T(8,128)S(1)}, u32[]{:S(2)}, u32[]{:S(2)}) collective-permute-start(f32[40,128]{1,0:T(8,128)S(1)} %get-tuple-element.47.refs_0_), channel_id=1, source_target_pairs={{0,24},{8,16},{16,8},{24,0},{1,25},{9,17},{17,9},{25,1},{2,26},{10... | collective-permute-start | bytes 61448 | tf_op jit(solution)/shard_map/ppermute | solution.py:22
  30.0 4.7 %collective-permute-start.14 = (f32[40,128]{1,0:T(8,128)S(1)}, f32[40,128]{1,0:T(8,128)S(1)}, u32[]{:S(2)}, u32[]{:S(2)}) collective-permute-start(f32[40,128]{1,0:T(8,128)S(1)} %get-tuple-element.47.refs_0_), channel_id=1, source_target_pairs={{0,16},{8,24},{16,0},{24,8},{1,17},{9,25},{17,1},{25,9},{2,18},{10... | collective-permute-start | bytes 61448 | tf_op jit(solution)/shard_map/ppermute | solution.py:22
  30.0 4.7 %collective-permute-start.13 = (f32[40,128]{1,0:T(8,128)S(1)}, f32[40,128]{1,0:T(8,128)S(1)}, u32[]{:S(2)}, u32[]{:S(2)}) collective-permute-start(f32[40,128]{1,0:T(8,128)S(1)} %get-tuple-element.47.refs_0_), channel_id=1, source_target_pairs={{0,8},{8,0},{16,24},{24,16},{1,9},{9,1},{17,25},{25,17},{2,10},{10... | collective-permute-start | bytes 61448 | tf_op jit(solution)/shard_map/ppermute | solution.py:22
  34.9 6.7 %collective-permute-start.18 = (bf16[16,4096]{1,0:T(8,128)(2,1)S(1)}, bf16[16,4096]{1,0:T(8,128)(2,1)S(1)}, u32[]{:S(2)}, u32[]{:S(2)}) collective-permute-start(bf16[16,4096]{1,0:T(8,128)(2,1)S(1)} %weights.1.refs_0_), channel_id=1, source_target_pairs={{0,6},{1,7},{2,4},{3,5},{4,2},{5,3},{6,0},{7,1},{8,14},{9,15},{10,... | collective-permute-start | bytes 393224 | tf_op jit(solution)/shard_map/ppermute | solution.py:22
  37.1 6.5 %collective-permute-start.17 = (bf16[16,4096]{1,0:T(8,128)(2,1)S(1)}, bf16[16,4096]{1,0:T(8,128)(2,1)S(1)}, u32[]{:S(2)}, u32[]{:S(2)}) collective-permute-start(bf16[16,4096]{1,0:T(8,128)(2,1)S(1)} %weights.1.refs_0_), channel_id=1, source_target_pairs={{0,4},{1,5},{2,6},{3,7},{4,0},{5,1},{6,2},{7,3},{8,12},{9,13},{10,... | collective-permute-start | bytes 393224 | tf_op jit(solution)/shard_map/ppermute | solution.py:22
  37.7 5.9 %collective-permute-start.16 = (bf16[16,4096]{1,0:T(8,128)(2,1)S(1)}, bf16[16,4096]{1,0:T(8,128)(2,1)S(1)}, u32[]{:S(2)}, u32[]{:S(2)}) collective-permute-start(bf16[16,4096]{1,0:T(8,128)(2,1)S(1)} %weights.1.refs_0_), channel_id=1, source_target_pairs={{0,2},{1,3},{2,0},{3,1},{4,6},{5,7},{6,4},{7,5},{8,10},{9,11},{10,... | collective-permute-start | bytes 393224 | tf_op jit(solution)/shard_map/ppermute | solution.py:22
  38.4 7.5 %collective-permute-start.21 = (bf16[16,4096]{1,0:T(8,128)(2,1)S(1)}, bf16[16,4096]{1,0:T(8,128)(2,1)S(1)}, u32[]{:S(2)}, u32[]{:S(2)}) collective-permute-start(bf16[16,4096]{1,0:T(8,128)(2,1)S(1)} %weights.1.refs_0_), channel_id=1, source_target_pairs={{0,1},{1,0},{2,3},{3,2},{4,5},{5,4},{6,7},{7,6},{8,9},{9,8},{10,11... | collective-permute-start | bytes 393224 | tf_op jit(solution)/shard_map/ppermute | solution.py:22
  41.6 4.4 %collective-permute-start.24 = (bf16[16,4096]{1,0:T(8,128)(2,1)S(1)}, bf16[16,4096]{1,0:T(8,128)(2,1)S(1)}, u32[]{:S(2)}, u32[]{:S(2)}) collective-permute-start(bf16[16,4096]{1,0:T(8,128)(2,1)S(1)} %collective-permute-done.18.refs_3_), channel_id=1, source_target_pairs={{0,1},{1,0},{2,3},{3,2},{4,5},{5,4},{6,7},{7,6},{8,9},{9,8},{10,11... | collective-permute-start | bytes 393224 | tf_op jit(solution)/shard_map/ppermute | solution.py:22
  43.6 2.4 %collective-permute-start.23 = (bf16[16,4096]{1,0:T(8,128)(2,1)S(1)}, bf16[16,4096]{1,0:T(8,128)(2,1)S(1)}, u32[]{:S(2)}, u32[]{:S(2)}) collective-permute-start(bf16[16,4096]{1,0:T(8,128)(2,1)S(1)} %collective-permute-done.17.refs_2_), channel_id=1, source_target_pairs={{0,1},{1,0},{2,3},{3,2},{4,5},{5,4},{6,7},{7,6},{8,9},{9,8},{10,11... | collective-permute-start | bytes 393224 | tf_op jit(solution)/shard_map/ppermute | solution.py:22
  43.7 2.3 %collective-permute-start.22 = (bf16[16,4096]{1,0:T(8,128)(2,1)S(1)}, bf16[16,4096]{1,0:T(8,128)(2,1)S(1)}, u32[]{:S(2)}, u32[]{:S(2)}) collective-permute-start(bf16[16,4096]{1,0:T(8,128)(2,1)S(1)} %collective-permute-done.16.refs_1_), channel_id=1, source_target_pairs={{0,1},{1,0},{2,3},{3,2},{4,5},{5,4},{6,7},{7,6},{8,9},{9,8},{10,11... | collective-permute-start | bytes 393224 | tf_op jit(solution)/shard_map/ppermute | solution.py:22
  45.0 4.4 %collective-permute-start.19 = (s16[17,16,128]{2,1,0:T(8,128)(2,1)S(1)}, s16[17,16,128]{2,1,0:T(8,128)(2,1)S(1)}, u32[]{:S(2)}, u32[]{:S(2)}) collective-permute-start(s16[17,16,128]{2,1,0:T(8,128)(2,1)S(1)} %gradients.2.mine), channel_id=1, source_target_pairs={{0,8},{8,0},{16,24},{24,16},{1,9},{9,1},{17,25},{25,17},{2,10},{10... | collective-permute-start | bytes 208904 | tf_op jit(solution)/shard_map/ppermute | solution.py:22
  46.9 4.4 %collective-permute-start.25 = (s16[17,16,128]{2,1,0:T(8,128)(2,1)S(1)}, s16[17,16,128]{2,1,0:T(8,128)(2,1)S(1)}, u32[]{:S(2)}, u32[]{:S(2)}) collective-permute-start(s16[17,16,128]{2,1,0:T(8,128)(2,1)S(1)} %gradients.3.mine), channel_id=1, source_target_pairs={{0,8},{8,0},{16,24},{24,16},{1,9},{9,1},{17,25},{25,17},{2,10},{10... | collective-permute-start | bytes 208904 | tf_op jit(solution)/shard_map/ppermute | solution.py:22
  49.4 7.2 %collective-permute-start.20 = (s16[17,16,128]{2,1,0:T(8,128)(2,1)S(1)}, s16[17,16,128]{2,1,0:T(8,128)(2,1)S(1)}, u32[]{:S(2)}, u32[]{:S(2)}) collective-permute-start(s16[17,16,128]{2,1,0:T(8,128)(2,1)S(1)} %merge.2.mine), channel_id=1, source_target_pairs={{0,16},{8,24},{16,0},{24,8},{1,17},{9,25},{17,1},{25,9},{2,18},{10... | collective-permute-start | bytes 208904 | tf_op jit(solution)/shard_map/ppermute | solution.py:22
  51.4 6.0 %collective-permute-start.26 = (s16[17,16,128]{2,1,0:T(8,128)(2,1)S(1)}, s16[17,16,128]{2,1,0:T(8,128)(2,1)S(1)}, u32[]{:S(2)}, u32[]{:S(2)}) collective-permute-start(s16[17,16,128]{2,1,0:T(8,128)(2,1)S(1)} %merge.3.mine), channel_id=1, source_target_pairs={{0,16},{8,24},{16,0},{24,8},{1,17},{9,25},{17,1},{25,9},{2,18},{10... | collective-permute-start | bytes 208904 | tf_op jit(solution)/shard_map/ppermute | solution.py:22
  (6 other events, 43.0 us)

commit v18 on v16

--- a/solution.py
+++ b/solution.py
@@ -11,7 +11,7 @@
 BF16 = jnp.bfloat16
 LO = 256
 NT = (((1,), (1,)), ((), ()))
-SPAN = 512
+SPAN = 256
 VMEM = pl.BlockSpec(memory_space=pltpu.VMEM)
 HBM = pl.BlockSpec(memory_space=pltpu.HBM)
 PARAMS = dict(vmem_limit_bytes=24 * 1024 * 1024)
@@ -111,7 +111,7 @@
     persons, variants = dosages.shape
     k = directions.shape[1]
     kf = k // feat
-    chunk = min(1024, persons)
+    chunk = min(2048, persons)
     piece = jax.ShapeDtypeStruct((kf, persons), F32)
     first = jax.ShapeDtypeStruct((kf, persons + LO), F32)
     out = pl.pallas_call(
@@ -643,7 +643,7 @@
     received = {q: swap(send[q], "feat", 1) for q in order + [0]}
     table = tables(rank, linear, rows)
     paired = pair(linear, received[order[0]], table)
-    middle = min(3 * SPAN, rows // 2)
+    middle = min(5 * SPAN, rows // 2)
     firsts = [
         swap(join(keep[q], received[q], 0, middle, paired, []), "feat", 2 * q) for q in order
     ]

time: 55.9 us -> 56.3 us (level)
  waiting for transfers between devices: 13.8 us -> 15.2 us
  starting transfers between devices: 28 us -> 27 us
    ppermute x26, waiting for transfers between devices: 13.8 us -> 15.2 us  [swap(): return lax.ppermute(x, axis, [(s, s ^ i) for s in range(count)])]
    ppermute x26, starting transfers between devices: 28 us -> 27 us  [swap(): return lax.ppermute(x, axis, [(s, s ^ i) for s in range(count)])]
  transfers between devices with their start and end apart: 26 -> 26, of which waited for: 10 -> 11; matrix products, arithmetic and copies ran while one was open for 0% -> 0% of each run, Pallas kernels for 16% -> 16%
where the time goes in v18:
time: 56.3 us; the launch traced here: 56.2 us
  starting transfers between devices  27 us (48%)
  waiting for transfers between devices  15.2 us (27%)
  Pallas kernels  13.8 us (25%)
    ppermute x26, starting transfers between devices, swap(): return lax.ppermute(x, axis, [(s, s ^ i) for s in range(count)])  27 us
    ppermute x26, waiting for transfers between devices, swap(): return lax.ppermute(x, axis, [(s, s ^ i) for s in range(count)])  15.2 us
    pallas_call x1, Pallas kernels, products(): pl.pallas_call(functools.partial(product_kernel, feat, kf, chunk), in_spe...  3.39 us
    pallas_call x2, Pallas kernels, ordered_values(): pl.pallas_call(functools.partial(order_kernel, start, len(messages)), in_...  1.95 us
    pallas_call x2, Pallas kernels, gradients(): pl.pallas_call(functools.partial(gradient_kernel, parts, kf), in_specs=[V...  1.76 us
    pallas_call x1, Pallas kernels, prefix_sums(): pl.pallas_call(prefix_kernel, in_specs=[VMEM] * 3, out_shape=jax.ShapeDty...  1.75 us
  transfers between devices with their start and end apart: 26, of which 11 were waited for; matrix products, arithmetic and copies ran while one was open for 0% of the time, Pallas kernels for 16%

profile of v18, /device:TPU:0, one launch (start us, length us, event | category | flops | bytes accessed | tf_op | source)
XLA Modules:
  0.0 56.2 jit_solution(8896083373748687934)
XLA Ops:
  0.0 3.4 %products.1 = (f32[16,256]{1,0:T(8,128)S(1)}, f32[16,4096]{1,0:T(8,128)S(1)}, f32[16,4096]{1,0:T(8,128)S(1)}, f32[16,4096]{1,0:T(8,128)S(1)}, f32[16,4096]{1,0:T...) custom-call(bf16[512,128]{1,0:T(8,128)(2,1)} %directions.1, ...), custom_call_target="tpu_custom_call" | custom-call | flops 536870912 | bytes 6291456 | tf_op jit(solution)/shard_map/products/pallas_call | solution.py:117
  5.3 3.9 %collective-permute-start.1 = (s16[16,1920]{1,0:T(8,128)(2,1)S(1)}, s16[16,1920]{1,0:T(8,128)(2,1)S(1)}, u32[]{:S(2)}, u32[]{:S(2)}) collective-permute-start(s16[16,1920]{1,0:T(8,128)(2,1)S(1)} %join.6), channel_id=1, source_target_pairs={{0,6},{1,7},{2,4},{3,5},{4,2},{5,3},{6,0},{7,1},{8,14},{9,15},{10,... | collective-permute-start | bytes 184328 | tf_op jit(solution)/shard_map/ppermute | solution.py:22
  10.4 2.9 %collective-permute-start.8 = (s16[16,2944]{1,0:T(8,128)(2,1)S(1)}, s16[16,2944]{1,0:T(8,128)(2,1)S(1)}, u32[]{:S(2)}, u32[]{:S(2)}) collective-permute-start(s16[16,2944]{1,0:T(8,128)(2,1)S(1)} %join.9), channel_id=1, source_target_pairs={{0,6},{1,7},{2,4},{3,5},{4,2},{5,3},{6,0},{7,1},{8,14},{9,15},{10,... | collective-permute-start | bytes 282632 | tf_op jit(solution)/shard_map/ppermute | solution.py:22
  15.0 0.9 %risks.1 = (f32[1,4096]{1,0:T(1,128)S(1)}, f32[16,256]{1,0:T(8,128)S(1)}, f32[16,256]{1,0:T(8,128)S(1)}, f32[8,128]{1,0:T(8,128)S(1)}) custom-call(f32[16,256]{1,0:T(8,128)S(1)} %pair.1.refs_0_.linear, s16[16,1920]{1,0:T(8,128)(2,1)S(1)} %collective-permute-done.1.refs_0_, s16[16,1920]{1,0:T(8,128)(2,1)S(1)} %collective-permute-done.3.refs_1_, ...), custom_call_target="tpu_custom_call" | custom-call | flops 134217728 | bytes 262144 | tf_op jit(solution)/shard_map/risks/pallas_call | solution.py:257
  15.9 1.6 %collective-permute-start.6 = (f32[8,128]{1,0:T(8,128)S(1)}, f32[8,128]{1,0:T(8,128)S(1)}, u32[]{:S(2)}, u32[]{:S(2)}) collective-permute-start(f32[8,128]{1,0:T(8,128)S(1)} %get-tuple-element.40.refs_0_), channel_id=1, source_target_pairs={{0,8},{8,0},{16,24},{24,16},{1,9},{9,1},{17,25},{25,17},{2,10},{10... | collective-permute-start | bytes 12296 | tf_op jit(solution)/shard_map/ppermute | solution.py:22
  18.2 1.3 %collective-permute-done.6.refs_1_ = f32[8,128]{1,0:T(8,128)S(1)} collective-permute-done((f32[8,128]{1,0:T(8,128)S(1)}, f32[8,128]{1,0:T(8,128)S(1)}, u32[]{:S(2)}, u32[]{:S(2)}) %collective-permute-start.6) | collective-permute-done | bytes 4128 | tf_op jit(solution)/shard_map/ppermute | solution.py:22
  19.6 2.7 %collective-permute-start.11 = (f32[8,128]{1,0:T(8,128)S(1)}, f32[8,128]{1,0:T(8,128)S(1)}, u32[]{:S(2)}, u32[]{:S(2)}) collective-permute-start(f32[8,128]{1,0:T(8,128)S(1)} %get-tuple-element.42.refs_0_), channel_id=1, source_target_pairs={{0,16},{8,24},{16,0},{24,8},{1,17},{9,25},{17,1},{25,9},{2,18},{10... | collective-permute-start | bytes 12296 | tf_op jit(solution)/shard_map/ppermute | solution.py:22
  22.3 1.3 %ordered_values.3 = (f32[16,2816]{1,0:T(8,128)S(1)}, f32[256,256]{1,0:T(8,128)S(1)}, f32[16,128]{1,0:T(8,128)S(1)}) custom-call(f32[16,4096]{1,0:T(8,128)S(1)} %get-tuple-element.47.own, f32[16,4096]{1,0:T(8,128)S(1)} %collective-permute-done.7.refs_1_.other, s16[16,2944]{1,0:T(8,128)(2,1)S(1)} %collective-permute-done.8.refs_3_.refs_0_, ...), custom_call_target="tpu_custom_call" | custom-call | flops 738197504 | bytes 1081344 | tf_op jit(solution)/shard_map/ordered_values/pallas_call | solution.py:386
  24.4 3.6 %collective-permute-start.14 = (f32[40,128]{1,0:T(8,128)S(1)}, f32[40,128]{1,0:T(8,128)S(1)}, u32[]{:S(2)}, u32[]{:S(2)}) collective-permute-start(f32[40,128]{1,0:T(8,128)S(1)} %get-tuple-element.53.refs_0_), channel_id=1, source_target_pairs={{0,24},{8,16},{16,8},{24,0},{1,25},{9,17},{17,9},{25,1},{2,26},{10... | collective-permute-start | bytes 61448 | tf_op jit(solution)/shard_map/ppermute | solution.py:22
  28.8 1.7 %prefix_sums.1.refs_6_ = f32[16,4096]{1,0:T(8,128)S(1)} custom-call(f32[256,256]{1,0:T(8,128)S(1)} %suffix_sums.1.ordered.sums, f32[16,256]{1,0:T(8,128)S(1)} %get-tuple-element.56.squares.square, s32[1,4096]{1,0:T(1,128)S(1)} %bitcast.6), custom_call_target="tpu_custom_call" | custom-call | flops 1073741824 | bytes 1572864 | tf_op jit(solution)/shard_map/prefix_sums/pallas_call | solution.py:452
  30.5 0.9 %hazards.1 = (f32[1,4096]{1,0:T(1,128)S(1)}, f32[1,4096]{1,0:T(1,128)S(1)}) custom-call(f32[16,256]{1,0:T(8,128)S(1)} %get-tuple-element.57.hazard, f32[16,256]{1,0:T(8,128)S(1)} %get-tuple-element.56.squares.square, s32[1,4096]{1,0:T(1,128)S(1)} %bitcast.7), custom_call_target="tpu_custom_call" | custom-call | flops 209715200 | bytes 262144 | tf_op jit(solution)/shard_map/hazards/pallas_call | solution.py:320
  31.4 1.2 %collective-permute-done.13.refs_2_ = f32[40,128]{1,0:T(8,128)S(1)} collective-permute-done((f32[40,128]{1,0:T(8,128)S(1)}, f32[40,128]{1,0:T(8,128)S(1)}, u32[]{:S(2)}, u32[]{:S(2)}) %collective-permute-start.13) | collective-permute-done | bytes 20512 | tf_op jit(solution)/shard_map/ppermute | solution.py:22
  32.9 2.3 %collective-permute-start.17 = (bf16[16,4096]{1,0:T(8,128)(2,1)S(1)}, bf16[16,4096]{1,0:T(8,128)(2,1)S(1)}, u32[]{:S(2)}, u32[]{:S(2)}) collective-permute-start(bf16[16,4096]{1,0:T(8,128)(2,1)S(1)} %weights.1.refs_0_), channel_id=1, source_target_pairs={{0,6},{1,7},{2,4},{3,5},{4,2},{5,3},{6,0},{7,1},{8,14},{9,15},{10,... | collective-permute-start | bytes 393224 | tf_op jit(solution)/shard_map/ppermute | solution.py:22
  36.4 2.4 %collective-permute-done.17.refs_3_ = bf16[16,4096]{1,0:T(8,128)(2,1)S(1)} collective-permute-done((bf16[16,4096]{1,0:T(8,128)(2,1)S(1)}, bf16[16,4096]{1,0:T(8,128)(2,1)S(1)}, u32[]{:S(2)}, u32[]{:S(2)}) %collective-permute-start.17) | collective-permute-done | bytes 131104 | tf_op jit(solution)/shard_map/ppermute | solution.py:22
  38.8 1.4 %collective-permute-done.16.refs_2_ = bf16[16,4096]{1,0:T(8,128)(2,1)S(1)} collective-permute-done((bf16[16,4096]{1,0:T(8,128)(2,1)S(1)}, bf16[16,4096]{1,0:T(8,128)(2,1)S(1)}, u32[]{:S(2)}, u32[]{:S(2)}) %collective-permute-start.16) | collective-permute-done | bytes 131104 | tf_op jit(solution)/shard_map/ppermute | solution.py:22
  40.7 0.9 %gradients.2.mine = s16[17,16,128]{2,1,0:T(8,128)(2,1)S(1)} custom-call(bf16[16,4096]{1,0:T(8,128)(2,1)S(1)} %weights.1.refs_0_, bf16[16,4096]{1,0:T(8,128)(2,1)S(1)} %collective-permute-done.15.refs_1_, bf16[16,4096]{1,0:T(8,128)(2,1)S(1)} %collective-permute-done.16.refs_2_, bf16[16,4096]{1,0:T(8,128)(2,1)S(1)} %collective-permute-done.17.refs_3_, ...), custom_call_target="tpu_custom_call" | custom-call | flops 268435456 | bytes 4718592 | tf_op jit(solution)/shard_map/gradients/pallas_call | solution.py:544
  42.0 0.9 %gradients.3.mine = s16[17,16,128]{2,1,0:T(8,128)(2,1)S(1)} custom-call(bf16[16,4096]{1,0:T(8,128)(2,1)S(1)} %collective-permute-done.20.refs_0_, bf16[16,4096]{1,0:T(8,128)(2,1)S(1)} %collective-permute-done.21.refs_1_, bf16[16,4096]{1,0:T(8,128)(2,1)S(1)} %collective-permute-done.22.refs_2_, bf16[16,4096]{1,0:T(8,128)(2,1)S(1)} %collective-permute-done.23.refs_3_, ...), custom_call_target="tpu_custom_call" | custom-call | flops 268435456 | bytes 4718592 | tf_op jit(solution)/shard_map/gradients/pallas_call | solution.py:544
  42.8 1.8 %collective-permute-start.24 = (s16[17,16,128]{2,1,0:T(8,128)(2,1)S(1)}, s16[17,16,128]{2,1,0:T(8,128)(2,1)S(1)}, u32[]{:S(2)}, u32[]{:S(2)}) collective-permute-start(s16[17,16,128]{2,1,0:T(8,128)(2,1)S(1)} %gradients.3.mine), channel_id=1, source_target_pairs={{0,8},{8,0},{16,24},{24,16},{1,9},{9,1},{17,25},{25,17},{2,10},{10... | collective-permute-start | bytes 208904 | tf_op jit(solution)/shard_map/ppermute | solution.py:22
  44.7 2.0 %collective-permute-done.18.other = s16[17,16,128]{2,1,0:T(8,128)(2,1)S(1)} collective-permute-done((s16[17,16,128]{2,1,0:T(8,128)(2,1)S(1)}, s16[17,16,128]{2,1,0:T(8,128)(2,1)S(1)}, u32[]{:S(2)}, u32[]{:S(2)}) %collective-permute-start.18) | collective-permute-done | bytes 69664 | tf_op jit(solution)/shard_map/ppermute | solution.py:22
  46.7 1.6 %collective-permute-start.19 = (s16[17,16,128]{2,1,0:T(8,128)(2,1)S(1)}, s16[17,16,128]{2,1,0:T(8,128)(2,1)S(1)}, u32[]{:S(2)}, u32[]{:S(2)}) collective-permute-start(s16[17,16,128]{2,1,0:T(8,128)(2,1)S(1)} %merge.2.mine), channel_id=1, source_target_pairs={{0,16},{8,24},{16,0},{24,8},{1,17},{9,25},{17,1},{25,9},{2,18},{10... | collective-permute-start | bytes 208904 | tf_op jit(solution)/shard_map/ppermute | solution.py:22
  48.4 1.6 %collective-permute-start.25 = (s16[17,16,128]{2,1,0:T(8,128)(2,1)S(1)}, s16[17,16,128]{2,1,0:T(8,128)(2,1)S(1)}, u32[]{:S(2)}, u32[]{:S(2)}) collective-permute-start(s16[17,16,128]{2,1,0:T(8,128)(2,1)S(1)} %merge.3.mine), channel_id=1, source_target_pairs={{0,16},{8,24},{16,0},{24,8},{1,17},{9,25},{17,1},{25,9},{2,18},{10... | collective-permute-start | bytes 208904 | tf_op jit(solution)/shard_map/ppermute | solution.py:22
  50.0 4.3 %collective-permute-done.19.other = s16[17,16,128]{2,1,0:T(8,128)(2,1)S(1)} collective-permute-done((s16[17,16,128]{2,1,0:T(8,128)(2,1)S(1)}, s16[17,16,128]{2,1,0:T(8,128)(2,1)S(1)}, u32[]{:S(2)}, u32[]{:S(2)}) %collective-permute-start.19) | collective-permute-done | bytes 69664 | tf_op jit(solution)/shard_map/ppermute | solution.py:22
  54.3 1.0 %collective-permute-done.25.other = s16[17,16,128]{2,1,0:T(8,128)(2,1)S(1)} collective-permute-done((s16[17,16,128]{2,1,0:T(8,128)(2,1)S(1)}, s16[17,16,128]{2,1,0:T(8,128)(2,1)S(1)}, u32[]{:S(2)}, u32[]{:S(2)}) %collective-permute-start.25) | collective-permute-done | bytes 69664 | tf_op jit(solution)/shard_map/ppermute | solution.py:22
  55.3 0.9 %finish.1 = f32[512,128]{1,0:T(8,128)} custom-call(f32[64,512]{1,0:T(8,128)S(1)} %add.1.first, s16[17,16,128]{2,1,0:T(8,128)(2,1)S(1)} %merge.3.mine, s16[17,16,128]{2,1,0:T(8,128)(2,1)S(1)} %collective-permute-done.25.other, f32[8,128]{1,0:T(8,128)S(1)} %get-tuple-element.60.count), custom_call_target="tpu_custom_call" | custom-call | tf_op jit(solution)/shard_map/finish/pallas_call | solution.py:615
  (60 shorter events, 9.4 us)
Async XLA Ops:
  3.4 1.8 %collective-permute-start = (f32[16,4352]{1,0:T(8,128)S(1)}, f32[16,4352]{1,0:T(8,128)S(1)}, u32[]{:S(2)}, u32[]{:S(2)}) collective-permute-start(f32[16,4352]{1,0:T(8,128)S(1)} %get-tuple-element.34), channel_id=1, source_target_pairs={{0,1},{1,0},{2,3},{3,2},{4,5},{5,4},{6,7},{7,6},{8,9},{9,8},{10,11... | collective-permute-start | bytes 835592 | tf_op jit(solution)/shard_map/ppermute | solution.py:22
  3.9 5.3 %collective-permute-start.2 = (f32[16,4096]{1,0:T(8,128)S(1)}, f32[16,4096]{1,0:T(8,128)S(1)}, u32[]{:S(2)}, u32[]{:S(2)}) collective-permute-start(f32[16,4096]{1,0:T(8,128)S(1)} %get-tuple-element.37), channel_id=1, source_target_pairs={{0,1},{1,0},{2,3},{3,2},{4,5},{5,4},{6,7},{7,6},{8,9},{9,8},{10,11... | collective-permute-start | bytes 786440 | tf_op jit(solution)/shard_map/ppermute | solution.py:22
  4.0 5.9 %collective-permute-start.4 = (f32[16,4096]{1,0:T(8,128)S(1)}, f32[16,4096]{1,0:T(8,128)S(1)}, u32[]{:S(2)}, u32[]{:S(2)}) collective-permute-start(f32[16,4096]{1,0:T(8,128)S(1)} %get-tuple-element.39), channel_id=1, source_target_pairs={{0,1},{1,0},{2,3},{3,2},{4,5},{5,4},{6,7},{7,6},{8,9},{9,8},{10,11... | collective-permute-start | bytes 786440 | tf_op jit(solution)/shard_map/ppermute | solution.py:22
  4.4 5.8 %collective-permute-start.7 = (f32[16,4096]{1,0:T(8,128)S(1)}, f32[16,4096]{1,0:T(8,128)S(1)}, u32[]{:S(2)}, u32[]{:S(2)}) collective-permute-start(f32[16,4096]{1,0:T(8,128)S(1)} %get-tuple-element.41), channel_id=1, source_target_pairs={{0,1},{1,0},{2,3},{3,2},{4,5},{5,4},{6,7},{7,6},{8,9},{9,8},{10,11... | collective-permute-start | bytes 786440 | tf_op jit(solution)/shard_map/ppermute | solution.py:22
  5.3 8.9 %collective-permute-start.1 = (s16[16,1920]{1,0:T(8,128)(2,1)S(1)}, s16[16,1920]{1,0:T(8,128)(2,1)S(1)}, u32[]{:S(2)}, u32[]{:S(2)}) collective-permute-start(s16[16,1920]{1,0:T(8,128)(2,1)S(1)} %join.6), channel_id=1, source_target_pairs={{0,6},{1,7},{2,4},{3,5},{4,2},{5,3},{6,0},{7,1},{8,14},{9,15},{10,... | collective-permute-start | bytes 184328 | tf_op jit(solution)/shard_map/ppermute | solution.py:22
  9.4 5.0 %collective-permute-start.3 = (s16[16,1920]{1,0:T(8,128)(2,1)S(1)}, s16[16,1920]{1,0:T(8,128)(2,1)S(1)}, u32[]{:S(2)}, u32[]{:S(2)}) collective-permute-start(s16[16,1920]{1,0:T(8,128)(2,1)S(1)} %join.7), channel_id=1, source_target_pairs={{0,4},{1,5},{2,6},{3,7},{4,0},{5,1},{6,2},{7,3},{8,12},{9,13},{10,... | collective-permute-start | bytes 184328 | tf_op jit(solution)/shard_map/ppermute | solution.py:22
  10.1 4.9 %collective-permute-start.5 = (s16[16,1920]{1,0:T(8,128)(2,1)S(1)}, s16[16,1920]{1,0:T(8,128)(2,1)S(1)}, u32[]{:S(2)}, u32[]{:S(2)}) collective-permute-start(s16[16,1920]{1,0:T(8,128)(2,1)S(1)} %join.8), channel_id=1, source_target_pairs={{0,2},{1,3},{2,0},{3,1},{4,6},{5,7},{6,4},{7,5},{8,10},{9,11},{10,... | collective-permute-start | bytes 184328 | tf_op jit(solution)/shard_map/ppermute | solution.py:22
  10.4 9.2 %collective-permute-start.8 = (s16[16,2944]{1,0:T(8,128)(2,1)S(1)}, s16[16,2944]{1,0:T(8,128)(2,1)S(1)}, u32[]{:S(2)}, u32[]{:S(2)}) collective-permute-start(s16[16,2944]{1,0:T(8,128)(2,1)S(1)} %join.9), channel_id=1, source_target_pairs={{0,6},{1,7},{2,4},{3,5},{4,2},{5,3},{6,0},{7,1},{8,14},{9,15},{10,... | collective-permute-start | bytes 282632 | tf_op jit(solution)/shard_map/ppermute | solution.py:22
  13.5 6.1 %collective-permute-start.9 = (s16[16,2944]{1,0:T(8,128)(2,1)S(1)}, s16[16,2944]{1,0:T(8,128)(2,1)S(1)}, u32[]{:S(2)}, u32[]{:S(2)}) collective-permute-start(s16[16,2944]{1,0:T(8,128)(2,1)S(1)} %join.10), channel_id=1, source_target_pairs={{0,4},{1,5},{2,6},{3,7},{4,0},{5,1},{6,2},{7,3},{8,12},{9,13},{10,... | collective-permute-start | bytes 282632 | tf_op jit(solution)/shard_map/ppermute | solution.py:22
  14.2 5.4 %collective-permute-start.10 = (s16[16,2944]{1,0:T(8,128)(2,1)S(1)}, s16[16,2944]{1,0:T(8,128)(2,1)S(1)}, u32[]{:S(2)}, u32[]{:S(2)}) collective-permute-start(s16[16,2944]{1,0:T(8,128)(2,1)S(1)} %join.11), channel_id=1, source_target_pairs={{0,2},{1,3},{2,0},{3,1},{4,6},{5,7},{6,4},{7,5},{8,10},{9,11},{10,... | collective-permute-start | bytes 282632 | tf_op jit(solution)/shard_map/ppermute | solution.py:22
  15.9 3.7 %collective-permute-start.6 = (f32[8,128]{1,0:T(8,128)S(1)}, f32[8,128]{1,0:T(8,128)S(1)}, u32[]{:S(2)}, u32[]{:S(2)}) collective-permute-start(f32[8,128]{1,0:T(8,128)S(1)} %get-tuple-element.40.refs_0_), channel_id=1, source_target_pairs={{0,8},{8,0},{16,24},{24,16},{1,9},{9,1},{17,25},{25,17},{2,10},{10... | collective-permute-start | bytes 12296 | tf_op jit(solution)/shard_map/ppermute | solution.py:22
  19.6 4.6 %collective-permute-start.11 = (f32[8,128]{1,0:T(8,128)S(1)}, f32[8,128]{1,0:T(8,128)S(1)}, u32[]{:S(2)}, u32[]{:S(2)}) collective-permute-start(f32[8,128]{1,0:T(8,128)S(1)} %get-tuple-element.42.refs_0_), channel_id=1, source_target_pairs={{0,16},{8,24},{16,0},{24,8},{1,17},{9,25},{17,1},{25,9},{2,18},{10... | collective-permute-start | bytes 12296 | tf_op jit(solution)/shard_map/ppermute | solution.py:22
  24.4 7.1 %collective-permute-start.14 = (f32[40,128]{1,0:T(8,128)S(1)}, f32[40,128]{1,0:T(8,128)S(1)}, u32[]{:S(2)}, u32[]{:S(2)}) collective-permute-start(f32[40,128]{1,0:T(8,128)S(1)} %get-tuple-element.53.refs_0_), channel_id=1, source_target_pairs={{0,24},{8,16},{16,8},{24,0},{1,25},{9,17},{17,9},{25,1},{2,26},{10... | collective-permute-start | bytes 61448 | tf_op jit(solution)/shard_map/ppermute | solution.py:22
  28.0 4.7 %collective-permute-start.13 = (f32[40,128]{1,0:T(8,128)S(1)}, f32[40,128]{1,0:T(8,128)S(1)}, u32[]{:S(2)}, u32[]{:S(2)}) collective-permute-start(f32[40,128]{1,0:T(8,128)S(1)} %get-tuple-element.53.refs_0_), channel_id=1, source_target_pairs={{0,16},{8,24},{16,0},{24,8},{1,17},{9,25},{17,1},{25,9},{2,18},{10... | collective-permute-start | bytes 61448 | tf_op jit(solution)/shard_map/ppermute | solution.py:22
  28.0 4.7 %collective-permute-start.12 = (f32[40,128]{1,0:T(8,128)S(1)}, f32[40,128]{1,0:T(8,128)S(1)}, u32[]{:S(2)}, u32[]{:S(2)}) collective-permute-start(f32[40,128]{1,0:T(8,128)S(1)} %get-tuple-element.53.refs_0_), channel_id=1, source_target_pairs={{0,8},{8,0},{16,24},{24,16},{1,9},{9,1},{17,25},{25,17},{2,10},{10... | collective-permute-start | bytes 61448 | tf_op jit(solution)/shard_map/ppermute | solution.py:22
  32.9 5.9 %collective-permute-start.17 = (bf16[16,4096]{1,0:T(8,128)(2,1)S(1)}, bf16[16,4096]{1,0:T(8,128)(2,1)S(1)}, u32[]{:S(2)}, u32[]{:S(2)}) collective-permute-start(bf16[16,4096]{1,0:T(8,128)(2,1)S(1)} %weights.1.refs_0_), channel_id=1, source_target_pairs={{0,6},{1,7},{2,4},{3,5},{4,2},{5,3},{6,0},{7,1},{8,14},{9,15},{10,... | collective-permute-start | bytes 393224 | tf_op jit(solution)/shard_map/ppermute | solution.py:22
  35.1 5.1 %collective-permute-start.16 = (bf16[16,4096]{1,0:T(8,128)(2,1)S(1)}, bf16[16,4096]{1,0:T(8,128)(2,1)S(1)}, u32[]{:S(2)}, u32[]{:S(2)}) collective-permute-start(bf16[16,4096]{1,0:T(8,128)(2,1)S(1)} %weights.1.refs_0_), channel_id=1, source_target_pairs={{0,4},{1,5},{2,6},{3,7},{4,0},{5,1},{6,2},{7,3},{8,12},{9,13},{10,... | collective-permute-start | bytes 393224 | tf_op jit(solution)/shard_map/ppermute | solution.py:22
  35.6 5.0 %collective-permute-start.15 = (bf16[16,4096]{1,0:T(8,128)(2,1)S(1)}, bf16[16,4096]{1,0:T(8,128)(2,1)S(1)}, u32[]{:S(2)}, u32[]{:S(2)}) collective-permute-start(bf16[16,4096]{1,0:T(8,128)(2,1)S(1)} %weights.1.refs_0_), channel_id=1, source_target_pairs={{0,2},{1,3},{2,0},{3,1},{4,6},{5,7},{6,4},{7,5},{8,10},{9,11},{10,... | collective-permute-start | bytes 393224 | tf_op jit(solution)/shard_map/ppermute | solution.py:22
  36.4 5.3 %collective-permute-start.20 = (bf16[16,4096]{1,0:T(8,128)(2,1)S(1)}, bf16[16,4096]{1,0:T(8,128)(2,1)S(1)}, u32[]{:S(2)}, u32[]{:S(2)}) collective-permute-start(bf16[16,4096]{1,0:T(8,128)(2,1)S(1)} %weights.1.refs_0_), channel_id=1, source_target_pairs={{0,1},{1,0},{2,3},{3,2},{4,5},{5,4},{6,7},{7,6},{8,9},{9,8},{10,11... | collective-permute-start | bytes 393224 | tf_op jit(solution)/shard_map/ppermute | solution.py:22
  38.8 2.9 %collective-permute-start.23 = (bf16[16,4096]{1,0:T(8,128)(2,1)S(1)}, bf16[16,4096]{1,0:T(8,128)(2,1)S(1)}, u32[]{:S(2)}, u32[]{:S(2)}) collective-permute-start(bf16[16,4096]{1,0:T(8,128)(2,1)S(1)} %collective-permute-done.17.refs_3_), channel_id=1, source_target_pairs={{0,1},{1,0},{2,3},{3,2},{4,5},{5,4},{6,7},{7,6},{8,9},{9,8},{10,11... | collective-permute-start | bytes 393224 | tf_op jit(solution)/shard_map/ppermute | solution.py:22
  41.6 5.1 %collective-permute-start.18 = (s16[17,16,128]{2,1,0:T(8,128)(2,1)S(1)}, s16[17,16,128]{2,1,0:T(8,128)(2,1)S(1)}, u32[]{:S(2)}, u32[]{:S(2)}) collective-permute-start(s16[17,16,128]{2,1,0:T(8,128)(2,1)S(1)} %gradients.2.mine), channel_id=1, source_target_pairs={{0,8},{8,0},{16,24},{24,16},{1,9},{9,1},{17,25},{25,17},{2,10},{10... | collective-permute-start | bytes 208904 | tf_op jit(solution)/shard_map/ppermute | solution.py:22
  42.8 5.5 %collective-permute-start.24 = (s16[17,16,128]{2,1,0:T(8,128)(2,1)S(1)}, s16[17,16,128]{2,1,0:T(8,128)(2,1)S(1)}, u32[]{:S(2)}, u32[]{:S(2)}) collective-permute-start(s16[17,16,128]{2,1,0:T(8,128)(2,1)S(1)} %gradients.3.mine), channel_id=1, source_target_pairs={{0,8},{8,0},{16,24},{24,16},{1,9},{9,1},{17,25},{25,17},{2,10},{10... | collective-permute-start | bytes 208904 | tf_op jit(solution)/shard_map/ppermute | solution.py:22
  46.7 7.6 %collective-permute-start.19 = (s16[17,16,128]{2,1,0:T(8,128)(2,1)S(1)}, s16[17,16,128]{2,1,0:T(8,128)(2,1)S(1)}, u32[]{:S(2)}, u32[]{:S(2)}) collective-permute-start(s16[17,16,128]{2,1,0:T(8,128)(2,1)S(1)} %merge.2.mine), channel_id=1, source_target_pairs={{0,16},{8,24},{16,0},{24,8},{1,17},{9,25},{17,1},{25,9},{2,18},{10... | collective-permute-start | bytes 208904 | tf_op jit(solution)/shard_map/ppermute | solution.py:22
  48.4 6.9 %collective-permute-start.25 = (s16[17,16,128]{2,1,0:T(8,128)(2,1)S(1)}, s16[17,16,128]{2,1,0:T(8,128)(2,1)S(1)}, u32[]{:S(2)}, u32[]{:S(2)}) collective-permute-start(s16[17,16,128]{2,1,0:T(8,128)(2,1)S(1)} %merge.3.mine), channel_id=1, source_target_pairs={{0,16},{8,24},{16,0},{24,8},{1,17},{9,25},{17,1},{25,9},{2,18},{10... | collective-permute-start | bytes 208904 | tf_op jit(solution)/shard_map/ppermute | solution.py:22
  (5 other events, 38.9 us)

commit v19 on v16

--- a/solution.py
+++ b/solution.py
@@ -462,13 +462,14 @@
     )(sums, squares, rank)
 
 
-def weight_kernel(ex, *refs):
+def weight_kernel(places, *refs):
+    ex = len(places)
     messages, (first, rest, local, risk, cumulative, squares) = refs[:ex], refs[ex : ex + 6]
     weighted, placed = refs[ex + 6 :]
     kf = first.shape[0]
     me = lax.axis_index("ex")
-    for i in range(ex):
-        placed[me ^ i] = messages[i][...]
+    for i, part in zip(places, messages):
+        placed[me ^ i] = part[...]
     later = jnp.zeros((kf, 128), F32)
     own_later, before = later, later
     hazard_before = jnp.zeros((1, 128), F32)
@@ -489,10 +490,10 @@
         weighted[:, at] = (risk[:, at] * value).astype(BF16)
 
 
-def weights(messages, first, rest, local, risk, cumulative, squares):
+def weights(places, messages, first, rest, local, risk, cumulative, squares):
     ex = len(messages)
     return pl.pallas_call(
-        functools.partial(weight_kernel, ex),
+        functools.partial(weight_kernel, tuple(places)),
         in_specs=[VMEM] * (ex + 6),
         out_shape=jax.ShapeDtypeStruct(local.shape, BF16),
         out_specs=VMEM,
@@ -586,15 +587,15 @@
     )(mine, other)
 
 
-def finish_kernel(feat, kf, first, mine, other, count, out, placed, total, sems):
+def finish_kernel(feat, kf, ring, first, mine, other, count, out, placed, total, sems):
     me = lax.axis_index("feat")
     variants = out.shape[0]
     scale = count[1:2, 0:1]
-    for q in range(feat // 2):
-        placed[me ^ (2 * q)] = first[q * kf : (q + 1) * kf]
+    for j, q in enumerate(ring):
+        placed[me ^ (2 * q)] = first[j * kf : (j + 1) * kf]
     for i, value in enumerate(decode_sum(mine, other, variants // 128)):
-        for q in range(feat // 2):
-            placed[me ^ (2 * q + 1), :, i * 128 : (i + 1) * 128] = value[q * kf : (q + 1) * kf]
+        for j, q in enumerate(ring):
+            placed[me ^ (2 * q + 1), :, i * 128 : (i + 1) * 128] = value[j * kf : (j + 1) * kf]
     copies = []
     for i in range(variants // 128):
         at = slice(i * 128, (i + 1) * 128)
@@ -609,11 +610,12 @@
         copy.wait()
 
 
-def finish(first, mine, other, count, feat):
+def finish(first, mine, other, count, ring):
+    feat = 2 * len(ring)
     k, variants = 2 * first.shape[0], first.shape[1]
     kf = k // feat
     return pl.pallas_call(
-        functools.partial(finish_kernel, feat, kf),
+        functools.partial(finish_kernel, feat, kf, tuple(ring)),
         in_specs=[VMEM] * 4,
         out_shape=jax.ShapeDtypeStruct((variants, k), F32),
         out_specs=HBM,
@@ -664,16 +666,19 @@
     )
     later_sums = suffix_sums(one, two, padded)
     hazard, ordered_squares, message = shares(later, sums, ordered_events, plain, more, later_sums)
-    messages = [message] + [swap(message, "ex", i) for i in range(1, ex)]
+    places = list(range(ex))
+    places[-2:] = places[:-3:-1]
+    messages = [swap(message, "ex", i) if i else message for i in places]
     cumulative, squares = hazards(hazard, ordered_squares, rank, rows)
     summed = prefix_sums(later_sums, ordered_squares, rank, padded)
-    own = weights(messages, tangent, more_tangent, summed, risk, cumulative, squares)
+    own = weights(places, messages, tangent, more_tangent, summed, risk, cumulative, squares)
 
     chips = {0: own}
     for q in range(1, feat // 2):
         chips[q] = swap(own, "feat", 2 * q)
-    near = [chips[q] for q in range(feat // 2)]
-    far = [swap(chips[q], "feat", 1) for q in range(feat // 2)]
+    ring = [0] + list(reversed(range(1, feat // 2)))
+    near = [chips[q] for q in ring]
+    far = [swap(chips[q], "feat", 1) for q in ring]
     partial_sums = [gradients(pieces, dosages) for pieces in (near, far)]
     bit = 1
     while 2 * bit < ex:
@@ -682,7 +687,7 @@
         bit *= 2
     received = [swap(message, "ex", bit) for message in partial_sums]
     first = add(partial_sums[0], received[0], variants)
-    result = finish(first, partial_sums[1], received[1], total, feat)
+    result = finish(first, partial_sums[1], received[1], total, ring)
     if padded != each:
         result = result.reshape(variants, feat, padded)[:, :, :each].reshape(variants, k)
     return result

time: 55.9 us -> 57.2 us (1.023)
  waiting for transfers between devices: 13.8 us -> 16.2 us
  starting transfers between devices: 28 us -> 26.9 us
    ppermute x26, waiting for transfers between devices: 13.8 us -> 16.2 us  [swap(): return lax.ppermute(x, axis, [(s, s ^ i) for s in range(count)])]
    ppermute x26, starting transfers between devices: 28 us -> 26.9 us  [swap(): return lax.ppermute(x, axis, [(s, s ^ i) for s in range(count)])]
where the time goes in v19:
time: 57.2 us; the launch traced here: 57.1 us
  starting transfers between devices  26.9 us (47%)
  waiting for transfers between devices  16.2 us (28%)
  Pallas kernels  13.7 us (24%)
    ppermute x26, starting transfers between devices, swap(): return lax.ppermute(x, axis, [(s, s ^ i) for s in range(count)])  26.9 us
    ppermute x26, waiting for transfers between devices, swap(): return lax.ppermute(x, axis, [(s, s ^ i) for s in range(count)])  16.2 us
    pallas_call x1, Pallas kernels, products(): pl.pallas_call(functools.partial(product_kernel, feat, kf, chunk), in_spe...  3.35 us
    pallas_call x2, Pallas kernels, ordered_values(): pl.pallas_call(functools.partial(order_kernel, start, len(messages)), in_...  1.97 us
    pallas_call x2, Pallas kernels, gradients(): pl.pallas_call(functools.partial(gradient_kernel, parts, kf), in_specs=[V...  1.76 us
    pallas_call x1, Pallas kernels, prefix_sums(): pl.pallas_call(prefix_kernel, in_specs=[VMEM] * 3, out_shape=jax.ShapeDty...  1.75 us
  transfers between devices with their start and end apart: 26, of which 10 were waited for; matrix products, arithmetic and copies ran while one was open for 0% of the time, Pallas kernels for 16%

profile of v19, /device:TPU:0, one launch (start us, length us, event | category | flops | bytes accessed | tf_op | source)
XLA Modules:
  0.0 57.1 jit_solution(2228549948541325182)
XLA Ops:
  0.0 3.3 %products.1 = (f32[16,256]{1,0:T(8,128)S(1)}, f32[16,4096]{1,0:T(8,128)S(1)}, f32[16,4096]{1,0:T(8,128)S(1)}, f32[16,4096]{1,0:T(8,128)S(1)}, f32[16,4096]{1,0:T...) custom-call(bf16[512,128]{1,0:T(8,128)(2,1)} %directions.1, ...), custom_call_target="tpu_custom_call" | custom-call | flops 536870912 | bytes 6291456 | tf_op jit(solution)/shard_map/products/pallas_call | solution.py:117
  5.3 3.9 %collective-permute-start.1 = (s16[16,2176]{1,0:T(8,128)(2,1)S(1)}, s16[16,2176]{1,0:T(8,128)(2,1)S(1)}, u32[]{:S(2)}, u32[]{:S(2)}) collective-permute-start(s16[16,2176]{1,0:T(8,128)(2,1)S(1)} %join.6), channel_id=1, source_target_pairs={{0,6},{1,7},{2,4},{3,5},{4,2},{5,3},{6,0},{7,1},{8,14},{9,15},{10,... | collective-permute-start | bytes 208904 | tf_op jit(solution)/shard_map/ppermute | solution.py:22
  10.3 2.9 %collective-permute-start.8 = (s16[16,2688]{1,0:T(8,128)(2,1)S(1)}, s16[16,2688]{1,0:T(8,128)(2,1)S(1)}, u32[]{:S(2)}, u32[]{:S(2)}) collective-permute-start(s16[16,2688]{1,0:T(8,128)(2,1)S(1)} %join.9), channel_id=1, source_target_pairs={{0,6},{1,7},{2,4},{3,5},{4,2},{5,3},{6,0},{7,1},{8,14},{9,15},{10,... | collective-permute-start | bytes 258056 | tf_op jit(solution)/shard_map/ppermute | solution.py:22
  15.1 0.9 %risks.1 = (f32[1,4096]{1,0:T(1,128)S(1)}, f32[16,256]{1,0:T(8,128)S(1)}, f32[16,256]{1,0:T(8,128)S(1)}, f32[8,128]{1,0:T(8,128)S(1)}) custom-call(f32[16,256]{1,0:T(8,128)S(1)} %pair.1.refs_0_.linear, s16[16,2176]{1,0:T(8,128)(2,1)S(1)} %collective-permute-done.1.refs_0_, s16[16,2176]{1,0:T(8,128)(2,1)S(1)} %collective-permute-done.3.refs_1_, ...), custom_call_target="tpu_custom_call" | custom-call | flops 134217728 | bytes 262144 | tf_op jit(solution)/shard_map/risks/pallas_call | solution.py:257
  16.0 1.6 %collective-permute-start.6 = (f32[8,128]{1,0:T(8,128)S(1)}, f32[8,128]{1,0:T(8,128)S(1)}, u32[]{:S(2)}, u32[]{:S(2)}) collective-permute-start(f32[8,128]{1,0:T(8,128)S(1)} %get-tuple-element.40.refs_0_), channel_id=1, source_target_pairs={{0,8},{8,0},{16,24},{24,16},{1,9},{9,1},{17,25},{25,17},{2,10},{10... | collective-permute-start | bytes 12296 | tf_op jit(solution)/shard_map/ppermute | solution.py:22
  18.5 1.2 %collective-permute-done.6.refs_1_ = f32[8,128]{1,0:T(8,128)S(1)} collective-permute-done((f32[8,128]{1,0:T(8,128)S(1)}, f32[8,128]{1,0:T(8,128)S(1)}, u32[]{:S(2)}, u32[]{:S(2)}) %collective-permute-start.6) | collective-permute-done | bytes 4128 | tf_op jit(solution)/shard_map/ppermute | solution.py:22
  19.8 2.6 %collective-permute-start.11 = (f32[8,128]{1,0:T(8,128)S(1)}, f32[8,128]{1,0:T(8,128)S(1)}, u32[]{:S(2)}, u32[]{:S(2)}) collective-permute-start(f32[8,128]{1,0:T(8,128)S(1)} %get-tuple-element.42.refs_0_), channel_id=1, source_target_pairs={{0,16},{8,24},{16,0},{24,8},{1,17},{9,25},{17,1},{25,9},{2,18},{10... | collective-permute-start | bytes 12296 | tf_op jit(solution)/shard_map/ppermute | solution.py:22
  22.4 1.2 %ordered_values.3 = (f32[16,2560]{1,0:T(8,128)S(1)}, f32[256,256]{1,0:T(8,128)S(1)}, f32[16,128]{1,0:T(8,128)S(1)}) custom-call(f32[16,4096]{1,0:T(8,128)S(1)} %get-tuple-element.47.own, f32[16,4096]{1,0:T(8,128)S(1)} %collective-permute-done.7.refs_1_.other, s16[16,2688]{1,0:T(8,128)(2,1)S(1)} %collective-permute-done.8.refs_3_.refs_0_, ...), custom_call_target="tpu_custom_call" | custom-call | flops 671088640 | bytes 983040 | tf_op jit(solution)/shard_map/ordered_values/pallas_call | solution.py:386
  24.5 2.6 %collective-permute-start.14 = (f32[40,128]{1,0:T(8,128)S(1)}, f32[40,128]{1,0:T(8,128)S(1)}, u32[]{:S(2)}, u32[]{:S(2)}) collective-permute-start(f32[40,128]{1,0:T(8,128)S(1)} %get-tuple-element.53.refs_0_), channel_id=1, source_target_pairs={{0,16},{8,24},{16,0},{24,8},{1,17},{9,25},{17,1},{25,9},{2,18},{10... | collective-permute-start | bytes 61448 | tf_op jit(solution)/shard_map/ppermute | solution.py:22
  27.1 1.3 %collective-permute-start.13 = (f32[40,128]{1,0:T(8,128)S(1)}, f32[40,128]{1,0:T(8,128)S(1)}, u32[]{:S(2)}, u32[]{:S(2)}) collective-permute-start(f32[40,128]{1,0:T(8,128)S(1)} %get-tuple-element.53.refs_0_), channel_id=1, source_target_pairs={{0,24},{8,16},{16,8},{24,0},{1,25},{9,17},{17,9},{25,1},{2,26},{10... | collective-permute-start | bytes 61448 | tf_op jit(solution)/shard_map/ppermute | solution.py:22
  28.9 1.7 %prefix_sums.1.refs_6_ = f32[16,4096]{1,0:T(8,128)S(1)} custom-call(f32[256,256]{1,0:T(8,128)S(1)} %suffix_sums.1.ordered.sums, f32[16,256]{1,0:T(8,128)S(1)} %get-tuple-element.56.squares.square, s32[1,4096]{1,0:T(1,128)S(1)} %bitcast.6), custom_call_target="tpu_custom_call" | custom-call | flops 1073741824 | bytes 1572864 | tf_op jit(solution)/shard_map/prefix_sums/pallas_call | solution.py:452
  30.7 0.9 %hazards.1 = (f32[1,4096]{1,0:T(1,128)S(1)}, f32[1,4096]{1,0:T(1,128)S(1)}) custom-call(f32[16,256]{1,0:T(8,128)S(1)} %get-tuple-element.57.hazard, f32[16,256]{1,0:T(8,128)S(1)} %get-tuple-element.56.squares.square, s32[1,4096]{1,0:T(1,128)S(1)} %bitcast.7), custom_call_target="tpu_custom_call" | custom-call | flops 209715200 | bytes 262144 | tf_op jit(solution)/shard_map/hazards/pallas_call | solution.py:320
  31.6 1.1 %collective-permute-done.13.refs_2_ = f32[40,128]{1,0:T(8,128)S(1)} collective-permute-done((f32[40,128]{1,0:T(8,128)S(1)}, f32[40,128]{1,0:T(8,128)S(1)}, u32[]{:S(2)}, u32[]{:S(2)}) %collective-permute-start.13) | collective-permute-done | bytes 20512 | tf_op jit(solution)/shard_map/ppermute | solution.py:22
  32.9 1.1 %collective-permute-start.17 = (bf16[16,4096]{1,0:T(8,128)(2,1)S(1)}, bf16[16,4096]{1,0:T(8,128)(2,1)S(1)}, u32[]{:S(2)}, u32[]{:S(2)}) collective-permute-start(bf16[16,4096]{1,0:T(8,128)(2,1)S(1)} %weights.1.refs_0_), channel_id=1, source_target_pairs={{0,2},{1,3},{2,0},{3,1},{4,6},{5,7},{6,4},{7,5},{8,10},{9,11},{10,... | collective-permute-start | bytes 393224 | tf_op jit(solution)/shard_map/ppermute | solution.py:22
  34.0 1.5 %collective-permute-start.16 = (bf16[16,4096]{1,0:T(8,128)(2,1)S(1)}, bf16[16,4096]{1,0:T(8,128)(2,1)S(1)}, u32[]{:S(2)}, u32[]{:S(2)}) collective-permute-start(bf16[16,4096]{1,0:T(8,128)(2,1)S(1)} %weights.1.refs_0_), channel_id=1, source_target_pairs={{0,4},{1,5},{2,6},{3,7},{4,0},{5,1},{6,2},{7,3},{8,12},{9,13},{10,... | collective-permute-start | bytes 393224 | tf_op jit(solution)/shard_map/ppermute | solution.py:22
  35.5 0.9 %collective-permute-start.15 = (bf16[16,4096]{1,0:T(8,128)(2,1)S(1)}, bf16[16,4096]{1,0:T(8,128)(2,1)S(1)}, u32[]{:S(2)}, u32[]{:S(2)}) collective-permute-start(bf16[16,4096]{1,0:T(8,128)(2,1)S(1)} %weights.1.refs_0_), channel_id=1, source_target_pairs={{0,6},{1,7},{2,4},{3,5},{4,2},{5,3},{6,0},{7,1},{8,14},{9,15},{10,... | collective-permute-start | bytes 393224 | tf_op jit(solution)/shard_map/ppermute | solution.py:22
  36.4 1.5 %collective-permute-done.17.refs_3_ = bf16[16,4096]{1,0:T(8,128)(2,1)S(1)} collective-permute-done((bf16[16,4096]{1,0:T(8,128)(2,1)S(1)}, bf16[16,4096]{1,0:T(8,128)(2,1)S(1)}, u32[]{:S(2)}, u32[]{:S(2)}) %collective-permute-start.17) | collective-permute-done | bytes 131104 | tf_op jit(solution)/shard_map/ppermute | solution.py:22
  37.9 1.1 %collective-permute-done.16.refs_2_ = bf16[16,4096]{1,0:T(8,128)(2,1)S(1)} collective-permute-done((bf16[16,4096]{1,0:T(8,128)(2,1)S(1)}, bf16[16,4096]{1,0:T(8,128)(2,1)S(1)}, u32[]{:S(2)}, u32[]{:S(2)}) %collective-permute-start.16) | collective-permute-done | bytes 131104 | tf_op jit(solution)/shard_map/ppermute | solution.py:22
  39.0 2.4 %collective-permute-done.15.refs_1_ = bf16[16,4096]{1,0:T(8,128)(2,1)S(1)} collective-permute-done((bf16[16,4096]{1,0:T(8,128)(2,1)S(1)}, bf16[16,4096]{1,0:T(8,128)(2,1)S(1)}, u32[]{:S(2)}, u32[]{:S(2)}) %collective-permute-start.15) | collective-permute-done | bytes 131104 | tf_op jit(solution)/shard_map/ppermute | solution.py:22
  43.7 1.6 %collective-permute-start.24 = (s16[17,16,128]{2,1,0:T(8,128)(2,1)S(1)}, s16[17,16,128]{2,1,0:T(8,128)(2,1)S(1)}, u32[]{:S(2)}, u32[]{:S(2)}) collective-permute-start(s16[17,16,128]{2,1,0:T(8,128)(2,1)S(1)} %gradients.3.mine), channel_id=1, source_target_pairs={{0,8},{8,0},{16,24},{24,16},{1,9},{9,1},{17,25},{25,17},{2,10},{10... | collective-permute-start | bytes 208904 | tf_op jit(solution)/shard_map/ppermute | solution.py:22
  45.3 2.0 %collective-permute-done.18.other = s16[17,16,128]{2,1,0:T(8,128)(2,1)S(1)} collective-permute-done((s16[17,16,128]{2,1,0:T(8,128)(2,1)S(1)}, s16[17,16,128]{2,1,0:T(8,128)(2,1)S(1)}, u32[]{:S(2)}, u32[]{:S(2)}) %collective-permute-start.18) | collective-permute-done | bytes 69664 | tf_op jit(solution)/shard_map/ppermute | solution.py:22
  47.4 1.2 %collective-permute-start.19 = (s16[17,16,128]{2,1,0:T(8,128)(2,1)S(1)}, s16[17,16,128]{2,1,0:T(8,128)(2,1)S(1)}, u32[]{:S(2)}, u32[]{:S(2)}) collective-permute-start(s16[17,16,128]{2,1,0:T(8,128)(2,1)S(1)} %merge.2.mine), channel_id=1, source_target_pairs={{0,16},{8,24},{16,0},{24,8},{1,17},{9,25},{17,1},{25,9},{2,18},{10... | collective-permute-start | bytes 208904 | tf_op jit(solution)/shard_map/ppermute | solution.py:22
  48.6 1.9 %collective-permute-start.25 = (s16[17,16,128]{2,1,0:T(8,128)(2,1)S(1)}, s16[17,16,128]{2,1,0:T(8,128)(2,1)S(1)}, u32[]{:S(2)}, u32[]{:S(2)}) collective-permute-start(s16[17,16,128]{2,1,0:T(8,128)(2,1)S(1)} %merge.3.mine), channel_id=1, source_target_pairs={{0,16},{8,24},{16,0},{24,8},{1,17},{9,25},{17,1},{25,9},{2,18},{10... | collective-permute-start | bytes 208904 | tf_op jit(solution)/shard_map/ppermute | solution.py:22
  50.5 4.7 %collective-permute-done.19.other = s16[17,16,128]{2,1,0:T(8,128)(2,1)S(1)} collective-permute-done((s16[17,16,128]{2,1,0:T(8,128)(2,1)S(1)}, s16[17,16,128]{2,1,0:T(8,128)(2,1)S(1)}, u32[]{:S(2)}, u32[]{:S(2)}) %collective-permute-start.19) | collective-permute-done | bytes 69664 | tf_op jit(solution)/shard_map/ppermute | solution.py:22
  (60 shorter events, 11.5 us)
Async XLA Ops:
  3.9 5.3 %collective-permute-start.2 = (f32[16,4096]{1,0:T(8,128)S(1)}, f32[16,4096]{1,0:T(8,128)S(1)}, u32[]{:S(2)}, u32[]{:S(2)}) collective-permute-start(f32[16,4096]{1,0:T(8,128)S(1)} %get-tuple-element.37), channel_id=1, source_target_pairs={{0,1},{1,0},{2,3},{3,2},{4,5},{5,4},{6,7},{7,6},{8,9},{9,8},{10,11... | collective-permute-start | bytes 786440 | tf_op jit(solution)/shard_map/ppermute | solution.py:22
  4.0 5.9 %collective-permute-start.4 = (f32[16,4096]{1,0:T(8,128)S(1)}, f32[16,4096]{1,0:T(8,128)S(1)}, u32[]{:S(2)}, u32[]{:S(2)}) collective-permute-start(f32[16,4096]{1,0:T(8,128)S(1)} %get-tuple-element.39), channel_id=1, source_target_pairs={{0,1},{1,0},{2,3},{3,2},{4,5},{5,4},{6,7},{7,6},{8,9},{9,8},{10,11... | collective-permute-start | bytes 786440 | tf_op jit(solution)/shard_map/ppermute | solution.py:22
  4.4 5.8 %collective-permute-start.7 = (f32[16,4096]{1,0:T(8,128)S(1)}, f32[16,4096]{1,0:T(8,128)S(1)}, u32[]{:S(2)}, u32[]{:S(2)}) collective-permute-start(f32[16,4096]{1,0:T(8,128)S(1)} %get-tuple-element.41), channel_id=1, source_target_pairs={{0,1},{1,0},{2,3},{3,2},{4,5},{5,4},{6,7},{7,6},{8,9},{9,8},{10,11... | collective-permute-start | bytes 786440 | tf_op jit(solution)/shard_map/ppermute | solution.py:22
  5.3 8.8 %collective-permute-start.1 = (s16[16,2176]{1,0:T(8,128)(2,1)S(1)}, s16[16,2176]{1,0:T(8,128)(2,1)S(1)}, u32[]{:S(2)}, u32[]{:S(2)}) collective-permute-start(s16[16,2176]{1,0:T(8,128)(2,1)S(1)} %join.6), channel_id=1, source_target_pairs={{0,6},{1,7},{2,4},{3,5},{4,2},{5,3},{6,0},{7,1},{8,14},{9,15},{10,... | collective-permute-start | bytes 208904 | tf_op jit(solution)/shard_map/ppermute | solution.py:22
  9.3 4.9 %collective-permute-start.3 = (s16[16,2176]{1,0:T(8,128)(2,1)S(1)}, s16[16,2176]{1,0:T(8,128)(2,1)S(1)}, u32[]{:S(2)}, u32[]{:S(2)}) collective-permute-start(s16[16,2176]{1,0:T(8,128)(2,1)S(1)} %join.7), channel_id=1, source_target_pairs={{0,4},{1,5},{2,6},{3,7},{4,0},{5,1},{6,2},{7,3},{8,12},{9,13},{10,... | collective-permute-start | bytes 208904 | tf_op jit(solution)/shard_map/ppermute | solution.py:22
  10.0 5.1 %collective-permute-start.5 = (s16[16,2176]{1,0:T(8,128)(2,1)S(1)}, s16[16,2176]{1,0:T(8,128)(2,1)S(1)}, u32[]{:S(2)}, u32[]{:S(2)}) collective-permute-start(s16[16,2176]{1,0:T(8,128)(2,1)S(1)} %join.8), channel_id=1, source_target_pairs={{0,2},{1,3},{2,0},{3,1},{4,6},{5,7},{6,4},{7,5},{8,10},{9,11},{10,... | collective-permute-start | bytes 208904 | tf_op jit(solution)/shard_map/ppermute | solution.py:22
  10.3 9.4 %collective-permute-start.8 = (s16[16,2688]{1,0:T(8,128)(2,1)S(1)}, s16[16,2688]{1,0:T(8,128)(2,1)S(1)}, u32[]{:S(2)}, u32[]{:S(2)}) collective-permute-start(s16[16,2688]{1,0:T(8,128)(2,1)S(1)} %join.9), channel_id=1, source_target_pairs={{0,6},{1,7},{2,4},{3,5},{4,2},{5,3},{6,0},{7,1},{8,14},{9,15},{10,... | collective-permute-start | bytes 258056 | tf_op jit(solution)/shard_map/ppermute | solution.py:22
  13.4 6.3 %collective-permute-start.9 = (s16[16,2688]{1,0:T(8,128)(2,1)S(1)}, s16[16,2688]{1,0:T(8,128)(2,1)S(1)}, u32[]{:S(2)}, u32[]{:S(2)}) collective-permute-start(s16[16,2688]{1,0:T(8,128)(2,1)S(1)} %join.10), channel_id=1, source_target_pairs={{0,4},{1,5},{2,6},{3,7},{4,0},{5,1},{6,2},{7,3},{8,12},{9,13},{10,... | collective-permute-start | bytes 258056 | tf_op jit(solution)/shard_map/ppermute | solution.py:22
  14.1 5.6 %collective-permute-start.10 = (s16[16,2688]{1,0:T(8,128)(2,1)S(1)}, s16[16,2688]{1,0:T(8,128)(2,1)S(1)}, u32[]{:S(2)}, u32[]{:S(2)}) collective-permute-start(s16[16,2688]{1,0:T(8,128)(2,1)S(1)} %join.11), channel_id=1, source_target_pairs={{0,2},{1,3},{2,0},{3,1},{4,6},{5,7},{6,4},{7,5},{8,10},{9,11},{10,... | collective-permute-start | bytes 258056 | tf_op jit(solution)/shard_map/ppermute | solution.py:22
  16.0 3.7 %collective-permute-start.6 = (f32[8,128]{1,0:T(8,128)S(1)}, f32[8,128]{1,0:T(8,128)S(1)}, u32[]{:S(2)}, u32[]{:S(2)}) collective-permute-start(f32[8,128]{1,0:T(8,128)S(1)} %get-tuple-element.40.refs_0_), channel_id=1, source_target_pairs={{0,8},{8,0},{16,24},{24,16},{1,9},{9,1},{17,25},{25,17},{2,10},{10... | collective-permute-start | bytes 12296 | tf_op jit(solution)/shard_map/ppermute | solution.py:22
  19.8 4.6 %collective-permute-start.11 = (f32[8,128]{1,0:T(8,128)S(1)}, f32[8,128]{1,0:T(8,128)S(1)}, u32[]{:S(2)}, u32[]{:S(2)}) collective-permute-start(f32[8,128]{1,0:T(8,128)S(1)} %get-tuple-element.42.refs_0_), channel_id=1, source_target_pairs={{0,16},{8,24},{16,0},{24,8},{1,17},{9,25},{17,1},{25,9},{2,18},{10... | collective-permute-start | bytes 12296 | tf_op jit(solution)/shard_map/ppermute | solution.py:22
  24.5 7.1 %collective-permute-start.14 = (f32[40,128]{1,0:T(8,128)S(1)}, f32[40,128]{1,0:T(8,128)S(1)}, u32[]{:S(2)}, u32[]{:S(2)}) collective-permute-start(f32[40,128]{1,0:T(8,128)S(1)} %get-tuple-element.53.refs_0_), channel_id=1, source_target_pairs={{0,16},{8,24},{16,0},{24,8},{1,17},{9,25},{17,1},{25,9},{2,18},{10... | collective-permute-start | bytes 61448 | tf_op jit(solution)/shard_map/ppermute | solution.py:22
  27.1 5.6 %collective-permute-start.13 = (f32[40,128]{1,0:T(8,128)S(1)}, f32[40,128]{1,0:T(8,128)S(1)}, u32[]{:S(2)}, u32[]{:S(2)}) collective-permute-start(f32[40,128]{1,0:T(8,128)S(1)} %get-tuple-element.53.refs_0_), channel_id=1, source_target_pairs={{0,24},{8,16},{16,8},{24,0},{1,25},{9,17},{17,9},{25,1},{2,26},{10... | collective-permute-start | bytes 61448 | tf_op jit(solution)/shard_map/ppermute | solution.py:22
  28.4 4.2 %collective-permute-start.12 = (f32[40,128]{1,0:T(8,128)S(1)}, f32[40,128]{1,0:T(8,128)S(1)}, u32[]{:S(2)}, u32[]{:S(2)}) collective-permute-start(f32[40,128]{1,0:T(8,128)S(1)} %get-tuple-element.53.refs_0_), channel_id=1, source_target_pairs={{0,8},{8,0},{16,24},{24,16},{1,9},{9,1},{17,25},{25,17},{2,10},{10... | collective-permute-start | bytes 61448 | tf_op jit(solution)/shard_map/ppermute | solution.py:22
  32.9 5.0 %collective-permute-start.17 = (bf16[16,4096]{1,0:T(8,128)(2,1)S(1)}, bf16[16,4096]{1,0:T(8,128)(2,1)S(1)}, u32[]{:S(2)}, u32[]{:S(2)}) collective-permute-start(bf16[16,4096]{1,0:T(8,128)(2,1)S(1)} %weights.1.refs_0_), channel_id=1, source_target_pairs={{0,2},{1,3},{2,0},{3,1},{4,6},{5,7},{6,4},{7,5},{8,10},{9,11},{10,... | collective-permute-start | bytes 393224 | tf_op jit(solution)/shard_map/ppermute | solution.py:22
  34.0 5.0 %collective-permute-start.16 = (bf16[16,4096]{1,0:T(8,128)(2,1)S(1)}, bf16[16,4096]{1,0:T(8,128)(2,1)S(1)}, u32[]{:S(2)}, u32[]{:S(2)}) collective-permute-start(bf16[16,4096]{1,0:T(8,128)(2,1)S(1)} %weights.1.refs_0_), channel_id=1, source_target_pairs={{0,4},{1,5},{2,6},{3,7},{4,0},{5,1},{6,2},{7,3},{8,12},{9,13},{10,... | collective-permute-start | bytes 393224 | tf_op jit(solution)/shard_map/ppermute | solution.py:22
  35.5 5.9 %collective-permute-start.15 = (bf16[16,4096]{1,0:T(8,128)(2,1)S(1)}, bf16[16,4096]{1,0:T(8,128)(2,1)S(1)}, u32[]{:S(2)}, u32[]{:S(2)}) collective-permute-start(bf16[16,4096]{1,0:T(8,128)(2,1)S(1)} %weights.1.refs_0_), channel_id=1, source_target_pairs={{0,6},{1,7},{2,4},{3,5},{4,2},{5,3},{6,0},{7,1},{8,14},{9,15},{10,... | collective-permute-start | bytes 393224 | tf_op jit(solution)/shard_map/ppermute | solution.py:22
  36.4 6.4 %collective-permute-start.20 = (bf16[16,4096]{1,0:T(8,128)(2,1)S(1)}, bf16[16,4096]{1,0:T(8,128)(2,1)S(1)}, u32[]{:S(2)}, u32[]{:S(2)}) collective-permute-start(bf16[16,4096]{1,0:T(8,128)(2,1)S(1)} %weights.1.refs_0_), channel_id=1, source_target_pairs={{0,1},{1,0},{2,3},{3,2},{4,5},{5,4},{6,7},{7,6},{8,9},{9,8},{10,11... | collective-permute-start | bytes 393224 | tf_op jit(solution)/shard_map/ppermute | solution.py:22
  37.9 4.9 %collective-permute-start.23 = (bf16[16,4096]{1,0:T(8,128)(2,1)S(1)}, bf16[16,4096]{1,0:T(8,128)(2,1)S(1)}, u32[]{:S(2)}, u32[]{:S(2)}) collective-permute-start(bf16[16,4096]{1,0:T(8,128)(2,1)S(1)} %collective-permute-done.17.refs_3_), channel_id=1, source_target_pairs={{0,1},{1,0},{2,3},{3,2},{4,5},{5,4},{6,7},{7,6},{8,9},{9,8},{10,11... | collective-permute-start | bytes 393224 | tf_op jit(solution)/shard_map/ppermute | solution.py:22
  38.9 3.9 %collective-permute-start.22 = (bf16[16,4096]{1,0:T(8,128)(2,1)S(1)}, bf16[16,4096]{1,0:T(8,128)(2,1)S(1)}, u32[]{:S(2)}, u32[]{:S(2)}) collective-permute-start(bf16[16,4096]{1,0:T(8,128)(2,1)S(1)} %collective-permute-done.16.refs_2_), channel_id=1, source_target_pairs={{0,1},{1,0},{2,3},{3,2},{4,5},{5,4},{6,7},{7,6},{8,9},{9,8},{10,11... | collective-permute-start | bytes 393224 | tf_op jit(solution)/shard_map/ppermute | solution.py:22
  42.3 5.0 %collective-permute-start.18 = (s16[17,16,128]{2,1,0:T(8,128)(2,1)S(1)}, s16[17,16,128]{2,1,0:T(8,128)(2,1)S(1)}, u32[]{:S(2)}, u32[]{:S(2)}) collective-permute-start(s16[17,16,128]{2,1,0:T(8,128)(2,1)S(1)} %gradients.2.mine), channel_id=1, source_target_pairs={{0,8},{8,0},{16,24},{24,16},{1,9},{9,1},{17,25},{25,17},{2,10},{10... | collective-permute-start | bytes 208904 | tf_op jit(solution)/shard_map/ppermute | solution.py:22
  43.7 4.8 %collective-permute-start.24 = (s16[17,16,128]{2,1,0:T(8,128)(2,1)S(1)}, s16[17,16,128]{2,1,0:T(8,128)(2,1)S(1)}, u32[]{:S(2)}, u32[]{:S(2)}) collective-permute-start(s16[17,16,128]{2,1,0:T(8,128)(2,1)S(1)} %gradients.3.mine), channel_id=1, source_target_pairs={{0,8},{8,0},{16,24},{24,16},{1,9},{9,1},{17,25},{25,17},{2,10},{10... | collective-permute-start | bytes 208904 | tf_op jit(solution)/shard_map/ppermute | solution.py:22
  47.4 7.9 %collective-permute-start.19 = (s16[17,16,128]{2,1,0:T(8,128)(2,1)S(1)}, s16[17,16,128]{2,1,0:T(8,128)(2,1)S(1)}, u32[]{:S(2)}, u32[]{:S(2)}) collective-permute-start(s16[17,16,128]{2,1,0:T(8,128)(2,1)S(1)} %merge.2.mine), channel_id=1, source_target_pairs={{0,16},{8,24},{16,0},{24,8},{1,17},{9,25},{17,1},{25,9},{2,18},{10... | collective-permute-start | bytes 208904 | tf_op jit(solution)/shard_map/ppermute | solution.py:22
  48.6 7.5 %collective-permute-start.25 = (s16[17,16,128]{2,1,0:T(8,128)(2,1)S(1)}, s16[17,16,128]{2,1,0:T(8,128)(2,1)S(1)}, u32[]{:S(2)}, u32[]{:S(2)}) collective-permute-start(s16[17,16,128]{2,1,0:T(8,128)(2,1)S(1)} %merge.3.mine), channel_id=1, source_target_pairs={{0,16},{8,24},{16,0},{24,8},{1,17},{9,25},{17,1},{25,9},{2,18},{10... | collective-permute-start | bytes 208904 | tf_op jit(solution)/shard_map/ppermute | solution.py:22
  (5 other events, 40.0 us)

commit v20 on v16

--- a/solution.py
+++ b/solution.py
@@ -224,8 +224,8 @@
 
 
 def risk_kernel(rows, parts, linear, *refs):
-    messages, (rank, events, table) = refs[:parts], refs[parts : parts + 3]
-    risk_out, sums_out, events_out, message = refs[-4:]
+    messages, events = refs[:parts], refs[parts]
+    risk_out, message = refs[parts + 1 :]
     groups = rows // LO
     total = linear[...]
     for part in messages:
@@ -233,41 +233,52 @@
         power = from_short(part[:, end:])[:, 127:]
         high, low = from_short(part[:, end - 2 * LO : end - LO]), from_short(part[:, end - LO : end])
         total = total + (high + low * (1.0 / 32768.0)) * jnp.exp2(power)
-    risk = jnp.exp(total)
+    risk = jnp.exp(total[:groups])
     for g in range(groups):
         risk_out[:, g * LO : (g + 1) * LO] = risk[g : g + 1]
+    everything = jnp.sum(jnp.sum(risk, axis=0, keepdims=True), axis=1, keepdims=True)
+    count = jnp.sum(events[...].astype(F32), axis=1, keepdims=True)
+    totals = [jnp.broadcast_to(value, (1, 128)) for value in (everything, count)]
+    message[...] = jnp.concatenate(totals + [jnp.zeros((6, 128), F32)], axis=0)
+
+
+def risks(linear, messages, events, rows):
+    return pl.pallas_call(
+        functools.partial(risk_kernel, rows, len(messages)),
+        in_specs=[VMEM] * (len(messages) + 2),
+        out_shape=[jax.ShapeDtypeStruct((1, rows), F32), jax.ShapeDtypeStruct((8, 128), F32)],
+        out_specs=[VMEM] * 2,
+        compiler_params=pltpu.CompilerParams(**PARAMS),
+        cost_estimate=pl.CostEstimate(flops=rows * 64, bytes_accessed=rows * 64, transcendentals=rows),
+        name="risks",
+    )(linear, *messages, events)
+
+
+def risk_sum_kernel(rows, risk, rank, events, table, sums_out, events_out):
+    groups = rows // LO
     mask = one_hot(lax.rem(rank[...], rows) // LO, groups, F32)
-    pieces = [mask * part for part in split_three(risk_out[...])] + [mask * events[...].astype(F32)]
+    pieces = [mask * part for part in split_three(risk[...])] + [mask * events[...].astype(F32)]
     lhs = jnp.concatenate(pieces, axis=0).astype(BF16)
     sorted_all = jnp.dot(lhs, table[...], preferred_element_type=F32)
     ordered = sorted_all[:groups] + sorted_all[groups : 2 * groups] + sorted_all[2 * groups : 3 * groups]
-    happened = sorted_all[3 * groups :]
     inside = dot_binary(ordered, triangle(LO, lambda a, b: a >= b))
     totals = jnp.broadcast_to(inside[:, :1], inside.shape)
     carried = binary_dot(triangle(groups, lambda a, b: a < b), totals)
     sums_out[...] = inside + carried
-    events_out[...] = happened
-    everything = jnp.sum(totals, axis=0, keepdims=True)[:, :128]
-    count = jnp.sum(dot_binary(happened, jnp.ones((LO, 128), F32)), axis=0, keepdims=True)
-    message[...] = jnp.concatenate([everything, count, jnp.zeros((6, 128), F32)], axis=0)
-
-
-def risks(linear, messages, rank, events, table, rows):
-    groups = rows // LO
-    return pl.pallas_call(
-        functools.partial(risk_kernel, rows, len(messages)),
-        in_specs=[VMEM] * (len(messages) + 4),
-        out_shape=[
-            jax.ShapeDtypeStruct((1, rows), F32),
-            jax.ShapeDtypeStruct((groups, LO), F32),
-            jax.ShapeDtypeStruct((groups, LO), F32),
-            jax.ShapeDtypeStruct((8, 128), F32),
-        ],
-        out_specs=[VMEM] * 4,
-        compiler_params=pltpu.CompilerParams(**PARAMS),
-        cost_estimate=pl.CostEstimate(flops=rows * LO * 128, bytes_accessed=rows * 64, transcendentals=rows),
-        name="risks",
-    )(linear, *messages, rank, events, table)
+    events_out[...] = sorted_all[3 * groups :]
+
+
+def risk_sums(risk, rank, events, table, rows):
+    flat = jax.ShapeDtypeStruct((rows // LO, LO), F32)
+    return pl.pallas_call(
+        functools.partial(risk_sum_kernel, rows),
+        in_specs=[VMEM] * 4,
+        out_shape=[flat, flat],
+        out_specs=[VMEM] * 2,
+        compiler_params=pltpu.CompilerParams(**PARAMS),
+        cost_estimate=pl.CostEstimate(flops=rows * LO * 128, bytes_accessed=rows * 64, transcendentals=0),
+        name="risk_sums",
+    )(risk, rank, events, table)
 
 
 def share_kernel(later, sums, events, plain, more, ordered, hazard_out, squares, message):
@@ -652,11 +663,12 @@
         for q in order
     ]
 
-    risk, sums, ordered_events, total = risks(paired, firsts, rank, event_row, table, rows)
+    risk, total = risks(paired, firsts, event_row, rows)
+    sums, ordered_events = risk_sums(risk, rank, event_row, table, rows)
     later = jnp.zeros_like(total)
     bit = 1
     while bit < ex:
-        total, later = ranges(bit, total, swap(total, "ex", bit), later, rests if bit == 1 else [])
+        total, later = ranges(bit, total, swap(total, "ex", bit), later, rests + [sums] if bit == 1 else [])
         bit *= 2
     tangent, one, plain = ordered_values(keep[0], received[0], firsts, risk, rank, table, 0, middle)
     more_tangent, two, more = ordered_values(

time: 55.9 us -> 55.1 us (0.986)
  waiting for transfers between devices: 13.8 us -> 12.8 us
    ppermute x26, waiting for transfers between devices: 13.8 us -> 12.8 us  [swap(): return lax.ppermute(x, axis, [(s, s ^ i) for s in range(count)])]
    pallas_call x0 -> x1, Pallas kernels: none -> 0.79 us  [risk_sums(): pl.pallas_call(functools.partial(risk_sum_kernel, rows), in_specs=[VMEM]...]
    pallas_call x1, Pallas kernels: 0.9 us -> 0.18 us  [risks(): pl.pallas_call(functools.partial(risk_kernel, rows, len(messages)), in_sp...]
  transfers between devices with their start and end apart: 26 -> 26, of which waited for: 10 -> 10; matrix products, arithmetic and copies ran while one was open for 0% -> 0% of each run, Pallas kernels for 16% -> 17%
where the time goes in v20:
time: 55.1 us; the launch traced here: 55 us
  starting transfers between devices  28.1 us (51%)
  Pallas kernels  13.8 us (25%)
  waiting for transfers between devices  12.8 us (23%)
    ppermute x26, starting transfers between devices, swap(): return lax.ppermute(x, axis, [(s, s ^ i) for s in range(count)])  28.1 us
    ppermute x26, waiting for transfers between devices, swap(): return lax.ppermute(x, axis, [(s, s ^ i) for s in range(count)])  12.8 us
    pallas_call x1, Pallas kernels, products(): pl.pallas_call(functools.partial(product_kernel, feat, kf, chunk), in_spe...  3.35 us
    pallas_call x2, Pallas kernels, ordered_values(): pl.pallas_call(functools.partial(order_kernel, start, len(messages)), in_...  1.97 us
    pallas_call x2, Pallas kernels, gradients(): pl.pallas_call(functools.partial(gradient_kernel, parts, kf), in_specs=[V...  1.76 us
    pallas_call x1, Pallas kernels, prefix_sums(): pl.pallas_call(prefix_kernel, in_specs=[VMEM] * 3, out_shape=jax.ShapeDty...  1.75 us
  transfers between devices with their start and end apart: 26, of which 10 were waited for; matrix products, arithmetic and copies ran while one was open for 0% of the time, Pallas kernels for 17%

profile of v20, /device:TPU:0, one launch (start us, length us, event | category | flops | bytes accessed | tf_op | source)
XLA Modules:
  0.0 55.0 jit_solution(6423218044932740347)
XLA Ops:
  0.0 3.3 %products.1 = (f32[16,256]{1,0:T(8,128)S(1)}, f32[16,4096]{1,0:T(8,128)S(1)}, f32[16,4096]{1,0:T(8,128)S(1)}, f32[16,4096]{1,0:T(8,128)S(1)}, f32[16,4096]{1,0:T...) custom-call(bf16[512,128]{1,0:T(8,128)(2,1)} %directions.1, ...), custom_call_target="tpu_custom_call" | custom-call | flops 536870912 | bytes 6291456 | tf_op jit(solution)/shard_map/products/pallas_call | solution.py:117
  5.3 3.9 %collective-permute-start.1 = (s16[16,2176]{1,0:T(8,128)(2,1)S(1)}, s16[16,2176]{1,0:T(8,128)(2,1)S(1)}, u32[]{:S(2)}, u32[]{:S(2)}) collective-permute-start(s16[16,2176]{1,0:T(8,128)(2,1)S(1)} %join.6), channel_id=1, source_target_pairs={{0,6},{1,7},{2,4},{3,5},{4,2},{5,3},{6,0},{7,1},{8,14},{9,15},{10,... | collective-permute-start | bytes 208904 | tf_op jit(solution)/shard_map/ppermute | solution.py:22
  10.3 2.9 %collective-permute-start.8 = (s16[16,2688]{1,0:T(8,128)(2,1)S(1)}, s16[16,2688]{1,0:T(8,128)(2,1)S(1)}, u32[]{:S(2)}, u32[]{:S(2)}) collective-permute-start(s16[16,2688]{1,0:T(8,128)(2,1)S(1)} %join.9), channel_id=1, source_target_pairs={{0,6},{1,7},{2,4},{3,5},{4,2},{5,3},{6,0},{7,1},{8,14},{9,15},{10,... | collective-permute-start | bytes 258056 | tf_op jit(solution)/shard_map/ppermute | solution.py:22
  14.3 0.9 %collective-permute-done.5.refs_2_ = s16[16,2176]{1,0:T(8,128)(2,1)S(1)} collective-permute-done((s16[16,2176]{1,0:T(8,128)(2,1)S(1)}, s16[16,2176]{1,0:T(8,128)(2,1)S(1)}, u32[]{:S(2)}, u32[]{:S(2)}) %collective-permute-start.5) | collective-permute-done | bytes 69664 | tf_op jit(solution)/shard_map/ppermute | solution.py:22
  15.3 1.6 %collective-permute-start.6 = (f32[8,128]{1,0:T(8,128)S(1)}, f32[8,128]{1,0:T(8,128)S(1)}, u32[]{:S(2)}, u32[]{:S(2)}) collective-permute-start(f32[8,128]{1,0:T(8,128)S(1)} %get-tuple-element.40.refs_0_), channel_id=1, source_target_pairs={{0,8},{8,0},{16,24},{24,16},{1,9},{9,1},{17,25},{25,17},{2,10},{10... | collective-permute-start | bytes 12296 | tf_op jit(solution)/shard_map/ppermute | solution.py:22
  19.0 2.7 %collective-permute-start.11 = (f32[8,128]{1,0:T(8,128)S(1)}, f32[8,128]{1,0:T(8,128)S(1)}, u32[]{:S(2)}, u32[]{:S(2)}) collective-permute-start(f32[8,128]{1,0:T(8,128)S(1)} %get-tuple-element.44.refs_0_), channel_id=1, source_target_pairs={{0,16},{8,24},{16,0},{24,8},{1,17},{9,25},{17,1},{25,9},{2,18},{10... | collective-permute-start | bytes 12296 | tf_op jit(solution)/shard_map/ppermute | solution.py:22
  21.6 1.2 %ordered_values.3 = (f32[16,2560]{1,0:T(8,128)S(1)}, f32[256,256]{1,0:T(8,128)S(1)}, f32[16,128]{1,0:T(8,128)S(1)}) custom-call(f32[16,4096]{1,0:T(8,128)S(1)} %get-tuple-element.48.own, f32[16,4096]{1,0:T(8,128)S(1)} %collective-permute-done.7.refs_1_.other, s16[16,2688]{1,0:T(8,128)(2,1)S(1)} %collective-permute-done.8.refs_3_.refs_0_, ...), custom_call_target="tpu_custom_call" | custom-call | flops 671088640 | bytes 983040 | tf_op jit(solution)/shard_map/ordered_values/pallas_call | solution.py:397
  23.7 3.7 %collective-permute-start.14 = (f32[40,128]{1,0:T(8,128)S(1)}, f32[40,128]{1,0:T(8,128)S(1)}, u32[]{:S(2)}, u32[]{:S(2)}) collective-permute-start(f32[40,128]{1,0:T(8,128)S(1)} %get-tuple-element.53.refs_0_), channel_id=1, source_target_pairs={{0,24},{8,16},{16,8},{24,0},{1,25},{9,17},{17,9},{25,1},{2,26},{10... | collective-permute-start | bytes 61448 | tf_op jit(solution)/shard_map/ppermute | solution.py:22
  28.1 1.7 %prefix_sums.1.refs_6_ = f32[16,4096]{1,0:T(8,128)S(1)} custom-call(f32[256,256]{1,0:T(8,128)S(1)} %suffix_sums.1.ordered.sums, f32[16,256]{1,0:T(8,128)S(1)} %get-tuple-element.56.squares.square, s32[1,4096]{1,0:T(1,128)S(1)} %bitcast.6), custom_call_target="tpu_custom_call" | custom-call | flops 1073741824 | bytes 1572864 | tf_op jit(solution)/shard_map/prefix_sums/pallas_call | solution.py:463
  29.9 0.9 %hazards.1 = (f32[1,4096]{1,0:T(1,128)S(1)}, f32[1,4096]{1,0:T(1,128)S(1)}) custom-call(f32[16,256]{1,0:T(8,128)S(1)} %get-tuple-element.57.hazard, f32[16,256]{1,0:T(8,128)S(1)} %get-tuple-element.56.squares.square, s32[1,4096]{1,0:T(1,128)S(1)} %bitcast.7), custom_call_target="tpu_custom_call" | custom-call | flops 209715200 | bytes 262144 | tf_op jit(solution)/shard_map/hazards/pallas_call | solution.py:331
  30.8 1.3 %collective-permute-done.13.refs_2_ = f32[40,128]{1,0:T(8,128)S(1)} collective-permute-done((f32[40,128]{1,0:T(8,128)S(1)}, f32[40,128]{1,0:T(8,128)S(1)}, u32[]{:S(2)}, u32[]{:S(2)}) %collective-permute-start.13) | collective-permute-done | bytes 20512 | tf_op jit(solution)/shard_map/ppermute | solution.py:22
  32.3 2.0 %collective-permute-start.17 = (bf16[16,4096]{1,0:T(8,128)(2,1)S(1)}, bf16[16,4096]{1,0:T(8,128)(2,1)S(1)}, u32[]{:S(2)}, u32[]{:S(2)}) collective-permute-start(bf16[16,4096]{1,0:T(8,128)(2,1)S(1)} %weights.1.refs_0_), channel_id=1, source_target_pairs={{0,6},{1,7},{2,4},{3,5},{4,2},{5,3},{6,0},{7,1},{8,14},{9,15},{10,... | collective-permute-start | bytes 393224 | tf_op jit(solution)/shard_map/ppermute | solution.py:22
  34.8 1.0 %collective-permute-start.15 = (bf16[16,4096]{1,0:T(8,128)(2,1)S(1)}, bf16[16,4096]{1,0:T(8,128)(2,1)S(1)}, u32[]{:S(2)}, u32[]{:S(2)}) collective-permute-start(bf16[16,4096]{1,0:T(8,128)(2,1)S(1)} %weights.1.refs_0_), channel_id=1, source_target_pairs={{0,2},{1,3},{2,0},{3,1},{4,6},{5,7},{6,4},{7,5},{8,10},{9,11},{10,... | collective-permute-start | bytes 393224 | tf_op jit(solution)/shard_map/ppermute | solution.py:22
  35.8 2.4 %collective-permute-done.17.refs_3_ = bf16[16,4096]{1,0:T(8,128)(2,1)S(1)} collective-permute-done((bf16[16,4096]{1,0:T(8,128)(2,1)S(1)}, bf16[16,4096]{1,0:T(8,128)(2,1)S(1)}, u32[]{:S(2)}, u32[]{:S(2)}) %collective-permute-start.17) | collective-permute-done | bytes 131104 | tf_op jit(solution)/shard_map/ppermute | solution.py:22
  38.2 1.4 %collective-permute-done.16.refs_2_ = bf16[16,4096]{1,0:T(8,128)(2,1)S(1)} collective-permute-done((bf16[16,4096]{1,0:T(8,128)(2,1)S(1)}, bf16[16,4096]{1,0:T(8,128)(2,1)S(1)}, u32[]{:S(2)}, u32[]{:S(2)}) %collective-permute-start.16) | collective-permute-done | bytes 131104 | tf_op jit(solution)/shard_map/ppermute | solution.py:22
  40.1 0.9 %gradients.2.mine = s16[17,16,128]{2,1,0:T(8,128)(2,1)S(1)} custom-call(bf16[16,4096]{1,0:T(8,128)(2,1)S(1)} %weights.1.refs_0_, bf16[16,4096]{1,0:T(8,128)(2,1)S(1)} %collective-permute-done.15.refs_1_, bf16[16,4096]{1,0:T(8,128)(2,1)S(1)} %collective-permute-done.16.refs_2_, bf16[16,4096]{1,0:T(8,128)(2,1)S(1)} %collective-permute-done.17.refs_3_, ...), custom_call_target="tpu_custom_call" | custom-call | flops 268435456 | bytes 4718592 | tf_op jit(solution)/shard_map/gradients/pallas_call | solution.py:555
  41.1 0.9 %gradients.3.mine = s16[17,16,128]{2,1,0:T(8,128)(2,1)S(1)} custom-call(bf16[16,4096]{1,0:T(8,128)(2,1)S(1)} %collective-permute-done.20.refs_0_, bf16[16,4096]{1,0:T(8,128)(2,1)S(1)} %collective-permute-done.21.refs_1_, bf16[16,4096]{1,0:T(8,128)(2,1)S(1)} %collective-permute-done.22.refs_2_, bf16[16,4096]{1,0:T(8,128)(2,1)S(1)} %collective-permute-done.23.refs_3_, ...), custom_call_target="tpu_custom_call" | custom-call | flops 268435456 | bytes 4718592 | tf_op jit(solution)/shard_map/gradients/pallas_call | solution.py:555
  42.0 2.1 %collective-permute-start.24 = (s16[17,16,128]{2,1,0:T(8,128)(2,1)S(1)}, s16[17,16,128]{2,1,0:T(8,128)(2,1)S(1)}, u32[]{:S(2)}, u32[]{:S(2)}) collective-permute-start(s16[17,16,128]{2,1,0:T(8,128)(2,1)S(1)} %gradients.3.mine), channel_id=1, source_target_pairs={{0,8},{8,0},{16,24},{24,16},{1,9},{9,1},{17,25},{25,17},{2,10},{10... | collective-permute-start | bytes 208904 | tf_op jit(solution)/shard_map/ppermute | solution.py:22
  44.1 1.8 %collective-permute-done.18.other = s16[17,16,128]{2,1,0:T(8,128)(2,1)S(1)} collective-permute-done((s16[17,16,128]{2,1,0:T(8,128)(2,1)S(1)}, s16[17,16,128]{2,1,0:T(8,128)(2,1)S(1)}, u32[]{:S(2)}, u32[]{:S(2)}) %collective-permute-start.18) | collective-permute-done | bytes 69664 | tf_op jit(solution)/shard_map/ppermute | solution.py:22
  45.9 1.6 %collective-permute-start.19 = (s16[17,16,128]{2,1,0:T(8,128)(2,1)S(1)}, s16[17,16,128]{2,1,0:T(8,128)(2,1)S(1)}, u32[]{:S(2)}, u32[]{:S(2)}) collective-permute-start(s16[17,16,128]{2,1,0:T(8,128)(2,1)S(1)} %merge.2.mine), channel_id=1, source_target_pairs={{0,16},{8,24},{16,0},{24,8},{1,17},{9,25},{17,1},{25,9},{2,18},{10... | collective-permute-start | bytes 208904 | tf_op jit(solution)/shard_map/ppermute | solution.py:22
  47.6 2.3 %collective-permute-start.25 = (s16[17,16,128]{2,1,0:T(8,128)(2,1)S(1)}, s16[17,16,128]{2,1,0:T(8,128)(2,1)S(1)}, u32[]{:S(2)}, u32[]{:S(2)}) collective-permute-start(s16[17,16,128]{2,1,0:T(8,128)(2,1)S(1)} %merge.3.mine), channel_id=1, source_target_pairs={{0,16},{8,24},{16,0},{24,8},{1,17},{9,25},{17,1},{25,9},{2,18},{10... | collective-permute-start | bytes 208904 | tf_op jit(solution)/shard_map/ppermute | solution.py:22
  50.0 2.7 %collective-permute-done.19.other = s16[17,16,128]{2,1,0:T(8,128)(2,1)S(1)} collective-permute-done((s16[17,16,128]{2,1,0:T(8,128)(2,1)S(1)}, s16[17,16,128]{2,1,0:T(8,128)(2,1)S(1)}, u32[]{:S(2)}, u32[]{:S(2)}) %collective-permute-start.19) | collective-permute-done | bytes 69664 | tf_op jit(solution)/shard_map/ppermute | solution.py:22
  52.7 1.4 %collective-permute-done.25.other = s16[17,16,128]{2,1,0:T(8,128)(2,1)S(1)} collective-permute-done((s16[17,16,128]{2,1,0:T(8,128)(2,1)S(1)}, s16[17,16,128]{2,1,0:T(8,128)(2,1)S(1)}, u32[]{:S(2)}, u32[]{:S(2)}) %collective-permute-start.25) | collective-permute-done | bytes 69664 | tf_op jit(solution)/shard_map/ppermute | solution.py:22
  54.1 0.9 %finish.1 = f32[512,128]{1,0:T(8,128)} custom-call(f32[64,512]{1,0:T(8,128)S(1)} %add.1.first, s16[17,16,128]{2,1,0:T(8,128)(2,1)S(1)} %merge.3.mine, s16[17,16,128]{2,1,0:T(8,128)(2,1)S(1)} %collective-permute-done.25.other, f32[8,128]{1,0:T(8,128)S(1)} %get-tuple-element.60.count), custom_call_target="tpu_custom_call" | custom-call | tf_op jit(solution)/shard_map/finish/pallas_call | solution.py:626
  (61 shorter events, 9.3 us)
Async XLA Ops:
  3.4 1.8 %collective-permute-start = (f32[16,4352]{1,0:T(8,128)S(1)}, f32[16,4352]{1,0:T(8,128)S(1)}, u32[]{:S(2)}, u32[]{:S(2)}) collective-permute-start(f32[16,4352]{1,0:T(8,128)S(1)} %get-tuple-element.34), channel_id=1, source_target_pairs={{0,1},{1,0},{2,3},{3,2},{4,5},{5,4},{6,7},{7,6},{8,9},{9,8},{10,11... | collective-permute-start | bytes 835592 | tf_op jit(solution)/shard_map/ppermute | solution.py:22
  3.9 5.3 %collective-permute-start.2 = (f32[16,4096]{1,0:T(8,128)S(1)}, f32[16,4096]{1,0:T(8,128)S(1)}, u32[]{:S(2)}, u32[]{:S(2)}) collective-permute-start(f32[16,4096]{1,0:T(8,128)S(1)} %get-tuple-element.37), channel_id=1, source_target_pairs={{0,1},{1,0},{2,3},{3,2},{4,5},{5,4},{6,7},{7,6},{8,9},{9,8},{10,11... | collective-permute-start | bytes 786440 | tf_op jit(solution)/shard_map/ppermute | solution.py:22
  4.0 5.9 %collective-permute-start.4 = (f32[16,4096]{1,0:T(8,128)S(1)}, f32[16,4096]{1,0:T(8,128)S(1)}, u32[]{:S(2)}, u32[]{:S(2)}) collective-permute-start(f32[16,4096]{1,0:T(8,128)S(1)} %get-tuple-element.39), channel_id=1, source_target_pairs={{0,1},{1,0},{2,3},{3,2},{4,5},{5,4},{6,7},{7,6},{8,9},{9,8},{10,11... | collective-permute-start | bytes 786440 | tf_op jit(solution)/shard_map/ppermute | solution.py:22
  4.4 5.8 %collective-permute-start.7 = (f32[16,4096]{1,0:T(8,128)S(1)}, f32[16,4096]{1,0:T(8,128)S(1)}, u32[]{:S(2)}, u32[]{:S(2)}) collective-permute-start(f32[16,4096]{1,0:T(8,128)S(1)} %get-tuple-element.41), channel_id=1, source_target_pairs={{0,1},{1,0},{2,3},{3,2},{4,5},{5,4},{6,7},{7,6},{8,9},{9,8},{10,11... | collective-permute-start | bytes 786440 | tf_op jit(solution)/shard_map/ppermute | solution.py:22
  5.3 8.8 %collective-permute-start.1 = (s16[16,2176]{1,0:T(8,128)(2,1)S(1)}, s16[16,2176]{1,0:T(8,128)(2,1)S(1)}, u32[]{:S(2)}, u32[]{:S(2)}) collective-permute-start(s16[16,2176]{1,0:T(8,128)(2,1)S(1)} %join.6), channel_id=1, source_target_pairs={{0,6},{1,7},{2,4},{3,5},{4,2},{5,3},{6,0},{7,1},{8,14},{9,15},{10,... | collective-permute-start | bytes 208904 | tf_op jit(solution)/shard_map/ppermute | solution.py:22
  9.3 4.9 %collective-permute-start.3 = (s16[16,2176]{1,0:T(8,128)(2,1)S(1)}, s16[16,2176]{1,0:T(8,128)(2,1)S(1)}, u32[]{:S(2)}, u32[]{:S(2)}) collective-permute-start(s16[16,2176]{1,0:T(8,128)(2,1)S(1)} %join.7), channel_id=1, source_target_pairs={{0,4},{1,5},{2,6},{3,7},{4,0},{5,1},{6,2},{7,3},{8,12},{9,13},{10,... | collective-permute-start | bytes 208904 | tf_op jit(solution)/shard_map/ppermute | solution.py:22
  10.0 5.1 %collective-permute-start.5 = (s16[16,2176]{1,0:T(8,128)(2,1)S(1)}, s16[16,2176]{1,0:T(8,128)(2,1)S(1)}, u32[]{:S(2)}, u32[]{:S(2)}) collective-permute-start(s16[16,2176]{1,0:T(8,128)(2,1)S(1)} %join.8), channel_id=1, source_target_pairs={{0,2},{1,3},{2,0},{3,1},{4,6},{5,7},{6,4},{7,5},{8,10},{9,11},{10,... | collective-permute-start | bytes 208904 | tf_op jit(solution)/shard_map/ppermute | solution.py:22
  10.3 8.6 %collective-permute-start.8 = (s16[16,2688]{1,0:T(8,128)(2,1)S(1)}, s16[16,2688]{1,0:T(8,128)(2,1)S(1)}, u32[]{:S(2)}, u32[]{:S(2)}) collective-permute-start(s16[16,2688]{1,0:T(8,128)(2,1)S(1)} %join.9), channel_id=1, source_target_pairs={{0,6},{1,7},{2,4},{3,5},{4,2},{5,3},{6,0},{7,1},{8,14},{9,15},{10,... | collective-permute-start | bytes 258056 | tf_op jit(solution)/shard_map/ppermute | solution.py:22
  13.4 5.6 %collective-permute-start.9 = (s16[16,2688]{1,0:T(8,128)(2,1)S(1)}, s16[16,2688]{1,0:T(8,128)(2,1)S(1)}, u32[]{:S(2)}, u32[]{:S(2)}) collective-permute-start(s16[16,2688]{1,0:T(8,128)(2,1)S(1)} %join.10), channel_id=1, source_target_pairs={{0,4},{1,5},{2,6},{3,7},{4,0},{5,1},{6,2},{7,3},{8,12},{9,13},{10,... | collective-permute-start | bytes 258056 | tf_op jit(solution)/shard_map/ppermute | solution.py:22
  14.1 4.9 %collective-permute-start.10 = (s16[16,2688]{1,0:T(8,128)(2,1)S(1)}, s16[16,2688]{1,0:T(8,128)(2,1)S(1)}, u32[]{:S(2)}, u32[]{:S(2)}) collective-permute-start(s16[16,2688]{1,0:T(8,128)(2,1)S(1)} %join.11), channel_id=1, source_target_pairs={{0,2},{1,3},{2,0},{3,1},{4,6},{5,7},{6,4},{7,5},{8,10},{9,11},{10,... | collective-permute-start | bytes 258056 | tf_op jit(solution)/shard_map/ppermute | solution.py:22
  15.3 3.6 %collective-permute-start.6 = (f32[8,128]{1,0:T(8,128)S(1)}, f32[8,128]{1,0:T(8,128)S(1)}, u32[]{:S(2)}, u32[]{:S(2)}) collective-permute-start(f32[8,128]{1,0:T(8,128)S(1)} %get-tuple-element.40.refs_0_), channel_id=1, source_target_pairs={{0,8},{8,0},{16,24},{24,16},{1,9},{9,1},{17,25},{25,17},{2,10},{10... | collective-permute-start | bytes 12296 | tf_op jit(solution)/shard_map/ppermute | solution.py:22
  19.0 4.6 %collective-permute-start.11 = (f32[8,128]{1,0:T(8,128)S(1)}, f32[8,128]{1,0:T(8,128)S(1)}, u32[]{:S(2)}, u32[]{:S(2)}) collective-permute-start(f32[8,128]{1,0:T(8,128)S(1)} %get-tuple-element.44.refs_0_), channel_id=1, source_target_pairs={{0,16},{8,24},{16,0},{24,8},{1,17},{9,25},{17,1},{25,9},{2,18},{10... | collective-permute-start | bytes 12296 | tf_op jit(solution)/shard_map/ppermute | solution.py:22
  23.7 7.1 %collective-permute-start.14 = (f32[40,128]{1,0:T(8,128)S(1)}, f32[40,128]{1,0:T(8,128)S(1)}, u32[]{:S(2)}, u32[]{:S(2)}) collective-permute-start(f32[40,128]{1,0:T(8,128)S(1)} %get-tuple-element.53.refs_0_), channel_id=1, source_target_pairs={{0,24},{8,16},{16,8},{24,0},{1,25},{9,17},{17,9},{25,1},{2,26},{10... | collective-permute-start | bytes 61448 | tf_op jit(solution)/shard_map/ppermute | solution.py:22
  27.4 4.7 %collective-permute-start.13 = (f32[40,128]{1,0:T(8,128)S(1)}, f32[40,128]{1,0:T(8,128)S(1)}, u32[]{:S(2)}, u32[]{:S(2)}) collective-permute-start(f32[40,128]{1,0:T(8,128)S(1)} %get-tuple-element.53.refs_0_), channel_id=1, source_target_pairs={{0,16},{8,24},{16,0},{24,8},{1,17},{9,25},{17,1},{25,9},{2,18},{10... | collective-permute-start | bytes 61448 | tf_op jit(solution)/shard_map/ppermute | solution.py:22
  27.4 4.7 %collective-permute-start.12 = (f32[40,128]{1,0:T(8,128)S(1)}, f32[40,128]{1,0:T(8,128)S(1)}, u32[]{:S(2)}, u32[]{:S(2)}) collective-permute-start(f32[40,128]{1,0:T(8,128)S(1)} %get-tuple-element.53.refs_0_), channel_id=1, source_target_pairs={{0,8},{8,0},{16,24},{24,16},{1,9},{9,1},{17,25},{25,17},{2,10},{10... | collective-permute-start | bytes 61448 | tf_op jit(solution)/shard_map/ppermute | solution.py:22
  32.3 6.0 %collective-permute-start.17 = (bf16[16,4096]{1,0:T(8,128)(2,1)S(1)}, bf16[16,4096]{1,0:T(8,128)(2,1)S(1)}, u32[]{:S(2)}, u32[]{:S(2)}) collective-permute-start(bf16[16,4096]{1,0:T(8,128)(2,1)S(1)} %weights.1.refs_0_), channel_id=1, source_target_pairs={{0,6},{1,7},{2,4},{3,5},{4,2},{5,3},{6,0},{7,1},{8,14},{9,15},{10,... | collective-permute-start | bytes 393224 | tf_op jit(solution)/shard_map/ppermute | solution.py:22
  34.3 5.3 %collective-permute-start.16 = (bf16[16,4096]{1,0:T(8,128)(2,1)S(1)}, bf16[16,4096]{1,0:T(8,128)(2,1)S(1)}, u32[]{:S(2)}, u32[]{:S(2)}) collective-permute-start(bf16[16,4096]{1,0:T(8,128)(2,1)S(1)} %weights.1.refs_0_), channel_id=1, source_target_pairs={{0,4},{1,5},{2,6},{3,7},{4,0},{5,1},{6,2},{7,3},{8,12},{9,13},{10,... | collective-permute-start | bytes 393224 | tf_op jit(solution)/shard_map/ppermute | solution.py:22
  34.8 5.0 %collective-permute-start.15 = (bf16[16,4096]{1,0:T(8,128)(2,1)S(1)}, bf16[16,4096]{1,0:T(8,128)(2,1)S(1)}, u32[]{:S(2)}, u32[]{:S(2)}) collective-permute-start(bf16[16,4096]{1,0:T(8,128)(2,1)S(1)} %weights.1.refs_0_), channel_id=1, source_target_pairs={{0,2},{1,3},{2,0},{3,1},{4,6},{5,7},{6,4},{7,5},{8,10},{9,11},{10,... | collective-permute-start | bytes 393224 | tf_op jit(solution)/shard_map/ppermute | solution.py:22
  35.8 5.3 %collective-permute-start.20 = (bf16[16,4096]{1,0:T(8,128)(2,1)S(1)}, bf16[16,4096]{1,0:T(8,128)(2,1)S(1)}, u32[]{:S(2)}, u32[]{:S(2)}) collective-permute-start(bf16[16,4096]{1,0:T(8,128)(2,1)S(1)} %weights.1.refs_0_), channel_id=1, source_target_pairs={{0,1},{1,0},{2,3},{3,2},{4,5},{5,4},{6,7},{7,6},{8,9},{9,8},{10,11... | collective-permute-start | bytes 393224 | tf_op jit(solution)/shard_map/ppermute | solution.py:22
  38.2 2.9 %collective-permute-start.23 = (bf16[16,4096]{1,0:T(8,128)(2,1)S(1)}, bf16[16,4096]{1,0:T(8,128)(2,1)S(1)}, u32[]{:S(2)}, u32[]{:S(2)}) collective-permute-start(bf16[16,4096]{1,0:T(8,128)(2,1)S(1)} %collective-permute-done.17.refs_3_), channel_id=1, source_target_pairs={{0,1},{1,0},{2,3},{3,2},{4,5},{5,4},{6,7},{7,6},{8,9},{9,8},{10,11... | collective-permute-start | bytes 393224 | tf_op jit(solution)/shard_map/ppermute | solution.py:22
  41.0 4.8 %collective-permute-start.18 = (s16[17,16,128]{2,1,0:T(8,128)(2,1)S(1)}, s16[17,16,128]{2,1,0:T(8,128)(2,1)S(1)}, u32[]{:S(2)}, u32[]{:S(2)}) collective-permute-start(s16[17,16,128]{2,1,0:T(8,128)(2,1)S(1)} %gradients.2.mine), channel_id=1, source_target_pairs={{0,8},{8,0},{16,24},{24,16},{1,9},{9,1},{17,25},{25,17},{2,10},{10... | collective-permute-start | bytes 208904 | tf_op jit(solution)/shard_map/ppermute | solution.py:22
  42.0 5.5 %collective-permute-start.24 = (s16[17,16,128]{2,1,0:T(8,128)(2,1)S(1)}, s16[17,16,128]{2,1,0:T(8,128)(2,1)S(1)}, u32[]{:S(2)}, u32[]{:S(2)}) collective-permute-start(s16[17,16,128]{2,1,0:T(8,128)(2,1)S(1)} %gradients.3.mine), channel_id=1, source_target_pairs={{0,8},{8,0},{16,24},{24,16},{1,9},{9,1},{17,25},{25,17},{2,10},{10... | collective-permute-start | bytes 208904 | tf_op jit(solution)/shard_map/ppermute | solution.py:22
  45.9 6.7 %collective-permute-start.19 = (s16[17,16,128]{2,1,0:T(8,128)(2,1)S(1)}, s16[17,16,128]{2,1,0:T(8,128)(2,1)S(1)}, u32[]{:S(2)}, u32[]{:S(2)}) collective-permute-start(s16[17,16,128]{2,1,0:T(8,128)(2,1)S(1)} %merge.2.mine), channel_id=1, source_target_pairs={{0,16},{8,24},{16,0},{24,8},{1,17},{9,25},{17,1},{25,9},{2,18},{10... | collective-permute-start | bytes 208904 | tf_op jit(solution)/shard_map/ppermute | solution.py:22
  47.6 6.5 %collective-permute-start.25 = (s16[17,16,128]{2,1,0:T(8,128)(2,1)S(1)}, s16[17,16,128]{2,1,0:T(8,128)(2,1)S(1)}, u32[]{:S(2)}, u32[]{:S(2)}) collective-permute-start(s16[17,16,128]{2,1,0:T(8,128)(2,1)S(1)} %merge.3.mine), channel_id=1, source_target_pairs={{0,16},{8,24},{16,0},{24,8},{1,17},{9,25},{17,1},{25,9},{2,18},{10... | collective-permute-start | bytes 208904 | tf_op jit(solution)/shard_map/ppermute | solution.py:22
  (5 other events, 39.2 us)

commit v21 on v20

--- a/solution.py
+++ b/solution.py
@@ -67,22 +67,23 @@
     return total
 
 
-def product_kernel(feat, kf, chunk, directions, coefficients, dosages, *refs):
+def product_kernel(feat, kf, sizes, directions, coefficients, dosages, *refs):
     linear, keep, send = refs[0], refs[1 : 1 + feat // 2], refs[1 + feat // 2 : 1 + feat]
     table, own_directions, own_coefficients, lhs, turned, sems = refs[1 + feat :]
     me = lax.axis_index("feat")
     width = feat * kf
     persons, variants = table.shape
-    steps = persons // chunk
+    steps = len(sizes)
+    starts = [sum(sizes[:i]) for i in range(steps)]
     small = [
         pltpu.make_async_copy(directions, own_directions, sems.at[steps]),
         pltpu.make_async_copy(coefficients, own_coefficients, sems.at[steps + 1]),
     ]
     large = [
         pltpu.make_async_copy(
-            dosages.at[pl.ds(i * chunk, chunk)], table.at[pl.ds(i * chunk, chunk)], sems.at[i]
+            dosages.at[pl.ds(first, chunk)], table.at[pl.ds(first, chunk)], sems.at[i]
         )
-        for i in range(steps)
+        for i, (first, chunk) in enumerate(zip(starts, sizes))
     ]
     for copy in small + large:
         copy.start()
@@ -92,9 +93,8 @@
     for j in range(feat):
         lhs[j * kf : (j + 1) * kf] = turned[me ^ j].astype(BF16)
     lhs[width:] = jnp.broadcast_to(own_coefficients[...].astype(F32)[None, :], (16, variants)).astype(BF16)
-    for i in range(steps):
-        large[i].wait()
-        first = i * chunk
+    for copy, first, chunk in zip(large, starts, sizes):
+        copy.wait()
         result = lax.dot_general(
             lhs[...], table[first : first + chunk], NT, preferred_element_type=F32
         )
@@ -112,10 +112,11 @@
     k = directions.shape[1]
     kf = k // feat
     chunk = min(1024, persons)
+    sizes = [chunk] * (persons // chunk - 1) + [chunk // 2] * 2
     piece = jax.ShapeDtypeStruct((kf, persons), F32)
     first = jax.ShapeDtypeStruct((kf, persons + LO), F32)
     out = pl.pallas_call(
-        functools.partial(product_kernel, feat, kf, chunk),
+        functools.partial(product_kernel, feat, kf, tuple(sizes)),
         in_specs=[HBM, HBM, HBM],
         out_shape=[jax.ShapeDtypeStruct((kf, LO), F32)]
         + [piece] * (feat - 1)
@@ -127,7 +128,7 @@
             pltpu.VMEM((variants,), BF16),
             pltpu.VMEM((k + 16, variants), BF16),
             pltpu.VMEM((feat, kf, variants), F32),
-            pltpu.SemaphoreType.DMA((persons // chunk + 2,)),
+            pltpu.SemaphoreType.DMA((len(sizes) + 2,)),
         ],
         compiler_params=pltpu.CompilerParams(**PARAMS),
         cost_estimate=pl.CostEstimate(
@@ -473,13 +474,14 @@
     )(sums, squares, rank)
 
 
-def weight_kernel(ex, *refs):
+def weight_kernel(places, *refs):
+    ex = len(places)
     messages, (first, rest, local, risk, cumulative, squares) = refs[:ex], refs[ex : ex + 6]
     weighted, placed = refs[ex + 6 :]
     kf = first.shape[0]
     me = lax.axis_index("ex")
-    for i in range(ex):
-        placed[me ^ i] = messages[i][...]
+    for i, part in zip(places, messages):
+        placed[me ^ i] = part[...]
     later = jnp.zeros((kf, 128), F32)
     own_later, before = later, later
     hazard_before = jnp.zeros((1, 128), F32)
@@ -500,10 +502,10 @@
         weighted[:, at] = (risk[:, at] * value).astype(BF16)
 
 
-def weights(messages, first, rest, local, risk, cumulative, squares):
+def weights(places, messages, first, rest, local, risk, cumulative, squares):
     ex = len(messages)
     return pl.pallas_call(
-        functools.partial(weight_kernel, ex),
+        functools.partial(weight_kernel, tuple(places)),
         in_specs=[VMEM] * (ex + 6),
         out_shape=jax.ShapeDtypeStruct(local.shape, BF16),
         out_specs=VMEM,
@@ -601,15 +603,14 @@
     me = lax.axis_index("feat")
     variants = out.shape[0]
     scale = count[1:2, 0:1]
-    for q in range(feat // 2):
-        placed[me ^ (2 * q)] = first[q * kf : (q + 1) * kf]
+    copies = []
     for i, value in enumerate(decode_sum(mine, other, variants // 128)):
+        at = slice(i * 128, (i + 1) * 128)
         for q in range(feat // 2):
-            placed[me ^ (2 * q + 1), :, i * 128 : (i + 1) * 128] = value[q * kf : (q + 1) * kf]
-    copies = []
-    for i in range(variants // 128):
-        at = slice(i * 128, (i + 1) * 128)
-        total[at] = placed[:, :, at].reshape(feat * kf, 128).T / scale
+            rows = slice(q * kf, (q + 1) * kf)
+            placed[i, me ^ (2 * q)] = first[rows, at]
+            placed[i, me ^ (2 * q + 1)] = value[rows]
+        total[at] = placed[i].reshape(feat * kf, 128).T / scale
         copies.append(
             pltpu.make_async_copy(
                 total.at[pl.ds(i * 128, 128)], out.at[pl.ds(i * 128, 128)], sems.at[i]
@@ -629,7 +630,7 @@
         out_shape=jax.ShapeDtypeStruct((variants, k), F32),
         out_specs=HBM,
         scratch_shapes=[
-            pltpu.VMEM((feat, kf, variants), F32),
+            pltpu.VMEM((variants // 128, feat, kf, 128), F32),
             pltpu.VMEM((variants, k), F32),
             pltpu.SemaphoreType.DMA((variants // 128,)),
         ],
@@ -676,10 +677,12 @@
     )
     later_sums = suffix_sums(one, two, padded)
     hazard, ordered_squares, message = shares(later, sums, ordered_events, plain, more, later_sums)
-    messages = [message] + [swap(message, "ex", i) for i in range(1, ex)]
+    places = list(range(ex))
+    places[-2:] = places[:-3:-1]
+    messages = [swap(message, "ex", i) if i else message for i in places]
     cumulative, squares = hazards(hazard, ordered_squares, rank, rows)
     summed = prefix_sums(later_sums, ordered_squares, rank, padded)
-    own = weights(messages, tangent, more_tangent, summed, risk, cumulative, squares)
+    own = weights(places, messages, tangent, more_tangent, summed, risk, cumulative, squares)
 
     chips = {0: own}
     for q in range(1, feat // 2):

time: 55.1 us -> 55.3 us (level)
  waiting for transfers between devices: 12.8 us -> 13.9 us
  starting transfers between devices: 28.1 us -> 27.1 us
    ppermute x26, waiting for transfers between devices: 12.8 us -> 13.9 us  [swap(): return lax.ppermute(x, axis, [(s, s ^ i) for s in range(count)])]
    ppermute x26, starting transfers between devices: 28.1 us -> 27.1 us  [swap(): return lax.ppermute(x, axis, [(s, s ^ i) for s in range(count)])]
where the time goes in v21:
time: 55.3 us; the launch traced here: 55.2 us
  starting transfers between devices  27.1 us (49%)
  Pallas kernels  13.9 us (25%)
  waiting for transfers between devices  13.9 us (25%)
    ppermute x26, starting transfers between devices, swap(): return lax.ppermute(x, axis, [(s, s ^ i) for s in range(count)])  27.1 us
    ppermute x26, waiting for transfers between devices, swap(): return lax.ppermute(x, axis, [(s, s ^ i) for s in range(count)])  13.9 us
    pallas_call x1, Pallas kernels, products(): pl.pallas_call(functools.partial(product_kernel, feat, kf, tuple(sizes)),...  3.49 us
    pallas_call x2, Pallas kernels, ordered_values(): pl.pallas_call(functools.partial(order_kernel, start, len(messages)), in_...  1.97 us
    pallas_call x2, Pallas kernels, gradients(): pl.pallas_call(functools.partial(gradient_kernel, parts, kf), in_specs=[V...  1.76 us
    pallas_call x1, Pallas kernels, prefix_sums(): pl.pallas_call(prefix_kernel, in_specs=[VMEM] * 3, out_shape=jax.ShapeDty...  1.75 us
  transfers between devices with their start and end apart: 26, of which 10 were waited for; matrix products, arithmetic and copies ran while one was open for 0% of the time, Pallas kernels for 17%

profile of v21, /device:TPU:0, one launch (start us, length us, event | category | flops | bytes accessed | tf_op | source)
XLA Modules:
  0.0 55.2 jit_solution(4437379619624897854)
XLA Ops:
  0.0 3.5 %products.1 = (f32[16,256]{1,0:T(8,128)S(1)}, f32[16,4096]{1,0:T(8,128)S(1)}, f32[16,4096]{1,0:T(8,128)S(1)}, f32[16,4096]{1,0:T(8,128)S(1)}, f32[16,4096]{1,0:T...) custom-call(bf16[512,128]{1,0:T(8,128)(2,1)} %directions.1, ...), custom_call_target="tpu_custom_call" | custom-call | flops 536870912 | bytes 6291456 | tf_op jit(solution)/shard_map/products/pallas_call | solution.py:118
  5.4 3.9 %collective-permute-start.1 = (s16[16,2176]{1,0:T(8,128)(2,1)S(1)}, s16[16,2176]{1,0:T(8,128)(2,1)S(1)}, u32[]{:S(2)}, u32[]{:S(2)}) collective-permute-start(s16[16,2176]{1,0:T(8,128)(2,1)S(1)} %join.6), channel_id=1, source_target_pairs={{0,6},{1,7},{2,4},{3,5},{4,2},{5,3},{6,0},{7,1},{8,14},{9,15},{10,... | collective-permute-start | bytes 208904 | tf_op jit(solution)/shard_map/ppermute | solution.py:22
  10.5 2.9 %collective-permute-start.8 = (s16[16,2688]{1,0:T(8,128)(2,1)S(1)}, s16[16,2688]{1,0:T(8,128)(2,1)S(1)}, u32[]{:S(2)}, u32[]{:S(2)}) collective-permute-start(s16[16,2688]{1,0:T(8,128)(2,1)S(1)} %join.9), channel_id=1, source_target_pairs={{0,6},{1,7},{2,4},{3,5},{4,2},{5,3},{6,0},{7,1},{8,14},{9,15},{10,... | collective-permute-start | bytes 258056 | tf_op jit(solution)/shard_map/ppermute | solution.py:22
  14.4 0.9 %collective-permute-done.5.refs_2_ = s16[16,2176]{1,0:T(8,128)(2,1)S(1)} collective-permute-done((s16[16,2176]{1,0:T(8,128)(2,1)S(1)}, s16[16,2176]{1,0:T(8,128)(2,1)S(1)}, u32[]{:S(2)}, u32[]{:S(2)}) %collective-permute-start.5) | collective-permute-done | bytes 69664 | tf_op jit(solution)/shard_map/ppermute | solution.py:22
  15.5 1.6 %collective-permute-start.6 = (f32[8,128]{1,0:T(8,128)S(1)}, f32[8,128]{1,0:T(8,128)S(1)}, u32[]{:S(2)}, u32[]{:S(2)}) collective-permute-start(f32[8,128]{1,0:T(8,128)S(1)} %get-tuple-element.40.refs_0_), channel_id=1, source_target_pairs={{0,8},{8,0},{16,24},{24,16},{1,9},{9,1},{17,25},{25,17},{2,10},{10... | collective-permute-start | bytes 12296 | tf_op jit(solution)/shard_map/ppermute | solution.py:22
  19.1 2.6 %collective-permute-start.11 = (f32[8,128]{1,0:T(8,128)S(1)}, f32[8,128]{1,0:T(8,128)S(1)}, u32[]{:S(2)}, u32[]{:S(2)}) collective-permute-start(f32[8,128]{1,0:T(8,128)S(1)} %get-tuple-element.44.refs_0_), channel_id=1, source_target_pairs={{0,16},{8,24},{16,0},{24,8},{1,17},{9,25},{17,1},{25,9},{2,18},{10... | collective-permute-start | bytes 12296 | tf_op jit(solution)/shard_map/ppermute | solution.py:22
  21.8 1.2 %ordered_values.3 = (f32[16,2560]{1,0:T(8,128)S(1)}, f32[256,256]{1,0:T(8,128)S(1)}, f32[16,128]{1,0:T(8,128)S(1)}) custom-call(f32[16,4096]{1,0:T(8,128)S(1)} %get-tuple-element.48.own, f32[16,4096]{1,0:T(8,128)S(1)} %collective-permute-done.7.refs_1_.other, s16[16,2688]{1,0:T(8,128)(2,1)S(1)} %collective-permute-done.8.refs_3_.refs_0_, ...), custom_call_target="tpu_custom_call" | custom-call | flops 671088640 | bytes 983040 | tf_op jit(solution)/shard_map/ordered_values/pallas_call | solution.py:398
  23.9 2.6 %collective-permute-start.14 = (f32[40,128]{1,0:T(8,128)S(1)}, f32[40,128]{1,0:T(8,128)S(1)}, u32[]{:S(2)}, u32[]{:S(2)}) collective-permute-start(f32[40,128]{1,0:T(8,128)S(1)} %get-tuple-element.53.refs_0_), channel_id=1, source_target_pairs={{0,16},{8,24},{16,0},{24,8},{1,17},{9,25},{17,1},{25,9},{2,18},{10... | collective-permute-start | bytes 61448 | tf_op jit(solution)/shard_map/ppermute | solution.py:22
  26.5 1.3 %collective-permute-start.13 = (f32[40,128]{1,0:T(8,128)S(1)}, f32[40,128]{1,0:T(8,128)S(1)}, u32[]{:S(2)}, u32[]{:S(2)}) collective-permute-start(f32[40,128]{1,0:T(8,128)S(1)} %get-tuple-element.53.refs_0_), channel_id=1, source_target_pairs={{0,24},{8,16},{16,8},{24,0},{1,25},{9,17},{17,9},{25,1},{2,26},{10... | collective-permute-start | bytes 61448 | tf_op jit(solution)/shard_map/ppermute | solution.py:22
  28.0 1.7 %prefix_sums.1.refs_6_ = f32[16,4096]{1,0:T(8,128)S(1)} custom-call(f32[256,256]{1,0:T(8,128)S(1)} %suffix_sums.1.ordered.sums, f32[16,256]{1,0:T(8,128)S(1)} %get-tuple-element.56.squares.square, s32[1,4096]{1,0:T(1,128)S(1)} %bitcast.6), custom_call_target="tpu_custom_call" | custom-call | flops 1073741824 | bytes 1572864 | tf_op jit(solution)/shard_map/prefix_sums/pallas_call | solution.py:464
  29.8 0.9 %hazards.1 = (f32[1,4096]{1,0:T(1,128)S(1)}, f32[1,4096]{1,0:T(1,128)S(1)}) custom-call(f32[16,256]{1,0:T(8,128)S(1)} %get-tuple-element.57.hazard, f32[16,256]{1,0:T(8,128)S(1)} %get-tuple-element.56.squares.square, s32[1,4096]{1,0:T(1,128)S(1)} %bitcast.7), custom_call_target="tpu_custom_call" | custom-call | flops 209715200 | bytes 262144 | tf_op jit(solution)/shard_map/hazards/pallas_call | solution.py:332
  30.7 1.3 %collective-permute-done.13.refs_2_ = f32[40,128]{1,0:T(8,128)S(1)} collective-permute-done((f32[40,128]{1,0:T(8,128)S(1)}, f32[40,128]{1,0:T(8,128)S(1)}, u32[]{:S(2)}, u32[]{:S(2)}) %collective-permute-start.13) | collective-permute-done | bytes 20512 | tf_op jit(solution)/shard_map/ppermute | solution.py:22
  32.2 2.1 %collective-permute-start.17 = (bf16[16,4096]{1,0:T(8,128)(2,1)S(1)}, bf16[16,4096]{1,0:T(8,128)(2,1)S(1)}, u32[]{:S(2)}, u32[]{:S(2)}) collective-permute-start(bf16[16,4096]{1,0:T(8,128)(2,1)S(1)} %weights.1.refs_0_), channel_id=1, source_target_pairs={{0,6},{1,7},{2,4},{3,5},{4,2},{5,3},{6,0},{7,1},{8,14},{9,15},{10,... | collective-permute-start | bytes 393224 | tf_op jit(solution)/shard_map/ppermute | solution.py:22
  34.8 1.0 %collective-permute-start.15 = (bf16[16,4096]{1,0:T(8,128)(2,1)S(1)}, bf16[16,4096]{1,0:T(8,128)(2,1)S(1)}, u32[]{:S(2)}, u32[]{:S(2)}) collective-permute-start(bf16[16,4096]{1,0:T(8,128)(2,1)S(1)} %weights.1.refs_0_), channel_id=1, source_target_pairs={{0,2},{1,3},{2,0},{3,1},{4,6},{5,7},{6,4},{7,5},{8,10},{9,11},{10,... | collective-permute-start | bytes 393224 | tf_op jit(solution)/shard_map/ppermute | solution.py:22
  35.8 2.4 %collective-permute-done.17.refs_3_ = bf16[16,4096]{1,0:T(8,128)(2,1)S(1)} collective-permute-done((bf16[16,4096]{1,0:T(8,128)(2,1)S(1)}, bf16[16,4096]{1,0:T(8,128)(2,1)S(1)}, u32[]{:S(2)}, u32[]{:S(2)}) %collective-permute-start.17) | collective-permute-done | bytes 131104 | tf_op jit(solution)/shard_map/ppermute | solution.py:22
  38.2 1.4 %collective-permute-done.16.refs_2_ = bf16[16,4096]{1,0:T(8,128)(2,1)S(1)} collective-permute-done((bf16[16,4096]{1,0:T(8,128)(2,1)S(1)}, bf16[16,4096]{1,0:T(8,128)(2,1)S(1)}, u32[]{:S(2)}, u32[]{:S(2)}) %collective-permute-start.16) | collective-permute-done | bytes 131104 | tf_op jit(solution)/shard_map/ppermute | solution.py:22
  40.1 0.9 %gradients.2.mine = s16[17,16,128]{2,1,0:T(8,128)(2,1)S(1)} custom-call(bf16[16,4096]{1,0:T(8,128)(2,1)S(1)} %weights.1.refs_0_, bf16[16,4096]{1,0:T(8,128)(2,1)S(1)} %collective-permute-done.15.refs_1_, bf16[16,4096]{1,0:T(8,128)(2,1)S(1)} %collective-permute-done.16.refs_2_, bf16[16,4096]{1,0:T(8,128)(2,1)S(1)} %collective-permute-done.17.refs_3_, ...), custom_call_target="tpu_custom_call" | custom-call | flops 268435456 | bytes 4718592 | tf_op jit(solution)/shard_map/gradients/pallas_call | solution.py:557
  41.5 0.9 %gradients.3.mine = s16[17,16,128]{2,1,0:T(8,128)(2,1)S(1)} custom-call(bf16[16,4096]{1,0:T(8,128)(2,1)S(1)} %collective-permute-done.20.refs_0_, bf16[16,4096]{1,0:T(8,128)(2,1)S(1)} %collective-permute-done.21.refs_1_, bf16[16,4096]{1,0:T(8,128)(2,1)S(1)} %collective-permute-done.22.refs_2_, bf16[16,4096]{1,0:T(8,128)(2,1)S(1)} %collective-permute-done.23.refs_3_, ...), custom_call_target="tpu_custom_call" | custom-call | flops 268435456 | bytes 4718592 | tf_op jit(solution)/shard_map/gradients/pallas_call | solution.py:557
  42.4 1.6 %collective-permute-start.24 = (s16[17,16,128]{2,1,0:T(8,128)(2,1)S(1)}, s16[17,16,128]{2,1,0:T(8,128)(2,1)S(1)}, u32[]{:S(2)}, u32[]{:S(2)}) collective-permute-start(s16[17,16,128]{2,1,0:T(8,128)(2,1)S(1)} %gradients.3.mine), channel_id=1, source_target_pairs={{0,8},{8,0},{16,24},{24,16},{1,9},{9,1},{17,25},{25,17},{2,10},{10... | collective-permute-start | bytes 208904 | tf_op jit(solution)/shard_map/ppermute | solution.py:22
  44.0 1.6 %collective-permute-done.18.other = s16[17,16,128]{2,1,0:T(8,128)(2,1)S(1)} collective-permute-done((s16[17,16,128]{2,1,0:T(8,128)(2,1)S(1)}, s16[17,16,128]{2,1,0:T(8,128)(2,1)S(1)}, u32[]{:S(2)}, u32[]{:S(2)}) %collective-permute-start.18) | collective-permute-done | bytes 69664 | tf_op jit(solution)/shard_map/ppermute | solution.py:22
  45.7 1.3 %collective-permute-start.19 = (s16[17,16,128]{2,1,0:T(8,128)(2,1)S(1)}, s16[17,16,128]{2,1,0:T(8,128)(2,1)S(1)}, u32[]{:S(2)}, u32[]{:S(2)}) collective-permute-start(s16[17,16,128]{2,1,0:T(8,128)(2,1)S(1)} %merge.2.mine), channel_id=1, source_target_pairs={{0,16},{8,24},{16,0},{24,8},{1,17},{9,25},{17,1},{25,9},{2,18},{10... | collective-permute-start | bytes 208904 | tf_op jit(solution)/shard_map/ppermute | solution.py:22
  47.1 2.0 %collective-permute-start.25 = (s16[17,16,128]{2,1,0:T(8,128)(2,1)S(1)}, s16[17,16,128]{2,1,0:T(8,128)(2,1)S(1)}, u32[]{:S(2)}, u32[]{:S(2)}) collective-permute-start(s16[17,16,128]{2,1,0:T(8,128)(2,1)S(1)} %merge.3.mine), channel_id=1, source_target_pairs={{0,16},{8,24},{16,0},{24,8},{1,17},{9,25},{17,1},{25,9},{2,18},{10... | collective-permute-start | bytes 208904 | tf_op jit(solution)/shard_map/ppermute | solution.py:22
  49.0 4.6 %collective-permute-done.19.other = s16[17,16,128]{2,1,0:T(8,128)(2,1)S(1)} collective-permute-done((s16[17,16,128]{2,1,0:T(8,128)(2,1)S(1)}, s16[17,16,128]{2,1,0:T(8,128)(2,1)S(1)}, u32[]{:S(2)}, u32[]{:S(2)}) %collective-permute-start.19) | collective-permute-done | bytes 69664 | tf_op jit(solution)/shard_map/ppermute | solution.py:22
  54.3 0.9 %finish.1 = f32[512,128]{1,0:T(8,128)} custom-call(f32[64,512]{1,0:T(8,128)S(1)} %add.1.first, s16[17,16,128]{2,1,0:T(8,128)(2,1)S(1)} %merge.3.mine, s16[17,16,128]{2,1,0:T(8,128)(2,1)S(1)} %collective-permute-done.25.other, f32[8,128]{1,0:T(8,128)S(1)} %get-tuple-element.60.count), custom_call_target="tpu_custom_call" | custom-call | tf_op jit(solution)/shard_map/finish/pallas_call | solution.py:627
  (61 shorter events, 10.0 us)
Async XLA Ops:
  4.0 5.3 %collective-permute-start.2 = (f32[16,4096]{1,0:T(8,128)S(1)}, f32[16,4096]{1,0:T(8,128)S(1)}, u32[]{:S(2)}, u32[]{:S(2)}) collective-permute-start(f32[16,4096]{1,0:T(8,128)S(1)} %get-tuple-element.37), channel_id=1, source_target_pairs={{0,1},{1,0},{2,3},{3,2},{4,5},{5,4},{6,7},{7,6},{8,9},{9,8},{10,11... | collective-permute-start | bytes 786440 | tf_op jit(solution)/shard_map/ppermute | solution.py:22
  4.1 5.9 %collective-permute-start.4 = (f32[16,4096]{1,0:T(8,128)S(1)}, f32[16,4096]{1,0:T(8,128)S(1)}, u32[]{:S(2)}, u32[]{:S(2)}) collective-permute-start(f32[16,4096]{1,0:T(8,128)S(1)} %get-tuple-element.39), channel_id=1, source_target_pairs={{0,1},{1,0},{2,3},{3,2},{4,5},{5,4},{6,7},{7,6},{8,9},{9,8},{10,11... | collective-permute-start | bytes 786440 | tf_op jit(solution)/shard_map/ppermute | solution.py:22
  4.5 5.8 %collective-permute-start.7 = (f32[16,4096]{1,0:T(8,128)S(1)}, f32[16,4096]{1,0:T(8,128)S(1)}, u32[]{:S(2)}, u32[]{:S(2)}) collective-permute-start(f32[16,4096]{1,0:T(8,128)S(1)} %get-tuple-element.41), channel_id=1, source_target_pairs={{0,1},{1,0},{2,3},{3,2},{4,5},{5,4},{6,7},{7,6},{8,9},{9,8},{10,11... | collective-permute-start | bytes 786440 | tf_op jit(solution)/shard_map/ppermute | solution.py:22
  5.4 8.8 %collective-permute-start.1 = (s16[16,2176]{1,0:T(8,128)(2,1)S(1)}, s16[16,2176]{1,0:T(8,128)(2,1)S(1)}, u32[]{:S(2)}, u32[]{:S(2)}) collective-permute-start(s16[16,2176]{1,0:T(8,128)(2,1)S(1)} %join.6), channel_id=1, source_target_pairs={{0,6},{1,7},{2,4},{3,5},{4,2},{5,3},{6,0},{7,1},{8,14},{9,15},{10,... | collective-permute-start | bytes 208904 | tf_op jit(solution)/shard_map/ppermute | solution.py:22
  9.5 4.9 %collective-permute-start.3 = (s16[16,2176]{1,0:T(8,128)(2,1)S(1)}, s16[16,2176]{1,0:T(8,128)(2,1)S(1)}, u32[]{:S(2)}, u32[]{:S(2)}) collective-permute-start(s16[16,2176]{1,0:T(8,128)(2,1)S(1)} %join.7), channel_id=1, source_target_pairs={{0,4},{1,5},{2,6},{3,7},{4,0},{5,1},{6,2},{7,3},{8,12},{9,13},{10,... | collective-permute-start | bytes 208904 | tf_op jit(solution)/shard_map/ppermute | solution.py:22
  10.2 5.1 %collective-permute-start.5 = (s16[16,2176]{1,0:T(8,128)(2,1)S(1)}, s16[16,2176]{1,0:T(8,128)(2,1)S(1)}, u32[]{:S(2)}, u32[]{:S(2)}) collective-permute-start(s16[16,2176]{1,0:T(8,128)(2,1)S(1)} %join.8), channel_id=1, source_target_pairs={{0,2},{1,3},{2,0},{3,1},{4,6},{5,7},{6,4},{7,5},{8,10},{9,11},{10,... | collective-permute-start | bytes 208904 | tf_op jit(solution)/shard_map/ppermute | solution.py:22
  10.5 8.6 %collective-permute-start.8 = (s16[16,2688]{1,0:T(8,128)(2,1)S(1)}, s16[16,2688]{1,0:T(8,128)(2,1)S(1)}, u32[]{:S(2)}, u32[]{:S(2)}) collective-permute-start(s16[16,2688]{1,0:T(8,128)(2,1)S(1)} %join.9), channel_id=1, source_target_pairs={{0,6},{1,7},{2,4},{3,5},{4,2},{5,3},{6,0},{7,1},{8,14},{9,15},{10,... | collective-permute-start | bytes 258056 | tf_op jit(solution)/shard_map/ppermute | solution.py:22
  13.5 5.6 %collective-permute-start.9 = (s16[16,2688]{1,0:T(8,128)(2,1)S(1)}, s16[16,2688]{1,0:T(8,128)(2,1)S(1)}, u32[]{:S(2)}, u32[]{:S(2)}) collective-permute-start(s16[16,2688]{1,0:T(8,128)(2,1)S(1)} %join.10), channel_id=1, source_target_pairs={{0,4},{1,5},{2,6},{3,7},{4,0},{5,1},{6,2},{7,3},{8,12},{9,13},{10,... | collective-permute-start | bytes 258056 | tf_op jit(solution)/shard_map/ppermute | solution.py:22
  14.2 4.9 %collective-permute-start.10 = (s16[16,2688]{1,0:T(8,128)(2,1)S(1)}, s16[16,2688]{1,0:T(8,128)(2,1)S(1)}, u32[]{:S(2)}, u32[]{:S(2)}) collective-permute-start(s16[16,2688]{1,0:T(8,128)(2,1)S(1)} %join.11), channel_id=1, source_target_pairs={{0,2},{1,3},{2,0},{3,1},{4,6},{5,7},{6,4},{7,5},{8,10},{9,11},{10,... | collective-permute-start | bytes 258056 | tf_op jit(solution)/shard_map/ppermute | solution.py:22
  15.5 3.6 %collective-permute-start.6 = (f32[8,128]{1,0:T(8,128)S(1)}, f32[8,128]{1,0:T(8,128)S(1)}, u32[]{:S(2)}, u32[]{:S(2)}) collective-permute-start(f32[8,128]{1,0:T(8,128)S(1)} %get-tuple-element.40.refs_0_), channel_id=1, source_target_pairs={{0,8},{8,0},{16,24},{24,16},{1,9},{9,1},{17,25},{25,17},{2,10},{10... | collective-permute-start | bytes 12296 | tf_op jit(solution)/shard_map/ppermute | solution.py:22
  19.1 4.6 %collective-permute-start.11 = (f32[8,128]{1,0:T(8,128)S(1)}, f32[8,128]{1,0:T(8,128)S(1)}, u32[]{:S(2)}, u32[]{:S(2)}) collective-permute-start(f32[8,128]{1,0:T(8,128)S(1)} %get-tuple-element.44.refs_0_), channel_id=1, source_target_pairs={{0,16},{8,24},{16,0},{24,8},{1,17},{9,25},{17,1},{25,9},{2,18},{10... | collective-permute-start | bytes 12296 | tf_op jit(solution)/shard_map/ppermute | solution.py:22
  23.9 6.8 %collective-permute-start.14 = (f32[40,128]{1,0:T(8,128)S(1)}, f32[40,128]{1,0:T(8,128)S(1)}, u32[]{:S(2)}, u32[]{:S(2)}) collective-permute-start(f32[40,128]{1,0:T(8,128)S(1)} %get-tuple-element.53.refs_0_), channel_id=1, source_target_pairs={{0,16},{8,24},{16,0},{24,8},{1,17},{9,25},{17,1},{25,9},{2,18},{10... | collective-permute-start | bytes 61448 | tf_op jit(solution)/shard_map/ppermute | solution.py:22
  26.5 5.6 %collective-permute-start.13 = (f32[40,128]{1,0:T(8,128)S(1)}, f32[40,128]{1,0:T(8,128)S(1)}, u32[]{:S(2)}, u32[]{:S(2)}) collective-permute-start(f32[40,128]{1,0:T(8,128)S(1)} %get-tuple-element.53.refs_0_), channel_id=1, source_target_pairs={{0,24},{8,16},{16,8},{24,0},{1,25},{9,17},{17,9},{25,1},{2,26},{10... | collective-permute-start | bytes 61448 | tf_op jit(solution)/shard_map/ppermute | solution.py:22
  27.8 4.2 %collective-permute-start.12 = (f32[40,128]{1,0:T(8,128)S(1)}, f32[40,128]{1,0:T(8,128)S(1)}, u32[]{:S(2)}, u32[]{:S(2)}) collective-permute-start(f32[40,128]{1,0:T(8,128)S(1)} %get-tuple-element.53.refs_0_), channel_id=1, source_target_pairs={{0,8},{8,0},{16,24},{24,16},{1,9},{9,1},{17,25},{25,17},{2,10},{10... | collective-permute-start | bytes 61448 | tf_op jit(solution)/shard_map/ppermute | solution.py:22
  32.2 6.0 %collective-permute-start.17 = (bf16[16,4096]{1,0:T(8,128)(2,1)S(1)}, bf16[16,4096]{1,0:T(8,128)(2,1)S(1)}, u32[]{:S(2)}, u32[]{:S(2)}) collective-permute-start(bf16[16,4096]{1,0:T(8,128)(2,1)S(1)} %weights.1.refs_0_), channel_id=1, source_target_pairs={{0,6},{1,7},{2,4},{3,5},{4,2},{5,3},{6,0},{7,1},{8,14},{9,15},{10,... | collective-permute-start | bytes 393224 | tf_op jit(solution)/shard_map/ppermute | solution.py:22
  34.3 5.3 %collective-permute-start.16 = (bf16[16,4096]{1,0:T(8,128)(2,1)S(1)}, bf16[16,4096]{1,0:T(8,128)(2,1)S(1)}, u32[]{:S(2)}, u32[]{:S(2)}) collective-permute-start(bf16[16,4096]{1,0:T(8,128)(2,1)S(1)} %weights.1.refs_0_), channel_id=1, source_target_pairs={{0,4},{1,5},{2,6},{3,7},{4,0},{5,1},{6,2},{7,3},{8,12},{9,13},{10,... | collective-permute-start | bytes 393224 | tf_op jit(solution)/shard_map/ppermute | solution.py:22
  34.8 5.0 %collective-permute-start.15 = (bf16[16,4096]{1,0:T(8,128)(2,1)S(1)}, bf16[16,4096]{1,0:T(8,128)(2,1)S(1)}, u32[]{:S(2)}, u32[]{:S(2)}) collective-permute-start(bf16[16,4096]{1,0:T(8,128)(2,1)S(1)} %weights.1.refs_0_), channel_id=1, source_target_pairs={{0,2},{1,3},{2,0},{3,1},{4,6},{5,7},{6,4},{7,5},{8,10},{9,11},{10,... | collective-permute-start | bytes 393224 | tf_op jit(solution)/shard_map/ppermute | solution.py:22
  35.8 5.7 %collective-permute-start.20 = (bf16[16,4096]{1,0:T(8,128)(2,1)S(1)}, bf16[16,4096]{1,0:T(8,128)(2,1)S(1)}, u32[]{:S(2)}, u32[]{:S(2)}) collective-permute-start(bf16[16,4096]{1,0:T(8,128)(2,1)S(1)} %weights.1.refs_0_), channel_id=1, source_target_pairs={{0,1},{1,0},{2,3},{3,2},{4,5},{5,4},{6,7},{7,6},{8,9},{9,8},{10,11... | collective-permute-start | bytes 393224 | tf_op jit(solution)/shard_map/ppermute | solution.py:22
  38.2 3.3 %collective-permute-start.23 = (bf16[16,4096]{1,0:T(8,128)(2,1)S(1)}, bf16[16,4096]{1,0:T(8,128)(2,1)S(1)}, u32[]{:S(2)}, u32[]{:S(2)}) collective-permute-start(bf16[16,4096]{1,0:T(8,128)(2,1)S(1)} %collective-permute-done.17.refs_3_), channel_id=1, source_target_pairs={{0,1},{1,0},{2,3},{3,2},{4,5},{5,4},{6,7},{7,6},{8,9},{9,8},{10,11... | collective-permute-start | bytes 393224 | tf_op jit(solution)/shard_map/ppermute | solution.py:22
  39.6 2.0 %collective-permute-start.22 = (bf16[16,4096]{1,0:T(8,128)(2,1)S(1)}, bf16[16,4096]{1,0:T(8,128)(2,1)S(1)}, u32[]{:S(2)}, u32[]{:S(2)}) collective-permute-start(bf16[16,4096]{1,0:T(8,128)(2,1)S(1)} %collective-permute-done.16.refs_2_), channel_id=1, source_target_pairs={{0,1},{1,0},{2,3},{3,2},{4,5},{5,4},{6,7},{7,6},{8,9},{9,8},{10,11... | collective-permute-start | bytes 393224 | tf_op jit(solution)/shard_map/ppermute | solution.py:22
  41.0 4.7 %collective-permute-start.18 = (s16[17,16,128]{2,1,0:T(8,128)(2,1)S(1)}, s16[17,16,128]{2,1,0:T(8,128)(2,1)S(1)}, u32[]{:S(2)}, u32[]{:S(2)}) collective-permute-start(s16[17,16,128]{2,1,0:T(8,128)(2,1)S(1)} %gradients.2.mine), channel_id=1, source_target_pairs={{0,8},{8,0},{16,24},{24,16},{1,9},{9,1},{17,25},{25,17},{2,10},{10... | collective-permute-start | bytes 208904 | tf_op jit(solution)/shard_map/ppermute | solution.py:22
  42.4 4.6 %collective-permute-start.24 = (s16[17,16,128]{2,1,0:T(8,128)(2,1)S(1)}, s16[17,16,128]{2,1,0:T(8,128)(2,1)S(1)}, u32[]{:S(2)}, u32[]{:S(2)}) collective-permute-start(s16[17,16,128]{2,1,0:T(8,128)(2,1)S(1)} %gradients.3.mine), channel_id=1, source_target_pairs={{0,8},{8,0},{16,24},{24,16},{1,9},{9,1},{17,25},{25,17},{2,10},{10... | collective-permute-start | bytes 208904 | tf_op jit(solution)/shard_map/ppermute | solution.py:22
  45.7 7.9 %collective-permute-start.19 = (s16[17,16,128]{2,1,0:T(8,128)(2,1)S(1)}, s16[17,16,128]{2,1,0:T(8,128)(2,1)S(1)}, u32[]{:S(2)}, u32[]{:S(2)}) collective-permute-start(s16[17,16,128]{2,1,0:T(8,128)(2,1)S(1)} %merge.2.mine), channel_id=1, source_target_pairs={{0,16},{8,24},{16,0},{24,8},{1,17},{9,25},{17,1},{25,9},{2,18},{10... | collective-permute-start | bytes 208904 | tf_op jit(solution)/shard_map/ppermute | solution.py:22
  47.1 7.3 %collective-permute-start.25 = (s16[17,16,128]{2,1,0:T(8,128)(2,1)S(1)}, s16[17,16,128]{2,1,0:T(8,128)(2,1)S(1)}, u32[]{:S(2)}, u32[]{:S(2)}) collective-permute-start(s16[17,16,128]{2,1,0:T(8,128)(2,1)S(1)} %merge.3.mine), channel_id=1, source_target_pairs={{0,16},{8,24},{16,0},{24,8},{1,17},{9,25},{17,1},{25,9},{2,18},{10... | collective-permute-start | bytes 208904 | tf_op jit(solution)/shard_map/ppermute | solution.py:22
  (5 other events, 39.8 us)

commit v22 on v21

--- a/solution.py
+++ b/solution.py
@@ -112,7 +112,7 @@
     k = directions.shape[1]
     kf = k // feat
     chunk = min(1024, persons)
-    sizes = [chunk] * (persons // chunk - 1) + [chunk // 2] * 2
+    sizes = [chunk] * (persons // chunk)
     piece = jax.ShapeDtypeStruct((kf, persons), F32)
     first = jax.ShapeDtypeStruct((kf, persons + LO), F32)
     out = pl.pallas_call(
@@ -546,8 +546,13 @@
     pieces, dosages, out, weighted = refs[:parts], refs[parts], refs[parts + 1], refs[parts + 2]
     for i in range(parts):
         weighted[i * kf : (i + 1) * kf, :] = pieces[i][...]
-    total = jnp.dot(weighted[...], dosages[...], preferred_element_type=F32)
-    encode([total[:, at : at + 128] for at in range(0, total.shape[1], 128)], out)
+    variants = dosages.shape[1]
+    block = min(256, variants)
+    values = []
+    for start in range(0, variants, block):
+        total = jnp.dot(weighted[...], dosages[:, start : start + block], preferred_element_type=F32)
+        values += [total[:, at : at + 128] for at in range(0, block, 128)]
+    encode(values, out)
 
 
 def gradients(pieces, dosages):

time: 55.3 us -> 55.2 us (level)
  no operation moved by 1% of the time
where the time goes in v22:
time: 55.2 us; the launch traced here: 55.1 us
  starting transfers between devices  27.1 us (49%)
  waiting for transfers between devices  13.9 us (25%)
  Pallas kernels  13.8 us (25%)
    ppermute x26, starting transfers between devices, swap(): return lax.ppermute(x, axis, [(s, s ^ i) for s in range(count)])  27.1 us
    ppermute x26, waiting for transfers between devices, swap(): return lax.ppermute(x, axis, [(s, s ^ i) for s in range(count)])  13.9 us
    pallas_call x1, Pallas kernels, products(): pl.pallas_call(functools.partial(product_kernel, feat, kf, tuple(sizes)),...  3.35 us
    pallas_call x2, Pallas kernels, ordered_values(): pl.pallas_call(functools.partial(order_kernel, start, len(messages)), in_...  1.97 us
    pallas_call x2, Pallas kernels, gradients(): pl.pallas_call(functools.partial(gradient_kernel, parts, kf), in_specs=[V...  1.76 us
    pallas_call x1, Pallas kernels, prefix_sums(): pl.pallas_call(prefix_kernel, in_specs=[VMEM] * 3, out_shape=jax.ShapeDty...  1.75 us
  transfers between devices with their start and end apart: 26, of which 10 were waited for; matrix products, arithmetic and copies ran while one was open for 0% of the time, Pallas kernels for 17%

profile of v22, /device:TPU:0, one launch (start us, length us, event | category | flops | bytes accessed | tf_op | source)
XLA Modules:
  0.0 55.1 jit_solution(2633091680087498957)
XLA Ops:
  0.0 3.3 %products.1 = (f32[16,256]{1,0:T(8,128)S(1)}, f32[16,4096]{1,0:T(8,128)S(1)}, f32[16,4096]{1,0:T(8,128)S(1)}, f32[16,4096]{1,0:T(8,128)S(1)}, f32[16,4096]{1,0:T...) custom-call(bf16[512,128]{1,0:T(8,128)(2,1)} %directions.1, ...), custom_call_target="tpu_custom_call" | custom-call | flops 536870912 | bytes 6291456 | tf_op jit(solution)/shard_map/products/pallas_call | solution.py:118
  5.3 3.9 %collective-permute-start.1 = (s16[16,2176]{1,0:T(8,128)(2,1)S(1)}, s16[16,2176]{1,0:T(8,128)(2,1)S(1)}, u32[]{:S(2)}, u32[]{:S(2)}) collective-permute-start(s16[16,2176]{1,0:T(8,128)(2,1)S(1)} %join.6), channel_id=1, source_target_pairs={{0,6},{1,7},{2,4},{3,5},{4,2},{5,3},{6,0},{7,1},{8,14},{9,15},{10,... | collective-permute-start | bytes 208904 | tf_op jit(solution)/shard_map/ppermute | solution.py:22
  10.3 2.9 %collective-permute-start.8 = (s16[16,2688]{1,0:T(8,128)(2,1)S(1)}, s16[16,2688]{1,0:T(8,128)(2,1)S(1)}, u32[]{:S(2)}, u32[]{:S(2)}) collective-permute-start(s16[16,2688]{1,0:T(8,128)(2,1)S(1)} %join.9), channel_id=1, source_target_pairs={{0,6},{1,7},{2,4},{3,5},{4,2},{5,3},{6,0},{7,1},{8,14},{9,15},{10,... | collective-permute-start | bytes 258056 | tf_op jit(solution)/shard_map/ppermute | solution.py:22
  14.3 0.9 %collective-permute-done.5.refs_2_ = s16[16,2176]{1,0:T(8,128)(2,1)S(1)} collective-permute-done((s16[16,2176]{1,0:T(8,128)(2,1)S(1)}, s16[16,2176]{1,0:T(8,128)(2,1)S(1)}, u32[]{:S(2)}, u32[]{:S(2)}) %collective-permute-start.5) | collective-permute-done | bytes 69664 | tf_op jit(solution)/shard_map/ppermute | solution.py:22
  15.3 1.6 %collective-permute-start.6 = (f32[8,128]{1,0:T(8,128)S(1)}, f32[8,128]{1,0:T(8,128)S(1)}, u32[]{:S(2)}, u32[]{:S(2)}) collective-permute-start(f32[8,128]{1,0:T(8,128)S(1)} %get-tuple-element.40.refs_0_), channel_id=1, source_target_pairs={{0,8},{8,0},{16,24},{24,16},{1,9},{9,1},{17,25},{25,17},{2,10},{10... | collective-permute-start | bytes 12296 | tf_op jit(solution)/shard_map/ppermute | solution.py:22
  19.0 2.7 %collective-permute-start.11 = (f32[8,128]{1,0:T(8,128)S(1)}, f32[8,128]{1,0:T(8,128)S(1)}, u32[]{:S(2)}, u32[]{:S(2)}) collective-permute-start(f32[8,128]{1,0:T(8,128)S(1)} %get-tuple-element.44.refs_0_), channel_id=1, source_target_pairs={{0,16},{8,24},{16,0},{24,8},{1,17},{9,25},{17,1},{25,9},{2,18},{10... | collective-permute-start | bytes 12296 | tf_op jit(solution)/shard_map/ppermute | solution.py:22
  21.6 1.2 %ordered_values.3 = (f32[16,2560]{1,0:T(8,128)S(1)}, f32[256,256]{1,0:T(8,128)S(1)}, f32[16,128]{1,0:T(8,128)S(1)}) custom-call(f32[16,4096]{1,0:T(8,128)S(1)} %get-tuple-element.48.own, f32[16,4096]{1,0:T(8,128)S(1)} %collective-permute-done.7.refs_1_.other, s16[16,2688]{1,0:T(8,128)(2,1)S(1)} %collective-permute-done.8.refs_3_.refs_0_, ...), custom_call_target="tpu_custom_call" | custom-call | flops 671088640 | bytes 983040 | tf_op jit(solution)/shard_map/ordered_values/pallas_call | solution.py:398
  23.7 2.6 %collective-permute-start.14 = (f32[40,128]{1,0:T(8,128)S(1)}, f32[40,128]{1,0:T(8,128)S(1)}, u32[]{:S(2)}, u32[]{:S(2)}) collective-permute-start(f32[40,128]{1,0:T(8,128)S(1)} %get-tuple-element.53.refs_0_), channel_id=1, source_target_pairs={{0,16},{8,24},{16,0},{24,8},{1,17},{9,25},{17,1},{25,9},{2,18},{10... | collective-permute-start | bytes 61448 | tf_op jit(solution)/shard_map/ppermute | solution.py:22
  26.3 1.3 %collective-permute-start.13 = (f32[40,128]{1,0:T(8,128)S(1)}, f32[40,128]{1,0:T(8,128)S(1)}, u32[]{:S(2)}, u32[]{:S(2)}) collective-permute-start(f32[40,128]{1,0:T(8,128)S(1)} %get-tuple-element.53.refs_0_), channel_id=1, source_target_pairs={{0,24},{8,16},{16,8},{24,0},{1,25},{9,17},{17,9},{25,1},{2,26},{10... | collective-permute-start | bytes 61448 | tf_op jit(solution)/shard_map/ppermute | solution.py:22
  27.9 1.8 %prefix_sums.1.refs_6_ = f32[16,4096]{1,0:T(8,128)S(1)} custom-call(f32[256,256]{1,0:T(8,128)S(1)} %suffix_sums.1.ordered.sums, f32[16,256]{1,0:T(8,128)S(1)} %get-tuple-element.56.squares.square, s32[1,4096]{1,0:T(1,128)S(1)} %bitcast.6), custom_call_target="tpu_custom_call" | custom-call | flops 1073741824 | bytes 1572864 | tf_op jit(solution)/shard_map/prefix_sums/pallas_call | solution.py:464
  29.6 0.9 %hazards.1 = (f32[1,4096]{1,0:T(1,128)S(1)}, f32[1,4096]{1,0:T(1,128)S(1)}) custom-call(f32[16,256]{1,0:T(8,128)S(1)} %get-tuple-element.57.hazard, f32[16,256]{1,0:T(8,128)S(1)} %get-tuple-element.56.squares.square, s32[1,4096]{1,0:T(1,128)S(1)} %bitcast.7), custom_call_target="tpu_custom_call" | custom-call | flops 209715200 | bytes 262144 | tf_op jit(solution)/shard_map/hazards/pallas_call | solution.py:332
  30.6 1.3 %collective-permute-done.13.refs_2_ = f32[40,128]{1,0:T(8,128)S(1)} collective-permute-done((f32[40,128]{1,0:T(8,128)S(1)}, f32[40,128]{1,0:T(8,128)S(1)}, u32[]{:S(2)}, u32[]{:S(2)}) %collective-permute-start.13) | collective-permute-done | bytes 20512 | tf_op jit(solution)/shard_map/ppermute | solution.py:22
  32.1 2.1 %collective-permute-start.17 = (bf16[16,4096]{1,0:T(8,128)(2,1)S(1)}, bf16[16,4096]{1,0:T(8,128)(2,1)S(1)}, u32[]{:S(2)}, u32[]{:S(2)}) collective-permute-start(bf16[16,4096]{1,0:T(8,128)(2,1)S(1)} %weights.1.refs_0_), channel_id=1, source_target_pairs={{0,6},{1,7},{2,4},{3,5},{4,2},{5,3},{6,0},{7,1},{8,14},{9,15},{10,... | collective-permute-start | bytes 393224 | tf_op jit(solution)/shard_map/ppermute | solution.py:22
  34.7 1.0 %collective-permute-start.15 = (bf16[16,4096]{1,0:T(8,128)(2,1)S(1)}, bf16[16,4096]{1,0:T(8,128)(2,1)S(1)}, u32[]{:S(2)}, u32[]{:S(2)}) collective-permute-start(bf16[16,4096]{1,0:T(8,128)(2,1)S(1)} %weights.1.refs_0_), channel_id=1, source_target_pairs={{0,2},{1,3},{2,0},{3,1},{4,6},{5,7},{6,4},{7,5},{8,10},{9,11},{10,... | collective-permute-start | bytes 393224 | tf_op jit(solution)/shard_map/ppermute | solution.py:22
  35.6 2.4 %collective-permute-done.17.refs_3_ = bf16[16,4096]{1,0:T(8,128)(2,1)S(1)} collective-permute-done((bf16[16,4096]{1,0:T(8,128)(2,1)S(1)}, bf16[16,4096]{1,0:T(8,128)(2,1)S(1)}, u32[]{:S(2)}, u32[]{:S(2)}) %collective-permute-start.17) | collective-permute-done | bytes 131104 | tf_op jit(solution)/shard_map/ppermute | solution.py:22
  38.0 1.4 %collective-permute-done.16.refs_2_ = bf16[16,4096]{1,0:T(8,128)(2,1)S(1)} collective-permute-done((bf16[16,4096]{1,0:T(8,128)(2,1)S(1)}, bf16[16,4096]{1,0:T(8,128)(2,1)S(1)}, u32[]{:S(2)}, u32[]{:S(2)}) %collective-permute-start.16) | collective-permute-done | bytes 131104 | tf_op jit(solution)/shard_map/ppermute | solution.py:22
  39.9 0.9 %gradients.2.mine = s16[17,16,128]{2,1,0:T(8,128)(2,1)S(1)} custom-call(bf16[16,4096]{1,0:T(8,128)(2,1)S(1)} %weights.1.refs_0_, bf16[16,4096]{1,0:T(8,128)(2,1)S(1)} %collective-permute-done.15.refs_1_, bf16[16,4096]{1,0:T(8,128)(2,1)S(1)} %collective-permute-done.16.refs_2_, bf16[16,4096]{1,0:T(8,128)(2,1)S(1)} %collective-permute-done.17.refs_3_, ...), custom_call_target="tpu_custom_call" | custom-call | flops 268435456 | bytes 4718592 | tf_op jit(solution)/shard_map/gradients/pallas_call | solution.py:562
  41.4 0.9 %gradients.3.mine = s16[17,16,128]{2,1,0:T(8,128)(2,1)S(1)} custom-call(bf16[16,4096]{1,0:T(8,128)(2,1)S(1)} %collective-permute-done.20.refs_0_, bf16[16,4096]{1,0:T(8,128)(2,1)S(1)} %collective-permute-done.21.refs_1_, bf16[16,4096]{1,0:T(8,128)(2,1)S(1)} %collective-permute-done.22.refs_2_, bf16[16,4096]{1,0:T(8,128)(2,1)S(1)} %collective-permute-done.23.refs_3_, ...), custom_call_target="tpu_custom_call" | custom-call | flops 268435456 | bytes 4718592 | tf_op jit(solution)/shard_map/gradients/pallas_call | solution.py:562
  42.3 1.6 %collective-permute-start.24 = (s16[17,16,128]{2,1,0:T(8,128)(2,1)S(1)}, s16[17,16,128]{2,1,0:T(8,128)(2,1)S(1)}, u32[]{:S(2)}, u32[]{:S(2)}) collective-permute-start(s16[17,16,128]{2,1,0:T(8,128)(2,1)S(1)} %gradients.3.mine), channel_id=1, source_target_pairs={{0,8},{8,0},{16,24},{24,16},{1,9},{9,1},{17,25},{25,17},{2,10},{10... | collective-permute-start | bytes 208904 | tf_op jit(solution)/shard_map/ppermute | solution.py:22
  43.9 1.6 %collective-permute-done.18.other = s16[17,16,128]{2,1,0:T(8,128)(2,1)S(1)} collective-permute-done((s16[17,16,128]{2,1,0:T(8,128)(2,1)S(1)}, s16[17,16,128]{2,1,0:T(8,128)(2,1)S(1)}, u32[]{:S(2)}, u32[]{:S(2)}) %collective-permute-start.18) | collective-permute-done | bytes 69664 | tf_op jit(solution)/shard_map/ppermute | solution.py:22
  45.6 1.3 %collective-permute-start.19 = (s16[17,16,128]{2,1,0:T(8,128)(2,1)S(1)}, s16[17,16,128]{2,1,0:T(8,128)(2,1)S(1)}, u32[]{:S(2)}, u32[]{:S(2)}) collective-permute-start(s16[17,16,128]{2,1,0:T(8,128)(2,1)S(1)} %merge.2.mine), channel_id=1, source_target_pairs={{0,16},{8,24},{16,0},{24,8},{1,17},{9,25},{17,1},{25,9},{2,18},{10... | collective-permute-start | bytes 208904 | tf_op jit(solution)/shard_map/ppermute | solution.py:22
  46.9 2.0 %collective-permute-start.25 = (s16[17,16,128]{2,1,0:T(8,128)(2,1)S(1)}, s16[17,16,128]{2,1,0:T(8,128)(2,1)S(1)}, u32[]{:S(2)}, u32[]{:S(2)}) collective-permute-start(s16[17,16,128]{2,1,0:T(8,128)(2,1)S(1)} %merge.3.mine), channel_id=1, source_target_pairs={{0,16},{8,24},{16,0},{24,8},{1,17},{9,25},{17,1},{25,9},{2,18},{10... | collective-permute-start | bytes 208904 | tf_op jit(solution)/shard_map/ppermute | solution.py:22
  48.9 4.6 %collective-permute-done.19.other = s16[17,16,128]{2,1,0:T(8,128)(2,1)S(1)} collective-permute-done((s16[17,16,128]{2,1,0:T(8,128)(2,1)S(1)}, s16[17,16,128]{2,1,0:T(8,128)(2,1)S(1)}, u32[]{:S(2)}, u32[]{:S(2)}) %collective-permute-start.19) | collective-permute-done | bytes 69664 | tf_op jit(solution)/shard_map/ppermute | solution.py:22
  54.2 0.9 %finish.1 = f32[512,128]{1,0:T(8,128)} custom-call(f32[64,512]{1,0:T(8,128)S(1)} %add.1.first, s16[17,16,128]{2,1,0:T(8,128)(2,1)S(1)} %merge.3.mine, s16[17,16,128]{2,1,0:T(8,128)(2,1)S(1)} %collective-permute-done.25.other, f32[8,128]{1,0:T(8,128)S(1)} %get-tuple-element.60.count), custom_call_target="tpu_custom_call" | custom-call | tf_op jit(solution)/shard_map/finish/pallas_call | solution.py:632
  (61 shorter events, 10.0 us)
Async XLA Ops:
  3.9 5.3 %collective-permute-start.2 = (f32[16,4096]{1,0:T(8,128)S(1)}, f32[16,4096]{1,0:T(8,128)S(1)}, u32[]{:S(2)}, u32[]{:S(2)}) collective-permute-start(f32[16,4096]{1,0:T(8,128)S(1)} %get-tuple-element.37), channel_id=1, source_target_pairs={{0,1},{1,0},{2,3},{3,2},{4,5},{5,4},{6,7},{7,6},{8,9},{9,8},{10,11... | collective-permute-start | bytes 786440 | tf_op jit(solution)/shard_map/ppermute | solution.py:22
  4.0 5.9 %collective-permute-start.4 = (f32[16,4096]{1,0:T(8,128)S(1)}, f32[16,4096]{1,0:T(8,128)S(1)}, u32[]{:S(2)}, u32[]{:S(2)}) collective-permute-start(f32[16,4096]{1,0:T(8,128)S(1)} %get-tuple-element.39), channel_id=1, source_target_pairs={{0,1},{1,0},{2,3},{3,2},{4,5},{5,4},{6,7},{7,6},{8,9},{9,8},{10,11... | collective-permute-start | bytes 786440 | tf_op jit(solution)/shard_map/ppermute | solution.py:22
  4.4 5.8 %collective-permute-start.7 = (f32[16,4096]{1,0:T(8,128)S(1)}, f32[16,4096]{1,0:T(8,128)S(1)}, u32[]{:S(2)}, u32[]{:S(2)}) collective-permute-start(f32[16,4096]{1,0:T(8,128)S(1)} %get-tuple-element.41), channel_id=1, source_target_pairs={{0,1},{1,0},{2,3},{3,2},{4,5},{5,4},{6,7},{7,6},{8,9},{9,8},{10,11... | collective-permute-start | bytes 786440 | tf_op jit(solution)/shard_map/ppermute | solution.py:22
  5.3 8.8 %collective-permute-start.1 = (s16[16,2176]{1,0:T(8,128)(2,1)S(1)}, s16[16,2176]{1,0:T(8,128)(2,1)S(1)}, u32[]{:S(2)}, u32[]{:S(2)}) collective-permute-start(s16[16,2176]{1,0:T(8,128)(2,1)S(1)} %join.6), channel_id=1, source_target_pairs={{0,6},{1,7},{2,4},{3,5},{4,2},{5,3},{6,0},{7,1},{8,14},{9,15},{10,... | collective-permute-start | bytes 208904 | tf_op jit(solution)/shard_map/ppermute | solution.py:22
  9.3 4.9 %collective-permute-start.3 = (s16[16,2176]{1,0:T(8,128)(2,1)S(1)}, s16[16,2176]{1,0:T(8,128)(2,1)S(1)}, u32[]{:S(2)}, u32[]{:S(2)}) collective-permute-start(s16[16,2176]{1,0:T(8,128)(2,1)S(1)} %join.7), channel_id=1, source_target_pairs={{0,4},{1,5},{2,6},{3,7},{4,0},{5,1},{6,2},{7,3},{8,12},{9,13},{10,... | collective-permute-start | bytes 208904 | tf_op jit(solution)/shard_map/ppermute | solution.py:22
  10.0 5.1 %collective-permute-start.5 = (s16[16,2176]{1,0:T(8,128)(2,1)S(1)}, s16[16,2176]{1,0:T(8,128)(2,1)S(1)}, u32[]{:S(2)}, u32[]{:S(2)}) collective-permute-start(s16[16,2176]{1,0:T(8,128)(2,1)S(1)} %join.8), channel_id=1, source_target_pairs={{0,2},{1,3},{2,0},{3,1},{4,6},{5,7},{6,4},{7,5},{8,10},{9,11},{10,... | collective-permute-start | bytes 208904 | tf_op jit(solution)/shard_map/ppermute | solution.py:22
  10.3 8.6 %collective-permute-start.8 = (s16[16,2688]{1,0:T(8,128)(2,1)S(1)}, s16[16,2688]{1,0:T(8,128)(2,1)S(1)}, u32[]{:S(2)}, u32[]{:S(2)}) collective-permute-start(s16[16,2688]{1,0:T(8,128)(2,1)S(1)} %join.9), channel_id=1, source_target_pairs={{0,6},{1,7},{2,4},{3,5},{4,2},{5,3},{6,0},{7,1},{8,14},{9,15},{10,... | collective-permute-start | bytes 258056 | tf_op jit(solution)/shard_map/ppermute | solution.py:22
  13.4 5.6 %collective-permute-start.9 = (s16[16,2688]{1,0:T(8,128)(2,1)S(1)}, s16[16,2688]{1,0:T(8,128)(2,1)S(1)}, u32[]{:S(2)}, u32[]{:S(2)}) collective-permute-start(s16[16,2688]{1,0:T(8,128)(2,1)S(1)} %join.10), channel_id=1, source_target_pairs={{0,4},{1,5},{2,6},{3,7},{4,0},{5,1},{6,2},{7,3},{8,12},{9,13},{10,... | collective-permute-start | bytes 258056 | tf_op jit(solution)/shard_map/ppermute | solution.py:22
  14.1 4.9 %collective-permute-start.10 = (s16[16,2688]{1,0:T(8,128)(2,1)S(1)}, s16[16,2688]{1,0:T(8,128)(2,1)S(1)}, u32[]{:S(2)}, u32[]{:S(2)}) collective-permute-start(s16[16,2688]{1,0:T(8,128)(2,1)S(1)} %join.11), channel_id=1, source_target_pairs={{0,2},{1,3},{2,0},{3,1},{4,6},{5,7},{6,4},{7,5},{8,10},{9,11},{10,... | collective-permute-start | bytes 258056 | tf_op jit(solution)/shard_map/ppermute | solution.py:22
  15.3 3.6 %collective-permute-start.6 = (f32[8,128]{1,0:T(8,128)S(1)}, f32[8,128]{1,0:T(8,128)S(1)}, u32[]{:S(2)}, u32[]{:S(2)}) collective-permute-start(f32[8,128]{1,0:T(8,128)S(1)} %get-tuple-element.40.refs_0_), channel_id=1, source_target_pairs={{0,8},{8,0},{16,24},{24,16},{1,9},{9,1},{17,25},{25,17},{2,10},{10... | collective-permute-start | bytes 12296 | tf_op jit(solution)/shard_map/ppermute | solution.py:22
  19.0 4.6 %collective-permute-start.11 = (f32[8,128]{1,0:T(8,128)S(1)}, f32[8,128]{1,0:T(8,128)S(1)}, u32[]{:S(2)}, u32[]{:S(2)}) collective-permute-start(f32[8,128]{1,0:T(8,128)S(1)} %get-tuple-element.44.refs_0_), channel_id=1, source_target_pairs={{0,16},{8,24},{16,0},{24,8},{1,17},{9,25},{17,1},{25,9},{2,18},{10... | collective-permute-start | bytes 12296 | tf_op jit(solution)/shard_map/ppermute | solution.py:22
  23.7 6.8 %collective-permute-start.14 = (f32[40,128]{1,0:T(8,128)S(1)}, f32[40,128]{1,0:T(8,128)S(1)}, u32[]{:S(2)}, u32[]{:S(2)}) collective-permute-start(f32[40,128]{1,0:T(8,128)S(1)} %get-tuple-element.53.refs_0_), channel_id=1, source_target_pairs={{0,16},{8,24},{16,0},{24,8},{1,17},{9,25},{17,1},{25,9},{2,18},{10... | collective-permute-start | bytes 61448 | tf_op jit(solution)/shard_map/ppermute | solution.py:22
  26.3 5.6 %collective-permute-start.13 = (f32[40,128]{1,0:T(8,128)S(1)}, f32[40,128]{1,0:T(8,128)S(1)}, u32[]{:S(2)}, u32[]{:S(2)}) collective-permute-start(f32[40,128]{1,0:T(8,128)S(1)} %get-tuple-element.53.refs_0_), channel_id=1, source_target_pairs={{0,24},{8,16},{16,8},{24,0},{1,25},{9,17},{17,9},{25,1},{2,26},{10... | collective-permute-start | bytes 61448 | tf_op jit(solution)/shard_map/ppermute | solution.py:22
  27.7 4.2 %collective-permute-start.12 = (f32[40,128]{1,0:T(8,128)S(1)}, f32[40,128]{1,0:T(8,128)S(1)}, u32[]{:S(2)}, u32[]{:S(2)}) collective-permute-start(f32[40,128]{1,0:T(8,128)S(1)} %get-tuple-element.53.refs_0_), channel_id=1, source_target_pairs={{0,8},{8,0},{16,24},{24,16},{1,9},{9,1},{17,25},{25,17},{2,10},{10... | collective-permute-start | bytes 61448 | tf_op jit(solution)/shard_map/ppermute | solution.py:22
  32.1 6.0 %collective-permute-start.17 = (bf16[16,4096]{1,0:T(8,128)(2,1)S(1)}, bf16[16,4096]{1,0:T(8,128)(2,1)S(1)}, u32[]{:S(2)}, u32[]{:S(2)}) collective-permute-start(bf16[16,4096]{1,0:T(8,128)(2,1)S(1)} %weights.1.refs_0_), channel_id=1, source_target_pairs={{0,6},{1,7},{2,4},{3,5},{4,2},{5,3},{6,0},{7,1},{8,14},{9,15},{10,... | collective-permute-start | bytes 393224 | tf_op jit(solution)/shard_map/ppermute | solution.py:22
  34.1 5.3 %collective-permute-start.16 = (bf16[16,4096]{1,0:T(8,128)(2,1)S(1)}, bf16[16,4096]{1,0:T(8,128)(2,1)S(1)}, u32[]{:S(2)}, u32[]{:S(2)}) collective-permute-start(bf16[16,4096]{1,0:T(8,128)(2,1)S(1)} %weights.1.refs_0_), channel_id=1, source_target_pairs={{0,4},{1,5},{2,6},{3,7},{4,0},{5,1},{6,2},{7,3},{8,12},{9,13},{10,... | collective-permute-start | bytes 393224 | tf_op jit(solution)/shard_map/ppermute | solution.py:22
  34.7 5.0 %collective-permute-start.15 = (bf16[16,4096]{1,0:T(8,128)(2,1)S(1)}, bf16[16,4096]{1,0:T(8,128)(2,1)S(1)}, u32[]{:S(2)}, u32[]{:S(2)}) collective-permute-start(bf16[16,4096]{1,0:T(8,128)(2,1)S(1)} %weights.1.refs_0_), channel_id=1, source_target_pairs={{0,2},{1,3},{2,0},{3,1},{4,6},{5,7},{6,4},{7,5},{8,10},{9,11},{10,... | collective-permute-start | bytes 393224 | tf_op jit(solution)/shard_map/ppermute | solution.py:22
  35.6 5.7 %collective-permute-start.20 = (bf16[16,4096]{1,0:T(8,128)(2,1)S(1)}, bf16[16,4096]{1,0:T(8,128)(2,1)S(1)}, u32[]{:S(2)}, u32[]{:S(2)}) collective-permute-start(bf16[16,4096]{1,0:T(8,128)(2,1)S(1)} %weights.1.refs_0_), channel_id=1, source_target_pairs={{0,1},{1,0},{2,3},{3,2},{4,5},{5,4},{6,7},{7,6},{8,9},{9,8},{10,11... | collective-permute-start | bytes 393224 | tf_op jit(solution)/shard_map/ppermute | solution.py:22
  38.0 3.3 %collective-permute-start.23 = (bf16[16,4096]{1,0:T(8,128)(2,1)S(1)}, bf16[16,4096]{1,0:T(8,128)(2,1)S(1)}, u32[]{:S(2)}, u32[]{:S(2)}) collective-permute-start(bf16[16,4096]{1,0:T(8,128)(2,1)S(1)} %collective-permute-done.17.refs_3_), channel_id=1, source_target_pairs={{0,1},{1,0},{2,3},{3,2},{4,5},{5,4},{6,7},{7,6},{8,9},{9,8},{10,11... | collective-permute-start | bytes 393224 | tf_op jit(solution)/shard_map/ppermute | solution.py:22
  39.4 2.0 %collective-permute-start.22 = (bf16[16,4096]{1,0:T(8,128)(2,1)S(1)}, bf16[16,4096]{1,0:T(8,128)(2,1)S(1)}, u32[]{:S(2)}, u32[]{:S(2)}) collective-permute-start(bf16[16,4096]{1,0:T(8,128)(2,1)S(1)} %collective-permute-done.16.refs_2_), channel_id=1, source_target_pairs={{0,1},{1,0},{2,3},{3,2},{4,5},{5,4},{6,7},{7,6},{8,9},{9,8},{10,11... | collective-permute-start | bytes 393224 | tf_op jit(solution)/shard_map/ppermute | solution.py:22
  40.8 4.7 %collective-permute-start.18 = (s16[17,16,128]{2,1,0:T(8,128)(2,1)S(1)}, s16[17,16,128]{2,1,0:T(8,128)(2,1)S(1)}, u32[]{:S(2)}, u32[]{:S(2)}) collective-permute-start(s16[17,16,128]{2,1,0:T(8,128)(2,1)S(1)} %gradients.2.mine), channel_id=1, source_target_pairs={{0,8},{8,0},{16,24},{24,16},{1,9},{9,1},{17,25},{25,17},{2,10},{10... | collective-permute-start | bytes 208904 | tf_op jit(solution)/shard_map/ppermute | solution.py:22
  42.3 4.6 %collective-permute-start.24 = (s16[17,16,128]{2,1,0:T(8,128)(2,1)S(1)}, s16[17,16,128]{2,1,0:T(8,128)(2,1)S(1)}, u32[]{:S(2)}, u32[]{:S(2)}) collective-permute-start(s16[17,16,128]{2,1,0:T(8,128)(2,1)S(1)} %gradients.3.mine), channel_id=1, source_target_pairs={{0,8},{8,0},{16,24},{24,16},{1,9},{9,1},{17,25},{25,17},{2,10},{10... | collective-permute-start | bytes 208904 | tf_op jit(solution)/shard_map/ppermute | solution.py:22
  45.6 7.9 %collective-permute-start.19 = (s16[17,16,128]{2,1,0:T(8,128)(2,1)S(1)}, s16[17,16,128]{2,1,0:T(8,128)(2,1)S(1)}, u32[]{:S(2)}, u32[]{:S(2)}) collective-permute-start(s16[17,16,128]{2,1,0:T(8,128)(2,1)S(1)} %merge.2.mine), channel_id=1, source_target_pairs={{0,16},{8,24},{16,0},{24,8},{1,17},{9,25},{17,1},{25,9},{2,18},{10... | collective-permute-start | bytes 208904 | tf_op jit(solution)/shard_map/ppermute | solution.py:22
  46.9 7.3 %collective-permute-start.25 = (s16[17,16,128]{2,1,0:T(8,128)(2,1)S(1)}, s16[17,16,128]{2,1,0:T(8,128)(2,1)S(1)}, u32[]{:S(2)}, u32[]{:S(2)}) collective-permute-start(s16[17,16,128]{2,1,0:T(8,128)(2,1)S(1)} %merge.3.mine), channel_id=1, source_target_pairs={{0,16},{8,24},{16,0},{24,8},{1,17},{9,25},{17,1},{25,9},{2,18},{10... | collective-permute-start | bytes 208904 | tf_op jit(solution)/shard_map/ppermute | solution.py:22
  (5 other events, 39.6 us)

commit v23 on v20

--- a/solution.py
+++ b/solution.py
@@ -566,6 +566,23 @@
     )(*pieces, dosages)
 
 
+def hold_kernel(parts, *refs):
+    for piece, out in zip(refs[:parts], refs[parts + 1 :]):
+        out[...] = piece[...]
+
+
+def hold(pieces, waited):
+    parts = len(pieces)
+    return pl.pallas_call(
+        functools.partial(hold_kernel, parts),
+        in_specs=[VMEM] * parts + [pl.BlockSpec(memory_space=pl.ANY)],
+        out_shape=[jax.ShapeDtypeStruct(piece.shape, piece.dtype) for piece in pieces],
+        out_specs=[VMEM] * parts,
+        compiler_params=pltpu.CompilerParams(**PARAMS),
+        name="hold",
+    )(*pieces, waited)
+
+
 def merge_kernel(columns, mine, other, out):
     encode(decode_sum(mine, other, columns), out)
 
@@ -685,8 +702,9 @@
     for q in range(1, feat // 2):
         chips[q] = swap(own, "feat", 2 * q)
     near = [chips[q] for q in range(feat // 2)]
-    far = [swap(chips[q], "feat", 1) for q in range(feat // 2)]
-    partial_sums = [gradients(pieces, dosages) for pieces in (near, far)]
+    first_sum = gradients(near, dosages)
+    far = [swap(piece, "feat", 1) for piece in hold(near, first_sum)]
+    partial_sums = [first_sum, gradients(far, dosages)]
     bit = 1
     while 2 * bit < ex:
         received = [swap(message, "ex", bit) for message in partial_sums]

time: 55.1 us -> 55.9 us (1.015)
  transfers between devices with their start and end apart: 26 -> 26, of which waited for: 10 -> 14; matrix products, arithmetic and copies ran while one was open for 0% -> 0% of each run, Pallas kernels for 17% -> 15%
where the time goes in v23:
time: 55.9 us; the launch traced here: 55.7 us
  starting transfers between devices  28.5 us (51%)
  Pallas kernels  13.9 us (25%)
  waiting for transfers between devices  13.1 us (23%)
    ppermute x26, starting transfers between devices, swap(): return lax.ppermute(x, axis, [(s, s ^ i) for s in range(count)])  28.5 us
    ppermute x26, waiting for transfers between devices, swap(): return lax.ppermute(x, axis, [(s, s ^ i) for s in range(count)])  13.1 us
    pallas_call x1, Pallas kernels, products(): pl.pallas_call(functools.partial(product_kernel, feat, kf, chunk), in_spe...  3.35 us
    pallas_call x2, Pallas kernels, ordered_values(): pl.pallas_call(functools.partial(order_kernel, start, len(messages)), in_...  1.97 us
    pallas_call x2, Pallas kernels, gradients(): pl.pallas_call(functools.partial(gradient_kernel, parts, kf), in_specs=[V...  1.77 us
    pallas_call x1, Pallas kernels, prefix_sums(): pl.pallas_call(prefix_kernel, in_specs=[VMEM] * 3, out_shape=jax.ShapeDty...  1.75 us
  transfers between devices with their start and end apart: 26, of which 14 were waited for; matrix products, arithmetic and copies ran while one was open for 0% of the time, Pallas kernels for 15%

profile of v23, /device:TPU:0, one launch (start us, length us, event | category | flops | bytes accessed | tf_op | source)
XLA Modules:
  0.0 55.7 jit_solution(7845087499686183171)
XLA Ops:
  0.0 3.3 %products.1 = (f32[16,256]{1,0:T(8,128)S(1)}, f32[16,4096]{1,0:T(8,128)S(1)}, f32[16,4096]{1,0:T(8,128)S(1)}, f32[16,4096]{1,0:T(8,128)S(1)}, f32[16,4096]{1,0:T...) custom-call(bf16[512,128]{1,0:T(8,128)(2,1)} %directions.1, ...), custom_call_target="tpu_custom_call" | custom-call | flops 536870912 | bytes 6291456 | tf_op jit(solution)/shard_map/products/pallas_call | solution.py:117
  5.3 3.9 %collective-permute-start.1 = (s16[16,2176]{1,0:T(8,128)(2,1)S(1)}, s16[16,2176]{1,0:T(8,128)(2,1)S(1)}, u32[]{:S(2)}, u32[]{:S(2)}) collective-permute-start(s16[16,2176]{1,0:T(8,128)(2,1)S(1)} %join.6), channel_id=1, source_target_pairs={{0,6},{1,7},{2,4},{3,5},{4,2},{5,3},{6,0},{7,1},{8,14},{9,15},{10,... | collective-permute-start | bytes 208904 | tf_op jit(solution)/shard_map/ppermute | solution.py:22
  10.3 2.9 %collective-permute-start.8 = (s16[16,2688]{1,0:T(8,128)(2,1)S(1)}, s16[16,2688]{1,0:T(8,128)(2,1)S(1)}, u32[]{:S(2)}, u32[]{:S(2)}) collective-permute-start(s16[16,2688]{1,0:T(8,128)(2,1)S(1)} %join.9), channel_id=1, source_target_pairs={{0,6},{1,7},{2,4},{3,5},{4,2},{5,3},{6,0},{7,1},{8,14},{9,15},{10,... | collective-permute-start | bytes 258056 | tf_op jit(solution)/shard_map/ppermute | solution.py:22
  14.3 0.9 %collective-permute-done.5.refs_2_ = s16[16,2176]{1,0:T(8,128)(2,1)S(1)} collective-permute-done((s16[16,2176]{1,0:T(8,128)(2,1)S(1)}, s16[16,2176]{1,0:T(8,128)(2,1)S(1)}, u32[]{:S(2)}, u32[]{:S(2)}) %collective-permute-start.5) | collective-permute-done | bytes 69664 | tf_op jit(solution)/shard_map/ppermute | solution.py:22
  15.3 1.6 %collective-permute-start.6 = (f32[8,128]{1,0:T(8,128)S(1)}, f32[8,128]{1,0:T(8,128)S(1)}, u32[]{:S(2)}, u32[]{:S(2)}) collective-permute-start(f32[8,128]{1,0:T(8,128)S(1)} %get-tuple-element.44.refs_0_), channel_id=1, source_target_pairs={{0,8},{8,0},{16,24},{24,16},{1,9},{9,1},{17,25},{25,17},{2,10},{10... | collective-permute-start | bytes 12296 | tf_op jit(solution)/shard_map/ppermute | solution.py:22
  19.0 2.7 %collective-permute-start.11 = (f32[8,128]{1,0:T(8,128)S(1)}, f32[8,128]{1,0:T(8,128)S(1)}, u32[]{:S(2)}, u32[]{:S(2)}) collective-permute-start(f32[8,128]{1,0:T(8,128)S(1)} %get-tuple-element.48.refs_0_), channel_id=1, source_target_pairs={{0,16},{8,24},{16,0},{24,8},{1,17},{9,25},{17,1},{25,9},{2,18},{10... | collective-permute-start | bytes 12296 | tf_op jit(solution)/shard_map/ppermute | solution.py:22
  21.6 1.2 %ordered_values.3 = (f32[16,2560]{1,0:T(8,128)S(1)}, f32[256,256]{1,0:T(8,128)S(1)}, f32[16,128]{1,0:T(8,128)S(1)}) custom-call(f32[16,4096]{1,0:T(8,128)S(1)} %get-tuple-element.52.own, f32[16,4096]{1,0:T(8,128)S(1)} %collective-permute-done.7.refs_1_.other, s16[16,2688]{1,0:T(8,128)(2,1)S(1)} %collective-permute-done.8.refs_3_.refs_0_, ...), custom_call_target="tpu_custom_call" | custom-call | flops 671088640 | bytes 983040 | tf_op jit(solution)/shard_map/ordered_values/pallas_call | solution.py:397
  23.7 3.7 %collective-permute-start.14 = (f32[40,128]{1,0:T(8,128)S(1)}, f32[40,128]{1,0:T(8,128)S(1)}, u32[]{:S(2)}, u32[]{:S(2)}) collective-permute-start(f32[40,128]{1,0:T(8,128)S(1)} %get-tuple-element.57.refs_0_), channel_id=1, source_target_pairs={{0,24},{8,16},{16,8},{24,0},{1,25},{9,17},{17,9},{25,1},{2,26},{10... | collective-permute-start | bytes 61448 | tf_op jit(solution)/shard_map/ppermute | solution.py:22
  28.1 1.7 %prefix_sums.1.refs_6_ = f32[16,4096]{1,0:T(8,128)S(1)} custom-call(f32[256,256]{1,0:T(8,128)S(1)} %suffix_sums.1.ordered.sums, f32[16,256]{1,0:T(8,128)S(1)} %get-tuple-element.60.squares.square, s32[1,4096]{1,0:T(1,128)S(1)} %bitcast.6), custom_call_target="tpu_custom_call" | custom-call | flops 1073741824 | bytes 1572864 | tf_op jit(solution)/shard_map/prefix_sums/pallas_call | solution.py:463
  29.9 0.9 %hazards.1 = (f32[1,4096]{1,0:T(1,128)S(1)}, f32[1,4096]{1,0:T(1,128)S(1)}) custom-call(f32[16,256]{1,0:T(8,128)S(1)} %get-tuple-element.61.hazard, f32[16,256]{1,0:T(8,128)S(1)} %get-tuple-element.60.squares.square, s32[1,4096]{1,0:T(1,128)S(1)} %bitcast.7), custom_call_target="tpu_custom_call" | custom-call | flops 209715200 | bytes 262144 | tf_op jit(solution)/shard_map/hazards/pallas_call | solution.py:331
  30.8 1.3 %collective-permute-done.13.refs_2_ = f32[40,128]{1,0:T(8,128)S(1)} collective-permute-done((f32[40,128]{1,0:T(8,128)S(1)}, f32[40,128]{1,0:T(8,128)S(1)}, u32[]{:S(2)}, u32[]{:S(2)}) %collective-permute-start.13) | collective-permute-done | bytes 20512 | tf_op jit(solution)/shard_map/ppermute | solution.py:22
  32.3 2.0 %collective-permute-start.17 = (bf16[16,4096]{1,0:T(8,128)(2,1)S(1)}, bf16[16,4096]{1,0:T(8,128)(2,1)S(1)}, u32[]{:S(2)}, u32[]{:S(2)}) collective-permute-start(bf16[16,4096]{1,0:T(8,128)(2,1)S(1)} %weights.1.refs_0_), channel_id=1, source_target_pairs={{0,6},{1,7},{2,4},{3,5},{4,2},{5,3},{6,0},{7,1},{8,14},{9,15},{10,... | collective-permute-start | bytes 393224 | tf_op jit(solution)/shard_map/ppermute | solution.py:22
  34.8 1.0 %collective-permute-start.15 = (bf16[16,4096]{1,0:T(8,128)(2,1)S(1)}, bf16[16,4096]{1,0:T(8,128)(2,1)S(1)}, u32[]{:S(2)}, u32[]{:S(2)}) collective-permute-start(bf16[16,4096]{1,0:T(8,128)(2,1)S(1)} %weights.1.refs_0_), channel_id=1, source_target_pairs={{0,2},{1,3},{2,0},{3,1},{4,6},{5,7},{6,4},{7,5},{8,10},{9,11},{10,... | collective-permute-start | bytes 393224 | tf_op jit(solution)/shard_map/ppermute | solution.py:22
  35.8 2.4 %collective-permute-done.17.refs_3_ = bf16[16,4096]{1,0:T(8,128)(2,1)S(1)} collective-permute-done((bf16[16,4096]{1,0:T(8,128)(2,1)S(1)}, bf16[16,4096]{1,0:T(8,128)(2,1)S(1)}, u32[]{:S(2)}, u32[]{:S(2)}) %collective-permute-start.17) | collective-permute-done | bytes 131104 | tf_op jit(solution)/shard_map/ppermute | solution.py:22
  38.2 1.4 %collective-permute-done.16.refs_2_ = bf16[16,4096]{1,0:T(8,128)(2,1)S(1)} collective-permute-done((bf16[16,4096]{1,0:T(8,128)(2,1)S(1)}, bf16[16,4096]{1,0:T(8,128)(2,1)S(1)}, u32[]{:S(2)}, u32[]{:S(2)}) %collective-permute-start.16) | collective-permute-done | bytes 131104 | tf_op jit(solution)/shard_map/ppermute | solution.py:22
  39.7 0.9 %gradients.2.mine.refs_4_ = s16[17,16,128]{2,1,0:T(8,128)(2,1)S(1)} custom-call(bf16[16,4096]{1,0:T(8,128)(2,1)S(1)} %weights.1.refs_0_, bf16[16,4096]{1,0:T(8,128)(2,1)S(1)} %collective-permute-done.15.refs_1_, bf16[16,4096]{1,0:T(8,128)(2,1)S(1)} %collective-permute-done.16.refs_2_, bf16[16,4096]{1,0:T(8,128)(2,1)S(1)} %collective-permute-done.17.refs_3_, ...), custom_call_target="tpu_custom_call" | custom-call | flops 268435456 | bytes 4718592 | tf_op jit(solution)/shard_map/gradients/pallas_call | solution.py:555
  42.8 0.9 %gradients.3.mine = s16[17,16,128]{2,1,0:T(8,128)(2,1)S(1)} custom-call(bf16[16,4096]{1,0:T(8,128)(2,1)S(1)} %collective-permute-done.20.refs_0_, bf16[16,4096]{1,0:T(8,128)(2,1)S(1)} %collective-permute-done.21.refs_1_, bf16[16,4096]{1,0:T(8,128)(2,1)S(1)} %collective-permute-done.22.refs_2_, bf16[16,4096]{1,0:T(8,128)(2,1)S(1)} %collective-permute-done.23.refs_3_, ...), custom_call_target="tpu_custom_call" | custom-call | flops 268435456 | bytes 4718592 | tf_op jit(solution)/shard_map/gradients/pallas_call | solution.py:555
  43.7 1.1 %collective-permute-start.24 = (s16[17,16,128]{2,1,0:T(8,128)(2,1)S(1)}, s16[17,16,128]{2,1,0:T(8,128)(2,1)S(1)}, u32[]{:S(2)}, u32[]{:S(2)}) collective-permute-start(s16[17,16,128]{2,1,0:T(8,128)(2,1)S(1)} %gradients.3.mine), channel_id=1, source_target_pairs={{0,8},{8,0},{16,24},{24,16},{1,9},{9,1},{17,25},{25,17},{2,10},{10... | collective-permute-start | bytes 208904 | tf_op jit(solution)/shard_map/ppermute | solution.py:22
  44.8 1.3 %collective-permute-done.18.other = s16[17,16,128]{2,1,0:T(8,128)(2,1)S(1)} collective-permute-done((s16[17,16,128]{2,1,0:T(8,128)(2,1)S(1)}, s16[17,16,128]{2,1,0:T(8,128)(2,1)S(1)}, u32[]{:S(2)}, u32[]{:S(2)}) %collective-permute-start.18) | collective-permute-done | bytes 69664 | tf_op jit(solution)/shard_map/ppermute | solution.py:22
  46.2 2.1 %collective-permute-start.19 = (s16[17,16,128]{2,1,0:T(8,128)(2,1)S(1)}, s16[17,16,128]{2,1,0:T(8,128)(2,1)S(1)}, u32[]{:S(2)}, u32[]{:S(2)}) collective-permute-start(s16[17,16,128]{2,1,0:T(8,128)(2,1)S(1)} %merge.2.mine), channel_id=1, source_target_pairs={{0,16},{8,24},{16,0},{24,8},{1,17},{9,25},{17,1},{25,9},{2,18},{10... | collective-permute-start | bytes 208904 | tf_op jit(solution)/shard_map/ppermute | solution.py:22
  48.3 2.6 %collective-permute-start.25 = (s16[17,16,128]{2,1,0:T(8,128)(2,1)S(1)}, s16[17,16,128]{2,1,0:T(8,128)(2,1)S(1)}, u32[]{:S(2)}, u32[]{:S(2)}) collective-permute-start(s16[17,16,128]{2,1,0:T(8,128)(2,1)S(1)} %merge.3.mine), channel_id=1, source_target_pairs={{0,16},{8,24},{16,0},{24,8},{1,17},{9,25},{17,1},{25,9},{2,18},{10... | collective-permute-start | bytes 208904 | tf_op jit(solution)/shard_map/ppermute | solution.py:22
  50.9 2.4 %collective-permute-done.19.other = s16[17,16,128]{2,1,0:T(8,128)(2,1)S(1)} collective-permute-done((s16[17,16,128]{2,1,0:T(8,128)(2,1)S(1)}, s16[17,16,128]{2,1,0:T(8,128)(2,1)S(1)}, u32[]{:S(2)}, u32[]{:S(2)}) %collective-permute-start.19) | collective-permute-done | bytes 69664 | tf_op jit(solution)/shard_map/ppermute | solution.py:22
  53.3 1.5 %collective-permute-done.25.other = s16[17,16,128]{2,1,0:T(8,128)(2,1)S(1)} collective-permute-done((s16[17,16,128]{2,1,0:T(8,128)(2,1)S(1)}, s16[17,16,128]{2,1,0:T(8,128)(2,1)S(1)}, u32[]{:S(2)}, u32[]{:S(2)}) %collective-permute-start.25) | collective-permute-done | bytes 69664 | tf_op jit(solution)/shard_map/ppermute | solution.py:22
  54.8 0.9 %finish.1 = f32[512,128]{1,0:T(8,128)} custom-call(f32[64,512]{1,0:T(8,128)S(1)} %add.1.first, s16[17,16,128]{2,1,0:T(8,128)(2,1)S(1)} %merge.3.mine, s16[17,16,128]{2,1,0:T(8,128)(2,1)S(1)} %collective-permute-done.25.other, f32[8,128]{1,0:T(8,128)S(1)} %get-tuple-element.68.count), custom_call_target="tpu_custom_call" | custom-call | tf_op jit(solution)/shard_map/finish/pallas_call | solution.py:643
  (62 shorter events, 10.9 us)
Async XLA Ops:
  3.4 1.8 %collective-permute-start = (f32[16,4352]{1,0:T(8,128)S(1)}, f32[16,4352]{1,0:T(8,128)S(1)}, u32[]{:S(2)}, u32[]{:S(2)}) collective-permute-start(f32[16,4352]{1,0:T(8,128)S(1)} %get-tuple-element.38), channel_id=1, source_target_pairs={{0,1},{1,0},{2,3},{3,2},{4,5},{5,4},{6,7},{7,6},{8,9},{9,8},{10,11... | collective-permute-start | bytes 835592 | tf_op jit(solution)/shard_map/ppermute | solution.py:22
  3.9 5.3 %collective-permute-start.2 = (f32[16,4096]{1,0:T(8,128)S(1)}, f32[16,4096]{1,0:T(8,128)S(1)}, u32[]{:S(2)}, u32[]{:S(2)}) collective-permute-start(f32[16,4096]{1,0:T(8,128)S(1)} %get-tuple-element.41), channel_id=1, source_target_pairs={{0,1},{1,0},{2,3},{3,2},{4,5},{5,4},{6,7},{7,6},{8,9},{9,8},{10,11... | collective-permute-start | bytes 786440 | tf_op jit(solution)/shard_map/ppermute | solution.py:22
  4.0 5.9 %collective-permute-start.4 = (f32[16,4096]{1,0:T(8,128)S(1)}, f32[16,4096]{1,0:T(8,128)S(1)}, u32[]{:S(2)}, u32[]{:S(2)}) collective-permute-start(f32[16,4096]{1,0:T(8,128)S(1)} %get-tuple-element.43), channel_id=1, source_target_pairs={{0,1},{1,0},{2,3},{3,2},{4,5},{5,4},{6,7},{7,6},{8,9},{9,8},{10,11... | collective-permute-start | bytes 786440 | tf_op jit(solution)/shard_map/ppermute | solution.py:22
  4.4 5.8 %collective-permute-start.7 = (f32[16,4096]{1,0:T(8,128)S(1)}, f32[16,4096]{1,0:T(8,128)S(1)}, u32[]{:S(2)}, u32[]{:S(2)}) collective-permute-start(f32[16,4096]{1,0:T(8,128)S(1)} %get-tuple-element.45), channel_id=1, source_target_pairs={{0,1},{1,0},{2,3},{3,2},{4,5},{5,4},{6,7},{7,6},{8,9},{9,8},{10,11... | collective-permute-start | bytes 786440 | tf_op jit(solution)/shard_map/ppermute | solution.py:22
  5.3 8.8 %collective-permute-start.1 = (s16[16,2176]{1,0:T(8,128)(2,1)S(1)}, s16[16,2176]{1,0:T(8,128)(2,1)S(1)}, u32[]{:S(2)}, u32[]{:S(2)}) collective-permute-start(s16[16,2176]{1,0:T(8,128)(2,1)S(1)} %join.6), channel_id=1, source_target_pairs={{0,6},{1,7},{2,4},{3,5},{4,2},{5,3},{6,0},{7,1},{8,14},{9,15},{10,... | collective-permute-start | bytes 208904 | tf_op jit(solution)/shard_map/ppermute | solution.py:22
  9.3 4.9 %collective-permute-start.3 = (s16[16,2176]{1,0:T(8,128)(2,1)S(1)}, s16[16,2176]{1,0:T(8,128)(2,1)S(1)}, u32[]{:S(2)}, u32[]{:S(2)}) collective-permute-start(s16[16,2176]{1,0:T(8,128)(2,1)S(1)} %join.7), channel_id=1, source_target_pairs={{0,4},{1,5},{2,6},{3,7},{4,0},{5,1},{6,2},{7,3},{8,12},{9,13},{10,... | collective-permute-start | bytes 208904 | tf_op jit(solution)/shard_map/ppermute | solution.py:22
  10.0 5.1 %collective-permute-start.5 = (s16[16,2176]{1,0:T(8,128)(2,1)S(1)}, s16[16,2176]{1,0:T(8,128)(2,1)S(1)}, u32[]{:S(2)}, u32[]{:S(2)}) collective-permute-start(s16[16,2176]{1,0:T(8,128)(2,1)S(1)} %join.8), channel_id=1, source_target_pairs={{0,2},{1,3},{2,0},{3,1},{4,6},{5,7},{6,4},{7,5},{8,10},{9,11},{10,... | collective-permute-start | bytes 208904 | tf_op jit(solution)/shard_map/ppermute | solution.py:22
  10.3 8.6 %collective-permute-start.8 = (s16[16,2688]{1,0:T(8,128)(2,1)S(1)}, s16[16,2688]{1,0:T(8,128)(2,1)S(1)}, u32[]{:S(2)}, u32[]{:S(2)}) collective-permute-start(s16[16,2688]{1,0:T(8,128)(2,1)S(1)} %join.9), channel_id=1, source_target_pairs={{0,6},{1,7},{2,4},{3,5},{4,2},{5,3},{6,0},{7,1},{8,14},{9,15},{10,... | collective-permute-start | bytes 258056 | tf_op jit(solution)/shard_map/ppermute | solution.py:22
  13.4 5.6 %collective-permute-start.9 = (s16[16,2688]{1,0:T(8,128)(2,1)S(1)}, s16[16,2688]{1,0:T(8,128)(2,1)S(1)}, u32[]{:S(2)}, u32[]{:S(2)}) collective-permute-start(s16[16,2688]{1,0:T(8,128)(2,1)S(1)} %join.10), channel_id=1, source_target_pairs={{0,4},{1,5},{2,6},{3,7},{4,0},{5,1},{6,2},{7,3},{8,12},{9,13},{10,... | collective-permute-start | bytes 258056 | tf_op jit(solution)/shard_map/ppermute | solution.py:22
  14.1 4.9 %collective-permute-start.10 = (s16[16,2688]{1,0:T(8,128)(2,1)S(1)}, s16[16,2688]{1,0:T(8,128)(2,1)S(1)}, u32[]{:S(2)}, u32[]{:S(2)}) collective-permute-start(s16[16,2688]{1,0:T(8,128)(2,1)S(1)} %join.11), channel_id=1, source_target_pairs={{0,2},{1,3},{2,0},{3,1},{4,6},{5,7},{6,4},{7,5},{8,10},{9,11},{10,... | collective-permute-start | bytes 258056 | tf_op jit(solution)/shard_map/ppermute | solution.py:22
  15.3 3.6 %collective-permute-start.6 = (f32[8,128]{1,0:T(8,128)S(1)}, f32[8,128]{1,0:T(8,128)S(1)}, u32[]{:S(2)}, u32[]{:S(2)}) collective-permute-start(f32[8,128]{1,0:T(8,128)S(1)} %get-tuple-element.44.refs_0_), channel_id=1, source_target_pairs={{0,8},{8,0},{16,24},{24,16},{1,9},{9,1},{17,25},{25,17},{2,10},{10... | collective-permute-start | bytes 12296 | tf_op jit(solution)/shard_map/ppermute | solution.py:22
  19.0 4.6 %collective-permute-start.11 = (f32[8,128]{1,0:T(8,128)S(1)}, f32[8,128]{1,0:T(8,128)S(1)}, u32[]{:S(2)}, u32[]{:S(2)}) collective-permute-start(f32[8,128]{1,0:T(8,128)S(1)} %get-tuple-element.48.refs_0_), channel_id=1, source_target_pairs={{0,16},{8,24},{16,0},{24,8},{1,17},{9,25},{17,1},{25,9},{2,18},{10... | collective-permute-start | bytes 12296 | tf_op jit(solution)/shard_map/ppermute | solution.py:22
  23.7 7.1 %collective-permute-start.14 = (f32[40,128]{1,0:T(8,128)S(1)}, f32[40,128]{1,0:T(8,128)S(1)}, u32[]{:S(2)}, u32[]{:S(2)}) collective-permute-start(f32[40,128]{1,0:T(8,128)S(1)} %get-tuple-element.57.refs_0_), channel_id=1, source_target_pairs={{0,24},{8,16},{16,8},{24,0},{1,25},{9,17},{17,9},{25,1},{2,26},{10... | collective-permute-start | bytes 61448 | tf_op jit(solution)/shard_map/ppermute | solution.py:22
  27.4 4.7 %collective-permute-start.13 = (f32[40,128]{1,0:T(8,128)S(1)}, f32[40,128]{1,0:T(8,128)S(1)}, u32[]{:S(2)}, u32[]{:S(2)}) collective-permute-start(f32[40,128]{1,0:T(8,128)S(1)} %get-tuple-element.57.refs_0_), channel_id=1, source_target_pairs={{0,16},{8,24},{16,0},{24,8},{1,17},{9,25},{17,1},{25,9},{2,18},{10... | collective-permute-start | bytes 61448 | tf_op jit(solution)/shard_map/ppermute | solution.py:22
  27.4 4.7 %collective-permute-start.12 = (f32[40,128]{1,0:T(8,128)S(1)}, f32[40,128]{1,0:T(8,128)S(1)}, u32[]{:S(2)}, u32[]{:S(2)}) collective-permute-start(f32[40,128]{1,0:T(8,128)S(1)} %get-tuple-element.57.refs_0_), channel_id=1, source_target_pairs={{0,8},{8,0},{16,24},{24,16},{1,9},{9,1},{17,25},{25,17},{2,10},{10... | collective-permute-start | bytes 61448 | tf_op jit(solution)/shard_map/ppermute | solution.py:22
  32.3 6.0 %collective-permute-start.17 = (bf16[16,4096]{1,0:T(8,128)(2,1)S(1)}, bf16[16,4096]{1,0:T(8,128)(2,1)S(1)}, u32[]{:S(2)}, u32[]{:S(2)}) collective-permute-start(bf16[16,4096]{1,0:T(8,128)(2,1)S(1)} %weights.1.refs_0_), channel_id=1, source_target_pairs={{0,6},{1,7},{2,4},{3,5},{4,2},{5,3},{6,0},{7,1},{8,14},{9,15},{10,... | collective-permute-start | bytes 393224 | tf_op jit(solution)/shard_map/ppermute | solution.py:22
  34.3 5.3 %collective-permute-start.16 = (bf16[16,4096]{1,0:T(8,128)(2,1)S(1)}, bf16[16,4096]{1,0:T(8,128)(2,1)S(1)}, u32[]{:S(2)}, u32[]{:S(2)}) collective-permute-start(bf16[16,4096]{1,0:T(8,128)(2,1)S(1)} %weights.1.refs_0_), channel_id=1, source_target_pairs={{0,4},{1,5},{2,6},{3,7},{4,0},{5,1},{6,2},{7,3},{8,12},{9,13},{10,... | collective-permute-start | bytes 393224 | tf_op jit(solution)/shard_map/ppermute | solution.py:22
  34.8 5.0 %collective-permute-start.15 = (bf16[16,4096]{1,0:T(8,128)(2,1)S(1)}, bf16[16,4096]{1,0:T(8,128)(2,1)S(1)}, u32[]{:S(2)}, u32[]{:S(2)}) collective-permute-start(bf16[16,4096]{1,0:T(8,128)(2,1)S(1)} %weights.1.refs_0_), channel_id=1, source_target_pairs={{0,2},{1,3},{2,0},{3,1},{4,6},{5,7},{6,4},{7,5},{8,10},{9,11},{10,... | collective-permute-start | bytes 393224 | tf_op jit(solution)/shard_map/ppermute | solution.py:22
  40.8 1.5 %collective-permute-start.21 = (bf16[16,4096]{1,0:T(8,128)(2,1)S(1)}, bf16[16,4096]{1,0:T(8,128)(2,1)S(1)}, u32[]{:S(2)}, u32[]{:S(2)}) collective-permute-start(bf16[16,4096]{1,0:T(8,128)(2,1)S(1)} %get-tuple-element.65), channel_id=1, source_target_pairs={{0,1},{1,0},{2,3},{3,2},{4,5},{5,4},{6,7},{7,6},{8,9},{9,8},{10,11... | collective-permute-start | bytes 393224 | tf_op jit(solution)/shard_map/ppermute | solution.py:22
  41.3 1.5 %collective-permute-start.23 = (bf16[16,4096]{1,0:T(8,128)(2,1)S(1)}, bf16[16,4096]{1,0:T(8,128)(2,1)S(1)}, u32[]{:S(2)}, u32[]{:S(2)}) collective-permute-start(bf16[16,4096]{1,0:T(8,128)(2,1)S(1)} %get-tuple-element.67), channel_id=1, source_target_pairs={{0,1},{1,0},{2,3},{3,2},{4,5},{5,4},{6,7},{7,6},{8,9},{9,8},{10,11... | collective-permute-start | bytes 393224 | tf_op jit(solution)/shard_map/ppermute | solution.py:22
  41.8 4.3 %collective-permute-start.18 = (s16[17,16,128]{2,1,0:T(8,128)(2,1)S(1)}, s16[17,16,128]{2,1,0:T(8,128)(2,1)S(1)}, u32[]{:S(2)}, u32[]{:S(2)}) collective-permute-start(s16[17,16,128]{2,1,0:T(8,128)(2,1)S(1)} %gradients.2.mine.refs_4_), channel_id=1, source_target_pairs={{0,8},{8,0},{16,24},{24,16},{1,9},{9,1},{17,25},{25,17},{2,10},{10... | collective-permute-start | bytes 208904 | tf_op jit(solution)/shard_map/ppermute | solution.py:22
  43.7 4.6 %collective-permute-start.24 = (s16[17,16,128]{2,1,0:T(8,128)(2,1)S(1)}, s16[17,16,128]{2,1,0:T(8,128)(2,1)S(1)}, u32[]{:S(2)}, u32[]{:S(2)}) collective-permute-start(s16[17,16,128]{2,1,0:T(8,128)(2,1)S(1)} %gradients.3.mine), channel_id=1, source_target_pairs={{0,8},{8,0},{16,24},{24,16},{1,9},{9,1},{17,25},{25,17},{2,10},{10... | collective-permute-start | bytes 208904 | tf_op jit(solution)/shard_map/ppermute | solution.py:22
  46.2 7.1 %collective-permute-start.19 = (s16[17,16,128]{2,1,0:T(8,128)(2,1)S(1)}, s16[17,16,128]{2,1,0:T(8,128)(2,1)S(1)}, u32[]{:S(2)}, u32[]{:S(2)}) collective-permute-start(s16[17,16,128]{2,1,0:T(8,128)(2,1)S(1)} %merge.2.mine), channel_id=1, source_target_pairs={{0,16},{8,24},{16,0},{24,8},{1,17},{9,25},{17,1},{25,9},{2,18},{10... | collective-permute-start | bytes 208904 | tf_op jit(solution)/shard_map/ppermute | solution.py:22
  48.3 6.5 %collective-permute-start.25 = (s16[17,16,128]{2,1,0:T(8,128)(2,1)S(1)}, s16[17,16,128]{2,1,0:T(8,128)(2,1)S(1)}, u32[]{:S(2)}, u32[]{:S(2)}) collective-permute-start(s16[17,16,128]{2,1,0:T(8,128)(2,1)S(1)} %merge.3.mine), channel_id=1, source_target_pairs={{0,16},{8,24},{16,0},{24,8},{1,17},{9,25},{17,1},{25,9},{2,18},{10... | collective-permute-start | bytes 208904 | tf_op jit(solution)/shard_map/ppermute | solution.py:22
  (5 other events, 38.7 us)

commit v24 on v20

--- a/solution.py
+++ b/solution.py
@@ -650,10 +650,10 @@
     rank, event_row = event_rank[None], events[None]
 
     linear, keep, send = products(dosages, coefficients, directions, feat)
-    order = list(reversed(range(1, feat // 2)))
-    received = {q: swap(send[q], "feat", 1) for q in order + [0]}
+    order = list(range(1, feat // 2))
+    received = {q: swap(send[q], "feat", 1) for q in order[::-1] + [0]}
     table = tables(rank, linear, rows)
-    paired = pair(linear, received[order[0]], table)
+    paired = pair(linear, received[order[-1]], table)
     middle = min(3 * SPAN, rows // 2)
     firsts = [
         swap(join(keep[q], received[q], 0, middle, paired, []), "feat", 2 * q) for q in order

time: 55.1 us -> 55.8 us (1.013)
  transfers between devices with their start and end apart: 26 -> 26, of which waited for: 10 -> 11; matrix products, arithmetic and copies ran while one was open for 0% -> 0% of each run, Pallas kernels for 17% -> 17%
where the time goes in v24:
time: 55.8 us; the launch traced here: 55.6 us
  starting transfers between devices  28.5 us (51%)
  Pallas kernels  13.8 us (25%)
  waiting for transfers between devices  13.2 us (24%)
    ppermute x26, starting transfers between devices, swap(): return lax.ppermute(x, axis, [(s, s ^ i) for s in range(count)])  28.5 us
    ppermute x26, waiting for transfers between devices, swap(): return lax.ppermute(x, axis, [(s, s ^ i) for s in range(count)])  13.2 us
    pallas_call x1, Pallas kernels, products(): pl.pallas_call(functools.partial(product_kernel, feat, kf, chunk), in_spe...  3.35 us
    pallas_call x2, Pallas kernels, ordered_values(): pl.pallas_call(functools.partial(order_kernel, start, len(messages)), in_...  1.97 us
    pallas_call x2, Pallas kernels, gradients(): pl.pallas_call(functools.partial(gradient_kernel, parts, kf), in_specs=[V...  1.76 us
    pallas_call x1, Pallas kernels, prefix_sums(): pl.pallas_call(prefix_kernel, in_specs=[VMEM] * 3, out_shape=jax.ShapeDty...  1.75 us
  transfers between devices with their start and end apart: 26, of which 11 were waited for; matrix products, arithmetic and copies ran while one was open for 0% of the time, Pallas kernels for 17%

profile of v24, /device:TPU:0, one launch (start us, length us, event | category | flops | bytes accessed | tf_op | source)
XLA Modules:
  0.0 55.6 jit_solution(8504327389824929909)
XLA Ops:
  0.0 3.3 %products.1 = (f32[16,256]{1,0:T(8,128)S(1)}, f32[16,4096]{1,0:T(8,128)S(1)}, f32[16,4096]{1,0:T(8,128)S(1)}, f32[16,4096]{1,0:T(8,128)S(1)}, f32[16,4096]{1,0:T...) custom-call(bf16[512,128]{1,0:T(8,128)(2,1)} %directions.1, ...), custom_call_target="tpu_custom_call" | custom-call | flops 536870912 | bytes 6291456 | tf_op jit(solution)/shard_map/products/pallas_call | solution.py:117
  5.6 2.9 %collective-permute-start.2 = (s16[16,2176]{1,0:T(8,128)(2,1)S(1)}, s16[16,2176]{1,0:T(8,128)(2,1)S(1)}, u32[]{:S(2)}, u32[]{:S(2)}) collective-permute-start(s16[16,2176]{1,0:T(8,128)(2,1)S(1)} %join.6), channel_id=1, source_target_pairs={{0,2},{1,3},{2,0},{3,1},{4,6},{5,7},{6,4},{7,5},{8,10},{9,11},{10,... | collective-permute-start | bytes 208904 | tf_op jit(solution)/shard_map/ppermute | solution.py:22
  8.6 1.6 %collective-permute-start.4 = (s16[16,2176]{1,0:T(8,128)(2,1)S(1)}, s16[16,2176]{1,0:T(8,128)(2,1)S(1)}, u32[]{:S(2)}, u32[]{:S(2)}) collective-permute-start(s16[16,2176]{1,0:T(8,128)(2,1)S(1)} %join.7), channel_id=1, source_target_pairs={{0,4},{1,5},{2,6},{3,7},{4,0},{5,1},{6,2},{7,3},{8,12},{9,13},{10,... | collective-permute-start | bytes 208904 | tf_op jit(solution)/shard_map/ppermute | solution.py:22
  10.6 1.9 %collective-permute-start.8 = (s16[16,2688]{1,0:T(8,128)(2,1)S(1)}, s16[16,2688]{1,0:T(8,128)(2,1)S(1)}, u32[]{:S(2)}, u32[]{:S(2)}) collective-permute-start(s16[16,2688]{1,0:T(8,128)(2,1)S(1)} %join.9), channel_id=1, source_target_pairs={{0,2},{1,3},{2,0},{3,1},{4,6},{5,7},{6,4},{7,5},{8,10},{9,11},{10,... | collective-permute-start | bytes 258056 | tf_op jit(solution)/shard_map/ppermute | solution.py:22
  12.7 1.6 %collective-permute-start.9 = (s16[16,2688]{1,0:T(8,128)(2,1)S(1)}, s16[16,2688]{1,0:T(8,128)(2,1)S(1)}, u32[]{:S(2)}, u32[]{:S(2)}) collective-permute-start(s16[16,2688]{1,0:T(8,128)(2,1)S(1)} %join.10), channel_id=1, source_target_pairs={{0,4},{1,5},{2,6},{3,7},{4,0},{5,1},{6,2},{7,3},{8,12},{9,13},{10,... | collective-permute-start | bytes 258056 | tf_op jit(solution)/shard_map/ppermute | solution.py:22
  14.6 1.4 %collective-permute-done.5.refs_2_ = s16[16,2176]{1,0:T(8,128)(2,1)S(1)} collective-permute-done((s16[16,2176]{1,0:T(8,128)(2,1)S(1)}, s16[16,2176]{1,0:T(8,128)(2,1)S(1)}, u32[]{:S(2)}, u32[]{:S(2)}) %collective-permute-start.5) | collective-permute-done | bytes 69664 | tf_op jit(solution)/shard_map/ppermute | solution.py:22
  16.1 1.6 %collective-permute-start.6 = (f32[8,128]{1,0:T(8,128)S(1)}, f32[8,128]{1,0:T(8,128)S(1)}, u32[]{:S(2)}, u32[]{:S(2)}) collective-permute-start(f32[8,128]{1,0:T(8,128)S(1)} %get-tuple-element.40.refs_0_), channel_id=1, source_target_pairs={{0,8},{8,0},{16,24},{24,16},{1,9},{9,1},{17,25},{25,17},{2,10},{10... | collective-permute-start | bytes 12296 | tf_op jit(solution)/shard_map/ppermute | solution.py:22
  19.8 2.7 %collective-permute-start.11 = (f32[8,128]{1,0:T(8,128)S(1)}, f32[8,128]{1,0:T(8,128)S(1)}, u32[]{:S(2)}, u32[]{:S(2)}) collective-permute-start(f32[8,128]{1,0:T(8,128)S(1)} %get-tuple-element.44.refs_0_), channel_id=1, source_target_pairs={{0,16},{8,24},{16,0},{24,8},{1,17},{9,25},{17,1},{25,9},{2,18},{10... | collective-permute-start | bytes 12296 | tf_op jit(solution)/shard_map/ppermute | solution.py:22
  22.5 1.2 %ordered_values.3 = (f32[16,2560]{1,0:T(8,128)S(1)}, f32[256,256]{1,0:T(8,128)S(1)}, f32[16,128]{1,0:T(8,128)S(1)}) custom-call(f32[16,4096]{1,0:T(8,128)S(1)} %get-tuple-element.48.own, f32[16,4096]{1,0:T(8,128)S(1)} %collective-permute-done.7.refs_1_.other, s16[16,2688]{1,0:T(8,128)(2,1)S(1)} %collective-permute-done.8.refs_3_.refs_0_, ...), custom_call_target="tpu_custom_call" | custom-call | flops 671088640 | bytes 983040 | tf_op jit(solution)/shard_map/ordered_values/pallas_call | solution.py:397
  24.6 3.6 %collective-permute-start.14 = (f32[40,128]{1,0:T(8,128)S(1)}, f32[40,128]{1,0:T(8,128)S(1)}, u32[]{:S(2)}, u32[]{:S(2)}) collective-permute-start(f32[40,128]{1,0:T(8,128)S(1)} %get-tuple-element.53.refs_0_), channel_id=1, source_target_pairs={{0,24},{8,16},{16,8},{24,0},{1,25},{9,17},{17,9},{25,1},{2,26},{10... | collective-permute-start | bytes 61448 | tf_op jit(solution)/shard_map/ppermute | solution.py:22
  29.0 1.7 %prefix_sums.1.refs_6_ = f32[16,4096]{1,0:T(8,128)S(1)} custom-call(f32[256,256]{1,0:T(8,128)S(1)} %suffix_sums.1.ordered.sums, f32[16,256]{1,0:T(8,128)S(1)} %get-tuple-element.56.squares.square, s32[1,4096]{1,0:T(1,128)S(1)} %bitcast.6), custom_call_target="tpu_custom_call" | custom-call | flops 1073741824 | bytes 1572864 | tf_op jit(solution)/shard_map/prefix_sums/pallas_call | solution.py:463
  30.7 0.9 %hazards.1 = (f32[1,4096]{1,0:T(1,128)S(1)}, f32[1,4096]{1,0:T(1,128)S(1)}) custom-call(f32[16,256]{1,0:T(8,128)S(1)} %get-tuple-element.57.hazard, f32[16,256]{1,0:T(8,128)S(1)} %get-tuple-element.56.squares.square, s32[1,4096]{1,0:T(1,128)S(1)} %bitcast.7), custom_call_target="tpu_custom_call" | custom-call | flops 209715200 | bytes 262144 | tf_op jit(solution)/shard_map/hazards/pallas_call | solution.py:331
  31.6 1.2 %collective-permute-done.13.refs_2_ = f32[40,128]{1,0:T(8,128)S(1)} collective-permute-done((f32[40,128]{1,0:T(8,128)S(1)}, f32[40,128]{1,0:T(8,128)S(1)}, u32[]{:S(2)}, u32[]{:S(2)}) %collective-permute-start.13) | collective-permute-done | bytes 20512 | tf_op jit(solution)/shard_map/ppermute | solution.py:22
  33.0 1.4 %collective-permute-start.17 = (bf16[16,4096]{1,0:T(8,128)(2,1)S(1)}, bf16[16,4096]{1,0:T(8,128)(2,1)S(1)}, u32[]{:S(2)}, u32[]{:S(2)}) collective-permute-start(bf16[16,4096]{1,0:T(8,128)(2,1)S(1)} %weights.1.refs_0_), channel_id=1, source_target_pairs={{0,6},{1,7},{2,4},{3,5},{4,2},{5,3},{6,0},{7,1},{8,14},{9,15},{10,... | collective-permute-start | bytes 393224 | tf_op jit(solution)/shard_map/ppermute | solution.py:22
  34.5 0.9 %collective-permute-start.16 = (bf16[16,4096]{1,0:T(8,128)(2,1)S(1)}, bf16[16,4096]{1,0:T(8,128)(2,1)S(1)}, u32[]{:S(2)}, u32[]{:S(2)}) collective-permute-start(bf16[16,4096]{1,0:T(8,128)(2,1)S(1)} %weights.1.refs_0_), channel_id=1, source_target_pairs={{0,4},{1,5},{2,6},{3,7},{4,0},{5,1},{6,2},{7,3},{8,12},{9,13},{10,... | collective-permute-start | bytes 393224 | tf_op jit(solution)/shard_map/ppermute | solution.py:22
  35.4 1.2 %collective-permute-start.15 = (bf16[16,4096]{1,0:T(8,128)(2,1)S(1)}, bf16[16,4096]{1,0:T(8,128)(2,1)S(1)}, u32[]{:S(2)}, u32[]{:S(2)}) collective-permute-start(bf16[16,4096]{1,0:T(8,128)(2,1)S(1)} %weights.1.refs_0_), channel_id=1, source_target_pairs={{0,2},{1,3},{2,0},{3,1},{4,6},{5,7},{6,4},{7,5},{8,10},{9,11},{10,... | collective-permute-start | bytes 393224 | tf_op jit(solution)/shard_map/ppermute | solution.py:22
  36.6 2.5 %collective-permute-done.17.refs_3_ = bf16[16,4096]{1,0:T(8,128)(2,1)S(1)} collective-permute-done((bf16[16,4096]{1,0:T(8,128)(2,1)S(1)}, bf16[16,4096]{1,0:T(8,128)(2,1)S(1)}, u32[]{:S(2)}, u32[]{:S(2)}) %collective-permute-start.17) | collective-permute-done | bytes 131104 | tf_op jit(solution)/shard_map/ppermute | solution.py:22
  39.1 1.3 %collective-permute-done.16.refs_2_ = bf16[16,4096]{1,0:T(8,128)(2,1)S(1)} collective-permute-done((bf16[16,4096]{1,0:T(8,128)(2,1)S(1)}, bf16[16,4096]{1,0:T(8,128)(2,1)S(1)}, u32[]{:S(2)}, u32[]{:S(2)}) %collective-permute-start.16) | collective-permute-done | bytes 131104 | tf_op jit(solution)/shard_map/ppermute | solution.py:22
  42.8 2.1 %collective-permute-start.24 = (s16[17,16,128]{2,1,0:T(8,128)(2,1)S(1)}, s16[17,16,128]{2,1,0:T(8,128)(2,1)S(1)}, u32[]{:S(2)}, u32[]{:S(2)}) collective-permute-start(s16[17,16,128]{2,1,0:T(8,128)(2,1)S(1)} %gradients.3.mine), channel_id=1, source_target_pairs={{0,8},{8,0},{16,24},{24,16},{1,9},{9,1},{17,25},{25,17},{2,10},{10... | collective-permute-start | bytes 208904 | tf_op jit(solution)/shard_map/ppermute | solution.py:22
  44.9 1.8 %collective-permute-done.18.other = s16[17,16,128]{2,1,0:T(8,128)(2,1)S(1)} collective-permute-done((s16[17,16,128]{2,1,0:T(8,128)(2,1)S(1)}, s16[17,16,128]{2,1,0:T(8,128)(2,1)S(1)}, u32[]{:S(2)}, u32[]{:S(2)}) %collective-permute-start.18) | collective-permute-done | bytes 69664 | tf_op jit(solution)/shard_map/ppermute | solution.py:22
  46.7 1.7 %collective-permute-start.19 = (s16[17,16,128]{2,1,0:T(8,128)(2,1)S(1)}, s16[17,16,128]{2,1,0:T(8,128)(2,1)S(1)}, u32[]{:S(2)}, u32[]{:S(2)}) collective-permute-start(s16[17,16,128]{2,1,0:T(8,128)(2,1)S(1)} %merge.2.mine), channel_id=1, source_target_pairs={{0,16},{8,24},{16,0},{24,8},{1,17},{9,25},{17,1},{25,9},{2,18},{10... | collective-permute-start | bytes 208904 | tf_op jit(solution)/shard_map/ppermute | solution.py:22
  48.5 2.4 %collective-permute-start.25 = (s16[17,16,128]{2,1,0:T(8,128)(2,1)S(1)}, s16[17,16,128]{2,1,0:T(8,128)(2,1)S(1)}, u32[]{:S(2)}, u32[]{:S(2)}) collective-permute-start(s16[17,16,128]{2,1,0:T(8,128)(2,1)S(1)} %merge.3.mine), channel_id=1, source_target_pairs={{0,16},{8,24},{16,0},{24,8},{1,17},{9,25},{17,1},{25,9},{2,18},{10... | collective-permute-start | bytes 208904 | tf_op jit(solution)/shard_map/ppermute | solution.py:22
  50.9 2.3 %collective-permute-done.19.other = s16[17,16,128]{2,1,0:T(8,128)(2,1)S(1)} collective-permute-done((s16[17,16,128]{2,1,0:T(8,128)(2,1)S(1)}, s16[17,16,128]{2,1,0:T(8,128)(2,1)S(1)}, u32[]{:S(2)}, u32[]{:S(2)}) %collective-permute-start.19) | collective-permute-done | bytes 69664 | tf_op jit(solution)/shard_map/ppermute | solution.py:22
  53.3 1.5 %collective-permute-done.25.other = s16[17,16,128]{2,1,0:T(8,128)(2,1)S(1)} collective-permute-done((s16[17,16,128]{2,1,0:T(8,128)(2,1)S(1)}, s16[17,16,128]{2,1,0:T(8,128)(2,1)S(1)}, u32[]{:S(2)}, u32[]{:S(2)}) %collective-permute-start.25) | collective-permute-done | bytes 69664 | tf_op jit(solution)/shard_map/ppermute | solution.py:22
  (61 shorter events, 10.7 us)
Async XLA Ops:
  3.4 1.8 %collective-permute-start = (f32[16,4352]{1,0:T(8,128)S(1)}, f32[16,4352]{1,0:T(8,128)S(1)}, u32[]{:S(2)}, u32[]{:S(2)}) collective-permute-start(f32[16,4352]{1,0:T(8,128)S(1)} %get-tuple-element.34), channel_id=1, source_target_pairs={{0,1},{1,0},{2,3},{3,2},{4,5},{5,4},{6,7},{7,6},{8,9},{9,8},{10,11... | collective-permute-start | bytes 835592 | tf_op jit(solution)/shard_map/ppermute | solution.py:22
  3.9 1.6 %collective-permute-start.1 = (f32[16,4096]{1,0:T(8,128)S(1)}, f32[16,4096]{1,0:T(8,128)S(1)}, u32[]{:S(2)}, u32[]{:S(2)}) collective-permute-start(f32[16,4096]{1,0:T(8,128)S(1)} %get-tuple-element.36), channel_id=1, source_target_pairs={{0,1},{1,0},{2,3},{3,2},{4,5},{5,4},{6,7},{7,6},{8,9},{9,8},{10,11... | collective-permute-start | bytes 786440 | tf_op jit(solution)/shard_map/ppermute | solution.py:22
  4.0 4.5 %collective-permute-start.3 = (f32[16,4096]{1,0:T(8,128)S(1)}, f32[16,4096]{1,0:T(8,128)S(1)}, u32[]{:S(2)}, u32[]{:S(2)}) collective-permute-start(f32[16,4096]{1,0:T(8,128)S(1)} %get-tuple-element.38), channel_id=1, source_target_pairs={{0,1},{1,0},{2,3},{3,2},{4,5},{5,4},{6,7},{7,6},{8,9},{9,8},{10,11... | collective-permute-start | bytes 786440 | tf_op jit(solution)/shard_map/ppermute | solution.py:22
  4.4 6.1 %collective-permute-start.7 = (f32[16,4096]{1,0:T(8,128)S(1)}, f32[16,4096]{1,0:T(8,128)S(1)}, u32[]{:S(2)}, u32[]{:S(2)}) collective-permute-start(f32[16,4096]{1,0:T(8,128)S(1)} %get-tuple-element.41), channel_id=1, source_target_pairs={{0,1},{1,0},{2,3},{3,2},{4,5},{5,4},{6,7},{7,6},{8,9},{9,8},{10,11... | collective-permute-start | bytes 786440 | tf_op jit(solution)/shard_map/ppermute | solution.py:22
  5.6 8.8 %collective-permute-start.2 = (s16[16,2176]{1,0:T(8,128)(2,1)S(1)}, s16[16,2176]{1,0:T(8,128)(2,1)S(1)}, u32[]{:S(2)}, u32[]{:S(2)}) collective-permute-start(s16[16,2176]{1,0:T(8,128)(2,1)S(1)} %join.6), channel_id=1, source_target_pairs={{0,2},{1,3},{2,0},{3,1},{4,6},{5,7},{6,4},{7,5},{8,10},{9,11},{10,... | collective-permute-start | bytes 208904 | tf_op jit(solution)/shard_map/ppermute | solution.py:22
  8.6 6.0 %collective-permute-start.4 = (s16[16,2176]{1,0:T(8,128)(2,1)S(1)}, s16[16,2176]{1,0:T(8,128)(2,1)S(1)}, u32[]{:S(2)}, u32[]{:S(2)}) collective-permute-start(s16[16,2176]{1,0:T(8,128)(2,1)S(1)} %join.7), channel_id=1, source_target_pairs={{0,4},{1,5},{2,6},{3,7},{4,0},{5,1},{6,2},{7,3},{8,12},{9,13},{10,... | collective-permute-start | bytes 208904 | tf_op jit(solution)/shard_map/ppermute | solution.py:22
  10.3 5.7 %collective-permute-start.5 = (s16[16,2176]{1,0:T(8,128)(2,1)S(1)}, s16[16,2176]{1,0:T(8,128)(2,1)S(1)}, u32[]{:S(2)}, u32[]{:S(2)}) collective-permute-start(s16[16,2176]{1,0:T(8,128)(2,1)S(1)} %join.8), channel_id=1, source_target_pairs={{0,6},{1,7},{2,4},{3,5},{4,2},{5,3},{6,0},{7,1},{8,14},{9,15},{10,... | collective-permute-start | bytes 208904 | tf_op jit(solution)/shard_map/ppermute | solution.py:22
  10.6 9.1 %collective-permute-start.8 = (s16[16,2688]{1,0:T(8,128)(2,1)S(1)}, s16[16,2688]{1,0:T(8,128)(2,1)S(1)}, u32[]{:S(2)}, u32[]{:S(2)}) collective-permute-start(s16[16,2688]{1,0:T(8,128)(2,1)S(1)} %join.9), channel_id=1, source_target_pairs={{0,2},{1,3},{2,0},{3,1},{4,6},{5,7},{6,4},{7,5},{8,10},{9,11},{10,... | collective-permute-start | bytes 258056 | tf_op jit(solution)/shard_map/ppermute | solution.py:22
  12.7 7.1 %collective-permute-start.9 = (s16[16,2688]{1,0:T(8,128)(2,1)S(1)}, s16[16,2688]{1,0:T(8,128)(2,1)S(1)}, u32[]{:S(2)}, u32[]{:S(2)}) collective-permute-start(s16[16,2688]{1,0:T(8,128)(2,1)S(1)} %join.10), channel_id=1, source_target_pairs={{0,4},{1,5},{2,6},{3,7},{4,0},{5,1},{6,2},{7,3},{8,12},{9,13},{10,... | collective-permute-start | bytes 258056 | tf_op jit(solution)/shard_map/ppermute | solution.py:22
  14.4 5.4 %collective-permute-start.10 = (s16[16,2688]{1,0:T(8,128)(2,1)S(1)}, s16[16,2688]{1,0:T(8,128)(2,1)S(1)}, u32[]{:S(2)}, u32[]{:S(2)}) collective-permute-start(s16[16,2688]{1,0:T(8,128)(2,1)S(1)} %join.11), channel_id=1, source_target_pairs={{0,6},{1,7},{2,4},{3,5},{4,2},{5,3},{6,0},{7,1},{8,14},{9,15},{10,... | collective-permute-start | bytes 258056 | tf_op jit(solution)/shard_map/ppermute | solution.py:22
  16.1 3.6 %collective-permute-start.6 = (f32[8,128]{1,0:T(8,128)S(1)}, f32[8,128]{1,0:T(8,128)S(1)}, u32[]{:S(2)}, u32[]{:S(2)}) collective-permute-start(f32[8,128]{1,0:T(8,128)S(1)} %get-tuple-element.40.refs_0_), channel_id=1, source_target_pairs={{0,8},{8,0},{16,24},{24,16},{1,9},{9,1},{17,25},{25,17},{2,10},{10... | collective-permute-start | bytes 12296 | tf_op jit(solution)/shard_map/ppermute | solution.py:22
  19.8 4.6 %collective-permute-start.11 = (f32[8,128]{1,0:T(8,128)S(1)}, f32[8,128]{1,0:T(8,128)S(1)}, u32[]{:S(2)}, u32[]{:S(2)}) collective-permute-start(f32[8,128]{1,0:T(8,128)S(1)} %get-tuple-element.44.refs_0_), channel_id=1, source_target_pairs={{0,16},{8,24},{16,0},{24,8},{1,17},{9,25},{17,1},{25,9},{2,18},{10... | collective-permute-start | bytes 12296 | tf_op jit(solution)/shard_map/ppermute | solution.py:22
  24.6 7.1 %collective-permute-start.14 = (f32[40,128]{1,0:T(8,128)S(1)}, f32[40,128]{1,0:T(8,128)S(1)}, u32[]{:S(2)}, u32[]{:S(2)}) collective-permute-start(f32[40,128]{1,0:T(8,128)S(1)} %get-tuple-element.53.refs_0_), channel_id=1, source_target_pairs={{0,24},{8,16},{16,8},{24,0},{1,25},{9,17},{17,9},{25,1},{2,26},{10... | collective-permute-start | bytes 61448 | tf_op jit(solution)/shard_map/ppermute | solution.py:22
  28.2 4.7 %collective-permute-start.13 = (f32[40,128]{1,0:T(8,128)S(1)}, f32[40,128]{1,0:T(8,128)S(1)}, u32[]{:S(2)}, u32[]{:S(2)}) collective-permute-start(f32[40,128]{1,0:T(8,128)S(1)} %get-tuple-element.53.refs_0_), channel_id=1, source_target_pairs={{0,16},{8,24},{16,0},{24,8},{1,17},{9,25},{17,1},{25,9},{2,18},{10... | collective-permute-start | bytes 61448 | tf_op jit(solution)/shard_map/ppermute | solution.py:22
  28.2 4.7 %collective-permute-start.12 = (f32[40,128]{1,0:T(8,128)S(1)}, f32[40,128]{1,0:T(8,128)S(1)}, u32[]{:S(2)}, u32[]{:S(2)}) collective-permute-start(f32[40,128]{1,0:T(8,128)S(1)} %get-tuple-element.53.refs_0_), channel_id=1, source_target_pairs={{0,8},{8,0},{16,24},{24,16},{1,9},{9,1},{17,25},{25,17},{2,10},{10... | collective-permute-start | bytes 61448 | tf_op jit(solution)/shard_map/ppermute | solution.py:22
  33.0 6.0 %collective-permute-start.17 = (bf16[16,4096]{1,0:T(8,128)(2,1)S(1)}, bf16[16,4096]{1,0:T(8,128)(2,1)S(1)}, u32[]{:S(2)}, u32[]{:S(2)}) collective-permute-start(bf16[16,4096]{1,0:T(8,128)(2,1)S(1)} %weights.1.refs_0_), channel_id=1, source_target_pairs={{0,6},{1,7},{2,4},{3,5},{4,2},{5,3},{6,0},{7,1},{8,14},{9,15},{10,... | collective-permute-start | bytes 393224 | tf_op jit(solution)/shard_map/ppermute | solution.py:22
  34.5 5.9 %collective-permute-start.16 = (bf16[16,4096]{1,0:T(8,128)(2,1)S(1)}, bf16[16,4096]{1,0:T(8,128)(2,1)S(1)}, u32[]{:S(2)}, u32[]{:S(2)}) collective-permute-start(bf16[16,4096]{1,0:T(8,128)(2,1)S(1)} %weights.1.refs_0_), channel_id=1, source_target_pairs={{0,4},{1,5},{2,6},{3,7},{4,0},{5,1},{6,2},{7,3},{8,12},{9,13},{10,... | collective-permute-start | bytes 393224 | tf_op jit(solution)/shard_map/ppermute | solution.py:22
  35.4 5.0 %collective-permute-start.15 = (bf16[16,4096]{1,0:T(8,128)(2,1)S(1)}, bf16[16,4096]{1,0:T(8,128)(2,1)S(1)}, u32[]{:S(2)}, u32[]{:S(2)}) collective-permute-start(bf16[16,4096]{1,0:T(8,128)(2,1)S(1)} %weights.1.refs_0_), channel_id=1, source_target_pairs={{0,2},{1,3},{2,0},{3,1},{4,6},{5,7},{6,4},{7,5},{8,10},{9,11},{10,... | collective-permute-start | bytes 393224 | tf_op jit(solution)/shard_map/ppermute | solution.py:22
  36.6 5.3 %collective-permute-start.20 = (bf16[16,4096]{1,0:T(8,128)(2,1)S(1)}, bf16[16,4096]{1,0:T(8,128)(2,1)S(1)}, u32[]{:S(2)}, u32[]{:S(2)}) collective-permute-start(bf16[16,4096]{1,0:T(8,128)(2,1)S(1)} %weights.1.refs_0_), channel_id=1, source_target_pairs={{0,1},{1,0},{2,3},{3,2},{4,5},{5,4},{6,7},{7,6},{8,9},{9,8},{10,11... | collective-permute-start | bytes 393224 | tf_op jit(solution)/shard_map/ppermute | solution.py:22
  39.1 2.8 %collective-permute-start.23 = (bf16[16,4096]{1,0:T(8,128)(2,1)S(1)}, bf16[16,4096]{1,0:T(8,128)(2,1)S(1)}, u32[]{:S(2)}, u32[]{:S(2)}) collective-permute-start(bf16[16,4096]{1,0:T(8,128)(2,1)S(1)} %collective-permute-done.17.refs_3_), channel_id=1, source_target_pairs={{0,1},{1,0},{2,3},{3,2},{4,5},{5,4},{6,7},{7,6},{8,9},{9,8},{10,11... | collective-permute-start | bytes 393224 | tf_op jit(solution)/shard_map/ppermute | solution.py:22
  41.8 4.9 %collective-permute-start.18 = (s16[17,16,128]{2,1,0:T(8,128)(2,1)S(1)}, s16[17,16,128]{2,1,0:T(8,128)(2,1)S(1)}, u32[]{:S(2)}, u32[]{:S(2)}) collective-permute-start(s16[17,16,128]{2,1,0:T(8,128)(2,1)S(1)} %gradients.2.mine), channel_id=1, source_target_pairs={{0,8},{8,0},{16,24},{24,16},{1,9},{9,1},{17,25},{25,17},{2,10},{10... | collective-permute-start | bytes 208904 | tf_op jit(solution)/shard_map/ppermute | solution.py:22
  42.8 5.7 %collective-permute-start.24 = (s16[17,16,128]{2,1,0:T(8,128)(2,1)S(1)}, s16[17,16,128]{2,1,0:T(8,128)(2,1)S(1)}, u32[]{:S(2)}, u32[]{:S(2)}) collective-permute-start(s16[17,16,128]{2,1,0:T(8,128)(2,1)S(1)} %gradients.3.mine), channel_id=1, source_target_pairs={{0,8},{8,0},{16,24},{24,16},{1,9},{9,1},{17,25},{25,17},{2,10},{10... | collective-permute-start | bytes 208904 | tf_op jit(solution)/shard_map/ppermute | solution.py:22
  46.7 6.5 %collective-permute-start.19 = (s16[17,16,128]{2,1,0:T(8,128)(2,1)S(1)}, s16[17,16,128]{2,1,0:T(8,128)(2,1)S(1)}, u32[]{:S(2)}, u32[]{:S(2)}) collective-permute-start(s16[17,16,128]{2,1,0:T(8,128)(2,1)S(1)} %merge.2.mine), channel_id=1, source_target_pairs={{0,16},{8,24},{16,0},{24,8},{1,17},{9,25},{17,1},{25,9},{2,18},{10... | collective-permute-start | bytes 208904 | tf_op jit(solution)/shard_map/ppermute | solution.py:22
  48.5 6.2 %collective-permute-start.25 = (s16[17,16,128]{2,1,0:T(8,128)(2,1)S(1)}, s16[17,16,128]{2,1,0:T(8,128)(2,1)S(1)}, u32[]{:S(2)}, u32[]{:S(2)}) collective-permute-start(s16[17,16,128]{2,1,0:T(8,128)(2,1)S(1)} %merge.3.mine), channel_id=1, source_target_pairs={{0,16},{8,24},{16,0},{24,8},{1,17},{9,25},{17,1},{25,9},{2,18},{10... | collective-permute-start | bytes 208904 | tf_op jit(solution)/shard_map/ppermute | solution.py:22
  (5 other events, 40.1 us)

commit v25 on v21

--- a/solution.py
+++ b/solution.py
@@ -112,7 +112,7 @@
     k = directions.shape[1]
     kf = k // feat
     chunk = min(1024, persons)
-    sizes = [chunk] * (persons // chunk - 1) + [chunk // 2] * 2
+    sizes = [chunk] * (persons // chunk)
     piece = jax.ShapeDtypeStruct((kf, persons), F32)
     first = jax.ShapeDtypeStruct((kf, persons + LO), F32)
     out = pl.pallas_call(

time: 55.3 us -> 55.2 us (level)
  no operation moved by 1% of the time
where the time goes in v25:
time: 55.2 us; the launch traced here: 55.1 us
  starting transfers between devices  27.1 us (49%)
  waiting for transfers between devices  13.9 us (25%)
  Pallas kernels  13.8 us (25%)
    ppermute x26, starting transfers between devices, swap(): return lax.ppermute(x, axis, [(s, s ^ i) for s in range(count)])  27.1 us
    ppermute x26, waiting for transfers between devices, swap(): return lax.ppermute(x, axis, [(s, s ^ i) for s in range(count)])  13.9 us
    pallas_call x1, Pallas kernels, products(): pl.pallas_call(functools.partial(product_kernel, feat, kf, tuple(sizes)),...  3.35 us
    pallas_call x2, Pallas kernels, ordered_values(): pl.pallas_call(functools.partial(order_kernel, start, len(messages)), in_...  1.97 us
    pallas_call x2, Pallas kernels, gradients(): pl.pallas_call(functools.partial(gradient_kernel, parts, kf), in_specs=[V...  1.76 us
    pallas_call x1, Pallas kernels, prefix_sums(): pl.pallas_call(prefix_kernel, in_specs=[VMEM] * 3, out_shape=jax.ShapeDty...  1.75 us
  transfers between devices with their start and end apart: 26, of which 10 were waited for; matrix products, arithmetic and copies ran while one was open for 0% of the time, Pallas kernels for 17%

profile of v25, /device:TPU:0, one launch (start us, length us, event | category | flops | bytes accessed | tf_op | source)
XLA Modules:
  0.0 55.1 jit_solution(2633091680087498957)
XLA Ops:
  0.0 3.3 %products.1 = (f32[16,256]{1,0:T(8,128)S(1)}, f32[16,4096]{1,0:T(8,128)S(1)}, f32[16,4096]{1,0:T(8,128)S(1)}, f32[16,4096]{1,0:T(8,128)S(1)}, f32[16,4096]{1,0:T...) custom-call(bf16[512,128]{1,0:T(8,128)(2,1)} %directions.1, ...), custom_call_target="tpu_custom_call" | custom-call | flops 536870912 | bytes 6291456 | tf_op jit(solution)/shard_map/products/pallas_call | solution.py:118
  5.3 3.9 %collective-permute-start.1 = (s16[16,2176]{1,0:T(8,128)(2,1)S(1)}, s16[16,2176]{1,0:T(8,128)(2,1)S(1)}, u32[]{:S(2)}, u32[]{:S(2)}) collective-permute-start(s16[16,2176]{1,0:T(8,128)(2,1)S(1)} %join.6), channel_id=1, source_target_pairs={{0,6},{1,7},{2,4},{3,5},{4,2},{5,3},{6,0},{7,1},{8,14},{9,15},{10,... | collective-permute-start | bytes 208904 | tf_op jit(solution)/shard_map/ppermute | solution.py:22
  10.3 2.9 %collective-permute-start.8 = (s16[16,2688]{1,0:T(8,128)(2,1)S(1)}, s16[16,2688]{1,0:T(8,128)(2,1)S(1)}, u32[]{:S(2)}, u32[]{:S(2)}) collective-permute-start(s16[16,2688]{1,0:T(8,128)(2,1)S(1)} %join.9), channel_id=1, source_target_pairs={{0,6},{1,7},{2,4},{3,5},{4,2},{5,3},{6,0},{7,1},{8,14},{9,15},{10,... | collective-permute-start | bytes 258056 | tf_op jit(solution)/shard_map/ppermute | solution.py:22
  14.3 0.9 %collective-permute-done.5.refs_2_ = s16[16,2176]{1,0:T(8,128)(2,1)S(1)} collective-permute-done((s16[16,2176]{1,0:T(8,128)(2,1)S(1)}, s16[16,2176]{1,0:T(8,128)(2,1)S(1)}, u32[]{:S(2)}, u32[]{:S(2)}) %collective-permute-start.5) | collective-permute-done | bytes 69664 | tf_op jit(solution)/shard_map/ppermute | solution.py:22
  15.3 1.6 %collective-permute-start.6 = (f32[8,128]{1,0:T(8,128)S(1)}, f32[8,128]{1,0:T(8,128)S(1)}, u32[]{:S(2)}, u32[]{:S(2)}) collective-permute-start(f32[8,128]{1,0:T(8,128)S(1)} %get-tuple-element.40.refs_0_), channel_id=1, source_target_pairs={{0,8},{8,0},{16,24},{24,16},{1,9},{9,1},{17,25},{25,17},{2,10},{10... | collective-permute-start | bytes 12296 | tf_op jit(solution)/shard_map/ppermute | solution.py:22
  19.0 2.7 %collective-permute-start.11 = (f32[8,128]{1,0:T(8,128)S(1)}, f32[8,128]{1,0:T(8,128)S(1)}, u32[]{:S(2)}, u32[]{:S(2)}) collective-permute-start(f32[8,128]{1,0:T(8,128)S(1)} %get-tuple-element.44.refs_0_), channel_id=1, source_target_pairs={{0,16},{8,24},{16,0},{24,8},{1,17},{9,25},{17,1},{25,9},{2,18},{10... | collective-permute-start | bytes 12296 | tf_op jit(solution)/shard_map/ppermute | solution.py:22
  21.6 1.2 %ordered_values.3 = (f32[16,2560]{1,0:T(8,128)S(1)}, f32[256,256]{1,0:T(8,128)S(1)}, f32[16,128]{1,0:T(8,128)S(1)}) custom-call(f32[16,4096]{1,0:T(8,128)S(1)} %get-tuple-element.48.own, f32[16,4096]{1,0:T(8,128)S(1)} %collective-permute-done.7.refs_1_.other, s16[16,2688]{1,0:T(8,128)(2,1)S(1)} %collective-permute-done.8.refs_3_.refs_0_, ...), custom_call_target="tpu_custom_call" | custom-call | flops 671088640 | bytes 983040 | tf_op jit(solution)/shard_map/ordered_values/pallas_call | solution.py:398
  23.7 2.6 %collective-permute-start.14 = (f32[40,128]{1,0:T(8,128)S(1)}, f32[40,128]{1,0:T(8,128)S(1)}, u32[]{:S(2)}, u32[]{:S(2)}) collective-permute-start(f32[40,128]{1,0:T(8,128)S(1)} %get-tuple-element.53.refs_0_), channel_id=1, source_target_pairs={{0,16},{8,24},{16,0},{24,8},{1,17},{9,25},{17,1},{25,9},{2,18},{10... | collective-permute-start | bytes 61448 | tf_op jit(solution)/shard_map/ppermute | solution.py:22
  26.3 1.3 %collective-permute-start.13 = (f32[40,128]{1,0:T(8,128)S(1)}, f32[40,128]{1,0:T(8,128)S(1)}, u32[]{:S(2)}, u32[]{:S(2)}) collective-permute-start(f32[40,128]{1,0:T(8,128)S(1)} %get-tuple-element.53.refs_0_), channel_id=1, source_target_pairs={{0,24},{8,16},{16,8},{24,0},{1,25},{9,17},{17,9},{25,1},{2,26},{10... | collective-permute-start | bytes 61448 | tf_op jit(solution)/shard_map/ppermute | solution.py:22
  27.9 1.8 %prefix_sums.1.refs_6_ = f32[16,4096]{1,0:T(8,128)S(1)} custom-call(f32[256,256]{1,0:T(8,128)S(1)} %suffix_sums.1.ordered.sums, f32[16,256]{1,0:T(8,128)S(1)} %get-tuple-element.56.squares.square, s32[1,4096]{1,0:T(1,128)S(1)} %bitcast.6), custom_call_target="tpu_custom_call" | custom-call | flops 1073741824 | bytes 1572864 | tf_op jit(solution)/shard_map/prefix_sums/pallas_call | solution.py:464
  29.6 0.9 %hazards.1 = (f32[1,4096]{1,0:T(1,128)S(1)}, f32[1,4096]{1,0:T(1,128)S(1)}) custom-call(f32[16,256]{1,0:T(8,128)S(1)} %get-tuple-element.57.hazard, f32[16,256]{1,0:T(8,128)S(1)} %get-tuple-element.56.squares.square, s32[1,4096]{1,0:T(1,128)S(1)} %bitcast.7), custom_call_target="tpu_custom_call" | custom-call | flops 209715200 | bytes 262144 | tf_op jit(solution)/shard_map/hazards/pallas_call | solution.py:332
  30.6 1.3 %collective-permute-done.13.refs_2_ = f32[40,128]{1,0:T(8,128)S(1)} collective-permute-done((f32[40,128]{1,0:T(8,128)S(1)}, f32[40,128]{1,0:T(8,128)S(1)}, u32[]{:S(2)}, u32[]{:S(2)}) %collective-permute-start.13) | collective-permute-done | bytes 20512 | tf_op jit(solution)/shard_map/ppermute | solution.py:22
  32.1 2.1 %collective-permute-start.17 = (bf16[16,4096]{1,0:T(8,128)(2,1)S(1)}, bf16[16,4096]{1,0:T(8,128)(2,1)S(1)}, u32[]{:S(2)}, u32[]{:S(2)}) collective-permute-start(bf16[16,4096]{1,0:T(8,128)(2,1)S(1)} %weights.1.refs_0_), channel_id=1, source_target_pairs={{0,6},{1,7},{2,4},{3,5},{4,2},{5,3},{6,0},{7,1},{8,14},{9,15},{10,... | collective-permute-start | bytes 393224 | tf_op jit(solution)/shard_map/ppermute | solution.py:22
  34.7 1.0 %collective-permute-start.15 = (bf16[16,4096]{1,0:T(8,128)(2,1)S(1)}, bf16[16,4096]{1,0:T(8,128)(2,1)S(1)}, u32[]{:S(2)}, u32[]{:S(2)}) collective-permute-start(bf16[16,4096]{1,0:T(8,128)(2,1)S(1)} %weights.1.refs_0_), channel_id=1, source_target_pairs={{0,2},{1,3},{2,0},{3,1},{4,6},{5,7},{6,4},{7,5},{8,10},{9,11},{10,... | collective-permute-start | bytes 393224 | tf_op jit(solution)/shard_map/ppermute | solution.py:22
  35.6 2.4 %collective-permute-done.17.refs_3_ = bf16[16,4096]{1,0:T(8,128)(2,1)S(1)} collective-permute-done((bf16[16,4096]{1,0:T(8,128)(2,1)S(1)}, bf16[16,4096]{1,0:T(8,128)(2,1)S(1)}, u32[]{:S(2)}, u32[]{:S(2)}) %collective-permute-start.17) | collective-permute-done | bytes 131104 | tf_op jit(solution)/shard_map/ppermute | solution.py:22
  38.0 1.4 %collective-permute-done.16.refs_2_ = bf16[16,4096]{1,0:T(8,128)(2,1)S(1)} collective-permute-done((bf16[16,4096]{1,0:T(8,128)(2,1)S(1)}, bf16[16,4096]{1,0:T(8,128)(2,1)S(1)}, u32[]{:S(2)}, u32[]{:S(2)}) %collective-permute-start.16) | collective-permute-done | bytes 131104 | tf_op jit(solution)/shard_map/ppermute | solution.py:22
  39.9 0.9 %gradients.2.mine = s16[17,16,128]{2,1,0:T(8,128)(2,1)S(1)} custom-call(bf16[16,4096]{1,0:T(8,128)(2,1)S(1)} %weights.1.refs_0_, bf16[16,4096]{1,0:T(8,128)(2,1)S(1)} %collective-permute-done.15.refs_1_, bf16[16,4096]{1,0:T(8,128)(2,1)S(1)} %collective-permute-done.16.refs_2_, bf16[16,4096]{1,0:T(8,128)(2,1)S(1)} %collective-permute-done.17.refs_3_, ...), custom_call_target="tpu_custom_call" | custom-call | flops 268435456 | bytes 4718592 | tf_op jit(solution)/shard_map/gradients/pallas_call | solution.py:557
  41.4 0.9 %gradients.3.mine = s16[17,16,128]{2,1,0:T(8,128)(2,1)S(1)} custom-call(bf16[16,4096]{1,0:T(8,128)(2,1)S(1)} %collective-permute-done.20.refs_0_, bf16[16,4096]{1,0:T(8,128)(2,1)S(1)} %collective-permute-done.21.refs_1_, bf16[16,4096]{1,0:T(8,128)(2,1)S(1)} %collective-permute-done.22.refs_2_, bf16[16,4096]{1,0:T(8,128)(2,1)S(1)} %collective-permute-done.23.refs_3_, ...), custom_call_target="tpu_custom_call" | custom-call | flops 268435456 | bytes 4718592 | tf_op jit(solution)/shard_map/gradients/pallas_call | solution.py:557
  42.3 1.6 %collective-permute-start.24 = (s16[17,16,128]{2,1,0:T(8,128)(2,1)S(1)}, s16[17,16,128]{2,1,0:T(8,128)(2,1)S(1)}, u32[]{:S(2)}, u32[]{:S(2)}) collective-permute-start(s16[17,16,128]{2,1,0:T(8,128)(2,1)S(1)} %gradients.3.mine), channel_id=1, source_target_pairs={{0,8},{8,0},{16,24},{24,16},{1,9},{9,1},{17,25},{25,17},{2,10},{10... | collective-permute-start | bytes 208904 | tf_op jit(solution)/shard_map/ppermute | solution.py:22
  43.9 1.6 %collective-permute-done.18.other = s16[17,16,128]{2,1,0:T(8,128)(2,1)S(1)} collective-permute-done((s16[17,16,128]{2,1,0:T(8,128)(2,1)S(1)}, s16[17,16,128]{2,1,0:T(8,128)(2,1)S(1)}, u32[]{:S(2)}, u32[]{:S(2)}) %collective-permute-start.18) | collective-permute-done | bytes 69664 | tf_op jit(solution)/shard_map/ppermute | solution.py:22
  45.6 1.3 %collective-permute-start.19 = (s16[17,16,128]{2,1,0:T(8,128)(2,1)S(1)}, s16[17,16,128]{2,1,0:T(8,128)(2,1)S(1)}, u32[]{:S(2)}, u32[]{:S(2)}) collective-permute-start(s16[17,16,128]{2,1,0:T(8,128)(2,1)S(1)} %merge.2.mine), channel_id=1, source_target_pairs={{0,16},{8,24},{16,0},{24,8},{1,17},{9,25},{17,1},{25,9},{2,18},{10... | collective-permute-start | bytes 208904 | tf_op jit(solution)/shard_map/ppermute | solution.py:22
  46.9 2.0 %collective-permute-start.25 = (s16[17,16,128]{2,1,0:T(8,128)(2,1)S(1)}, s16[17,16,128]{2,1,0:T(8,128)(2,1)S(1)}, u32[]{:S(2)}, u32[]{:S(2)}) collective-permute-start(s16[17,16,128]{2,1,0:T(8,128)(2,1)S(1)} %merge.3.mine), channel_id=1, source_target_pairs={{0,16},{8,24},{16,0},{24,8},{1,17},{9,25},{17,1},{25,9},{2,18},{10... | collective-permute-start | bytes 208904 | tf_op jit(solution)/shard_map/ppermute | solution.py:22
  48.9 4.6 %collective-permute-done.19.other = s16[17,16,128]{2,1,0:T(8,128)(2,1)S(1)} collective-permute-done((s16[17,16,128]{2,1,0:T(8,128)(2,1)S(1)}, s16[17,16,128]{2,1,0:T(8,128)(2,1)S(1)}, u32[]{:S(2)}, u32[]{:S(2)}) %collective-permute-start.19) | collective-permute-done | bytes 69664 | tf_op jit(solution)/shard_map/ppermute | solution.py:22
  54.2 0.9 %finish.1 = f32[512,128]{1,0:T(8,128)} custom-call(f32[64,512]{1,0:T(8,128)S(1)} %add.1.first, s16[17,16,128]{2,1,0:T(8,128)(2,1)S(1)} %merge.3.mine, s16[17,16,128]{2,1,0:T(8,128)(2,1)S(1)} %collective-permute-done.25.other, f32[8,128]{1,0:T(8,128)S(1)} %get-tuple-element.60.count), custom_call_target="tpu_custom_call" | custom-call | tf_op jit(solution)/shard_map/finish/pallas_call | solution.py:627
  (61 shorter events, 10.0 us)
Async XLA Ops:
  3.9 5.3 %collective-permute-start.2 = (f32[16,4096]{1,0:T(8,128)S(1)}, f32[16,4096]{1,0:T(8,128)S(1)}, u32[]{:S(2)}, u32[]{:S(2)}) collective-permute-start(f32[16,4096]{1,0:T(8,128)S(1)} %get-tuple-element.37), channel_id=1, source_target_pairs={{0,1},{1,0},{2,3},{3,2},{4,5},{5,4},{6,7},{7,6},{8,9},{9,8},{10,11... | collective-permute-start | bytes 786440 | tf_op jit(solution)/shard_map/ppermute | solution.py:22
  4.0 5.9 %collective-permute-start.4 = (f32[16,4096]{1,0:T(8,128)S(1)}, f32[16,4096]{1,0:T(8,128)S(1)}, u32[]{:S(2)}, u32[]{:S(2)}) collective-permute-start(f32[16,4096]{1,0:T(8,128)S(1)} %get-tuple-element.39), channel_id=1, source_target_pairs={{0,1},{1,0},{2,3},{3,2},{4,5},{5,4},{6,7},{7,6},{8,9},{9,8},{10,11... | collective-permute-start | bytes 786440 | tf_op jit(solution)/shard_map/ppermute | solution.py:22
  4.4 5.8 %collective-permute-start.7 = (f32[16,4096]{1,0:T(8,128)S(1)}, f32[16,4096]{1,0:T(8,128)S(1)}, u32[]{:S(2)}, u32[]{:S(2)}) collective-permute-start(f32[16,4096]{1,0:T(8,128)S(1)} %get-tuple-element.41), channel_id=1, source_target_pairs={{0,1},{1,0},{2,3},{3,2},{4,5},{5,4},{6,7},{7,6},{8,9},{9,8},{10,11... | collective-permute-start | bytes 786440 | tf_op jit(solution)/shard_map/ppermute | solution.py:22
  5.3 8.8 %collective-permute-start.1 = (s16[16,2176]{1,0:T(8,128)(2,1)S(1)}, s16[16,2176]{1,0:T(8,128)(2,1)S(1)}, u32[]{:S(2)}, u32[]{:S(2)}) collective-permute-start(s16[16,2176]{1,0:T(8,128)(2,1)S(1)} %join.6), channel_id=1, source_target_pairs={{0,6},{1,7},{2,4},{3,5},{4,2},{5,3},{6,0},{7,1},{8,14},{9,15},{10,... | collective-permute-start | bytes 208904 | tf_op jit(solution)/shard_map/ppermute | solution.py:22
  9.3 4.9 %collective-permute-start.3 = (s16[16,2176]{1,0:T(8,128)(2,1)S(1)}, s16[16,2176]{1,0:T(8,128)(2,1)S(1)}, u32[]{:S(2)}, u32[]{:S(2)}) collective-permute-start(s16[16,2176]{1,0:T(8,128)(2,1)S(1)} %join.7), channel_id=1, source_target_pairs={{0,4},{1,5},{2,6},{3,7},{4,0},{5,1},{6,2},{7,3},{8,12},{9,13},{10,... | collective-permute-start | bytes 208904 | tf_op jit(solution)/shard_map/ppermute | solution.py:22
  10.0 5.1 %collective-permute-start.5 = (s16[16,2176]{1,0:T(8,128)(2,1)S(1)}, s16[16,2176]{1,0:T(8,128)(2,1)S(1)}, u32[]{:S(2)}, u32[]{:S(2)}) collective-permute-start(s16[16,2176]{1,0:T(8,128)(2,1)S(1)} %join.8), channel_id=1, source_target_pairs={{0,2},{1,3},{2,0},{3,1},{4,6},{5,7},{6,4},{7,5},{8,10},{9,11},{10,... | collective-permute-start | bytes 208904 | tf_op jit(solution)/shard_map/ppermute | solution.py:22
  10.3 8.6 %collective-permute-start.8 = (s16[16,2688]{1,0:T(8,128)(2,1)S(1)}, s16[16,2688]{1,0:T(8,128)(2,1)S(1)}, u32[]{:S(2)}, u32[]{:S(2)}) collective-permute-start(s16[16,2688]{1,0:T(8,128)(2,1)S(1)} %join.9), channel_id=1, source_target_pairs={{0,6},{1,7},{2,4},{3,5},{4,2},{5,3},{6,0},{7,1},{8,14},{9,15},{10,... | collective-permute-start | bytes 258056 | tf_op jit(solution)/shard_map/ppermute | solution.py:22
  13.4 5.6 %collective-permute-start.9 = (s16[16,2688]{1,0:T(8,128)(2,1)S(1)}, s16[16,2688]{1,0:T(8,128)(2,1)S(1)}, u32[]{:S(2)}, u32[]{:S(2)}) collective-permute-start(s16[16,2688]{1,0:T(8,128)(2,1)S(1)} %join.10), channel_id=1, source_target_pairs={{0,4},{1,5},{2,6},{3,7},{4,0},{5,1},{6,2},{7,3},{8,12},{9,13},{10,... | collective-permute-start | bytes 258056 | tf_op jit(solution)/shard_map/ppermute | solution.py:22
  14.1 4.9 %collective-permute-start.10 = (s16[16,2688]{1,0:T(8,128)(2,1)S(1)}, s16[16,2688]{1,0:T(8,128)(2,1)S(1)}, u32[]{:S(2)}, u32[]{:S(2)}) collective-permute-start(s16[16,2688]{1,0:T(8,128)(2,1)S(1)} %join.11), channel_id=1, source_target_pairs={{0,2},{1,3},{2,0},{3,1},{4,6},{5,7},{6,4},{7,5},{8,10},{9,11},{10,... | collective-permute-start | bytes 258056 | tf_op jit(solution)/shard_map/ppermute | solution.py:22
  15.3 3.6 %collective-permute-start.6 = (f32[8,128]{1,0:T(8,128)S(1)}, f32[8,128]{1,0:T(8,128)S(1)}, u32[]{:S(2)}, u32[]{:S(2)}) collective-permute-start(f32[8,128]{1,0:T(8,128)S(1)} %get-tuple-element.40.refs_0_), channel_id=1, source_target_pairs={{0,8},{8,0},{16,24},{24,16},{1,9},{9,1},{17,25},{25,17},{2,10},{10... | collective-permute-start | bytes 12296 | tf_op jit(solution)/shard_map/ppermute | solution.py:22
  19.0 4.6 %collective-permute-start.11 = (f32[8,128]{1,0:T(8,128)S(1)}, f32[8,128]{1,0:T(8,128)S(1)}, u32[]{:S(2)}, u32[]{:S(2)}) collective-permute-start(f32[8,128]{1,0:T(8,128)S(1)} %get-tuple-element.44.refs_0_), channel_id=1, source_target_pairs={{0,16},{8,24},{16,0},{24,8},{1,17},{9,25},{17,1},{25,9},{2,18},{10... | collective-permute-start | bytes 12296 | tf_op jit(solution)/shard_map/ppermute | solution.py:22
  23.7 6.8 %collective-permute-start.14 = (f32[40,128]{1,0:T(8,128)S(1)}, f32[40,128]{1,0:T(8,128)S(1)}, u32[]{:S(2)}, u32[]{:S(2)}) collective-permute-start(f32[40,128]{1,0:T(8,128)S(1)} %get-tuple-element.53.refs_0_), channel_id=1, source_target_pairs={{0,16},{8,24},{16,0},{24,8},{1,17},{9,25},{17,1},{25,9},{2,18},{10... | collective-permute-start | bytes 61448 | tf_op jit(solution)/shard_map/ppermute | solution.py:22
  26.3 5.6 %collective-permute-start.13 = (f32[40,128]{1,0:T(8,128)S(1)}, f32[40,128]{1,0:T(8,128)S(1)}, u32[]{:S(2)}, u32[]{:S(2)}) collective-permute-start(f32[40,128]{1,0:T(8,128)S(1)} %get-tuple-element.53.refs_0_), channel_id=1, source_target_pairs={{0,24},{8,16},{16,8},{24,0},{1,25},{9,17},{17,9},{25,1},{2,26},{10... | collective-permute-start | bytes 61448 | tf_op jit(solution)/shard_map/ppermute | solution.py:22
  27.7 4.2 %collective-permute-start.12 = (f32[40,128]{1,0:T(8,128)S(1)}, f32[40,128]{1,0:T(8,128)S(1)}, u32[]{:S(2)}, u32[]{:S(2)}) collective-permute-start(f32[40,128]{1,0:T(8,128)S(1)} %get-tuple-element.53.refs_0_), channel_id=1, source_target_pairs={{0,8},{8,0},{16,24},{24,16},{1,9},{9,1},{17,25},{25,17},{2,10},{10... | collective-permute-start | bytes 61448 | tf_op jit(solution)/shard_map/ppermute | solution.py:22
  32.1 6.0 %collective-permute-start.17 = (bf16[16,4096]{1,0:T(8,128)(2,1)S(1)}, bf16[16,4096]{1,0:T(8,128)(2,1)S(1)}, u32[]{:S(2)}, u32[]{:S(2)}) collective-permute-start(bf16[16,4096]{1,0:T(8,128)(2,1)S(1)} %weights.1.refs_0_), channel_id=1, source_target_pairs={{0,6},{1,7},{2,4},{3,5},{4,2},{5,3},{6,0},{7,1},{8,14},{9,15},{10,... | collective-permute-start | bytes 393224 | tf_op jit(solution)/shard_map/ppermute | solution.py:22
  34.1 5.3 %collective-permute-start.16 = (bf16[16,4096]{1,0:T(8,128)(2,1)S(1)}, bf16[16,4096]{1,0:T(8,128)(2,1)S(1)}, u32[]{:S(2)}, u32[]{:S(2)}) collective-permute-start(bf16[16,4096]{1,0:T(8,128)(2,1)S(1)} %weights.1.refs_0_), channel_id=1, source_target_pairs={{0,4},{1,5},{2,6},{3,7},{4,0},{5,1},{6,2},{7,3},{8,12},{9,13},{10,... | collective-permute-start | bytes 393224 | tf_op jit(solution)/shard_map/ppermute | solution.py:22
  34.7 5.0 %collective-permute-start.15 = (bf16[16,4096]{1,0:T(8,128)(2,1)S(1)}, bf16[16,4096]{1,0:T(8,128)(2,1)S(1)}, u32[]{:S(2)}, u32[]{:S(2)}) collective-permute-start(bf16[16,4096]{1,0:T(8,128)(2,1)S(1)} %weights.1.refs_0_), channel_id=1, source_target_pairs={{0,2},{1,3},{2,0},{3,1},{4,6},{5,7},{6,4},{7,5},{8,10},{9,11},{10,... | collective-permute-start | bytes 393224 | tf_op jit(solution)/shard_map/ppermute | solution.py:22
  35.6 5.7 %collective-permute-start.20 = (bf16[16,4096]{1,0:T(8,128)(2,1)S(1)}, bf16[16,4096]{1,0:T(8,128)(2,1)S(1)}, u32[]{:S(2)}, u32[]{:S(2)}) collective-permute-start(bf16[16,4096]{1,0:T(8,128)(2,1)S(1)} %weights.1.refs_0_), channel_id=1, source_target_pairs={{0,1},{1,0},{2,3},{3,2},{4,5},{5,4},{6,7},{7,6},{8,9},{9,8},{10,11... | collective-permute-start | bytes 393224 | tf_op jit(solution)/shard_map/ppermute | solution.py:22
  38.0 3.3 %collective-permute-start.23 = (bf16[16,4096]{1,0:T(8,128)(2,1)S(1)}, bf16[16,4096]{1,0:T(8,128)(2,1)S(1)}, u32[]{:S(2)}, u32[]{:S(2)}) collective-permute-start(bf16[16,4096]{1,0:T(8,128)(2,1)S(1)} %collective-permute-done.17.refs_3_), channel_id=1, source_target_pairs={{0,1},{1,0},{2,3},{3,2},{4,5},{5,4},{6,7},{7,6},{8,9},{9,8},{10,11... | collective-permute-start | bytes 393224 | tf_op jit(solution)/shard_map/ppermute | solution.py:22
  39.4 2.0 %collective-permute-start.22 = (bf16[16,4096]{1,0:T(8,128)(2,1)S(1)}, bf16[16,4096]{1,0:T(8,128)(2,1)S(1)}, u32[]{:S(2)}, u32[]{:S(2)}) collective-permute-start(bf16[16,4096]{1,0:T(8,128)(2,1)S(1)} %collective-permute-done.16.refs_2_), channel_id=1, source_target_pairs={{0,1},{1,0},{2,3},{3,2},{4,5},{5,4},{6,7},{7,6},{8,9},{9,8},{10,11... | collective-permute-start | bytes 393224 | tf_op jit(solution)/shard_map/ppermute | solution.py:22
  40.8 4.7 %collective-permute-start.18 = (s16[17,16,128]{2,1,0:T(8,128)(2,1)S(1)}, s16[17,16,128]{2,1,0:T(8,128)(2,1)S(1)}, u32[]{:S(2)}, u32[]{:S(2)}) collective-permute-start(s16[17,16,128]{2,1,0:T(8,128)(2,1)S(1)} %gradients.2.mine), channel_id=1, source_target_pairs={{0,8},{8,0},{16,24},{24,16},{1,9},{9,1},{17,25},{25,17},{2,10},{10... | collective-permute-start | bytes 208904 | tf_op jit(solution)/shard_map/ppermute | solution.py:22
  42.3 4.6 %collective-permute-start.24 = (s16[17,16,128]{2,1,0:T(8,128)(2,1)S(1)}, s16[17,16,128]{2,1,0:T(8,128)(2,1)S(1)}, u32[]{:S(2)}, u32[]{:S(2)}) collective-permute-start(s16[17,16,128]{2,1,0:T(8,128)(2,1)S(1)} %gradients.3.mine), channel_id=1, source_target_pairs={{0,8},{8,0},{16,24},{24,16},{1,9},{9,1},{17,25},{25,17},{2,10},{10... | collective-permute-start | bytes 208904 | tf_op jit(solution)/shard_map/ppermute | solution.py:22
  45.6 7.9 %collective-permute-start.19 = (s16[17,16,128]{2,1,0:T(8,128)(2,1)S(1)}, s16[17,16,128]{2,1,0:T(8,128)(2,1)S(1)}, u32[]{:S(2)}, u32[]{:S(2)}) collective-permute-start(s16[17,16,128]{2,1,0:T(8,128)(2,1)S(1)} %merge.2.mine), channel_id=1, source_target_pairs={{0,16},{8,24},{16,0},{24,8},{1,17},{9,25},{17,1},{25,9},{2,18},{10... | collective-permute-start | bytes 208904 | tf_op jit(solution)/shard_map/ppermute | solution.py:22
  46.9 7.3 %collective-permute-start.25 = (s16[17,16,128]{2,1,0:T(8,128)(2,1)S(1)}, s16[17,16,128]{2,1,0:T(8,128)(2,1)S(1)}, u32[]{:S(2)}, u32[]{:S(2)}) collective-permute-start(s16[17,16,128]{2,1,0:T(8,128)(2,1)S(1)} %merge.3.mine), channel_id=1, source_target_pairs={{0,16},{8,24},{16,0},{24,8},{1,17},{9,25},{17,1},{25,9},{2,18},{10... | collective-permute-start | bytes 208904 | tf_op jit(solution)/shard_map/ppermute | solution.py:22
  (5 other events, 39.6 us)
